TPU v7x, 32 devices: a whole 2x2x4 slice. The times are simulated.
32 devices in a mesh: member: 2 (over x), dp: 16 (over z, y, core).
Axes of the slice: x: 2, y: 2, z: 4, core: 2. Of those that a mesh axis runs over, the one named last changes fastest.
Arguments:
- features: bfloat16 [64, 256, 1024], P(('dp', 'member')), may hold values from -10 to 10
- teacher_logits: bfloat16 [4, 64, 256, 256], P('member', 'dp'), may hold values from -320 to 320
- lengths: int32 [64], P(('dp', 'member')), may hold values from 16 to 256
- gain_conv: float32 [1024], replicated, may hold values from 0.5 to 1.5
- weight_in: bfloat16 [1024, 2048], replicated, may hold values from -0.1875 to 0.1875
- weight_depth: float32 [31, 1024], replicated, may hold values from -1 to 1
- weight_out: bfloat16 [1024, 1024], replicated, may hold values from -0.1875 to 0.1875
- gain_out: float32 [1024], replicated, may hold values from 0.5 to 1.5
- head_weight: bfloat16 [1024, 256], replicated, may hold values from -1 to 1
Outputs:
- grad_gain_conv: float32 [1024], replicated
- grad_weight_in: float32 [1024, 2048], replicated
- grad_weight_depth: float32 [31, 1024], replicated
- grad_weight_out: float32 [1024, 1024], replicated
- grad_gain_out: float32 [1024], replicated
- grad_head: float32 [1024, 256], replicated
- utt_loss: float32 [64], P(('dp', 'member'))
All inputs are finite; a program needn't handle non-finite values.
Results may differ from a plain program's by a relative error of at most 0.015.
Values may be sent and summed in bfloat16 or wider, within the bound.
No kernel may reach another device: no remote copies, remote signals or barrier semaphores. Data moves between devices by JAX's collectives and lax.ppermute only.
A program may use at most 128 MiB of HBM per device.

v0:
```python
import jax
import jax.numpy as jnp
from jax import lax
from jax.sharding import PartitionSpec as P

TEACHERS = 4


def normalize(values, gain):
    average = jnp.mean(values, axis=-1, keepdims=True)
    centred = values - average
    spread = jnp.mean(centred * centred, axis=-1, keepdims=True)
    return centred * lax.rsqrt(spread + 1e-05) * gain


def live_frames(lengths, frames):
    return (jnp.arange(frames, dtype=jnp.int32)[None, :] < lengths[:, None]).astype(jnp.float32)


def lower_part(conv_weights, features, lengths):
    gain_conv, weight_in, weight_depth, weight_out = conv_weights
    utterances, frames, model_width = features.shape
    widened = features.astype(jnp.float32)
    normed = (
        normalize(widened, gain_conv).astype(jnp.bfloat16).reshape(utterances * frames, model_width)
    )
    projected = jnp.dot(normed, weight_in, preferred_element_type=jnp.float32)
    live_mask = live_frames(lengths, frames)
    gated = (projected[:, :model_width] * jax.nn.sigmoid(projected[:, model_width:])).reshape(
        utterances, frames, model_width
    ) * live_mask[:, :, None]
    half_width = weight_depth.shape[0] // 2
    convolved = lax.conv_general_dilated(
        gated,
        weight_depth[:, None, :],
        (1,),
        [(half_width, half_width)],
        dimension_numbers=("NWC", "WIO", "NWC"),
        feature_group_count=model_width,
        precision=lax.Precision.HIGHEST,
    )
    activated = (
        (convolved * jax.nn.sigmoid(convolved))
        .astype(jnp.bfloat16)
        .reshape(utterances * frames, model_width)
    )
    update = jnp.dot(activated, weight_out, preferred_element_type=jnp.float32)
    return widened + update.reshape(utterances, frames, model_width)


def upper_part(top_weights, residual_sum, target, lengths, mean_frames):
    gain_out, head_weight = top_weights
    utterances, frames, model_width = residual_sum.shape
    final_norm = (
        normalize(residual_sum, gain_out)
        .astype(jnp.bfloat16)
        .reshape(utterances * frames, model_width)
    )
    student_logits = jnp.dot(final_norm, head_weight, preferred_element_type=jnp.float32)
    student_logp = jax.nn.log_softmax(student_logits, axis=-1).reshape(utterances, frames, -1)
    cross_entropy = -jnp.sum(target * student_logp, axis=-1)
    return jnp.sum(cross_entropy * live_frames(lengths, frames), axis=-1) / mean_frames


def student_losses(weights, features, target, lengths, mean_frames):
    residual_sum = lower_part(weights[:4], features, lengths)
    return upper_part(weights[4:], residual_sum, target, lengths, mean_frames)


def teacher_target(summed):
    return jnp.exp(jax.nn.log_softmax(summed / TEACHERS, axis=-1))


def on_device(
    features,
    teacher_logits,
    lengths,
    gain_conv,
    weight_in,
    weight_depth,
    weight_out,
    gain_out,
    head_weight,
):
    frame_total = lax.psum(jnp.sum(lengths.astype(jnp.float32)), ("member", "dp"))
    own_count = lengths.shape[0]
    mean_frames = frame_total / (own_count * lax.axis_size("member") * lax.axis_size("dp"))
    local_sum = jnp.sum(jax.nn.log_softmax(teacher_logits.astype(jnp.float32), axis=-1), axis=0)
    own_sum = lax.psum_scatter(local_sum, "member", scatter_dimension=0, tiled=True)
    target = teacher_target(own_sum)
    weights = (gain_conv, weight_in, weight_depth, weight_out, gain_out, head_weight)

    def local_loss(trainable):
        return student_losses(trainable, features, target, lengths, mean_frames)

    losses, pullback = jax.vjp(local_loss, weights)
    gradients = pullback(jnp.ones_like(losses))[0]
    totals = lax.psum(
        (
            gradients[0],
            gradients[1].astype(jnp.float32),
            gradients[2],
            gradients[3].astype(jnp.float32),
            gradients[4],
            gradients[5].astype(jnp.float32),
        ),
        ("member", "dp"),
    )
    return (totals[0], totals[1], totals[2], totals[3], totals[4], totals[5], losses)


def solution(mesh):
    in_specs = (
        P(("dp", "member"), None, None),
        P("member", "dp", None, None),
        P(("dp", "member")),
        P(),
        P(),
        P(),
        P(),
        P(),
        P(),
    )
    out_specs = (P(), P(), P(), P(), P(), P(), P(("dp", "member")))
    return jax.shard_map(
        on_device, mesh=mesh, in_specs=in_specs, out_specs=out_specs, check_vma=False
    )
```

profile of v0, /device:TPU:0, one launch (start us, length us, event | category | flops | bytes accessed | tf_op | source)
XLA Modules:
  0.0 468.6 jit_solution(11123050680221878610)
XLA Ops:
  7.2 1.6 reduce_max.35
  8.9 14.1 %fusion.27 = f32[4,256,256]{2,1,0:T(8,128)} fusion(bf16[2,4,256,256]{3,2,1,0:T(8,128)(2,1)} %param.10, f32[2,4,256]{2,1,0:T(4,128)S(1)} %reduce_max.36), kind=kOutput, calls=%fused_computation.43 | output fusion | flops 2885887 | bytes 2105344 | tf_op jit(solution)/shard_map/jit(log_softmax)/reduce_sum | solution.py:88
  23.7 42.8 %psum.49 = f32[]{:T(128)} all-reduce(f32[]{:T(128)} %convert_reduce_fusion.1), channel_id=1, replica_groups=mesh['member'=2,'dp'=16] {'member','dp'}, use_global_device_ids=true, to_apply=%region_9.10 | all-reduce | flops 1 | bytes 8 | tf_op jit(solution)/shard_map/psum | solution.py:85
  67.6 1.0 copy-done.24
  69.1 2.4 fusion.72
  72.2 1.3 copy-done.4
  73.7 1.4 copy-done.11
  75.1 1.6 copy.69
  78.1 1.9 fusion.3
  80.0 11.0 %multiply_convert_fusion = (bf16[16,36,1024]{2,0,1:T(8,128)(2,1)S(1)}, f32[16,36,1024]{2,0,1:T(8,128)}, f32[16,36,1024]{2,0,1:T(8,128)}, f32[16,36,1024]{2,0,1:T(8,128)}) fusion(f32[31,1,1024]{2,0,1:T(8,128)S(1)} %bitcast.83, f32[2,8,66,1024]{3,0,2,1:T(2,128)S(1)} %fusion.3, pred[16,36]{0,1:T(8,128)(4,1)S(1)} %copy-done.32), kind=kOutput, calls=%fused_computation.32 | convolution fusion | flops 224133120 | bytes 12710464 | tf_op jit(solution)/shard_map/jvp()/conv_general_dilated | solution.py:33
  91.0 1.7 copy.49
  92.8 2.4 reshape.152
  95.1 2.6 fusion.70
  99.0 1.0 copy-done.7
  100.5 0.8 copy-done.9
  101.6 2.9 copy.56
  104.5 2.9 reshape.165
  107.3 1.7 copy-done.20
  109.0 2.9 copy.50
  111.9 2.9 reshape.161
  114.8 1.7 copy-done.19
  116.4 2.9 copy.53
  119.3 3.0 reshape.163
  123.1 2.0 subtract_subtract_fusion
  125.1 1.3 fusion.46
  126.4 2.1 fusion.69
  128.8 1.4 fusion.45
  131.3 1.1 fusion.25
  133.1 1.3 fusion.73
  135.3 0.9 slice-done
  136.2 9.8 %fusion.31 = f32[2,256,1024]{2,0,1:T(2,128)S(1)} fusion(f32[2,256,1024]{2,1,0:T(8,128)S(1)} %slice-done, f32[2,256,1024]{2,1,0:T(8,128)S(1)} %slice-done.2, f32[2,256,1024]{2,1,0:T(8,128)S(1)} %slice-done.1, f32[2,256,1024]{2,1,0:T(8,128)S(1)} %convert.9), kind=kLoop, calls=%fused_computation.50 | loop fusion | flops 2097152 | bytes 10485760 | tf_op jit(solution)/shard_map/transpose(jvp())/add_any | solution.py:43
  146.0 27.6 %fusion.67 = f32[31,1,1024]{2,1,0:T(1,128)S(1)} fusion(f32[2,256,1024]{2,0,1:T(2,128)S(1)} %fusion.31, f32[2,256,1024]{2,1,0:T(8,128)S(1)} %copy-done.12), kind=kOutput, calls=%fused_computation.114 | convolution fusion | flops 189136896 | bytes 4321280 | tf_op jit(solution)/shard_map/transpose(jvp())/conv_general_dilated | solution.py:33
  174.9 3.3 fusion.35
  178.8 1.4 copy.59
  180.4 5.5 %fusion.39 = f32[16,36,1024]{2,0,1:T(8,128)S(1)} fusion(f32[2,7,30,1024]{3,1,0,2:T(8,128)S(1)} %slice.22, f32[2,8,36,1024]{3,1,0,2:T(8,128)S(1)} %copy.59, pred[16,36]{0,1:T(8,128)(4,1)S(1)} %copy-done.32, f32[31,1024,1]{1,0,2:T(8,128)S(1)} %bitcast.84), kind=kOutput, calls=%fused_computation.67 | convolution fusion | flops 223248384 | bytes 6566464 | tf_op jit(solution)/shard_map/transpose(jvp())/conv_general_dilated | solution.py:33
  185.9 2.9 copy.61
  188.8 3.1 reshape.159
  191.9 1.9 slice_multiply_fusion
  193.9 0.9 copy-done.5
  194.7 1.0 fusion.26
  196.0 5.8 %convert_convert_fusion = f32[1024,2048]{1,0:T(8,128)} fusion(bf16[512,1024]{1,0:T(8,128)(2,1)S(1)} %bitcast.80, f32[512,1024]{1,0:T(8,128)S(1)} %get-tuple-element.18, f32[512,1024]{1,0:T(8,128)S(1)} %get-tuple-element.17), kind=kOutput, calls=%fused_computation.15 | convolution fusion | flops 2152726528 | bytes 13631488 | tf_op jit(solution)/shard_map/transpose(jvp())/dot_general | solution.py:27
  201.8 1.6 copy-done.14
  203.3 5.2 %fusion.22 = f32[1024]{0:T(1024)S(1)} fusion(bf16[2,256,1024]{2,1,0:T(8,128)(2,1)S(1)} %copy-done.6, f32[2,256]{1,0:T(2,128)S(1)} %add_rsqrt_fusion, f32[2,256]{1,0:T(2,128)S(1)} %broadcast_multiply_fusion.3, bf16[1024,2048]{1,0:T(8,128)(2,1)} %param.13, f32[512,1024]{1,0:T(8,128)} %copy-done.15, f32[512,1024]{1,0:T(8,128)S(1)} %copy-done.14), kind=kOutput, calls=%fused_computation.37 | convolution fusion | flops 2152201216 | bytes 9445376 | tf_op jit(solution)/shard_map/transpose(jvp())/dot_general | solution.py:27
  208.6 42.5 %all-reduce.2 = (f32[1024]{0:T(1024)}, f32[1024]{0:T(1024)}) all-reduce(f32[1024]{0:T(1024)S(1)} %fusion.22, f32[1024]{0:T(1024)S(1)} %get-tuple-element.7), channel_id=1, replica_groups=mesh['member'=2,'dp'=16] {'member','dp'}, use_global_device_ids=true, to_apply=%region_18.19 | all-reduce | flops 2048 | bytes 16384 | tf_op jit(solution)/shard_map/psum | solution.py:98
  251.8 197.2 %all-reduce.6.cloned.1.call-done = (f32[1024,2048]{1,0:T(8,128)}, f32[31,1024]{1,0:T(8,128)}, f32[1024,1024]{1,0:T(8,128)}, f32[1024,256]{1,0:T(8,128)}) async-done(((f32[1024,2048]{1,0:T(8,128)}, f32[31,1024]{1,0:T(8,128)}, f32[1024,1024]{1,0:T(8,128)}, f32[1024,256]{1,0:T(8,128)}), (f32[1024,2048]{1,0:T(8,128)}, f32[31,1024]{1,0:T(8,128)}, f32[1024,1024]{1,0:T(8,128)}, ...) | async-done | bytes 13758480 | tf_op jit(solution)/shard_map/psum | solution.py:98
  449.0 8.0 %copy.103 = f32[1024,2048]{1,0:T(8,128)} copy(f32[1024,2048]{1,0:T(8,128)} %get-tuple-element.29) | data formatting | bytes 16777216
  457.7 2.1 copy.105
  459.9 1.0 copy.106
  (103 shorter events, 14.0 us)
Async XLA Ops:
  7.2 88.0 %copy-start = (bf16[1024,1024]{1,0:T(8,128)(2,1)S(1)}, bf16[1024,1024]{1,0:T(8,128)(2,1)}, u32[]{:S(2)}) copy-start(bf16[1024,1024]{1,0:T(8,128)(2,1)} %param.15) | copy-start | bytes 6291460
  7.2 117.9 %reduce-scatter.2.cloned.1.call-start = ((), (), s32[]{:S(2)}) async-start(), calls=%async_computation.1 | async-start | bytes 1572864 | tf_op jit(solution)/shard_map/reduce_scatter | solution.py:89
  8.8 14.2 %copy-start.29 = (s32[2]{0:T(128)S(1)}, s32[2]{0:T(128)}, u32[]{:S(2)}) copy-start(s32[2]{0:T(128)} %param.11) | copy-start | bytes 28
  8.9 57.7 %copy-start.6 = (bf16[2,256,1024]{2,1,0:T(8,128)(2,1)S(1)}, bf16[2,256,1024]{2,1,0:T(8,128)(2,1)}, u32[]{:S(2)}) copy-start(bf16[2,256,1024]{2,1,0:T(8,128)(2,1)} %param.9) | copy-start | bytes 3145732
  22.9 44.3 %copy-start.30 = (f32[1024]{0:T(1024)S(1)}, f32[1024]{0:T(1024)}, u32[]{:S(2)}) copy-start(f32[1024]{0:T(1024)} %param.12) | copy-start | bytes 12292
  23.0 426.1 %all-reduce.6.cloned.1.call-start = ((), (), s32[]{:S(2)}) async-start(), calls=%async_computation.2 | async-start | bytes 27525120 | tf_op jit(solution)/shard_map/psum | solution.py:98
  66.5 2.6 copy-start.18
  67.6 1.1 copy-start.24
  71.5 2.0 copy-start.4
  73.7 1.4 copy-start.11
  78.1 1.9 copy-start.31
  78.1 1.9 copy-start.32
  97.7 1.3 copy-start.2
  97.7 0.7 copy-start.28
  98.1 1.9 copy-start.22
  99.0 1.0 copy-start.7
  99.0 2.6 copy-start.21
  100.5 0.8 copy-start.9
  107.3 1.7 copy-start.20
  114.8 1.7 copy-start.19
  125.1 3.5 copy-start.10
  125.1 3.7 copy-start.8
  128.6 1.7 copy-start.23
  128.8 2.0 copy-start.3
  133.1 1.6 slice-start.1
  133.1 2.2 slice-start.2
  134.4 1.8 slice-start
  136.2 9.8 %copy-start.12 = (f32[2,256,1024]{2,1,0:T(8,128)S(1)}, f32[2,256,1024]{2,1,0:T(8,128)}, u32[]{:S(2)}) copy-start(f32[2,256,1024]{2,1,0:T(8,128)} %copy-done.11) | copy-start | bytes 6291460
  173.6 1.3 copy-start.16
  191.9 2.8 copy-start.5
  194.7 1.2 copy-start.25
  195.7 6.0 %copy-start.13 = (f32[512,1024]{1,0:T(8,128)}, f32[512,1024]{1,0:T(8,128)S(1)}, u32[]{:S(2)}) copy-start(f32[512,1024]{1,0:T(8,128)S(1)} %get-tuple-element.17) | copy-start | bytes 6291460
  195.8 6.0 %copy-start.15 = (f32[512,1024]{1,0:T(8,128)}, f32[512,1024]{1,0:T(8,128)S(1)}, u32[]{:S(2)}) copy-start(f32[512,1024]{1,0:T(8,128)S(1)} %get-tuple-element.18) | copy-start | bytes 6291460
  201.8 1.6 copy-start.14
  449.0 8.0 %copy-start.27 = (f32[31,1024]{1,0:T(8,128)S(1)}, f32[31,1024]{1,0:T(8,128)}, u32[]{:S(2)}) copy-start(f32[31,1024]{1,0:T(8,128)} %get-tuple-element.30) | copy-start | bytes 380932
  449.0 8.7 %copy-start.17 = (f32[1024,1024]{1,0:T(8,128)S(1)}, f32[1024,1024]{1,0:T(8,128)}, u32[]{:S(2)}) copy-start(f32[1024,1024]{1,0:T(8,128)} %get-tuple-element.31) | copy-start | bytes 12582916
  457.7 2.1 copy-start.26
  457.7 3.8 copy-start.1
Sparse Core Ops, SparseCore 0:
  23.1 23.5 reduce-scatter.1
  201.9 247.0 all-reduce.5
where the time goes:
time: 472 us; the launch traced here: 469 us
  waiting for transfers between devices  197 us (42%)
  blocking collectives  85.4 us (18%)
  matrix products  67.1 us (14%)
  local copies, waits for them, and re-layouts  60.6 us (13%)
  other arithmetic  42.7 us (9%)
  between operations  15.5 us (3%)
    psum x1, waiting for transfers between devices, on_device(): lax.psum((gradients[0], gradients[1].astype(jnp.float32), gradients[2], g...  197 us
    conv_general_dilated x3, matrix products, lower_part(): lax.conv_general_dilated(gated, weight_depth[:, None, :], (1,), [(half_wi...  44.1 us
    psum x1, blocking collectives, on_device(): lax.psum(jnp.sum(lengths.astype(jnp.float32)), ('member', 'dp'))  42.8 us
    psum x1, blocking collectives, on_device(): lax.psum((gradients[0], gradients[1].astype(jnp.float32), gradients[2], g...  42.5 us
    unnamed x73, local copies, waits for them, and re-layouts  27.9 us
    conv_general_dilated x9, local copies, waits for them, and re-layouts, lower_part(): lax.conv_general_dilated(gated, weight_depth[:, None, :], (1,), [(half_wi...  14.7 us
    reduce_sum x1, other arithmetic, on_device(): jax.nn.log_softmax(teacher_logits.astype(jnp.float32), axis=-1)  14.1 us
    dot_general x3, matrix products, lower_part(): projected = jnp.dot(normed, weight_in, preferred_element_type=jnp.float32)  13.4 us
  transfers between devices with their start and end apart: 2, of which 1 were waited for; matrix products, arithmetic and copies ran while one was open for 12% of the time, Pallas kernels for 0%

commit v1 on v0

v1 whole, which is shorter than its diff:
```python
import functools

import jax
import jax.numpy as jnp
from jax import lax
from jax.experimental import pallas as pl
from jax.experimental.pallas import tpu as pltpu
from jax.sharding import PartitionSpec as P

TEACHERS = 4
AXES = ("member", "dp")
PLACE_BITS = 4
PLACES = 1 << PLACE_BITS
WIDE = 256
LANES = 128
TILE = 128
MARGIN = 16
CHUNKS = 2
VMEM = 56 << 20
SMEM_SPEC = pl.BlockSpec(memory_space=pltpu.SMEM)
F32 = jnp.float32
BF16 = jnp.bfloat16


def params():
    return pltpu.CompilerParams(vmem_limit_bytes=VMEM)


def dot(left, right, left_axis=1, right_axis=0):
    return lax.dot_general(
        left, right, (((left_axis,), (right_axis,)), ((), ())), preferred_element_type=F32
    )


def fixed(*shape):
    return pl.BlockSpec(shape, lambda i, *_: (0,) * len(shape))


def bit_orders(count):
    top = count.bit_length() - 2
    middle = list(range(2, top))
    return [top, 1] + middle, [1, top] + middle


def place_of(device, order):
    own = jnp.int32(0)
    for index, bit in enumerate(order[:PLACE_BITS]):
        own = own | (((device >> bit) & 1) << (PLACE_BITS - 1 - index))
    return own


def swap(values, bit, count):
    return lax.ppermute(values, AXES, [(i, i ^ (1 << bit)) for i in range(count)])


def add_pair(own, other):
    return (own.astype(F32) + other.astype(F32)).astype(own.dtype)


def sum_pieces(send, keep, orders, count):
    both = add_pair(keep, swap(send, 0, count))
    parts = [both[0], both[1]]
    for index in range(len(orders[0])):
        received = []
        for part, order in zip(parts, orders):
            half = part.shape[0] // 2 if index < PLACE_BITS else 0
            received.append(swap(part[half:], order[index], count))
        for group, other in enumerate(received):
            parts[group] = add_pair(parts[group][: other.shape[0]], other)
    for index in reversed(range(PLACE_BITS)):
        received = [swap(part, order[index], count) for part, order in zip(parts, orders)]
        parts = [jnp.concatenate([part, other], axis=0) for part, other in zip(parts, received)]
    own = jnp.stack(parts)
    return own, swap(own, 0, count)


def all_sum(values, count):
    for bit in range(count.bit_length() - 1):
        values = values + swap(values, bit, count)
    return values


def write_pieces(place, core, product, send_ref, keep_ref, lead, columns):
    rows = keep_ref.shape[-2]

    def one(piece, carry):
        base = (piece ^ place) * (2 * rows)
        kept = pl.multiple_of(base + core * rows, rows)
        sent = pl.multiple_of(base + (1 - core) * rows, rows)
        keep_ref[lead, piece, :, columns] = product[pl.ds(kept, rows), :].astype(BF16)
        send_ref[lead, piece, :, columns] = product[pl.ds(sent, rows), :].astype(BF16)
        return carry

    lax.fori_loop(0, PLACES, one, 0)


def teacher_kernel(member_ref, logits_ref, give_ref, keep_ref, *, own_count):
    step = pl.program_id(0)
    total = None
    for teacher in range(logits_ref.shape[0]):
        logits = logits_ref[teacher, 0].astype(F32)
        shifted = logits - jnp.max(logits, axis=-1, keepdims=True)
        logp = shifted - jnp.log(jnp.sum(jnp.exp(shifted), axis=-1, keepdims=True))
        total = logp if total is None else total + logp

    @pl.when(step < own_count)
    def _():
        give_ref[0] = total

    @pl.when(step >= own_count)
    def _():
        keep_ref[0] = total


def teacher_sums(member, logits, own_count):
    teachers, utterances, frames, symbols = logits.shape
    shape = jax.ShapeDtypeStruct((own_count, frames, symbols), F32)

    def source(i, member_ref):
        mine = member_ref[0] * own_count
        theirs = (1 - member_ref[0]) * own_count
        return (0, jnp.where(i < own_count, theirs + i, mine + i - own_count), 0, 0)

    return pl.pallas_call(
        functools.partial(teacher_kernel, own_count=own_count),
        out_shape=(shape, shape),
        grid_spec=pltpu.PrefetchScalarGridSpec(
            num_scalar_prefetch=1,
            grid=(2 * own_count,),
            in_specs=[pl.BlockSpec((teachers, 1, frames, symbols), source)],
            out_specs=(
                pl.BlockSpec(
                    (1, frames, symbols), lambda i, _: (jnp.minimum(i, own_count - 1), 0, 0)
                ),
                pl.BlockSpec(
                    (1, frames, symbols), lambda i, _: (jnp.maximum(i - own_count, 0), 0, 0)
                ),
            ),
        ),
        compiler_params=params(),
        name="teachers",
    )(member, logits)


def live_column(lengths_ref, utterance, frames):
    position = lax.broadcasted_iota(jnp.int32, (frames, 1), 0)
    return (position < lengths_ref[utterance]).astype(F32)


def clear_margins(pad_ref):
    frames = pad_ref.shape[2] - 2 * MARGIN
    zeros = jnp.zeros(pad_ref.shape[:2] + (MARGIN, LANES), F32)
    pad_ref[:, :, :MARGIN, :] = zeros
    pad_ref[:, :, MARGIN + frames :, :] = zeros


def shifted_views(pad_ref, lane, utterance, start, taps):
    first = MARGIN - taps // 2
    for phase in range(8):
        offsets = [offset for offset in range(first, first + taps) if offset % 8 == phase]
        if not offsets:
            continue
        low = offsets[0]
        span = offsets[-1] - low + TILE
        view = pad_ref[lane, utterance, start + low : start + low + span, :]
        for offset in offsets:
            yield offset - first, view[offset - low : offset - low + TILE]


def convolve(pad_ref, lane, utterance, start, depth_ref, flipped):
    taps = depth_ref.shape[0]
    columns = slice(lane * LANES, (lane + 1) * LANES)
    total = jnp.zeros((TILE, LANES), F32)
    for tap, view in shifted_views(pad_ref, lane, utterance, start, taps):
        row = taps - 1 - tap if flipped else tap
        total = total + view * depth_ref[row : row + 1, columns]
    return total


def forward_kernel(
    lengths_ref,
    features_ref,
    gain_ref,
    value_weight_ref,
    gate_weight_ref,
    depth_ref,
    out_weight_ref,
    normed_ref,
    gated_ref,
    gate_ref,
    slope_ref,
    active_ref,
    residual_ref,
    pad_ref,
):
    utterances = pad_ref.shape[1]
    frames = pad_ref.shape[2] - 2 * MARGIN

    @pl.when(pl.program_id(0) == 0)
    def _():
        values = features_ref[...].astype(F32)
        centred = values - jnp.mean(values, axis=-1, keepdims=True)
        spread = jnp.mean(centred * centred, axis=-1, keepdims=True)
        normed_ref[...] = (centred * lax.rsqrt(spread + 1e-05) * gain_ref[...]).astype(BF16)
        residual_ref[...] = values
        clear_margins(pad_ref)

    for utterance in range(utterances):
        rows = slice(utterance * frames, (utterance + 1) * frames)
        normed = normed_ref[rows, :]
        gate = jax.nn.sigmoid(dot(normed, gate_weight_ref[...]))
        gated = dot(normed, value_weight_ref[...]) * gate
        gated = gated * live_column(lengths_ref, utterance, frames)
        gate_ref[rows, :] = gate
        gated_ref[rows, :] = gated
        for lane in range(WIDE // LANES):
            pad_ref[lane, utterance, MARGIN : MARGIN + frames, :] = gated[
                :, lane * LANES : (lane + 1) * LANES
            ]

    for lane in range(WIDE // LANES):
        columns = slice(lane * LANES, (lane + 1) * LANES)

        def one(utterance, carry, lane=lane, columns=columns):
            for start in range(0, frames, TILE):
                rows = pl.ds(pl.multiple_of(utterance * frames + start, TILE), TILE)
                convolved = convolve(pad_ref, lane, utterance, start, depth_ref, False)
                squash = jax.nn.sigmoid(convolved)
                active_ref[rows, columns] = (convolved * squash).astype(BF16)
                slope_ref[rows, columns] = squash * (1.0 + convolved * (1.0 - squash))
            return carry

        lax.fori_loop(0, utterances, one, 0)

    residual_ref[...] += dot(active_ref[...], out_weight_ref[...])


def forward(lengths, features, gain, weight_in, depth, weight_out, utterances):
    rows, model = features.shape
    frames = rows // utterances
    steps = model // WIDE
    column = pl.BlockSpec((rows, WIDE), lambda i: (0, i))
    wide = jax.ShapeDtypeStruct((rows, model), F32)
    narrow = jax.ShapeDtypeStruct((rows, model), BF16)
    return pl.pallas_call(
        forward_kernel,
        grid=(steps,),
        out_shape=(narrow, wide, wide, wide, narrow, wide),
        in_specs=[
            SMEM_SPEC,
            fixed(rows, model),
            fixed(1, model),
            pl.BlockSpec((model, WIDE), lambda i: (0, i)),
            pl.BlockSpec((model, WIDE), lambda i: (0, steps + i)),
            pl.BlockSpec((depth.shape[0], WIDE), lambda i: (0, i)),
            pl.BlockSpec((WIDE, model), lambda i: (i, 0)),
        ],
        out_specs=(fixed(rows, model), column, column, column, column, fixed(rows, model)),
        scratch_shapes=[pltpu.VMEM((WIDE // LANES, utterances, frames + 2 * MARGIN, LANES), F32)],
        compiler_params=params(),
        name="forward",
    )(lengths, features, gain, weight_in, weight_in, depth, weight_out)


def top_kernel(
    lengths_ref,
    residual_ref,
    gain_ref,
    head_ref,
    kept_ref,
    got_ref,
    loss_ref,
    final_ref,
    dlogits_ref,
    dresidual_ref,
):
    frames = residual_ref.shape[0]
    live = live_column(lengths_ref, pl.program_id(0), frames)
    values = residual_ref[...]
    centred = values - jnp.mean(values, axis=-1, keepdims=True)
    spread = jnp.mean(centred * centred, axis=-1, keepdims=True)
    inverse = lax.rsqrt(spread + 1e-05)
    unit = centred * inverse
    final = (unit * gain_ref[...]).astype(BF16)
    final_ref[...] = final

    def log_softmax(logits):
        shifted = logits - jnp.max(logits, axis=-1, keepdims=True)
        return shifted - jnp.log(jnp.sum(jnp.exp(shifted), axis=-1, keepdims=True))

    target = jnp.exp(log_softmax((kept_ref[0] + got_ref[0]) * (1.0 / TEACHERS)))
    logp = log_softmax(dot(final, head_ref[...]))
    cross = -jnp.sum(target * logp, axis=-1, keepdims=True)
    loss_ref[...] = jnp.broadcast_to(jnp.sum(cross * live, axis=0, keepdims=True), (1, 1, LANES))
    weight = jnp.sum(target, axis=-1, keepdims=True)
    dlogits = ((jnp.exp(logp) * weight - target) * live).astype(BF16)
    dlogits_ref[...] = dlogits
    dunit = dot(dlogits, head_ref[...], 1, 1) * gain_ref[...]
    average = jnp.mean(dunit, axis=-1, keepdims=True)
    along = jnp.mean(dunit * unit, axis=-1, keepdims=True)
    dresidual_ref[...] = (inverse * (dunit - average - unit * along)).astype(BF16)


def top(lengths, residual, gain, head, kept, got):
    rows, model = residual.shape
    utterances, frames, symbols = kept.shape
    per_row = pl.BlockSpec((frames, model), lambda i: (i, 0))
    sums = pl.BlockSpec((1, frames, symbols), lambda i: (i, 0, 0))
    return pl.pallas_call(
        top_kernel,
        grid=(utterances,),
        out_shape=(
            jax.ShapeDtypeStruct((utterances, 1, LANES), F32),
            jax.ShapeDtypeStruct((rows, model), BF16),
            jax.ShapeDtypeStruct((rows, symbols), BF16),
            jax.ShapeDtypeStruct((rows, model), BF16),
        ),
        in_specs=[SMEM_SPEC, per_row, fixed(1, model), fixed(model, symbols), sums, sums],
        out_specs=(
            pl.BlockSpec((1, 1, LANES), lambda i: (i, 0, 0)),
            per_row,
            pl.BlockSpec((frames, symbols), lambda i: (i, 0)),
            per_row,
        ),
        compiler_params=params(),
        name="top",
    )(lengths, residual, gain, head, kept, got)


def outer_kernel(
    own_ref, active_ref, dresidual_ref, final_ref, dlogits_ref, send_ref, keep_ref, product_ref
):
    group = pl.program_id(0)
    width = dresidual_ref.shape[1]
    product_ref[:, :width] = dot(active_ref[...], dresidual_ref[...], 0, 0)
    product_ref[:, width:] = dot(final_ref[...], dlogits_ref[...], 0, 0)
    write_pieces(own_ref[group], own_ref[2], product_ref, send_ref, keep_ref, 0, slice(None))


def outer(own, active, dresidual, final, dlogits):
    rows, model = active.shape
    half_out = dresidual.shape[1] // 2
    half_head = dlogits.shape[1] // 2
    width = half_out + half_head
    piece = (PLACES, model // (2 * PLACES), width)
    shape = jax.ShapeDtypeStruct((2,) + piece, BF16)
    out = pl.BlockSpec((1,) + piece, lambda i: (i, 0, 0, 0))
    return pl.pallas_call(
        outer_kernel,
        grid=(2,),
        out_shape=(shape, shape),
        in_specs=[
            SMEM_SPEC,
            fixed(rows, model),
            pl.BlockSpec((rows, half_out), lambda i: (0, i)),
            fixed(rows, model),
            pl.BlockSpec((rows, half_head), lambda i: (0, i)),
        ],
        out_specs=(out, out),
        scratch_shapes=[pltpu.VMEM((model, width), F32)],
        compiler_params=params(),
        name="outer",
    )(own, active, dresidual, final, dlogits)


def inner_kernel(
    own_ref,
    lengths_ref,
    dresidual_ref,
    out_weight_ref,
    slope_ref,
    gated_ref,
    gate_ref,
    normed_ref,
    depth_ref,
    send_ref,
    keep_ref,
    dconv_ref,
    pad_ref,
    dvalue_ref,
    dgate_ref,
    product_ref,
):
    utterances = pad_ref.shape[1]
    frames = pad_ref.shape[2] - 2 * MARGIN

    @pl.when(pl.program_id(0) == 0)
    def _():
        clear_margins(pad_ref)

    for utterance in range(utterances):
        rows = slice(utterance * frames, (utterance + 1) * frames)
        dconv = dot(dresidual_ref[rows, :], out_weight_ref[...], 1, 1) * slope_ref[rows, :]
        dconv_ref[rows, :] = dconv
        for lane in range(WIDE // LANES):
            pad_ref[lane, utterance, MARGIN : MARGIN + frames, :] = dconv[
                :, lane * LANES : (lane + 1) * LANES
            ]

    for lane in range(WIDE // LANES):
        columns = slice(lane * LANES, (lane + 1) * LANES)

        def one(utterance, carry, lane=lane, columns=columns):
            for start in range(0, frames, TILE):
                rows = pl.ds(pl.multiple_of(utterance * frames + start, TILE), TILE)
                position = lax.broadcasted_iota(jnp.int32, (TILE, 1), 0) + start
                live = (position < lengths_ref[utterance]).astype(F32)
                dgated = convolve(pad_ref, lane, utterance, start, depth_ref, True) * live
                gate = gate_ref[rows, columns]
                dvalue_ref[rows, columns] = (dgated * gate).astype(BF16)
                dgate_ref[rows, columns] = (dgated * gated_ref[rows, columns] * (1.0 - gate)).astype(
                    BF16
                )
            return carry

        lax.fori_loop(0, utterances, one, 0)

    for group, source in ((0, dvalue_ref), (1, dgate_ref)):
        product_ref[...] = dot(normed_ref[...], source[...], 0, 0)
        write_pieces(own_ref[group], own_ref[2], product_ref, send_ref, keep_ref, group, slice(None))


def inner(own, lengths, dresidual, weight_out, slope, gated, gate, normed, depth, chunk, utterances):
    rows, model = normed.shape
    frames = rows // utterances
    steps = model // WIDE // CHUNKS
    first = chunk * steps
    column = pl.BlockSpec((rows, WIDE), lambda i: (0, first + i))
    piece = (2, PLACES, model // (2 * PLACES))
    shape = jax.ShapeDtypeStruct(piece + (steps * WIDE,), BF16)
    out = pl.BlockSpec(piece + (WIDE,), lambda i: (0, 0, 0, i))
    return pl.pallas_call(
        inner_kernel,
        grid=(steps,),
        out_shape=(shape, shape, jax.ShapeDtypeStruct((rows, steps * WIDE), F32)),
        in_specs=[
            SMEM_SPEC,
            SMEM_SPEC,
            fixed(rows, model),
            pl.BlockSpec((WIDE, model), lambda i: (first + i, 0)),
            column,
            column,
            column,
            fixed(rows, model),
            pl.BlockSpec((depth.shape[0], WIDE), lambda i: (0, first + i)),
        ],
        out_specs=(out, out, pl.BlockSpec((rows, WIDE), lambda i: (0, i))),
        scratch_shapes=[
            pltpu.VMEM((WIDE // LANES, utterances, frames + 2 * MARGIN, LANES), F32),
            pltpu.VMEM((rows, WIDE), BF16),
            pltpu.VMEM((rows, WIDE), BF16),
            pltpu.VMEM((model, WIDE), F32),
        ],
        compiler_params=params(),
        name="inner",
    )(own, lengths, dresidual, weight_out, slope, gated, gate, normed, depth)


def taps_kernel(lengths_ref, gated_ref, dconv_ref, out_ref, pad_ref, sums_ref):
    utterances = pad_ref.shape[1]
    frames = pad_ref.shape[2] - 2 * MARGIN
    taps = out_ref.shape[0] - 1
    valid = lengths_ref[0]
    for utterance in range(1, utterances):
        valid = valid + lengths_ref[utterance]

    @pl.when(pl.program_id(0) == 0)
    def _():
        clear_margins(pad_ref)

    for lane in range(WIDE // LANES):
        columns = slice(lane * LANES, (lane + 1) * LANES)
        for utterance in range(utterances):
            rows = slice(utterance * frames, (utterance + 1) * frames)
            pad_ref[lane, utterance, MARGIN : MARGIN + frames, :] = gated_ref[rows, columns]
        sums_ref[...] = jnp.zeros_like(sums_ref)

        def one(utterance, carry, lane=lane, columns=columns):
            for start in range(0, frames, TILE):
                rows = pl.ds(pl.multiple_of(utterance * frames + start, TILE), TILE)
                dconv = dconv_ref[rows, columns]
                for tap, view in shifted_views(pad_ref, lane, utterance, start, taps):
                    sums_ref[tap] += jnp.sum((view * dconv).reshape(TILE // 8, 8, LANES), axis=0)
            return carry

        lax.fori_loop(0, utterances, one, 0)
        out_ref[:taps, columns] = jnp.sum(sums_ref[...], axis=1)
    out_ref[taps:, :] = jnp.zeros((1, WIDE), F32) + valid.astype(F32)


def tap_sums(lengths, gated, dconv, taps, chunk, utterances):
    rows, width = dconv.shape
    steps = width // WIDE
    first = chunk * steps
    return pl.pallas_call(
        taps_kernel,
        grid=(steps,),
        out_shape=jax.ShapeDtypeStruct((taps + 1, width), F32),
        in_specs=[
            SMEM_SPEC,
            pl.BlockSpec((rows, WIDE), lambda i: (0, first + i)),
            pl.BlockSpec((rows, WIDE), lambda i: (0, i)),
        ],
        out_specs=pl.BlockSpec((taps + 1, WIDE), lambda i: (0, i)),
        scratch_shapes=[
            pltpu.VMEM((WIDE // LANES, utterances, rows // utterances + 2 * MARGIN, LANES), F32),
            pltpu.VMEM((taps, 8, LANES), F32),
        ],
        compiler_params=params(),
        name="taps",
    )(lengths, gated, dconv)


def unpack_kernel(utts, per_step, own_ref, small_ref, weight_ref, head_ref, *refs):
    arrays = (len(refs) - 5) // 4
    pieces, (win_ref, wout_ref, dhead_ref, gain_in_ref, gain_out_ref) = refs[:-5], refs[-5:]
    scale = utts / small_ref[small_ref.shape[0] - 1 :, 0:1]
    core = own_ref[2]
    rows = pieces[0].shape[2]
    half_out = wout_ref.shape[1] // 2
    half_in = win_ref.shape[1] // 2
    half_head = dhead_ref.shape[1] // 2
    for index in range(per_step):
        for group in range(2):
            piece = index ^ (own_ref[group] & (per_step - 1))
            for whose in range(2):
                side = core if whose == 0 else 1 - core
                here = pl.ds(pl.multiple_of(index * 2 * rows + side * rows, rows), rows)
                for array in range(arrays):
                    source = pieces[(array * 2 + whose) * 2 + group]
                    wide = source[0, piece].astype(F32) * scale
                    if array == 0:
                        wout_ref[here, group * half_out : (group + 1) * half_out] = wide[:, :half_out]
                        dhead_ref[here, group * half_head : (group + 1) * half_head] = wide[
                            :, half_out:
                        ]
                    else:
                        width = wide.shape[1]
                        first = group * half_in + (array - 1) * width
                        win_ref[here, first : first + width] = wide
    gain_in_ref[...] = jnp.sum(weight_ref[...].astype(F32) * win_ref[...], axis=1, keepdims=True)
    gain_out_ref[...] = jnp.sum(head_ref[...].astype(F32) * dhead_ref[...], axis=1, keepdims=True)


def unpack(utts, own, small, weight_in, head, sums, width_out):
    steps = 4
    per_step = PLACES // steps
    model = head.shape[0]
    rows = model // steps
    widths = (weight_in.shape[1], width_out, head.shape[1], 1, 1)
    operands = []
    specs = []
    for pair in sums:
        for array in pair:
            for group in range(2):
                operands.append(array)
                specs.append(
                    pl.BlockSpec(
                        (1, per_step) + array.shape[2:],
                        lambda i, own_ref, group=group: (
                            group,
                            i ^ (own_ref[group] // per_step),
                            0,
                            0,
                        ),
                    )
                )

    def block(width):
        return pl.BlockSpec((rows, width), lambda i, own_ref: (i, 0))

    return pl.pallas_call(
        functools.partial(unpack_kernel, utts, per_step),
        out_shape=tuple(jax.ShapeDtypeStruct((model, width), F32) for width in widths),
        grid_spec=pltpu.PrefetchScalarGridSpec(
            num_scalar_prefetch=1,
            grid=(steps,),
            in_specs=[fixed(*small.shape), block(weight_in.shape[1]), block(head.shape[1])] + specs,
            out_specs=tuple(block(width) for width in widths),
        ),
        compiler_params=params(),
        name="unpack",
    )(own, small, weight_in, head, *operands)


def on_device(
    features,
    teacher_logits,
    lengths,
    gain_conv,
    weight_in,
    weight_depth,
    weight_out,
    gain_out,
    head_weight,
):
    count = lax.axis_size("member") * lax.axis_size("dp")
    member = lax.axis_index("member").astype(jnp.int32)
    device = member * lax.axis_size("dp") + lax.axis_index("dp")
    orders = bit_orders(count)
    own = jnp.stack([place_of(device, order) for order in orders] + [device & 1]).astype(jnp.int32)
    taps, model = weight_depth.shape
    utterances, frames, _ = features.shape
    utts = float(utterances * count)

    give, kept = teacher_sums(member[None], teacher_logits, utterances)
    got = swap(give, count.bit_length() - 2, count)
    flat = features.reshape(utterances * frames, model)
    normed, gated, gate, slope, active, residual = forward(
        lengths, flat, gain_conv[None], weight_in, weight_depth, weight_out, utterances
    )
    losses, final, dlogits, dresidual = top(
        lengths, residual, gain_out[None], head_weight, kept, got
    )
    sums = [sum_pieces(*outer(own, active, dresidual, final, dlogits), orders, count)]
    dconvs = []
    for chunk in range(CHUNKS):
        send, keep, dconv = inner(
            own,
            lengths,
            dresidual,
            weight_out,
            slope,
            gated,
            gate,
            normed,
            weight_depth,
            chunk,
            utterances,
        )
        dconvs.append(dconv)
        sums.append(sum_pieces(send, keep, orders, count))
    small = jnp.concatenate(
        [
            tap_sums(lengths, gated, dconv, taps, chunk, utterances)
            for chunk, dconv in enumerate(dconvs)
        ],
        axis=1,
    )
    small = all_sum(small, count)
    grad_in, grad_out, grad_head, by_in, by_head = unpack(
        utts, own, small, weight_in, head_weight, sums, weight_out.shape[1]
    )
    scale = utts / small[taps, 0]
    return (
        by_in.reshape(model) / gain_conv,
        grad_in,
        small[:taps] * scale,
        grad_out,
        by_head.reshape(model) / gain_out,
        grad_head,
        losses[:, 0, 0] * scale,
    )


def solution(mesh):
    in_specs = (
        P(("dp", "member"), None, None),
        P("member", "dp", None, None),
        P(("dp", "member")),
        P(),
        P(),
        P(),
        P(),
        P(),
        P(),
    )
    out_specs = (P(), P(), P(), P(), P(), P(), P(("dp", "member")))
    return jax.shard_map(
        on_device, mesh=mesh, in_specs=in_specs, out_specs=out_specs, check_vma=False
    )
```

time: 472 us -> 234 us (0.50)
  waiting for transfers between devices: 197 us -> 64.9 us
  blocking collectives: 85.4 us -> 0 us
  starting transfers between devices: 0.08 us -> 82.1 us
  Pallas kernels: 0 us -> 71.8 us
  matrix products: 67.1 us -> 0 us
  local copies, waits for them, and re-layouts: 60.6 us -> 4.31 us
  other arithmetic: 42.7 us -> 8.39 us
  between operations: 15.5 us -> 2.22 us
    psum x1 -> x0, waiting for transfers between devices: 197 us -> none  [on_device(): lax.psum((gradients[0], gradients[1].astype(jnp.float32), gradients[2], g...]
    psum x2 -> x0, blocking collectives: 85.4 us -> none  [the longest x1 42.8 us: on_device(): lax.psum(jnp.sum(lengths.astype(jnp.float32)), ('member', 'dp'))]
    ppermute x0 -> x60, starting transfers between devices: none -> 82.1 us  [swap(): return lax.ppermute(values, AXES, [(i, i ^ 1 << bit) for i in range(count)])]
    pallas_call x0 -> x9, Pallas kernels: none -> 71.8 us  [the longest x2 22.1 us: inner(): pl.pallas_call(inner_kernel, grid=(steps,), out_shape=(shape, shape, jax....]
    ppermute x0 -> x60, waiting for transfers between devices: none -> 64.9 us  [swap(): return lax.ppermute(values, AXES, [(i, i ^ 1 << bit) for i in range(count)])]
    conv_general_dilated x3 -> x0, matrix products: 44.1 us -> none  [lower_part(): lax.conv_general_dilated(gated, weight_depth[:, None, :], (1,), [(half_wi...]
    unnamed x73 -> x50, local copies, waits for them, and re-layouts: 27.9 us -> 3.34 us
    dot_general x9 -> x0, matrix products: 22.9 us -> none  [the longest x3 13.4 us: lower_part(): projected = jnp.dot(normed, weight_in, preferred_element_type=jnp.float32)]
  transfers between devices with their start and end apart: 2 -> 60, of which waited for: 1 -> 33; matrix products, arithmetic and copies ran while one was open for 12% -> 3% of each run, Pallas kernels for 0% -> 17%
where the time goes in v1:
time: 234 us
  starting transfers between devices  82.1 us (35%)
  Pallas kernels  71.8 us (31%)
  waiting for transfers between devices  64.9 us (28%)
  other arithmetic  8.39 us (4%)
  local copies, waits for them, and re-layouts  4.31 us (2%)
    ppermute x60, starting transfers between devices, swap(): return lax.ppermute(values, AXES, [(i, i ^ 1 << bit) for i in range(count)])  82.1 us
    ppermute x60, waiting for transfers between devices, swap(): return lax.ppermute(values, AXES, [(i, i ^ 1 << bit) for i in range(count)])  64.9 us
    pallas_call x2, Pallas kernels, inner(): pl.pallas_call(inner_kernel, grid=(steps,), out_shape=(shape, shape, jax....  22.1 us
    pallas_call x1, Pallas kernels, forward(): pl.pallas_call(forward_kernel, grid=(steps,), out_shape=(narrow, wide, wi...  15 us
    pallas_call x1, Pallas kernels, unpack(): pl.pallas_call(functools.partial(unpack_kernel, utts, per_step), out_shap...  11.2 us
    pallas_call x2, Pallas kernels, tap_sums(): pl.pallas_call(taps_kernel, grid=(steps,), out_shape=jax.ShapeDtypeStruct...  8.75 us
    pallas_call x1, Pallas kernels, outer(): pl.pallas_call(outer_kernel, grid=(2,), out_shape=(shape, shape), in_spec...  5.38 us
    pallas_call x1, Pallas kernels, top(): pl.pallas_call(top_kernel, grid=(utterances,), out_shape=(jax.ShapeDtypeS...  5.33 us
  transfers between devices with their start and end apart: 60, of which 33 were waited for; matrix products, arithmetic and copies ran while one was open for 3% of the time, Pallas kernels for 17%

profile of v1, /device:TPU:0, one launch (start us, length us, event | category | flops | bytes accessed | tf_op | source)
XLA Modules:
  0.0 233.7 jit_solution(17416206740108333760)
XLA Ops:
  0.6 4.0 %teachers.1 = (f32[2,256,256]{2,1,0:T(8,128)}, f32[2,256,256]{2,1,0:T(8,128)}) custom-call(s32[1]{0:T(128)} %bitcast.6.member_ref, bf16[2,4,256,256]{3,2,1,0:T(8,128)(2,1)} %logits_ref.1), custom_call_target="tpu_custom_call" | custom-call | tf_op jit(solution)/shard_map/teachers/pallas_call | solution.py:124
  4.7 2.9 %collective-permute-start = (f32[2,256,256]{2,1,0:T(8,128)}, f32[2,256,256]{2,1,0:T(8,128)S(1)}, u32[]{:S(2)}, u32[]{:S(2)}) collective-permute-start(f32[2,256,256]{2,1,0:T(8,128)} %get-tuple-element.35), channel_id=1, source_target_pairs={{0,16},{1,17},{2,18},{3,19},{4,20},{5,21},{6,22},{7,23},{8,24},{9,... | collective-permute-start | bytes 1572872 | tf_op jit(solution)/shard_map/ppermute | solution.py:53
  7.6 15.0 %forward.1 = (bf16[512,1024]{1,0:T(8,128)(2,1)}, f32[512,1024]{1,0:T(8,128)}, f32[512,1024]{1,0:T(8,128)}, f32[512,1024]{1,0:T(8,128)}, bf16[512,1024]{1,0:T(8,128)(2,1)}, /*index=5*/f32[512,1024]{1,0:T(8,128)}) custom-call(s32[2]{0:T(128)} %lengths_ref.11, bf16[512,1024]{1,0:T(8,128)(2,1)} %bitcast.56, f32[1,1024]{1,0:T(1,128)} %bitcast.63, ...), custom_call_target="tpu_custom_call" | custom-call | tf_op jit(solution)/shard_map/forward/pallas_call | solution.py:245
  24.1 5.3 %top.1 = (f32[2,1,128]{2,1,0:T(1,128)}, bf16[512,1024]{1,0:T(8,128)(2,1)}, bf16[512,256]{1,0:T(8,128)(2,1)}, bf16[512,1024]{1,0:T(8,128)(2,1)}) custom-call(s32[2]{0:T(128)} %lengths_ref.11, f32[512,1024]{1,0:T(8,128)} %get-tuple-element.33.residual_ref, f32[1,1024]{1,0:T(1,128)} %bitcast.64, bf16[1024,256]{1,0:T(8,128)(2,1)} %head_ref.3, ...), custom_call_target="tpu_custom_call" | custom-call | tf_op jit(solution)/shard_map/top/pallas_call | solution.py:309
  29.4 11.1 %inner.3 = (bf16[2,16,32,512]{3,2,1,0:T(8,128)(2,1)}, bf16[2,16,32,512]{3,2,1,0:T(8,128)(2,1)}, f32[512,512]{1,0:T(8,128)}) custom-call(s32[3]{0:T(128)} %pad_add_fusion.own_ref, s32[2]{0:T(128)} %lengths_ref.11, bf16[512,1024]{1,0:T(8,128)(2,1)} %get-tuple-element.36.dresidual_ref, bf16[1024,1024]{1,0:T(8,128)(2,1)} %out_weight_ref.5, ...), custom_call_target="tpu_custom_call" | custom-call | tf_op jit(solution)/shard_map/inner/pallas_call | solution.py:432
  40.5 11.0 %inner.2 = (bf16[2,16,32,512]{3,2,1,0:T(8,128)(2,1)}, bf16[2,16,32,512]{3,2,1,0:T(8,128)(2,1)}, f32[512,512]{1,0:T(8,128)}) custom-call(s32[3]{0:T(128)} %pad_add_fusion.own_ref, s32[2]{0:T(128)} %lengths_ref.11, bf16[512,1024]{1,0:T(8,128)(2,1)} %get-tuple-element.36.dresidual_ref, bf16[1024,1024]{1,0:T(8,128)(2,1)} %out_weight_ref.5, ...), custom_call_target="tpu_custom_call" | custom-call | tf_op jit(solution)/shard_map/inner/pallas_call | solution.py:432
  52.0 5.4 %outer.1 = (bf16[2,16,32,640]{3,2,1,0:T(8,128)(2,1)}, bf16[2,16,32,640]{3,2,1,0:T(8,128)(2,1)}) custom-call(s32[3]{0:T(128)} %pad_add_fusion.own_ref, bf16[512,1024]{1,0:T(8,128)(2,1)} %get-tuple-element.42.active_ref, bf16[512,1024]{1,0:T(8,128)(2,1)} %get-tuple-element.36.dresidual_ref, bf16[512,1024]{1,0:T(8,128)(2,1)} %get-tuple-element.43.final_ref, ...), custom_call_target="tpu_custom_call" | custom-call | tf_op jit(solution)/shard_map/outer/pallas_call | solution.py:348
  57.4 4.3 %taps.2 = f32[32,512]{1,0:T(8,128)} custom-call(s32[2]{0:T(128)} %lengths_ref.11, f32[512,1024]{1,0:T(8,128)} %get-tuple-element.32.gated_ref, f32[512,512]{1,0:T(8,128)} %get-tuple-element.40.dconv_ref), custom_call_target="tpu_custom_call" | custom-call | tf_op jit(solution)/shard_map/taps/pallas_call | solution.py:495
  61.8 4.4 %taps.3 = f32[32,512]{1,0:T(8,128)} custom-call(s32[2]{0:T(128)} %lengths_ref.11, f32[512,1024]{1,0:T(8,128)} %get-tuple-element.32.gated_ref, f32[512,512]{1,0:T(8,128)} %get-tuple-element.41.dconv_ref), custom_call_target="tpu_custom_call" | custom-call | tf_op jit(solution)/shard_map/taps/pallas_call | solution.py:495
  66.7 2.1 collective-permute-start.51
  71.3 4.5 %collective-permute-done.43 = bf16[8,32,512]{2,1,0:T(8,128)(2,1)S(1)} collective-permute-done((bf16[8,32,512]{2,1,0:T(8,128)(2,1)S(1)}, bf16[8,32,512]{2,1,0:T(8,128)(2,1)S(1)}, u32[]{:S(2)}, u32[]{:S(2)}) %collective-permute-start.43) | collective-permute-done | bytes 262176 | tf_op jit(solution)/shard_map/ppermute | solution.py:53
  76.1 2.1 collective-permute-start.44
  78.2 2.8 %collective-permute-done.25 = bf16[8,32,512]{2,1,0:T(8,128)(2,1)S(1)} collective-permute-done((bf16[8,32,512]{2,1,0:T(8,128)(2,1)S(1)}, bf16[8,32,512]{2,1,0:T(8,128)(2,1)S(1)}, u32[]{:S(2)}, u32[]{:S(2)}) %collective-permute-start.25) | collective-permute-done | bytes 262176 | tf_op jit(solution)/shard_map/ppermute | solution.py:53
  81.7 2.1 collective-permute-start.26
  96.7 2.6 %collective-permute-start.46 = (bf16[1,32,512]{2,1,0:T(8,128)(2,1)S(1)}, bf16[1,32,512]{2,1,0:T(8,128)(2,1)S(1)}, u32[]{:S(2)}, u32[]{:S(2)}) collective-permute-start(bf16[1,32,512]{2,1,0:T(8,128)(2,1)S(1)} %slice.291), channel_id=1, source_target_pairs={{0,8},{1,9},{2,10},{3,11},{4,12},{5,13},{6,14},{7,15},{8,0},{9,1},... | collective-permute-start | bytes 98312 | tf_op jit(solution)/shard_map/ppermute | solution.py:53
  99.6 2.3 %collective-permute-start.54 = (bf16[1,32,512]{2,1,0:T(8,128)(2,1)S(1)}, bf16[1,32,512]{2,1,0:T(8,128)(2,1)S(1)}, u32[]{:S(2)}, u32[]{:S(2)}) collective-permute-start(bf16[1,32,512]{2,1,0:T(8,128)(2,1)S(1)} %slice.299), channel_id=1, source_target_pairs={{0,8},{1,9},{2,10},{3,11},{4,12},{5,13},{6,14},{7,15},{8,0},{9,1},... | collective-permute-start | bytes 98312 | tf_op jit(solution)/shard_map/ppermute | solution.py:53
  102.0 2.2 collective-permute-start.28
  104.5 2.6 %collective-permute-start.36 = (bf16[1,32,512]{2,1,0:T(8,128)(2,1)S(1)}, bf16[1,32,512]{2,1,0:T(8,128)(2,1)S(1)}, u32[]{:S(2)}, u32[]{:S(2)}) collective-permute-start(bf16[1,32,512]{2,1,0:T(8,128)(2,1)S(1)} %slice.283), channel_id=1, source_target_pairs={{0,8},{1,9},{2,10},{3,11},{4,12},{5,13},{6,14},{7,15},{8,0},{9,1},... | collective-permute-start | bytes 98312 | tf_op jit(solution)/shard_map/ppermute | solution.py:53
  107.1 1.9 collective-permute-start.47
  109.6 2.4 %collective-permute-start.55 = (bf16[1,32,512]{2,1,0:T(8,128)(2,1)S(1)}, bf16[1,32,512]{2,1,0:T(8,128)(2,1)S(1)}, u32[]{:S(2)}, u32[]{:S(2)}) collective-permute-start(bf16[1,32,512]{2,1,0:T(8,128)(2,1)S(1)} %get-tuple-element.60), channel_id=1, source_target_pairs={{0,8},{1,9},{2,10},{3,11},{4,12},{5,13},{6,14},{7,15},{8,0},{9,1},... | collective-permute-start | bytes 98312 | tf_op jit(solution)/shard_map/ppermute | solution.py:53
  112.0 2.0 collective-permute-start.29
  114.5 2.6 %collective-permute-start.37 = (bf16[1,32,512]{2,1,0:T(8,128)(2,1)S(1)}, bf16[1,32,512]{2,1,0:T(8,128)(2,1)S(1)}, u32[]{:S(2)}, u32[]{:S(2)}) collective-permute-start(bf16[1,32,512]{2,1,0:T(8,128)(2,1)S(1)} %get-tuple-element.64), channel_id=1, source_target_pairs={{0,8},{1,9},{2,10},{3,11},{4,12},{5,13},{6,14},{7,15},{8,0},{9,1},... | collective-permute-start | bytes 98312 | tf_op jit(solution)/shard_map/ppermute | solution.py:53
  117.2 1.9 collective-permute-start.48
  125.8 2.5 %collective-permute-start.49 = (bf16[4,32,512]{2,1,0:T(8,128)(2,1)S(1)}, bf16[4,32,512]{2,1,0:T(8,128)(2,1)S(1)}, u32[]{:S(2)}, u32[]{:S(2)}) collective-permute-start(bf16[4,32,512]{2,1,0:T(8,128)(2,1)S(1)} %pad_maximum_fusion.14), channel_id=1, source_target_pairs={{0,2},{1,3},{2,0},{3,1},{4,6},{5,7},{6,4},{7,5},{8,10},{9,11},{10,... | collective-permute-start | bytes 393224 | tf_op jit(solution)/shard_map/ppermute | solution.py:53
  138.9 1.9 collective-permute-start.9
  140.9 2.5 %collective-permute-done.9 = bf16[2,32,640]{2,1,0:T(8,128)(2,1)S(1)} collective-permute-done((bf16[2,32,640]{2,1,0:T(8,128)(2,1)S(1)}, bf16[2,32,640]{2,1,0:T(8,128)(2,1)S(1)}, u32[]{:S(2)}, u32[]{:S(2)}) %collective-permute-start.9) | collective-permute-done | bytes 81952 | tf_op jit(solution)/shard_map/ppermute | solution.py:53
  143.4 1.9 collective-permute-start.17
  145.3 2.5 %collective-permute-done.17 = bf16[2,32,640]{2,1,0:T(8,128)(2,1)S(1)} collective-permute-done((bf16[2,32,640]{2,1,0:T(8,128)(2,1)S(1)}, bf16[2,32,640]{2,1,0:T(8,128)(2,1)S(1)}, u32[]{:S(2)}, u32[]{:S(2)}) %collective-permute-start.17) | collective-permute-done | bytes 81952 | tf_op jit(solution)/shard_map/ppermute | solution.py:53
  147.8 2.4 %collective-permute-start.10 = (bf16[1,32,640]{2,1,0:T(8,128)(2,1)S(1)}, bf16[1,32,640]{2,1,0:T(8,128)(2,1)S(1)}, u32[]{:S(2)}, u32[]{:S(2)}) collective-permute-start(bf16[1,32,640]{2,1,0:T(8,128)(2,1)S(1)} %slice.259), channel_id=1, source_target_pairs={{0,8},{1,9},{2,10},{3,11},{4,12},{5,13},{6,14},{7,15},{8,0},{9,1},... | collective-permute-start | bytes 122888 | tf_op jit(solution)/shard_map/ppermute | solution.py:53
  150.2 2.5 %collective-permute-done.10 = bf16[1,32,640]{2,1,0:T(8,128)(2,1)S(1)} collective-permute-done((bf16[1,32,640]{2,1,0:T(8,128)(2,1)S(1)}, bf16[1,32,640]{2,1,0:T(8,128)(2,1)S(1)}, u32[]{:S(2)}, u32[]{:S(2)}) %collective-permute-start.10) | collective-permute-done | bytes 40992 | tf_op jit(solution)/shard_map/ppermute | solution.py:53
  152.7 2.5 %collective-permute-start.18 = (bf16[1,32,640]{2,1,0:T(8,128)(2,1)S(1)}, bf16[1,32,640]{2,1,0:T(8,128)(2,1)S(1)}, u32[]{:S(2)}, u32[]{:S(2)}) collective-permute-start(bf16[1,32,640]{2,1,0:T(8,128)(2,1)S(1)} %slice.267), channel_id=1, source_target_pairs={{0,8},{1,9},{2,10},{3,11},{4,12},{5,13},{6,14},{7,15},{8,0},{9,1},... | collective-permute-start | bytes 122888 | tf_op jit(solution)/shard_map/ppermute | solution.py:53
  155.3 2.3 %collective-permute-done.18 = bf16[1,32,640]{2,1,0:T(8,128)(2,1)S(1)} collective-permute-done((bf16[1,32,640]{2,1,0:T(8,128)(2,1)S(1)}, bf16[1,32,640]{2,1,0:T(8,128)(2,1)S(1)}, u32[]{:S(2)}, u32[]{:S(2)}) %collective-permute-start.18) | collective-permute-done | bytes 40992 | tf_op jit(solution)/shard_map/ppermute | solution.py:53
  157.6 2.6 %collective-permute-start.11 = (bf16[1,32,640]{2,1,0:T(8,128)(2,1)S(1)}, bf16[1,32,640]{2,1,0:T(8,128)(2,1)S(1)}, u32[]{:S(2)}, u32[]{:S(2)}) collective-permute-start(bf16[1,32,640]{2,1,0:T(8,128)(2,1)S(1)} %get-tuple-element.66), channel_id=1, source_target_pairs={{0,8},{1,9},{2,10},{3,11},{4,12},{5,13},{6,14},{7,15},{8,0},{9,1},... | collective-permute-start | bytes 122888 | tf_op jit(solution)/shard_map/ppermute | solution.py:53
  160.2 2.3 collective-permute-done.11
  162.5 2.6 %collective-permute-start.19 = (bf16[1,32,640]{2,1,0:T(8,128)(2,1)S(1)}, bf16[1,32,640]{2,1,0:T(8,128)(2,1)S(1)}, u32[]{:S(2)}, u32[]{:S(2)}) collective-permute-start(bf16[1,32,640]{2,1,0:T(8,128)(2,1)S(1)} %get-tuple-element.68), channel_id=1, source_target_pairs={{0,8},{1,9},{2,10},{3,11},{4,12},{5,13},{6,14},{7,15},{8,0},{9,1},... | collective-permute-start | bytes 122888 | tf_op jit(solution)/shard_map/ppermute | solution.py:53
  165.1 2.3 collective-permute-done.19
  169.3 2.1 collective-permute-start.12
  171.7 2.1 collective-permute-done.12
  176.6 2.6 %collective-permute-done.13 = bf16[4,32,640]{2,1,0:T(8,128)(2,1)S(1)} collective-permute-done((bf16[4,32,640]{2,1,0:T(8,128)(2,1)S(1)}, bf16[4,32,640]{2,1,0:T(8,128)(2,1)S(1)}, u32[]{:S(2)}, u32[]{:S(2)}) %collective-permute-start.13) | collective-permute-done | bytes 163872 | tf_op jit(solution)/shard_map/ppermute | solution.py:53
  180.1 2.9 %collective-permute-done.21 = bf16[4,32,640]{2,1,0:T(8,128)(2,1)S(1)} collective-permute-done((bf16[4,32,640]{2,1,0:T(8,128)(2,1)S(1)}, bf16[4,32,640]{2,1,0:T(8,128)(2,1)S(1)}, u32[]{:S(2)}, u32[]{:S(2)}) %collective-permute-start.21) | collective-permute-done | bytes 163872 | tf_op jit(solution)/shard_map/ppermute | solution.py:53
  183.1 4.8 %collective-permute-done.14 = bf16[8,32,640]{2,1,0:T(8,128)(2,1)S(1)} collective-permute-done((bf16[8,32,640]{2,1,0:T(8,128)(2,1)S(1)}, bf16[8,32,640]{2,1,0:T(8,128)(2,1)S(1)}, u32[]{:S(2)}, u32[]{:S(2)}) %collective-permute-start.14) | collective-permute-done | bytes 327712 | tf_op jit(solution)/shard_map/ppermute | solution.py:53
  188.0 2.1 collective-permute-done.22
  191.3 5.4 %collective-permute-done.2 = f32[32,1024]{1,0:T(8,128)S(1)} collective-permute-done((f32[32,1024]{1,0:T(8,128)S(1)}, f32[32,1024]{1,0:T(8,128)S(1)}, u32[]{:S(2)}, u32[]{:S(2)}) %collective-permute-start.2) | collective-permute-done | bytes 131104 | tf_op jit(solution)/shard_map/ppermute | solution.py:53
  196.8 4.9 %collective-permute-done.3 = f32[32,1024]{1,0:T(8,128)S(1)} collective-permute-done((f32[32,1024]{1,0:T(8,128)S(1)}, f32[32,1024]{1,0:T(8,128)S(1)}, u32[]{:S(2)}, u32[]{:S(2)}) %collective-permute-start.3) | collective-permute-done | bytes 131104 | tf_op jit(solution)/shard_map/ppermute | solution.py:53
  201.7 2.6 %collective-permute-start.4 = (f32[32,1024]{1,0:T(8,128)S(1)}, f32[32,1024]{1,0:T(8,128)S(1)}, u32[]{:S(2)}, u32[]{:S(2)}) collective-permute-start(f32[32,1024]{1,0:T(8,128)S(1)} %add.102), channel_id=1, source_target_pairs={{0,8},{1,9},{2,10},{3,11},{4,12},{5,13},{6,14},{7,15},{8,0},{9,1},... | collective-permute-start | bytes 393224 | tf_op jit(solution)/shard_map/ppermute | solution.py:53
  204.3 4.5 %collective-permute-done.4 = f32[32,1024]{1,0:T(8,128)S(1)} collective-permute-done((f32[32,1024]{1,0:T(8,128)S(1)}, f32[32,1024]{1,0:T(8,128)S(1)}, u32[]{:S(2)}, u32[]{:S(2)}) %collective-permute-start.4) | collective-permute-done | bytes 131104 | tf_op jit(solution)/shard_map/ppermute | solution.py:53
  209.5 4.4 %collective-permute-done.5 = f32[32,1024]{1,0:T(8,128)S(1)} collective-permute-done((f32[32,1024]{1,0:T(8,128)S(1)}, f32[32,1024]{1,0:T(8,128)S(1)}, u32[]{:S(2)}, u32[]{:S(2)}) %collective-permute-start.5) | collective-permute-done | bytes 131104 | tf_op jit(solution)/shard_map/ppermute | solution.py:53
  218.8 11.2 %unpack.1 = (f32[1024,2048]{1,0:T(8,128)}, f32[1024,1024]{1,0:T(8,128)}, f32[1024,256]{1,0:T(8,128)}, f32[1024,1]{1,0:T(8,128)}, f32[1024,1]{1,0:T(8,128)}) custom-call(s32[3]{0:T(128)} %pad_add_fusion.own_ref, f32[32,1024]{1,0:T(8,128)} %copy-done.7, bf16[1024,2048]{1,0:T(8,128)(2,1)} %weight_ref.1, bf16[1024,256]{1,0:T(8,128)(2,1)} %head_ref.3, ...), custom_call_target="tpu_custom_call" | custom-call | tf_op jit(solution)/shard_map/unpack/pallas_call | solution.py:572
  (217 shorter events, 53.5 us)
Async XLA Ops:
  4.7 18.6 %collective-permute-start = (f32[2,256,256]{2,1,0:T(8,128)}, f32[2,256,256]{2,1,0:T(8,128)S(1)}, u32[]{:S(2)}, u32[]{:S(2)}) collective-permute-start(f32[2,256,256]{2,1,0:T(8,128)} %get-tuple-element.35), channel_id=1, source_target_pairs={{0,16},{1,17},{2,18},{3,19},{4,20},{5,21},{6,22},{7,23},{8,24},{9,... | collective-permute-start | bytes 1572872 | tf_op jit(solution)/shard_map/ppermute | solution.py:53
  40.5 25.7 %collective-permute-start.42 = (bf16[2,16,32,512]{3,2,1,0:T(8,128)(2,1)}, bf16[2,16,32,512]{3,2,1,0:T(8,128)(2,1)S(1)}, u32[]{:S(2)}, u32[]{:S(2)}) collective-permute-start(bf16[2,16,32,512]{3,2,1,0:T(8,128)(2,1)} %get-tuple-element.50), channel_id=1, source_target_pairs={{0,1},{1,0},{2,3},{3,2},{4,5},{5,4},{6,7},{7,6},{8,9},{9,8},{10,11... | collective-permute-start | bytes 3145736 | tf_op jit(solution)/shard_map/ppermute | solution.py:53
  51.5 17.3 %collective-permute-start.24 = (bf16[2,16,32,512]{3,2,1,0:T(8,128)(2,1)}, bf16[2,16,32,512]{3,2,1,0:T(8,128)(2,1)S(1)}, u32[]{:S(2)}, u32[]{:S(2)}) collective-permute-start(bf16[2,16,32,512]{3,2,1,0:T(8,128)(2,1)} %get-tuple-element.48), channel_id=1, source_target_pairs={{0,1},{1,0},{2,3},{3,2},{4,5},{5,4},{6,7},{7,6},{8,9},{9,8},{10,11... | collective-permute-start | bytes 3145736 | tf_op jit(solution)/shard_map/ppermute | solution.py:53
  57.4 26.4 %collective-permute-start.6 = (bf16[2,16,32,640]{3,2,1,0:T(8,128)(2,1)}, bf16[2,16,32,640]{3,2,1,0:T(8,128)(2,1)S(1)}, u32[]{:S(2)}, u32[]{:S(2)}) collective-permute-start(bf16[2,16,32,640]{3,2,1,0:T(8,128)(2,1)} %get-tuple-element.46), channel_id=1, source_target_pairs={{0,1},{1,0},{2,3},{3,2},{4,5},{5,4},{6,7},{7,6},{8,9},{9,8},{10,11... | collective-permute-start | bytes 3932168 | tf_op jit(solution)/shard_map/ppermute | solution.py:53
  66.6 9.2 %collective-permute-start.43 = (bf16[8,32,512]{2,1,0:T(8,128)(2,1)S(1)}, bf16[8,32,512]{2,1,0:T(8,128)(2,1)S(1)}, u32[]{:S(2)}, u32[]{:S(2)}) collective-permute-start(bf16[8,32,512]{2,1,0:T(8,128)(2,1)S(1)} %get-tuple-element.75), channel_id=1, source_target_pairs={{0,16},{1,17},{2,18},{3,19},{4,20},{5,21},{6,22},{7,23},{8,24},{9,... | collective-permute-start | bytes 786440 | tf_op jit(solution)/shard_map/ppermute | solution.py:53
  66.7 9.2 %collective-permute-start.51 = (bf16[8,32,512]{2,1,0:T(8,128)(2,1)S(1)}, bf16[8,32,512]{2,1,0:T(8,128)(2,1)S(1)}, u32[]{:S(2)}, u32[]{:S(2)}) collective-permute-start(bf16[8,32,512]{2,1,0:T(8,128)(2,1)S(1)} %get-tuple-element.76), channel_id=1, source_target_pairs={{0,2},{1,3},{2,0},{3,1},{4,6},{5,7},{6,4},{7,5},{8,10},{9,11},{10,... | collective-permute-start | bytes 786440 | tf_op jit(solution)/shard_map/ppermute | solution.py:53
  69.2 11.8 %collective-permute-start.25 = (bf16[8,32,512]{2,1,0:T(8,128)(2,1)S(1)}, bf16[8,32,512]{2,1,0:T(8,128)(2,1)S(1)}, u32[]{:S(2)}, u32[]{:S(2)}) collective-permute-start(bf16[8,32,512]{2,1,0:T(8,128)(2,1)S(1)} %get-tuple-element.79), channel_id=1, source_target_pairs={{0,16},{1,17},{2,18},{3,19},{4,20},{5,21},{6,22},{7,23},{8,24},{9,... | collective-permute-start | bytes 786440 | tf_op jit(solution)/shard_map/ppermute | solution.py:53
  70.8 10.8 %collective-permute-start.33 = (bf16[8,32,512]{2,1,0:T(8,128)(2,1)S(1)}, bf16[8,32,512]{2,1,0:T(8,128)(2,1)S(1)}, u32[]{:S(2)}, u32[]{:S(2)}) collective-permute-start(bf16[8,32,512]{2,1,0:T(8,128)(2,1)S(1)} %get-tuple-element.80), channel_id=1, source_target_pairs={{0,2},{1,3},{2,0},{3,1},{4,6},{5,7},{6,4},{7,5},{8,10},{9,11},{10,... | collective-permute-start | bytes 786440 | tf_op jit(solution)/shard_map/ppermute | solution.py:53
  75.8 115.3 %collective-permute-start.1 = (f32[32,1024]{1,0:T(8,128)S(1)}, f32[32,1024]{1,0:T(8,128)S(1)}, u32[]{:S(2)}, u32[]{:S(2)}) collective-permute-start(f32[32,1024]{1,0:T(8,128)S(1)} %pad_maximum_fusion.11), channel_id=1, source_target_pairs={{0,1},{1,0},{2,3},{3,2},{4,5},{5,4},{6,7},{7,6},{8,9},{9,8},{10,11... | collective-permute-start | bytes 393224 | tf_op jit(solution)/shard_map/ppermute | solution.py:53
  76.1 9.7 %collective-permute-start.44 = (bf16[4,32,512]{2,1,0:T(8,128)(2,1)S(1)}, bf16[4,32,512]{2,1,0:T(8,128)(2,1)S(1)}, u32[]{:S(2)}, u32[]{:S(2)}) collective-permute-start(bf16[4,32,512]{2,1,0:T(8,128)(2,1)S(1)} %slice.287), channel_id=1, source_target_pairs={{0,2},{1,3},{2,0},{3,1},{4,6},{5,7},{6,4},{7,5},{8,10},{9,11},{10,... | collective-permute-start | bytes 393224 | tf_op jit(solution)/shard_map/ppermute | solution.py:53
  81.0 6.1 %collective-permute-start.52 = (bf16[4,32,512]{2,1,0:T(8,128)(2,1)S(1)}, bf16[4,32,512]{2,1,0:T(8,128)(2,1)S(1)}, u32[]{:S(2)}, u32[]{:S(2)}) collective-permute-start(bf16[4,32,512]{2,1,0:T(8,128)(2,1)S(1)} %slice.295), channel_id=1, source_target_pairs={{0,16},{1,17},{2,18},{3,19},{4,20},{5,21},{6,22},{7,23},{8,24},{9,... | collective-permute-start | bytes 393224 | tf_op jit(solution)/shard_map/ppermute | solution.py:53
  81.7 5.8 %collective-permute-start.26 = (bf16[4,32,512]{2,1,0:T(8,128)(2,1)S(1)}, bf16[4,32,512]{2,1,0:T(8,128)(2,1)S(1)}, u32[]{:S(2)}, u32[]{:S(2)}) collective-permute-start(bf16[4,32,512]{2,1,0:T(8,128)(2,1)S(1)} %slice.271), channel_id=1, source_target_pairs={{0,2},{1,3},{2,0},{3,1},{4,6},{5,7},{6,4},{7,5},{8,10},{9,11},{10,... | collective-permute-start | bytes 393224 | tf_op jit(solution)/shard_map/ppermute | solution.py:53
  83.8 6.5 %collective-permute-start.34 = (bf16[4,32,512]{2,1,0:T(8,128)(2,1)S(1)}, bf16[4,32,512]{2,1,0:T(8,128)(2,1)S(1)}, u32[]{:S(2)}, u32[]{:S(2)}) collective-permute-start(bf16[4,32,512]{2,1,0:T(8,128)(2,1)S(1)} %slice.279), channel_id=1, source_target_pairs={{0,16},{1,17},{2,18},{3,19},{4,20},{5,21},{6,22},{7,23},{8,24},{9,... | collective-permute-start | bytes 393224 | tf_op jit(solution)/shard_map/ppermute | solution.py:53
  85.8 44.2 %collective-permute-start.15 = (bf16[8,32,640]{2,1,0:T(8,128)(2,1)S(1)}, bf16[8,32,640]{2,1,0:T(8,128)(2,1)S(1)}, u32[]{:S(2)}, u32[]{:S(2)}) collective-permute-start(bf16[8,32,640]{2,1,0:T(8,128)(2,1)S(1)} %get-tuple-element.72), channel_id=1, source_target_pairs={{0,2},{1,3},{2,0},{3,1},{4,6},{5,7},{6,4},{7,5},{8,10},{9,11},{10,... | collective-permute-start | bytes 983048 | tf_op jit(solution)/shard_map/ppermute | solution.py:53
  87.1 44.0 %collective-permute-start.7 = (bf16[8,32,640]{2,1,0:T(8,128)(2,1)S(1)}, bf16[8,32,640]{2,1,0:T(8,128)(2,1)S(1)}, u32[]{:S(2)}, u32[]{:S(2)}) collective-permute-start(bf16[8,32,640]{2,1,0:T(8,128)(2,1)S(1)} %get-tuple-element.71), channel_id=1, source_target_pairs={{0,16},{1,17},{2,18},{3,19},{4,20},{5,21},{6,22},{7,23},{8,24},{9,... | collective-permute-start | bytes 983048 | tf_op jit(solution)/shard_map/ppermute | solution.py:53
  96.7 5.3 %collective-permute-start.46 = (bf16[1,32,512]{2,1,0:T(8,128)(2,1)S(1)}, bf16[1,32,512]{2,1,0:T(8,128)(2,1)S(1)}, u32[]{:S(2)}, u32[]{:S(2)}) collective-permute-start(bf16[1,32,512]{2,1,0:T(8,128)(2,1)S(1)} %slice.291), channel_id=1, source_target_pairs={{0,8},{1,9},{2,10},{3,11},{4,12},{5,13},{6,14},{7,15},{8,0},{9,1},... | collective-permute-start | bytes 98312 | tf_op jit(solution)/shard_map/ppermute | solution.py:53
  99.6 4.9 %collective-permute-start.54 = (bf16[1,32,512]{2,1,0:T(8,128)(2,1)S(1)}, bf16[1,32,512]{2,1,0:T(8,128)(2,1)S(1)}, u32[]{:S(2)}, u32[]{:S(2)}) collective-permute-start(bf16[1,32,512]{2,1,0:T(8,128)(2,1)S(1)} %slice.299), channel_id=1, source_target_pairs={{0,8},{1,9},{2,10},{3,11},{4,12},{5,13},{6,14},{7,15},{8,0},{9,1},... | collective-permute-start | bytes 98312 | tf_op jit(solution)/shard_map/ppermute | solution.py:53
  102.0 5.2 %collective-permute-start.28 = (bf16[1,32,512]{2,1,0:T(8,128)(2,1)S(1)}, bf16[1,32,512]{2,1,0:T(8,128)(2,1)S(1)}, u32[]{:S(2)}, u32[]{:S(2)}) collective-permute-start(bf16[1,32,512]{2,1,0:T(8,128)(2,1)S(1)} %slice.275), channel_id=1, source_target_pairs={{0,8},{1,9},{2,10},{3,11},{4,12},{5,13},{6,14},{7,15},{8,0},{9,1},... | collective-permute-start | bytes 98312 | tf_op jit(solution)/shard_map/ppermute | solution.py:53
  104.5 5.1 %collective-permute-start.36 = (bf16[1,32,512]{2,1,0:T(8,128)(2,1)S(1)}, bf16[1,32,512]{2,1,0:T(8,128)(2,1)S(1)}, u32[]{:S(2)}, u32[]{:S(2)}) collective-permute-start(bf16[1,32,512]{2,1,0:T(8,128)(2,1)S(1)} %slice.283), channel_id=1, source_target_pairs={{0,8},{1,9},{2,10},{3,11},{4,12},{5,13},{6,14},{7,15},{8,0},{9,1},... | collective-permute-start | bytes 98312 | tf_op jit(solution)/shard_map/ppermute | solution.py:53
  107.1 4.9 %collective-permute-start.47 = (bf16[1,32,512]{2,1,0:T(8,128)(2,1)S(1)}, bf16[1,32,512]{2,1,0:T(8,128)(2,1)S(1)}, u32[]{:S(2)}, u32[]{:S(2)}) collective-permute-start(bf16[1,32,512]{2,1,0:T(8,128)(2,1)S(1)} %get-tuple-element.58), channel_id=1, source_target_pairs={{0,8},{1,9},{2,10},{3,11},{4,12},{5,13},{6,14},{7,15},{8,0},{9,1},... | collective-permute-start | bytes 98312 | tf_op jit(solution)/shard_map/ppermute | solution.py:53
  109.6 4.9 %collective-permute-start.55 = (bf16[1,32,512]{2,1,0:T(8,128)(2,1)S(1)}, bf16[1,32,512]{2,1,0:T(8,128)(2,1)S(1)}, u32[]{:S(2)}, u32[]{:S(2)}) collective-permute-start(bf16[1,32,512]{2,1,0:T(8,128)(2,1)S(1)} %get-tuple-element.60), channel_id=1, source_target_pairs={{0,8},{1,9},{2,10},{3,11},{4,12},{5,13},{6,14},{7,15},{8,0},{9,1},... | collective-permute-start | bytes 98312 | tf_op jit(solution)/shard_map/ppermute | solution.py:53
  112.0 5.1 %collective-permute-start.29 = (bf16[1,32,512]{2,1,0:T(8,128)(2,1)S(1)}, bf16[1,32,512]{2,1,0:T(8,128)(2,1)S(1)}, u32[]{:S(2)}, u32[]{:S(2)}) collective-permute-start(bf16[1,32,512]{2,1,0:T(8,128)(2,1)S(1)} %get-tuple-element.62), channel_id=1, source_target_pairs={{0,8},{1,9},{2,10},{3,11},{4,12},{5,13},{6,14},{7,15},{8,0},{9,1},... | collective-permute-start | bytes 98312 | tf_op jit(solution)/shard_map/ppermute | solution.py:53
  114.5 4.8 %collective-permute-start.37 = (bf16[1,32,512]{2,1,0:T(8,128)(2,1)S(1)}, bf16[1,32,512]{2,1,0:T(8,128)(2,1)S(1)}, u32[]{:S(2)}, u32[]{:S(2)}) collective-permute-start(bf16[1,32,512]{2,1,0:T(8,128)(2,1)S(1)} %get-tuple-element.64), channel_id=1, source_target_pairs={{0,8},{1,9},{2,10},{3,11},{4,12},{5,13},{6,14},{7,15},{8,0},{9,1},... | collective-permute-start | bytes 98312 | tf_op jit(solution)/shard_map/ppermute | solution.py:53
  125.8 6.5 %collective-permute-start.49 = (bf16[4,32,512]{2,1,0:T(8,128)(2,1)S(1)}, bf16[4,32,512]{2,1,0:T(8,128)(2,1)S(1)}, u32[]{:S(2)}, u32[]{:S(2)}) collective-permute-start(bf16[4,32,512]{2,1,0:T(8,128)(2,1)S(1)} %pad_maximum_fusion.14), channel_id=1, source_target_pairs={{0,2},{1,3},{2,0},{3,1},{4,6},{5,7},{6,4},{7,5},{8,10},{9,11},{10,... | collective-permute-start | bytes 393224 | tf_op jit(solution)/shard_map/ppermute | solution.py:53
  128.3 5.0 %collective-permute-start.57 = (bf16[4,32,512]{2,1,0:T(8,128)(2,1)S(1)}, bf16[4,32,512]{2,1,0:T(8,128)(2,1)S(1)}, u32[]{:S(2)}, u32[]{:S(2)}) collective-permute-start(bf16[4,32,512]{2,1,0:T(8,128)(2,1)S(1)} %pad_maximum_fusion.15), channel_id=1, source_target_pairs={{0,16},{1,17},{2,18},{3,19},{4,20},{5,21},{6,22},{7,23},{8,24},{9,... | collective-permute-start | bytes 393224 | tf_op jit(solution)/shard_map/ppermute | solution.py:53
  130.0 5.0 %collective-permute-start.31 = (bf16[4,32,512]{2,1,0:T(8,128)(2,1)S(1)}, bf16[4,32,512]{2,1,0:T(8,128)(2,1)S(1)}, u32[]{:S(2)}, u32[]{:S(2)}) collective-permute-start(bf16[4,32,512]{2,1,0:T(8,128)(2,1)S(1)} %pad_maximum_fusion.12), channel_id=1, source_target_pairs={{0,2},{1,3},{2,0},{3,1},{4,6},{5,7},{6,4},{7,5},{8,10},{9,11},{10,... | collective-permute-start | bytes 393224 | tf_op jit(solution)/shard_map/ppermute | solution.py:53
  131.1 5.0 %collective-permute-start.39 = (bf16[4,32,512]{2,1,0:T(8,128)(2,1)S(1)}, bf16[4,32,512]{2,1,0:T(8,128)(2,1)S(1)}, u32[]{:S(2)}, u32[]{:S(2)}) collective-permute-start(bf16[4,32,512]{2,1,0:T(8,128)(2,1)S(1)} %pad_maximum_fusion.13), channel_id=1, source_target_pairs={{0,16},{1,17},{2,18},{3,19},{4,20},{5,21},{6,22},{7,23},{8,24},{9,... | collective-permute-start | bytes 393224 | tf_op jit(solution)/shard_map/ppermute | solution.py:53
  132.2 5.4 %collective-permute-start.8 = (bf16[4,32,640]{2,1,0:T(8,128)(2,1)S(1)}, bf16[4,32,640]{2,1,0:T(8,128)(2,1)S(1)}, u32[]{:S(2)}, u32[]{:S(2)}) collective-permute-start(bf16[4,32,640]{2,1,0:T(8,128)(2,1)S(1)} %slice.255), channel_id=1, source_target_pairs={{0,2},{1,3},{2,0},{3,1},{4,6},{5,7},{6,4},{7,5},{8,10},{9,11},{10,... | collective-permute-start | bytes 491528 | tf_op jit(solution)/shard_map/ppermute | solution.py:53
  133.3 5.5 %collective-permute-start.16 = (bf16[4,32,640]{2,1,0:T(8,128)(2,1)S(1)}, bf16[4,32,640]{2,1,0:T(8,128)(2,1)S(1)}, u32[]{:S(2)}, u32[]{:S(2)}) collective-permute-start(bf16[4,32,640]{2,1,0:T(8,128)(2,1)S(1)} %slice.263), channel_id=1, source_target_pairs={{0,16},{1,17},{2,18},{3,19},{4,20},{5,21},{6,22},{7,23},{8,24},{9,... | collective-permute-start | bytes 491528 | tf_op jit(solution)/shard_map/ppermute | solution.py:53
  135.0 34.3 %collective-permute-start.50 = (bf16[8,32,512]{2,1,0:T(8,128)(2,1)S(1)}, bf16[8,32,512]{2,1,0:T(8,128)(2,1)S(1)}, u32[]{:S(2)}, u32[]{:S(2)}) collective-permute-start(bf16[8,32,512]{2,1,0:T(8,128)(2,1)S(1)} %pad_maximum_fusion.7), channel_id=1, source_target_pairs={{0,16},{1,17},{2,18},{3,19},{4,20},{5,21},{6,22},{7,23},{8,24},{9,... | collective-permute-start | bytes 786440 | tf_op jit(solution)/shard_map/ppermute | solution.py:53
  136.1 35.3 %collective-permute-start.58 = (bf16[8,32,512]{2,1,0:T(8,128)(2,1)S(1)}, bf16[8,32,512]{2,1,0:T(8,128)(2,1)S(1)}, u32[]{:S(2)}, u32[]{:S(2)}) collective-permute-start(bf16[8,32,512]{2,1,0:T(8,128)(2,1)S(1)} %pad_maximum_fusion.8), channel_id=1, source_target_pairs={{0,2},{1,3},{2,0},{3,1},{4,6},{5,7},{6,4},{7,5},{8,10},{9,11},{10,... | collective-permute-start | bytes 786440 | tf_op jit(solution)/shard_map/ppermute | solution.py:53
  137.7 34.0 %collective-permute-start.32 = (bf16[8,32,512]{2,1,0:T(8,128)(2,1)S(1)}, bf16[8,32,512]{2,1,0:T(8,128)(2,1)S(1)}, u32[]{:S(2)}, u32[]{:S(2)}) collective-permute-start(bf16[8,32,512]{2,1,0:T(8,128)(2,1)S(1)} %pad_maximum_fusion.5), channel_id=1, source_target_pairs={{0,16},{1,17},{2,18},{3,19},{4,20},{5,21},{6,22},{7,23},{8,24},{9,... | collective-permute-start | bytes 786440 | tf_op jit(solution)/shard_map/ppermute | solution.py:53
  147.8 4.9 %collective-permute-start.10 = (bf16[1,32,640]{2,1,0:T(8,128)(2,1)S(1)}, bf16[1,32,640]{2,1,0:T(8,128)(2,1)S(1)}, u32[]{:S(2)}, u32[]{:S(2)}) collective-permute-start(bf16[1,32,640]{2,1,0:T(8,128)(2,1)S(1)} %slice.259), channel_id=1, source_target_pairs={{0,8},{1,9},{2,10},{3,11},{4,12},{5,13},{6,14},{7,15},{8,0},{9,1},... | collective-permute-start | bytes 122888 | tf_op jit(solution)/shard_map/ppermute | solution.py:53
  152.7 4.9 %collective-permute-start.18 = (bf16[1,32,640]{2,1,0:T(8,128)(2,1)S(1)}, bf16[1,32,640]{2,1,0:T(8,128)(2,1)S(1)}, u32[]{:S(2)}, u32[]{:S(2)}) collective-permute-start(bf16[1,32,640]{2,1,0:T(8,128)(2,1)S(1)} %slice.267), channel_id=1, source_target_pairs={{0,8},{1,9},{2,10},{3,11},{4,12},{5,13},{6,14},{7,15},{8,0},{9,1},... | collective-permute-start | bytes 122888 | tf_op jit(solution)/shard_map/ppermute | solution.py:53
  157.6 4.9 %collective-permute-start.11 = (bf16[1,32,640]{2,1,0:T(8,128)(2,1)S(1)}, bf16[1,32,640]{2,1,0:T(8,128)(2,1)S(1)}, u32[]{:S(2)}, u32[]{:S(2)}) collective-permute-start(bf16[1,32,640]{2,1,0:T(8,128)(2,1)S(1)} %get-tuple-element.66), channel_id=1, source_target_pairs={{0,8},{1,9},{2,10},{3,11},{4,12},{5,13},{6,14},{7,15},{8,0},{9,1},... | collective-permute-start | bytes 122888 | tf_op jit(solution)/shard_map/ppermute | solution.py:53
  162.5 4.9 %collective-permute-start.19 = (bf16[1,32,640]{2,1,0:T(8,128)(2,1)S(1)}, bf16[1,32,640]{2,1,0:T(8,128)(2,1)S(1)}, u32[]{:S(2)}, u32[]{:S(2)}) collective-permute-start(bf16[1,32,640]{2,1,0:T(8,128)(2,1)S(1)} %get-tuple-element.68), channel_id=1, source_target_pairs={{0,8},{1,9},{2,10},{3,11},{4,12},{5,13},{6,14},{7,15},{8,0},{9,1},... | collective-permute-start | bytes 122888 | tf_op jit(solution)/shard_map/ppermute | solution.py:53
  167.4 23.0 %collective-permute-start.40 = (bf16[8,32,512]{2,1,0:T(8,128)(2,1)S(1)}, bf16[8,32,512]{2,1,0:T(8,128)(2,1)S(1)}, u32[]{:S(2)}, u32[]{:S(2)}) collective-permute-start(bf16[8,32,512]{2,1,0:T(8,128)(2,1)S(1)} %pad_maximum_fusion.6), channel_id=1, source_target_pairs={{0,2},{1,3},{2,0},{3,1},{4,6},{5,7},{6,4},{7,5},{8,10},{9,11},{10,... | collective-permute-start | bytes 786440 | tf_op jit(solution)/shard_map/ppermute | solution.py:53
  171.6 44.8 %collective-permute-start.59 = (bf16[2,16,32,512]{3,2,1,0:T(8,128)(2,1)S(1)}, bf16[2,16,32,512]{3,2,1,0:T(8,128)(2,1)S(1)}, u32[]{:S(2)}, u32[]{:S(2)}) collective-permute-start(bf16[2,16,32,512]{3,2,1,0:T(8,128)(2,1)S(1)} %pad_maximum_fusion.2.refs_8_.refs_9_), channel_id=1, source_target_pairs={{0,1},{1,0},{2,3},{3,2},{4,5},{5,4},{6,7},{7,6},{8,9},{9,8},{10,11... | collective-permute-start | bytes 3145736 | tf_op jit(solution)/shard_map/ppermute | solution.py:53
  173.8 5.4 %collective-permute-start.13 = (bf16[4,32,640]{2,1,0:T(8,128)(2,1)S(1)}, bf16[4,32,640]{2,1,0:T(8,128)(2,1)S(1)}, u32[]{:S(2)}, u32[]{:S(2)}) collective-permute-start(bf16[4,32,640]{2,1,0:T(8,128)(2,1)S(1)} %pad_maximum_fusion.9), channel_id=1, source_target_pairs={{0,2},{1,3},{2,0},{3,1},{4,6},{5,7},{6,4},{7,5},{8,10},{9,11},{10,... | collective-permute-start | bytes 491528 | tf_op jit(solution)/shard_map/ppermute | solution.py:53
  175.9 7.0 %collective-permute-start.21 = (bf16[4,32,640]{2,1,0:T(8,128)(2,1)S(1)}, bf16[4,32,640]{2,1,0:T(8,128)(2,1)S(1)}, u32[]{:S(2)}, u32[]{:S(2)}) collective-permute-start(bf16[4,32,640]{2,1,0:T(8,128)(2,1)S(1)} %pad_maximum_fusion.10), channel_id=1, source_target_pairs={{0,16},{1,17},{2,18},{3,19},{4,20},{5,21},{6,22},{7,23},{8,24},{9,... | collective-permute-start | bytes 491528 | tf_op jit(solution)/shard_map/ppermute | solution.py:53
  179.2 8.7 %collective-permute-start.14 = (bf16[8,32,640]{2,1,0:T(8,128)(2,1)S(1)}, bf16[8,32,640]{2,1,0:T(8,128)(2,1)S(1)}, u32[]{:S(2)}, u32[]{:S(2)}) collective-permute-start(bf16[8,32,640]{2,1,0:T(8,128)(2,1)S(1)} %pad_maximum_fusion.3), channel_id=1, source_target_pairs={{0,16},{1,17},{2,18},{3,19},{4,20},{5,21},{6,22},{7,23},{8,24},{9,... | collective-permute-start | bytes 983048 | tf_op jit(solution)/shard_map/ppermute | solution.py:53
  183.0 7.1 %collective-permute-start.22 = (bf16[8,32,640]{2,1,0:T(8,128)(2,1)S(1)}, bf16[8,32,640]{2,1,0:T(8,128)(2,1)S(1)}, u32[]{:S(2)}, u32[]{:S(2)}) collective-permute-start(bf16[8,32,640]{2,1,0:T(8,128)(2,1)S(1)} %pad_maximum_fusion.4), channel_id=1, source_target_pairs={{0,2},{1,3},{2,0},{3,1},{4,6},{5,7},{6,4},{7,5},{8,10},{9,11},{10,... | collective-permute-start | bytes 983048 | tf_op jit(solution)/shard_map/ppermute | solution.py:53
  190.4 26.1 %collective-permute-start.23 = (bf16[2,16,32,640]{3,2,1,0:T(8,128)(2,1)S(1)}, bf16[2,16,32,640]{3,2,1,0:T(8,128)(2,1)S(1)}, u32[]{:S(2)}, u32[]{:S(2)}) collective-permute-start(bf16[2,16,32,640]{3,2,1,0:T(8,128)(2,1)S(1)} %pad_maximum_fusion.refs_0_.refs_1_), channel_id=1, source_target_pairs={{0,1},{1,0},{2,3},{3,2},{4,5},{5,4},{6,7},{7,6},{8,9},{9,8},{10,11... | collective-permute-start | bytes 3932168 | tf_op jit(solution)/shard_map/ppermute | solution.py:53
  190.6 25.8 %collective-permute-start.41 = (bf16[2,16,32,512]{3,2,1,0:T(8,128)(2,1)S(1)}, bf16[2,16,32,512]{3,2,1,0:T(8,128)(2,1)S(1)}, u32[]{:S(2)}, u32[]{:S(2)}) collective-permute-start(bf16[2,16,32,512]{3,2,1,0:T(8,128)(2,1)S(1)} %pad_maximum_fusion.1.refs_4_.refs_5_), channel_id=1, source_target_pairs={{0,1},{1,0},{2,3},{3,2},{4,5},{5,4},{6,7},{7,6},{8,9},{9,8},{10,11... | collective-permute-start | bytes 3145736 | tf_op jit(solution)/shard_map/ppermute | solution.py:53
  191.2 5.5 %collective-permute-start.2 = (f32[32,1024]{1,0:T(8,128)S(1)}, f32[32,1024]{1,0:T(8,128)S(1)}, u32[]{:S(2)}, u32[]{:S(2)}) collective-permute-start(f32[32,1024]{1,0:T(8,128)S(1)} %fusion.6), channel_id=1, source_target_pairs={{0,2},{1,3},{2,0},{3,1},{4,6},{5,7},{6,4},{7,5},{8,10},{9,11},{10,... | collective-permute-start | bytes 393224 | tf_op jit(solution)/shard_map/ppermute | solution.py:53
  196.7 5.0 %collective-permute-start.3 = (f32[32,1024]{1,0:T(8,128)S(1)}, f32[32,1024]{1,0:T(8,128)S(1)}, u32[]{:S(2)}, u32[]{:S(2)}) collective-permute-start(f32[32,1024]{1,0:T(8,128)S(1)} %add.101), channel_id=1, source_target_pairs={{0,4},{1,5},{2,6},{3,7},{4,0},{5,1},{6,2},{7,3},{8,12},{9,13},{10,... | collective-permute-start | bytes 393224 | tf_op jit(solution)/shard_map/ppermute | solution.py:53
  201.7 7.1 %collective-permute-start.4 = (f32[32,1024]{1,0:T(8,128)S(1)}, f32[32,1024]{1,0:T(8,128)S(1)}, u32[]{:S(2)}, u32[]{:S(2)}) collective-permute-start(f32[32,1024]{1,0:T(8,128)S(1)} %add.102), channel_id=1, source_target_pairs={{0,8},{1,9},{2,10},{3,11},{4,12},{5,13},{6,14},{7,15},{8,0},{9,1},... | collective-permute-start | bytes 393224 | tf_op jit(solution)/shard_map/ppermute | solution.py:53
  208.8 5.0 %collective-permute-start.5 = (f32[32,1024]{1,0:T(8,128)S(1)}, f32[32,1024]{1,0:T(8,128)S(1)}, u32[]{:S(2)}, u32[]{:S(2)}) collective-permute-start(f32[32,1024]{1,0:T(8,128)S(1)} %add.103), channel_id=1, source_target_pairs={{0,16},{1,17},{2,18},{3,19},{4,20},{5,21},{6,22},{7,23},{8,24},{9,... | collective-permute-start | bytes 393224 | tf_op jit(solution)/shard_map/ppermute | solution.py:53
  (28 other events, 205.9 us)

commit v2 on v1

--- a/solution.py
+++ b/solution.py
@@ -8,9 +8,7 @@
 from jax.sharding import PartitionSpec as P
 
 TEACHERS = 4
-AXES = ("member", "dp")
-PLACE_BITS = 4
-PLACES = 1 << PLACE_BITS
+PLACES = 16
 WIDE = 256
 LANES = 128
 TILE = 128
@@ -36,62 +34,66 @@
     return pl.BlockSpec(shape, lambda i, *_: (0,) * len(shape))
 
 
-def bit_orders(count):
-    top = count.bit_length() - 2
-    middle = list(range(2, top))
-    return [top, 1] + middle, [1, top] + middle
-
-
-def place_of(device, order):
-    own = jnp.int32(0)
-    for index, bit in enumerate(order[:PLACE_BITS]):
-        own = own | (((device >> bit) & 1) << (PLACE_BITS - 1 - index))
-    return own
-
-
-def swap(values, bit, count):
-    return lax.ppermute(values, AXES, [(i, i ^ (1 << bit)) for i in range(count)])
-
-
-def add_pair(own, other):
-    return (own.astype(F32) + other.astype(F32)).astype(own.dtype)
-
-
-def sum_pieces(send, keep, orders, count):
-    both = add_pair(keep, swap(send, 0, count))
-    parts = [both[0], both[1]]
-    for index in range(len(orders[0])):
-        received = []
-        for part, order in zip(parts, orders):
-            half = part.shape[0] // 2 if index < PLACE_BITS else 0
-            received.append(swap(part[half:], order[index], count))
-        for group, other in enumerate(received):
-            parts[group] = add_pair(parts[group][: other.shape[0]], other)
-    for index in reversed(range(PLACE_BITS)):
-        received = [swap(part, order[index], count) for part, order in zip(parts, orders)]
-        parts = [jnp.concatenate([part, other], axis=0) for part, other in zip(parts, received)]
-    own = jnp.stack(parts)
-    return own, swap(own, 0, count)
-
-
-def all_sum(values, count):
-    for bit in range(count.bit_length() - 1):
-        values = values + swap(values, bit, count)
-    return values
-
-
-def write_pieces(place, core, product, send_ref, keep_ref, lead, columns):
+NEAR = ("member", "near")
+FAR = "far"
+REST = "rest"
+CORE = "core"
+
+
+def other_core(values):
+    return lax.ppermute(values, CORE, [(0, 1), (1, 0)])
+
+
+def sum_core(send, keep):
+    return (keep.astype(F32) + other_core(send).astype(F32)).astype(BF16)
+
+
+def sum_over(values, axis):
+    got = lax.all_to_all(values, axis, 0, 0)
+    return jnp.sum(got.astype(F32), axis=0).astype(values.dtype)
+
+
+def gather_over(values, axis):
+    return lax.all_to_all(
+        jnp.broadcast_to(values[None], (lax.axis_size(axis),) + values.shape), axis, 0, 0
+    )
+
+
+def sum_near(pieces):
+    near = lax.axis_size(NEAR)
+    return sum_over(pieces.reshape((near, pieces.shape[0] // near) + pieces.shape[1:]), NEAR)
+
+
+def sum_far(pieces):
+    own = sum_over(pieces, FAR)
+    return lax.psum(own, REST) if lax.axis_size(REST) > 1 else own
+
+
+def gather_near(pieces):
+    got = gather_over(pieces, NEAR)
+    return got.reshape((got.shape[0] * got.shape[1],) + got.shape[2:])
+
+
+def all_sum(values):
+    for axis in (NEAR, FAR):
+        values = jnp.sum(gather_over(values, axis), axis=0)
+    if lax.axis_size(REST) > 1:
+        values = lax.psum(values, REST)
+    return values + other_core(values)
+
+
+def write_pieces(core, product, send_ref, keep_ref, columns):
     rows = keep_ref.shape[-2]
 
     def one(piece, carry):
-        base = (piece ^ place) * (2 * rows)
+        base = piece * (2 * rows)
         kept = pl.multiple_of(base + core * rows, rows)
         sent = pl.multiple_of(base + (1 - core) * rows, rows)
-        keep_ref[lead, piece, :, columns] = product[pl.ds(kept, rows), :].astype(BF16)
-        send_ref[lead, piece, :, columns] = product[pl.ds(sent, rows), :].astype(BF16)
+        keep_ref[piece, :, columns] = product[pl.ds(kept, rows), :].astype(BF16)
+        send_ref[piece, :, columns] = product[pl.ds(sent, rows), :].astype(BF16)
         return carry
 
-    lax.fori_loop(0, PLACES, one, 0)
+    lax.fori_loop(0, keep_ref.shape[0], one, 0)
 
 
 def teacher_kernel(member_ref, logits_ref, give_ref, keep_ref, *, own_count):
@@ -328,23 +330,22 @@
 
 
 def outer_kernel(
-    own_ref, active_ref, dresidual_ref, final_ref, dlogits_ref, send_ref, keep_ref, product_ref
+    core_ref, active_ref, dresidual_ref, final_ref, dlogits_ref, send_ref, keep_ref, product_ref
 ):
-    group = pl.program_id(0)
     width = dresidual_ref.shape[1]
     product_ref[:, :width] = dot(active_ref[...], dresidual_ref[...], 0, 0)
     product_ref[:, width:] = dot(final_ref[...], dlogits_ref[...], 0, 0)
-    write_pieces(own_ref[group], own_ref[2], product_ref, send_ref, keep_ref, 0, slice(None))
-
-
-def outer(own, active, dresidual, final, dlogits):
+    write_pieces(core_ref[0], product_ref, send_ref, keep_ref, slice(None))
+
+
+def outer(core, active, dresidual, final, dlogits):
     rows, model = active.shape
     half_out = dresidual.shape[1] // 2
     half_head = dlogits.shape[1] // 2
     width = half_out + half_head
-    piece = (PLACES, model // (2 * PLACES), width)
-    shape = jax.ShapeDtypeStruct((2,) + piece, BF16)
-    out = pl.BlockSpec((1,) + piece, lambda i: (i, 0, 0, 0))
+    piece = (PLACES, model // (2 * PLACES))
+    shape = jax.ShapeDtypeStruct(piece + (2 * width,), BF16)
+    out = pl.BlockSpec(piece + (width,), lambda i: (0, 0, i))
     return pl.pallas_call(
         outer_kernel,
         grid=(2,),
@@ -360,11 +361,11 @@
         scratch_shapes=[pltpu.VMEM((model, width), F32)],
         compiler_params=params(),
         name="outer",
-    )(own, active, dresidual, final, dlogits)
+    )(core, active, dresidual, final, dlogits)
 
 
 def inner_kernel(
-    own_ref,
+    core_ref,
     lengths_ref,
     dresidual_ref,
     out_weight_ref,
@@ -417,18 +418,19 @@
 
     for group, source in ((0, dvalue_ref), (1, dgate_ref)):
         product_ref[...] = dot(normed_ref[...], source[...], 0, 0)
-        write_pieces(own_ref[group], own_ref[2], product_ref, send_ref, keep_ref, group, slice(None))
-
-
-def inner(own, lengths, dresidual, weight_out, slope, gated, gate, normed, depth, chunk, utterances):
+        columns = slice(group * WIDE, (group + 1) * WIDE)
+        write_pieces(core_ref[0], product_ref, send_ref, keep_ref, columns)
+
+
+def inner(core, lengths, dresidual, weight_out, slope, gated, gate, normed, depth, chunk, utterances):
     rows, model = normed.shape
     frames = rows // utterances
     steps = model // WIDE // CHUNKS
     first = chunk * steps
     column = pl.BlockSpec((rows, WIDE), lambda i: (0, first + i))
-    piece = (2, PLACES, model // (2 * PLACES))
-    shape = jax.ShapeDtypeStruct(piece + (steps * WIDE,), BF16)
-    out = pl.BlockSpec(piece + (WIDE,), lambda i: (0, 0, 0, i))
+    piece = (PLACES, model // (2 * PLACES))
+    shape = jax.ShapeDtypeStruct(piece + (steps * 2 * WIDE,), BF16)
+    out = pl.BlockSpec(piece + (2 * WIDE,), lambda i: (0, 0, i))
     return pl.pallas_call(
         inner_kernel,
         grid=(steps,),
@@ -453,7 +455,7 @@
         ],
         compiler_params=params(),
         name="inner",
-    )(own, lengths, dresidual, weight_out, slope, gated, gate, normed, depth)
+    )(core, lengths, dresidual, weight_out, slope, gated, gate, normed, depth)
 
 
 def taps_kernel(lengths_ref, gated_ref, dconv_ref, out_ref, pad_ref, sums_ref):
@@ -511,76 +513,133 @@
     )(lengths, gated, dconv)
 
 
-def unpack_kernel(utts, per_step, own_ref, small_ref, weight_ref, head_ref, *refs):
-    arrays = (len(refs) - 5) // 4
-    pieces, (win_ref, wout_ref, dhead_ref, gain_in_ref, gain_out_ref) = refs[:-5], refs[-5:]
+def gain_row(weight, grad, gain):
+    along = jnp.sum(weight.astype(F32) * grad, axis=1, keepdims=True)
+    return jnp.broadcast_to(along, (along.shape[0], LANES)).T[0:1, :] / gain
+
+
+def write_rows(core, pieces, other, scale, targets):
+    rows = pieces.shape[1]
+    for index in range(pieces.shape[0]):
+        for side, source in ((core, pieces), (1 - core, other)):
+            here = pl.ds(pl.multiple_of(index * 2 * rows + side * rows, rows), rows)
+            for target, there, first, width in targets:
+                target[here, there : there + width] = (
+                    source[index, :, first : first + width].astype(F32) * scale
+                )
+
+
+def unpack_top_kernel(
+    utts,
+    core_ref,
+    small_ref,
+    own_ref,
+    other_ref,
+    head_ref,
+    gain_ref,
+    losses_ref,
+    wout_ref,
+    dhead_ref,
+    dgain_ref,
+    depth_ref,
+    loss_ref,
+):
+    taps = depth_ref.shape[0]
+    scale = utts / small_ref[taps:, 0:1]
+    half_out = wout_ref.shape[1] // 2
+    half_head = dhead_ref.shape[1] // 2
+    targets = []
+    for half in range(2):
+        first = half * (half_out + half_head)
+        targets.append((wout_ref, half * half_out, first, half_out))
+        targets.append((dhead_ref, half * half_head, first + half_out, half_head))
+    write_rows(core_ref[0], own_ref, other_ref, scale, targets)
+    dgain_ref[...] = gain_row(head_ref[...], dhead_ref[...], gain_ref[...])
+    depth_ref[...] = small_ref[:taps, :] * scale
+    loss_ref[...] = losses_ref[...] * scale[None]
+
+
+def unpack_inner_kernel(utts, core_ref, small_ref, weight_ref, gain_ref, *refs):
+    pieces, (win_ref, dgain_ref) = refs[:-2], refs[-2:]
     scale = utts / small_ref[small_ref.shape[0] - 1 :, 0:1]
-    core = own_ref[2]
-    rows = pieces[0].shape[2]
-    half_out = wout_ref.shape[1] // 2
     half_in = win_ref.shape[1] // 2
-    half_head = dhead_ref.shape[1] // 2
-    for index in range(per_step):
-        for group in range(2):
-            piece = index ^ (own_ref[group] & (per_step - 1))
-            for whose in range(2):
-                side = core if whose == 0 else 1 - core
-                here = pl.ds(pl.multiple_of(index * 2 * rows + side * rows, rows), rows)
-                for array in range(arrays):
-                    source = pieces[(array * 2 + whose) * 2 + group]
-                    wide = source[0, piece].astype(F32) * scale
-                    if array == 0:
-                        wout_ref[here, group * half_out : (group + 1) * half_out] = wide[:, :half_out]
-                        dhead_ref[here, group * half_head : (group + 1) * half_head] = wide[
-                            :, half_out:
-                        ]
-                    else:
-                        width = wide.shape[1]
-                        first = group * half_in + (array - 1) * width
-                        win_ref[here, first : first + width] = wide
-    gain_in_ref[...] = jnp.sum(weight_ref[...].astype(F32) * win_ref[...], axis=1, keepdims=True)
-    gain_out_ref[...] = jnp.sum(head_ref[...].astype(F32) * dhead_ref[...], axis=1, keepdims=True)
-
-
-def unpack(utts, own, small, weight_in, head, sums, width_out):
+    column = 0
+    for chunk in range(len(pieces) // 2):
+        own_ref, other_ref = pieces[2 * chunk : 2 * chunk + 2]
+        targets = []
+        for first in range(0, own_ref.shape[2], 2 * WIDE):
+            targets.append((win_ref, column, first, WIDE))
+            targets.append((win_ref, half_in + column, first + WIDE, WIDE))
+            column += WIDE
+        write_rows(core_ref[0], own_ref, other_ref, scale, targets)
+    dgain_ref[...] = gain_row(weight_ref[...], win_ref[...], gain_ref[...])
+
+
+def piece_spec(array, steps):
+    return pl.BlockSpec((array.shape[0] // steps,) + array.shape[1:], lambda i: (i, 0, 0))
+
+
+def unpack_top(utts, core, small, own, other, head, gain, losses, width_out):
     steps = 4
-    per_step = PLACES // steps
-    model = head.shape[0]
+    model, symbols = head.shape
     rows = model // steps
-    widths = (weight_in.shape[1], width_out, head.shape[1], 1, 1)
-    operands = []
-    specs = []
-    for pair in sums:
-        for array in pair:
-            for group in range(2):
-                operands.append(array)
-                specs.append(
-                    pl.BlockSpec(
-                        (1, per_step) + array.shape[2:],
-                        lambda i, own_ref, group=group: (
-                            group,
-                            i ^ (own_ref[group] // per_step),
-                            0,
-                            0,
-                        ),
-                    )
-                )
+    taps = small.shape[0] - 1
+    row = pl.BlockSpec((1, rows), lambda i: (0, i))
 
     def block(width):
-        return pl.BlockSpec((rows, width), lambda i, own_ref: (i, 0))
+        return pl.BlockSpec((rows, width), lambda i: (i, 0))
 
     return pl.pallas_call(
-        functools.partial(unpack_kernel, utts, per_step),
-        out_shape=tuple(jax.ShapeDtypeStruct((model, width), F32) for width in widths),
-        grid_spec=pltpu.PrefetchScalarGridSpec(
-            num_scalar_prefetch=1,
-            grid=(steps,),
-            in_specs=[fixed(*small.shape), block(weight_in.shape[1]), block(head.shape[1])] + specs,
-            out_specs=tuple(block(width) for width in widths),
+        functools.partial(unpack_top_kernel, utts),
+        grid=(steps,),
+        out_shape=(
+            jax.ShapeDtypeStruct((model, width_out), F32),
+            jax.ShapeDtypeStruct((model, symbols), F32),
+            jax.ShapeDtypeStruct((1, model), F32),
+            jax.ShapeDtypeStruct((taps, model), F32),
+            jax.ShapeDtypeStruct(losses.shape, F32),
+        ),
+        in_specs=[
+            SMEM_SPEC,
+            fixed(*small.shape),
+            piece_spec(own, steps),
+            piece_spec(other, steps),
+            block(symbols),
+            row,
+            fixed(*losses.shape),
+        ],
+        out_specs=(
+            block(width_out),
+            block(symbols),
+            row,
+            fixed(taps, model),
+            fixed(*losses.shape),
         ),
         compiler_params=params(),
-        name="unpack",
-    )(own, small, weight_in, head, *operands)
+        name="unpack_top",
+    )(core, small, own, other, head, gain, losses)
+
+
+def unpack_inner(utts, core, small, sums, weight, gain):
+    steps = 8
+    model, width = weight.shape
+    rows = model // steps
+    row = pl.BlockSpec((1, rows), lambda i: (0, i))
+    block = pl.BlockSpec((rows, width), lambda i: (i, 0))
+    pieces = [array for pair in sums for array in pair]
+    return pl.pallas_call(
+        functools.partial(unpack_inner_kernel, utts),
+        grid=(steps,),
+        out_shape=(
+            jax.ShapeDtypeStruct((model, width), F32),
+            jax.ShapeDtypeStruct((1, model), F32),
+        ),
+        in_specs=[SMEM_SPEC, fixed(*small.shape), block, row]
+        + [piece_spec(array, steps) for array in pieces],
+        out_specs=(block, row),
+        compiler_params=params(),
+        name="unpack_inner",
+    )(core, small, weight, gain, *pieces)
 
 
 def on_device(
@@ -594,17 +653,16 @@
     gain_out,
     head_weight,
 ):
-    count = lax.axis_size("member") * lax.axis_size("dp")
-    member = lax.axis_index("member").astype(jnp.int32)
-    device = member * lax.axis_size("dp") + lax.axis_index("dp")
-    orders = bit_orders(count)
-    own = jnp.stack([place_of(device, order) for order in orders] + [device & 1]).astype(jnp.int32)
+    count = lax.axis_size(NEAR) * lax.axis_size(FAR) * lax.axis_size(REST) * lax.axis_size(CORE)
+    member = lax.axis_index("member").astype(jnp.int32)[None]
+    core = lax.axis_index(CORE).astype(jnp.int32)[None]
     taps, model = weight_depth.shape
     utterances, frames, _ = features.shape
     utts = float(utterances * count)
-
-    give, kept = teacher_sums(member[None], teacher_logits, utterances)
-    got = swap(give, count.bit_length() - 2, count)
+    tie = lax.optimization_barrier
+
+    give, kept = teacher_sums(member, teacher_logits, utterances)
+    got = lax.ppermute(give, "member", [(0, 1), (1, 0)])
     flat = features.reshape(utterances * frames, model)
     normed, gated, gate, slope, active, residual = forward(
         lengths, flat, gain_conv[None], weight_in, weight_depth, weight_out, utterances
@@ -612,11 +670,10 @@
     losses, final, dlogits, dresidual = top(
         lengths, residual, gain_out[None], head_weight, kept, got
     )
-    sums = [sum_pieces(*outer(own, active, dresidual, final, dlogits), orders, count)]
-    dconvs = []
-    for chunk in range(CHUNKS):
-        send, keep, dconv = inner(
-            own,
+
+    def weight_in_chunk(chunk, dresidual):
+        return inner(
+            core,
             lengths,
             dresidual,
             weight_out,
@@ -628,8 +685,19 @@
             chunk,
             utterances,
         )
+
+    send, keep = outer(core, active, dresidual, final, dlogits)
+    send, keep, dresidual = tie((send, keep, dresidual))
+    top_sum = sum_core(send, keep)
+    inner_sums = []
+    dconvs = []
+    for chunk in range(CHUNKS):
+        send, keep, dconv = weight_in_chunk(chunk, dresidual)
+        inner_sums.append(sum_core(send, keep))
         dconvs.append(dconv)
-        sums.append(sum_pieces(send, keep, orders, count))
+        if chunk == 0:
+            top_sum, dresidual = tie((top_sum, dresidual))
+    dconvs[0], inner_sums[0] = tie((dconvs[0], inner_sums[0]))
     small = jnp.concatenate(
         [
             tap_sums(lengths, gated, dconv, taps, chunk, utterances)
@@ -637,27 +705,50 @@
         ],
         axis=1,
     )
-    small = all_sum(small, count)
-    grad_in, grad_out, grad_head, by_in, by_head = unpack(
-        utts, own, small, weight_in, head_weight, sums, weight_out.shape[1]
-    )
-    scale = utts / small[taps, 0]
+    top_all = gather_near(gather_over(sum_far(sum_near(top_sum)), FAR))
+    top_other = other_core(top_all)
+    small = all_sum(small)
+    pairs = []
+    for values in inner_sums:
+        every = gather_near(gather_over(sum_far(sum_near(values)), FAR))
+        pairs.append((every, other_core(every)))
+    grad_out, grad_head, by_head, grad_depth, losses = unpack_top(
+        utts,
+        core,
+        small,
+        top_all,
+        top_other,
+        head_weight,
+        gain_out[None],
+        losses,
+        weight_out.shape[1],
+    )
+    grad_in, by_in = unpack_inner(utts, core, small, pairs, weight_in, gain_conv[None])
     return (
-        by_in.reshape(model) / gain_conv,
+        by_in.reshape(model),
         grad_in,
-        small[:taps] * scale,
+        grad_depth,
         grad_out,
-        by_head.reshape(model) / gain_out,
+        by_head.reshape(model),
         grad_head,
-        losses[:, 0, 0] * scale,
+        losses[:, 0, 0],
     )
 
 
 def solution(mesh):
+    members, others = mesh.devices.shape
+    near, cores = 2, 2
+    far = PLACES // (members * near)
+    rest = others // (far * near * cores)
+    split = jax.sharding.Mesh(
+        mesh.devices.reshape(members, rest, far, near, cores),
+        ("member", REST, FAR, "near", CORE),
+    )
+    dp = (REST, FAR, "near", CORE)
     in_specs = (
-        P(("dp", "member"), None, None),
-        P("member", "dp", None, None),
-        P(("dp", "member")),
+        P(dp + ("member",), None, None),
+        P("member", dp, None, None),
+        P(dp + ("member",)),
         P(),
         P(),
         P(),
@@ -665,7 +756,7 @@
         P(),
         P(),
     )
-    out_specs = (P(), P(), P(), P(), P(), P(), P(("dp", "member")))
+    out_specs = (P(), P(), P(), P(), P(), P(), P(dp + ("member",)))
     return jax.shard_map(
-        on_device, mesh=mesh, in_specs=in_specs, out_specs=out_specs, check_vma=False
-    )
+        on_device, mesh=split, in_specs=in_specs, out_specs=out_specs, check_vma=False
+    )

time: 234 us -> 280 us (1.20)
  blocking collectives: 0 us -> 77.8 us
  starting transfers between devices: 82.1 us -> 44 us
  waiting for transfers between devices: 64.9 us -> 60 us
  other arithmetic: 8.39 us -> 12.7 us
  local copies, waits for them, and re-layouts: 4.31 us -> 8.05 us
  Pallas kernels: 71.8 us -> 75.4 us
    ppermute x60 -> x8, starting transfers between devices: 82.1 us -> 4.23 us  [the longest x1 2.94 us: on_device(): got = lax.ppermute(give, 'member', [(0, 1), (1, 0)])]
    all_to_all x0 -> x5, blocking collectives: none -> 77.8 us  [the longest x3 50.2 us: gather_over(): lax.all_to_all(jnp.broadcast_to(values[None], (lax.axis_size(axis),) + va...]
    ppermute x60 -> x8, waiting for transfers between devices: 64.9 us -> 4.47 us  [the longest x7 4.47 us: other_core(): return lax.ppermute(values, CORE, [(0, 1), (1, 0)])]
    all_to_all x0 -> x9, waiting for transfers between devices: none -> 55.5 us  [the longest x5 33.8 us: gather_over(): lax.all_to_all(jnp.broadcast_to(values[None], (lax.axis_size(axis),) + va...]
    all_to_all x0 -> x9, starting transfers between devices: none -> 39.8 us  [the longest x5 22.5 us: gather_over(): lax.all_to_all(jnp.broadcast_to(values[None], (lax.axis_size(axis),) + va...]
    broadcast_in_dim x0 -> x8, local copies, waits for them, and re-layouts: none -> 5.9 us  [gather_over(): jnp.broadcast_to(values[None], (lax.axis_size(axis),) + values.shape)]
    reduce_sum x0 -> x8, other arithmetic: none -> 5.45 us  [the longest x6 3.29 us: sum_over(): return jnp.sum(got.astype(F32), axis=0).astype(values.dtype)]
    convert_element_type x18 -> x3, other arithmetic: 1.89 us -> 5.77 us  [sum_core(): return (keep.astype(F32) + other_core(send).astype(F32)).astype(BF16)]
  transfers between devices with their start and end apart: 60 -> 17, of which waited for: 33 -> 11; matrix products, arithmetic and copies ran while one was open for 3% -> 5% of each run, Pallas kernels for 17% -> 14%
where the time goes in v2:
time: 280 us; the launch traced here: 279 us
  blocking collectives  77.8 us (28%)
  Pallas kernels  75.4 us (27%)
  waiting for transfers between devices  60 us (21%)
  starting transfers between devices  44 us (16%)
  other arithmetic  12.7 us (5%)
  local copies, waits for them, and re-layouts  8.05 us (3%)
    all_to_all x3, blocking collectives, gather_over(): lax.all_to_all(jnp.broadcast_to(values[None], (lax.axis_size(axis),) + va...  50.2 us
    all_to_all x5, waiting for transfers between devices, gather_over(): lax.all_to_all(jnp.broadcast_to(values[None], (lax.axis_size(axis),) + va...  33.8 us
    all_to_all x2, blocking collectives, sum_over(): got = lax.all_to_all(values, axis, 0, 0)  27.6 us
    all_to_all x5, starting transfers between devices, gather_over(): lax.all_to_all(jnp.broadcast_to(values[None], (lax.axis_size(axis),) + va...  22.5 us
    pallas_call x2, Pallas kernels, inner(): pl.pallas_call(inner_kernel, grid=(steps,), out_shape=(shape, shape, jax....  22.1 us
    all_to_all x4, waiting for transfers between devices, sum_over(): got = lax.all_to_all(values, axis, 0, 0)  21.6 us
    all_to_all x4, starting transfers between devices, sum_over(): got = lax.all_to_all(values, axis, 0, 0)  17.3 us
    pallas_call x1, Pallas kernels, forward(): pl.pallas_call(forward_kernel, grid=(steps,), out_shape=(narrow, wide, wi...  15 us
  transfers between devices with their start and end apart: 17, of which 11 were waited for; matrix products, arithmetic and copies ran while one was open for 5% of the time, Pallas kernels for 14%

profile of v2, /device:TPU:0, one launch (start us, length us, event | category | flops | bytes accessed | tf_op | source)
XLA Modules:
  0.0 278.8 jit_solution(17797091802698047139)
XLA Ops:
  0.6 4.0 %teachers.1 = (f32[2,256,256]{2,1,0:T(8,128)}, f32[2,256,256]{2,1,0:T(8,128)}) custom-call(s32[1]{0:T(128)} %bitcast.4.member_ref, bf16[2,4,256,256]{3,2,1,0:T(8,128)(2,1)} %logits_ref.1), custom_call_target="tpu_custom_call" | custom-call | tf_op jit(solution)/shard_map/teachers/pallas_call | solution.py:126
  4.6 2.9 %collective-permute-start = (f32[2,256,256]{2,1,0:T(8,128)}, f32[2,256,256]{2,1,0:T(8,128)S(1)}, u32[]{:S(2)}, u32[]{:S(2)}) collective-permute-start(f32[2,256,256]{2,1,0:T(8,128)} %get-tuple-element.45), channel_id=1, source_target_pairs={{0,16},{16,0},{1,17},{17,1},{2,18},{18,2},{3,19},{19,3},{4,20},{20... | collective-permute-start | bytes 1572872 | tf_op jit(solution)/shard_map/ppermute | solution.py:665
  7.6 15.0 %forward.1 = (bf16[512,1024]{1,0:T(8,128)(2,1)}, f32[512,1024]{1,0:T(8,128)}, f32[512,1024]{1,0:T(8,128)}, f32[512,1024]{1,0:T(8,128)}, bf16[512,1024]{1,0:T(8,128)(2,1)}, /*index=5*/f32[512,1024]{1,0:T(8,128)}) custom-call(s32[2]{0:T(128)} %lengths_ref.11, bf16[512,1024]{1,0:T(8,128)(2,1)} %bitcast.20, f32[1,1024]{1,0:T(1,128)} %bitcast.23, ...), custom_call_target="tpu_custom_call" | custom-call | tf_op jit(solution)/shard_map/forward/pallas_call | solution.py:247
  23.4 5.3 %top.1 = (f32[2,1,128]{2,1,0:T(1,128)}, bf16[512,1024]{1,0:T(8,128)(2,1)}, bf16[512,256]{1,0:T(8,128)(2,1)}, bf16[512,1024]{1,0:T(8,128)(2,1)}) custom-call(s32[2]{0:T(128)} %lengths_ref.11, f32[512,1024]{1,0:T(8,128)} %get-tuple-element.43.residual_ref, f32[1,1024]{1,0:T(1,128)} %bitcast.21, bf16[1024,256]{1,0:T(8,128)(2,1)} %head_ref.3, ...), custom_call_target="tpu_custom_call" | custom-call | tf_op jit(solution)/shard_map/top/pallas_call | solution.py:311
  28.7 5.4 %outer.1 = (bf16[16,32,1280]{2,1,0:T(8,128)(2,1)}, bf16[16,32,1280]{2,1,0:T(8,128)(2,1)}) custom-call(s32[1]{0:T(128)} %bitcast.core_ref, bf16[512,1024]{1,0:T(8,128)(2,1)} %get-tuple-element.42.active_ref, bf16[512,1024]{1,0:T(8,128)(2,1)} %get-tuple-element.61.dresidual_ref, bf16[512,1024]{1,0:T(8,128)(2,1)} %get-tuple-element.47.final_ref, ...), custom_call_target="tpu_custom_call" | custom-call | tf_op jit(solution)/shard_map/outer/pallas_call | solution.py:349
  34.2 11.1 %inner.2 = (bf16[16,32,1024]{2,1,0:T(8,128)(2,1)}, bf16[16,32,1024]{2,1,0:T(8,128)(2,1)}, f32[512,512]{1,0:T(8,128)}) custom-call(s32[1]{0:T(128)} %bitcast.core_ref, s32[2]{0:T(128)} %lengths_ref.11, bf16[512,1024]{1,0:T(8,128)(2,1)} %get-tuple-element.61.dresidual_ref, bf16[1024,1024]{1,0:T(8,128)(2,1)} %out_weight_ref.5, ...), custom_call_target="tpu_custom_call" | custom-call | tf_op jit(solution)/shard_map/inner/pallas_call | solution.py:434
  45.8 3.1 %collective-permute-done.1 = bf16[16,32,1024]{2,1,0:T(8,128)(2,1)S(1)} collective-permute-done((bf16[16,32,1024]{2,1,0:T(8,128)(2,1)}, bf16[16,32,1024]{2,1,0:T(8,128)(2,1)S(1)}, u32[]{:S(2)}, u32[]{:S(2)}) %collective-permute-start.1) | collective-permute-done | bytes 1048608 | tf_op jit(solution)/shard_map/ppermute | solution.py:44
  48.9 1.6 add_convert_fusion.2
  50.5 17.3 %all_to_all.70 = bf16[4,4,32,1024]{3,2,1,0:T(8,128)(2,1)S(1)} all-to-all(bf16[4,4,32,1024]{3,2,1,0:T(8,128)(2,1)S(1)} %bitcast.15), channel_id=1, replica_groups=mesh['member'=2,'rest'=1,'far'=4,'near'=2,'core'=2] {'member','near'}, dimensions={0} | all-to-all | bytes 2097152 | tf_op jit(solution)/shard_map/all_to_all | solution.py:52
  67.8 0.9 reduce_sum.92
  68.7 4.9 %all-to-all-start.3 = ((bf16[4,32,1024]{2,1,0:T(8,128)(2,1)}), bf16[4,32,1024]{2,1,0:T(8,128)(2,1)S(1)}, u32[]{:S(2)}, u32[]{:S(2)}) async-start(bf16[4,32,1024]{2,1,0:T(8,128)(2,1)} %reduce_sum.92), calls=%async_computation.3 | async-start | bytes 524288 | tf_op jit(solution)/shard_map/all_to_all | solution.py:52
  73.6 2.7 add_convert_fusion
  76.3 5.3 %all-to-all-done.3 = bf16[4,32,1024]{2,1,0:T(8,128)(2,1)S(1)} async-done(((bf16[4,32,1024]{2,1,0:T(8,128)(2,1)}), bf16[4,32,1024]{2,1,0:T(8,128)(2,1)S(1)}, u32[]{:S(2)}, u32[]{:S(2)}) %all-to-all-start.3) | async-done | bytes 262176 | tf_op jit(solution)/shard_map/all_to_all | solution.py:52
  81.6 3.5 %all-to-all-start.10 = ((bf16[4,4,32,1280]{3,2,1,0:T(8,128)(2,1)}), bf16[4,4,32,1280]{3,2,1,0:T(8,128)(2,1)S(1)}, u32[]{:S(2)}, u32[]{:S(2)}) async-start(bf16[4,4,32,1280]{3,2,1,0:T(8,128)(2,1)} %bitcast.10), calls=%async_computation.10 | async-start | bytes 2621440 | tf_op jit(solution)/shard_map/all_to_all | solution.py:52
  85.1 11.0 %inner.3 = (bf16[16,32,1024]{2,1,0:T(8,128)(2,1)}, bf16[16,32,1024]{2,1,0:T(8,128)(2,1)}, f32[512,512]{1,0:T(8,128)}) custom-call(s32[1]{0:T(128)} %bitcast.core_ref, s32[2]{0:T(128)} %lengths_ref.11, bf16[512,1024]{1,0:T(8,128)(2,1)} %get-tuple-element.61.dresidual_ref, bf16[1024,1024]{1,0:T(8,128)(2,1)} %out_weight_ref.5, ...), custom_call_target="tpu_custom_call" | custom-call | tf_op jit(solution)/shard_map/inner/pallas_call | solution.py:434
  96.3 1.1 reduce_sum.93
  97.3 0.9 all-to-all-done.10
  98.9 5.2 %all-to-all-start.4 = ((bf16[4,32,1024]{2,1,0:T(8,128)(2,1)}), bf16[4,32,1024]{2,1,0:T(8,128)(2,1)}, u32[]{:S(2)}, u32[]{:S(2)}) async-start(bf16[4,32,1024]{2,1,0:T(8,128)(2,1)} %broadcast_in_dim.30), calls=%async_computation.4 | async-start | bytes 524288 | tf_op jit(solution)/shard_map/all_to_all | solution.py:57
  104.1 1.0 reduce_sum.96
  105.1 7.1 %all-to-all-done.4 = bf16[4,32,1024]{2,1,0:T(8,128)(2,1)} async-done(((bf16[4,32,1024]{2,1,0:T(8,128)(2,1)}), bf16[4,32,1024]{2,1,0:T(8,128)(2,1)}, u32[]{:S(2)}, u32[]{:S(2)}) %all-to-all-start.4) | async-done | bytes 262176 | tf_op jit(solution)/shard_map/all_to_all | solution.py:57
  112.3 3.6 %all-to-all-start.11 = ((bf16[4,32,1280]{2,1,0:T(8,128)(2,1)}), bf16[4,32,1280]{2,1,0:T(8,128)(2,1)S(1)}, u32[]{:S(2)}, u32[]{:S(2)}) async-start(bf16[4,32,1280]{2,1,0:T(8,128)(2,1)} %reduce_sum.96), calls=%async_computation.11 | async-start | bytes 655360 | tf_op jit(solution)/shard_map/all_to_all | solution.py:52
  115.9 1.4 add_convert_fusion.1
  117.3 5.7 %all-to-all-done.11 = bf16[4,32,1280]{2,1,0:T(8,128)(2,1)S(1)} async-done(((bf16[4,32,1280]{2,1,0:T(8,128)(2,1)}), bf16[4,32,1280]{2,1,0:T(8,128)(2,1)S(1)}, u32[]{:S(2)}, u32[]{:S(2)}) %all-to-all-start.11) | async-done | bytes 327712 | tf_op jit(solution)/shard_map/all_to_all | solution.py:52
  123.1 5.2 %all-to-all-start.6 = ((bf16[4,4,32,1024]{3,2,1,0:T(8,128)(2,1)}), bf16[4,4,32,1024]{3,2,1,0:T(8,128)(2,1)S(1)}, u32[]{:S(2)}, u32[]{:S(2)}) async-start(bf16[4,4,32,1024]{3,2,1,0:T(8,128)(2,1)} %bitcast.7), calls=%async_computation.6 | async-start | bytes 2097152 | tf_op jit(solution)/shard_map/all_to_all | solution.py:52
  128.4 9.8 %all-to-all-done.6 = bf16[4,4,32,1024]{3,2,1,0:T(8,128)(2,1)S(1)} async-done(((bf16[4,4,32,1024]{3,2,1,0:T(8,128)(2,1)}), bf16[4,4,32,1024]{3,2,1,0:T(8,128)(2,1)S(1)}, u32[]{:S(2)}, u32[]{:S(2)}) %all-to-all-start.6) | async-done | bytes 1048608 | tf_op jit(solution)/shard_map/all_to_all | solution.py:52
  138.9 5.8 %all-to-all-start.12 = ((bf16[4,32,1280]{2,1,0:T(8,128)(2,1)}), bf16[4,32,1280]{2,1,0:T(8,128)(2,1)S(1)}, u32[]{:S(2)}, u32[]{:S(2)}) async-start(bf16[4,32,1280]{2,1,0:T(8,128)(2,1)} %broadcast_in_dim.34), calls=%async_computation.12 | async-start | bytes 655360 | tf_op jit(solution)/shard_map/all_to_all | solution.py:57
  144.9 8.8 %all-to-all-done.12 = bf16[4,32,1280]{2,1,0:T(8,128)(2,1)S(1)} async-done(((bf16[4,32,1280]{2,1,0:T(8,128)(2,1)}), bf16[4,32,1280]{2,1,0:T(8,128)(2,1)S(1)}, u32[]{:S(2)}, u32[]{:S(2)}) %all-to-all-start.12) | async-done | bytes 327712 | tf_op jit(solution)/shard_map/all_to_all | solution.py:57
  153.7 10.3 %all_to_all.71 = bf16[4,32,1024]{2,1,0:T(8,128)(2,1)S(1)} all-to-all(bf16[4,32,1024]{2,1,0:T(8,128)(2,1)S(1)} %reduce_sum.94), channel_id=1, replica_groups=mesh['member'=2,'rest'=1,'far'=4,'near'=2,'core'=2] {'far'}, dimensions={0} | all-to-all | bytes 524288 | tf_op jit(solution)/shard_map/all_to_all | solution.py:52
  164.0 2.0 broadcast_in_dim.31
  166.1 3.8 %all-to-all-start.5 = ((bf16[4,4,32,1024]{3,2,1,0:T(8,128)(2,1)}), bf16[4,4,32,1024]{3,2,1,0:T(8,128)(2,1)S(1)}, u32[]{:S(2)}, u32[]{:S(2)}) async-start(bf16[4,4,32,1024]{3,2,1,0:T(8,128)(2,1)} %broadcast_in_dim.31), calls=%async_computation.5 | async-start | bytes 2097152 | tf_op jit(solution)/shard_map/all_to_all | solution.py:57
  169.9 11.3 %all-to-all-done.5 = bf16[4,4,32,1024]{3,2,1,0:T(8,128)(2,1)S(1)} async-done(((bf16[4,4,32,1024]{3,2,1,0:T(8,128)(2,1)}), bf16[4,4,32,1024]{3,2,1,0:T(8,128)(2,1)S(1)}, u32[]{:S(2)}, u32[]{:S(2)}) %all-to-all-start.5) | async-done | bytes 1048608 | tf_op jit(solution)/shard_map/all_to_all | solution.py:57
  181.2 12.9 %all_to_all.72 = bf16[4,32,1024]{2,1,0:T(8,128)(2,1)S(1)} all-to-all(bf16[4,32,1024]{2,1,0:T(8,128)(2,1)S(1)} %broadcast_in_dim.32), channel_id=1, replica_groups=mesh['member'=2,'rest'=1,'far'=4,'near'=2,'core'=2] {'far'}, dimensions={0} | all-to-all | bytes 524288 | tf_op jit(solution)/shard_map/all_to_all | solution.py:57
  194.2 17.8 %all_to_all.73 = bf16[4,4,32,1280]{3,2,1,0:T(8,128)(2,1)S(1)} all-to-all(bf16[4,4,32,1280]{3,2,1,0:T(8,128)(2,1)S(1)} %broadcast_in_dim.35), channel_id=1, replica_groups=mesh['member'=2,'rest'=1,'far'=4,'near'=2,'core'=2] {'member','near'}, dimensions={0} | all-to-all | bytes 2621440 | tf_op jit(solution)/shard_map/all_to_all | solution.py:57
  212.0 1.3 broadcast_in_dim.33
  213.3 3.5 %all-to-all-start.9 = ((bf16[4,4,32,1024]{3,2,1,0:T(8,128)(2,1)}), bf16[4,4,32,1024]{3,2,1,0:T(8,128)(2,1)S(1)}, u32[]{:S(2)}, u32[]{:S(2)}) async-start(bf16[4,4,32,1024]{3,2,1,0:T(8,128)(2,1)} %broadcast_in_dim.33), calls=%async_computation.9 | async-start | bytes 2097152 | tf_op jit(solution)/shard_map/all_to_all | solution.py:57
  216.8 4.3 %taps.2 = f32[32,512]{1,0:T(8,128)} custom-call(s32[2]{0:T(128)} %lengths_ref.11, f32[512,1024]{1,0:T(8,128)} %get-tuple-element.41.gated_ref, f32[512,512]{1,0:T(8,128)} %get-tuple-element.58.dconv_ref), custom_call_target="tpu_custom_call" | custom-call | tf_op jit(solution)/shard_map/taps/pallas_call | solution.py:497
  221.1 4.4 %taps.3 = f32[32,512]{1,0:T(8,128)} custom-call(s32[2]{0:T(128)} %lengths_ref.11, f32[512,1024]{1,0:T(8,128)} %get-tuple-element.41.gated_ref, f32[512,512]{1,0:T(8,128)} %get-tuple-element.62.dconv_ref), custom_call_target="tpu_custom_call" | custom-call | tf_op jit(solution)/shard_map/taps/pallas_call | solution.py:497
  225.5 0.8 pad_maximum_fusion
  227.0 0.9 broadcast_in_dim.28
  228.0 4.1 %all-to-all-start = ((f32[4,32,1024]{2,1,0:T(8,128)}), f32[4,32,1024]{2,1,0:T(8,128)}, u32[]{:S(2)}, u32[]{:S(2)}) async-start(f32[4,32,1024]{2,1,0:T(8,128)} %broadcast_in_dim.28), calls=%async_computation | async-start | bytes 1048576 | tf_op jit(solution)/shard_map/all_to_all | solution.py:57
  232.8 6.0 %all-to-all-done = f32[4,32,1024]{2,1,0:T(8,128)} async-done(((f32[4,32,1024]{2,1,0:T(8,128)}), f32[4,32,1024]{2,1,0:T(8,128)}, u32[]{:S(2)}, u32[]{:S(2)}) %all-to-all-start) | async-done | bytes 524320 | tf_op jit(solution)/shard_map/all_to_all | solution.py:57
  238.8 1.1 reduce_sum.90
  239.9 19.6 %all_to_all.74 = f32[4,32,1024]{2,1,0:T(8,128)} all-to-all(f32[4,32,1024]{2,1,0:T(8,128)S(1)} %broadcast_in_dim.29), channel_id=1, replica_groups=mesh['member'=2,'rest'=1,'far'=4,'near'=2,'core'=2] {'far'}, dimensions={0} | all-to-all | bytes 1048576 | tf_op jit(solution)/shard_map/all_to_all | solution.py:57
  259.5 1.1 reduce_sum.91
  260.6 1.3 collective-permute-done.3
  262.6 5.1 %unpack_top.1 = (f32[1024,1024]{1,0:T(8,128)}, f32[1024,256]{1,0:T(8,128)}, f32[1,1024]{1,0:T(1,128)}, f32[31,1024]{1,0:T(8,128)}, f32[2,1,128]{2,1,0:T(1,128)}) custom-call(s32[1]{0:T(128)} %bitcast.core_ref, f32[32,1024]{1,0:T(8,128)} %add.14.small_ref, bf16[16,32,1280]{2,1,0:T(8,128)(2,1)} %bitcast.14, ...), custom_call_target="tpu_custom_call" | custom-call | tf_op jit(solution)/shard_map/unpack_top/pallas_call | solution.py:592
  267.8 1.3 slice_reduce_fusion
  269.1 9.7 %unpack_inner.1 = (f32[1024,2048]{1,0:T(8,128)}, f32[1,1024]{1,0:T(1,128)}) custom-call(s32[1]{0:T(128)} %bitcast.core_ref, f32[32,1024]{1,0:T(8,128)} %add.14.small_ref, bf16[1024,2048]{1,0:T(8,128)(2,1)} %weight_ref.1, f32[1,1024]{1,0:T(1,128)} %bitcast.24, bf16[16,32,1024]{2,1,0:T(8,128)(2,1)} %bitcast.17, ...), custom_call_target="tpu_custom_call" | custom-call | tf_op jit(solution)/shard_map/unpack_inner/pallas_call | solution.py:630
  (39 shorter events, 5.5 us)
Async XLA Ops:
  4.6 17.9 %collective-permute-start = (f32[2,256,256]{2,1,0:T(8,128)}, f32[2,256,256]{2,1,0:T(8,128)S(1)}, u32[]{:S(2)}, u32[]{:S(2)}) collective-permute-start(f32[2,256,256]{2,1,0:T(8,128)} %get-tuple-element.45), channel_id=1, source_target_pairs={{0,16},{16,0},{1,17},{17,1},{2,18},{18,2},{3,19},{19,3},{4,20},{20... | collective-permute-start | bytes 1572872 | tf_op jit(solution)/shard_map/ppermute | solution.py:665
  22.6 0.8 copy-start.6
  45.2 3.6 %collective-permute-start.1 = (bf16[16,32,1024]{2,1,0:T(8,128)(2,1)}, bf16[16,32,1024]{2,1,0:T(8,128)(2,1)S(1)}, u32[]{:S(2)}, u32[]{:S(2)}) collective-permute-start(bf16[16,32,1024]{2,1,0:T(8,128)(2,1)} %get-tuple-element.57), channel_id=1, source_target_pairs={{0,1},{1,0},{2,3},{3,2},{4,5},{5,4},{6,7},{7,6},{8,9},{9,8},{10,11... | collective-permute-start | bytes 3145736 | tf_op jit(solution)/shard_map/ppermute | solution.py:44
  45.2 28.3 %collective-permute-start.2 = (bf16[16,32,1280]{2,1,0:T(8,128)(2,1)}, bf16[16,32,1280]{2,1,0:T(8,128)(2,1)}, u32[]{:S(2)}, u32[]{:S(2)}) collective-permute-start(bf16[16,32,1280]{2,1,0:T(8,128)(2,1)} %get-tuple-element.60), channel_id=1, source_target_pairs={{0,1},{1,0},{2,3},{3,2},{4,5},{5,4},{6,7},{7,6},{8,9},{9,8},{10,11... | collective-permute-start | bytes 3932168 | tf_op jit(solution)/shard_map/ppermute | solution.py:44
  50.5 23.1 %copy-start.3 = (bf16[16,32,1280]{2,1,0:T(8,128)(2,1)S(1)}, bf16[16,32,1280]{2,1,0:T(8,128)(2,1)}, u32[]{:S(2)}) copy-start(bf16[16,32,1280]{2,1,0:T(8,128)(2,1)} %get-tuple-element.59) | copy-start | bytes 3932164
  68.7 12.9 %all-to-all-start.3 = ((bf16[4,32,1024]{2,1,0:T(8,128)(2,1)}), bf16[4,32,1024]{2,1,0:T(8,128)(2,1)S(1)}, u32[]{:S(2)}, u32[]{:S(2)}) async-start(bf16[4,32,1024]{2,1,0:T(8,128)(2,1)} %reduce_sum.92), calls=%async_computation.3 | async-start | bytes 524288 | tf_op jit(solution)/shard_map/all_to_all | solution.py:52
  81.6 14.6 %copy-start.5 = (bf16[4,32,1024]{2,1,0:T(8,128)(2,1)}, bf16[4,32,1024]{2,1,0:T(8,128)(2,1)S(1)}, u32[]{:S(2)}) copy-start(bf16[4,32,1024]{2,1,0:T(8,128)(2,1)S(1)} %all-to-all-done.3) | copy-start | bytes 786436
  81.6 16.6 %all-to-all-start.10 = ((bf16[4,4,32,1280]{3,2,1,0:T(8,128)(2,1)}), bf16[4,4,32,1280]{3,2,1,0:T(8,128)(2,1)S(1)}, u32[]{:S(2)}, u32[]{:S(2)}) async-start(bf16[4,4,32,1280]{3,2,1,0:T(8,128)(2,1)} %bitcast.10), calls=%async_computation.10 | async-start | bytes 2621440 | tf_op jit(solution)/shard_map/all_to_all | solution.py:52
  96.2 19.7 %copy-start.4 = (bf16[16,32,1024]{2,1,0:T(8,128)(2,1)S(1)}, bf16[16,32,1024]{2,1,0:T(8,128)(2,1)}, u32[]{:S(2)}) copy-start(bf16[16,32,1024]{2,1,0:T(8,128)(2,1)} %get-tuple-element.64) | copy-start | bytes 3145732
  96.2 19.7 %collective-permute-start.5 = (bf16[16,32,1024]{2,1,0:T(8,128)(2,1)}, bf16[16,32,1024]{2,1,0:T(8,128)(2,1)S(1)}, u32[]{:S(2)}, u32[]{:S(2)}) collective-permute-start(bf16[16,32,1024]{2,1,0:T(8,128)(2,1)} %get-tuple-element.65), channel_id=1, source_target_pairs={{0,1},{1,0},{2,3},{3,2},{4,5},{5,4},{6,7},{7,6},{8,9},{9,8},{10,11... | collective-permute-start | bytes 3145736 | tf_op jit(solution)/shard_map/ppermute | solution.py:44
  98.9 13.3 %all-to-all-start.4 = ((bf16[4,32,1024]{2,1,0:T(8,128)(2,1)}), bf16[4,32,1024]{2,1,0:T(8,128)(2,1)}, u32[]{:S(2)}, u32[]{:S(2)}) async-start(bf16[4,32,1024]{2,1,0:T(8,128)(2,1)} %broadcast_in_dim.30), calls=%async_computation.4 | async-start | bytes 524288 | tf_op jit(solution)/shard_map/all_to_all | solution.py:57
  112.3 10.8 %all-to-all-start.11 = ((bf16[4,32,1280]{2,1,0:T(8,128)(2,1)}), bf16[4,32,1280]{2,1,0:T(8,128)(2,1)S(1)}, u32[]{:S(2)}, u32[]{:S(2)}) async-start(bf16[4,32,1280]{2,1,0:T(8,128)(2,1)} %reduce_sum.96), calls=%async_computation.11 | async-start | bytes 655360 | tf_op jit(solution)/shard_map/all_to_all | solution.py:52
  123.1 15.1 %all-to-all-start.6 = ((bf16[4,4,32,1024]{3,2,1,0:T(8,128)(2,1)}), bf16[4,4,32,1024]{3,2,1,0:T(8,128)(2,1)S(1)}, u32[]{:S(2)}, u32[]{:S(2)}) async-start(bf16[4,4,32,1024]{3,2,1,0:T(8,128)(2,1)} %bitcast.7), calls=%async_computation.6 | async-start | bytes 2097152 | tf_op jit(solution)/shard_map/all_to_all | solution.py:52
  138.9 14.8 %all-to-all-start.12 = ((bf16[4,32,1280]{2,1,0:T(8,128)(2,1)}), bf16[4,32,1280]{2,1,0:T(8,128)(2,1)S(1)}, u32[]{:S(2)}, u32[]{:S(2)}) async-start(bf16[4,32,1280]{2,1,0:T(8,128)(2,1)} %broadcast_in_dim.34), calls=%async_computation.12 | async-start | bytes 655360 | tf_op jit(solution)/shard_map/all_to_all | solution.py:57
  166.1 15.1 %all-to-all-start.5 = ((bf16[4,4,32,1024]{3,2,1,0:T(8,128)(2,1)}), bf16[4,4,32,1024]{3,2,1,0:T(8,128)(2,1)S(1)}, u32[]{:S(2)}, u32[]{:S(2)}) async-start(bf16[4,4,32,1024]{3,2,1,0:T(8,128)(2,1)} %broadcast_in_dim.31), calls=%async_computation.5 | async-start | bytes 2097152 | tf_op jit(solution)/shard_map/all_to_all | solution.py:57
  181.2 51.0 %copy-start.1 = (bf16[4,4,32,1024]{3,2,1,0:T(8,128)(2,1)}, bf16[4,4,32,1024]{3,2,1,0:T(8,128)(2,1)S(1)}, u32[]{:S(2)}) copy-start(bf16[4,4,32,1024]{3,2,1,0:T(8,128)(2,1)S(1)} %all-to-all-done.5) | copy-start | bytes 3145732
  212.0 20.1 %copy-start = (bf16[4,4,32,1280]{3,2,1,0:T(8,128)(2,1)}, bf16[4,4,32,1280]{3,2,1,0:T(8,128)(2,1)S(1)}, u32[]{:S(2)}) copy-start(bf16[4,4,32,1280]{3,2,1,0:T(8,128)(2,1)S(1)} %all_to_all.73) | copy-start | bytes 3932164
  213.3 13.8 %all-to-all-start.9 = ((bf16[4,4,32,1024]{3,2,1,0:T(8,128)(2,1)}), bf16[4,4,32,1024]{3,2,1,0:T(8,128)(2,1)S(1)}, u32[]{:S(2)}, u32[]{:S(2)}) async-start(bf16[4,4,32,1024]{3,2,1,0:T(8,128)(2,1)} %broadcast_in_dim.33), calls=%async_computation.9 | async-start | bytes 2097152 | tf_op jit(solution)/shard_map/all_to_all | solution.py:57
  221.1 4.4 %copy-start.7 = (f32[32,512]{1,0:T(8,128)S(1)}, f32[32,512]{1,0:T(8,128)}, u32[]{:S(2)}) copy-start(f32[32,512]{1,0:T(8,128)} %taps.2) | copy-start | bytes 196612
  227.0 33.5 %copy-start.2 = (bf16[4,4,32,1024]{3,2,1,0:T(8,128)(2,1)}, bf16[4,4,32,1024]{3,2,1,0:T(8,128)(2,1)S(1)}, u32[]{:S(2)}) copy-start(bf16[4,4,32,1024]{3,2,1,0:T(8,128)(2,1)S(1)} %all-to-all-done.9) | copy-start | bytes 3145732
  228.0 10.8 %all-to-all-start = ((f32[4,32,1024]{2,1,0:T(8,128)}), f32[4,32,1024]{2,1,0:T(8,128)}, u32[]{:S(2)}, u32[]{:S(2)}) async-start(f32[4,32,1024]{2,1,0:T(8,128)} %broadcast_in_dim.28), calls=%async_computation | async-start | bytes 1048576 | tf_op jit(solution)/shard_map/all_to_all | solution.py:57
  232.1 30.5 %collective-permute-start.7 = (bf16[16,32,1280]{2,1,0:T(8,128)(2,1)S(1)}, bf16[16,32,1280]{2,1,0:T(8,128)(2,1)}, u32[]{:S(2)}, u32[]{:S(2)}) collective-permute-start(bf16[16,32,1280]{2,1,0:T(8,128)(2,1)S(1)} %bitcast.13), channel_id=1, source_target_pairs={{0,1},{1,0},{2,3},{3,2},{4,5},{5,4},{6,7},{7,6},{8,9},{9,8},{10,11... | collective-permute-start | bytes 3932168 | tf_op jit(solution)/shard_map/ppermute | solution.py:44
  232.2 36.9 %collective-permute-start.4 = (bf16[16,32,1024]{2,1,0:T(8,128)(2,1)S(1)}, bf16[16,32,1024]{2,1,0:T(8,128)(2,1)}, u32[]{:S(2)}, u32[]{:S(2)}) collective-permute-start(bf16[16,32,1024]{2,1,0:T(8,128)(2,1)S(1)} %bitcast.16), channel_id=1, source_target_pairs={{0,1},{1,0},{2,3},{3,2},{4,5},{5,4},{6,7},{7,6},{8,9},{9,8},{10,11... | collective-permute-start | bytes 3145736 | tf_op jit(solution)/shard_map/ppermute | solution.py:44
  232.7 36.4 %collective-permute-start.6 = (bf16[16,32,1024]{2,1,0:T(8,128)(2,1)S(1)}, bf16[16,32,1024]{2,1,0:T(8,128)(2,1)}, u32[]{:S(2)}, u32[]{:S(2)}) collective-permute-start(bf16[16,32,1024]{2,1,0:T(8,128)(2,1)S(1)} %bitcast.18), channel_id=1, source_target_pairs={{0,1},{1,0},{2,3},{3,2},{4,5},{5,4},{6,7},{7,6},{8,9},{9,8},{10,11... | collective-permute-start | bytes 3145736 | tf_op jit(solution)/shard_map/ppermute | solution.py:44
  260.5 1.4 collective-permute-start.3

commit v3 on v2

--- a/solution.py
+++ b/solution.py
@@ -24,6 +24,10 @@
     return pltpu.CompilerParams(vmem_limit_bytes=VMEM)
 
 
+def cost(microseconds):
+    return pl.CostEstimate(flops=int(microseconds * 1.15e9), bytes_accessed=1 << 20, transcendentals=0)
+
+
 def dot(left, right, left_axis=1, right_axis=0):
     return lax.dot_general(
         left, right, (((left_axis,), (right_axis,)), ((), ())), preferred_element_type=F32
@@ -34,7 +38,8 @@
     return pl.BlockSpec(shape, lambda i, *_: (0,) * len(shape))
 
 
-NEAR = ("member", "near")
+XY = ("member", "near")
+YX = ("near", "member")
 FAR = "far"
 REST = "rest"
 CORE = "core"
@@ -48,45 +53,51 @@
     return (keep.astype(F32) + other_core(send).astype(F32)).astype(BF16)
 
 
-def sum_over(values, axis):
-    got = lax.all_to_all(values, axis, 0, 0)
-    return jnp.sum(got.astype(F32), axis=0).astype(values.dtype)
-
-
-def gather_over(values, axis):
-    return lax.all_to_all(
-        jnp.broadcast_to(values[None], (lax.axis_size(axis),) + values.shape), axis, 0, 0
-    )
-
-
-def sum_near(pieces):
-    near = lax.axis_size(NEAR)
-    return sum_over(pieces.reshape((near, pieces.shape[0] // near) + pieces.shape[1:]), NEAR)
-
-
-def sum_far(pieces):
-    own = sum_over(pieces, FAR)
-    return lax.psum(own, REST) if lax.axis_size(REST) > 1 else own
-
-
-def gather_near(pieces):
-    got = gather_over(pieces, NEAR)
-    return got.reshape((got.shape[0] * got.shape[1],) + got.shape[2:])
+def halve(pieces, dim, axis, bit):
+    size = lax.axis_size(axis)
+    got = lax.ppermute(
+        lax.index_in_dim(pieces, 1, dim, keepdims=False), axis, [(i, i ^ bit) for i in range(size)]
+    )
+    kept = lax.index_in_dim(pieces, 0, dim, keepdims=False)
+    return (kept.astype(F32) + got.astype(F32)).astype(pieces.dtype)
+
+
+def sum_chips(pieces, order):
+    pieces = pieces.reshape((2, 2, 2, 2) + pieces.shape[1:])
+    pieces = halve(pieces, 0, order[0], 1)
+    pieces = halve(pieces, 0, order[1], 1)
+    pieces = halve(pieces, 1, FAR, 1)
+    pieces = halve(pieces, 0, FAR, 2)
+    return over_rest(pieces)
+
+
+def over_rest(values):
+    return lax.psum(values, REST) if lax.axis_size(REST) > 1 else values
+
+
+def gather(shard, order):
+    return lax.all_gather(shard, order + (FAR,), axis=0, tiled=False)
+
+
+def own_place(order):
+    place = lax.axis_index(order[0]) * 8 + lax.axis_index(order[1]) * 4 + lax.axis_index(FAR)
+    return place.astype(jnp.int32)
 
 
 def all_sum(values):
-    for axis in (NEAR, FAR):
-        values = jnp.sum(gather_over(values, axis), axis=0)
-    if lax.axis_size(REST) > 1:
-        values = lax.psum(values, REST)
+    for axis, bit in (("member", 1), ("near", 1), (FAR, 1), (FAR, 2)):
+        size = lax.axis_size(axis)
+        values = values + lax.ppermute(values, axis, [(i, i ^ bit) for i in range(size)])
+    values = over_rest(values)
     return values + other_core(values)
 
 
-def write_pieces(core, product, send_ref, keep_ref, columns):
+def write_pieces(own_ref, product, send_ref, keep_ref, columns):
     rows = keep_ref.shape[-2]
+    core, place = own_ref[0], own_ref[1]
 
     def one(piece, carry):
-        base = piece * (2 * rows)
+        base = (piece ^ place) * (2 * rows)
         kept = pl.multiple_of(base + core * rows, rows)
         sent = pl.multiple_of(base + (1 - core) * rows, rows)
         keep_ref[piece, :, columns] = product[pl.ds(kept, rows), :].astype(BF16)
@@ -140,6 +151,7 @@
             ),
         ),
         compiler_params=params(),
+        cost_estimate=cost(4),
         name="teachers",
     )(member, logits)
 
@@ -260,6 +272,7 @@
         out_specs=(fixed(rows, model), column, column, column, column, fixed(rows, model)),
         scratch_shapes=[pltpu.VMEM((WIDE // LANES, utterances, frames + 2 * MARGIN, LANES), F32)],
         compiler_params=params(),
+        cost_estimate=cost(15),
         name="forward",
     )(lengths, features, gain, weight_in, weight_in, depth, weight_out)
 
@@ -325,20 +338,21 @@
             per_row,
         ),
         compiler_params=params(),
+        cost_estimate=cost(5),
         name="top",
     )(lengths, residual, gain, head, kept, got)
 
 
 def outer_kernel(
-    core_ref, active_ref, dresidual_ref, final_ref, dlogits_ref, send_ref, keep_ref, product_ref
+    own_ref, active_ref, dresidual_ref, final_ref, dlogits_ref, send_ref, keep_ref, product_ref
 ):
     width = dresidual_ref.shape[1]
     product_ref[:, :width] = dot(active_ref[...], dresidual_ref[...], 0, 0)
     product_ref[:, width:] = dot(final_ref[...], dlogits_ref[...], 0, 0)
-    write_pieces(core_ref[0], product_ref, send_ref, keep_ref, slice(None))
-
-
-def outer(core, active, dresidual, final, dlogits):
+    write_pieces(own_ref, product_ref, send_ref, keep_ref, slice(None))
+
+
+def outer(own, active, dresidual, final, dlogits):
     rows, model = active.shape
     half_out = dresidual.shape[1] // 2
     half_head = dlogits.shape[1] // 2
@@ -360,12 +374,13 @@
         out_specs=(out, out),
         scratch_shapes=[pltpu.VMEM((model, width), F32)],
         compiler_params=params(),
+        cost_estimate=cost(5),
         name="outer",
-    )(core, active, dresidual, final, dlogits)
+    )(own, active, dresidual, final, dlogits)
 
 
 def inner_kernel(
-    core_ref,
+    own_ref,
     lengths_ref,
     dresidual_ref,
     out_weight_ref,
@@ -419,10 +434,10 @@
     for group, source in ((0, dvalue_ref), (1, dgate_ref)):
         product_ref[...] = dot(normed_ref[...], source[...], 0, 0)
         columns = slice(group * WIDE, (group + 1) * WIDE)
-        write_pieces(core_ref[0], product_ref, send_ref, keep_ref, columns)
-
-
-def inner(core, lengths, dresidual, weight_out, slope, gated, gate, normed, depth, chunk, utterances):
+        write_pieces(own_ref, product_ref, send_ref, keep_ref, columns)
+
+
+def inner(own, lengths, dresidual, weight_out, slope, gated, gate, normed, depth, chunk, utterances):
     rows, model = normed.shape
     frames = rows // utterances
     steps = model // WIDE // CHUNKS
@@ -454,8 +469,9 @@
             pltpu.VMEM((model, WIDE), F32),
         ],
         compiler_params=params(),
+        cost_estimate=cost(11),
         name="inner",
-    )(core, lengths, dresidual, weight_out, slope, gated, gate, normed, depth)
+    )(own, lengths, dresidual, weight_out, slope, gated, gate, normed, depth)
 
 
 def taps_kernel(lengths_ref, gated_ref, dconv_ref, out_ref, pad_ref, sums_ref):
@@ -509,6 +525,7 @@
             pltpu.VMEM((taps, 8, LANES), F32),
         ],
         compiler_params=params(),
+        cost_estimate=cost(4),
         name="taps",
     )(lengths, gated, dconv)
 
@@ -616,6 +633,7 @@
             fixed(*losses.shape),
         ),
         compiler_params=params(),
+        cost_estimate=cost(5),
         name="unpack_top",
     )(core, small, own, other, head, gain, losses)
 
@@ -638,6 +656,7 @@
         + [piece_spec(array, steps) for array in pieces],
         out_specs=(block, row),
         compiler_params=params(),
+        cost_estimate=cost(9),
         name="unpack_inner",
     )(core, small, weight, gain, *pieces)
 
@@ -653,7 +672,7 @@
     gain_out,
     head_weight,
 ):
-    count = lax.axis_size(NEAR) * lax.axis_size(FAR) * lax.axis_size(REST) * lax.axis_size(CORE)
+    count = lax.axis_size(XY) * lax.axis_size(FAR) * lax.axis_size(REST) * lax.axis_size(CORE)
     member = lax.axis_index("member").astype(jnp.int32)[None]
     core = lax.axis_index(CORE).astype(jnp.int32)[None]
     taps, model = weight_depth.shape
@@ -671,9 +690,9 @@
         lengths, residual, gain_out[None], head_weight, kept, got
     )
 
-    def weight_in_chunk(chunk, dresidual):
+    def weight_in_chunk(chunk, order, dresidual):
         return inner(
-            core,
+            jnp.stack([core[0], own_place(order)]),
             lengths,
             dresidual,
             weight_out,
@@ -686,13 +705,15 @@
             utterances,
         )
 
-    send, keep = outer(core, active, dresidual, final, dlogits)
+    unordered = jnp.stack([core[0], jnp.int32(0)])
+    send, keep = outer(unordered, active, dresidual, final, dlogits)
     send, keep, dresidual = tie((send, keep, dresidual))
     top_sum = sum_core(send, keep)
     inner_sums = []
     dconvs = []
     for chunk in range(CHUNKS):
-        send, keep, dconv = weight_in_chunk(chunk, dresidual)
+        order = XY if chunk % 2 else YX
+        send, keep, dconv = weight_in_chunk(chunk, order, dresidual)
         inner_sums.append(sum_core(send, keep))
         dconvs.append(dconv)
         if chunk == 0:
@@ -705,12 +726,14 @@
         ],
         axis=1,
     )
-    top_all = gather_near(gather_over(sum_far(sum_near(top_sum)), FAR))
+    top_own = over_rest(lax.psum_scatter(top_sum, XY + (FAR,), scatter_dimension=0, tiled=False))
+    top_all = gather(top_own, XY)
     top_other = other_core(top_all)
     small = all_sum(small)
     pairs = []
-    for values in inner_sums:
-        every = gather_near(gather_over(sum_far(sum_near(values)), FAR))
+    for chunk, values in enumerate(inner_sums):
+        order = XY if chunk % 2 else YX
+        every = gather(sum_chips(values, order), order)
         pairs.append((every, other_core(every)))
     grad_out, grad_head, by_head, grad_depth, losses = unpack_top(
         utts,

time: 280 us -> 353 us (1.26)
  waiting for transfers between devices: 60 us -> 223 us
  blocking collectives: 77.8 us -> 0 us
  starting transfers between devices: 44 us -> 25.1 us
  between operations: 0.88 us -> 14 us
  other arithmetic: 12.7 us -> 8.98 us
    all_gather x0 -> x3, waiting for transfers between devices: none -> 149 us  [gather(): return lax.all_gather(shard, order + (FAR,), axis=0, tiled=False)]
    all_to_all x5 -> x0, blocking collectives: 77.8 us -> none  [the longest x3 50.2 us: gather_over(): lax.all_to_all(jnp.broadcast_to(values[None], (lax.axis_size(axis),) + va...]
    all_to_all x9 -> x0, waiting for transfers between devices: 55.5 us -> none  [the longest x5 33.8 us: gather_over(): lax.all_to_all(jnp.broadcast_to(values[None], (lax.axis_size(axis),) + va...]
    ppermute x0 -> x12, waiting for transfers between devices: none -> 48.9 us  [the longest x8 32 us: halve(): lax.ppermute(lax.index_in_dim(pieces, 1, dim, keepdims=False), axis, [(i,...]
    all_to_all x9 -> x0, starting transfers between devices: 39.8 us -> none  [the longest x5 22.5 us: gather_over(): lax.all_to_all(jnp.broadcast_to(values[None], (lax.axis_size(axis),) + va...]
    ppermute x0 -> x12, starting transfers between devices: none -> 21.1 us  [the longest x8 16.7 us: halve(): lax.ppermute(lax.index_in_dim(pieces, 1, dim, keepdims=False), axis, [(i,...]
    reduce_scatter x0 -> x1, waiting for transfers between devices: none -> 20.9 us  [on_device(): lax.psum_scatter(top_sum, XY + (FAR,), scatter_dimension=0, tiled=False)]
    broadcast_in_dim x8 -> x0, local copies, waits for them, and re-layouts: 5.9 us -> none  [gather_over(): jnp.broadcast_to(values[None], (lax.axis_size(axis),) + values.shape)]
  transfers between devices with their start and end apart: 17 -> 24, of which waited for: 11 -> 15; matrix products, arithmetic and copies ran while one was open for 5% -> 3% of each run, Pallas kernels for 14% -> 13%
where the time goes in v3:
time: 353 us
  waiting for transfers between devices  223 us (63%)
  Pallas kernels  75.6 us (21%)
  starting transfers between devices  25.1 us (7%)
  between operations  14 us (4%)
  other arithmetic  8.98 us (3%)
  local copies, waits for them, and re-layouts  5.45 us (2%)
    all_gather x3, waiting for transfers between devices, gather(): return lax.all_gather(shard, order + (FAR,), axis=0, tiled=False)  149 us
    ppermute x8, waiting for transfers between devices, halve(): lax.ppermute(lax.index_in_dim(pieces, 1, dim, keepdims=False), axis, [(i,...  32 us
    pallas_call x2, Pallas kernels, inner(): pl.pallas_call(inner_kernel, grid=(steps,), out_shape=(shape, shape, jax....  22.2 us
    reduce_scatter x1, waiting for transfers between devices, on_device(): lax.psum_scatter(top_sum, XY + (FAR,), scatter_dimension=0, tiled=False)  20.9 us
    ppermute x4, waiting for transfers between devices, all_sum(): lax.ppermute(values, axis, [(i, i ^ bit) for i in range(size)])  16.9 us
    ppermute x8, starting transfers between devices, halve(): lax.ppermute(lax.index_in_dim(pieces, 1, dim, keepdims=False), axis, [(i,...  16.7 us
    pallas_call x1, Pallas kernels, forward(): pl.pallas_call(forward_kernel, grid=(steps,), out_shape=(narrow, wide, wi...  15 us
    pallas_call x1, Pallas kernels, unpack_inner(): pl.pallas_call(functools.partial(unpack_inner_kernel, utts), grid=(steps,...  9.68 us
  transfers between devices with their start and end apart: 24, of which 15 were waited for; matrix products, arithmetic and copies ran while one was open for 3% of the time, Pallas kernels for 13%

profile of v3, /device:TPU:0, one launch (start us, length us, event | category | flops | bytes accessed | tf_op | source)
XLA Modules:
  0.0 352.7 jit_solution(6751537591965744974)
XLA Ops:
  7.2 4.0 %teachers.1 = (f32[2,256,256]{2,1,0:T(8,128)}, f32[2,256,256]{2,1,0:T(8,128)}) custom-call(s32[1]{0:T(128)} %bitcast.5.member_ref, bf16[2,4,256,256]{3,2,1,0:T(8,128)(2,1)} %logits_ref.1), custom_call_target="tpu_custom_call" | custom-call | flops 4600000000 | bytes 1048576 | tf_op jit(solution)/shard_map/teachers/pallas_call | solution.py:137
  11.2 2.9 collective-permute-start
  14.1 15.0 %forward.1 = (bf16[512,1024]{1,0:T(8,128)(2,1)}, f32[512,1024]{1,0:T(8,128)}, f32[512,1024]{1,0:T(8,128)}, f32[512,1024]{1,0:T(8,128)}, bf16[512,1024]{1,0:T(8,128)(2,1)}, /*index=5*/f32[512,1024]{1,0:T(8,128)}) custom-call(s32[2]{0:T(128)} %lengths_ref.11, bf16[512,1024]{1,0:T(8,128)(2,1)} %bitcast.63, f32[1,1024]{1,0:T(1,128)} %bitcast.68, ...), custom_call_target="tpu_custom_call" | custom-call | flops 17250000896 | bytes 1048576 | tf_op jit(solution)/shard_map/forward/pallas_call | solution.py:259
  30.4 0.9 copy-done.7
  31.2 5.3 %top.1 = (f32[2,1,128]{2,1,0:T(1,128)}, bf16[512,1024]{1,0:T(8,128)(2,1)}, bf16[512,256]{1,0:T(8,128)(2,1)}, bf16[512,1024]{1,0:T(8,128)(2,1)}) custom-call(s32[2]{0:T(128)} %lengths_ref.11, f32[512,1024]{1,0:T(8,128)} %get-tuple-element.43.residual_ref, f32[1,1024]{1,0:T(1,128)} %bitcast.70, bf16[1024,256]{1,0:T(8,128)(2,1)} %head_ref.3, ...), custom_call_target="tpu_custom_call" | custom-call | flops 5750000128 | bytes 1048576 | tf_op jit(solution)/shard_map/top/pallas_call | solution.py:324
  36.5 5.5 %outer.1 = (bf16[16,32,1280]{2,1,0:T(8,128)(2,1)}, bf16[16,32,1280]{2,1,0:T(8,128)(2,1)}) custom-call(s32[2]{0:T(128)} %pad_add_fusion.1.own_ref, bf16[512,1024]{1,0:T(8,128)(2,1)} %get-tuple-element.42.active_ref, bf16[512,1024]{1,0:T(8,128)(2,1)} %get-tuple-element.61.dresidual_ref, bf16[512,1024]{1,0:T(8,128)(2,1)} %get-tuple-element.47.final_ref, ...), custom_call_target="tpu_custom_call" | custom-call | flops 5750000128 | bytes 1048576 | tf_op jit(solution)/shard_map/outer/pallas_call | solution.py:363
  42.1 11.2 %inner.2 = (bf16[16,32,1024]{2,1,0:T(8,128)(2,1)}, bf16[16,32,1024]{2,1,0:T(8,128)(2,1)}, f32[512,512]{1,0:T(8,128)}) custom-call(s32[2]{0:T(128)} %get-tuple-element.79.own_ref, s32[2]{0:T(128)} %lengths_ref.11, bf16[512,1024]{1,0:T(8,128)(2,1)} %get-tuple-element.61.dresidual_ref, bf16[1024,1024]{1,0:T(8,128)(2,1)} %out_weight_ref.5, ...), custom_call_target="tpu_custom_call" | custom-call | flops 12650000384 | bytes 1048576 | tf_op jit(solution)/shard_map/inner/pallas_call | solution.py:449
  53.8 3.0 collective-permute-done.1
  56.8 1.6 add_convert_fusion.2
  58.5 1.6 collective-permute-start.8
  60.1 1.5 add_convert_fusion
  61.8 11.1 %inner.3 = (bf16[16,32,1024]{2,1,0:T(8,128)(2,1)}, bf16[16,32,1024]{2,1,0:T(8,128)(2,1)}, f32[512,512]{1,0:T(8,128)}) custom-call(s32[2]{0:T(128)} %get-tuple-element.80.own_ref, s32[2]{0:T(128)} %lengths_ref.11, bf16[512,1024]{1,0:T(8,128)(2,1)} %get-tuple-element.61.dresidual_ref, bf16[1024,1024]{1,0:T(8,128)(2,1)} %out_weight_ref.5, ...), custom_call_target="tpu_custom_call" | custom-call | flops 12650000384 | bytes 1048576 | tf_op jit(solution)/shard_map/inner/pallas_call | solution.py:449
  73.2 0.6 collective-permute-start.9
  73.8 8.2 %collective-permute-done.9 = bf16[2,2,32,1024]{3,2,0,1:T(8,128)(2,1)S(1)} collective-permute-done((bf16[2,2,32,1024]{3,2,0,1:T(8,128)(2,1)S(1)}, bf16[2,2,32,1024]{3,2,0,1:T(8,128)(2,1)S(1)}, u32[]{:S(2)}, u32[]{:S(2)}) %collective-permute-start.9) | collective-permute-done | bytes 262176 | tf_op jit(solution)/shard_map/ppermute | solution.py:58
  82.1 1.6 collective-permute-start.10
  84.9 3.9 %collective-permute-done.10 = bf16[2,32,1024]{2,1,0:T(8,128)(2,1)S(1)} collective-permute-done((bf16[2,32,1024]{2,1,0:T(8,128)(2,1)S(1)}, bf16[2,32,1024]{2,1,0:T(8,128)(2,1)S(1)}, u32[]{:S(2)}, u32[]{:S(2)}) %collective-permute-start.10) | collective-permute-done | bytes 131104 | tf_op jit(solution)/shard_map/ppermute | solution.py:58
  88.8 4.0 %collective-permute-start.11 = (bf16[32,1024]{1,0:T(8,128)(2,1)S(1)}, bf16[32,1024]{1,0:T(8,128)(2,1)S(1)}, u32[]{:S(2)}, u32[]{:S(2)}) collective-permute-start(bf16[32,1024]{1,0:T(8,128)(2,1)S(1)} %slice_bitcast_fusion.10), channel_id=1, source_target_pairs={{0,8},{4,12},{8,0},{12,4},{1,9},{5,13},{9,1},{13,5},{2,10},{6,14},... | collective-permute-start | bytes 196616 | tf_op jit(solution)/shard_map/ppermute | solution.py:58
  92.8 4.3 %collective-permute-done.11 = bf16[32,1024]{1,0:T(8,128)(2,1)S(1)} collective-permute-done((bf16[32,1024]{1,0:T(8,128)(2,1)S(1)}, bf16[32,1024]{1,0:T(8,128)(2,1)S(1)}, u32[]{:S(2)}, u32[]{:S(2)}) %collective-permute-start.11) | collective-permute-done | bytes 65568 | tf_op jit(solution)/shard_map/ppermute | solution.py:58
  97.0 0.6 fusion.7
  98.0 3.3 collective-permute-start.15
  101.3 6.2 %collective-permute-done.15 = bf16[2,2,32,1024]{3,2,0,1:T(8,128)(2,1)S(1)} collective-permute-done((bf16[2,2,32,1024]{3,2,0,1:T(8,128)(2,1)S(1)}, bf16[2,2,32,1024]{3,2,0,1:T(8,128)(2,1)S(1)}, u32[]{:S(2)}, u32[]{:S(2)}) %collective-permute-start.15) | collective-permute-done | bytes 262176 | tf_op jit(solution)/shard_map/ppermute | solution.py:58
  107.7 6.1 %collective-permute-done.16 = bf16[2,32,1024]{2,1,0:T(8,128)(2,1)S(1)} collective-permute-done((bf16[2,32,1024]{2,1,0:T(8,128)(2,1)S(1)}, bf16[2,32,1024]{2,1,0:T(8,128)(2,1)S(1)}, u32[]{:S(2)}, u32[]{:S(2)}) %collective-permute-start.16) | collective-permute-done | bytes 131104 | tf_op jit(solution)/shard_map/ppermute | solution.py:58
  113.8 4.9 %collective-permute-start.17 = (bf16[32,1024]{1,0:T(8,128)(2,1)S(1)}, bf16[32,1024]{1,0:T(8,128)(2,1)S(1)}, u32[]{:S(2)}, u32[]{:S(2)}) collective-permute-start(bf16[32,1024]{1,0:T(8,128)(2,1)S(1)} %slice_bitcast_fusion.8), channel_id=1, source_target_pairs={{0,8},{4,12},{8,0},{12,4},{1,9},{5,13},{9,1},{13,5},{2,10},{6,14},... | collective-permute-start | bytes 196616 | tf_op jit(solution)/shard_map/ppermute | solution.py:58
  118.8 3.3 collective-permute-done.17
  122.1 0.6 fusion.6
  122.8 20.9 %reduce-scatter.2.cloned.1.call-done = bf16[1,32,1280]{2,1,0:T(8,128)(2,1)} async-done(((bf16[16,32,1280]{2,1,0:T(8,128)(2,1)}), bf16[1,32,1280]{2,1,0:T(8,128)(2,1)}) %reduce-scatter.2.cloned.1.call-update) | async-done | bytes 81936 | tf_op jit(solution)/shard_map/reduce_scatter | solution.py:729
  143.8 4.3 %taps.2 = f32[32,512]{1,0:T(8,128)} custom-call(s32[2]{0:T(128)} %lengths_ref.11, f32[512,1024]{1,0:T(8,128)} %get-tuple-element.41.gated_ref, f32[512,512]{1,0:T(8,128)} %get-tuple-element.58.dconv_ref), custom_call_target="tpu_custom_call" | custom-call | flops 4600000000 | bytes 1048576 | tf_op jit(solution)/shard_map/taps/pallas_call | solution.py:513
  148.1 51.3 %all-gather.8.cloned.1.call-done = bf16[512,1024]{1,0:T(8,128)(2,1)} async-done(((bf16[32,1024]{1,0:T(8,128)(2,1)}), bf16[512,1024]{1,0:T(8,128)(2,1)}) %all-gather.8.cloned.1.call-update) | async-done | bytes 1048592 | tf_op jit(solution)/shard_map/all_gather | solution.py:79
  199.4 57.5 %all-gather.10.cloned.1.call-done = bf16[512,1024]{1,0:T(8,128)(2,1)} async-done(((bf16[32,1024]{1,0:T(8,128)(2,1)}), bf16[512,1024]{1,0:T(8,128)(2,1)}) %all-gather.10.cloned.1.call-update) | async-done | bytes 1048592 | tf_op jit(solution)/shard_map/all_gather | solution.py:79
  257.0 4.4 %taps.3 = f32[32,512]{1,0:T(8,128)} custom-call(s32[2]{0:T(128)} %lengths_ref.11, f32[512,1024]{1,0:T(8,128)} %get-tuple-element.41.gated_ref, f32[512,512]{1,0:T(8,128)} %get-tuple-element.62.dconv_ref), custom_call_target="tpu_custom_call" | custom-call | flops 4600000000 | bytes 1048576 | tf_op jit(solution)/shard_map/taps/pallas_call | solution.py:513
  261.4 0.8 pad_maximum_fusion
  262.2 1.5 collective-permute-start.3
  263.7 4.5 %collective-permute-done.3 = f32[32,1024]{1,0:T(8,128)S(1)} collective-permute-done((f32[32,1024]{1,0:T(8,128)S(1)}, f32[32,1024]{1,0:T(8,128)S(1)}, u32[]{:S(2)}, u32[]{:S(2)}) %collective-permute-start.3) | collective-permute-done | bytes 131104 | tf_op jit(solution)/shard_map/ppermute | solution.py:90
  268.2 0.9 fusion.8
  269.0 1.5 collective-permute-start.4
  270.6 3.7 %collective-permute-done.4 = f32[32,1024]{1,0:T(8,128)S(1)} collective-permute-done((f32[32,1024]{1,0:T(8,128)S(1)}, f32[32,1024]{1,0:T(8,128)S(1)}, u32[]{:S(2)}, u32[]{:S(2)}) %collective-permute-start.4) | collective-permute-done | bytes 131104 | tf_op jit(solution)/shard_map/ppermute | solution.py:90
  274.2 0.8 collective-permute-start.5
  275.0 40.4 %all-gather.6.cloned.1.call-done.own_ref = bf16[16,32,1280]{2,1,0:T(8,128)(2,1)} async-done(((bf16[1,32,1280]{2,1,0:T(8,128)(2,1)}), bf16[16,32,1280]{2,1,0:T(8,128)(2,1)}) %all-gather.6.cloned.1.call-update) | async-done | bytes 1310736 | tf_op jit(solution)/shard_map/all_gather | solution.py:79
  315.4 0.7 collective-permute-start.6
  316.1 8.8 %collective-permute-done.6 = f32[32,1024]{1,0:T(8,128)S(1)} collective-permute-done((f32[32,1024]{1,0:T(8,128)S(1)}, f32[32,1024]{1,0:T(8,128)S(1)}, u32[]{:S(2)}, u32[]{:S(2)}) %collective-permute-start.6) | collective-permute-done | bytes 131104 | tf_op jit(solution)/shard_map/ppermute | solution.py:90
  325.1 1.3 collective-permute-done.7
  326.4 0.7 add.72.small_ref
  327.1 1.0 copy-done.5
  328.0 1.0 copy-done.6
  329.0 9.7 %unpack_inner.1 = (f32[1024,2048]{1,0:T(8,128)}, f32[1,1024]{1,0:T(1,128)}) custom-call(s32[1]{0:T(128)} %bitcast.core_ref, f32[32,1024]{1,0:T(8,128)} %add.72.small_ref, bf16[1024,2048]{1,0:T(8,128)(2,1)} %weight_ref.1, f32[1,1024]{1,0:T(1,128)} %bitcast.69, bf16[16,32,1024]{2,1,0:T(8,128)(2,1)} %bitcast.65, bf16[16,32,1024]{2,1,0:T(8,128)(2,1)} %copy-done.5, ...), custom_call_target="tpu_custom_call" | custom-call | flops 10350000128 | bytes 1048576 | tf_op jit(solution)/shard_map/unpack_inner/pallas_call | solution.py:648
  338.7 1.1 copy-done.3
  339.7 5.1 %unpack_top.1 = (f32[1024,1024]{1,0:T(8,128)}, f32[1024,256]{1,0:T(8,128)}, f32[1,1024]{1,0:T(1,128)}, f32[31,1024]{1,0:T(8,128)}, f32[2,1,128]{2,1,0:T(1,128)}) custom-call(s32[1]{0:T(128)} %bitcast.core_ref, f32[32,1024]{1,0:T(8,128)} %add.72.small_ref, bf16[16,32,1280]{2,1,0:T(8,128)(2,1)} %all-gather.6.cloned.1.call-done.own_ref, ...), custom_call_target="tpu_custom_call" | custom-call | flops 5750000128 | bytes 1048576 | tf_op jit(solution)/shard_map/unpack_top/pallas_call | solution.py:609
  344.9 1.3 slice_reduce_fusion
  (60 shorter events, 4.4 us)
Async XLA Ops:
  7.2 136.6 %reduce-scatter.2.cloned.1.call-start = ((), (), s32[]{:S(2)}) async-start(), calls=%async_computation.1 | async-start | bytes 1392640 | tf_op jit(solution)/shard_map/reduce_scatter | solution.py:729
  11.2 19.2 %collective-permute-start = (f32[2,256,256]{2,1,0:T(8,128)}, f32[2,256,256]{2,1,0:T(8,128)S(1)}, u32[]{:S(2)}, u32[]{:S(2)}) collective-permute-start(f32[2,256,256]{2,1,0:T(8,128)} %get-tuple-element.45), channel_id=1, source_target_pairs={{0,16},{16,0},{1,17},{17,1},{2,18},{18,2},{3,19},{19,3},{4,20},{20... | collective-permute-start | bytes 1572872 | tf_op jit(solution)/shard_map/ppermute | solution.py:684
  30.4 0.9 copy-start.7
  42.1 11.2 %copy-start.4 = (bf16[16,32,1280]{2,1,0:T(8,128)(2,1)S(1)}, bf16[16,32,1280]{2,1,0:T(8,128)(2,1)}, u32[]{:S(2)}) copy-start(bf16[16,32,1280]{2,1,0:T(8,128)(2,1)} %get-tuple-element.60) | copy-start | bytes 3932164
  53.2 3.5 %collective-permute-start.1 = (bf16[16,32,1024]{2,1,0:T(8,128)(2,1)}, bf16[16,32,1024]{2,1,0:T(8,128)(2,1)S(1)}, u32[]{:S(2)}, u32[]{:S(2)}) collective-permute-start(bf16[16,32,1024]{2,1,0:T(8,128)(2,1)} %get-tuple-element.57), channel_id=1, source_target_pairs={{0,1},{1,0},{2,3},{3,2},{4,5},{5,4},{6,7},{7,6},{8,9},{9,8},{10,11... | collective-permute-start | bytes 3145736 | tf_op jit(solution)/shard_map/ppermute | solution.py:49
  53.3 6.9 %collective-permute-start.2 = (bf16[16,32,1280]{2,1,0:T(8,128)(2,1)S(1)}, bf16[16,32,1280]{2,1,0:T(8,128)(2,1)S(1)}, u32[]{:S(2)}, u32[]{:S(2)}) collective-permute-start(bf16[16,32,1280]{2,1,0:T(8,128)(2,1)S(1)} %copy-done.4), channel_id=1, source_target_pairs={{0,1},{1,0},{2,3},{3,2},{4,5},{5,4},{6,7},{7,6},{8,9},{9,8},{10,11... | collective-permute-start | bytes 3932168 | tf_op jit(solution)/shard_map/ppermute | solution.py:49
  58.4 1.7 copy-start
  58.5 14.5 %collective-permute-start.8 = (bf16[2,2,2,32,1024]{4,3,1,2,0:T(8,128)(2,1)S(1)}, bf16[2,2,2,32,1024]{4,3,1,2,0:T(8,128)(2,1)S(1)}, u32[]{:S(2)}, u32[]{:S(2)}) collective-permute-start(bf16[2,2,2,32,1024]{4,3,1,2,0:T(8,128)(2,1)S(1)} %copy.24), channel_id=1, source_target_pairs={{0,2},{2,0},{1,3},{3,1},{4,6},{6,4},{5,7},{7,5},{8,10},{10,8},{9,1... | collective-permute-start | bytes 1572872 | tf_op jit(solution)/shard_map/ppermute | solution.py:58
  61.6 137.8 %all-gather.8.cloned.1.call-start = ((), (), s32[]{:S(2)}) async-start(), calls=%async_computation.3 | async-start | bytes 1114112 | tf_op jit(solution)/shard_map/all_gather | solution.py:79
  72.9 10.8 %copy-start.1 = (bf16[16,32,1024]{2,1,0:T(8,128)(2,1)S(1)}, bf16[16,32,1024]{2,1,0:T(8,128)(2,1)}, u32[]{:S(2)}) copy-start(bf16[16,32,1024]{2,1,0:T(8,128)(2,1)} %get-tuple-element.64) | copy-start | bytes 3145732
  72.9 10.8 %collective-permute-start.13 = (bf16[16,32,1024]{2,1,0:T(8,128)(2,1)}, bf16[16,32,1024]{2,1,0:T(8,128)(2,1)S(1)}, u32[]{:S(2)}, u32[]{:S(2)}) collective-permute-start(bf16[16,32,1024]{2,1,0:T(8,128)(2,1)} %get-tuple-element.65), channel_id=1, source_target_pairs={{0,1},{1,0},{2,3},{3,2},{4,5},{5,4},{6,7},{7,6},{8,9},{9,8},{10,11... | collective-permute-start | bytes 3145736 | tf_op jit(solution)/shard_map/ppermute | solution.py:49
  73.2 8.8 %collective-permute-start.9 = (bf16[2,2,32,1024]{3,2,0,1:T(8,128)(2,1)S(1)}, bf16[2,2,32,1024]{3,2,0,1:T(8,128)(2,1)S(1)}, u32[]{:S(2)}, u32[]{:S(2)}) collective-permute-start(bf16[2,2,32,1024]{3,2,0,1:T(8,128)(2,1)S(1)} %slice_bitcast_fusion.2), channel_id=1, source_target_pairs={{0,16},{16,0},{1,17},{17,1},{2,18},{18,2},{3,19},{19,3},{4,20},{20... | collective-permute-start | bytes 786440 | tf_op jit(solution)/shard_map/ppermute | solution.py:58
  82.1 6.7 %collective-permute-start.10 = (bf16[2,32,1024]{2,1,0:T(8,128)(2,1)S(1)}, bf16[2,32,1024]{2,1,0:T(8,128)(2,1)S(1)}, u32[]{:S(2)}, u32[]{:S(2)}) collective-permute-start(bf16[2,32,1024]{2,1,0:T(8,128)(2,1)S(1)} %slice_bitcast_fusion.6), channel_id=1, source_target_pairs={{0,4},{4,0},{8,12},{12,8},{1,5},{5,1},{9,13},{13,9},{2,6},{6,2},{1... | collective-permute-start | bytes 393224 | tf_op jit(solution)/shard_map/ppermute | solution.py:58
  84.3 13.5 %collective-permute-start.14 = (bf16[2,2,2,32,1024]{4,3,1,2,0:T(8,128)(2,1)S(1)}, bf16[2,2,2,32,1024]{4,3,1,2,0:T(8,128)(2,1)S(1)}, u32[]{:S(2)}, u32[]{:S(2)}) collective-permute-start(bf16[2,2,2,32,1024]{4,3,1,2,0:T(8,128)(2,1)S(1)} %copy.26), channel_id=1, source_target_pairs={{0,16},{16,0},{1,17},{17,1},{2,18},{18,2},{3,19},{19,3},{4,20},{20... | collective-permute-start | bytes 1572872 | tf_op jit(solution)/shard_map/ppermute | solution.py:58
  88.8 8.2 %collective-permute-start.11 = (bf16[32,1024]{1,0:T(8,128)(2,1)S(1)}, bf16[32,1024]{1,0:T(8,128)(2,1)S(1)}, u32[]{:S(2)}, u32[]{:S(2)}) collective-permute-start(bf16[32,1024]{1,0:T(8,128)(2,1)S(1)} %slice_bitcast_fusion.10), channel_id=1, source_target_pairs={{0,8},{4,12},{8,0},{12,4},{1,9},{5,13},{9,1},{13,5},{2,10},{6,14},... | collective-permute-start | bytes 196616 | tf_op jit(solution)/shard_map/ppermute | solution.py:58
  97.7 159.3 %all-gather.10.cloned.1.call-start = ((), (), s32[]{:S(2)}) async-start(), calls=%async_computation.4 | async-start | bytes 1114112 | tf_op jit(solution)/shard_map/all_gather | solution.py:79
  98.0 9.5 %collective-permute-start.15 = (bf16[2,2,32,1024]{3,2,0,1:T(8,128)(2,1)S(1)}, bf16[2,2,32,1024]{3,2,0,1:T(8,128)(2,1)S(1)}, u32[]{:S(2)}, u32[]{:S(2)}) collective-permute-start(bf16[2,2,32,1024]{3,2,0,1:T(8,128)(2,1)S(1)} %slice_bitcast_fusion), channel_id=1, source_target_pairs={{0,2},{2,0},{1,3},{3,1},{4,6},{6,4},{5,7},{7,5},{8,10},{10,8},{9,1... | collective-permute-start | bytes 786440 | tf_op jit(solution)/shard_map/ppermute | solution.py:58
  107.6 6.2 %collective-permute-start.16 = (bf16[2,32,1024]{2,1,0:T(8,128)(2,1)S(1)}, bf16[2,32,1024]{2,1,0:T(8,128)(2,1)S(1)}, u32[]{:S(2)}, u32[]{:S(2)}) collective-permute-start(bf16[2,32,1024]{2,1,0:T(8,128)(2,1)S(1)} %slice_bitcast_fusion.4), channel_id=1, source_target_pairs={{0,4},{4,0},{8,12},{12,8},{1,5},{5,1},{9,13},{13,9},{2,6},{6,2},{1... | collective-permute-start | bytes 393224 | tf_op jit(solution)/shard_map/ppermute | solution.py:58
  113.8 8.2 %collective-permute-start.17 = (bf16[32,1024]{1,0:T(8,128)(2,1)S(1)}, bf16[32,1024]{1,0:T(8,128)(2,1)S(1)}, u32[]{:S(2)}, u32[]{:S(2)}) collective-permute-start(bf16[32,1024]{1,0:T(8,128)(2,1)S(1)} %slice_bitcast_fusion.8), channel_id=1, source_target_pairs={{0,8},{4,12},{8,0},{12,4},{1,9},{5,13},{9,1},{13,5},{2,10},{6,14},... | collective-permute-start | bytes 196616 | tf_op jit(solution)/shard_map/ppermute | solution.py:58
  122.8 192.7 %all-gather.6.cloned.1.call-start = ((), (), s32[]{:S(2)}) async-start(), calls=%async_computation.2 | async-start | bytes 1392640 | tf_op jit(solution)/shard_map/all_gather | solution.py:79
  199.4 127.6 %collective-permute-start.12 = (bf16[16,32,1024]{2,1,0:T(8,128)(2,1)}, bf16[16,32,1024]{2,1,0:T(8,128)(2,1)S(1)}, u32[]{:S(2)}, u32[]{:S(2)}) collective-permute-start(bf16[16,32,1024]{2,1,0:T(8,128)(2,1)} %bitcast.64), channel_id=1, source_target_pairs={{0,1},{1,0},{2,3},{3,2},{4,5},{5,4},{6,7},{7,6},{8,9},{9,8},{10,11... | collective-permute-start | bytes 3145736 | tf_op jit(solution)/shard_map/ppermute | solution.py:49
  257.0 70.1 %collective-permute-start.18 = (bf16[16,32,1024]{2,1,0:T(8,128)(2,1)}, bf16[16,32,1024]{2,1,0:T(8,128)(2,1)S(1)}, u32[]{:S(2)}, u32[]{:S(2)}) collective-permute-start(bf16[16,32,1024]{2,1,0:T(8,128)(2,1)} %bitcast.66), channel_id=1, source_target_pairs={{0,1},{1,0},{2,3},{3,2},{4,5},{5,4},{6,7},{7,6},{8,9},{9,8},{10,11... | collective-permute-start | bytes 3145736 | tf_op jit(solution)/shard_map/ppermute | solution.py:49
  257.0 4.4 %copy-start.2 = (f32[32,512]{1,0:T(8,128)S(1)}, f32[32,512]{1,0:T(8,128)}, u32[]{:S(2)}) copy-start(f32[32,512]{1,0:T(8,128)} %taps.2) | copy-start | bytes 196612
  262.2 6.0 %collective-permute-start.3 = (f32[32,1024]{1,0:T(8,128)S(1)}, f32[32,1024]{1,0:T(8,128)S(1)}, u32[]{:S(2)}, u32[]{:S(2)}) collective-permute-start(f32[32,1024]{1,0:T(8,128)S(1)} %pad_maximum_fusion), channel_id=1, source_target_pairs={{0,16},{16,0},{1,17},{17,1},{2,18},{18,2},{3,19},{19,3},{4,20},{20... | collective-permute-start | bytes 393224 | tf_op jit(solution)/shard_map/ppermute | solution.py:90
  269.0 5.2 %collective-permute-start.4 = (f32[32,1024]{1,0:T(8,128)S(1)}, f32[32,1024]{1,0:T(8,128)S(1)}, u32[]{:S(2)}, u32[]{:S(2)}) collective-permute-start(f32[32,1024]{1,0:T(8,128)S(1)} %fusion.8), channel_id=1, source_target_pairs={{0,2},{2,0},{1,3},{3,1},{4,6},{6,4},{5,7},{7,5},{8,10},{10,8},{9,1... | collective-permute-start | bytes 393224 | tf_op jit(solution)/shard_map/ppermute | solution.py:90
  274.2 41.2 %collective-permute-start.5 = (f32[32,1024]{1,0:T(8,128)S(1)}, f32[32,1024]{1,0:T(8,128)S(1)}, u32[]{:S(2)}, u32[]{:S(2)}) collective-permute-start(f32[32,1024]{1,0:T(8,128)S(1)} %add.69), channel_id=1, source_target_pairs={{0,4},{4,0},{8,12},{12,8},{1,5},{5,1},{9,13},{13,9},{2,6},{6,2},{1... | collective-permute-start | bytes 393224 | tf_op jit(solution)/shard_map/ppermute | solution.py:90
  315.4 23.3 %collective-permute-start.19 = (bf16[16,32,1280]{2,1,0:T(8,128)(2,1)}, bf16[16,32,1280]{2,1,0:T(8,128)(2,1)S(1)}, u32[]{:S(2)}, u32[]{:S(2)}) collective-permute-start(bf16[16,32,1280]{2,1,0:T(8,128)(2,1)} %all-gather.6.cloned.1.call-done.own_ref), channel_id=1, source_target_pairs={{0,1},{1,0},{2,3},{3,2},{4,5},{5,4},{6,7},{7,6},{8,9},{9,8},{10,11... | collective-permute-start | bytes 3932168 | tf_op jit(solution)/shard_map/ppermute | solution.py:49
  315.4 9.5 %collective-permute-start.6 = (f32[32,1024]{1,0:T(8,128)S(1)}, f32[32,1024]{1,0:T(8,128)S(1)}, u32[]{:S(2)}, u32[]{:S(2)}) collective-permute-start(f32[32,1024]{1,0:T(8,128)S(1)} %add.70), channel_id=1, source_target_pairs={{0,8},{4,12},{8,0},{12,4},{1,9},{5,13},{9,1},{13,5},{2,10},{6,14},... | collective-permute-start | bytes 393224 | tf_op jit(solution)/shard_map/ppermute | solution.py:90
  325.0 1.4 collective-permute-start.7
  327.0 1.0 copy-start.5
  328.0 1.0 copy-start.6
  338.7 1.1 copy-start.3
Sparse Core Ops, SparseCore 0:
  61.7 81.9 reduce-scatter.1
  147.1 52.3 all-gather.7
  202.8 54.1 all-gather.9
  259.6 55.7 all-gather.5

commit v4 on v3

--- a/solution.py
+++ b/solution.py
@@ -8,7 +8,7 @@
 from jax.sharding import PartitionSpec as P
 
 TEACHERS = 4
-PLACES = 16
+PLACES = 8
 WIDE = 256
 LANES = 128
 TILE = 128
@@ -38,61 +38,46 @@
     return pl.BlockSpec(shape, lambda i, *_: (0,) * len(shape))
 
 
-XY = ("member", "near")
-YX = ("near", "member")
 FAR = "far"
 REST = "rest"
 CORE = "core"
 
 
-def other_core(values):
-    return lax.ppermute(values, CORE, [(0, 1), (1, 0)])
-
-
-def sum_core(send, keep):
-    return (keep.astype(F32) + other_core(send).astype(F32)).astype(BF16)
-
-
-def halve(pieces, dim, axis, bit):
+def exchange(values, axis, bit=1):
     size = lax.axis_size(axis)
-    got = lax.ppermute(
-        lax.index_in_dim(pieces, 1, dim, keepdims=False), axis, [(i, i ^ bit) for i in range(size)]
-    )
-    kept = lax.index_in_dim(pieces, 0, dim, keepdims=False)
-    return (kept.astype(F32) + got.astype(F32)).astype(pieces.dtype)
-
-
-def sum_chips(pieces, order):
-    pieces = pieces.reshape((2, 2, 2, 2) + pieces.shape[1:])
-    pieces = halve(pieces, 0, order[0], 1)
-    pieces = halve(pieces, 0, order[1], 1)
-    pieces = halve(pieces, 1, FAR, 1)
-    pieces = halve(pieces, 0, FAR, 2)
-    return over_rest(pieces)
-
-
-def over_rest(values):
+    return lax.ppermute(values, axis, [(i, i ^ bit) for i in range(size)])
+
+
+def add(own, other):
+    return (own.astype(F32) + other.astype(F32)).astype(own.dtype)
+
+
+def halve(pieces, axis):
+    half = pieces.shape[1] // 2
+    return add(pieces[:, :half], exchange(pieces[:, half:], axis))
+
+
+def double(pieces):
+    pieces = add(pieces, exchange(pieces, FAR, 2))
+    return lax.psum(pieces, REST) if lax.axis_size(REST) > 1 else pieces
+
+
+def gather(pieces, axis):
+    return jnp.concatenate([pieces, exchange(pieces, axis)], axis=1)
+
+
+def own_place(order):
+    place = lax.axis_index(order[0]) * 4 + lax.axis_index(order[1]) * 2 + (lax.axis_index(FAR) & 1)
+    return place.astype(jnp.int32)
+
+
+def all_sum(values):
+    for axis, bit in ((CORE, 1), ("member", 1), ("near", 1), (FAR, 1), (FAR, 2)):
+        values = values + exchange(values, axis, bit)
     return lax.psum(values, REST) if lax.axis_size(REST) > 1 else values
 
 
-def gather(shard, order):
-    return lax.all_gather(shard, order + (FAR,), axis=0, tiled=False)
-
-
-def own_place(order):
-    place = lax.axis_index(order[0]) * 8 + lax.axis_index(order[1]) * 4 + lax.axis_index(FAR)
-    return place.astype(jnp.int32)
-
-
-def all_sum(values):
-    for axis, bit in (("member", 1), ("near", 1), (FAR, 1), (FAR, 2)):
-        size = lax.axis_size(axis)
-        values = values + lax.ppermute(values, axis, [(i, i ^ bit) for i in range(size)])
-    values = over_rest(values)
-    return values + other_core(values)
-
-
-def write_pieces(own_ref, product, send_ref, keep_ref, columns):
+def write_pieces(own_ref, product, send_ref, keep_ref, group):
     rows = keep_ref.shape[-2]
     core, place = own_ref[0], own_ref[1]
 
@@ -100,11 +85,11 @@
         base = (piece ^ place) * (2 * rows)
         kept = pl.multiple_of(base + core * rows, rows)
         sent = pl.multiple_of(base + (1 - core) * rows, rows)
-        keep_ref[piece, :, columns] = product[pl.ds(kept, rows), :].astype(BF16)
-        send_ref[piece, :, columns] = product[pl.ds(sent, rows), :].astype(BF16)
+        keep_ref[group, piece] = product[pl.ds(kept, rows), :].astype(BF16)
+        send_ref[group, piece] = product[pl.ds(sent, rows), :].astype(BF16)
         return carry
 
-    lax.fori_loop(0, keep_ref.shape[0], one, 0)
+    lax.fori_loop(0, keep_ref.shape[1], one, 0)
 
 
 def teacher_kernel(member_ref, logits_ref, give_ref, keep_ref, *, own_count):
@@ -349,7 +334,7 @@
     width = dresidual_ref.shape[1]
     product_ref[:, :width] = dot(active_ref[...], dresidual_ref[...], 0, 0)
     product_ref[:, width:] = dot(final_ref[...], dlogits_ref[...], 0, 0)
-    write_pieces(own_ref, product_ref, send_ref, keep_ref, slice(None))
+    write_pieces(own_ref, product_ref, send_ref, keep_ref, 0)
 
 
 def outer(own, active, dresidual, final, dlogits):
@@ -357,9 +342,9 @@
     half_out = dresidual.shape[1] // 2
     half_head = dlogits.shape[1] // 2
     width = half_out + half_head
-    piece = (PLACES, model // (2 * PLACES))
-    shape = jax.ShapeDtypeStruct(piece + (2 * width,), BF16)
-    out = pl.BlockSpec(piece + (width,), lambda i: (0, 0, i))
+    piece = (PLACES, model // (2 * PLACES), width)
+    shape = jax.ShapeDtypeStruct((2,) + piece, BF16)
+    out = pl.BlockSpec((1,) + piece, lambda i: (i, 0, 0, 0))
     return pl.pallas_call(
         outer_kernel,
         grid=(2,),
@@ -433,8 +418,7 @@
 
     for group, source in ((0, dvalue_ref), (1, dgate_ref)):
         product_ref[...] = dot(normed_ref[...], source[...], 0, 0)
-        columns = slice(group * WIDE, (group + 1) * WIDE)
-        write_pieces(own_ref, product_ref, send_ref, keep_ref, columns)
+        write_pieces(own_ref, product_ref, send_ref, keep_ref, group)
 
 
 def inner(own, lengths, dresidual, weight_out, slope, gated, gate, normed, depth, chunk, utterances):
@@ -443,9 +427,9 @@
     steps = model // WIDE // CHUNKS
     first = chunk * steps
     column = pl.BlockSpec((rows, WIDE), lambda i: (0, first + i))
-    piece = (PLACES, model // (2 * PLACES))
-    shape = jax.ShapeDtypeStruct(piece + (steps * 2 * WIDE,), BF16)
-    out = pl.BlockSpec(piece + (2 * WIDE,), lambda i: (0, 0, i))
+    piece = (2, PLACES, model // (2 * PLACES))
+    shape = jax.ShapeDtypeStruct(piece + (steps * WIDE,), BF16)
+    out = pl.BlockSpec(piece + (WIDE,), lambda i: (0, 0, 0, i))
     return pl.pallas_call(
         inner_kernel,
         grid=(steps,),
@@ -530,27 +514,30 @@
     )(lengths, gated, dconv)
 
 
-def gain_row(weight, grad, gain):
+def gain_row(weight, grad):
     along = jnp.sum(weight.astype(F32) * grad, axis=1, keepdims=True)
-    return jnp.broadcast_to(along, (along.shape[0], LANES)).T[0:1, :] / gain
-
-
-def write_rows(core, pieces, other, scale, targets):
-    rows = pieces.shape[1]
-    for index in range(pieces.shape[0]):
-        for side, source in ((core, pieces), (1 - core, other)):
+    return jnp.broadcast_to(along, (along.shape[0], LANES)).T[0:1, :]
+
+
+def write_rows(own_ref, step, piece_refs, group, scale, targets):
+    mine_ref, other_ref = piece_refs
+    places, rows = mine_ref.shape[1:3]
+    core, place = own_ref[0], own_ref[1]
+    for index in range(places):
+        piece = index ^ (place & (places - 1))
+        for side, source in ((core, mine_ref), (1 - core, other_ref)):
             here = pl.ds(pl.multiple_of(index * 2 * rows + side * rows, rows), rows)
             for target, there, first, width in targets:
                 target[here, there : there + width] = (
-                    source[index, :, first : first + width].astype(F32) * scale
+                    source[group, piece, :, first : first + width].astype(F32) * scale
                 )
 
 
 def unpack_top_kernel(
     utts,
-    core_ref,
+    own_ref,
     small_ref,
-    own_ref,
+    mine_ref,
     other_ref,
     head_ref,
     gain_ref,
@@ -565,50 +552,33 @@
     scale = utts / small_ref[taps:, 0:1]
     half_out = wout_ref.shape[1] // 2
     half_head = dhead_ref.shape[1] // 2
-    targets = []
-    for half in range(2):
-        first = half * (half_out + half_head)
-        targets.append((wout_ref, half * half_out, first, half_out))
-        targets.append((dhead_ref, half * half_head, first + half_out, half_head))
-    write_rows(core_ref[0], own_ref, other_ref, scale, targets)
-    dgain_ref[...] = gain_row(head_ref[...], dhead_ref[...], gain_ref[...])
+    for group in range(2):
+        targets = (
+            (wout_ref, group * half_out, 0, half_out),
+            (dhead_ref, group * half_head, half_out, half_head),
+        )
+        write_rows(own_ref, pl.program_id(0), (mine_ref, other_ref), group, scale, targets)
+    dgain_ref[...] = gain_row(head_ref[...], dhead_ref[...]) / gain_ref[...]
     depth_ref[...] = small_ref[:taps, :] * scale
     loss_ref[...] = losses_ref[...] * scale[None]
 
 
-def unpack_inner_kernel(utts, core_ref, small_ref, weight_ref, gain_ref, *refs):
-    pieces, (win_ref, dgain_ref) = refs[:-2], refs[-2:]
-    scale = utts / small_ref[small_ref.shape[0] - 1 :, 0:1]
-    half_in = win_ref.shape[1] // 2
-    column = 0
-    for chunk in range(len(pieces) // 2):
-        own_ref, other_ref = pieces[2 * chunk : 2 * chunk + 2]
-        targets = []
-        for first in range(0, own_ref.shape[2], 2 * WIDE):
-            targets.append((win_ref, column, first, WIDE))
-            targets.append((win_ref, half_in + column, first + WIDE, WIDE))
-            column += WIDE
-        write_rows(core_ref[0], own_ref, other_ref, scale, targets)
-    dgain_ref[...] = gain_row(weight_ref[...], win_ref[...], gain_ref[...])
-
-
-def piece_spec(array, steps):
-    return pl.BlockSpec((array.shape[0] // steps,) + array.shape[1:], lambda i: (i, 0, 0))
-
-
-def unpack_top(utts, core, small, own, other, head, gain, losses, width_out):
+def unpack_top(utts, own, small, mine, other, head, gain, losses, width_out):
     steps = 4
     model, symbols = head.shape
     rows = model // steps
     taps = small.shape[0] - 1
-    row = pl.BlockSpec((1, rows), lambda i: (0, i))
+    places = PLACES // steps
+    row = pl.BlockSpec((1, rows), lambda i, own_ref: (0, i))
+    piece = pl.BlockSpec(
+        (2, places) + mine.shape[2:], lambda i, own_ref: (0, i ^ (own_ref[1] // places), 0, 0)
+    )
 
     def block(width):
-        return pl.BlockSpec((rows, width), lambda i: (i, 0))
+        return pl.BlockSpec((rows, width), lambda i, own_ref: (i, 0))
 
     return pl.pallas_call(
         functools.partial(unpack_top_kernel, utts),
-        grid=(steps,),
         out_shape=(
             jax.ShapeDtypeStruct((model, width_out), F32),
             jax.ShapeDtypeStruct((model, symbols), F32),
@@ -616,49 +586,85 @@
             jax.ShapeDtypeStruct((taps, model), F32),
             jax.ShapeDtypeStruct(losses.shape, F32),
         ),
-        in_specs=[
-            SMEM_SPEC,
-            fixed(*small.shape),
-            piece_spec(own, steps),
-            piece_spec(other, steps),
-            block(symbols),
-            row,
-            fixed(*losses.shape),
-        ],
-        out_specs=(
-            block(width_out),
-            block(symbols),
-            row,
-            fixed(taps, model),
-            fixed(*losses.shape),
+        grid_spec=pltpu.PrefetchScalarGridSpec(
+            num_scalar_prefetch=1,
+            grid=(steps,),
+            in_specs=[
+                fixed(*small.shape),
+                piece,
+                piece,
+                block(symbols),
+                row,
+                fixed(*losses.shape),
+            ],
+            out_specs=(
+                block(width_out),
+                block(symbols),
+                row,
+                fixed(taps, model),
+                fixed(*losses.shape),
+            ),
         ),
         compiler_params=params(),
         cost_estimate=cost(5),
         name="unpack_top",
-    )(core, small, own, other, head, gain, losses)
-
-
-def unpack_inner(utts, core, small, sums, weight, gain):
-    steps = 8
+    )(own, small, mine, other, head, gain, losses)
+
+
+def unpack_inner_kernel(
+    utts, last, own_ref, small_ref, mine_ref, other_ref, weight_ref, gain_ref, *refs
+):
+    win_ref, dgain_ref = refs[-2:]
+    scale = utts / small_ref[small_ref.shape[0] - 1 :, 0:1]
+    targets = ((win_ref, 0, 0, win_ref.shape[1]),)
+    write_rows(own_ref, pl.program_id(0), (mine_ref, other_ref), 0, scale, targets)
+    row = gain_row(weight_ref[...], win_ref[...])
+
+    @pl.when(pl.program_id(1) == 0)
+    def _():
+        dgain_ref[...] = row + refs[1][...] if len(refs) > 2 else row
+
+    @pl.when(pl.program_id(1) == 1)
+    def _():
+        total = dgain_ref[...] + row
+        dgain_ref[...] = total / gain_ref[...] if last else total
+
+
+def unpack_inner(utts, own, small, mine, other, weight, gain, chunk, before):
+    steps = 2
     model, width = weight.shape
     rows = model // steps
-    row = pl.BlockSpec((1, rows), lambda i: (0, i))
-    block = pl.BlockSpec((rows, width), lambda i: (i, 0))
-    pieces = [array for pair in sums for array in pair]
+    wide = mine.shape[3]
+    places = PLACES // steps
+    row = pl.BlockSpec((1, rows), lambda i, j, own_ref: (0, i))
+    block = pl.BlockSpec((rows, wide), lambda i, j, own_ref: (i, j * CHUNKS + chunk))
+    piece = pl.BlockSpec(
+        (1, places) + mine.shape[2:], lambda i, j, own_ref: (j, i ^ (own_ref[1] // places), 0, 0)
+    )
     return pl.pallas_call(
-        functools.partial(unpack_inner_kernel, utts),
-        grid=(steps,),
+        functools.partial(unpack_inner_kernel, utts, chunk == CHUNKS - 1),
         out_shape=(
             jax.ShapeDtypeStruct((model, width), F32),
             jax.ShapeDtypeStruct((1, model), F32),
         ),
-        in_specs=[SMEM_SPEC, fixed(*small.shape), block, row]
-        + [piece_spec(array, steps) for array in pieces],
-        out_specs=(block, row),
+        grid_spec=pltpu.PrefetchScalarGridSpec(
+            num_scalar_prefetch=1,
+            grid=(steps, 2),
+            in_specs=[
+                pl.BlockSpec(small.shape, lambda i, j, own_ref: (0, 0)),
+                piece,
+                piece,
+                block,
+                row,
+            ]
+            + ([pl.BlockSpec(memory_space=pl.ANY), row] if before else []),
+            out_specs=(block, row),
+        ),
+        input_output_aliases={6: 0} if before else {},
         compiler_params=params(),
-        cost_estimate=cost(9),
+        cost_estimate=cost(4),
         name="unpack_inner",
-    )(core, small, weight, gain, *pieces)
+    )(own, small, mine, other, weight, gain, *before)
 
 
 def on_device(
@@ -672,16 +678,20 @@
     gain_out,
     head_weight,
 ):
-    count = lax.axis_size(XY) * lax.axis_size(FAR) * lax.axis_size(REST) * lax.axis_size(CORE)
+    count = 1
+    for axis in ("member", "near", FAR, REST, CORE):
+        count *= lax.axis_size(axis)
     member = lax.axis_index("member").astype(jnp.int32)[None]
-    core = lax.axis_index(CORE).astype(jnp.int32)[None]
+    core = lax.axis_index(CORE).astype(jnp.int32)
+    orders = (("near", "member"), ("member", "near"))
+    owns = [jnp.stack([core, own_place(order)]) for order in orders]
     taps, model = weight_depth.shape
     utterances, frames, _ = features.shape
     utts = float(utterances * count)
     tie = lax.optimization_barrier
 
     give, kept = teacher_sums(member, teacher_logits, utterances)
-    got = lax.ppermute(give, "member", [(0, 1), (1, 0)])
+    got = exchange(give, "member")
     flat = features.reshape(utterances * frames, model)
     normed, gated, gate, slope, active, residual = forward(
         lengths, flat, gain_conv[None], weight_in, weight_depth, weight_out, utterances
@@ -690,9 +700,9 @@
         lengths, residual, gain_out[None], head_weight, kept, got
     )
 
-    def weight_in_chunk(chunk, order, dresidual):
-        return inner(
-            jnp.stack([core[0], own_place(order)]),
+    def weight_in_chunk(chunk, dresidual):
+        send, keep, dconv = inner(
+            owns[chunk],
             lengths,
             dresidual,
             weight_out,
@@ -704,49 +714,54 @@
             chunk,
             utterances,
         )
-
-    unordered = jnp.stack([core[0], jnp.int32(0)])
-    send, keep = outer(unordered, active, dresidual, final, dlogits)
+        return add(keep, exchange(send, CORE)), dconv
+
+    def chip_sums(pieces, order):
+        pieces = double(halve(halve(pieces, order[1]), FAR))
+        return gather(gather(gather(pieces, FAR), order[1]), order[0])
+
+    send, keep = outer(owns[1], active, dresidual, final, dlogits)
     send, keep, dresidual = tie((send, keep, dresidual))
-    top_sum = sum_core(send, keep)
-    inner_sums = []
-    dconvs = []
-    for chunk in range(CHUNKS):
-        order = XY if chunk % 2 else YX
-        send, keep, dconv = weight_in_chunk(chunk, order, dresidual)
-        inner_sums.append(sum_core(send, keep))
-        dconvs.append(dconv)
-        if chunk == 0:
-            top_sum, dresidual = tie((top_sum, dresidual))
-    dconvs[0], inner_sums[0] = tie((dconvs[0], inner_sums[0]))
-    small = jnp.concatenate(
-        [
-            tap_sums(lengths, gated, dconv, taps, chunk, utterances)
-            for chunk, dconv in enumerate(dconvs)
-        ],
-        axis=1,
-    )
-    top_own = over_rest(lax.psum_scatter(top_sum, XY + (FAR,), scatter_dimension=0, tiled=False))
-    top_all = gather(top_own, XY)
-    top_other = other_core(top_all)
-    small = all_sum(small)
-    pairs = []
-    for chunk, values in enumerate(inner_sums):
-        order = XY if chunk % 2 else YX
-        every = gather(sum_chips(values, order), order)
-        pairs.append((every, other_core(every)))
+    top_sum = add(keep, exchange(send, CORE))
+    first_sum, first_dconv = weight_in_chunk(0, dresidual)
+    top_sum, dresidual = tie((top_sum, dresidual))
+    top_sum = halve(top_sum, orders[1][0])
+    second_sum, second_dconv = weight_in_chunk(1, dresidual)
+    top_sum, first_sum, first_dconv = tie((top_sum, first_sum, first_dconv))
+    first_sum = halve(first_sum, orders[0][0])
+    first_taps = tap_sums(lengths, gated, first_dconv, taps, 0, utterances)
+    second_sum, second_dconv = tie((second_sum, second_dconv))
+    second_sum = halve(second_sum, orders[1][0])
+    second_taps = tap_sums(lengths, gated, second_dconv, taps, 1, utterances)
+    small = all_sum(jnp.concatenate([first_taps, second_taps], axis=1))
+
+    top_all = chip_sums(top_sum, orders[1])
     grad_out, grad_head, by_head, grad_depth, losses = unpack_top(
         utts,
-        core,
+        owns[1],
         small,
         top_all,
-        top_other,
+        exchange(top_all, CORE),
         head_weight,
         gain_out[None],
         losses,
         weight_out.shape[1],
     )
-    grad_in, by_in = unpack_inner(utts, core, small, pairs, weight_in, gain_conv[None])
+    unpacked = ()
+    for chunk, values in enumerate((first_sum, second_sum)):
+        every = chip_sums(values, orders[chunk])
+        unpacked = unpack_inner(
+            utts,
+            owns[chunk],
+            small,
+            every,
+            exchange(every, CORE),
+            weight_in,
+            gain_conv[None],
+            chunk,
+            unpacked,
+        )
+    grad_in, by_in = unpacked
     return (
         by_in.reshape(model),
         grad_in,
@@ -761,7 +776,7 @@
 def solution(mesh):
     members, others = mesh.devices.shape
     near, cores = 2, 2
-    far = PLACES // (members * near)
+    far = 2 * PLACES // (members * near)
     rest = others // (far * near * cores)
     split = jax.sharding.Mesh(
         mesh.devices.reshape(members, rest, far, near, cores),

time: 353 us -> 179 us (0.51)
  waiting for transfers between devices: 223 us -> 51.9 us
  between operations: 14 us -> 1.08 us
  starting transfers between devices: 25.1 us -> 35.7 us
  other arithmetic: 8.98 us -> 5.34 us
    all_gather x3 -> x0, waiting for transfers between devices: 149 us -> none  [gather(): return lax.all_gather(shard, order + (FAR,), axis=0, tiled=False)]
    reduce_scatter x1 -> x0, waiting for transfers between devices: 20.9 us -> none  [on_device(): lax.psum_scatter(top_sum, XY + (FAR,), scatter_dimension=0, tiled=False)]
    ppermute x20 -> x33, starting transfers between devices: 24.8 us -> 35.7 us  [exchange(): return lax.ppermute(values, axis, [(i, i ^ bit) for i in range(size)])]
    pallas_call x2 -> x3, Pallas kernels: 14.8 us -> 18 us  [the longest x2 12.3 us: unpack_inner(): pl.pallas_call(functools.partial(unpack_inner_kernel, utts, chunk == CHUN...]
    ppermute x20 -> x33, waiting for transfers between devices: 53.2 us -> 51.9 us  [exchange(): return lax.ppermute(values, axis, [(i, i ^ bit) for i in range(size)])]
  transfers between devices with their start and end apart: 24 -> 33, of which waited for: 15 -> 18; matrix products, arithmetic and copies ran while one was open for 3% -> 4% of each run, Pallas kernels for 13% -> 32%
where the time goes in v4:
time: 179 us; the launch traced here: 178 us
  Pallas kernels  78 us (44%)
  waiting for transfers between devices  51.9 us (29%)
  starting transfers between devices  35.7 us (20%)
  local copies, waits for them, and re-layouts  6.12 us (3%)
  other arithmetic  5.34 us (3%)
    ppermute x33, waiting for transfers between devices, exchange(): return lax.ppermute(values, axis, [(i, i ^ bit) for i in range(size)])  51.9 us
    ppermute x33, starting transfers between devices, exchange(): return lax.ppermute(values, axis, [(i, i ^ bit) for i in range(size)])  35.7 us
    pallas_call x2, Pallas kernels, inner(): pl.pallas_call(inner_kernel, grid=(steps,), out_shape=(shape, shape, jax....  21.7 us
    pallas_call x1, Pallas kernels, forward(): pl.pallas_call(forward_kernel, grid=(steps,), out_shape=(narrow, wide, wi...  15 us
    pallas_call x2, Pallas kernels, unpack_inner(): pl.pallas_call(functools.partial(unpack_inner_kernel, utts, chunk == CHUN...  12.3 us
    pallas_call x2, Pallas kernels, tap_sums(): pl.pallas_call(taps_kernel, grid=(steps,), out_shape=jax.ShapeDtypeStruct...  8.65 us
    pallas_call x1, Pallas kernels, unpack_top(): pl.pallas_call(functools.partial(unpack_top_kernel, utts), out_shape=(jax...  5.68 us
    pallas_call x1, Pallas kernels, outer(): pl.pallas_call(outer_kernel, grid=(2,), out_shape=(shape, shape), in_spec...  5.34 us
  transfers between devices with their start and end apart: 33, of which 18 were waited for; matrix products, arithmetic and copies ran while one was open for 4% of the time, Pallas kernels for 32%

profile of v4, /device:TPU:0, one launch (start us, length us, event | category | flops | bytes accessed | tf_op | source)
XLA Modules:
  0.0 178.2 jit_solution(5777052874041872908)
XLA Ops:
  0.6 4.0 %teachers.1 = (f32[2,256,256]{2,1,0:T(8,128)}, f32[2,256,256]{2,1,0:T(8,128)}) custom-call(s32[1]{0:T(128)} %bitcast.5.member_ref, bf16[2,4,256,256]{3,2,1,0:T(8,128)(2,1)} %logits_ref.1), custom_call_target="tpu_custom_call" | custom-call | flops 4600000000 | bytes 1048576 | tf_op jit(solution)/shard_map/teachers/pallas_call | solution.py:122
  4.6 2.9 %collective-permute-start = (f32[2,256,256]{2,1,0:T(8,128)}, f32[2,256,256]{2,1,0:T(8,128)S(1)}, u32[]{:S(2)}, u32[]{:S(2)}) collective-permute-start(f32[2,256,256]{2,1,0:T(8,128)} %get-tuple-element.50), channel_id=1, source_target_pairs={{0,16},{16,0},{1,17},{17,1},{2,18},{18,2},{3,19},{19,3},{4,20},{20... | collective-permute-start | bytes 1572872 | tf_op jit(solution)/shard_map/ppermute | solution.py:48
  7.6 15.0 %forward.1 = (bf16[512,1024]{1,0:T(8,128)(2,1)}, f32[512,1024]{1,0:T(8,128)}, f32[512,1024]{1,0:T(8,128)}, f32[512,1024]{1,0:T(8,128)}, bf16[512,1024]{1,0:T(8,128)(2,1)}, /*index=5*/f32[512,1024]{1,0:T(8,128)}) custom-call(s32[2]{0:T(128)} %lengths_ref.11, bf16[512,1024]{1,0:T(8,128)(2,1)} %bitcast.9, f32[1,1024]{1,0:T(1,128)} %bitcast.12, ...), custom_call_target="tpu_custom_call" | custom-call | flops 17250000896 | bytes 1048576 | tf_op jit(solution)/shard_map/forward/pallas_call | solution.py:244
  23.2 0.8 copy-done.11
  24.0 5.3 %top.1 = (f32[2,1,128]{2,1,0:T(1,128)}, bf16[512,1024]{1,0:T(8,128)(2,1)}, bf16[512,256]{1,0:T(8,128)(2,1)}, bf16[512,1024]{1,0:T(8,128)(2,1)}) custom-call(s32[2]{0:T(128)} %lengths_ref.11, f32[512,1024]{1,0:T(8,128)} %get-tuple-element.48.residual_ref, f32[1,1024]{1,0:T(1,128)} %bitcast.10, bf16[1024,256]{1,0:T(8,128)(2,1)} %head_ref.3, ...), custom_call_target="tpu_custom_call" | custom-call | flops 5750000128 | bytes 1048576 | tf_op jit(solution)/shard_map/top/pallas_call | solution.py:309
  29.3 5.3 %outer.1 = (bf16[2,8,64,640]{3,2,1,0:T(8,128)(2,1)}, bf16[2,8,64,640]{3,2,1,0:T(8,128)(2,1)}) custom-call(s32[2]{0:T(128)} %pad_add_fusion.own_ref, bf16[512,1024]{1,0:T(8,128)(2,1)} %get-tuple-element.47.active_ref, bf16[512,1024]{1,0:T(8,128)(2,1)} %get-tuple-element.67.dresidual_ref, bf16[512,1024]{1,0:T(8,128)(2,1)} %get-tuple-element.52.final_ref, ...), custom_call_target="tpu_custom_call" | custom-call | flops 5750000128 | bytes 1048576 | tf_op jit(solution)/shard_map/outer/pallas_call | solution.py:348
  35.3 10.9 %inner.2 = (bf16[2,8,64,512]{3,2,1,0:T(8,128)(2,1)}, bf16[2,8,64,512]{3,2,1,0:T(8,128)(2,1)}, f32[512,512]{1,0:T(8,128)}) custom-call(s32[2]{0:T(128)} %pad_add_fusion.1.own_ref, s32[2]{0:T(128)} %lengths_ref.11, bf16[512,1024]{1,0:T(8,128)(2,1)} %get-tuple-element.67.dresidual_ref, bf16[1024,1024]{1,0:T(8,128)(2,1)} %out_weight_ref.5, ...), custom_call_target="tpu_custom_call" | custom-call | flops 12650000384 | bytes 1048576 | tf_op jit(solution)/shard_map/inner/pallas_call | solution.py:433
  47.2 10.9 %inner.3 = (bf16[2,8,64,512]{3,2,1,0:T(8,128)(2,1)}, bf16[2,8,64,512]{3,2,1,0:T(8,128)(2,1)}, f32[512,512]{1,0:T(8,128)}) custom-call(s32[2]{0:T(128)} %pad_add_fusion.own_ref, s32[2]{0:T(128)} %lengths_ref.11, bf16[512,1024]{1,0:T(8,128)(2,1)} %get-tuple-element.67.dresidual_ref, bf16[1024,1024]{1,0:T(8,128)(2,1)} %out_weight_ref.5, ...), custom_call_target="tpu_custom_call" | custom-call | flops 12650000384 | bytes 1048576 | tf_op jit(solution)/shard_map/inner/pallas_call | solution.py:433
  58.4 5.4 %collective-permute-done.2 = bf16[2,4,64,640]{3,2,1,0:T(8,128)(2,1)S(1)} collective-permute-done((bf16[2,4,64,640]{3,2,1,0:T(8,128)(2,1)S(1)}, bf16[2,4,64,640]{3,2,1,0:T(8,128)(2,1)S(1)}, u32[]{:S(2)}, u32[]{:S(2)}) %collective-permute-start.2) | collective-permute-done | bytes 655392 | tf_op jit(solution)/shard_map/ppermute | solution.py:48
  64.0 1.6 collective-permute-start.26
  66.2 8.5 %collective-permute-done.26 = bf16[2,2,64,640]{3,2,1,0:T(8,128)(2,1)S(1)} collective-permute-done((bf16[2,2,64,640]{3,2,1,0:T(8,128)(2,1)S(1)}, bf16[2,2,64,640]{3,2,1,0:T(8,128)(2,1)S(1)}, u32[]{:S(2)}, u32[]{:S(2)}) %collective-permute-start.26) | collective-permute-done | bytes 327712 | tf_op jit(solution)/shard_map/ppermute | solution.py:48
  74.9 1.6 collective-permute-start.27
  77.5 4.4 %collective-permute-done.27 = bf16[2,1,64,640]{3,2,1,0:T(8,128)(2,1)S(1)} collective-permute-done((bf16[2,1,64,640]{3,2,1,0:T(8,128)(2,1)S(1)}, bf16[2,1,64,640]{3,2,1,0:T(8,128)(2,1)S(1)}, u32[]{:S(2)}, u32[]{:S(2)}) %collective-permute-start.27) | collective-permute-done | bytes 163872 | tf_op jit(solution)/shard_map/ppermute | solution.py:48
  82.0 2.6 %collective-permute-start.28 = (bf16[2,1,64,640]{3,2,1,0:T(8,128)(2,1)S(1)}, bf16[2,1,64,640]{3,2,1,0:T(8,128)(2,1)S(1)}, u32[]{:S(2)}, u32[]{:S(2)}) collective-permute-start(bf16[2,1,64,640]{3,2,1,0:T(8,128)(2,1)S(1)} %add_convert_fusion.10), channel_id=1, source_target_pairs={{0,8},{4,12},{8,0},{12,4},{1,9},{5,13},{9,1},{13,5},{2,10},{6,14},... | collective-permute-start | bytes 491528 | tf_op jit(solution)/shard_map/ppermute | solution.py:48
  85.4 4.3 %taps.2 = f32[32,512]{1,0:T(8,128)} custom-call(s32[2]{0:T(128)} %lengths_ref.11, f32[512,1024]{1,0:T(8,128)} %get-tuple-element.46.gated_ref, f32[512,512]{1,0:T(8,128)} %get-tuple-element.66.dconv_ref), custom_call_target="tpu_custom_call" | custom-call | flops 4600000000 | bytes 1048576 | tf_op jit(solution)/shard_map/taps/pallas_call | solution.py:497
  90.1 0.8 collective-permute-start.29
  90.9 1.7 collective-permute-done.19
  93.3 1.6 collective-permute-start.11
  94.9 1.9 %collective-permute-done.29 = bf16[2,1,64,640]{3,2,1,0:T(8,128)(2,1)S(1)} collective-permute-done((bf16[2,1,64,640]{3,2,1,0:T(8,128)(2,1)S(1)}, bf16[2,1,64,640]{3,2,1,0:T(8,128)(2,1)S(1)}, u32[]{:S(2)}, u32[]{:S(2)}) %collective-permute-start.29) | collective-permute-done | bytes 163872 | tf_op jit(solution)/shard_map/ppermute | solution.py:48
  96.9 1.6 collective-permute-start.30
  98.5 1.8 %collective-permute-start.21 = (bf16[2,1,64,512]{3,2,1,0:T(8,128)(2,1)S(1)}, bf16[2,1,64,512]{3,2,1,0:T(8,128)(2,1)S(1)}, u32[]{:S(2)}, u32[]{:S(2)}) collective-permute-start(bf16[2,1,64,512]{3,2,1,0:T(8,128)(2,1)S(1)} %add_convert_fusion.12), channel_id=1, source_target_pairs={{0,8},{4,12},{8,0},{12,4},{1,9},{5,13},{9,1},{13,5},{2,10},{6,14},... | collective-permute-start | bytes 393224 | tf_op jit(solution)/shard_map/ppermute | solution.py:48
  100.4 2.3 %collective-permute-done.11 = bf16[2,2,64,512]{3,2,1,0:T(8,128)(2,1)S(1)} collective-permute-done((bf16[2,2,64,512]{3,2,1,0:T(8,128)(2,1)S(1)}, bf16[2,2,64,512]{3,2,1,0:T(8,128)(2,1)S(1)}, u32[]{:S(2)}, u32[]{:S(2)}) %collective-permute-start.11) | collective-permute-done | bytes 262176 | tf_op jit(solution)/shard_map/ppermute | solution.py:48
  102.7 1.7 collective-permute-start.12
  104.4 1.5 collective-permute-done.21
  106.0 2.8 %collective-permute-done.12 = bf16[2,1,64,512]{3,2,1,0:T(8,128)(2,1)S(1)} collective-permute-done((bf16[2,1,64,512]{3,2,1,0:T(8,128)(2,1)S(1)}, bf16[2,1,64,512]{3,2,1,0:T(8,128)(2,1)S(1)}, u32[]{:S(2)}, u32[]{:S(2)}) %collective-permute-start.12) | collective-permute-done | bytes 131104 | tf_op jit(solution)/shard_map/ppermute | solution.py:48
  108.8 2.0 %collective-permute-start.13 = (bf16[2,1,64,512]{3,2,1,0:T(8,128)(2,1)S(1)}, bf16[2,1,64,512]{3,2,1,0:T(8,128)(2,1)S(1)}, u32[]{:S(2)}, u32[]{:S(2)}) collective-permute-start(bf16[2,1,64,512]{3,2,1,0:T(8,128)(2,1)S(1)} %add_convert_fusion.14), channel_id=1, source_target_pairs={{0,8},{4,12},{8,0},{12,4},{1,9},{5,13},{9,1},{13,5},{2,10},{6,14},... | collective-permute-start | bytes 393224 | tf_op jit(solution)/shard_map/ppermute | solution.py:48
  112.4 1.4 collective-permute-start.31
  113.8 1.1 collective-permute-done.13
  114.9 2.8 %collective-permute-start.14 = (bf16[2,1,64,512]{3,2,1,0:T(8,128)(2,1)S(1)}, bf16[2,1,64,512]{3,2,1,0:T(8,128)(2,1)S(1)}, u32[]{:S(2)}, u32[]{:S(2)}) collective-permute-start(bf16[2,1,64,512]{3,2,1,0:T(8,128)(2,1)S(1)} %add_convert_fusion.13), channel_id=1, source_target_pairs={{0,4},{4,0},{8,12},{12,8},{1,5},{5,1},{9,13},{13,9},{2,6},{6,2},{1... | collective-permute-start | bytes 393224 | tf_op jit(solution)/shard_map/ppermute | solution.py:48
  117.7 3.1 %collective-permute-done.23 = bf16[2,2,64,512]{3,2,1,0:T(8,128)(2,1)S(1)} collective-permute-done((bf16[2,2,64,512]{3,2,1,0:T(8,128)(2,1)S(1)}, bf16[2,2,64,512]{3,2,1,0:T(8,128)(2,1)S(1)}, u32[]{:S(2)}, u32[]{:S(2)}) %collective-permute-start.23) | collective-permute-done | bytes 262176 | tf_op jit(solution)/shard_map/ppermute | solution.py:48
  120.9 1.6 collective-permute-start.24
  122.6 4.3 %taps.3 = f32[32,512]{1,0:T(8,128)} custom-call(s32[2]{0:T(128)} %lengths_ref.11, f32[512,1024]{1,0:T(8,128)} %get-tuple-element.46.gated_ref, f32[512,512]{1,0:T(8,128)} %get-tuple-element.71.dconv_ref), custom_call_target="tpu_custom_call" | custom-call | flops 4600000000 | bytes 1048576 | tf_op jit(solution)/shard_map/taps/pallas_call | solution.py:497
  126.9 0.8 pad_maximum_fusion.9
  128.4 1.8 collective-permute-done.24
  132.0 4.6 %collective-permute-done.15 = bf16[2,2,64,512]{3,2,1,0:T(8,128)(2,1)S(1)} collective-permute-done((bf16[2,2,64,512]{3,2,1,0:T(8,128)(2,1)S(1)}, bf16[2,2,64,512]{3,2,1,0:T(8,128)(2,1)S(1)}, u32[]{:S(2)}, u32[]{:S(2)}) %collective-permute-start.15) | collective-permute-done | bytes 262176 | tf_op jit(solution)/shard_map/ppermute | solution.py:48
  137.3 1.8 %collective-permute-start.7 = (f32[32,1024]{1,0:T(8,128)S(1)}, f32[32,1024]{1,0:T(8,128)S(1)}, u32[]{:S(2)}, u32[]{:S(2)}) collective-permute-start(f32[32,1024]{1,0:T(8,128)S(1)} %add.81), channel_id=1, source_target_pairs={{0,2},{2,0},{1,3},{3,1},{4,6},{6,4},{5,7},{7,5},{8,10},{10,8},{9,1... | collective-permute-start | bytes 393224 | tf_op jit(solution)/shard_map/ppermute | solution.py:48
  139.1 3.4 %collective-permute-done.7 = f32[32,1024]{1,0:T(8,128)S(1)} collective-permute-done((f32[32,1024]{1,0:T(8,128)S(1)}, f32[32,1024]{1,0:T(8,128)S(1)}, u32[]{:S(2)}, u32[]{:S(2)}) %collective-permute-start.7) | collective-permute-done | bytes 131104 | tf_op jit(solution)/shard_map/ppermute | solution.py:48
  142.5 1.6 collective-permute-start.8
  144.2 3.4 %collective-permute-done.8 = f32[32,1024]{1,0:T(8,128)S(1)} collective-permute-done((f32[32,1024]{1,0:T(8,128)S(1)}, f32[32,1024]{1,0:T(8,128)S(1)}, u32[]{:S(2)}, u32[]{:S(2)}) %collective-permute-start.8) | collective-permute-done | bytes 131104 | tf_op jit(solution)/shard_map/ppermute | solution.py:48
  147.6 2.5 %collective-permute-start.9 = (f32[32,1024]{1,0:T(8,128)S(1)}, f32[32,1024]{1,0:T(8,128)S(1)}, u32[]{:S(2)}, u32[]{:S(2)}) collective-permute-start(f32[32,1024]{1,0:T(8,128)S(1)} %add.83), channel_id=1, source_target_pairs={{0,8},{4,12},{8,0},{12,4},{1,9},{5,13},{9,1},{13,5},{2,10},{6,14},... | collective-permute-start | bytes 393224 | tf_op jit(solution)/shard_map/ppermute | solution.py:48
  150.1 4.8 %collective-permute-done.9 = f32[32,1024]{1,0:T(8,128)S(1)} collective-permute-done((f32[32,1024]{1,0:T(8,128)S(1)}, f32[32,1024]{1,0:T(8,128)S(1)}, u32[]{:S(2)}, u32[]{:S(2)}) %collective-permute-start.9) | collective-permute-done | bytes 131104 | tf_op jit(solution)/shard_map/ppermute | solution.py:48
  155.8 1.0 copy-done.9
  156.9 6.1 %unpack_inner.2 = (f32[1024,2048]{1,0:T(8,128)}, f32[1,1024]{1,0:T(1,128)}) custom-call(s32[2]{0:T(128)} %pad_add_fusion.1.own_ref, f32[32,1024]{1,0:T(8,128)} %add.84.small_ref, bf16[2,8,64,512]{3,2,1,0:T(8,128)(2,1)} %copy-done.4, bf16[2,8,64,512]{3,2,1,0:T(8,128)(2,1)} %copy-done.9, bf16[1024,2048]{1,0:T(8,128)(2,1)} %weight_ref.3, f32[1,1024]{1,0:T(1,128)} %bitcast.13), custom_call_target="tpu_custom_call" | custom-call | flops 4600000000 | bytes 1048576 | tf_op jit(solution)/shard_map/unpack_inner/pallas_call | solution.py:644
  163.1 1.0 copy-done.8
  164.1 5.7 %unpack_top.1 = (f32[1024,1024]{1,0:T(8,128)}, f32[1024,256]{1,0:T(8,128)}, f32[1,1024]{1,0:T(1,128)}, f32[31,1024]{1,0:T(8,128)}, f32[2,1,128]{2,1,0:T(1,128)}) custom-call(s32[2]{0:T(128)} %pad_add_fusion.own_ref, f32[32,1024]{1,0:T(8,128)} %add.84.small_ref, bf16[2,8,64,640]{3,2,1,0:T(8,128)(2,1)} %copy-done, bf16[2,8,64,640]{3,2,1,0:T(8,128)(2,1)} %copy-done.8, ...), custom_call_target="tpu_custom_call" | custom-call | flops 5750000128 | bytes 1048576 | tf_op jit(solution)/shard_map/unpack_top/pallas_call | solution.py:580
  169.8 1.3 slice_reduce_fusion
  171.1 1.0 copy-done.10
  172.0 6.2 %unpack_inner.3 = (f32[1024,2048]{1,0:T(8,128)}, f32[1,1024]{1,0:T(1,128)}) custom-call(s32[2]{0:T(128)} %pad_add_fusion.own_ref, f32[32,1024]{1,0:T(8,128)} %add.84.small_ref, bf16[2,8,64,512]{3,2,1,0:T(8,128)(2,1)} %copy-done.5, bf16[2,8,64,512]{3,2,1,0:T(8,128)(2,1)} %copy-done.10, ...), custom_call_target="tpu_custom_call", output_to_operand_aliasing={{0}: (6, {})} | custom-call | flops 4600000000 | bytes 1048576 | tf_op jit(solution)/shard_map/unpack_inner/pallas_call | solution.py:644
  (95 shorter events, 12.3 us)
Async XLA Ops:
  4.6 18.6 %collective-permute-start = (f32[2,256,256]{2,1,0:T(8,128)}, f32[2,256,256]{2,1,0:T(8,128)S(1)}, u32[]{:S(2)}, u32[]{:S(2)}) collective-permute-start(f32[2,256,256]{2,1,0:T(8,128)} %get-tuple-element.50), channel_id=1, source_target_pairs={{0,16},{16,0},{1,17},{17,1},{2,18},{18,2},{3,19},{19,3},{4,20},{20... | collective-permute-start | bytes 1572872 | tf_op jit(solution)/shard_map/ppermute | solution.py:48
  23.2 0.8 copy-start.11
  34.7 12.0 %collective-permute-start.1 = (bf16[2,8,64,640]{3,2,1,0:T(8,128)(2,1)}, bf16[2,8,64,640]{3,2,1,0:T(8,128)(2,1)S(1)}, u32[]{:S(2)}, u32[]{:S(2)}) collective-permute-start(bf16[2,8,64,640]{3,2,1,0:T(8,128)(2,1)} %get-tuple-element.57), channel_id=1, source_target_pairs={{0,1},{1,0},{2,3},{3,2},{4,5},{5,4},{6,7},{7,6},{8,9},{9,8},{10,11... | collective-permute-start | bytes 3932168 | tf_op jit(solution)/shard_map/ppermute | solution.py:48
  35.3 11.4 %copy-start.1 = (bf16[2,8,64,640]{3,2,1,0:T(8,128)(2,1)S(1)}, bf16[2,8,64,640]{3,2,1,0:T(8,128)(2,1)}, u32[]{:S(2)}) copy-start(bf16[2,8,64,640]{3,2,1,0:T(8,128)(2,1)} %get-tuple-element.56) | copy-start | bytes 3932164
  46.1 11.9 %collective-permute-start.3 = (bf16[2,8,64,512]{3,2,1,0:T(8,128)(2,1)}, bf16[2,8,64,512]{3,2,1,0:T(8,128)(2,1)S(1)}, u32[]{:S(2)}, u32[]{:S(2)}) collective-permute-start(bf16[2,8,64,512]{3,2,1,0:T(8,128)(2,1)} %get-tuple-element.64), channel_id=1, source_target_pairs={{0,1},{1,0},{2,3},{3,2},{4,5},{5,4},{6,7},{7,6},{8,9},{9,8},{10,11... | collective-permute-start | bytes 3145736 | tf_op jit(solution)/shard_map/ppermute | solution.py:48
  47.1 11.0 %copy-start.3 = (bf16[2,8,64,512]{3,2,1,0:T(8,128)(2,1)S(1)}, bf16[2,8,64,512]{3,2,1,0:T(8,128)(2,1)}, u32[]{:S(2)}) copy-start(bf16[2,8,64,512]{3,2,1,0:T(8,128)(2,1)} %get-tuple-element.63) | copy-start | bytes 3145732
  47.1 16.7 %collective-permute-start.2 = (bf16[2,4,64,640]{3,2,1,0:T(8,128)(2,1)S(1)}, bf16[2,4,64,640]{3,2,1,0:T(8,128)(2,1)S(1)}, u32[]{:S(2)}, u32[]{:S(2)}) collective-permute-start(bf16[2,4,64,640]{3,2,1,0:T(8,128)(2,1)S(1)} %slice.58), channel_id=1, source_target_pairs={{0,16},{16,0},{1,17},{17,1},{2,18},{18,2},{3,19},{19,3},{4,20},{20... | collective-permute-start | bytes 1966088 | tf_op jit(solution)/shard_map/ppermute | solution.py:48
  58.1 18.5 %collective-permute-start.4 = (bf16[2,8,64,512]{3,2,1,0:T(8,128)(2,1)}, bf16[2,8,64,512]{3,2,1,0:T(8,128)(2,1)S(1)}, u32[]{:S(2)}, u32[]{:S(2)}) collective-permute-start(bf16[2,8,64,512]{3,2,1,0:T(8,128)(2,1)} %get-tuple-element.69), channel_id=1, source_target_pairs={{0,1},{1,0},{2,3},{3,2},{4,5},{5,4},{6,7},{7,6},{8,9},{9,8},{10,11... | collective-permute-start | bytes 3145736 | tf_op jit(solution)/shard_map/ppermute | solution.py:48
  64.0 12.5 %copy-start.2 = (bf16[2,8,64,512]{3,2,1,0:T(8,128)(2,1)S(1)}, bf16[2,8,64,512]{3,2,1,0:T(8,128)(2,1)}, u32[]{:S(2)}) copy-start(bf16[2,8,64,512]{3,2,1,0:T(8,128)(2,1)} %get-tuple-element.68) | copy-start | bytes 3145732
  64.0 10.7 %collective-permute-start.26 = (bf16[2,2,64,640]{3,2,1,0:T(8,128)(2,1)S(1)}, bf16[2,2,64,640]{3,2,1,0:T(8,128)(2,1)S(1)}, u32[]{:S(2)}, u32[]{:S(2)}) collective-permute-start(bf16[2,2,64,640]{3,2,1,0:T(8,128)(2,1)S(1)} %slice.72), channel_id=1, source_target_pairs={{0,2},{2,0},{1,3},{3,1},{4,6},{6,4},{5,7},{7,5},{8,10},{10,8},{9,1... | collective-permute-start | bytes 983048 | tf_op jit(solution)/shard_map/ppermute | solution.py:48
  65.7 18.9 %collective-permute-start.18 = (bf16[2,4,64,512]{3,2,1,0:T(8,128)(2,1)S(1)}, bf16[2,4,64,512]{3,2,1,0:T(8,128)(2,1)S(1)}, u32[]{:S(2)}, u32[]{:S(2)}) collective-permute-start(bf16[2,4,64,512]{3,2,1,0:T(8,128)(2,1)S(1)} %slice.66), channel_id=1, source_target_pairs={{0,2},{2,0},{1,3},{3,1},{4,6},{6,4},{5,7},{7,5},{8,10},{10,8},{9,1... | collective-permute-start | bytes 1572872 | tf_op jit(solution)/shard_map/ppermute | solution.py:48
  74.9 7.1 %collective-permute-start.27 = (bf16[2,1,64,640]{3,2,1,0:T(8,128)(2,1)S(1)}, bf16[2,1,64,640]{3,2,1,0:T(8,128)(2,1)S(1)}, u32[]{:S(2)}, u32[]{:S(2)}) collective-permute-start(bf16[2,1,64,640]{3,2,1,0:T(8,128)(2,1)S(1)} %slice.85), channel_id=1, source_target_pairs={{0,4},{4,0},{8,12},{12,8},{1,5},{5,1},{9,13},{13,9},{2,6},{6,2},{1... | collective-permute-start | bytes 491528 | tf_op jit(solution)/shard_map/ppermute | solution.py:48
  76.9 16.2 %collective-permute-start.10 = (bf16[2,4,64,512]{3,2,1,0:T(8,128)(2,1)S(1)}, bf16[2,4,64,512]{3,2,1,0:T(8,128)(2,1)S(1)}, u32[]{:S(2)}, u32[]{:S(2)}) collective-permute-start(bf16[2,4,64,512]{3,2,1,0:T(8,128)(2,1)S(1)} %slice.60), channel_id=1, source_target_pairs={{0,16},{16,0},{1,17},{17,1},{2,18},{18,2},{3,19},{19,3},{4,20},{20... | collective-permute-start | bytes 1572872 | tf_op jit(solution)/shard_map/ppermute | solution.py:48
  82.0 8.0 %collective-permute-start.28 = (bf16[2,1,64,640]{3,2,1,0:T(8,128)(2,1)S(1)}, bf16[2,1,64,640]{3,2,1,0:T(8,128)(2,1)S(1)}, u32[]{:S(2)}, u32[]{:S(2)}) collective-permute-start(bf16[2,1,64,640]{3,2,1,0:T(8,128)(2,1)S(1)} %add_convert_fusion.10), channel_id=1, source_target_pairs={{0,8},{4,12},{8,0},{12,4},{1,9},{5,13},{9,1},{13,5},{2,10},{6,14},... | collective-permute-start | bytes 491528 | tf_op jit(solution)/shard_map/ppermute | solution.py:48
  84.8 7.8 %collective-permute-start.19 = (bf16[2,2,64,512]{3,2,1,0:T(8,128)(2,1)S(1)}, bf16[2,2,64,512]{3,2,1,0:T(8,128)(2,1)S(1)}, u32[]{:S(2)}, u32[]{:S(2)}) collective-permute-start(bf16[2,2,64,512]{3,2,1,0:T(8,128)(2,1)S(1)} %slice.81), channel_id=1, source_target_pairs={{0,16},{16,0},{1,17},{17,1},{2,18},{18,2},{3,19},{19,3},{4,20},{20... | collective-permute-start | bytes 786440 | tf_op jit(solution)/shard_map/ppermute | solution.py:48
  90.1 6.8 %collective-permute-start.29 = (bf16[2,1,64,640]{3,2,1,0:T(8,128)(2,1)S(1)}, bf16[2,1,64,640]{3,2,1,0:T(8,128)(2,1)S(1)}, u32[]{:S(2)}, u32[]{:S(2)}) collective-permute-start(bf16[2,1,64,640]{3,2,1,0:T(8,128)(2,1)S(1)} %add_convert_fusion.9), channel_id=1, source_target_pairs={{0,4},{4,0},{8,12},{12,8},{1,5},{5,1},{9,13},{13,9},{2,6},{6,2},{1... | collective-permute-start | bytes 491528 | tf_op jit(solution)/shard_map/ppermute | solution.py:48
  92.7 5.8 %collective-permute-start.20 = (bf16[2,1,64,512]{3,2,1,0:T(8,128)(2,1)S(1)}, bf16[2,1,64,512]{3,2,1,0:T(8,128)(2,1)S(1)}, u32[]{:S(2)}, u32[]{:S(2)}) collective-permute-start(bf16[2,1,64,512]{3,2,1,0:T(8,128)(2,1)S(1)} %slice.83), channel_id=1, source_target_pairs={{0,4},{4,0},{8,12},{12,8},{1,5},{5,1},{9,13},{13,9},{2,6},{6,2},{1... | collective-permute-start | bytes 393224 | tf_op jit(solution)/shard_map/ppermute | solution.py:48
  93.3 9.3 %collective-permute-start.11 = (bf16[2,2,64,512]{3,2,1,0:T(8,128)(2,1)S(1)}, bf16[2,2,64,512]{3,2,1,0:T(8,128)(2,1)S(1)}, u32[]{:S(2)}, u32[]{:S(2)}) collective-permute-start(bf16[2,2,64,512]{3,2,1,0:T(8,128)(2,1)S(1)} %slice.77), channel_id=1, source_target_pairs={{0,2},{2,0},{1,3},{3,1},{4,6},{6,4},{5,7},{7,5},{8,10},{10,8},{9,1... | collective-permute-start | bytes 786440 | tf_op jit(solution)/shard_map/ppermute | solution.py:48
  96.9 15.4 %collective-permute-start.30 = (bf16[2,2,64,640]{3,2,1,0:T(8,128)(2,1)S(1)}, bf16[2,2,64,640]{3,2,1,0:T(8,128)(2,1)S(1)}, u32[]{:S(2)}, u32[]{:S(2)}) collective-permute-start(bf16[2,2,64,640]{3,2,1,0:T(8,128)(2,1)S(1)} %pad_maximum_fusion.6), channel_id=1, source_target_pairs={{0,2},{2,0},{1,3},{3,1},{4,6},{6,4},{5,7},{7,5},{8,10},{10,8},{9,1... | collective-permute-start | bytes 983048 | tf_op jit(solution)/shard_map/ppermute | solution.py:48
  98.5 7.3 %collective-permute-start.21 = (bf16[2,1,64,512]{3,2,1,0:T(8,128)(2,1)S(1)}, bf16[2,1,64,512]{3,2,1,0:T(8,128)(2,1)S(1)}, u32[]{:S(2)}, u32[]{:S(2)}) collective-permute-start(bf16[2,1,64,512]{3,2,1,0:T(8,128)(2,1)S(1)} %add_convert_fusion.12), channel_id=1, source_target_pairs={{0,8},{4,12},{8,0},{12,4},{1,9},{5,13},{9,1},{13,5},{2,10},{6,14},... | collective-permute-start | bytes 393224 | tf_op jit(solution)/shard_map/ppermute | solution.py:48
  102.7 6.0 %collective-permute-start.12 = (bf16[2,1,64,512]{3,2,1,0:T(8,128)(2,1)S(1)}, bf16[2,1,64,512]{3,2,1,0:T(8,128)(2,1)S(1)}, u32[]{:S(2)}, u32[]{:S(2)}) collective-permute-start(bf16[2,1,64,512]{3,2,1,0:T(8,128)(2,1)S(1)} %slice.79), channel_id=1, source_target_pairs={{0,4},{4,0},{8,12},{12,8},{1,5},{5,1},{9,13},{13,9},{2,6},{6,2},{1... | collective-permute-start | bytes 393224 | tf_op jit(solution)/shard_map/ppermute | solution.py:48
  105.9 5.6 %collective-permute-start.22 = (bf16[2,1,64,512]{3,2,1,0:T(8,128)(2,1)S(1)}, bf16[2,1,64,512]{3,2,1,0:T(8,128)(2,1)S(1)}, u32[]{:S(2)}, u32[]{:S(2)}) collective-permute-start(bf16[2,1,64,512]{3,2,1,0:T(8,128)(2,1)S(1)} %add_convert_fusion.11), channel_id=1, source_target_pairs={{0,4},{4,0},{8,12},{12,8},{1,5},{5,1},{9,13},{13,9},{2,6},{6,2},{1... | collective-permute-start | bytes 393224 | tf_op jit(solution)/shard_map/ppermute | solution.py:48
  108.8 6.0 %collective-permute-start.13 = (bf16[2,1,64,512]{3,2,1,0:T(8,128)(2,1)S(1)}, bf16[2,1,64,512]{3,2,1,0:T(8,128)(2,1)S(1)}, u32[]{:S(2)}, u32[]{:S(2)}) collective-permute-start(bf16[2,1,64,512]{3,2,1,0:T(8,128)(2,1)S(1)} %add_convert_fusion.14), channel_id=1, source_target_pairs={{0,8},{4,12},{8,0},{12,4},{1,9},{5,13},{9,1},{13,5},{2,10},{6,14},... | collective-permute-start | bytes 393224 | tf_op jit(solution)/shard_map/ppermute | solution.py:48
  111.5 9.3 %collective-permute-start.23 = (bf16[2,2,64,512]{3,2,1,0:T(8,128)(2,1)S(1)}, bf16[2,2,64,512]{3,2,1,0:T(8,128)(2,1)S(1)}, u32[]{:S(2)}, u32[]{:S(2)}) collective-permute-start(bf16[2,2,64,512]{3,2,1,0:T(8,128)(2,1)S(1)} %pad_maximum_fusion.8), channel_id=1, source_target_pairs={{0,16},{16,0},{1,17},{17,1},{2,18},{18,2},{3,19},{19,3},{4,20},{20... | collective-permute-start | bytes 786440 | tf_op jit(solution)/shard_map/ppermute | solution.py:48
  112.4 18.1 %collective-permute-start.31 = (bf16[2,4,64,640]{3,2,1,0:T(8,128)(2,1)S(1)}, bf16[2,4,64,640]{3,2,1,0:T(8,128)(2,1)S(1)}, u32[]{:S(2)}, u32[]{:S(2)}) collective-permute-start(bf16[2,4,64,640]{3,2,1,0:T(8,128)(2,1)S(1)} %pad_maximum_fusion.3), channel_id=1, source_target_pairs={{0,16},{16,0},{1,17},{17,1},{2,18},{18,2},{3,19},{19,3},{4,20},{20... | collective-permute-start | bytes 1966088 | tf_op jit(solution)/shard_map/ppermute | solution.py:48
  114.9 12.9 %collective-permute-start.14 = (bf16[2,1,64,512]{3,2,1,0:T(8,128)(2,1)S(1)}, bf16[2,1,64,512]{3,2,1,0:T(8,128)(2,1)S(1)}, u32[]{:S(2)}, u32[]{:S(2)}) collective-permute-start(bf16[2,1,64,512]{3,2,1,0:T(8,128)(2,1)S(1)} %add_convert_fusion.13), channel_id=1, source_target_pairs={{0,4},{4,0},{8,12},{12,8},{1,5},{5,1},{9,13},{13,9},{2,6},{6,2},{1... | collective-permute-start | bytes 393224 | tf_op jit(solution)/shard_map/ppermute | solution.py:48
  120.9 6.0 %copy-start.6 = (f32[32,512]{1,0:T(8,128)S(1)}, f32[32,512]{1,0:T(8,128)}, u32[]{:S(2)}) copy-start(f32[32,512]{1,0:T(8,128)} %taps.2) | copy-start | bytes 196612
  120.9 9.2 %collective-permute-start.24 = (bf16[2,4,64,512]{3,2,1,0:T(8,128)(2,1)S(1)}, bf16[2,4,64,512]{3,2,1,0:T(8,128)(2,1)S(1)}, u32[]{:S(2)}, u32[]{:S(2)}) collective-permute-start(bf16[2,4,64,512]{3,2,1,0:T(8,128)(2,1)S(1)} %pad_maximum_fusion.5), channel_id=1, source_target_pairs={{0,2},{2,0},{1,3},{3,1},{4,6},{6,4},{5,7},{7,5},{8,10},{10,8},{9,1... | collective-permute-start | bytes 1572872 | tf_op jit(solution)/shard_map/ppermute | solution.py:48
  127.8 3.5 %collective-permute-start.5 = (f32[32,1024]{1,0:T(8,128)S(1)}, f32[32,1024]{1,0:T(8,128)S(1)}, u32[]{:S(2)}, u32[]{:S(2)}) collective-permute-start(f32[32,1024]{1,0:T(8,128)S(1)} %pad_maximum_fusion.9), channel_id=1, source_target_pairs={{0,1},{1,0},{2,3},{3,2},{4,5},{5,4},{6,7},{7,6},{8,9},{9,8},{10,11... | collective-permute-start | bytes 393224 | tf_op jit(solution)/shard_map/ppermute | solution.py:48
  127.9 8.8 %collective-permute-start.15 = (bf16[2,2,64,512]{3,2,1,0:T(8,128)(2,1)S(1)}, bf16[2,2,64,512]{3,2,1,0:T(8,128)(2,1)S(1)}, u32[]{:S(2)}, u32[]{:S(2)}) collective-permute-start(bf16[2,2,64,512]{3,2,1,0:T(8,128)(2,1)S(1)} %pad_maximum_fusion.7), channel_id=1, source_target_pairs={{0,2},{2,0},{1,3},{3,1},{4,6},{6,4},{5,7},{7,5},{8,10},{10,8},{9,1... | collective-permute-start | bytes 786440 | tf_op jit(solution)/shard_map/ppermute | solution.py:48
  130.3 1.0 copy-start.4
  130.3 1.0 copy-start.7
  130.3 25.5 %collective-permute-start.25 = (bf16[2,8,64,512]{3,2,1,0:T(8,128)(2,1)S(1)}, bf16[2,8,64,512]{3,2,1,0:T(8,128)(2,1)S(1)}, u32[]{:S(2)}, u32[]{:S(2)}) collective-permute-start(bf16[2,8,64,512]{3,2,1,0:T(8,128)(2,1)S(1)} %pad_maximum_fusion.2.mine_ref), channel_id=1, source_target_pairs={{0,1},{1,0},{2,3},{3,2},{4,5},{5,4},{6,7},{7,6},{8,9},{9,8},{10,11... | collective-permute-start | bytes 3145736 | tf_op jit(solution)/shard_map/ppermute | solution.py:48
  131.3 16.3 %copy-start = (bf16[2,8,64,640]{3,2,1,0:T(8,128)(2,1)}, bf16[2,8,64,640]{3,2,1,0:T(8,128)(2,1)S(1)}, u32[]{:S(2)}) copy-start(bf16[2,8,64,640]{3,2,1,0:T(8,128)(2,1)S(1)} %pad_maximum_fusion.mine_ref) | copy-start | bytes 3932164
  131.3 31.8 %collective-permute-start.32 = (bf16[2,8,64,640]{3,2,1,0:T(8,128)(2,1)S(1)}, bf16[2,8,64,640]{3,2,1,0:T(8,128)(2,1)S(1)}, u32[]{:S(2)}, u32[]{:S(2)}) collective-permute-start(bf16[2,8,64,640]{3,2,1,0:T(8,128)(2,1)S(1)} %pad_maximum_fusion.mine_ref), channel_id=1, source_target_pairs={{0,1},{1,0},{2,3},{3,2},{4,5},{5,4},{6,7},{7,6},{8,9},{9,8},{10,11... | collective-permute-start | bytes 3932168 | tf_op jit(solution)/shard_map/ppermute | solution.py:48
  131.3 6.0 %collective-permute-start.6 = (f32[32,1024]{1,0:T(8,128)S(1)}, f32[32,1024]{1,0:T(8,128)S(1)}, u32[]{:S(2)}, u32[]{:S(2)}) collective-permute-start(f32[32,1024]{1,0:T(8,128)S(1)} %fusion), channel_id=1, source_target_pairs={{0,16},{16,0},{1,17},{17,1},{2,18},{18,2},{3,19},{19,3},{4,20},{20... | collective-permute-start | bytes 393224 | tf_op jit(solution)/shard_map/ppermute | solution.py:48
  136.7 18.9 %collective-permute-start.16 = (bf16[2,4,64,512]{3,2,1,0:T(8,128)(2,1)S(1)}, bf16[2,4,64,512]{3,2,1,0:T(8,128)(2,1)S(1)}, u32[]{:S(2)}, u32[]{:S(2)}) collective-permute-start(bf16[2,4,64,512]{3,2,1,0:T(8,128)(2,1)S(1)} %pad_maximum_fusion.4), channel_id=1, source_target_pairs={{0,16},{16,0},{1,17},{17,1},{2,18},{18,2},{3,19},{19,3},{4,20},{20... | collective-permute-start | bytes 1572872 | tf_op jit(solution)/shard_map/ppermute | solution.py:48
  137.3 5.2 %collective-permute-start.7 = (f32[32,1024]{1,0:T(8,128)S(1)}, f32[32,1024]{1,0:T(8,128)S(1)}, u32[]{:S(2)}, u32[]{:S(2)}) collective-permute-start(f32[32,1024]{1,0:T(8,128)S(1)} %add.81), channel_id=1, source_target_pairs={{0,2},{2,0},{1,3},{3,1},{4,6},{6,4},{5,7},{7,5},{8,10},{10,8},{9,1... | collective-permute-start | bytes 393224 | tf_op jit(solution)/shard_map/ppermute | solution.py:48
  142.5 5.0 %collective-permute-start.8 = (f32[32,1024]{1,0:T(8,128)S(1)}, f32[32,1024]{1,0:T(8,128)S(1)}, u32[]{:S(2)}, u32[]{:S(2)}) collective-permute-start(f32[32,1024]{1,0:T(8,128)S(1)} %add.82), channel_id=1, source_target_pairs={{0,4},{4,0},{8,12},{12,8},{1,5},{5,1},{9,13},{13,9},{2,6},{6,2},{1... | collective-permute-start | bytes 393224 | tf_op jit(solution)/shard_map/ppermute | solution.py:48
  147.6 7.3 %collective-permute-start.9 = (f32[32,1024]{1,0:T(8,128)S(1)}, f32[32,1024]{1,0:T(8,128)S(1)}, u32[]{:S(2)}, u32[]{:S(2)}) collective-permute-start(f32[32,1024]{1,0:T(8,128)S(1)} %add.83), channel_id=1, source_target_pairs={{0,8},{4,12},{8,0},{12,4},{1,9},{5,13},{9,1},{13,5},{2,10},{6,14},... | collective-permute-start | bytes 393224 | tf_op jit(solution)/shard_map/ppermute | solution.py:48
  155.7 7.3 %copy-start.5 = (bf16[2,8,64,512]{3,2,1,0:T(8,128)(2,1)}, bf16[2,8,64,512]{3,2,1,0:T(8,128)(2,1)S(1)}, u32[]{:S(2)}) copy-start(bf16[2,8,64,512]{3,2,1,0:T(8,128)(2,1)S(1)} %pad_maximum_fusion.1.mine_ref) | copy-start | bytes 3145732
  155.7 15.3 %collective-permute-start.17 = (bf16[2,8,64,512]{3,2,1,0:T(8,128)(2,1)S(1)}, bf16[2,8,64,512]{3,2,1,0:T(8,128)(2,1)S(1)}, u32[]{:S(2)}, u32[]{:S(2)}) collective-permute-start(bf16[2,8,64,512]{3,2,1,0:T(8,128)(2,1)S(1)} %pad_maximum_fusion.1.mine_ref), channel_id=1, source_target_pairs={{0,1},{1,0},{2,3},{3,2},{4,5},{5,4},{6,7},{7,6},{8,9},{9,8},{10,11... | collective-permute-start | bytes 3145736 | tf_op jit(solution)/shard_map/ppermute | solution.py:48
  155.8 1.1 copy-start.9
  163.0 1.1 copy-start.8
  171.1 1.0 copy-start.10

commit v5 on v4

--- a/solution.py
+++ b/solution.py
@@ -15,6 +15,11 @@
 MARGIN = 16
 CHUNKS = 2
 VMEM = 56 << 20
+ORDER = (
+    "in0", "in1", "top", "small", "in0", "top", "in1", "small", "in0", "top", "in1", "small",
+    "in0", "top", "in1", "small", "in0", "top", "in1", "small", "top", "in0", "in1", "top",
+    "write_top", "in0", "in0", "write0", "in1", "in1", "write1",
+)
 SMEM_SPEC = pl.BlockSpec(memory_space=pltpu.SMEM)
 F32 = jnp.float32
 BF16 = jnp.bfloat16
@@ -41,6 +46,7 @@
 FAR = "far"
 REST = "rest"
 CORE = "core"
+SMALL_STEPS = ((CORE, 1), ("member", 1), ("near", 1), (FAR, 1), (FAR, 2))
 
 
 def exchange(values, axis, bit=1):
@@ -52,29 +58,87 @@
     return (own.astype(F32) + other.astype(F32)).astype(own.dtype)
 
 
-def halve(pieces, axis):
-    half = pieces.shape[1] // 2
-    return add(pieces[:, :half], exchange(pieces[:, half:], axis))
-
-
-def double(pieces):
-    pieces = add(pieces, exchange(pieces, FAR, 2))
-    return lax.psum(pieces, REST) if lax.axis_size(REST) > 1 else pieces
-
-
-def gather(pieces, axis):
-    return jnp.concatenate([pieces, exchange(pieces, axis)], axis=1)
-
-
 def own_place(order):
     place = lax.axis_index(order[0]) * 4 + lax.axis_index(order[1]) * 2 + (lax.axis_index(FAR) & 1)
     return place.astype(jnp.int32)
 
 
-def all_sum(values):
-    for axis, bit in ((CORE, 1), ("member", 1), ("near", 1), (FAR, 1), (FAR, 2)):
-        values = values + exchange(values, axis, bit)
+def over_rest(values):
     return lax.psum(values, REST) if lax.axis_size(REST) > 1 else values
+
+
+class Line:
+    def __init__(self):
+        self.values = {}
+        self.pending = {}
+        self.steps = {}
+        self.last = None
+
+    def after_last(self, value):
+        if self.last is not None:
+            value, self.values[self.last] = lax.optimization_barrier(
+                (value, self.values[self.last])
+            )
+        return value
+
+    def before_kernel(self, value):
+        value = self.after_last(value)
+        if self.last in self.steps and self.last not in self.pending:
+            self.start(self.last)
+        return value
+
+    def put(self, name, value):
+        self.values[name] = value
+        self.last = name
+
+    def begin(self, name, send, keep, order):
+        self.values[name] = keep
+        self.pending[name] = exchange(send, CORE)
+        halve, gather = [("halve", axis) for axis in order], [("gather", axis) for axis in order]
+        self.steps[name] = (
+            [("add", CORE)]
+            + halve
+            + [("halve", FAR), ("double", FAR), ("gather", FAR)]
+            + gather[::-1]
+            + [("done", CORE)]
+        )
+
+    def begin_small(self, name, value):
+        self.values[name] = value
+        self.steps[name] = [("sum", step) for step in SMALL_STEPS]
+        self.start(name)
+
+    def start(self, name):
+        if not self.steps[name]:
+            return
+        kind, axis = self.steps[name][0]
+        values = self.values[name]
+        if kind == "halve":
+            self.pending[name] = exchange(values[:, values.shape[1] // 2 :], axis)
+        elif kind == "double":
+            self.pending[name] = exchange(values, axis, 2)
+        elif kind == "sum":
+            self.pending[name] = exchange(values, *axis)
+        else:
+            self.pending[name] = exchange(values, axis)
+
+    def step(self, name, start=True):
+        kind, _ = self.steps[name].pop(0)
+        got = self.after_last(self.pending.pop(name))
+        own = self.values[name]
+        if kind == "halve":
+            own = own[:, : got.shape[1]]
+        if kind == "gather":
+            result = jnp.concatenate([own, got], axis=1)
+        elif kind == "done":
+            result = (own, got)
+        else:
+            result = add(own, got)
+        if kind == "double" or (kind == "sum" and not self.steps[name]):
+            result = over_rest(result)
+        self.put(name, result)
+        if start:
+            self.start(name)
 
 
 def write_pieces(own_ref, product, send_ref, keep_ref, group):
@@ -184,12 +248,13 @@
     gate_weight_ref,
     depth_ref,
     out_weight_ref,
-    normed_ref,
+    turned_ref,
     gated_ref,
     gate_ref,
     slope_ref,
     active_ref,
     residual_ref,
+    normed_ref,
     pad_ref,
 ):
     utterances = pad_ref.shape[1]
@@ -200,7 +265,9 @@
         values = features_ref[...].astype(F32)
         centred = values - jnp.mean(values, axis=-1, keepdims=True)
         spread = jnp.mean(centred * centred, axis=-1, keepdims=True)
-        normed_ref[...] = (centred * lax.rsqrt(spread + 1e-05) * gain_ref[...]).astype(BF16)
+        normed = centred * lax.rsqrt(spread + 1e-05) * gain_ref[...]
+        normed_ref[...] = normed.astype(BF16)
+        turned_ref[...] = normed.T.astype(BF16)
         residual_ref[...] = values
         clear_margins(pad_ref)
 
@@ -244,7 +311,7 @@
     return pl.pallas_call(
         forward_kernel,
         grid=(steps,),
-        out_shape=(narrow, wide, wide, wide, narrow, wide),
+        out_shape=(jax.ShapeDtypeStruct((model, rows), BF16), wide, wide, wide, narrow, wide),
         in_specs=[
             SMEM_SPEC,
             fixed(rows, model),
@@ -254,8 +321,11 @@
             pl.BlockSpec((depth.shape[0], WIDE), lambda i: (0, i)),
             pl.BlockSpec((WIDE, model), lambda i: (i, 0)),
         ],
-        out_specs=(fixed(rows, model), column, column, column, column, fixed(rows, model)),
-        scratch_shapes=[pltpu.VMEM((WIDE // LANES, utterances, frames + 2 * MARGIN, LANES), F32)],
+        out_specs=(fixed(model, rows), column, column, column, column, fixed(rows, model)),
+        scratch_shapes=[
+            pltpu.VMEM((rows, model), BF16),
+            pltpu.VMEM((WIDE // LANES, utterances, frames + 2 * MARGIN, LANES), F32),
+        ],
         compiler_params=params(),
         cost_estimate=cost(15),
         name="forward",
@@ -329,35 +399,57 @@
 
 
 def outer_kernel(
-    own_ref, active_ref, dresidual_ref, final_ref, dlogits_ref, send_ref, keep_ref, product_ref
+    own_ref,
+    active_ref,
+    dresidual_ref,
+    final_ref,
+    dlogits_ref,
+    send_ref,
+    keep_ref,
+    update_ref,
+    head_ref,
 ):
-    width = dresidual_ref.shape[1]
-    product_ref[:, :width] = dot(active_ref[...], dresidual_ref[...], 0, 0)
-    product_ref[:, width:] = dot(final_ref[...], dlogits_ref[...], 0, 0)
-    write_pieces(own_ref, product_ref, send_ref, keep_ref, 0)
+    core, place = own_ref[0], own_ref[1]
+    _, places, rows, _ = keep_ref.shape
+    half_out = update_ref.shape[1] // 2
+    half_head = head_ref.shape[1] // 2
+    update_ref[...] = dot(active_ref[...], dresidual_ref[...], 0, 0)
+    head_ref[...] = dot(final_ref[...], dlogits_ref[...], 0, 0)
+    for index in range(places):
+        piece = index ^ (place & (places - 1))
+        for side, target in ((core, keep_ref), (1 - core, send_ref)):
+            here = pl.ds(pl.multiple_of(index * 2 * rows + side * rows, rows), rows)
+            for group in range(2):
+                target[group, piece, :, :half_out] = update_ref[
+                    here, group * half_out : (group + 1) * half_out
+                ].astype(BF16)
+                target[group, piece, :, half_out:] = head_ref[
+                    here, group * half_head : (group + 1) * half_head
+                ].astype(BF16)
 
 
 def outer(own, active, dresidual, final, dlogits):
+    steps = 4
     rows, model = active.shape
-    half_out = dresidual.shape[1] // 2
-    half_head = dlogits.shape[1] // 2
-    width = half_out + half_head
-    piece = (PLACES, model // (2 * PLACES), width)
-    shape = jax.ShapeDtypeStruct((2,) + piece, BF16)
-    out = pl.BlockSpec((1,) + piece, lambda i: (i, 0, 0, 0))
+    symbols = dlogits.shape[1]
+    places = PLACES // steps
+    block = model // steps
+    piece = (model // (2 * PLACES), (model + symbols) // 2)
+    shape = jax.ShapeDtypeStruct((2, PLACES) + piece, BF16)
+    out = pl.BlockSpec(
+        (2, places) + piece, lambda i, own_ref: (0, i ^ (own_ref[1] // places), 0, 0)
+    )
+    column = pl.BlockSpec((rows, block), lambda i, own_ref: (0, i))
     return pl.pallas_call(
         outer_kernel,
-        grid=(2,),
         out_shape=(shape, shape),
-        in_specs=[
-            SMEM_SPEC,
-            fixed(rows, model),
-            pl.BlockSpec((rows, half_out), lambda i: (0, i)),
-            fixed(rows, model),
-            pl.BlockSpec((rows, half_head), lambda i: (0, i)),
-        ],
-        out_specs=(out, out),
-        scratch_shapes=[pltpu.VMEM((model, width), F32)],
+        grid_spec=pltpu.PrefetchScalarGridSpec(
+            num_scalar_prefetch=1,
+            grid=(steps,),
+            in_specs=[column, fixed(rows, model), column, fixed(rows, symbols)],
+            out_specs=(out, out),
+            scratch_shapes=[pltpu.VMEM((block, model), F32), pltpu.VMEM((block, symbols), F32)],
+        ),
         compiler_params=params(),
         cost_estimate=cost(5),
         name="outer",
@@ -372,7 +464,7 @@
     slope_ref,
     gated_ref,
     gate_ref,
-    normed_ref,
+    turned_ref,
     depth_ref,
     send_ref,
     keep_ref,
@@ -417,12 +509,12 @@
         lax.fori_loop(0, utterances, one, 0)
 
     for group, source in ((0, dvalue_ref), (1, dgate_ref)):
-        product_ref[...] = dot(normed_ref[...], source[...], 0, 0)
+        product_ref[...] = dot(turned_ref[...], source[...])
         write_pieces(own_ref, product_ref, send_ref, keep_ref, group)
 
 
-def inner(own, lengths, dresidual, weight_out, slope, gated, gate, normed, depth, chunk, utterances):
-    rows, model = normed.shape
+def inner(own, lengths, dresidual, weight_out, slope, gated, gate, turned, depth, chunk, utterances):
+    model, rows = turned.shape
     frames = rows // utterances
     steps = model // WIDE // CHUNKS
     first = chunk * steps
@@ -442,7 +534,7 @@
             column,
             column,
             column,
-            fixed(rows, model),
+            fixed(model, rows),
             pl.BlockSpec((depth.shape[0], WIDE), lambda i: (0, first + i)),
         ],
         out_specs=(out, out, pl.BlockSpec((rows, WIDE), lambda i: (0, i))),
@@ -455,7 +547,7 @@
         compiler_params=params(),
         cost_estimate=cost(11),
         name="inner",
-    )(own, lengths, dresidual, weight_out, slope, gated, gate, normed, depth)
+    )(own, lengths, dresidual, weight_out, slope, gated, gate, turned, depth)
 
 
 def taps_kernel(lengths_ref, gated_ref, dconv_ref, out_ref, pad_ref, sums_ref):
@@ -509,14 +601,17 @@
             pltpu.VMEM((taps, 8, LANES), F32),
         ],
         compiler_params=params(),
-        cost_estimate=cost(4),
+        cost_estimate=cost(1),
         name="taps",
     )(lengths, gated, dconv)
 
 
 def gain_row(weight, grad):
-    along = jnp.sum(weight.astype(F32) * grad, axis=1, keepdims=True)
-    return jnp.broadcast_to(along, (along.shape[0], LANES)).T[0:1, :]
+    terms = weight.astype(F32) * grad
+    high = terms.astype(BF16)
+    low = (terms - high.astype(F32)).astype(BF16)
+    ones = jnp.ones((8, terms.shape[1]), BF16)
+    return (dot(ones, high, 1, 1) + dot(ones, low, 1, 1))[0:1, :]
 
 
 def write_rows(own_ref, step, piece_refs, group, scale, targets):
@@ -693,14 +788,18 @@
     give, kept = teacher_sums(member, teacher_logits, utterances)
     got = exchange(give, "member")
     flat = features.reshape(utterances * frames, model)
-    normed, gated, gate, slope, active, residual = forward(
+    turned, gated, gate, slope, active, residual = forward(
         lengths, flat, gain_conv[None], weight_in, weight_depth, weight_out, utterances
     )
     losses, final, dlogits, dresidual = top(
         lengths, residual, gain_out[None], head_weight, kept, got
     )
 
-    def weight_in_chunk(chunk, dresidual):
+    line = Line()
+
+    def products(name, chunk):
+        nonlocal dresidual
+        dresidual = line.before_kernel(dresidual)
         send, keep, dconv = inner(
             owns[chunk],
             lengths,
@@ -709,67 +808,83 @@
             slope,
             gated,
             gate,
-            normed,
+            turned,
             weight_depth,
             chunk,
             utterances,
         )
-        return add(keep, exchange(send, CORE)), dconv
-
-    def chip_sums(pieces, order):
-        pieces = double(halve(halve(pieces, order[1]), FAR))
-        return gather(gather(gather(pieces, FAR), order[1]), order[0])
+        line.begin(name, send, keep, orders[chunk])
+        line.put(name + "_conv", dconv)
+
+    def tap_rows(name, chunk):
+        dconv = line.before_kernel(line.values[name + "_conv"])
+        line.put(name + "_taps", tap_sums(lengths, gated, dconv, taps, chunk, utterances))
 
     send, keep = outer(owns[1], active, dresidual, final, dlogits)
     send, keep, dresidual = tie((send, keep, dresidual))
-    top_sum = add(keep, exchange(send, CORE))
-    first_sum, first_dconv = weight_in_chunk(0, dresidual)
-    top_sum, dresidual = tie((top_sum, dresidual))
-    top_sum = halve(top_sum, orders[1][0])
-    second_sum, second_dconv = weight_in_chunk(1, dresidual)
-    top_sum, first_sum, first_dconv = tie((top_sum, first_sum, first_dconv))
-    first_sum = halve(first_sum, orders[0][0])
-    first_taps = tap_sums(lengths, gated, first_dconv, taps, 0, utterances)
-    second_sum, second_dconv = tie((second_sum, second_dconv))
-    second_sum = halve(second_sum, orders[1][0])
-    second_taps = tap_sums(lengths, gated, second_dconv, taps, 1, utterances)
-    small = all_sum(jnp.concatenate([first_taps, second_taps], axis=1))
-
-    top_all = chip_sums(top_sum, orders[1])
-    grad_out, grad_head, by_head, grad_depth, losses = unpack_top(
-        utts,
-        owns[1],
-        small,
-        top_all,
-        exchange(top_all, CORE),
-        head_weight,
-        gain_out[None],
-        losses,
-        weight_out.shape[1],
-    )
-    unpacked = ()
-    for chunk, values in enumerate((first_sum, second_sum)):
-        every = chip_sums(values, orders[chunk])
-        unpacked = unpack_inner(
+    line.begin("top", send, keep, orders[1])
+    products("in0", 0)
+    line.step("top", False)
+    products("in1", 1)
+    line.step("top")
+    line.step("in0")
+    line.step("in1")
+    tap_rows("in0", 0)
+    tap_rows("in1", 1)
+    small = jnp.concatenate([line.values["in0_taps"], line.values["in1_taps"]], axis=1)
+    line.begin_small("small", small)
+    written = {}
+
+    def write_top():
+        mine, other = line.values["top"]
+        *rest, written["losses"] = unpack_top(
+            utts,
+            owns[1],
+            line.values["small"],
+            line.after_last(mine),
+            other,
+            head_weight,
+            gain_out[None],
+            losses,
+            weight_out.shape[1],
+        )
+        written["out"], written["head"], by_head, written["depth"] = rest
+        line.put("by_head", by_head)
+
+    def write_in(chunk, name):
+        mine, other = line.values[name]
+        before = (written["in"], line.values["by_in"]) if chunk else ()
+        written["in"], by_in = unpack_inner(
             utts,
             owns[chunk],
-            small,
-            every,
-            exchange(every, CORE),
+            line.values["small"],
+            line.after_last(mine),
+            other,
             weight_in,
             gain_conv[None],
             chunk,
-            unpacked,
+            before,
         )
-    grad_in, by_in = unpacked
+        line.put("by_in", by_in)
+
+    writes = {
+        "write_top": write_top,
+        "write0": functools.partial(write_in, 0, "in0"),
+        "write1": functools.partial(write_in, 1, "in1"),
+    }
+    for name in ORDER:
+        if name in writes:
+            writes[name]()
+        else:
+            line.step(name)
     return (
-        by_in.reshape(model),
-        grad_in,
-        grad_depth,
-        grad_out,
-        by_head.reshape(model),
-        grad_head,
-        losses[:, 0, 0],
+        line.values["by_in"].reshape(model),
+        written["in"],
+        written["depth"],
+        written["out"],
+        line.values["by_head"].reshape(model),
+        written["head"],
+        written["losses"][:, 0, 0],
     )
 
 

time: 179 us -> 186 us (1.039)
  waiting for transfers between devices: 51.9 us -> 56.8 us
  Pallas kernels: 78 us -> 80 us
    ppermute x33, waiting for transfers between devices: 51.9 us -> 56.8 us  [exchange(): return lax.ppermute(values, axis, [(i, i ^ bit) for i in range(size)])]
    unnamed x24 -> x35, local copies, waits for them, and re-layouts: 4.61 us -> 4.46 us
  transfers between devices with their start and end apart: 33 -> 33, of which waited for: 18 -> 18; matrix products, arithmetic and copies ran while one was open for 4% -> 3% of each run, Pallas kernels for 32% -> 31%
where the time goes in v5:
time: 186 us; the launch traced here: 185 us
  Pallas kernels  80 us (43%)
  waiting for transfers between devices  56.8 us (31%)
  starting transfers between devices  36.4 us (20%)
  local copies, waits for them, and re-layouts  5.73 us (3%)
  other arithmetic  4.79 us (3%)
    ppermute x33, waiting for transfers between devices, exchange(): return lax.ppermute(values, axis, [(i, i ^ bit) for i in range(size)])  56.8 us
    ppermute x33, starting transfers between devices, exchange(): return lax.ppermute(values, axis, [(i, i ^ bit) for i in range(size)])  36.4 us
    pallas_call x2, Pallas kernels, inner(): pl.pallas_call(inner_kernel, grid=(steps,), out_shape=(shape, shape, jax....  21.5 us
    pallas_call x1, Pallas kernels, forward(): pl.pallas_call(forward_kernel, grid=(steps,), out_shape=(jax.ShapeDtypeSt...  15.2 us
    pallas_call x2, Pallas kernels, unpack_inner(): pl.pallas_call(functools.partial(unpack_inner_kernel, utts, chunk == CHUN...  13.2 us
    pallas_call x2, Pallas kernels, tap_sums(): pl.pallas_call(taps_kernel, grid=(steps,), out_shape=jax.ShapeDtypeStruct...  8.85 us
    pallas_call x1, Pallas kernels, outer(): pl.pallas_call(outer_kernel, out_shape=(shape, shape), grid_spec=pltpu.Pr...  6.33 us
    pallas_call x1, Pallas kernels, unpack_top(): pl.pallas_call(functools.partial(unpack_top_kernel, utts), out_shape=(jax...  5.68 us
  transfers between devices with their start and end apart: 33, of which 18 were waited for; matrix products, arithmetic and copies ran while one was open for 3% of the time, Pallas kernels for 31%

profile of v5, /device:TPU:0, one launch (start us, length us, event | category | flops | bytes accessed | tf_op | source)
XLA Modules:
  0.0 184.9 jit_solution(1661839148578115415)
XLA Ops:
  0.6 4.0 %teachers.1 = (f32[2,256,256]{2,1,0:T(8,128)}, f32[2,256,256]{2,1,0:T(8,128)}) custom-call(s32[1]{0:T(128)} %bitcast.5.member_ref, bf16[2,4,256,256]{3,2,1,0:T(8,128)(2,1)} %logits_ref.1), custom_call_target="tpu_custom_call" | custom-call | flops 4600000000 | bytes 1048576 | tf_op jit(solution)/shard_map/teachers/pallas_call | solution.py:186
  4.6 2.9 %collective-permute-start = (f32[2,256,256]{2,1,0:T(8,128)}, f32[2,256,256]{2,1,0:T(8,128)S(1)}, u32[]{:S(2)}, u32[]{:S(2)}) collective-permute-start(f32[2,256,256]{2,1,0:T(8,128)} %get-tuple-element.114), channel_id=1, source_target_pairs={{0,16},{16,0},{1,17},{17,1},{2,18},{18,2},{3,19},{19,3},{4,20},{20... | collective-permute-start | bytes 1572872 | tf_op jit(solution)/shard_map/ppermute | solution.py:54
  7.5 15.2 %forward.1 = (bf16[1024,512]{1,0:T(8,128)(2,1)}, f32[512,1024]{1,0:T(8,128)}, f32[512,1024]{1,0:T(8,128)}, f32[512,1024]{1,0:T(8,128)}, bf16[512,1024]{1,0:T(8,128)(2,1)}, /*index=5*/f32[512,1024]{1,0:T(8,128)}) custom-call(s32[2]{0:T(128)} %lengths_ref.11, bf16[512,1024]{1,0:T(8,128)(2,1)} %bitcast.9, f32[1,1024]{1,0:T(1,128)} %bitcast.12, ...), custom_call_target="tpu_custom_call" | custom-call | flops 17250000896 | bytes 1048576 | tf_op jit(solution)/shard_map/forward/pallas_call | solution.py:311
  23.4 0.9 copy-done.11
  24.2 5.3 %top.1 = (f32[2,1,128]{2,1,0:T(1,128)}, bf16[512,1024]{1,0:T(8,128)(2,1)}, bf16[512,256]{1,0:T(8,128)(2,1)}, bf16[512,1024]{1,0:T(8,128)(2,1)}) custom-call(s32[2]{0:T(128)} %lengths_ref.11, f32[512,1024]{1,0:T(8,128)} %get-tuple-element.112.residual_ref, f32[1,1024]{1,0:T(1,128)} %bitcast.10, bf16[1024,256]{1,0:T(8,128)(2,1)} %head_ref.3, ...), custom_call_target="tpu_custom_call" | custom-call | flops 5750000128 | bytes 1048576 | tf_op jit(solution)/shard_map/top/pallas_call | solution.py:379
  29.5 6.3 %outer.1 = (bf16[2,8,64,640]{3,2,1,0:T(8,128)(2,1)}, bf16[2,8,64,640]{3,2,1,0:T(8,128)(2,1)}) custom-call(s32[2]{0:T(128)} %pad_add_fusion.own_ref, bf16[512,1024]{1,0:T(8,128)(2,1)} %get-tuple-element.111.active_ref, bf16[512,1024]{1,0:T(8,128)(2,1)} %get-tuple-element.130.dresidual_ref, bf16[512,1024]{1,0:T(8,128)(2,1)} %get-tuple-element.116.final_ref, ...), custom_call_target="tpu_custom_call" | custom-call | flops 5750000128 | bytes 1048576 | tf_op jit(solution)/shard_map/outer/pallas_call | solution.py:443
  36.5 10.8 %inner.2 = (bf16[2,8,64,512]{3,2,1,0:T(8,128)(2,1)}, bf16[2,8,64,512]{3,2,1,0:T(8,128)(2,1)}, f32[512,512]{1,0:T(8,128)}) custom-call(s32[2]{0:T(128)} %pad_add_fusion.1.own_ref, s32[2]{0:T(128)} %lengths_ref.11, bf16[512,1024]{1,0:T(8,128)(2,1)} %get-tuple-element.130.dresidual_ref, bf16[1024,1024]{1,0:T(8,128)(2,1)} %out_weight_ref.5, ...), custom_call_target="tpu_custom_call" | custom-call | flops 12650000384 | bytes 1048576 | tf_op jit(solution)/shard_map/inner/pallas_call | solution.py:525
  48.4 10.7 %inner.3 = (bf16[2,8,64,512]{3,2,1,0:T(8,128)(2,1)}, bf16[2,8,64,512]{3,2,1,0:T(8,128)(2,1)}, f32[512,512]{1,0:T(8,128)}) custom-call(s32[2]{0:T(128)} %pad_add_fusion.own_ref, s32[2]{0:T(128)} %lengths_ref.11, bf16[512,1024]{1,0:T(8,128)(2,1)} %get-tuple-element.130.dresidual_ref, bf16[1024,1024]{1,0:T(8,128)(2,1)} %out_weight_ref.5, ...), custom_call_target="tpu_custom_call" | custom-call | flops 12650000384 | bytes 1048576 | tf_op jit(solution)/shard_map/inner/pallas_call | solution.py:525
  59.2 5.8 %collective-permute-done.2 = bf16[2,4,64,640]{3,2,1,0:T(8,128)(2,1)S(1)} collective-permute-done((bf16[2,4,64,640]{3,2,1,0:T(8,128)(2,1)S(1)}, bf16[2,4,64,640]{3,2,1,0:T(8,128)(2,1)S(1)}, u32[]{:S(2)}, u32[]{:S(2)}) %collective-permute-start.2) | collective-permute-done | bytes 655392 | tf_op jit(solution)/shard_map/ppermute | solution.py:54
  65.2 1.6 collective-permute-start.6
  69.0 4.3 %taps.2 = f32[32,512]{1,0:T(8,128)} custom-call(s32[2]{0:T(128)} %lengths_ref.11, f32[512,1024]{1,0:T(8,128)} %get-tuple-element.124.gated_ref, f32[512,512]{1,0:T(8,128)} %get-tuple-element.141.dconv_ref), custom_call_target="tpu_custom_call" | custom-call | flops 1150000000 | bytes 1048576 | tf_op jit(solution)/shard_map/taps/pallas_call | solution.py:589
  73.3 4.5 %taps.3 = f32[32,512]{1,0:T(8,128)} custom-call(s32[2]{0:T(128)} %lengths_ref.11, f32[512,1024]{1,0:T(8,128)} %get-tuple-element.124.gated_ref, f32[512,512]{1,0:T(8,128)} %get-tuple-element.143.dconv_ref), custom_call_target="tpu_custom_call" | custom-call | flops 1150000000 | bytes 1048576 | tf_op jit(solution)/shard_map/taps/pallas_call | solution.py:589
  77.9 0.8 pad_maximum_fusion
  78.8 6.5 %collective-permute-done.8 = bf16[2,4,64,512]{3,2,1,0:T(8,128)(2,1)S(1)} collective-permute-done((bf16[2,4,64,512]{3,2,1,0:T(8,128)(2,1)S(1)}, bf16[2,4,64,512]{3,2,1,0:T(8,128)(2,1)S(1)}, u32[]{:S(2)}, u32[]{:S(2)}) %collective-permute-start.8) | collective-permute-done | bytes 524320 | tf_op jit(solution)/shard_map/ppermute | solution.py:54
  86.4 1.5 collective-permute-start.9
  88.0 5.4 %collective-permute-done.12 = bf16[2,2,64,512]{3,2,1,0:T(8,128)(2,1)S(1)} collective-permute-done((bf16[2,2,64,512]{3,2,1,0:T(8,128)(2,1)S(1)}, bf16[2,2,64,512]{3,2,1,0:T(8,128)(2,1)S(1)}, u32[]{:S(2)}, u32[]{:S(2)}) %collective-permute-start.12) | collective-permute-done | bytes 262176 | tf_op jit(solution)/shard_map/ppermute | solution.py:54
  93.4 1.6 collective-permute-start.11
  95.0 1.5 collective-permute-start.10
  97.1 3.4 %collective-permute-done.11 = bf16[2,1,64,640]{3,2,1,0:T(8,128)(2,1)S(1)} collective-permute-done((bf16[2,1,64,640]{3,2,1,0:T(8,128)(2,1)S(1)}, bf16[2,1,64,640]{3,2,1,0:T(8,128)(2,1)S(1)}, u32[]{:S(2)}, u32[]{:S(2)}) %collective-permute-start.11) | collective-permute-done | bytes 163872 | tf_op jit(solution)/shard_map/ppermute | solution.py:54
  100.5 2.1 %collective-permute-start.14 = (bf16[2,1,64,640]{3,2,1,0:T(8,128)(2,1)S(1)}, bf16[2,1,64,640]{3,2,1,0:T(8,128)(2,1)S(1)}, u32[]{:S(2)}, u32[]{:S(2)}) collective-permute-start(bf16[2,1,64,640]{3,2,1,0:T(8,128)(2,1)S(1)} %add_convert_fusion.10), channel_id=1, source_target_pairs={{0,8},{4,12},{8,0},{12,4},{1,9},{5,13},{9,1},{13,5},{2,10},{6,14},... | collective-permute-start | bytes 491528 | tf_op jit(solution)/shard_map/ppermute | solution.py:54
  102.9 3.5 %collective-permute-start.19 = (f32[32,1024]{1,0:T(8,128)S(1)}, f32[32,1024]{1,0:T(8,128)S(1)}, u32[]{:S(2)}, u32[]{:S(2)}) collective-permute-start(f32[32,1024]{1,0:T(8,128)S(1)} %add.87), channel_id=1, source_target_pairs={{0,2},{2,0},{1,3},{3,1},{4,6},{6,4},{5,7},{7,5},{8,10},{10,8},{9,1... | collective-permute-start | bytes 393224 | tf_op jit(solution)/shard_map/ppermute | solution.py:54
  106.3 2.6 %collective-permute-start.13 = (bf16[2,1,64,512]{3,2,1,0:T(8,128)(2,1)S(1)}, bf16[2,1,64,512]{3,2,1,0:T(8,128)(2,1)S(1)}, u32[]{:S(2)}, u32[]{:S(2)}) collective-permute-start(bf16[2,1,64,512]{3,2,1,0:T(8,128)(2,1)S(1)} %slice.82), channel_id=1, source_target_pairs={{0,4},{4,0},{8,12},{12,8},{1,5},{5,1},{9,13},{13,9},{2,6},{6,2},{1... | collective-permute-start | bytes 393224 | tf_op jit(solution)/shard_map/ppermute | solution.py:54
  109.4 1.8 collective-permute-done.14
  111.4 4.4 %collective-permute-done.13 = bf16[2,1,64,512]{3,2,1,0:T(8,128)(2,1)S(1)} collective-permute-done((bf16[2,1,64,512]{3,2,1,0:T(8,128)(2,1)S(1)}, bf16[2,1,64,512]{3,2,1,0:T(8,128)(2,1)S(1)}, u32[]{:S(2)}, u32[]{:S(2)}) %collective-permute-start.13) | collective-permute-done | bytes 131104 | tf_op jit(solution)/shard_map/ppermute | solution.py:54
  116.6 2.5 %collective-permute-start.22 = (f32[32,1024]{1,0:T(8,128)S(1)}, f32[32,1024]{1,0:T(8,128)S(1)}, u32[]{:S(2)}, u32[]{:S(2)}) collective-permute-start(f32[32,1024]{1,0:T(8,128)S(1)} %add.91), channel_id=1, source_target_pairs={{0,4},{4,0},{8,12},{12,8},{1,5},{5,1},{9,13},{13,9},{2,6},{6,2},{1... | collective-permute-start | bytes 393224 | tf_op jit(solution)/shard_map/ppermute | solution.py:54
  119.4 1.8 collective-permute-start.20
  121.2 3.6 %collective-permute-done.16 = bf16[2,1,64,512]{3,2,1,0:T(8,128)(2,1)S(1)} collective-permute-done((bf16[2,1,64,512]{3,2,1,0:T(8,128)(2,1)S(1)}, bf16[2,1,64,512]{3,2,1,0:T(8,128)(2,1)S(1)}, u32[]{:S(2)}, u32[]{:S(2)}) %collective-permute-start.16) | collective-permute-done | bytes 131104 | tf_op jit(solution)/shard_map/ppermute | solution.py:54
  125.4 1.4 collective-permute-done.21
  126.9 1.3 collective-permute-start.23
  128.2 1.0 collective-permute-start.25
  129.2 1.9 %collective-permute-start.24 = (f32[32,1024]{1,0:T(8,128)S(1)}, f32[32,1024]{1,0:T(8,128)S(1)}, u32[]{:S(2)}, u32[]{:S(2)}) collective-permute-start(f32[32,1024]{1,0:T(8,128)S(1)} %add.94), channel_id=1, source_target_pairs={{0,8},{4,12},{8,0},{12,4},{1,9},{5,13},{9,1},{13,5},{2,10},{6,14},... | collective-permute-start | bytes 393224 | tf_op jit(solution)/shard_map/ppermute | solution.py:54
  131.1 2.1 %collective-permute-done.25 = bf16[2,1,64,512]{3,2,1,0:T(8,128)(2,1)S(1)} collective-permute-done((bf16[2,1,64,512]{3,2,1,0:T(8,128)(2,1)S(1)}, bf16[2,1,64,512]{3,2,1,0:T(8,128)(2,1)S(1)}, u32[]{:S(2)}, u32[]{:S(2)}) %collective-permute-start.25) | collective-permute-done | bytes 131104 | tf_op jit(solution)/shard_map/ppermute | solution.py:54
  133.2 3.2 %collective-permute-done.24 = f32[32,1024]{1,0:T(8,128)S(1)} collective-permute-done((f32[32,1024]{1,0:T(8,128)S(1)}, f32[32,1024]{1,0:T(8,128)S(1)}, u32[]{:S(2)}, u32[]{:S(2)}) %collective-permute-start.24) | collective-permute-done | bytes 131104 | tf_op jit(solution)/shard_map/ppermute | solution.py:54
  137.7 1.3 collective-permute-start.28
  139.1 1.6 collective-permute-start.27
  140.7 5.7 %collective-permute-done.28 = bf16[2,2,64,512]{3,2,1,0:T(8,128)(2,1)S(1)} collective-permute-done((bf16[2,2,64,512]{3,2,1,0:T(8,128)(2,1)S(1)}, bf16[2,2,64,512]{3,2,1,0:T(8,128)(2,1)S(1)}, u32[]{:S(2)}, u32[]{:S(2)}) %collective-permute-start.28) | collective-permute-done | bytes 262176 | tf_op jit(solution)/shard_map/ppermute | solution.py:54
  146.5 1.5 collective-permute-start.30
  148.1 1.1 copy-done.8
  149.1 5.7 %unpack_top.1 = (f32[1024,1024]{1,0:T(8,128)}, f32[1024,256]{1,0:T(8,128)}, f32[1,1024]{1,0:T(1,128)}, f32[31,1024]{1,0:T(8,128)}, f32[2,1,128]{2,1,0:T(1,128)}) custom-call(s32[2]{0:T(128)} %pad_add_fusion.own_ref, f32[32,1024]{1,0:T(8,128)} %add.95.small_ref, bf16[2,8,64,640]{3,2,1,0:T(8,128)(2,1)} %copy-done.3, bf16[2,8,64,640]{3,2,1,0:T(8,128)(2,1)} %copy-done.8, ...), custom_call_target="tpu_custom_call" | custom-call | flops 5750000128 | bytes 1048576 | tf_op jit(solution)/shard_map/unpack_top/pallas_call | solution.py:675
  154.8 5.2 %collective-permute-done.30 = bf16[2,4,64,512]{3,2,1,0:T(8,128)(2,1)S(1)} collective-permute-done((bf16[2,4,64,512]{3,2,1,0:T(8,128)(2,1)S(1)}, bf16[2,4,64,512]{3,2,1,0:T(8,128)(2,1)S(1)}, u32[]{:S(2)}, u32[]{:S(2)}) %collective-permute-start.30) | collective-permute-done | bytes 524320 | tf_op jit(solution)/shard_map/ppermute | solution.py:54
  160.2 1.3 collective-permute-start.29
  161.6 1.3 collective-permute-done.31.other_ref
  162.8 1.0 copy-done.10
  163.8 6.5 %unpack_inner.2 = (f32[1024,2048]{1,0:T(8,128)}, f32[1,1024]{1,0:T(1,128)}) custom-call(s32[2]{0:T(128)} %pad_add_fusion.1.own_ref, f32[32,1024]{1,0:T(8,128)} %add.95.small_ref, bf16[2,8,64,512]{3,2,1,0:T(8,128)(2,1)} %copy-done.4, bf16[2,8,64,512]{3,2,1,0:T(8,128)(2,1)} %copy-done.10, bf16[1024,2048]{1,0:T(8,128)(2,1)} %weight_ref.3, f32[1,1024]{1,0:T(1,128)} %bitcast.13), custom_call_target="tpu_custom_call" | custom-call | flops 4600000000 | bytes 1048576 | tf_op jit(solution)/shard_map/unpack_inner/pallas_call | solution.py:739
  170.3 4.2 %collective-permute-done.29 = bf16[2,4,64,512]{3,2,1,0:T(8,128)(2,1)S(1)} collective-permute-done((bf16[2,4,64,512]{3,2,1,0:T(8,128)(2,1)S(1)}, bf16[2,4,64,512]{3,2,1,0:T(8,128)(2,1)S(1)}, u32[]{:S(2)}, u32[]{:S(2)}) %collective-permute-start.29) | collective-permute-done | bytes 524320 | tf_op jit(solution)/shard_map/ppermute | solution.py:54
  175.4 1.9 %collective-permute-done.32.other_ref = bf16[2,8,64,512]{3,2,1,0:T(8,128)(2,1)S(1)} collective-permute-done((bf16[2,8,64,512]{3,2,1,0:T(8,128)(2,1)S(1)}, bf16[2,8,64,512]{3,2,1,0:T(8,128)(2,1)S(1)}, u32[]{:S(2)}, u32[]{:S(2)}) %collective-permute-start.32) | collective-permute-done | bytes 1048608 | tf_op jit(solution)/shard_map/ppermute | solution.py:54
  177.3 1.0 copy-done.9
  178.3 6.6 %unpack_inner.3 = (f32[1024,2048]{1,0:T(8,128)}, f32[1,1024]{1,0:T(1,128)}) custom-call(s32[2]{0:T(128)} %pad_add_fusion.own_ref, f32[32,1024]{1,0:T(8,128)} %add.95.small_ref, bf16[2,8,64,512]{3,2,1,0:T(8,128)(2,1)} %copy-done.5, bf16[2,8,64,512]{3,2,1,0:T(8,128)(2,1)} %copy-done.9, bf16[1024,2048]{1,0:T(8,128)(2,1)} %weight_ref.3, ...), custom_call_target="tpu_custom_call", output_to_operand_aliasing={{0}: (6, {})} | custom-call | flops 4600000000 | bytes 1048576 | tf_op jit(solution)/shard_map/unpack_inner/pallas_call | solution.py:739
  (106 shorter events, 11.5 us)
Async XLA Ops:
  4.6 18.7 %collective-permute-start = (f32[2,256,256]{2,1,0:T(8,128)}, f32[2,256,256]{2,1,0:T(8,128)S(1)}, u32[]{:S(2)}, u32[]{:S(2)}) collective-permute-start(f32[2,256,256]{2,1,0:T(8,128)} %get-tuple-element.114), channel_id=1, source_target_pairs={{0,16},{16,0},{1,17},{17,1},{2,18},{18,2},{3,19},{19,3},{4,20},{20... | collective-permute-start | bytes 1572872 | tf_op jit(solution)/shard_map/ppermute | solution.py:54
  23.3 0.9 copy-start.11
  35.8 12.0 %collective-permute-start.1 = (bf16[2,8,64,640]{3,2,1,0:T(8,128)(2,1)}, bf16[2,8,64,640]{3,2,1,0:T(8,128)(2,1)S(1)}, u32[]{:S(2)}, u32[]{:S(2)}) collective-permute-start(bf16[2,8,64,640]{3,2,1,0:T(8,128)(2,1)} %get-tuple-element.122), channel_id=1, source_target_pairs={{0,1},{1,0},{2,3},{3,2},{4,5},{5,4},{6,7},{7,6},{8,9},{9,8},{10,11... | collective-permute-start | bytes 3932168 | tf_op jit(solution)/shard_map/ppermute | solution.py:54
  36.5 11.3 %copy-start = (bf16[2,8,64,640]{3,2,1,0:T(8,128)(2,1)S(1)}, bf16[2,8,64,640]{3,2,1,0:T(8,128)(2,1)}, u32[]{:S(2)}) copy-start(bf16[2,8,64,640]{3,2,1,0:T(8,128)(2,1)} %get-tuple-element.121) | copy-start | bytes 3932164
  47.3 19.5 %collective-permute-start.4 = (bf16[2,8,64,512]{3,2,1,0:T(8,128)(2,1)}, bf16[2,8,64,512]{3,2,1,0:T(8,128)(2,1)S(1)}, u32[]{:S(2)}, u32[]{:S(2)}) collective-permute-start(bf16[2,8,64,512]{3,2,1,0:T(8,128)(2,1)} %get-tuple-element.137), channel_id=1, source_target_pairs={{0,1},{1,0},{2,3},{3,2},{4,5},{5,4},{6,7},{7,6},{8,9},{9,8},{10,11... | collective-permute-start | bytes 3145736 | tf_op jit(solution)/shard_map/ppermute | solution.py:54
  48.3 16.7 %collective-permute-start.2 = (bf16[2,4,64,640]{3,2,1,0:T(8,128)(2,1)S(1)}, bf16[2,4,64,640]{3,2,1,0:T(8,128)(2,1)S(1)}, u32[]{:S(2)}, u32[]{:S(2)}) collective-permute-start(bf16[2,4,64,640]{3,2,1,0:T(8,128)(2,1)S(1)} %slice.57), channel_id=1, source_target_pairs={{0,16},{16,0},{1,17},{17,1},{2,18},{18,2},{3,19},{19,3},{4,20},{20... | collective-permute-start | bytes 1966088 | tf_op jit(solution)/shard_map/ppermute | solution.py:54
  59.1 7.7 %copy-start.1 = (bf16[2,8,64,512]{3,2,1,0:T(8,128)(2,1)S(1)}, bf16[2,8,64,512]{3,2,1,0:T(8,128)(2,1)}, u32[]{:S(2)}) copy-start(bf16[2,8,64,512]{3,2,1,0:T(8,128)(2,1)} %get-tuple-element.136) | copy-start | bytes 3145732
  59.1 8.6 %collective-permute-start.3 = (bf16[2,8,64,512]{3,2,1,0:T(8,128)(2,1)}, bf16[2,8,64,512]{3,2,1,0:T(8,128)(2,1)S(1)}, u32[]{:S(2)}, u32[]{:S(2)}) collective-permute-start(bf16[2,8,64,512]{3,2,1,0:T(8,128)(2,1)} %get-tuple-element.135), channel_id=1, source_target_pairs={{0,1},{1,0},{2,3},{3,2},{4,5},{5,4},{6,7},{7,6},{8,9},{9,8},{10,11... | collective-permute-start | bytes 3145736 | tf_op jit(solution)/shard_map/ppermute | solution.py:54
  65.2 21.1 %collective-permute-start.6 = (bf16[2,2,64,640]{3,2,1,0:T(8,128)(2,1)S(1)}, bf16[2,2,64,640]{3,2,1,0:T(8,128)(2,1)S(1)}, u32[]{:S(2)}, u32[]{:S(2)}) collective-permute-start(bf16[2,2,64,640]{3,2,1,0:T(8,128)(2,1)S(1)} %slice.76), channel_id=1, source_target_pairs={{0,2},{2,0},{1,3},{3,1},{4,6},{6,4},{5,7},{7,5},{8,10},{10,8},{9,1... | collective-permute-start | bytes 983048 | tf_op jit(solution)/shard_map/ppermute | solution.py:54
  66.8 1.2 copy-start.2
  67.2 18.1 %collective-permute-start.8 = (bf16[2,4,64,512]{3,2,1,0:T(8,128)(2,1)S(1)}, bf16[2,4,64,512]{3,2,1,0:T(8,128)(2,1)S(1)}, u32[]{:S(2)}, u32[]{:S(2)}) collective-permute-start(bf16[2,4,64,512]{3,2,1,0:T(8,128)(2,1)S(1)} %slice.78), channel_id=1, source_target_pairs={{0,2},{2,0},{1,3},{3,1},{4,6},{6,4},{5,7},{7,5},{8,10},{10,8},{9,1... | collective-permute-start | bytes 1572872 | tf_op jit(solution)/shard_map/ppermute | solution.py:54
  68.4 17.7 %collective-permute-start.7 = (bf16[2,4,64,512]{3,2,1,0:T(8,128)(2,1)S(1)}, bf16[2,4,64,512]{3,2,1,0:T(8,128)(2,1)S(1)}, u32[]{:S(2)}, u32[]{:S(2)}) collective-permute-start(bf16[2,4,64,512]{3,2,1,0:T(8,128)(2,1)S(1)} %slice.77), channel_id=1, source_target_pairs={{0,16},{16,0},{1,17},{17,1},{2,18},{18,2},{3,19},{19,3},{4,20},{20... | collective-permute-start | bytes 1572872 | tf_op jit(solution)/shard_map/ppermute | solution.py:54
  73.3 4.5 %copy-start.6 = (f32[32,512]{1,0:T(8,128)S(1)}, f32[32,512]{1,0:T(8,128)}, u32[]{:S(2)}) copy-start(f32[32,512]{1,0:T(8,128)} %taps.2) | copy-start | bytes 196612
  78.7 7.7 %collective-permute-start.5 = (f32[32,1024]{1,0:T(8,128)S(1)}, f32[32,1024]{1,0:T(8,128)S(1)}, u32[]{:S(2)}, u32[]{:S(2)}) collective-permute-start(f32[32,1024]{1,0:T(8,128)S(1)} %pad_maximum_fusion), channel_id=1, source_target_pairs={{0,1},{1,0},{2,3},{3,2},{4,5},{5,4},{6,7},{7,6},{8,9},{9,8},{10,11... | collective-permute-start | bytes 393224 | tf_op jit(solution)/shard_map/ppermute | solution.py:54
  85.4 1.0 copy-start.7
  85.5 7.9 %collective-permute-start.12 = (bf16[2,2,64,512]{3,2,1,0:T(8,128)(2,1)S(1)}, bf16[2,2,64,512]{3,2,1,0:T(8,128)(2,1)S(1)}, u32[]{:S(2)}, u32[]{:S(2)}) collective-permute-start(bf16[2,2,64,512]{3,2,1,0:T(8,128)(2,1)S(1)} %slice.81), channel_id=1, source_target_pairs={{0,16},{16,0},{1,17},{17,1},{2,18},{18,2},{3,19},{19,3},{4,20},{20... | collective-permute-start | bytes 786440 | tf_op jit(solution)/shard_map/ppermute | solution.py:54
  86.4 16.4 %collective-permute-start.9 = (f32[32,1024]{1,0:T(8,128)S(1)}, f32[32,1024]{1,0:T(8,128)S(1)}, u32[]{:S(2)}, u32[]{:S(2)}) collective-permute-start(f32[32,1024]{1,0:T(8,128)S(1)} %fusion), channel_id=1, source_target_pairs={{0,16},{16,0},{1,17},{17,1},{2,18},{18,2},{3,19},{19,3},{4,20},{20... | collective-permute-start | bytes 393224 | tf_op jit(solution)/shard_map/ppermute | solution.py:54
  93.4 7.1 %collective-permute-start.11 = (bf16[2,1,64,640]{3,2,1,0:T(8,128)(2,1)S(1)}, bf16[2,1,64,640]{3,2,1,0:T(8,128)(2,1)S(1)}, u32[]{:S(2)}, u32[]{:S(2)}) collective-permute-start(bf16[2,1,64,640]{3,2,1,0:T(8,128)(2,1)S(1)} %slice.80), channel_id=1, source_target_pairs={{0,4},{4,0},{8,12},{12,8},{1,5},{5,1},{9,13},{13,9},{2,6},{6,2},{1... | collective-permute-start | bytes 491528 | tf_op jit(solution)/shard_map/ppermute | solution.py:54
  95.0 7.8 %collective-permute-start.10 = (bf16[2,2,64,512]{3,2,1,0:T(8,128)(2,1)S(1)}, bf16[2,2,64,512]{3,2,1,0:T(8,128)(2,1)S(1)}, u32[]{:S(2)}, u32[]{:S(2)}) collective-permute-start(bf16[2,2,64,512]{3,2,1,0:T(8,128)(2,1)S(1)} %slice.79), channel_id=1, source_target_pairs={{0,2},{2,0},{1,3},{3,1},{4,6},{6,4},{5,7},{7,5},{8,10},{10,8},{9,1... | collective-permute-start | bytes 786440 | tf_op jit(solution)/shard_map/ppermute | solution.py:54
  96.6 9.7 %collective-permute-start.15 = (bf16[2,1,64,512]{3,2,1,0:T(8,128)(2,1)S(1)}, bf16[2,1,64,512]{3,2,1,0:T(8,128)(2,1)S(1)}, u32[]{:S(2)}, u32[]{:S(2)}) collective-permute-start(bf16[2,1,64,512]{3,2,1,0:T(8,128)(2,1)S(1)} %slice.83), channel_id=1, source_target_pairs={{0,4},{4,0},{8,12},{12,8},{1,5},{5,1},{9,13},{13,9},{2,6},{6,2},{1... | collective-permute-start | bytes 393224 | tf_op jit(solution)/shard_map/ppermute | solution.py:54
  100.5 10.7 %collective-permute-start.14 = (bf16[2,1,64,640]{3,2,1,0:T(8,128)(2,1)S(1)}, bf16[2,1,64,640]{3,2,1,0:T(8,128)(2,1)S(1)}, u32[]{:S(2)}, u32[]{:S(2)}) collective-permute-start(bf16[2,1,64,640]{3,2,1,0:T(8,128)(2,1)S(1)} %add_convert_fusion.10), channel_id=1, source_target_pairs={{0,8},{4,12},{8,0},{12,4},{1,9},{5,13},{9,1},{13,5},{2,10},{6,14},... | collective-permute-start | bytes 491528 | tf_op jit(solution)/shard_map/ppermute | solution.py:54
  102.9 13.7 %collective-permute-start.19 = (f32[32,1024]{1,0:T(8,128)S(1)}, f32[32,1024]{1,0:T(8,128)S(1)}, u32[]{:S(2)}, u32[]{:S(2)}) collective-permute-start(f32[32,1024]{1,0:T(8,128)S(1)} %add.87), channel_id=1, source_target_pairs={{0,2},{2,0},{1,3},{3,1},{4,6},{6,4},{5,7},{7,5},{8,10},{10,8},{9,1... | collective-permute-start | bytes 393224 | tf_op jit(solution)/shard_map/ppermute | solution.py:54
  106.3 9.4 %collective-permute-start.13 = (bf16[2,1,64,512]{3,2,1,0:T(8,128)(2,1)S(1)}, bf16[2,1,64,512]{3,2,1,0:T(8,128)(2,1)S(1)}, u32[]{:S(2)}, u32[]{:S(2)}) collective-permute-start(bf16[2,1,64,512]{3,2,1,0:T(8,128)(2,1)S(1)} %slice.82), channel_id=1, source_target_pairs={{0,4},{4,0},{8,12},{12,8},{1,5},{5,1},{9,13},{13,9},{2,6},{6,2},{1... | collective-permute-start | bytes 393224 | tf_op jit(solution)/shard_map/ppermute | solution.py:54
  109.0 10.2 %collective-permute-start.18 = (bf16[2,1,64,512]{3,2,1,0:T(8,128)(2,1)S(1)}, bf16[2,1,64,512]{3,2,1,0:T(8,128)(2,1)S(1)}, u32[]{:S(2)}, u32[]{:S(2)}) collective-permute-start(bf16[2,1,64,512]{3,2,1,0:T(8,128)(2,1)S(1)} %add_convert_fusion.14), channel_id=1, source_target_pairs={{0,8},{4,12},{8,0},{12,4},{1,9},{5,13},{9,1},{13,5},{2,10},{6,14},... | collective-permute-start | bytes 393224 | tf_op jit(solution)/shard_map/ppermute | solution.py:54
  111.3 8.0 %collective-permute-start.17 = (bf16[2,1,64,640]{3,2,1,0:T(8,128)(2,1)S(1)}, bf16[2,1,64,640]{3,2,1,0:T(8,128)(2,1)S(1)}, u32[]{:S(2)}, u32[]{:S(2)}) collective-permute-start(bf16[2,1,64,640]{3,2,1,0:T(8,128)(2,1)S(1)} %add_convert_fusion.9), channel_id=1, source_target_pairs={{0,4},{4,0},{8,12},{12,8},{1,5},{5,1},{9,13},{13,9},{2,6},{6,2},{1... | collective-permute-start | bytes 491528 | tf_op jit(solution)/shard_map/ppermute | solution.py:54
  115.8 9.1 %collective-permute-start.16 = (bf16[2,1,64,512]{3,2,1,0:T(8,128)(2,1)S(1)}, bf16[2,1,64,512]{3,2,1,0:T(8,128)(2,1)S(1)}, u32[]{:S(2)}, u32[]{:S(2)}) collective-permute-start(bf16[2,1,64,512]{3,2,1,0:T(8,128)(2,1)S(1)} %add_convert_fusion.13), channel_id=1, source_target_pairs={{0,8},{4,12},{8,0},{12,4},{1,9},{5,13},{9,1},{13,5},{2,10},{6,14},... | collective-permute-start | bytes 393224 | tf_op jit(solution)/shard_map/ppermute | solution.py:54
  116.6 8.7 %collective-permute-start.22 = (f32[32,1024]{1,0:T(8,128)S(1)}, f32[32,1024]{1,0:T(8,128)S(1)}, u32[]{:S(2)}, u32[]{:S(2)}) collective-permute-start(f32[32,1024]{1,0:T(8,128)S(1)} %add.91), channel_id=1, source_target_pairs={{0,4},{4,0},{8,12},{12,8},{1,5},{5,1},{9,13},{13,9},{2,6},{6,2},{1... | collective-permute-start | bytes 393224 | tf_op jit(solution)/shard_map/ppermute | solution.py:54
  119.2 7.6 %collective-permute-start.21 = (bf16[2,1,64,512]{3,2,1,0:T(8,128)(2,1)S(1)}, bf16[2,1,64,512]{3,2,1,0:T(8,128)(2,1)S(1)}, u32[]{:S(2)}, u32[]{:S(2)}) collective-permute-start(bf16[2,1,64,512]{3,2,1,0:T(8,128)(2,1)S(1)} %add_convert_fusion.12), channel_id=1, source_target_pairs={{0,4},{4,0},{8,12},{12,8},{1,5},{5,1},{9,13},{13,9},{2,6},{6,2},{1... | collective-permute-start | bytes 393224 | tf_op jit(solution)/shard_map/ppermute | solution.py:54
  119.4 7.5 %collective-permute-start.20 = (bf16[2,2,64,640]{3,2,1,0:T(8,128)(2,1)S(1)}, bf16[2,2,64,640]{3,2,1,0:T(8,128)(2,1)S(1)}, u32[]{:S(2)}, u32[]{:S(2)}) collective-permute-start(bf16[2,2,64,640]{3,2,1,0:T(8,128)(2,1)S(1)} %constant_dynamic-update-slice_fusion), channel_id=1, source_target_pairs={{0,2},{2,0},{1,3},{3,1},{4,6},{6,4},{5,7},{7,5},{8,10},{10,8},{9,1... | collective-permute-start | bytes 983048 | tf_op jit(solution)/shard_map/ppermute | solution.py:54
  126.9 10.7 %collective-permute-start.23 = (bf16[2,4,64,640]{3,2,1,0:T(8,128)(2,1)S(1)}, bf16[2,4,64,640]{3,2,1,0:T(8,128)(2,1)S(1)}, u32[]{:S(2)}, u32[]{:S(2)}) collective-permute-start(bf16[2,4,64,640]{3,2,1,0:T(8,128)(2,1)S(1)} %constant_dynamic-update-slice_fusion.4), channel_id=1, source_target_pairs={{0,16},{16,0},{1,17},{17,1},{2,18},{18,2},{3,19},{19,3},{4,20},{20... | collective-permute-start | bytes 1966088 | tf_op jit(solution)/shard_map/ppermute | solution.py:54
  128.2 5.0 %collective-permute-start.25 = (bf16[2,1,64,512]{3,2,1,0:T(8,128)(2,1)S(1)}, bf16[2,1,64,512]{3,2,1,0:T(8,128)(2,1)S(1)}, u32[]{:S(2)}, u32[]{:S(2)}) collective-permute-start(bf16[2,1,64,512]{3,2,1,0:T(8,128)(2,1)S(1)} %add_convert_fusion.11), channel_id=1, source_target_pairs={{0,4},{4,0},{8,12},{12,8},{1,5},{5,1},{9,13},{13,9},{2,6},{6,2},{1... | collective-permute-start | bytes 393224 | tf_op jit(solution)/shard_map/ppermute | solution.py:54
  129.2 7.3 %collective-permute-start.24 = (f32[32,1024]{1,0:T(8,128)S(1)}, f32[32,1024]{1,0:T(8,128)S(1)}, u32[]{:S(2)}, u32[]{:S(2)}) collective-permute-start(f32[32,1024]{1,0:T(8,128)S(1)} %add.94), channel_id=1, source_target_pairs={{0,8},{4,12},{8,0},{12,4},{1,9},{5,13},{9,1},{13,5},{2,10},{6,14},... | collective-permute-start | bytes 393224 | tf_op jit(solution)/shard_map/ppermute | solution.py:54
  137.6 10.4 %copy-start.3 = (bf16[2,8,64,640]{3,2,1,0:T(8,128)(2,1)}, bf16[2,8,64,640]{3,2,1,0:T(8,128)(2,1)S(1)}, u32[]{:S(2)}) copy-start(bf16[2,8,64,640]{3,2,1,0:T(8,128)(2,1)S(1)} %constant_dynamic-update-slice_fusion.8.mine_ref) | copy-start | bytes 3932164
  137.7 10.4 %collective-permute-start.26 = (bf16[2,8,64,640]{3,2,1,0:T(8,128)(2,1)S(1)}, bf16[2,8,64,640]{3,2,1,0:T(8,128)(2,1)S(1)}, u32[]{:S(2)}, u32[]{:S(2)}) collective-permute-start(bf16[2,8,64,640]{3,2,1,0:T(8,128)(2,1)S(1)} %constant_dynamic-update-slice_fusion.8.mine_ref), channel_id=1, source_target_pairs={{0,1},{1,0},{2,3},{3,2},{4,5},{5,4},{6,7},{7,6},{8,9},{9,8},{10,11... | collective-permute-start | bytes 3932168 | tf_op jit(solution)/shard_map/ppermute | solution.py:54
  137.7 8.7 %collective-permute-start.28 = (bf16[2,2,64,512]{3,2,1,0:T(8,128)(2,1)S(1)}, bf16[2,2,64,512]{3,2,1,0:T(8,128)(2,1)S(1)}, u32[]{:S(2)}, u32[]{:S(2)}) collective-permute-start(bf16[2,2,64,512]{3,2,1,0:T(8,128)(2,1)S(1)} %constant_dynamic-update-slice_fusion.2), channel_id=1, source_target_pairs={{0,16},{16,0},{1,17},{17,1},{2,18},{18,2},{3,19},{19,3},{4,20},{20... | collective-permute-start | bytes 786440 | tf_op jit(solution)/shard_map/ppermute | solution.py:54
  139.1 8.9 %collective-permute-start.27 = (bf16[2,2,64,512]{3,2,1,0:T(8,128)(2,1)S(1)}, bf16[2,2,64,512]{3,2,1,0:T(8,128)(2,1)S(1)}, u32[]{:S(2)}, u32[]{:S(2)}) collective-permute-start(bf16[2,2,64,512]{3,2,1,0:T(8,128)(2,1)S(1)} %constant_dynamic-update-slice_fusion.6), channel_id=1, source_target_pairs={{0,2},{2,0},{1,3},{3,1},{4,6},{6,4},{5,7},{7,5},{8,10},{10,8},{9,1... | collective-permute-start | bytes 786440 | tf_op jit(solution)/shard_map/ppermute | solution.py:54
  146.5 13.6 %collective-permute-start.30 = (bf16[2,4,64,512]{3,2,1,0:T(8,128)(2,1)S(1)}, bf16[2,4,64,512]{3,2,1,0:T(8,128)(2,1)S(1)}, u32[]{:S(2)}, u32[]{:S(2)}) collective-permute-start(bf16[2,4,64,512]{3,2,1,0:T(8,128)(2,1)S(1)} %constant_dynamic-update-slice_fusion.10), channel_id=1, source_target_pairs={{0,2},{2,0},{1,3},{3,1},{4,6},{6,4},{5,7},{7,5},{8,10},{10,8},{9,1... | collective-permute-start | bytes 1572872 | tf_op jit(solution)/shard_map/ppermute | solution.py:54
  148.1 1.1 copy-start.8
  160.1 2.7 %copy-start.4 = (bf16[2,8,64,512]{3,2,1,0:T(8,128)(2,1)}, bf16[2,8,64,512]{3,2,1,0:T(8,128)(2,1)S(1)}, u32[]{:S(2)}) copy-start(bf16[2,8,64,512]{3,2,1,0:T(8,128)(2,1)S(1)} %constant_dynamic-update-slice_fusion.14.mine_ref) | copy-start | bytes 3145732
  160.1 2.7 %collective-permute-start.31 = (bf16[2,8,64,512]{3,2,1,0:T(8,128)(2,1)S(1)}, bf16[2,8,64,512]{3,2,1,0:T(8,128)(2,1)S(1)}, u32[]{:S(2)}, u32[]{:S(2)}) collective-permute-start(bf16[2,8,64,512]{3,2,1,0:T(8,128)(2,1)S(1)} %constant_dynamic-update-slice_fusion.14.mine_ref), channel_id=1, source_target_pairs={{0,1},{1,0},{2,3},{3,2},{4,5},{5,4},{6,7},{7,6},{8,9},{9,8},{10,11... | collective-permute-start | bytes 3145736 | tf_op jit(solution)/shard_map/ppermute | solution.py:54
  160.2 14.3 %collective-permute-start.29 = (bf16[2,4,64,512]{3,2,1,0:T(8,128)(2,1)S(1)}, bf16[2,4,64,512]{3,2,1,0:T(8,128)(2,1)S(1)}, u32[]{:S(2)}, u32[]{:S(2)}) collective-permute-start(bf16[2,4,64,512]{3,2,1,0:T(8,128)(2,1)S(1)} %constant_dynamic-update-slice_fusion.12), channel_id=1, source_target_pairs={{0,16},{16,0},{1,17},{17,1},{2,18},{18,2},{3,19},{19,3},{4,20},{20... | collective-permute-start | bytes 1572872 | tf_op jit(solution)/shard_map/ppermute | solution.py:54
  161.5 13.1 %copy-start.12 = (f32[2,1,128]{2,1,0:T(1,128)S(1)}, f32[2,1,128]{2,1,0:T(1,128)}, u32[]{:S(2)}) copy-start(f32[2,1,128]{2,1,0:T(1,128)} %get-tuple-element.214) | copy-start | bytes 3076
  162.8 1.0 copy-start.10
  174.5 2.7 %copy-start.5 = (bf16[2,8,64,512]{3,2,1,0:T(8,128)(2,1)}, bf16[2,8,64,512]{3,2,1,0:T(8,128)(2,1)S(1)}, u32[]{:S(2)}) copy-start(bf16[2,8,64,512]{3,2,1,0:T(8,128)(2,1)S(1)} %constant_dynamic-update-slice_fusion.16.mine_ref) | copy-start | bytes 3145732
  174.5 2.7 %collective-permute-start.32 = (bf16[2,8,64,512]{3,2,1,0:T(8,128)(2,1)S(1)}, bf16[2,8,64,512]{3,2,1,0:T(8,128)(2,1)S(1)}, u32[]{:S(2)}, u32[]{:S(2)}) collective-permute-start(bf16[2,8,64,512]{3,2,1,0:T(8,128)(2,1)S(1)} %constant_dynamic-update-slice_fusion.16.mine_ref), channel_id=1, source_target_pairs={{0,1},{1,0},{2,3},{3,2},{4,5},{5,4},{6,7},{7,6},{8,9},{9,8},{10,11... | collective-permute-start | bytes 3145736 | tf_op jit(solution)/shard_map/ppermute | solution.py:54
  177.3 1.0 copy-start.9

commit v6 on v5

--- a/solution.py
+++ b/solution.py
@@ -15,11 +15,6 @@
 MARGIN = 16
 CHUNKS = 2
 VMEM = 56 << 20
-ORDER = (
-    "in0", "in1", "top", "small", "in0", "top", "in1", "small", "in0", "top", "in1", "small",
-    "in0", "top", "in1", "small", "in0", "top", "in1", "small", "top", "in0", "in1", "top",
-    "write_top", "in0", "in0", "write0", "in1", "in1", "write1",
-)
 SMEM_SPEC = pl.BlockSpec(memory_space=pltpu.SMEM)
 F32 = jnp.float32
 BF16 = jnp.bfloat16
@@ -122,9 +117,18 @@
         else:
             self.pending[name] = exchange(values, axis)
 
-    def step(self, name, start=True):
+    def meet(self, *names):
+        met = lax.optimization_barrier(tuple(self.values[name] for name in names))
+        self.values.update(zip(names, met))
+        for name in names:
+            if name in self.steps and name not in self.pending:
+                self.start(name)
+
+    def step(self, name, start=True, tied=False):
         kind, _ = self.steps[name].pop(0)
-        got = self.after_last(self.pending.pop(name))
+        got = self.pending.pop(name)
+        if tied:
+            got = self.after_last(got)
         own = self.values[name]
         if kind == "halve":
             own = own[:, : got.shape[1]]
@@ -399,57 +403,35 @@
 
 
 def outer_kernel(
-    own_ref,
-    active_ref,
-    dresidual_ref,
-    final_ref,
-    dlogits_ref,
-    send_ref,
-    keep_ref,
-    update_ref,
-    head_ref,
+    own_ref, active_ref, dresidual_ref, final_ref, dlogits_ref, send_ref, keep_ref, product_ref
 ):
-    core, place = own_ref[0], own_ref[1]
-    _, places, rows, _ = keep_ref.shape
-    half_out = update_ref.shape[1] // 2
-    half_head = head_ref.shape[1] // 2
-    update_ref[...] = dot(active_ref[...], dresidual_ref[...], 0, 0)
-    head_ref[...] = dot(final_ref[...], dlogits_ref[...], 0, 0)
-    for index in range(places):
-        piece = index ^ (place & (places - 1))
-        for side, target in ((core, keep_ref), (1 - core, send_ref)):
-            here = pl.ds(pl.multiple_of(index * 2 * rows + side * rows, rows), rows)
-            for group in range(2):
-                target[group, piece, :, :half_out] = update_ref[
-                    here, group * half_out : (group + 1) * half_out
-                ].astype(BF16)
-                target[group, piece, :, half_out:] = head_ref[
-                    here, group * half_head : (group + 1) * half_head
-                ].astype(BF16)
+    width = dresidual_ref.shape[1]
+    product_ref[:, :width] = dot(active_ref[...], dresidual_ref[...], 0, 0)
+    product_ref[:, width:] = dot(final_ref[...], dlogits_ref[...], 0, 0)
+    write_pieces(own_ref, product_ref, send_ref, keep_ref, 0)
 
 
 def outer(own, active, dresidual, final, dlogits):
-    steps = 4
     rows, model = active.shape
-    symbols = dlogits.shape[1]
-    places = PLACES // steps
-    block = model // steps
-    piece = (model // (2 * PLACES), (model + symbols) // 2)
-    shape = jax.ShapeDtypeStruct((2, PLACES) + piece, BF16)
-    out = pl.BlockSpec(
-        (2, places) + piece, lambda i, own_ref: (0, i ^ (own_ref[1] // places), 0, 0)
-    )
-    column = pl.BlockSpec((rows, block), lambda i, own_ref: (0, i))
+    half_out = dresidual.shape[1] // 2
+    half_head = dlogits.shape[1] // 2
+    width = half_out + half_head
+    piece = (PLACES, model // (2 * PLACES), width)
+    shape = jax.ShapeDtypeStruct((2,) + piece, BF16)
+    out = pl.BlockSpec((1,) + piece, lambda i: (i, 0, 0, 0))
     return pl.pallas_call(
         outer_kernel,
+        grid=(2,),
         out_shape=(shape, shape),
-        grid_spec=pltpu.PrefetchScalarGridSpec(
-            num_scalar_prefetch=1,
-            grid=(steps,),
-            in_specs=[column, fixed(rows, model), column, fixed(rows, symbols)],
-            out_specs=(out, out),
-            scratch_shapes=[pltpu.VMEM((block, model), F32), pltpu.VMEM((block, symbols), F32)],
-        ),
+        in_specs=[
+            SMEM_SPEC,
+            fixed(rows, model),
+            pl.BlockSpec((rows, half_out), lambda i: (0, i)),
+            fixed(rows, model),
+            pl.BlockSpec((rows, half_head), lambda i: (0, i)),
+        ],
+        out_specs=(out, out),
+        scratch_shapes=[pltpu.VMEM((model, width), F32)],
         compiler_params=params(),
         cost_estimate=cost(5),
         name="outer",
@@ -550,15 +532,18 @@
     )(own, lengths, dresidual, weight_out, slope, gated, gate, turned, depth)
 
 
-def taps_kernel(lengths_ref, gated_ref, dconv_ref, out_ref, pad_ref, sums_ref):
+def taps_kernel(lengths_ref, gated_ref, *refs):
+    *dconv_refs, out_ref, pad_ref, sums_ref = refs
     utterances = pad_ref.shape[1]
     frames = pad_ref.shape[2] - 2 * MARGIN
     taps = out_ref.shape[0] - 1
+    step = pl.program_id(0)
+    per_chunk = pl.num_programs(0) // len(dconv_refs)
     valid = lengths_ref[0]
     for utterance in range(1, utterances):
         valid = valid + lengths_ref[utterance]
 
-    @pl.when(pl.program_id(0) == 0)
+    @pl.when(step == 0)
     def _():
         clear_margins(pad_ref)
 
@@ -567,43 +552,55 @@
         for utterance in range(utterances):
             rows = slice(utterance * frames, (utterance + 1) * frames)
             pad_ref[lane, utterance, MARGIN : MARGIN + frames, :] = gated_ref[rows, columns]
-        sums_ref[...] = jnp.zeros_like(sums_ref)
-
-        def one(utterance, carry, lane=lane, columns=columns):
-            for start in range(0, frames, TILE):
-                rows = pl.ds(pl.multiple_of(utterance * frames + start, TILE), TILE)
-                dconv = dconv_ref[rows, columns]
-                for tap, view in shifted_views(pad_ref, lane, utterance, start, taps):
-                    sums_ref[tap] += jnp.sum((view * dconv).reshape(TILE // 8, 8, LANES), axis=0)
-            return carry
-
-        lax.fori_loop(0, utterances, one, 0)
-        out_ref[:taps, columns] = jnp.sum(sums_ref[...], axis=1)
+
+    for chunk, dconv_ref in enumerate(dconv_refs):
+
+        @pl.when(step // per_chunk == chunk)
+        def _(dconv_ref=dconv_ref):
+            for lane in range(WIDE // LANES):
+                columns = slice(lane * LANES, (lane + 1) * LANES)
+                sums_ref[...] = jnp.zeros_like(sums_ref)
+
+                def one(utterance, carry, lane=lane, columns=columns):
+                    for start in range(0, frames, TILE):
+                        rows = pl.ds(pl.multiple_of(utterance * frames + start, TILE), TILE)
+                        dconv = dconv_ref[rows, columns]
+                        for tap, view in shifted_views(pad_ref, lane, utterance, start, taps):
+                            sums_ref[tap] += jnp.sum(
+                                (view * dconv).reshape(TILE // 8, 8, LANES), axis=0
+                            )
+                    return carry
+
+                lax.fori_loop(0, utterances, one, 0)
+                out_ref[:taps, columns] = jnp.sum(sums_ref[...], axis=1)
+
     out_ref[taps:, :] = jnp.zeros((1, WIDE), F32) + valid.astype(F32)
 
 
-def tap_sums(lengths, gated, dconv, taps, chunk, utterances):
-    rows, width = dconv.shape
-    steps = width // WIDE
-    first = chunk * steps
+def tap_sums(lengths, gated, dconvs, taps, utterances):
+    rows, model = gated.shape
+    steps = model // WIDE
+    per_chunk = steps // len(dconvs)
+
+    def part(chunk):
+        low = chunk * per_chunk
+        return pl.BlockSpec((rows, WIDE), lambda i: (0, jnp.clip(i - low, 0, per_chunk - 1)))
+
     return pl.pallas_call(
         taps_kernel,
         grid=(steps,),
-        out_shape=jax.ShapeDtypeStruct((taps + 1, width), F32),
-        in_specs=[
-            SMEM_SPEC,
-            pl.BlockSpec((rows, WIDE), lambda i: (0, first + i)),
-            pl.BlockSpec((rows, WIDE), lambda i: (0, i)),
-        ],
+        out_shape=jax.ShapeDtypeStruct((taps + 1, model), F32),
+        in_specs=[SMEM_SPEC, pl.BlockSpec((rows, WIDE), lambda i: (0, i))]
+        + [part(chunk) for chunk in range(len(dconvs))],
         out_specs=pl.BlockSpec((taps + 1, WIDE), lambda i: (0, i)),
         scratch_shapes=[
             pltpu.VMEM((WIDE // LANES, utterances, rows // utterances + 2 * MARGIN, LANES), F32),
             pltpu.VMEM((taps, 8, LANES), F32),
         ],
         compiler_params=params(),
-        cost_estimate=cost(1),
+        cost_estimate=cost(9),
         name="taps",
-    )(lengths, gated, dconv)
+    )(lengths, gated, *dconvs)
 
 
 def gain_row(weight, grad):
@@ -816,23 +813,23 @@
         line.begin(name, send, keep, orders[chunk])
         line.put(name + "_conv", dconv)
 
-    def tap_rows(name, chunk):
-        dconv = line.before_kernel(line.values[name + "_conv"])
-        line.put(name + "_taps", tap_sums(lengths, gated, dconv, taps, chunk, utterances))
-
     send, keep = outer(owns[1], active, dresidual, final, dlogits)
     send, keep, dresidual = tie((send, keep, dresidual))
     line.begin("top", send, keep, orders[1])
     products("in0", 0)
-    line.step("top", False)
+    line.step("top", start=False)
     products("in1", 1)
-    line.step("top")
-    line.step("in0")
-    line.step("in1")
-    tap_rows("in0", 0)
-    tap_rows("in1", 1)
-    small = jnp.concatenate([line.values["in0_taps"], line.values["in1_taps"]], axis=1)
-    line.begin_small("small", small)
+    line.last = None
+    line.step("top", start=False)
+    line.step("in0", start=False, tied=True)
+    line.step("in1", start=False, tied=True)
+    line.meet("top", "in0", "in1", "in0_conv", "in1_conv")
+    dconvs = (line.values["in0_conv"], line.values["in1_conv"])
+    line.put("taps", tap_sums(lengths, gated, dconvs, taps, utterances))
+    line.begin_small("small", line.values["taps"])
+    line.step("in0", tied=True)
+    line.step("in1", tied=True, start=False)
+    line.step("top", tied=True)
     written = {}
 
     def write_top():
@@ -841,7 +838,7 @@
             utts,
             owns[1],
             line.values["small"],
-            line.after_last(mine),
+            mine,
             other,
             head_weight,
             gain_out[None],
@@ -858,7 +855,7 @@
             utts,
             owns[chunk],
             line.values["small"],
-            line.after_last(mine),
+            mine,
             other,
             weight_in,
             gain_conv[None],
@@ -867,16 +864,32 @@
         )
         line.put("by_in", by_in)
 
-    writes = {
-        "write_top": write_top,
-        "write0": functools.partial(write_in, 0, "in0"),
-        "write1": functools.partial(write_in, 1, "in1"),
-    }
-    for name in ORDER:
-        if name in writes:
-            writes[name]()
-        else:
-            line.step(name)
+    line.step("small")
+    line.meet("in1", "small")
+    line.step("small")
+    line.step("in1", start=False)
+    line.meet("in1", "small")
+    line.step("small")
+    line.step("small")
+    line.step("in1", start=False)
+    line.meet("in1", "small")
+    line.step("small")
+    line.step("in1", start=False)
+    line.meet("in1", "small")
+    for _ in range(4):
+        line.step("top")
+    line.step("in1", tied=True)
+    line.step("top")
+    line.step("top")
+    write_top()
+    while line.steps["in0"]:
+        line.step("in0")
+    line.step("in1")
+    line.last = "by_head"
+    line.step("in1", tied=True)
+    write_in(0, "in0")
+    line.step("in1")
+    write_in(1, "in1")
     return (
         line.values["by_in"].reshape(model),
         written["in"],

time: 186 us -> 184 us (0.989)
  waiting for transfers between devices: 56.8 us -> 66.3 us
  starting transfers between devices: 36.4 us -> 29.7 us
  Pallas kernels: 80 us -> 77.3 us
    ppermute x33, waiting for transfers between devices: 56.8 us -> 66.3 us  [exchange(): return lax.ppermute(values, axis, [(i, i ^ bit) for i in range(size)])]
    ppermute x33, starting transfers between devices: 36.4 us -> 29.7 us  [exchange(): return lax.ppermute(values, axis, [(i, i ^ bit) for i in range(size)])]
    pallas_call x2 -> x1, Pallas kernels: 8.85 us -> 7.14 us  [tap_sums(): pl.pallas_call(taps_kernel, grid=(steps,), out_shape=jax.ShapeDtypeStruct...]
    unnamed x35 -> x28, local copies, waits for them, and re-layouts: 4.46 us -> 4.2 us
  transfers between devices with their start and end apart: 33 -> 33, of which waited for: 18 -> 15; matrix products, arithmetic and copies ran while one was open for 3% -> 3% of each run, Pallas kernels for 31% -> 30%
where the time goes in v6:
time: 184 us
  Pallas kernels  77.3 us (42%)
  waiting for transfers between devices  66.3 us (36%)
  starting transfers between devices  29.7 us (16%)
  local copies, waits for them, and re-layouts  5.17 us (3%)
  other arithmetic  4.26 us (2%)
    ppermute x33, waiting for transfers between devices, exchange(): return lax.ppermute(values, axis, [(i, i ^ bit) for i in range(size)])  66.3 us
    ppermute x33, starting transfers between devices, exchange(): return lax.ppermute(values, axis, [(i, i ^ bit) for i in range(size)])  29.7 us
    pallas_call x2, Pallas kernels, inner(): pl.pallas_call(inner_kernel, grid=(steps,), out_shape=(shape, shape, jax....  21.5 us
    pallas_call x1, Pallas kernels, forward(): pl.pallas_call(forward_kernel, grid=(steps,), out_shape=(jax.ShapeDtypeSt...  15.2 us
    pallas_call x2, Pallas kernels, unpack_inner(): pl.pallas_call(functools.partial(unpack_inner_kernel, utts, chunk == CHUN...  13.2 us
    pallas_call x1, Pallas kernels, tap_sums(): pl.pallas_call(taps_kernel, grid=(steps,), out_shape=jax.ShapeDtypeStruct...  7.14 us
    pallas_call x1, Pallas kernels, unpack_top(): pl.pallas_call(functools.partial(unpack_top_kernel, utts), out_shape=(jax...  5.68 us
    pallas_call x1, Pallas kernels, outer(): pl.pallas_call(outer_kernel, grid=(2,), out_shape=(shape, shape), in_spec...  5.33 us
  transfers between devices with their start and end apart: 33, of which 15 were waited for; matrix products, arithmetic and copies ran while one was open for 3% of the time, Pallas kernels for 30%

profile of v6, /device:TPU:0, one launch (start us, length us, event | category | flops | bytes accessed | tf_op | source)
XLA Modules:
  0.0 183.9 jit_solution(14664272779703389908)
XLA Ops:
  0.6 4.0 %teachers.1 = (f32[2,256,256]{2,1,0:T(8,128)}, f32[2,256,256]{2,1,0:T(8,128)}) custom-call(s32[1]{0:T(128)} %bitcast.6.member_ref, bf16[2,4,256,256]{3,2,1,0:T(8,128)(2,1)} %logits_ref.1), custom_call_target="tpu_custom_call" | custom-call | flops 4600000000 | bytes 1048576 | tf_op jit(solution)/shard_map/teachers/pallas_call | solution.py:190
  4.6 2.9 %collective-permute-start = (f32[2,256,256]{2,1,0:T(8,128)}, f32[2,256,256]{2,1,0:T(8,128)S(1)}, u32[]{:S(2)}, u32[]{:S(2)}) collective-permute-start(f32[2,256,256]{2,1,0:T(8,128)} %get-tuple-element.70), channel_id=1, source_target_pairs={{0,16},{16,0},{1,17},{17,1},{2,18},{18,2},{3,19},{19,3},{4,20},{20... | collective-permute-start | bytes 1572872 | tf_op jit(solution)/shard_map/ppermute | solution.py:49
  7.6 15.2 %forward.1 = (bf16[1024,512]{1,0:T(8,128)(2,1)}, f32[512,1024]{1,0:T(8,128)}, f32[512,1024]{1,0:T(8,128)}, f32[512,1024]{1,0:T(8,128)}, bf16[512,1024]{1,0:T(8,128)(2,1)}, /*index=5*/f32[512,1024]{1,0:T(8,128)}) custom-call(s32[2]{0:T(128)} %lengths_ref.9, bf16[512,1024]{1,0:T(8,128)(2,1)} %bitcast.9, f32[1,1024]{1,0:T(1,128)} %bitcast.12, ...), custom_call_target="tpu_custom_call" | custom-call | flops 17250000896 | bytes 1048576 | tf_op jit(solution)/shard_map/forward/pallas_call | solution.py:315
  23.3 0.8 copy-done.10
  24.2 5.3 %top.1 = (f32[2,1,128]{2,1,0:T(1,128)}, bf16[512,1024]{1,0:T(8,128)(2,1)}, bf16[512,256]{1,0:T(8,128)(2,1)}, bf16[512,1024]{1,0:T(8,128)(2,1)}) custom-call(s32[2]{0:T(128)} %lengths_ref.9, f32[512,1024]{1,0:T(8,128)} %get-tuple-element.68.residual_ref, f32[1,1024]{1,0:T(1,128)} %bitcast.10, bf16[1024,256]{1,0:T(8,128)(2,1)} %head_ref.3, ...), custom_call_target="tpu_custom_call" | custom-call | flops 5750000128 | bytes 1048576 | tf_op jit(solution)/shard_map/top/pallas_call | solution.py:383
  29.5 5.3 %outer.1 = (bf16[2,8,64,640]{3,2,1,0:T(8,128)(2,1)}, bf16[2,8,64,640]{3,2,1,0:T(8,128)(2,1)}) custom-call(s32[2]{0:T(128)} %pad_add_fusion.own_ref, bf16[512,1024]{1,0:T(8,128)(2,1)} %get-tuple-element.67.active_ref, bf16[512,1024]{1,0:T(8,128)(2,1)} %get-tuple-element.86.dresidual_ref, bf16[512,1024]{1,0:T(8,128)(2,1)} %get-tuple-element.72.final_ref, ...), custom_call_target="tpu_custom_call" | custom-call | flops 5750000128 | bytes 1048576 | tf_op jit(solution)/shard_map/outer/pallas_call | solution.py:422
  35.4 10.8 %inner.2 = (bf16[2,8,64,512]{3,2,1,0:T(8,128)(2,1)}, bf16[2,8,64,512]{3,2,1,0:T(8,128)(2,1)}, f32[512,512]{1,0:T(8,128)}) custom-call(s32[2]{0:T(128)} %pad_add_fusion.1.own_ref, s32[2]{0:T(128)} %lengths_ref.9, bf16[512,1024]{1,0:T(8,128)(2,1)} %get-tuple-element.86.dresidual_ref, bf16[1024,1024]{1,0:T(8,128)(2,1)} %out_weight_ref.5, ...), custom_call_target="tpu_custom_call" | custom-call | flops 12650000384 | bytes 1048576 | tf_op jit(solution)/shard_map/inner/pallas_call | solution.py:507
  47.3 10.7 %inner.3 = (bf16[2,8,64,512]{3,2,1,0:T(8,128)(2,1)}, bf16[2,8,64,512]{3,2,1,0:T(8,128)(2,1)}, f32[512,512]{1,0:T(8,128)}) custom-call(s32[2]{0:T(128)} %pad_add_fusion.own_ref, s32[2]{0:T(128)} %lengths_ref.9, bf16[512,1024]{1,0:T(8,128)(2,1)} %get-tuple-element.86.dresidual_ref, bf16[1024,1024]{1,0:T(8,128)(2,1)} %out_weight_ref.5, ...), custom_call_target="tpu_custom_call" | custom-call | flops 12650000384 | bytes 1048576 | tf_op jit(solution)/shard_map/inner/pallas_call | solution.py:507
  58.1 5.8 %collective-permute-done.3 = bf16[2,4,64,640]{3,2,1,0:T(8,128)(2,1)S(1)} collective-permute-done((bf16[2,4,64,640]{3,2,1,0:T(8,128)(2,1)S(1)}, bf16[2,4,64,640]{3,2,1,0:T(8,128)(2,1)S(1)}, u32[]{:S(2)}, u32[]{:S(2)}) %collective-permute-start.3) | collective-permute-done | bytes 655392 | tf_op jit(solution)/shard_map/ppermute | solution.py:49
  64.9 1.6 collective-permute-start.5
  67.4 7.1 %taps.1 = f32[32,1024]{1,0:T(8,128)} custom-call(s32[2]{0:T(128)} %lengths_ref.9, f32[512,1024]{1,0:T(8,128)} %get-tuple-element.78.gated_ref, f32[512,512]{1,0:T(8,128)} %get-tuple-element.98.refs_0_, f32[512,512]{1,0:T(8,128)} %get-tuple-element.99.refs_1_), custom_call_target="tpu_custom_call" | custom-call | flops 10350000128 | bytes 1048576 | tf_op jit(solution)/shard_map/taps/pallas_call | solution.py:589
  74.5 10.4 %collective-permute-done.7 = bf16[2,4,64,512]{3,2,1,0:T(8,128)(2,1)S(1)} collective-permute-done((bf16[2,4,64,512]{3,2,1,0:T(8,128)(2,1)S(1)}, bf16[2,4,64,512]{3,2,1,0:T(8,128)(2,1)S(1)}, u32[]{:S(2)}, u32[]{:S(2)}) %collective-permute-start.7) | collective-permute-done | bytes 524320 | tf_op jit(solution)/shard_map/ppermute | solution.py:49
  85.4 1.6 collective-permute-start.17
  87.0 3.7 %collective-permute-done.17 = bf16[2,1,64,640]{3,2,1,0:T(8,128)(2,1)S(1)} collective-permute-done((bf16[2,1,64,640]{3,2,1,0:T(8,128)(2,1)S(1)}, bf16[2,1,64,640]{3,2,1,0:T(8,128)(2,1)S(1)}, u32[]{:S(2)}, u32[]{:S(2)}) %collective-permute-start.17) | collective-permute-done | bytes 163872 | tf_op jit(solution)/shard_map/ppermute | solution.py:49
  90.8 2.9 %collective-permute-start.18 = (bf16[2,1,64,640]{3,2,1,0:T(8,128)(2,1)S(1)}, bf16[2,1,64,640]{3,2,1,0:T(8,128)(2,1)S(1)}, u32[]{:S(2)}, u32[]{:S(2)}) collective-permute-start(bf16[2,1,64,640]{3,2,1,0:T(8,128)(2,1)S(1)} %add_convert_fusion.10), channel_id=1, source_target_pairs={{0,8},{4,12},{8,0},{12,4},{1,9},{5,13},{9,1},{13,5},{2,10},{6,14},... | collective-permute-start | bytes 491528 | tf_op jit(solution)/shard_map/ppermute | solution.py:49
  94.4 1.6 collective-permute-start.9
  95.9 1.6 collective-permute-start.26
  97.5 1.3 collective-permute-done.10
  98.9 1.5 collective-permute-start.12
  100.4 1.5 collective-permute-start.19
  102.0 0.8 collective-permute-start.11
  102.8 1.6 collective-permute-done.12
  104.4 2.2 %collective-permute-start.13 = (f32[32,1024]{1,0:T(8,128)S(1)}, f32[32,1024]{1,0:T(8,128)S(1)}, u32[]{:S(2)}, u32[]{:S(2)}) collective-permute-start(f32[32,1024]{1,0:T(8,128)S(1)} %add.86), channel_id=1, source_target_pairs={{0,4},{4,0},{8,12},{12,8},{1,5},{5,1},{9,13},{13,9},{2,6},{6,2},{1... | collective-permute-start | bytes 393224 | tf_op jit(solution)/shard_map/ppermute | solution.py:49
  106.7 1.9 %collective-permute-done.19 = bf16[2,1,64,640]{3,2,1,0:T(8,128)(2,1)S(1)} collective-permute-done((bf16[2,1,64,640]{3,2,1,0:T(8,128)(2,1)S(1)}, bf16[2,1,64,640]{3,2,1,0:T(8,128)(2,1)S(1)}, u32[]{:S(2)}, u32[]{:S(2)}) %collective-permute-start.19) | collective-permute-done | bytes 163872 | tf_op jit(solution)/shard_map/ppermute | solution.py:49
  108.8 0.8 collective-permute-start.27
  109.7 3.0 %collective-permute-done.13 = f32[32,1024]{1,0:T(8,128)S(1)} collective-permute-done((f32[32,1024]{1,0:T(8,128)S(1)}, f32[32,1024]{1,0:T(8,128)S(1)}, u32[]{:S(2)}, u32[]{:S(2)}) %collective-permute-start.13) | collective-permute-done | bytes 131104 | tf_op jit(solution)/shard_map/ppermute | solution.py:49
  112.8 3.0 %collective-permute-start.14 = (bf16[2,1,64,512]{3,2,1,0:T(8,128)(2,1)S(1)}, bf16[2,1,64,512]{3,2,1,0:T(8,128)(2,1)S(1)}, u32[]{:S(2)}, u32[]{:S(2)}) collective-permute-start(bf16[2,1,64,512]{3,2,1,0:T(8,128)(2,1)S(1)} %add_convert_fusion.14), channel_id=1, source_target_pairs={{0,8},{4,12},{8,0},{12,4},{1,9},{5,13},{9,1},{13,5},{2,10},{6,14},... | collective-permute-start | bytes 393224 | tf_op jit(solution)/shard_map/ppermute | solution.py:49
  115.9 0.6 collective-permute-start.23
  116.7 4.0 %collective-permute-done.15 = f32[32,1024]{1,0:T(8,128)S(1)} collective-permute-done((f32[32,1024]{1,0:T(8,128)S(1)}, f32[32,1024]{1,0:T(8,128)S(1)}, u32[]{:S(2)}, u32[]{:S(2)}) %collective-permute-start.15) | collective-permute-done | bytes 131104 | tf_op jit(solution)/shard_map/ppermute | solution.py:49
  120.7 0.7 add.89.small_ref
  121.4 2.9 %collective-permute-done.14 = bf16[2,1,64,512]{3,2,1,0:T(8,128)(2,1)S(1)} collective-permute-done((bf16[2,1,64,512]{3,2,1,0:T(8,128)(2,1)S(1)}, bf16[2,1,64,512]{3,2,1,0:T(8,128)(2,1)S(1)}, u32[]{:S(2)}, u32[]{:S(2)}) %collective-permute-start.14) | collective-permute-done | bytes 131104 | tf_op jit(solution)/shard_map/ppermute | solution.py:49
  124.4 1.3 collective-permute-done.28
  125.7 0.8 collective-permute-start.29
  126.5 2.8 %collective-permute-done.16 = bf16[2,1,64,512]{3,2,1,0:T(8,128)(2,1)S(1)} collective-permute-done((bf16[2,1,64,512]{3,2,1,0:T(8,128)(2,1)S(1)}, bf16[2,1,64,512]{3,2,1,0:T(8,128)(2,1)S(1)}, u32[]{:S(2)}, u32[]{:S(2)}) %collective-permute-start.16) | collective-permute-done | bytes 131104 | tf_op jit(solution)/shard_map/ppermute | solution.py:49
  129.6 1.1 collective-permute-done.29
  130.8 0.7 collective-permute-start.30
  131.5 6.9 %collective-permute-done.30 = bf16[2,2,64,512]{3,2,1,0:T(8,128)(2,1)S(1)} collective-permute-done((bf16[2,2,64,512]{3,2,1,0:T(8,128)(2,1)S(1)}, bf16[2,2,64,512]{3,2,1,0:T(8,128)(2,1)S(1)}, u32[]{:S(2)}, u32[]{:S(2)}) %collective-permute-start.30) | collective-permute-done | bytes 262176 | tf_op jit(solution)/shard_map/ppermute | solution.py:49
  139.1 1.6 collective-permute-start.21
  140.7 15.7 %collective-permute-done.21 = bf16[2,2,64,512]{3,2,1,0:T(8,128)(2,1)S(1)} collective-permute-done((bf16[2,2,64,512]{3,2,1,0:T(8,128)(2,1)S(1)}, bf16[2,2,64,512]{3,2,1,0:T(8,128)(2,1)S(1)}, u32[]{:S(2)}, u32[]{:S(2)}) %collective-permute-start.21) | collective-permute-done | bytes 262176 | tf_op jit(solution)/shard_map/ppermute | solution.py:49
  156.5 0.7 collective-permute-start.22
  157.5 1.2 copy-done.7
  158.7 5.7 %unpack_top.1 = (f32[1024,1024]{1,0:T(8,128)}, f32[1024,256]{1,0:T(8,128)}, f32[1,1024]{1,0:T(1,128)}, f32[31,1024]{1,0:T(8,128)}, f32[2,1,128]{2,1,0:T(1,128)}) custom-call(s32[2]{0:T(128)} %pad_add_fusion.own_ref, f32[32,1024]{1,0:T(8,128)} %add.89.small_ref, bf16[2,8,64,640]{3,2,1,0:T(8,128)(2,1)} %copy-done.4, bf16[2,8,64,640]{3,2,1,0:T(8,128)(2,1)} %copy-done.7, ...), custom_call_target="tpu_custom_call" | custom-call | flops 5750000128 | bytes 1048576 | tf_op jit(solution)/shard_map/unpack_top/pallas_call | solution.py:672
  164.4 3.6 %collective-permute-done.22 = bf16[2,4,64,512]{3,2,1,0:T(8,128)(2,1)S(1)} collective-permute-done((bf16[2,4,64,512]{3,2,1,0:T(8,128)(2,1)S(1)}, bf16[2,4,64,512]{3,2,1,0:T(8,128)(2,1)S(1)}, u32[]{:S(2)}, u32[]{:S(2)}) %collective-permute-start.22) | collective-permute-done | bytes 524320 | tf_op jit(solution)/shard_map/ppermute | solution.py:49
  168.1 1.1 copy-done.8
  169.1 6.5 %unpack_inner.2 = (f32[1024,2048]{1,0:T(8,128)}, f32[1,1024]{1,0:T(1,128)}) custom-call(s32[2]{0:T(128)} %pad_add_fusion.1.own_ref, f32[32,1024]{1,0:T(8,128)} %add.89.small_ref, bf16[2,8,64,512]{3,2,1,0:T(8,128)(2,1)} %copy-done.3, bf16[2,8,64,512]{3,2,1,0:T(8,128)(2,1)} %copy-done.8, bf16[1024,2048]{1,0:T(8,128)(2,1)} %weight_ref.3, f32[1,1024]{1,0:T(1,128)} %bitcast.13), custom_call_target="tpu_custom_call" | custom-call | flops 4600000000 | bytes 1048576 | tf_op jit(solution)/shard_map/unpack_inner/pallas_call | solution.py:736
  175.7 0.6 slice_reduce_fusion
  176.3 1.0 copy-done.9
  177.3 6.6 %unpack_inner.3 = (f32[1024,2048]{1,0:T(8,128)}, f32[1,1024]{1,0:T(1,128)}) custom-call(s32[2]{0:T(128)} %pad_add_fusion.own_ref, f32[32,1024]{1,0:T(8,128)} %add.89.small_ref, bf16[2,8,64,512]{3,2,1,0:T(8,128)(2,1)} %copy-done.6, bf16[2,8,64,512]{3,2,1,0:T(8,128)(2,1)} %copy-done.9, bf16[1024,2048]{1,0:T(8,128)(2,1)} %weight_ref.3, ...), custom_call_target="tpu_custom_call", output_to_operand_aliasing={{0}: (6, {})} | custom-call | flops 4600000000 | bytes 1048576 | tf_op jit(solution)/shard_map/unpack_inner/pallas_call | solution.py:736
  (97 shorter events, 7.4 us)
Async XLA Ops:
  4.6 18.7 %collective-permute-start = (f32[2,256,256]{2,1,0:T(8,128)}, f32[2,256,256]{2,1,0:T(8,128)S(1)}, u32[]{:S(2)}, u32[]{:S(2)}) collective-permute-start(f32[2,256,256]{2,1,0:T(8,128)} %get-tuple-element.70), channel_id=1, source_target_pairs={{0,16},{16,0},{1,17},{17,1},{2,18},{18,2},{3,19},{19,3},{4,20},{20... | collective-permute-start | bytes 1572872 | tf_op jit(solution)/shard_map/ppermute | solution.py:49
  23.3 0.8 copy-start.10
  34.8 11.9 %collective-permute-start.2 = (bf16[2,8,64,640]{3,2,1,0:T(8,128)(2,1)}, bf16[2,8,64,640]{3,2,1,0:T(8,128)(2,1)S(1)}, u32[]{:S(2)}, u32[]{:S(2)}) collective-permute-start(bf16[2,8,64,640]{3,2,1,0:T(8,128)(2,1)} %get-tuple-element.83), channel_id=1, source_target_pairs={{0,1},{1,0},{2,3},{3,2},{4,5},{5,4},{6,7},{7,6},{8,9},{9,8},{10,11... | collective-permute-start | bytes 3932168 | tf_op jit(solution)/shard_map/ppermute | solution.py:49
  35.4 11.3 %copy-start = (bf16[2,8,64,640]{3,2,1,0:T(8,128)(2,1)S(1)}, bf16[2,8,64,640]{3,2,1,0:T(8,128)(2,1)}, u32[]{:S(2)}) copy-start(bf16[2,8,64,640]{3,2,1,0:T(8,128)(2,1)} %get-tuple-element.82) | copy-start | bytes 3932164
  46.2 17.8 %collective-permute-start.1 = (bf16[2,8,64,512]{3,2,1,0:T(8,128)(2,1)}, bf16[2,8,64,512]{3,2,1,0:T(8,128)(2,1)S(1)}, u32[]{:S(2)}, u32[]{:S(2)}) collective-permute-start(bf16[2,8,64,512]{3,2,1,0:T(8,128)(2,1)} %get-tuple-element.81), channel_id=1, source_target_pairs={{0,1},{1,0},{2,3},{3,2},{4,5},{5,4},{6,7},{7,6},{8,9},{9,8},{10,11... | collective-permute-start | bytes 3145736 | tf_op jit(solution)/shard_map/ppermute | solution.py:49
  47.2 16.7 %collective-permute-start.3 = (bf16[2,4,64,640]{3,2,1,0:T(8,128)(2,1)S(1)}, bf16[2,4,64,640]{3,2,1,0:T(8,128)(2,1)S(1)}, u32[]{:S(2)}, u32[]{:S(2)}) collective-permute-start(bf16[2,4,64,640]{3,2,1,0:T(8,128)(2,1)S(1)} %slice.58), channel_id=1, source_target_pairs={{0,16},{16,0},{1,17},{17,1},{2,18},{18,2},{3,19},{19,3},{4,20},{20... | collective-permute-start | bytes 1966088 | tf_op jit(solution)/shard_map/ppermute | solution.py:49
  58.0 6.1 %copy-start.1 = (bf16[2,8,64,512]{3,2,1,0:T(8,128)(2,1)S(1)}, bf16[2,8,64,512]{3,2,1,0:T(8,128)(2,1)}, u32[]{:S(2)}) copy-start(bf16[2,8,64,512]{3,2,1,0:T(8,128)(2,1)} %get-tuple-element.88) | copy-start | bytes 3145732
  58.0 6.4 %copy-start.2 = (bf16[2,8,64,512]{3,2,1,0:T(8,128)(2,1)S(1)}, bf16[2,8,64,512]{3,2,1,0:T(8,128)(2,1)}, u32[]{:S(2)}) copy-start(bf16[2,8,64,512]{3,2,1,0:T(8,128)(2,1)} %get-tuple-element.91) | copy-start | bytes 3145732
  58.0 6.4 %collective-permute-start.4 = (bf16[2,8,64,512]{3,2,1,0:T(8,128)(2,1)}, bf16[2,8,64,512]{3,2,1,0:T(8,128)(2,1)S(1)}, u32[]{:S(2)}, u32[]{:S(2)}) collective-permute-start(bf16[2,8,64,512]{3,2,1,0:T(8,128)(2,1)} %get-tuple-element.87), channel_id=1, source_target_pairs={{0,1},{1,0},{2,3},{3,2},{4,5},{5,4},{6,7},{7,6},{8,9},{9,8},{10,11... | collective-permute-start | bytes 3145736 | tf_op jit(solution)/shard_map/ppermute | solution.py:49
  64.9 20.4 %collective-permute-start.5 = (bf16[2,2,64,640]{3,2,1,0:T(8,128)(2,1)S(1)}, bf16[2,2,64,640]{3,2,1,0:T(8,128)(2,1)S(1)}, u32[]{:S(2)}, u32[]{:S(2)}) collective-permute-start(bf16[2,2,64,640]{3,2,1,0:T(8,128)(2,1)S(1)} %slice.59), channel_id=1, source_target_pairs={{0,2},{2,0},{1,3},{3,1},{4,6},{6,4},{5,7},{7,5},{8,10},{10,8},{9,1... | collective-permute-start | bytes 983048 | tf_op jit(solution)/shard_map/ppermute | solution.py:49
  66.5 18.4 %collective-permute-start.7 = (bf16[2,4,64,512]{3,2,1,0:T(8,128)(2,1)S(1)}, bf16[2,4,64,512]{3,2,1,0:T(8,128)(2,1)S(1)}, u32[]{:S(2)}, u32[]{:S(2)}) collective-permute-start(bf16[2,4,64,512]{3,2,1,0:T(8,128)(2,1)S(1)} %slice.63), channel_id=1, source_target_pairs={{0,2},{2,0},{1,3},{3,1},{4,6},{6,4},{5,7},{7,5},{8,10},{10,8},{9,1... | collective-permute-start | bytes 1572872 | tf_op jit(solution)/shard_map/ppermute | solution.py:49
  67.1 18.0 %collective-permute-start.6 = (bf16[2,4,64,512]{3,2,1,0:T(8,128)(2,1)S(1)}, bf16[2,4,64,512]{3,2,1,0:T(8,128)(2,1)S(1)}, u32[]{:S(2)}, u32[]{:S(2)}) collective-permute-start(bf16[2,4,64,512]{3,2,1,0:T(8,128)(2,1)S(1)} %slice.61), channel_id=1, source_target_pairs={{0,16},{16,0},{1,17},{17,1},{2,18},{18,2},{3,19},{19,3},{4,20},{20... | collective-permute-start | bytes 1572872 | tf_op jit(solution)/shard_map/ppermute | solution.py:49
  74.5 12.5 %copy-start.5 = (f32[32,1024]{1,0:T(8,128)S(1)}, f32[32,1024]{1,0:T(8,128)}, u32[]{:S(2)}) copy-start(f32[32,1024]{1,0:T(8,128)} %taps.1) | copy-start | bytes 393220
  85.4 5.4 %collective-permute-start.17 = (bf16[2,1,64,640]{3,2,1,0:T(8,128)(2,1)S(1)}, bf16[2,1,64,640]{3,2,1,0:T(8,128)(2,1)S(1)}, u32[]{:S(2)}, u32[]{:S(2)}) collective-permute-start(bf16[2,1,64,640]{3,2,1,0:T(8,128)(2,1)S(1)} %slice.77), channel_id=1, source_target_pairs={{0,4},{4,0},{8,12},{12,8},{1,5},{5,1},{9,13},{13,9},{2,6},{6,2},{1... | collective-permute-start | bytes 491528 | tf_op jit(solution)/shard_map/ppermute | solution.py:49
  87.0 6.7 %collective-permute-start.8 = (f32[32,1024]{1,0:T(8,128)S(1)}, f32[32,1024]{1,0:T(8,128)S(1)}, u32[]{:S(2)}, u32[]{:S(2)}) collective-permute-start(f32[32,1024]{1,0:T(8,128)S(1)} %copy-done.5), channel_id=1, source_target_pairs={{0,1},{1,0},{2,3},{3,2},{4,5},{5,4},{6,7},{7,6},{8,9},{9,8},{10,11... | collective-permute-start | bytes 393224 | tf_op jit(solution)/shard_map/ppermute | solution.py:49
  90.8 9.6 %collective-permute-start.18 = (bf16[2,1,64,640]{3,2,1,0:T(8,128)(2,1)S(1)}, bf16[2,1,64,640]{3,2,1,0:T(8,128)(2,1)S(1)}, u32[]{:S(2)}, u32[]{:S(2)}) collective-permute-start(bf16[2,1,64,640]{3,2,1,0:T(8,128)(2,1)S(1)} %add_convert_fusion.10), channel_id=1, source_target_pairs={{0,8},{4,12},{8,0},{12,4},{1,9},{5,13},{9,1},{13,5},{2,10},{6,14},... | collective-permute-start | bytes 491528 | tf_op jit(solution)/shard_map/ppermute | solution.py:49
  93.8 5.1 %collective-permute-start.10 = (f32[32,1024]{1,0:T(8,128)S(1)}, f32[32,1024]{1,0:T(8,128)S(1)}, u32[]{:S(2)}, u32[]{:S(2)}) collective-permute-start(f32[32,1024]{1,0:T(8,128)S(1)} %add.82), channel_id=1, source_target_pairs={{0,16},{16,0},{1,17},{17,1},{2,18},{18,2},{3,19},{19,3},{4,20},{20... | collective-permute-start | bytes 393224 | tf_op jit(solution)/shard_map/ppermute | solution.py:49
  94.4 7.5 %collective-permute-start.9 = (bf16[2,2,64,512]{3,2,1,0:T(8,128)(2,1)S(1)}, bf16[2,2,64,512]{3,2,1,0:T(8,128)(2,1)S(1)}, u32[]{:S(2)}, u32[]{:S(2)}) collective-permute-start(bf16[2,2,64,512]{3,2,1,0:T(8,128)(2,1)S(1)} %slice.65), channel_id=1, source_target_pairs={{0,2},{2,0},{1,3},{3,1},{4,6},{6,4},{5,7},{7,5},{8,10},{10,8},{9,1... | collective-permute-start | bytes 786440 | tf_op jit(solution)/shard_map/ppermute | solution.py:49
  95.9 12.8 %collective-permute-start.26 = (bf16[2,2,64,512]{3,2,1,0:T(8,128)(2,1)S(1)}, bf16[2,2,64,512]{3,2,1,0:T(8,128)(2,1)S(1)}, u32[]{:S(2)}, u32[]{:S(2)}) collective-permute-start(bf16[2,2,64,512]{3,2,1,0:T(8,128)(2,1)S(1)} %slice.78), channel_id=1, source_target_pairs={{0,16},{16,0},{1,17},{17,1},{2,18},{18,2},{3,19},{19,3},{4,20},{20... | collective-permute-start | bytes 786440 | tf_op jit(solution)/shard_map/ppermute | solution.py:49
  98.9 5.5 %collective-permute-start.12 = (f32[32,1024]{1,0:T(8,128)S(1)}, f32[32,1024]{1,0:T(8,128)S(1)}, u32[]{:S(2)}, u32[]{:S(2)}) collective-permute-start(f32[32,1024]{1,0:T(8,128)S(1)} %add.84), channel_id=1, source_target_pairs={{0,2},{2,0},{1,3},{3,1},{4,6},{6,4},{5,7},{7,5},{8,10},{10,8},{9,1... | collective-permute-start | bytes 393224 | tf_op jit(solution)/shard_map/ppermute | solution.py:49
  100.4 8.2 %collective-permute-start.19 = (bf16[2,1,64,640]{3,2,1,0:T(8,128)(2,1)S(1)}, bf16[2,1,64,640]{3,2,1,0:T(8,128)(2,1)S(1)}, u32[]{:S(2)}, u32[]{:S(2)}) collective-permute-start(bf16[2,1,64,640]{3,2,1,0:T(8,128)(2,1)S(1)} %add_convert_fusion.9), channel_id=1, source_target_pairs={{0,4},{4,0},{8,12},{12,8},{1,5},{5,1},{9,13},{13,9},{2,6},{6,2},{1... | collective-permute-start | bytes 491528 | tf_op jit(solution)/shard_map/ppermute | solution.py:49
  102.0 10.8 %collective-permute-start.11 = (bf16[2,1,64,512]{3,2,1,0:T(8,128)(2,1)S(1)}, bf16[2,1,64,512]{3,2,1,0:T(8,128)(2,1)S(1)}, u32[]{:S(2)}, u32[]{:S(2)}) collective-permute-start(bf16[2,1,64,512]{3,2,1,0:T(8,128)(2,1)S(1)} %slice.67), channel_id=1, source_target_pairs={{0,4},{4,0},{8,12},{12,8},{1,5},{5,1},{9,13},{13,9},{2,6},{6,2},{1... | collective-permute-start | bytes 393224 | tf_op jit(solution)/shard_map/ppermute | solution.py:49
  104.4 8.2 %collective-permute-start.13 = (f32[32,1024]{1,0:T(8,128)S(1)}, f32[32,1024]{1,0:T(8,128)S(1)}, u32[]{:S(2)}, u32[]{:S(2)}) collective-permute-start(f32[32,1024]{1,0:T(8,128)S(1)} %add.86), channel_id=1, source_target_pairs={{0,4},{4,0},{8,12},{12,8},{1,5},{5,1},{9,13},{13,9},{2,6},{6,2},{1... | collective-permute-start | bytes 393224 | tf_op jit(solution)/shard_map/ppermute | solution.py:49
  108.7 7.1 %collective-permute-start.20 = (bf16[2,2,64,640]{3,2,1,0:T(8,128)(2,1)S(1)}, bf16[2,2,64,640]{3,2,1,0:T(8,128)(2,1)S(1)}, u32[]{:S(2)}, u32[]{:S(2)}) collective-permute-start(bf16[2,2,64,640]{3,2,1,0:T(8,128)(2,1)S(1)} %pad_maximum_fusion.4), channel_id=1, source_target_pairs={{0,2},{2,0},{1,3},{3,1},{4,6},{6,4},{5,7},{7,5},{8,10},{10,8},{9,1... | collective-permute-start | bytes 983048 | tf_op jit(solution)/shard_map/ppermute | solution.py:49
  108.8 7.7 %collective-permute-start.27 = (bf16[2,1,64,512]{3,2,1,0:T(8,128)(2,1)S(1)}, bf16[2,1,64,512]{3,2,1,0:T(8,128)(2,1)S(1)}, u32[]{:S(2)}, u32[]{:S(2)}) collective-permute-start(bf16[2,1,64,512]{3,2,1,0:T(8,128)(2,1)S(1)} %slice.80), channel_id=1, source_target_pairs={{0,4},{4,0},{8,12},{12,8},{1,5},{5,1},{9,13},{13,9},{2,6},{6,2},{1... | collective-permute-start | bytes 393224 | tf_op jit(solution)/shard_map/ppermute | solution.py:49
  112.7 8.0 %collective-permute-start.15 = (f32[32,1024]{1,0:T(8,128)S(1)}, f32[32,1024]{1,0:T(8,128)S(1)}, u32[]{:S(2)}, u32[]{:S(2)}) collective-permute-start(f32[32,1024]{1,0:T(8,128)S(1)} %add.87), channel_id=1, source_target_pairs={{0,8},{4,12},{8,0},{12,4},{1,9},{5,13},{9,1},{13,5},{2,10},{6,14},... | collective-permute-start | bytes 393224 | tf_op jit(solution)/shard_map/ppermute | solution.py:49
  112.8 11.5 %collective-permute-start.14 = (bf16[2,1,64,512]{3,2,1,0:T(8,128)(2,1)S(1)}, bf16[2,1,64,512]{3,2,1,0:T(8,128)(2,1)S(1)}, u32[]{:S(2)}, u32[]{:S(2)}) collective-permute-start(bf16[2,1,64,512]{3,2,1,0:T(8,128)(2,1)S(1)} %add_convert_fusion.14), channel_id=1, source_target_pairs={{0,8},{4,12},{8,0},{12,4},{1,9},{5,13},{9,1},{13,5},{2,10},{6,14},... | collective-permute-start | bytes 393224 | tf_op jit(solution)/shard_map/ppermute | solution.py:49
  115.9 13.6 %collective-permute-start.23 = (bf16[2,4,64,640]{3,2,1,0:T(8,128)(2,1)S(1)}, bf16[2,4,64,640]{3,2,1,0:T(8,128)(2,1)S(1)}, u32[]{:S(2)}, u32[]{:S(2)}) collective-permute-start(bf16[2,4,64,640]{3,2,1,0:T(8,128)(2,1)S(1)} %pad_maximum_fusion.1), channel_id=1, source_target_pairs={{0,16},{16,0},{1,17},{17,1},{2,18},{18,2},{3,19},{19,3},{4,20},{20... | collective-permute-start | bytes 1966088 | tf_op jit(solution)/shard_map/ppermute | solution.py:49
  116.5 9.2 %collective-permute-start.28 = (bf16[2,1,64,512]{3,2,1,0:T(8,128)(2,1)S(1)}, bf16[2,1,64,512]{3,2,1,0:T(8,128)(2,1)S(1)}, u32[]{:S(2)}, u32[]{:S(2)}) collective-permute-start(bf16[2,1,64,512]{3,2,1,0:T(8,128)(2,1)S(1)} %add_convert_fusion.12), channel_id=1, source_target_pairs={{0,8},{4,12},{8,0},{12,4},{1,9},{5,13},{9,1},{13,5},{2,10},{6,14},... | collective-permute-start | bytes 393224 | tf_op jit(solution)/shard_map/ppermute | solution.py:49
  124.3 5.0 %collective-permute-start.16 = (bf16[2,1,64,512]{3,2,1,0:T(8,128)(2,1)S(1)}, bf16[2,1,64,512]{3,2,1,0:T(8,128)(2,1)S(1)}, u32[]{:S(2)}, u32[]{:S(2)}) collective-permute-start(bf16[2,1,64,512]{3,2,1,0:T(8,128)(2,1)S(1)} %add_convert_fusion.13), channel_id=1, source_target_pairs={{0,4},{4,0},{8,12},{12,8},{1,5},{5,1},{9,13},{13,9},{2,6},{6,2},{1... | collective-permute-start | bytes 393224 | tf_op jit(solution)/shard_map/ppermute | solution.py:49
  125.7 5.0 %collective-permute-start.29 = (bf16[2,1,64,512]{3,2,1,0:T(8,128)(2,1)S(1)}, bf16[2,1,64,512]{3,2,1,0:T(8,128)(2,1)S(1)}, u32[]{:S(2)}, u32[]{:S(2)}) collective-permute-start(bf16[2,1,64,512]{3,2,1,0:T(8,128)(2,1)S(1)} %add_convert_fusion.11), channel_id=1, source_target_pairs={{0,4},{4,0},{8,12},{12,8},{1,5},{5,1},{9,13},{13,9},{2,6},{6,2},{1... | collective-permute-start | bytes 393224 | tf_op jit(solution)/shard_map/ppermute | solution.py:49
  129.5 27.8 %copy-start.4 = (bf16[2,8,64,640]{3,2,1,0:T(8,128)(2,1)}, bf16[2,8,64,640]{3,2,1,0:T(8,128)(2,1)S(1)}, u32[]{:S(2)}) copy-start(bf16[2,8,64,640]{3,2,1,0:T(8,128)(2,1)S(1)} %constant_dynamic-update-slice_fusion.mine_ref) | copy-start | bytes 3932164
  129.6 27.9 %collective-permute-start.24 = (bf16[2,8,64,640]{3,2,1,0:T(8,128)(2,1)S(1)}, bf16[2,8,64,640]{3,2,1,0:T(8,128)(2,1)S(1)}, u32[]{:S(2)}, u32[]{:S(2)}) collective-permute-start(bf16[2,8,64,640]{3,2,1,0:T(8,128)(2,1)S(1)} %constant_dynamic-update-slice_fusion.mine_ref), channel_id=1, source_target_pairs={{0,1},{1,0},{2,3},{3,2},{4,5},{5,4},{6,7},{7,6},{8,9},{9,8},{10,11... | collective-permute-start | bytes 3932168 | tf_op jit(solution)/shard_map/ppermute | solution.py:49
  130.8 7.6 %collective-permute-start.30 = (bf16[2,2,64,512]{3,2,1,0:T(8,128)(2,1)S(1)}, bf16[2,2,64,512]{3,2,1,0:T(8,128)(2,1)S(1)}, u32[]{:S(2)}, u32[]{:S(2)}) collective-permute-start(bf16[2,2,64,512]{3,2,1,0:T(8,128)(2,1)S(1)} %pad_maximum_fusion.6), channel_id=1, source_target_pairs={{0,16},{16,0},{1,17},{17,1},{2,18},{18,2},{3,19},{19,3},{4,20},{20... | collective-permute-start | bytes 786440 | tf_op jit(solution)/shard_map/ppermute | solution.py:49
  138.5 18.7 %collective-permute-start.31 = (bf16[2,4,64,512]{3,2,1,0:T(8,128)(2,1)S(1)}, bf16[2,4,64,512]{3,2,1,0:T(8,128)(2,1)S(1)}, u32[]{:S(2)}, u32[]{:S(2)}) collective-permute-start(bf16[2,4,64,512]{3,2,1,0:T(8,128)(2,1)S(1)} %pad_maximum_fusion.3), channel_id=1, source_target_pairs={{0,2},{2,0},{1,3},{3,1},{4,6},{6,4},{5,7},{7,5},{8,10},{10,8},{9,1... | collective-permute-start | bytes 1572872 | tf_op jit(solution)/shard_map/ppermute | solution.py:49
  139.1 17.4 %collective-permute-start.21 = (bf16[2,2,64,512]{3,2,1,0:T(8,128)(2,1)S(1)}, bf16[2,2,64,512]{3,2,1,0:T(8,128)(2,1)S(1)}, u32[]{:S(2)}, u32[]{:S(2)}) collective-permute-start(bf16[2,2,64,512]{3,2,1,0:T(8,128)(2,1)S(1)} %pad_maximum_fusion.5), channel_id=1, source_target_pairs={{0,2},{2,0},{1,3},{3,1},{4,6},{6,4},{5,7},{7,5},{8,10},{10,8},{9,1... | collective-permute-start | bytes 786440 | tf_op jit(solution)/shard_map/ppermute | solution.py:49
  156.5 11.4 %collective-permute-start.22 = (bf16[2,4,64,512]{3,2,1,0:T(8,128)(2,1)S(1)}, bf16[2,4,64,512]{3,2,1,0:T(8,128)(2,1)S(1)}, u32[]{:S(2)}, u32[]{:S(2)}) collective-permute-start(bf16[2,4,64,512]{3,2,1,0:T(8,128)(2,1)S(1)} %pad_maximum_fusion.2), channel_id=1, source_target_pairs={{0,16},{16,0},{1,17},{17,1},{2,18},{18,2},{3,19},{19,3},{4,20},{20... | collective-permute-start | bytes 1572872 | tf_op jit(solution)/shard_map/ppermute | solution.py:49
  157.4 7.0 %copy-start.3 = (bf16[2,8,64,512]{3,2,1,0:T(8,128)(2,1)}, bf16[2,8,64,512]{3,2,1,0:T(8,128)(2,1)S(1)}, u32[]{:S(2)}) copy-start(bf16[2,8,64,512]{3,2,1,0:T(8,128)(2,1)S(1)} %pad_maximum_fusion.mine_ref) | copy-start | bytes 3145732
  157.4 10.7 %collective-permute-start.32 = (bf16[2,8,64,512]{3,2,1,0:T(8,128)(2,1)S(1)}, bf16[2,8,64,512]{3,2,1,0:T(8,128)(2,1)S(1)}, u32[]{:S(2)}, u32[]{:S(2)}) collective-permute-start(bf16[2,8,64,512]{3,2,1,0:T(8,128)(2,1)S(1)} %pad_maximum_fusion.mine_ref), channel_id=1, source_target_pairs={{0,1},{1,0},{2,3},{3,2},{4,5},{5,4},{6,7},{7,6},{8,9},{9,8},{10,11... | collective-permute-start | bytes 3145736 | tf_op jit(solution)/shard_map/ppermute | solution.py:49
  157.5 1.2 copy-start.7
  167.9 7.7 %copy-start.6 = (bf16[2,8,64,512]{3,2,1,0:T(8,128)(2,1)}, bf16[2,8,64,512]{3,2,1,0:T(8,128)(2,1)S(1)}, u32[]{:S(2)}) copy-start(bf16[2,8,64,512]{3,2,1,0:T(8,128)(2,1)S(1)} %constant_dynamic-update-slice_fusion.2.mine_ref) | copy-start | bytes 3145732
  168.0 7.7 %copy-start.11 = (f32[2,1,128]{2,1,0:T(1,128)S(1)}, f32[2,1,128]{2,1,0:T(1,128)}, u32[]{:S(2)}) copy-start(f32[2,1,128]{2,1,0:T(1,128)} %get-tuple-element.126) | copy-start | bytes 3076
  168.0 8.3 %collective-permute-start.25 = (bf16[2,8,64,512]{3,2,1,0:T(8,128)(2,1)S(1)}, bf16[2,8,64,512]{3,2,1,0:T(8,128)(2,1)S(1)}, u32[]{:S(2)}, u32[]{:S(2)}) collective-permute-start(bf16[2,8,64,512]{3,2,1,0:T(8,128)(2,1)S(1)} %constant_dynamic-update-slice_fusion.2.mine_ref), channel_id=1, source_target_pairs={{0,1},{1,0},{2,3},{3,2},{4,5},{5,4},{6,7},{7,6},{8,9},{9,8},{10,11... | collective-permute-start | bytes 3145736 | tf_op jit(solution)/shard_map/ppermute | solution.py:49
  168.1 1.1 copy-start.8
  176.3 1.0 copy-start.9

commit v7 on v6

--- a/solution.py
+++ b/solution.py
@@ -15,6 +15,11 @@
 MARGIN = 16
 CHUNKS = 2
 VMEM = 56 << 20
+ORDER = (
+    "top", "in0", "in1", "taps", "in0", "small", "in1", "top", "in0", "small", "top", "in1",
+    "in0", "small", "in1", "top", "small", "in0", "top", "in1", "in0", "small", "in1", "top",
+    "in0", "in1", "top", "in0", "top", "in0", "write_top", "in1", "write0", "in1", "write1",
+)
 SMEM_SPEC = pl.BlockSpec(memory_space=pltpu.SMEM)
 F32 = jnp.float32
 BF16 = jnp.bfloat16
@@ -117,18 +122,9 @@
         else:
             self.pending[name] = exchange(values, axis)
 
-    def meet(self, *names):
-        met = lax.optimization_barrier(tuple(self.values[name] for name in names))
-        self.values.update(zip(names, met))
-        for name in names:
-            if name in self.steps and name not in self.pending:
-                self.start(name)
-
-    def step(self, name, start=True, tied=False):
+    def step(self, name, start=True):
         kind, _ = self.steps[name].pop(0)
-        got = self.pending.pop(name)
-        if tied:
-            got = self.after_last(got)
+        got = self.after_last(self.pending.pop(name))
         own = self.values[name]
         if kind == "halve":
             own = own[:, : got.shape[1]]
@@ -603,11 +599,18 @@
     )(lengths, gated, *dconvs)
 
 
-def gain_row(weight, grad):
+def gain_terms(weight, grad):
     terms = weight.astype(F32) * grad
+    total = terms[:, :LANES]
+    for first in range(LANES, terms.shape[1], LANES):
+        total = total + terms[:, first : first + LANES]
+    return total
+
+
+def gain_row(terms):
     high = terms.astype(BF16)
     low = (terms - high.astype(F32)).astype(BF16)
-    ones = jnp.ones((8, terms.shape[1]), BF16)
+    ones = jnp.ones((8, LANES), BF16)
     return (dot(ones, high, 1, 1) + dot(ones, low, 1, 1))[0:1, :]
 
 
@@ -650,7 +653,7 @@
             (dhead_ref, group * half_head, half_out, half_head),
         )
         write_rows(own_ref, pl.program_id(0), (mine_ref, other_ref), group, scale, targets)
-    dgain_ref[...] = gain_row(head_ref[...], dhead_ref[...]) / gain_ref[...]
+    dgain_ref[...] = gain_row(gain_terms(head_ref[...], dhead_ref[...])) / gain_ref[...]
     depth_ref[...] = small_ref[:taps, :] * scale
     loss_ref[...] = losses_ref[...] * scale[None]
 
@@ -706,19 +709,21 @@
 def unpack_inner_kernel(
     utts, last, own_ref, small_ref, mine_ref, other_ref, weight_ref, gain_ref, *refs
 ):
-    win_ref, dgain_ref = refs[-2:]
+    win_ref, dgain_ref, sums_ref = refs[-3:]
     scale = utts / small_ref[small_ref.shape[0] - 1 :, 0:1]
     targets = ((win_ref, 0, 0, win_ref.shape[1]),)
     write_rows(own_ref, pl.program_id(0), (mine_ref, other_ref), 0, scale, targets)
-    row = gain_row(weight_ref[...], win_ref[...])
+    terms = gain_terms(weight_ref[...], win_ref[...])
 
     @pl.when(pl.program_id(1) == 0)
     def _():
-        dgain_ref[...] = row + refs[1][...] if len(refs) > 2 else row
+        sums_ref[...] = terms
 
     @pl.when(pl.program_id(1) == 1)
     def _():
-        total = dgain_ref[...] + row
+        total = gain_row(sums_ref[...] + terms)
+        if len(refs) > 3:
+            total = total + refs[1][...]
         dgain_ref[...] = total / gain_ref[...] if last else total
 
 
@@ -751,6 +756,7 @@
             ]
             + ([pl.BlockSpec(memory_space=pl.ANY), row] if before else []),
             out_specs=(block, row),
+            scratch_shapes=[pltpu.VMEM((rows, LANES), F32)],
         ),
         input_output_aliases={6: 0} if before else {},
         compiler_params=params(),
@@ -819,17 +825,6 @@
     products("in0", 0)
     line.step("top", start=False)
     products("in1", 1)
-    line.last = None
-    line.step("top", start=False)
-    line.step("in0", start=False, tied=True)
-    line.step("in1", start=False, tied=True)
-    line.meet("top", "in0", "in1", "in0_conv", "in1_conv")
-    dconvs = (line.values["in0_conv"], line.values["in1_conv"])
-    line.put("taps", tap_sums(lengths, gated, dconvs, taps, utterances))
-    line.begin_small("small", line.values["taps"])
-    line.step("in0", tied=True)
-    line.step("in1", tied=True, start=False)
-    line.step("top", tied=True)
     written = {}
 
     def write_top():
@@ -838,7 +833,7 @@
             utts,
             owns[1],
             line.values["small"],
-            mine,
+            line.after_last(mine),
             other,
             head_weight,
             gain_out[None],
@@ -855,7 +850,7 @@
             utts,
             owns[chunk],
             line.values["small"],
-            mine,
+            line.after_last(mine),
             other,
             weight_in,
             gain_conv[None],
@@ -864,32 +859,23 @@
         )
         line.put("by_in", by_in)
 
-    line.step("small")
-    line.meet("in1", "small")
-    line.step("small")
-    line.step("in1", start=False)
-    line.meet("in1", "small")
-    line.step("small")
-    line.step("small")
-    line.step("in1", start=False)
-    line.meet("in1", "small")
-    line.step("small")
-    line.step("in1", start=False)
-    line.meet("in1", "small")
-    for _ in range(4):
-        line.step("top")
-    line.step("in1", tied=True)
-    line.step("top")
-    line.step("top")
-    write_top()
-    while line.steps["in0"]:
-        line.step("in0")
-    line.step("in1")
-    line.last = "by_head"
-    line.step("in1", tied=True)
-    write_in(0, "in0")
-    line.step("in1")
-    write_in(1, "in1")
+    def sum_taps():
+        names = ("in0_conv", "in1_conv")
+        dconvs = line.after_last(tuple(line.values[name] for name in names))
+        line.put("taps", tap_sums(lengths, gated, dconvs, taps, utterances))
+        line.begin_small("small", line.values["taps"])
+
+    kernels = {
+        "taps": sum_taps,
+        "write_top": write_top,
+        "write0": functools.partial(write_in, 0, "in0"),
+        "write1": functools.partial(write_in, 1, "in1"),
+    }
+    for name in ORDER:
+        if name in kernels:
+            kernels[name]()
+        else:
+            line.step(name)
     return (
         line.values["by_in"].reshape(model),
         written["in"],

time: 184 us -> 178 us (0.967)
  waiting for transfers between devices: 66.3 us -> 51.2 us
  starting transfers between devices: 29.7 us -> 40.5 us
    ppermute x33, waiting for transfers between devices: 66.3 us -> 51.2 us  [exchange(): return lax.ppermute(values, axis, [(i, i ^ bit) for i in range(size)])]
    ppermute x33, starting transfers between devices: 29.7 us -> 40.5 us  [exchange(): return lax.ppermute(values, axis, [(i, i ^ bit) for i in range(size)])]
    unnamed x28 -> x31, local copies, waits for them, and re-layouts: 4.2 us -> 2.35 us
  transfers between devices with their start and end apart: 33 -> 33, of which waited for: 15 -> 15; matrix products, arithmetic and copies ran while one was open for 3% -> 3% of each run, Pallas kernels for 30% -> 31%
where the time goes in v7:
time: 178 us
  Pallas kernels  76.7 us (43%)
  waiting for transfers between devices  51.2 us (29%)
  starting transfers between devices  40.5 us (23%)
  local copies, waits for them, and re-layouts  4.16 us (2%)
  other arithmetic  3.86 us (2%)
    ppermute x33, waiting for transfers between devices, exchange(): return lax.ppermute(values, axis, [(i, i ^ bit) for i in range(size)])  51.2 us
    ppermute x33, starting transfers between devices, exchange(): return lax.ppermute(values, axis, [(i, i ^ bit) for i in range(size)])  40.5 us
    pallas_call x2, Pallas kernels, inner(): pl.pallas_call(inner_kernel, grid=(steps,), out_shape=(shape, shape, jax....  21.5 us
    pallas_call x1, Pallas kernels, forward(): pl.pallas_call(forward_kernel, grid=(steps,), out_shape=(jax.ShapeDtypeSt...  15.2 us
    pallas_call x2, Pallas kernels, unpack_inner(): pl.pallas_call(functools.partial(unpack_inner_kernel, utts, chunk == CHUN...  12.6 us
    pallas_call x1, Pallas kernels, tap_sums(): pl.pallas_call(taps_kernel, grid=(steps,), out_shape=jax.ShapeDtypeStruct...  7.14 us
    pallas_call x1, Pallas kernels, unpack_top(): pl.pallas_call(functools.partial(unpack_top_kernel, utts), out_shape=(jax...  5.68 us
    pallas_call x1, Pallas kernels, outer(): pl.pallas_call(outer_kernel, grid=(2,), out_shape=(shape, shape), in_spec...  5.32 us
  transfers between devices with their start and end apart: 33, of which 15 were waited for; matrix products, arithmetic and copies ran while one was open for 3% of the time, Pallas kernels for 31%

profile of v7, /device:TPU:0, one launch (start us, length us, event | category | flops | bytes accessed | tf_op | source)
XLA Modules:
  0.0 177.5 jit_solution(12899863943558159043)
XLA Ops:
  0.6 4.0 %teachers.1 = (f32[2,256,256]{2,1,0:T(8,128)}, f32[2,256,256]{2,1,0:T(8,128)}) custom-call(s32[1]{0:T(128)} %bitcast.5.member_ref, bf16[2,4,256,256]{3,2,1,0:T(8,128)(2,1)} %logits_ref.1), custom_call_target="tpu_custom_call" | custom-call | flops 4600000000 | bytes 1048576 | tf_op jit(solution)/shard_map/teachers/pallas_call | solution.py:186
  4.7 2.9 %collective-permute-start = (f32[2,256,256]{2,1,0:T(8,128)}, f32[2,256,256]{2,1,0:T(8,128)S(1)}, u32[]{:S(2)}, u32[]{:S(2)}) collective-permute-start(f32[2,256,256]{2,1,0:T(8,128)} %get-tuple-element.117), channel_id=1, source_target_pairs={{0,16},{16,0},{1,17},{17,1},{2,18},{18,2},{3,19},{19,3},{4,20},{20... | collective-permute-start | bytes 1572872 | tf_op jit(solution)/shard_map/ppermute | solution.py:54
  7.6 15.2 %forward.1 = (bf16[1024,512]{1,0:T(8,128)(2,1)}, f32[512,1024]{1,0:T(8,128)}, f32[512,1024]{1,0:T(8,128)}, f32[512,1024]{1,0:T(8,128)}, bf16[512,1024]{1,0:T(8,128)(2,1)}, /*index=5*/f32[512,1024]{1,0:T(8,128)}) custom-call(s32[2]{0:T(128)} %lengths_ref.9, bf16[512,1024]{1,0:T(8,128)(2,1)} %bitcast.9, f32[1,1024]{1,0:T(1,128)} %bitcast.12, ...), custom_call_target="tpu_custom_call" | custom-call | flops 17250000896 | bytes 1048576 | tf_op jit(solution)/shard_map/forward/pallas_call | solution.py:311
  22.8 0.6 pad_add_fusion.own_ref
  23.4 0.8 copy-done.10
  24.3 5.3 %top.1 = (f32[2,1,128]{2,1,0:T(1,128)}, bf16[512,1024]{1,0:T(8,128)(2,1)}, bf16[512,256]{1,0:T(8,128)(2,1)}, bf16[512,1024]{1,0:T(8,128)(2,1)}) custom-call(s32[2]{0:T(128)} %lengths_ref.9, f32[512,1024]{1,0:T(8,128)} %get-tuple-element.115.residual_ref, f32[1,1024]{1,0:T(1,128)} %bitcast.10, bf16[1024,256]{1,0:T(8,128)(2,1)} %head_ref.3, ...), custom_call_target="tpu_custom_call" | custom-call | flops 5750000128 | bytes 1048576 | tf_op jit(solution)/shard_map/top/pallas_call | solution.py:379
  29.6 5.3 %outer.1 = (bf16[2,8,64,640]{3,2,1,0:T(8,128)(2,1)}, bf16[2,8,64,640]{3,2,1,0:T(8,128)(2,1)}) custom-call(s32[2]{0:T(128)} %pad_add_fusion.own_ref, bf16[512,1024]{1,0:T(8,128)(2,1)} %get-tuple-element.114.active_ref, bf16[512,1024]{1,0:T(8,128)(2,1)} %get-tuple-element.132.dresidual_ref, bf16[512,1024]{1,0:T(8,128)(2,1)} %get-tuple-element.119.final_ref, ...), custom_call_target="tpu_custom_call" | custom-call | flops 5750000128 | bytes 1048576 | tf_op jit(solution)/shard_map/outer/pallas_call | solution.py:418
  35.5 10.8 %inner.2 = (bf16[2,8,64,512]{3,2,1,0:T(8,128)(2,1)}, bf16[2,8,64,512]{3,2,1,0:T(8,128)(2,1)}, f32[512,512]{1,0:T(8,128)}) custom-call(s32[2]{0:T(128)} %pad_add_fusion.1.own_ref, s32[2]{0:T(128)} %lengths_ref.9, bf16[512,1024]{1,0:T(8,128)(2,1)} %get-tuple-element.132.dresidual_ref, bf16[1024,1024]{1,0:T(8,128)(2,1)} %out_weight_ref.5, ...), custom_call_target="tpu_custom_call" | custom-call | flops 12650000384 | bytes 1048576 | tf_op jit(solution)/shard_map/inner/pallas_call | solution.py:503
  47.3 10.7 %inner.3 = (bf16[2,8,64,512]{3,2,1,0:T(8,128)(2,1)}, bf16[2,8,64,512]{3,2,1,0:T(8,128)(2,1)}, f32[512,512]{1,0:T(8,128)}) custom-call(s32[2]{0:T(128)} %pad_add_fusion.own_ref, s32[2]{0:T(128)} %lengths_ref.9, bf16[512,1024]{1,0:T(8,128)(2,1)} %get-tuple-element.132.dresidual_ref, bf16[1024,1024]{1,0:T(8,128)(2,1)} %out_weight_ref.5, ...), custom_call_target="tpu_custom_call" | custom-call | flops 12650000384 | bytes 1048576 | tf_op jit(solution)/shard_map/inner/pallas_call | solution.py:503
  58.1 5.8 %collective-permute-done.4 = bf16[2,4,64,640]{3,2,1,0:T(8,128)(2,1)S(1)} collective-permute-done((bf16[2,4,64,640]{3,2,1,0:T(8,128)(2,1)S(1)}, bf16[2,4,64,640]{3,2,1,0:T(8,128)(2,1)S(1)}, u32[]{:S(2)}, u32[]{:S(2)}) %collective-permute-start.4) | collective-permute-done | bytes 655392 | tf_op jit(solution)/shard_map/ppermute | solution.py:54
  64.2 1.6 collective-permute-start.7
  68.0 7.1 %taps.1 = f32[32,1024]{1,0:T(8,128)} custom-call(s32[2]{0:T(128)} %lengths_ref.9, f32[512,1024]{1,0:T(8,128)} %get-tuple-element.127.gated_ref, f32[512,512]{1,0:T(8,128)} %get-tuple-element.145.refs_0_, f32[512,512]{1,0:T(8,128)} %get-tuple-element.146.refs_1_), custom_call_target="tpu_custom_call" | custom-call | flops 10350000128 | bytes 1048576 | tf_op jit(solution)/shard_map/taps/pallas_call | solution.py:585
  75.1 9.2 %collective-permute-done.5 = bf16[2,4,64,512]{3,2,1,0:T(8,128)(2,1)S(1)} collective-permute-done((bf16[2,4,64,512]{3,2,1,0:T(8,128)(2,1)S(1)}, bf16[2,4,64,512]{3,2,1,0:T(8,128)(2,1)S(1)}, u32[]{:S(2)}, u32[]{:S(2)}) %collective-permute-start.5) | collective-permute-done | bytes 524320 | tf_op jit(solution)/shard_map/ppermute | solution.py:54
  84.5 0.7 collective-permute-start.6
  85.2 1.5 collective-permute-start.11
  86.9 5.5 %collective-permute-done.6 = bf16[2,2,64,512]{3,2,1,0:T(8,128)(2,1)S(1)} collective-permute-done((bf16[2,2,64,512]{3,2,1,0:T(8,128)(2,1)S(1)}, bf16[2,2,64,512]{3,2,1,0:T(8,128)(2,1)S(1)}, u32[]{:S(2)}, u32[]{:S(2)}) %collective-permute-start.6) | collective-permute-done | bytes 262176 | tf_op jit(solution)/shard_map/ppermute | solution.py:54
  92.4 1.6 collective-permute-start.10
  94.0 1.5 collective-permute-start.14
  96.1 0.9 collective-permute-start.16
  97.0 0.9 collective-permute-done.10
  97.9 5.8 %collective-permute-start.12 = (bf16[2,1,64,640]{3,2,1,0:T(8,128)(2,1)S(1)}, bf16[2,1,64,640]{3,2,1,0:T(8,128)(2,1)S(1)}, u32[]{:S(2)}, u32[]{:S(2)}) collective-permute-start(bf16[2,1,64,640]{3,2,1,0:T(8,128)(2,1)S(1)} %add_convert_fusion.10), channel_id=1, source_target_pairs={{0,8},{4,12},{8,0},{12,4},{1,9},{5,13},{9,1},{13,5},{2,10},{6,14},... | collective-permute-start | bytes 491528 | tf_op jit(solution)/shard_map/ppermute | solution.py:54
  103.8 0.7 collective-permute-done.13
  104.5 2.0 %collective-permute-start.15 = (bf16[2,1,64,512]{3,2,1,0:T(8,128)(2,1)S(1)}, bf16[2,1,64,512]{3,2,1,0:T(8,128)(2,1)S(1)}, u32[]{:S(2)}, u32[]{:S(2)}) collective-permute-start(bf16[2,1,64,512]{3,2,1,0:T(8,128)(2,1)S(1)} %slice.83), channel_id=1, source_target_pairs={{0,4},{4,0},{8,12},{12,8},{1,5},{5,1},{9,13},{13,9},{2,6},{6,2},{1... | collective-permute-start | bytes 393224 | tf_op jit(solution)/shard_map/ppermute | solution.py:54
  106.5 2.6 %collective-permute-start.20 = (bf16[2,1,64,512]{3,2,1,0:T(8,128)(2,1)S(1)}, bf16[2,1,64,512]{3,2,1,0:T(8,128)(2,1)S(1)}, u32[]{:S(2)}, u32[]{:S(2)}) collective-permute-start(bf16[2,1,64,512]{3,2,1,0:T(8,128)(2,1)S(1)} %add_convert_fusion.14), channel_id=1, source_target_pairs={{0,8},{4,12},{8,0},{12,4},{1,9},{5,13},{9,1},{13,5},{2,10},{6,14},... | collective-permute-start | bytes 393224 | tf_op jit(solution)/shard_map/ppermute | solution.py:54
  109.2 4.8 %collective-permute-done.15 = bf16[2,1,64,512]{3,2,1,0:T(8,128)(2,1)S(1)} collective-permute-done((bf16[2,1,64,512]{3,2,1,0:T(8,128)(2,1)S(1)}, bf16[2,1,64,512]{3,2,1,0:T(8,128)(2,1)S(1)}, u32[]{:S(2)}, u32[]{:S(2)}) %collective-permute-start.15) | collective-permute-done | bytes 131104 | tf_op jit(solution)/shard_map/ppermute | solution.py:54
  114.1 1.8 %collective-permute-start.17 = (bf16[2,1,64,512]{3,2,1,0:T(8,128)(2,1)S(1)}, bf16[2,1,64,512]{3,2,1,0:T(8,128)(2,1)S(1)}, u32[]{:S(2)}, u32[]{:S(2)}) collective-permute-start(bf16[2,1,64,512]{3,2,1,0:T(8,128)(2,1)S(1)} %add_convert_fusion.13), channel_id=1, source_target_pairs={{0,8},{4,12},{8,0},{12,4},{1,9},{5,13},{9,1},{13,5},{2,10},{6,14},... | collective-permute-start | bytes 393224 | tf_op jit(solution)/shard_map/ppermute | solution.py:54
  115.9 2.5 %collective-permute-start.19 = (bf16[2,1,64,640]{3,2,1,0:T(8,128)(2,1)S(1)}, bf16[2,1,64,640]{3,2,1,0:T(8,128)(2,1)S(1)}, u32[]{:S(2)}, u32[]{:S(2)}) collective-permute-start(bf16[2,1,64,640]{3,2,1,0:T(8,128)(2,1)S(1)} %add_convert_fusion.9), channel_id=1, source_target_pairs={{0,4},{4,0},{8,12},{12,8},{1,5},{5,1},{9,13},{13,9},{2,6},{6,2},{1... | collective-permute-start | bytes 491528 | tf_op jit(solution)/shard_map/ppermute | solution.py:54
  118.5 2.9 %collective-permute-start.22 = (f32[32,1024]{1,0:T(8,128)S(1)}, f32[32,1024]{1,0:T(8,128)S(1)}, u32[]{:S(2)}, u32[]{:S(2)}) collective-permute-start(f32[32,1024]{1,0:T(8,128)S(1)} %add.92), channel_id=1, source_target_pairs={{0,8},{4,12},{8,0},{12,4},{1,9},{5,13},{9,1},{13,5},{2,10},{6,14},... | collective-permute-start | bytes 393224 | tf_op jit(solution)/shard_map/ppermute | solution.py:54
  121.4 3.0 %collective-permute-start.23 = (bf16[2,1,64,512]{3,2,1,0:T(8,128)(2,1)S(1)}, bf16[2,1,64,512]{3,2,1,0:T(8,128)(2,1)S(1)}, u32[]{:S(2)}, u32[]{:S(2)}) collective-permute-start(bf16[2,1,64,512]{3,2,1,0:T(8,128)(2,1)S(1)} %add_convert_fusion.12), channel_id=1, source_target_pairs={{0,4},{4,0},{8,12},{12,8},{1,5},{5,1},{9,13},{13,9},{2,6},{6,2},{1... | collective-permute-start | bytes 393224 | tf_op jit(solution)/shard_map/ppermute | solution.py:54
  124.6 1.6 collective-permute-start.26
  126.4 1.0 collective-permute-done.23
  127.4 0.6 collective-permute-start.25
  128.1 0.7 add.95.small_ref
  128.8 2.5 %collective-permute-done.21 = bf16[2,1,64,512]{3,2,1,0:T(8,128)(2,1)S(1)} collective-permute-done((bf16[2,1,64,512]{3,2,1,0:T(8,128)(2,1)S(1)}, bf16[2,1,64,512]{3,2,1,0:T(8,128)(2,1)S(1)}, u32[]{:S(2)}, u32[]{:S(2)}) %collective-permute-start.21) | collective-permute-done | bytes 131104 | tf_op jit(solution)/shard_map/ppermute | solution.py:54
  131.3 4.0 %collective-permute-done.26 = bf16[2,2,64,640]{3,2,1,0:T(8,128)(2,1)S(1)} collective-permute-done((bf16[2,2,64,640]{3,2,1,0:T(8,128)(2,1)S(1)}, bf16[2,2,64,640]{3,2,1,0:T(8,128)(2,1)S(1)}, u32[]{:S(2)}, u32[]{:S(2)}) %collective-permute-start.26) | collective-permute-done | bytes 327712 | tf_op jit(solution)/shard_map/ppermute | solution.py:54
  135.3 0.7 collective-permute-start.28
  136.0 1.6 collective-permute-start.24
  138.3 4.2 %collective-permute-done.24 = bf16[2,2,64,512]{3,2,1,0:T(8,128)(2,1)S(1)} collective-permute-done((bf16[2,2,64,512]{3,2,1,0:T(8,128)(2,1)S(1)}, bf16[2,2,64,512]{3,2,1,0:T(8,128)(2,1)S(1)}, u32[]{:S(2)}, u32[]{:S(2)}) %collective-permute-start.24) | collective-permute-done | bytes 262176 | tf_op jit(solution)/shard_map/ppermute | solution.py:54
  142.5 3.5 %collective-permute-done.28 = bf16[2,4,64,640]{3,2,1,0:T(8,128)(2,1)S(1)} collective-permute-done((bf16[2,4,64,640]{3,2,1,0:T(8,128)(2,1)S(1)}, bf16[2,4,64,640]{3,2,1,0:T(8,128)(2,1)S(1)}, u32[]{:S(2)}, u32[]{:S(2)}) %collective-permute-start.28) | collective-permute-done | bytes 655392 | tf_op jit(solution)/shard_map/ppermute | solution.py:54
  146.2 1.9 %collective-permute-done.27 = bf16[2,4,64,512]{3,2,1,0:T(8,128)(2,1)S(1)} collective-permute-done((bf16[2,4,64,512]{3,2,1,0:T(8,128)(2,1)S(1)}, bf16[2,4,64,512]{3,2,1,0:T(8,128)(2,1)S(1)}, u32[]{:S(2)}, u32[]{:S(2)}) %collective-permute-start.27) | collective-permute-done | bytes 524320 | tf_op jit(solution)/shard_map/ppermute | solution.py:54
  148.2 1.5 collective-permute-start.31
  149.8 1.1 collective-permute-done.29.other_ref
  150.9 5.7 %unpack_top.1 = (f32[1024,1024]{1,0:T(8,128)}, f32[1024,256]{1,0:T(8,128)}, f32[1,1024]{1,0:T(1,128)}, f32[31,1024]{1,0:T(8,128)}, f32[2,1,128]{2,1,0:T(1,128)}) custom-call(s32[2]{0:T(128)} %pad_add_fusion.own_ref, f32[32,1024]{1,0:T(8,128)} %add.95.small_ref, bf16[2,8,64,640]{3,2,1,0:T(8,128)(2,1)} %copy-done.3, bf16[2,8,64,640]{3,2,1,0:T(8,128)(2,1)} %copy-done.7, ...), custom_call_target="tpu_custom_call" | custom-call | flops 5750000128 | bytes 1048576 | tf_op jit(solution)/shard_map/unpack_top/pallas_call | solution.py:675
  156.6 6.0 %collective-permute-done.31 = bf16[2,4,64,512]{3,2,1,0:T(8,128)(2,1)S(1)} collective-permute-done((bf16[2,4,64,512]{3,2,1,0:T(8,128)(2,1)S(1)}, bf16[2,4,64,512]{3,2,1,0:T(8,128)(2,1)S(1)}, u32[]{:S(2)}, u32[]{:S(2)}) %collective-permute-start.31) | collective-permute-done | bytes 524320 | tf_op jit(solution)/shard_map/ppermute | solution.py:54
  162.7 1.3 slice_reduce_fusion
  164.0 6.3 %unpack_inner.2 = (f32[1024,2048]{1,0:T(8,128)}, f32[1,1024]{1,0:T(1,128)}) custom-call(s32[2]{0:T(128)} %pad_add_fusion.1.own_ref, f32[32,1024]{1,0:T(8,128)} %add.95.small_ref, bf16[2,8,64,512]{3,2,1,0:T(8,128)(2,1)} %copy-done.5, bf16[2,8,64,512]{3,2,1,0:T(8,128)(2,1)} %copy-done.8, bf16[1024,2048]{1,0:T(8,128)(2,1)} %weight_ref.3, f32[1,1024]{1,0:T(1,128)} %bitcast.13), custom_call_target="tpu_custom_call" | custom-call | flops 4600000000 | bytes 1048576 | tf_op jit(solution)/shard_map/unpack_inner/pallas_call | solution.py:741
  170.3 1.0 copy-done.9
  171.2 6.3 %unpack_inner.3 = (f32[1024,2048]{1,0:T(8,128)}, f32[1,1024]{1,0:T(1,128)}) custom-call(s32[2]{0:T(128)} %pad_add_fusion.own_ref, f32[32,1024]{1,0:T(8,128)} %add.95.small_ref, bf16[2,8,64,512]{3,2,1,0:T(8,128)(2,1)} %copy-done.4, bf16[2,8,64,512]{3,2,1,0:T(8,128)(2,1)} %copy-done.9, bf16[1024,2048]{1,0:T(8,128)(2,1)} %weight_ref.3, ...), custom_call_target="tpu_custom_call", output_to_operand_aliasing={{0}: (6, {})} | custom-call | flops 4600000000 | bytes 1048576 | tf_op jit(solution)/shard_map/unpack_inner/pallas_call | solution.py:741
  (100 shorter events, 7.0 us)
Async XLA Ops:
  4.7 18.8 %collective-permute-start = (f32[2,256,256]{2,1,0:T(8,128)}, f32[2,256,256]{2,1,0:T(8,128)S(1)}, u32[]{:S(2)}, u32[]{:S(2)}) collective-permute-start(f32[2,256,256]{2,1,0:T(8,128)} %get-tuple-element.117), channel_id=1, source_target_pairs={{0,16},{16,0},{1,17},{17,1},{2,18},{18,2},{3,19},{19,3},{4,20},{20... | collective-permute-start | bytes 1572872 | tf_op jit(solution)/shard_map/ppermute | solution.py:54
  23.4 0.8 copy-start.10
  34.9 11.9 %collective-permute-start.1 = (bf16[2,8,64,640]{3,2,1,0:T(8,128)(2,1)}, bf16[2,8,64,640]{3,2,1,0:T(8,128)(2,1)S(1)}, u32[]{:S(2)}, u32[]{:S(2)}) collective-permute-start(bf16[2,8,64,640]{3,2,1,0:T(8,128)(2,1)} %get-tuple-element.125), channel_id=1, source_target_pairs={{0,1},{1,0},{2,3},{3,2},{4,5},{5,4},{6,7},{7,6},{8,9},{9,8},{10,11... | collective-permute-start | bytes 3932168 | tf_op jit(solution)/shard_map/ppermute | solution.py:54
  35.5 11.3 %copy-start = (bf16[2,8,64,640]{3,2,1,0:T(8,128)(2,1)S(1)}, bf16[2,8,64,640]{3,2,1,0:T(8,128)(2,1)}, u32[]{:S(2)}) copy-start(bf16[2,8,64,640]{3,2,1,0:T(8,128)(2,1)} %get-tuple-element.124) | copy-start | bytes 3932164
  46.3 19.5 %collective-permute-start.3 = (bf16[2,8,64,512]{3,2,1,0:T(8,128)(2,1)}, bf16[2,8,64,512]{3,2,1,0:T(8,128)(2,1)S(1)}, u32[]{:S(2)}, u32[]{:S(2)}) collective-permute-start(bf16[2,8,64,512]{3,2,1,0:T(8,128)(2,1)} %get-tuple-element.135), channel_id=1, source_target_pairs={{0,1},{1,0},{2,3},{3,2},{4,5},{5,4},{6,7},{7,6},{8,9},{9,8},{10,11... | collective-permute-start | bytes 3145736 | tf_op jit(solution)/shard_map/ppermute | solution.py:54
  47.3 16.7 %collective-permute-start.4 = (bf16[2,4,64,640]{3,2,1,0:T(8,128)(2,1)S(1)}, bf16[2,4,64,640]{3,2,1,0:T(8,128)(2,1)S(1)}, u32[]{:S(2)}, u32[]{:S(2)}) collective-permute-start(bf16[2,4,64,640]{3,2,1,0:T(8,128)(2,1)S(1)} %slice.58), channel_id=1, source_target_pairs={{0,16},{16,0},{1,17},{17,1},{2,18},{18,2},{3,19},{19,3},{4,20},{20... | collective-permute-start | bytes 1966088 | tf_op jit(solution)/shard_map/ppermute | solution.py:54
  58.1 7.7 %copy-start.1 = (bf16[2,8,64,512]{3,2,1,0:T(8,128)(2,1)S(1)}, bf16[2,8,64,512]{3,2,1,0:T(8,128)(2,1)}, u32[]{:S(2)}) copy-start(bf16[2,8,64,512]{3,2,1,0:T(8,128)(2,1)} %get-tuple-element.134) | copy-start | bytes 3145732
  58.1 8.7 %collective-permute-start.2 = (bf16[2,8,64,512]{3,2,1,0:T(8,128)(2,1)}, bf16[2,8,64,512]{3,2,1,0:T(8,128)(2,1)S(1)}, u32[]{:S(2)}, u32[]{:S(2)}) collective-permute-start(bf16[2,8,64,512]{3,2,1,0:T(8,128)(2,1)} %get-tuple-element.133), channel_id=1, source_target_pairs={{0,1},{1,0},{2,3},{3,2},{4,5},{5,4},{6,7},{7,6},{8,9},{9,8},{10,11... | collective-permute-start | bytes 3145736 | tf_op jit(solution)/shard_map/ppermute | solution.py:54
  64.2 22.6 %collective-permute-start.7 = (bf16[2,2,64,640]{3,2,1,0:T(8,128)(2,1)S(1)}, bf16[2,2,64,640]{3,2,1,0:T(8,128)(2,1)S(1)}, u32[]{:S(2)}, u32[]{:S(2)}) collective-permute-start(bf16[2,2,64,640]{3,2,1,0:T(8,128)(2,1)S(1)} %slice.78), channel_id=1, source_target_pairs={{0,2},{2,0},{1,3},{3,1},{4,6},{6,4},{5,7},{7,5},{8,10},{10,8},{9,1... | collective-permute-start | bytes 983048 | tf_op jit(solution)/shard_map/ppermute | solution.py:54
  65.8 1.2 copy-start.2
  66.2 18.1 %collective-permute-start.5 = (bf16[2,4,64,512]{3,2,1,0:T(8,128)(2,1)S(1)}, bf16[2,4,64,512]{3,2,1,0:T(8,128)(2,1)S(1)}, u32[]{:S(2)}, u32[]{:S(2)}) collective-permute-start(bf16[2,4,64,512]{3,2,1,0:T(8,128)(2,1)S(1)} %slice.76), channel_id=1, source_target_pairs={{0,2},{2,0},{1,3},{3,1},{4,6},{6,4},{5,7},{7,5},{8,10},{10,8},{9,1... | collective-permute-start | bytes 1572872 | tf_op jit(solution)/shard_map/ppermute | solution.py:54
  67.4 19.3 %collective-permute-start.8 = (bf16[2,4,64,512]{3,2,1,0:T(8,128)(2,1)S(1)}, bf16[2,4,64,512]{3,2,1,0:T(8,128)(2,1)S(1)}, u32[]{:S(2)}, u32[]{:S(2)}) collective-permute-start(bf16[2,4,64,512]{3,2,1,0:T(8,128)(2,1)S(1)} %slice.79), channel_id=1, source_target_pairs={{0,16},{16,0},{1,17},{17,1},{2,18},{18,2},{3,19},{19,3},{4,20},{20... | collective-permute-start | bytes 1572872 | tf_op jit(solution)/shard_map/ppermute | solution.py:54
  75.1 10.0 %copy-start.6 = (f32[32,1024]{1,0:T(8,128)S(1)}, f32[32,1024]{1,0:T(8,128)}, u32[]{:S(2)}) copy-start(f32[32,1024]{1,0:T(8,128)} %taps.1) | copy-start | bytes 393220
  75.1 10.0 %collective-permute-start.9 = (f32[32,1024]{1,0:T(8,128)}, f32[32,1024]{1,0:T(8,128)S(1)}, u32[]{:S(2)}, u32[]{:S(2)}) collective-permute-start(f32[32,1024]{1,0:T(8,128)} %taps.1), channel_id=1, source_target_pairs={{0,1},{1,0},{2,3},{3,2},{4,5},{5,4},{6,7},{7,6},{8,9},{9,8},{10,11... | collective-permute-start | bytes 393224 | tf_op jit(solution)/shard_map/ppermute | solution.py:54
  84.5 7.9 %collective-permute-start.6 = (bf16[2,2,64,512]{3,2,1,0:T(8,128)(2,1)S(1)}, bf16[2,2,64,512]{3,2,1,0:T(8,128)(2,1)S(1)}, u32[]{:S(2)}, u32[]{:S(2)}) collective-permute-start(bf16[2,2,64,512]{3,2,1,0:T(8,128)(2,1)S(1)} %slice.77), channel_id=1, source_target_pairs={{0,16},{16,0},{1,17},{17,1},{2,18},{18,2},{3,19},{19,3},{4,20},{20... | collective-permute-start | bytes 786440 | tf_op jit(solution)/shard_map/ppermute | solution.py:54
  85.2 10.4 %collective-permute-start.11 = (f32[32,1024]{1,0:T(8,128)S(1)}, f32[32,1024]{1,0:T(8,128)S(1)}, u32[]{:S(2)}, u32[]{:S(2)}) collective-permute-start(f32[32,1024]{1,0:T(8,128)S(1)} %add.81), channel_id=1, source_target_pairs={{0,16},{16,0},{1,17},{17,1},{2,18},{18,2},{3,19},{19,3},{4,20},{20... | collective-permute-start | bytes 393224 | tf_op jit(solution)/shard_map/ppermute | solution.py:54
  92.4 5.5 %collective-permute-start.10 = (bf16[2,1,64,640]{3,2,1,0:T(8,128)(2,1)S(1)}, bf16[2,1,64,640]{3,2,1,0:T(8,128)(2,1)S(1)}, u32[]{:S(2)}, u32[]{:S(2)}) collective-permute-start(bf16[2,1,64,640]{3,2,1,0:T(8,128)(2,1)S(1)} %slice.80), channel_id=1, source_target_pairs={{0,4},{4,0},{8,12},{12,8},{1,5},{5,1},{9,13},{13,9},{2,6},{6,2},{1... | collective-permute-start | bytes 491528 | tf_op jit(solution)/shard_map/ppermute | solution.py:54
  94.0 9.7 %collective-permute-start.14 = (bf16[2,2,64,512]{3,2,1,0:T(8,128)(2,1)S(1)}, bf16[2,2,64,512]{3,2,1,0:T(8,128)(2,1)S(1)}, u32[]{:S(2)}, u32[]{:S(2)}) collective-permute-start(bf16[2,2,64,512]{3,2,1,0:T(8,128)(2,1)S(1)} %slice.82), channel_id=1, source_target_pairs={{0,2},{2,0},{1,3},{3,1},{4,6},{6,4},{5,7},{7,5},{8,10},{10,8},{9,1... | collective-permute-start | bytes 786440 | tf_op jit(solution)/shard_map/ppermute | solution.py:54
  95.6 8.9 %collective-permute-start.13 = (bf16[2,1,64,512]{3,2,1,0:T(8,128)(2,1)S(1)}, bf16[2,1,64,512]{3,2,1,0:T(8,128)(2,1)S(1)}, u32[]{:S(2)}, u32[]{:S(2)}) collective-permute-start(bf16[2,1,64,512]{3,2,1,0:T(8,128)(2,1)S(1)} %slice.81), channel_id=1, source_target_pairs={{0,4},{4,0},{8,12},{12,8},{1,5},{5,1},{9,13},{13,9},{2,6},{6,2},{1... | collective-permute-start | bytes 393224 | tf_op jit(solution)/shard_map/ppermute | solution.py:54
  96.1 13.0 %collective-permute-start.16 = (f32[32,1024]{1,0:T(8,128)S(1)}, f32[32,1024]{1,0:T(8,128)S(1)}, u32[]{:S(2)}, u32[]{:S(2)}) collective-permute-start(f32[32,1024]{1,0:T(8,128)S(1)} %add.85), channel_id=1, source_target_pairs={{0,2},{2,0},{1,3},{3,1},{4,6},{6,4},{5,7},{7,5},{8,10},{10,8},{9,1... | collective-permute-start | bytes 393224 | tf_op jit(solution)/shard_map/ppermute | solution.py:54
  97.9 17.9 %collective-permute-start.12 = (bf16[2,1,64,640]{3,2,1,0:T(8,128)(2,1)S(1)}, bf16[2,1,64,640]{3,2,1,0:T(8,128)(2,1)S(1)}, u32[]{:S(2)}, u32[]{:S(2)}) collective-permute-start(bf16[2,1,64,640]{3,2,1,0:T(8,128)(2,1)S(1)} %add_convert_fusion.10), channel_id=1, source_target_pairs={{0,8},{4,12},{8,0},{12,4},{1,9},{5,13},{9,1},{13,5},{2,10},{6,14},... | collective-permute-start | bytes 491528 | tf_op jit(solution)/shard_map/ppermute | solution.py:54
  104.5 9.5 %collective-permute-start.15 = (bf16[2,1,64,512]{3,2,1,0:T(8,128)(2,1)S(1)}, bf16[2,1,64,512]{3,2,1,0:T(8,128)(2,1)S(1)}, u32[]{:S(2)}, u32[]{:S(2)}) collective-permute-start(bf16[2,1,64,512]{3,2,1,0:T(8,128)(2,1)S(1)} %slice.83), channel_id=1, source_target_pairs={{0,4},{4,0},{8,12},{12,8},{1,5},{5,1},{9,13},{13,9},{2,6},{6,2},{1... | collective-permute-start | bytes 393224 | tf_op jit(solution)/shard_map/ppermute | solution.py:54
  106.5 14.9 %collective-permute-start.20 = (bf16[2,1,64,512]{3,2,1,0:T(8,128)(2,1)S(1)}, bf16[2,1,64,512]{3,2,1,0:T(8,128)(2,1)S(1)}, u32[]{:S(2)}, u32[]{:S(2)}) collective-permute-start(bf16[2,1,64,512]{3,2,1,0:T(8,128)(2,1)S(1)} %add_convert_fusion.14), channel_id=1, source_target_pairs={{0,8},{4,12},{8,0},{12,4},{1,9},{5,13},{9,1},{13,5},{2,10},{6,14},... | collective-permute-start | bytes 393224 | tf_op jit(solution)/shard_map/ppermute | solution.py:54
  109.1 9.3 %collective-permute-start.18 = (f32[32,1024]{1,0:T(8,128)S(1)}, f32[32,1024]{1,0:T(8,128)S(1)}, u32[]{:S(2)}, u32[]{:S(2)}) collective-permute-start(f32[32,1024]{1,0:T(8,128)S(1)} %add.89), channel_id=1, source_target_pairs={{0,4},{4,0},{8,12},{12,8},{1,5},{5,1},{9,13},{13,9},{2,6},{6,2},{1... | collective-permute-start | bytes 393224 | tf_op jit(solution)/shard_map/ppermute | solution.py:54
  114.1 12.2 %collective-permute-start.17 = (bf16[2,1,64,512]{3,2,1,0:T(8,128)(2,1)S(1)}, bf16[2,1,64,512]{3,2,1,0:T(8,128)(2,1)S(1)}, u32[]{:S(2)}, u32[]{:S(2)}) collective-permute-start(bf16[2,1,64,512]{3,2,1,0:T(8,128)(2,1)S(1)} %add_convert_fusion.13), channel_id=1, source_target_pairs={{0,8},{4,12},{8,0},{12,4},{1,9},{5,13},{9,1},{13,5},{2,10},{6,14},... | collective-permute-start | bytes 393224 | tf_op jit(solution)/shard_map/ppermute | solution.py:54
  115.9 8.7 %collective-permute-start.19 = (bf16[2,1,64,640]{3,2,1,0:T(8,128)(2,1)S(1)}, bf16[2,1,64,640]{3,2,1,0:T(8,128)(2,1)S(1)}, u32[]{:S(2)}, u32[]{:S(2)}) collective-permute-start(bf16[2,1,64,640]{3,2,1,0:T(8,128)(2,1)S(1)} %add_convert_fusion.9), channel_id=1, source_target_pairs={{0,4},{4,0},{8,12},{12,8},{1,5},{5,1},{9,13},{13,9},{2,6},{6,2},{1... | collective-permute-start | bytes 491528 | tf_op jit(solution)/shard_map/ppermute | solution.py:54
  118.5 9.6 %collective-permute-start.22 = (f32[32,1024]{1,0:T(8,128)S(1)}, f32[32,1024]{1,0:T(8,128)S(1)}, u32[]{:S(2)}, u32[]{:S(2)}) collective-permute-start(f32[32,1024]{1,0:T(8,128)S(1)} %add.92), channel_id=1, source_target_pairs={{0,8},{4,12},{8,0},{12,4},{1,9},{5,13},{9,1},{13,5},{2,10},{6,14},... | collective-permute-start | bytes 393224 | tf_op jit(solution)/shard_map/ppermute | solution.py:54
  121.4 6.0 %collective-permute-start.23 = (bf16[2,1,64,512]{3,2,1,0:T(8,128)(2,1)S(1)}, bf16[2,1,64,512]{3,2,1,0:T(8,128)(2,1)S(1)}, u32[]{:S(2)}, u32[]{:S(2)}) collective-permute-start(bf16[2,1,64,512]{3,2,1,0:T(8,128)(2,1)S(1)} %add_convert_fusion.12), channel_id=1, source_target_pairs={{0,4},{4,0},{8,12},{12,8},{1,5},{5,1},{9,13},{13,9},{2,6},{6,2},{1... | collective-permute-start | bytes 393224 | tf_op jit(solution)/shard_map/ppermute | solution.py:54
  124.6 10.7 %collective-permute-start.26 = (bf16[2,2,64,640]{3,2,1,0:T(8,128)(2,1)S(1)}, bf16[2,2,64,640]{3,2,1,0:T(8,128)(2,1)S(1)}, u32[]{:S(2)}, u32[]{:S(2)}) collective-permute-start(bf16[2,2,64,640]{3,2,1,0:T(8,128)(2,1)S(1)} %constant_dynamic-update-slice_fusion), channel_id=1, source_target_pairs={{0,2},{2,0},{1,3},{3,1},{4,6},{6,4},{5,7},{7,5},{8,10},{10,8},{9,1... | collective-permute-start | bytes 983048 | tf_op jit(solution)/shard_map/ppermute | solution.py:54
  126.3 5.0 %collective-permute-start.21 = (bf16[2,1,64,512]{3,2,1,0:T(8,128)(2,1)S(1)}, bf16[2,1,64,512]{3,2,1,0:T(8,128)(2,1)S(1)}, u32[]{:S(2)}, u32[]{:S(2)}) collective-permute-start(bf16[2,1,64,512]{3,2,1,0:T(8,128)(2,1)S(1)} %add_convert_fusion.11), channel_id=1, source_target_pairs={{0,4},{4,0},{8,12},{12,8},{1,5},{5,1},{9,13},{13,9},{2,6},{6,2},{1... | collective-permute-start | bytes 393224 | tf_op jit(solution)/shard_map/ppermute | solution.py:54
  127.4 10.2 %collective-permute-start.25 = (bf16[2,2,64,512]{3,2,1,0:T(8,128)(2,1)S(1)}, bf16[2,2,64,512]{3,2,1,0:T(8,128)(2,1)S(1)}, u32[]{:S(2)}, u32[]{:S(2)}) collective-permute-start(bf16[2,2,64,512]{3,2,1,0:T(8,128)(2,1)S(1)} %constant_dynamic-update-slice_fusion.2), channel_id=1, source_target_pairs={{0,16},{16,0},{1,17},{17,1},{2,18},{18,2},{3,19},{19,3},{4,20},{20... | collective-permute-start | bytes 786440 | tf_op jit(solution)/shard_map/ppermute | solution.py:54
  135.3 10.7 %collective-permute-start.28 = (bf16[2,4,64,640]{3,2,1,0:T(8,128)(2,1)S(1)}, bf16[2,4,64,640]{3,2,1,0:T(8,128)(2,1)S(1)}, u32[]{:S(2)}, u32[]{:S(2)}) collective-permute-start(bf16[2,4,64,640]{3,2,1,0:T(8,128)(2,1)S(1)} %constant_dynamic-update-slice_fusion.6), channel_id=1, source_target_pairs={{0,16},{16,0},{1,17},{17,1},{2,18},{18,2},{3,19},{19,3},{4,20},{20... | collective-permute-start | bytes 1966088 | tf_op jit(solution)/shard_map/ppermute | solution.py:54
  136.0 6.4 %collective-permute-start.24 = (bf16[2,2,64,512]{3,2,1,0:T(8,128)(2,1)S(1)}, bf16[2,2,64,512]{3,2,1,0:T(8,128)(2,1)S(1)}, u32[]{:S(2)}, u32[]{:S(2)}) collective-permute-start(bf16[2,2,64,512]{3,2,1,0:T(8,128)(2,1)S(1)} %constant_dynamic-update-slice_fusion.4), channel_id=1, source_target_pairs={{0,2},{2,0},{1,3},{3,1},{4,6},{6,4},{5,7},{7,5},{8,10},{10,8},{9,1... | collective-permute-start | bytes 786440 | tf_op jit(solution)/shard_map/ppermute | solution.py:54
  137.6 10.4 %collective-permute-start.27 = (bf16[2,4,64,512]{3,2,1,0:T(8,128)(2,1)S(1)}, bf16[2,4,64,512]{3,2,1,0:T(8,128)(2,1)S(1)}, u32[]{:S(2)}, u32[]{:S(2)}) collective-permute-start(bf16[2,4,64,512]{3,2,1,0:T(8,128)(2,1)S(1)} %constant_dynamic-update-slice_fusion.8), channel_id=1, source_target_pairs={{0,2},{2,0},{1,3},{3,1},{4,6},{6,4},{5,7},{7,5},{8,10},{10,8},{9,1... | collective-permute-start | bytes 1572872 | tf_op jit(solution)/shard_map/ppermute | solution.py:54
  146.1 4.8 %copy-start.3 = (bf16[2,8,64,640]{3,2,1,0:T(8,128)(2,1)}, bf16[2,8,64,640]{3,2,1,0:T(8,128)(2,1)S(1)}, u32[]{:S(2)}) copy-start(bf16[2,8,64,640]{3,2,1,0:T(8,128)(2,1)S(1)} %constant_dynamic-update-slice_fusion.12.mine_ref) | copy-start | bytes 3932164
  146.1 3.6 %collective-permute-start.30 = (bf16[2,8,64,640]{3,2,1,0:T(8,128)(2,1)S(1)}, bf16[2,8,64,640]{3,2,1,0:T(8,128)(2,1)S(1)}, u32[]{:S(2)}, u32[]{:S(2)}) collective-permute-start(bf16[2,8,64,640]{3,2,1,0:T(8,128)(2,1)S(1)} %constant_dynamic-update-slice_fusion.12.mine_ref), channel_id=1, source_target_pairs={{0,1},{1,0},{2,3},{3,2},{4,5},{5,4},{6,7},{7,6},{8,9},{9,8},{10,11... | collective-permute-start | bytes 3932168 | tf_op jit(solution)/shard_map/ppermute | solution.py:54
  148.1 8.4 %copy-start.5 = (bf16[2,8,64,512]{3,2,1,0:T(8,128)(2,1)}, bf16[2,8,64,512]{3,2,1,0:T(8,128)(2,1)S(1)}, u32[]{:S(2)}) copy-start(bf16[2,8,64,512]{3,2,1,0:T(8,128)(2,1)S(1)} %constant_dynamic-update-slice_fusion.14.mine_ref) | copy-start | bytes 3145732
  148.1 2.7 %collective-permute-start.29 = (bf16[2,8,64,512]{3,2,1,0:T(8,128)(2,1)S(1)}, bf16[2,8,64,512]{3,2,1,0:T(8,128)(2,1)S(1)}, u32[]{:S(2)}, u32[]{:S(2)}) collective-permute-start(bf16[2,8,64,512]{3,2,1,0:T(8,128)(2,1)S(1)} %constant_dynamic-update-slice_fusion.14.mine_ref), channel_id=1, source_target_pairs={{0,1},{1,0},{2,3},{3,2},{4,5},{5,4},{6,7},{7,6},{8,9},{9,8},{10,11... | collective-permute-start | bytes 3145736 | tf_op jit(solution)/shard_map/ppermute | solution.py:54
  148.2 14.3 %collective-permute-start.31 = (bf16[2,4,64,512]{3,2,1,0:T(8,128)(2,1)S(1)}, bf16[2,4,64,512]{3,2,1,0:T(8,128)(2,1)S(1)}, u32[]{:S(2)}, u32[]{:S(2)}) collective-permute-start(bf16[2,4,64,512]{3,2,1,0:T(8,128)(2,1)S(1)} %constant_dynamic-update-slice_fusion.10), channel_id=1, source_target_pairs={{0,16},{16,0},{1,17},{17,1},{2,18},{18,2},{3,19},{19,3},{4,20},{20... | collective-permute-start | bytes 1572872 | tf_op jit(solution)/shard_map/ppermute | solution.py:54
  149.7 1.1 copy-start.7
  150.9 5.7 %copy-start.8 = (bf16[2,8,64,512]{3,2,1,0:T(8,128)(2,1)}, bf16[2,8,64,512]{3,2,1,0:T(8,128)(2,1)S(1)}, u32[]{:S(2)}) copy-start(bf16[2,8,64,512]{3,2,1,0:T(8,128)(2,1)S(1)} %collective-permute-done.29.other_ref) | copy-start | bytes 3145732
  162.6 7.7 %copy-start.4 = (bf16[2,8,64,512]{3,2,1,0:T(8,128)(2,1)}, bf16[2,8,64,512]{3,2,1,0:T(8,128)(2,1)S(1)}, u32[]{:S(2)}) copy-start(bf16[2,8,64,512]{3,2,1,0:T(8,128)(2,1)S(1)} %constant_dynamic-update-slice_fusion.16.mine_ref) | copy-start | bytes 3145732
  162.6 7.7 %collective-permute-start.32 = (bf16[2,8,64,512]{3,2,1,0:T(8,128)(2,1)S(1)}, bf16[2,8,64,512]{3,2,1,0:T(8,128)(2,1)S(1)}, u32[]{:S(2)}, u32[]{:S(2)}) collective-permute-start(bf16[2,8,64,512]{3,2,1,0:T(8,128)(2,1)S(1)} %constant_dynamic-update-slice_fusion.16.mine_ref), channel_id=1, source_target_pairs={{0,1},{1,0},{2,3},{3,2},{4,5},{5,4},{6,7},{7,6},{8,9},{9,8},{10,11... | collective-permute-start | bytes 3145736 | tf_op jit(solution)/shard_map/ppermute | solution.py:54
  170.3 1.0 copy-start.9

commit v8 on v7

--- a/solution.py
+++ b/solution.py
@@ -16,9 +16,9 @@
 CHUNKS = 2
 VMEM = 56 << 20
 ORDER = (
-    "top", "in0", "in1", "taps", "in0", "small", "in1", "top", "in0", "small", "top", "in1",
-    "in0", "small", "in1", "top", "small", "in0", "top", "in1", "in0", "small", "in1", "top",
-    "in0", "in1", "top", "in0", "top", "in0", "write_top", "in1", "write0", "in1", "write1",
+    "top", "in0", "in1", "taps", "top", "in0", "in1", "small", "in0", "top", "in1", "in0",
+    "small", "top", "in1", "in0", "small", "top", "in0", "in1", "small", "top", "in1", "in0",
+    "top", "small", "in1", "top", "write_top", "in0", "in1", "in0", "in1", "write_in",
 )
 SMEM_SPEC = pl.BlockSpec(memory_space=pltpu.SMEM)
 F32 = jnp.float32
@@ -46,21 +46,34 @@
 FAR = "far"
 REST = "rest"
 CORE = "core"
-SMALL_STEPS = ((CORE, 1), ("member", 1), ("near", 1), (FAR, 1), (FAR, 2))
+ALL = ("member", REST, FAR, "near", CORE)
+FIRST, SECOND = "first", "second"
+SMALL_STEPS = ((CORE, 1), (FIRST, 1), (SECOND, 1), (FAR, 1), (FAR, 2))
 
 
 def exchange(values, axis, bit=1):
-    size = lax.axis_size(axis)
-    return lax.ppermute(values, axis, [(i, i ^ bit) for i in range(size)])
+    if axis not in (FIRST, SECOND):
+        size = lax.axis_size(axis)
+        return lax.ppermute(values, axis, [(i, i ^ bit) for i in range(size)])
+    count = 1
+    for name in ALL:
+        count *= lax.axis_size(name)
+    near, member = 2, count // 2
+    pairs = [(i, i ^ (member if (i % 2 == 0) == (axis == FIRST) else near)) for i in range(count)]
+    return lax.ppermute(values, ALL, pairs)
 
 
 def add(own, other):
     return (own.astype(F32) + other.astype(F32)).astype(own.dtype)
 
 
-def own_place(order):
-    place = lax.axis_index(order[0]) * 4 + lax.axis_index(order[1]) * 2 + (lax.axis_index(FAR) & 1)
-    return place.astype(jnp.int32)
+def own_places():
+    core, member, near = lax.axis_index(CORE), lax.axis_index("member"), lax.axis_index("near")
+    low = lax.axis_index(FAR) & 1
+    places = (member * 4 + near * 2 + low, near * 4 + member * 2 + low)
+    own = jnp.where(core == 0, places[0], places[1])
+    other = jnp.where(core == 0, places[1], places[0])
+    return jnp.stack([core, own, other]).astype(jnp.int32)
 
 
 def over_rest(values):
@@ -91,17 +104,20 @@
         self.values[name] = value
         self.last = name
 
-    def begin(self, name, send, keep, order):
+    def begin(self, name, send, keep):
         self.values[name] = keep
         self.pending[name] = exchange(send, CORE)
-        halve, gather = [("halve", axis) for axis in order], [("gather", axis) for axis in order]
-        self.steps[name] = (
-            [("add", CORE)]
-            + halve
-            + [("halve", FAR), ("double", FAR), ("gather", FAR)]
-            + gather[::-1]
-            + [("done", CORE)]
-        )
+        self.steps[name] = [
+            ("add", CORE),
+            ("halve", FIRST),
+            ("halve", SECOND),
+            ("halve", FAR),
+            ("double", FAR),
+            ("gather", FAR),
+            ("gather", SECOND),
+            ("gather", FIRST),
+            ("done", CORE),
+        ]
 
     def begin_small(self, name, value):
         self.values[name] = value
@@ -143,12 +159,11 @@
 
 def write_pieces(own_ref, product, send_ref, keep_ref, group):
     rows = keep_ref.shape[-2]
-    core, place = own_ref[0], own_ref[1]
+    core = own_ref[0]
 
     def one(piece, carry):
-        base = (piece ^ place) * (2 * rows)
-        kept = pl.multiple_of(base + core * rows, rows)
-        sent = pl.multiple_of(base + (1 - core) * rows, rows)
+        kept = pl.multiple_of((2 * (piece ^ own_ref[1]) + core) * rows, rows)
+        sent = pl.multiple_of((2 * (piece ^ own_ref[2]) + 1 - core) * rows, rows)
         keep_ref[group, piece] = product[pl.ds(kept, rows), :].astype(BF16)
         send_ref[group, piece] = product[pl.ds(sent, rows), :].astype(BF16)
         return carry
@@ -614,18 +629,23 @@
     return (dot(ones, high, 1, 1) + dot(ones, low, 1, 1))[0:1, :]
 
 
-def write_rows(own_ref, step, piece_refs, group, scale, targets):
-    mine_ref, other_ref = piece_refs
-    places, rows = mine_ref.shape[1:3]
-    core, place = own_ref[0], own_ref[1]
+def write_rows(own_ref, piece_refs, group, scale, targets):
+    places, rows = piece_refs[0].shape[1:3]
+    core = own_ref[0]
     for index in range(places):
-        piece = index ^ (place & (places - 1))
-        for side, source in ((core, mine_ref), (1 - core, other_ref)):
+        for whose, (side, source) in enumerate(zip((core, 1 - core), piece_refs)):
+            piece = index ^ (own_ref[1 + whose] & (places - 1))
             here = pl.ds(pl.multiple_of(index * 2 * rows + side * rows, rows), rows)
             for target, there, first, width in targets:
                 target[here, there : there + width] = (
                     source[group, piece, :, first : first + width].astype(F32) * scale
                 )
+
+
+def piece_spec(array, places, whose):
+    return pl.BlockSpec(
+        (2, places) + array.shape[2:], lambda i, own_ref: (0, i ^ (own_ref[1 + whose] // places), 0, 0)
+    )
 
 
 def unpack_top_kernel(
@@ -652,7 +672,7 @@
             (wout_ref, group * half_out, 0, half_out),
             (dhead_ref, group * half_head, half_out, half_head),
         )
-        write_rows(own_ref, pl.program_id(0), (mine_ref, other_ref), group, scale, targets)
+        write_rows(own_ref, (mine_ref, other_ref), group, scale, targets)
     dgain_ref[...] = gain_row(gain_terms(head_ref[...], dhead_ref[...])) / gain_ref[...]
     depth_ref[...] = small_ref[:taps, :] * scale
     loss_ref[...] = losses_ref[...] * scale[None]
@@ -665,9 +685,6 @@
     taps = small.shape[0] - 1
     places = PLACES // steps
     row = pl.BlockSpec((1, rows), lambda i, own_ref: (0, i))
-    piece = pl.BlockSpec(
-        (2, places) + mine.shape[2:], lambda i, own_ref: (0, i ^ (own_ref[1] // places), 0, 0)
-    )
 
     def block(width):
         return pl.BlockSpec((rows, width), lambda i, own_ref: (i, 0))
@@ -686,8 +703,8 @@
             grid=(steps,),
             in_specs=[
                 fixed(*small.shape),
-                piece,
-                piece,
+                piece_spec(mine, places, 0),
+                piece_spec(other, places, 1),
                 block(symbols),
                 row,
                 fixed(*losses.shape),
@@ -706,63 +723,43 @@
     )(own, small, mine, other, head, gain, losses)
 
 
-def unpack_inner_kernel(
-    utts, last, own_ref, small_ref, mine_ref, other_ref, weight_ref, gain_ref, *refs
-):
-    win_ref, dgain_ref, sums_ref = refs[-3:]
+def unpack_inner_kernel(utts, own_ref, small_ref, weight_ref, gain_ref, *refs):
+    *piece_refs, win_ref, dgain_ref = refs
     scale = utts / small_ref[small_ref.shape[0] - 1 :, 0:1]
-    targets = ((win_ref, 0, 0, win_ref.shape[1]),)
-    write_rows(own_ref, pl.program_id(0), (mine_ref, other_ref), 0, scale, targets)
-    terms = gain_terms(weight_ref[...], win_ref[...])
-
-    @pl.when(pl.program_id(1) == 0)
-    def _():
-        sums_ref[...] = terms
-
-    @pl.when(pl.program_id(1) == 1)
-    def _():
-        total = gain_row(sums_ref[...] + terms)
-        if len(refs) > 3:
-            total = total + refs[1][...]
-        dgain_ref[...] = total / gain_ref[...] if last else total
-
-
-def unpack_inner(utts, own, small, mine, other, weight, gain, chunk, before):
-    steps = 2
+    half = win_ref.shape[1] // 2
+    for chunk in range(CHUNKS):
+        pair = piece_refs[2 * chunk : 2 * chunk + 2]
+        width = pair[0].shape[3]
+        for group in range(2):
+            targets = ((win_ref, group * half + chunk * width, 0, width),)
+            write_rows(own_ref, pair, group, scale, targets)
+    dgain_ref[...] = gain_row(gain_terms(weight_ref[...], win_ref[...])) / gain_ref[...]
+
+
+def unpack_inner(utts, own, small, pieces, weight, gain):
+    steps = 4
     model, width = weight.shape
     rows = model // steps
-    wide = mine.shape[3]
     places = PLACES // steps
-    row = pl.BlockSpec((1, rows), lambda i, j, own_ref: (0, i))
-    block = pl.BlockSpec((rows, wide), lambda i, j, own_ref: (i, j * CHUNKS + chunk))
-    piece = pl.BlockSpec(
-        (1, places) + mine.shape[2:], lambda i, j, own_ref: (j, i ^ (own_ref[1] // places), 0, 0)
-    )
+    row = pl.BlockSpec((1, rows), lambda i, own_ref: (0, i))
+    block = pl.BlockSpec((rows, width), lambda i, own_ref: (i, 0))
     return pl.pallas_call(
-        functools.partial(unpack_inner_kernel, utts, chunk == CHUNKS - 1),
+        functools.partial(unpack_inner_kernel, utts),
         out_shape=(
             jax.ShapeDtypeStruct((model, width), F32),
             jax.ShapeDtypeStruct((1, model), F32),
         ),
         grid_spec=pltpu.PrefetchScalarGridSpec(
             num_scalar_prefetch=1,
-            grid=(steps, 2),
-            in_specs=[
-                pl.BlockSpec(small.shape, lambda i, j, own_ref: (0, 0)),
-                piece,
-                piece,
-                block,
-                row,
-            ]
-            + ([pl.BlockSpec(memory_space=pl.ANY), row] if before else []),
+            grid=(steps,),
+            in_specs=[fixed(*small.shape), block, row]
+            + [piece_spec(array, places, index % 2) for index, array in enumerate(pieces)],
             out_specs=(block, row),
-            scratch_shapes=[pltpu.VMEM((rows, LANES), F32)],
         ),
-        input_output_aliases={6: 0} if before else {},
         compiler_params=params(),
-        cost_estimate=cost(4),
+        cost_estimate=cost(8),
         name="unpack_inner",
-    )(own, small, mine, other, weight, gain, *before)
+    )(own, small, weight, gain, *pieces)
 
 
 def on_device(
@@ -780,9 +777,7 @@
     for axis in ("member", "near", FAR, REST, CORE):
         count *= lax.axis_size(axis)
     member = lax.axis_index("member").astype(jnp.int32)[None]
-    core = lax.axis_index(CORE).astype(jnp.int32)
-    orders = (("near", "member"), ("member", "near"))
-    owns = [jnp.stack([core, own_place(order)]) for order in orders]
+    own = own_places()
     taps, model = weight_depth.shape
     utterances, frames, _ = features.shape
     utts = float(utterances * count)
@@ -804,7 +799,7 @@
         nonlocal dresidual
         dresidual = line.before_kernel(dresidual)
         send, keep, dconv = inner(
-            owns[chunk],
+            own,
             lengths,
             dresidual,
             weight_out,
@@ -816,12 +811,12 @@
             chunk,
             utterances,
         )
-        line.begin(name, send, keep, orders[chunk])
+        line.begin(name, send, keep)
         line.put(name + "_conv", dconv)
 
-    send, keep = outer(owns[1], active, dresidual, final, dlogits)
+    send, keep = outer(own, active, dresidual, final, dlogits)
     send, keep, dresidual = tie((send, keep, dresidual))
-    line.begin("top", send, keep, orders[1])
+    line.begin("top", send, keep)
     products("in0", 0)
     line.step("top", start=False)
     products("in1", 1)
@@ -831,7 +826,7 @@
         mine, other = line.values["top"]
         *rest, written["losses"] = unpack_top(
             utts,
-            owns[1],
+            own,
             line.values["small"],
             line.after_last(mine),
             other,
@@ -843,19 +838,10 @@
         written["out"], written["head"], by_head, written["depth"] = rest
         line.put("by_head", by_head)
 
-    def write_in(chunk, name):
-        mine, other = line.values[name]
-        before = (written["in"], line.values["by_in"]) if chunk else ()
+    def write_in():
+        pieces = [array for name in ("in0", "in1") for array in line.values[name]]
         written["in"], by_in = unpack_inner(
-            utts,
-            owns[chunk],
-            line.values["small"],
-            line.after_last(mine),
-            other,
-            weight_in,
-            gain_conv[None],
-            chunk,
-            before,
+            utts, own, line.values["small"], pieces, weight_in, gain_conv[None]
         )
         line.put("by_in", by_in)
 
@@ -868,8 +854,7 @@
     kernels = {
         "taps": sum_taps,
         "write_top": write_top,
-        "write0": functools.partial(write_in, 0, "in0"),
-        "write1": functools.partial(write_in, 1, "in1"),
+        "write_in": write_in,
     }
     for name in ORDER:
         if name in kernels:

time: 178 us -> 159 us (0.89)
  waiting for transfers between devices: 51.2 us -> 42.7 us
  starting transfers between devices: 40.5 us -> 35 us
  Pallas kernels: 76.7 us -> 72.2 us
    ppermute x33 -> x19, waiting for transfers between devices: 51.2 us -> 31.4 us  [exchange(): return lax.ppermute(values, axis, [(i, i ^ bit) for i in range(size)])]
    ppermute x33 -> x19, starting transfers between devices: 40.5 us -> 23.9 us  [exchange(): return lax.ppermute(values, axis, [(i, i ^ bit) for i in range(size)])]
    ppermute x0 -> x14, waiting for transfers between devices: none -> 11.3 us  [exchange(): return lax.ppermute(values, ALL, pairs)]
    ppermute x0 -> x14, starting transfers between devices: none -> 11.1 us  [exchange(): return lax.ppermute(values, ALL, pairs)]
    pallas_call x2 -> x1, Pallas kernels: 12.6 us -> 7.77 us  [unpack_inner(): pl.pallas_call(functools.partial(unpack_inner_kernel, utts), out_shape=(j...]
  transfers between devices with their start and end apart: 33 -> 33, of which waited for: 15 -> 17; matrix products, arithmetic and copies ran while one was open for 3% -> 3% of each run, Pallas kernels for 31% -> 31%
where the time goes in v8:
time: 159 us
  Pallas kernels  72.2 us (45%)
  waiting for transfers between devices  42.7 us (27%)
  starting transfers between devices  35 us (22%)
  local copies, waits for them, and re-layouts  4.58 us (3%)
  other arithmetic  3.31 us (2%)
    ppermute x19, waiting for transfers between devices, exchange(): return lax.ppermute(values, axis, [(i, i ^ bit) for i in range(size)])  31.4 us
    ppermute x19, starting transfers between devices, exchange(): return lax.ppermute(values, axis, [(i, i ^ bit) for i in range(size)])  23.9 us
    pallas_call x2, Pallas kernels, inner(): pl.pallas_call(inner_kernel, grid=(steps,), out_shape=(shape, shape, jax....  21.7 us
    pallas_call x1, Pallas kernels, forward(): pl.pallas_call(forward_kernel, grid=(steps,), out_shape=(jax.ShapeDtypeSt...  15.2 us
    ppermute x14, waiting for transfers between devices, exchange(): return lax.ppermute(values, ALL, pairs)  11.3 us
    ppermute x14, starting transfers between devices, exchange(): return lax.ppermute(values, ALL, pairs)  11.1 us
    pallas_call x1, Pallas kernels, unpack_inner(): pl.pallas_call(functools.partial(unpack_inner_kernel, utts), out_shape=(j...  7.77 us
    pallas_call x1, Pallas kernels, tap_sums(): pl.pallas_call(taps_kernel, grid=(steps,), out_shape=jax.ShapeDtypeStruct...  7.14 us
  transfers between devices with their start and end apart: 33, of which 17 were waited for; matrix products, arithmetic and copies ran while one was open for 3% of the time, Pallas kernels for 31%

profile of v8, /device:TPU:0, one launch (start us, length us, event | category | flops | bytes accessed | tf_op | source)
XLA Modules:
  0.0 159.0 jit_solution(16741970674205983299)
XLA Ops:
  0.6 4.0 %teachers.1 = (f32[2,256,256]{2,1,0:T(8,128)}, f32[2,256,256]{2,1,0:T(8,128)}) custom-call(s32[1]{0:T(128)} %bitcast.6.member_ref, bf16[2,4,256,256]{3,2,1,0:T(8,128)(2,1)} %logits_ref.1), custom_call_target="tpu_custom_call" | custom-call | flops 4600000000 | bytes 1048576 | tf_op jit(solution)/shard_map/teachers/pallas_call | solution.py:201
  4.7 2.9 %collective-permute-start = (f32[2,256,256]{2,1,0:T(8,128)}, f32[2,256,256]{2,1,0:T(8,128)S(1)}, u32[]{:S(2)}, u32[]{:S(2)}) collective-permute-start(f32[2,256,256]{2,1,0:T(8,128)} %get-tuple-element.110), channel_id=1, source_target_pairs={{0,16},{16,0},{1,17},{17,1},{2,18},{18,2},{3,19},{19,3},{4,20},{20... | collective-permute-start | bytes 1572872 | tf_op jit(solution)/shard_map/ppermute | solution.py:57
  7.6 15.2 %forward.1 = (bf16[1024,512]{1,0:T(8,128)(2,1)}, f32[512,1024]{1,0:T(8,128)}, f32[512,1024]{1,0:T(8,128)}, f32[512,1024]{1,0:T(8,128)}, bf16[512,1024]{1,0:T(8,128)(2,1)}, /*index=5*/f32[512,1024]{1,0:T(8,128)}) custom-call(s32[2]{0:T(128)} %lengths_ref.9, bf16[512,1024]{1,0:T(8,128)(2,1)} %bitcast.9, f32[1,1024]{1,0:T(1,128)} %bitcast.12, ...), custom_call_target="tpu_custom_call" | custom-call | flops 17250000896 | bytes 1048576 | tf_op jit(solution)/shard_map/forward/pallas_call | solution.py:326
  22.8 0.6 pad_add_fusion.own_ref
  23.4 0.8 copy-done.10
  24.3 5.3 %top.1 = (f32[2,1,128]{2,1,0:T(1,128)}, bf16[512,1024]{1,0:T(8,128)(2,1)}, bf16[512,256]{1,0:T(8,128)(2,1)}, bf16[512,1024]{1,0:T(8,128)(2,1)}) custom-call(s32[2]{0:T(128)} %lengths_ref.9, f32[512,1024]{1,0:T(8,128)} %get-tuple-element.108.residual_ref, f32[1,1024]{1,0:T(1,128)} %bitcast.10, bf16[1024,256]{1,0:T(8,128)(2,1)} %head_ref.3, ...), custom_call_target="tpu_custom_call" | custom-call | flops 5750000128 | bytes 1048576 | tf_op jit(solution)/shard_map/top/pallas_call | solution.py:394
  29.6 5.4 %outer.1 = (bf16[2,8,64,640]{3,2,1,0:T(8,128)(2,1)}, bf16[2,8,64,640]{3,2,1,0:T(8,128)(2,1)}) custom-call(s32[3]{0:T(128)} %pad_add_fusion.own_ref, bf16[512,1024]{1,0:T(8,128)(2,1)} %get-tuple-element.107.active_ref, bf16[512,1024]{1,0:T(8,128)(2,1)} %get-tuple-element.128.dresidual_ref, bf16[512,1024]{1,0:T(8,128)(2,1)} %get-tuple-element.112.final_ref, ...), custom_call_target="tpu_custom_call" | custom-call | flops 5750000128 | bytes 1048576 | tf_op jit(solution)/shard_map/outer/pallas_call | solution.py:433
  35.0 10.9 %inner.2 = (bf16[2,8,64,512]{3,2,1,0:T(8,128)(2,1)}, bf16[2,8,64,512]{3,2,1,0:T(8,128)(2,1)}, f32[512,512]{1,0:T(8,128)}) custom-call(s32[3]{0:T(128)} %pad_add_fusion.own_ref, s32[2]{0:T(128)} %lengths_ref.9, bf16[512,1024]{1,0:T(8,128)(2,1)} %get-tuple-element.128.dresidual_ref, bf16[1024,1024]{1,0:T(8,128)(2,1)} %out_weight_ref.5, ...), custom_call_target="tpu_custom_call" | custom-call | flops 12650000384 | bytes 1048576 | tf_op jit(solution)/shard_map/inner/pallas_call | solution.py:518
  46.9 10.8 %inner.3 = (bf16[2,8,64,512]{3,2,1,0:T(8,128)(2,1)}, bf16[2,8,64,512]{3,2,1,0:T(8,128)(2,1)}, f32[512,512]{1,0:T(8,128)}) custom-call(s32[3]{0:T(128)} %pad_add_fusion.own_ref, s32[2]{0:T(128)} %lengths_ref.9, bf16[512,1024]{1,0:T(8,128)(2,1)} %get-tuple-element.128.dresidual_ref, bf16[1024,1024]{1,0:T(8,128)(2,1)} %out_weight_ref.5, ...), custom_call_target="tpu_custom_call" | custom-call | flops 12650000384 | bytes 1048576 | tf_op jit(solution)/shard_map/inner/pallas_call | solution.py:518
  57.7 1.2 collective-permute-start.6
  59.2 0.9 collective-permute-start.5
  60.6 1.4 collective-permute-start.4
  62.4 1.2 collective-permute-start.8
  63.6 7.1 %taps.1 = f32[32,1024]{1,0:T(8,128)} custom-call(s32[2]{0:T(128)} %lengths_ref.9, f32[512,1024]{1,0:T(8,128)} %get-tuple-element.118.gated_ref, f32[512,512]{1,0:T(8,128)} %get-tuple-element.138.refs_0_, f32[512,512]{1,0:T(8,128)} %get-tuple-element.139.refs_1_), custom_call_target="tpu_custom_call" | custom-call | flops 10350000128 | bytes 1048576 | tf_op jit(solution)/shard_map/taps/pallas_call | solution.py:600
  70.8 1.6 %collective-permute-start.7 = (bf16[2,1,64,640]{3,2,1,0:T(8,128)(2,1)S(1)}, bf16[2,1,64,640]{3,2,1,0:T(8,128)(2,1)S(1)}, u32[]{:S(2)}, u32[]{:S(2)}) collective-permute-start(bf16[2,1,64,640]{3,2,1,0:T(8,128)(2,1)S(1)} %slice.78), channel_id=1, source_target_pairs={{0,4},{4,0},{8,12},{12,8},{1,5},{5,1},{9,13},{13,9},{2,6},{6,2},{1... | collective-permute-start | bytes 491528 | tf_op jit(solution)/shard_map/ppermute | solution.py:57
  72.7 1.1 collective-permute-start.9
  73.7 3.8 %collective-permute-done.8 = bf16[2,4,64,512]{3,2,1,0:T(8,128)(2,1)S(1)} collective-permute-done((bf16[2,4,64,512]{3,2,1,0:T(8,128)(2,1)S(1)}, bf16[2,4,64,512]{3,2,1,0:T(8,128)(2,1)S(1)}, u32[]{:S(2)}, u32[]{:S(2)}) %collective-permute-start.8) | collective-permute-done | bytes 524320 | tf_op jit(solution)/shard_map/ppermute | solution.py:63
  77.8 1.6 %collective-permute-start.12 = (f32[32,1024]{1,0:T(8,128)S(1)}, f32[32,1024]{1,0:T(8,128)S(1)}, u32[]{:S(2)}, u32[]{:S(2)}) collective-permute-start(f32[32,1024]{1,0:T(8,128)S(1)} %add.83), channel_id=1, source_target_pairs={{0,16},{1,3},{2,18},{3,1},{4,20},{5,7},{6,22},{7,5},{8,24},{9,11},... | collective-permute-start | bytes 393224 | tf_op jit(solution)/shard_map/ppermute | solution.py:63
  79.4 0.9 collective-permute-done.9
  80.3 1.2 collective-permute-start.14
  81.6 1.9 %collective-permute-start.13 = (bf16[2,1,64,512]{3,2,1,0:T(8,128)(2,1)S(1)}, bf16[2,1,64,512]{3,2,1,0:T(8,128)(2,1)S(1)}, u32[]{:S(2)}, u32[]{:S(2)}) collective-permute-start(bf16[2,1,64,512]{3,2,1,0:T(8,128)(2,1)S(1)} %slice.81), channel_id=1, source_target_pairs={{0,4},{4,0},{8,12},{12,8},{1,5},{5,1},{9,13},{13,9},{2,6},{6,2},{1... | collective-permute-start | bytes 393224 | tf_op jit(solution)/shard_map/ppermute | solution.py:57
  83.5 2.7 %collective-permute-start.11 = (bf16[2,1,64,640]{3,2,1,0:T(8,128)(2,1)S(1)}, bf16[2,1,64,640]{3,2,1,0:T(8,128)(2,1)S(1)}, u32[]{:S(2)}, u32[]{:S(2)}) collective-permute-start(bf16[2,1,64,640]{3,2,1,0:T(8,128)(2,1)S(1)} %add_convert_fusion.10), channel_id=1, source_target_pairs={{0,8},{4,12},{8,0},{12,4},{1,9},{5,13},{9,1},{13,5},{2,10},{6,14},... | collective-permute-start | bytes 491528 | tf_op jit(solution)/shard_map/ppermute | solution.py:57
  86.8 2.4 %collective-permute-done.13 = bf16[2,1,64,512]{3,2,1,0:T(8,128)(2,1)S(1)} collective-permute-done((bf16[2,1,64,512]{3,2,1,0:T(8,128)(2,1)S(1)}, bf16[2,1,64,512]{3,2,1,0:T(8,128)(2,1)S(1)}, u32[]{:S(2)}, u32[]{:S(2)}) %collective-permute-start.13) | collective-permute-done | bytes 131104 | tf_op jit(solution)/shard_map/ppermute | solution.py:57
  89.3 1.6 %collective-permute-start.16 = (bf16[2,1,64,512]{3,2,1,0:T(8,128)(2,1)S(1)}, bf16[2,1,64,512]{3,2,1,0:T(8,128)(2,1)S(1)}, u32[]{:S(2)}, u32[]{:S(2)}) collective-permute-start(bf16[2,1,64,512]{3,2,1,0:T(8,128)(2,1)S(1)} %add_convert_fusion.14), channel_id=1, source_target_pairs={{0,8},{4,12},{8,0},{12,4},{1,9},{5,13},{9,1},{13,5},{2,10},{6,14},... | collective-permute-start | bytes 393224 | tf_op jit(solution)/shard_map/ppermute | solution.py:57
  90.9 0.8 collective-permute-start.15
  91.7 6.2 %collective-permute-done.11 = bf16[2,1,64,640]{3,2,1,0:T(8,128)(2,1)S(1)} collective-permute-done((bf16[2,1,64,640]{3,2,1,0:T(8,128)(2,1)S(1)}, bf16[2,1,64,640]{3,2,1,0:T(8,128)(2,1)S(1)}, u32[]{:S(2)}, u32[]{:S(2)}) %collective-permute-start.11) | collective-permute-done | bytes 163872 | tf_op jit(solution)/shard_map/ppermute | solution.py:57
  98.0 2.1 %collective-permute-start.21 = (bf16[2,1,64,640]{3,2,1,0:T(8,128)(2,1)S(1)}, bf16[2,1,64,640]{3,2,1,0:T(8,128)(2,1)S(1)}, u32[]{:S(2)}, u32[]{:S(2)}) collective-permute-start(bf16[2,1,64,640]{3,2,1,0:T(8,128)(2,1)S(1)} %add_convert_fusion.9), channel_id=1, source_target_pairs={{0,4},{4,0},{8,12},{12,8},{1,5},{5,1},{9,13},{13,9},{2,6},{6,2},{1... | collective-permute-start | bytes 491528 | tf_op jit(solution)/shard_map/ppermute | solution.py:57
  100.0 4.2 %collective-permute-done.17 = bf16[2,1,64,512]{3,2,1,0:T(8,128)(2,1)S(1)} collective-permute-done((bf16[2,1,64,512]{3,2,1,0:T(8,128)(2,1)S(1)}, bf16[2,1,64,512]{3,2,1,0:T(8,128)(2,1)S(1)}, u32[]{:S(2)}, u32[]{:S(2)}) %collective-permute-start.17) | collective-permute-done | bytes 131104 | tf_op jit(solution)/shard_map/ppermute | solution.py:57
  104.8 2.5 %collective-permute-start.20 = (bf16[2,1,64,512]{3,2,1,0:T(8,128)(2,1)S(1)}, bf16[2,1,64,512]{3,2,1,0:T(8,128)(2,1)S(1)}, u32[]{:S(2)}, u32[]{:S(2)}) collective-permute-start(bf16[2,1,64,512]{3,2,1,0:T(8,128)(2,1)S(1)} %add_convert_fusion.12), channel_id=1, source_target_pairs={{0,4},{4,0},{8,12},{12,8},{1,5},{5,1},{9,13},{13,9},{2,6},{6,2},{1... | collective-permute-start | bytes 393224 | tf_op jit(solution)/shard_map/ppermute | solution.py:57
  107.5 1.3 collective-permute-done.21
  108.9 4.1 %collective-permute-done.20 = bf16[2,1,64,512]{3,2,1,0:T(8,128)(2,1)S(1)} collective-permute-done((bf16[2,1,64,512]{3,2,1,0:T(8,128)(2,1)S(1)}, bf16[2,1,64,512]{3,2,1,0:T(8,128)(2,1)S(1)}, u32[]{:S(2)}, u32[]{:S(2)}) %collective-permute-start.20) | collective-permute-done | bytes 131104 | tf_op jit(solution)/shard_map/ppermute | solution.py:57
  113.1 1.3 collective-permute-done.18
  114.5 1.6 collective-permute-done.23
  116.2 3.7 %collective-permute-start.22 = (bf16[2,1,64,512]{3,2,1,0:T(8,128)(2,1)S(1)}, bf16[2,1,64,512]{3,2,1,0:T(8,128)(2,1)S(1)}, u32[]{:S(2)}, u32[]{:S(2)}) collective-permute-start(bf16[2,1,64,512]{3,2,1,0:T(8,128)(2,1)S(1)} %add_convert_fusion.11), channel_id=1, source_target_pairs={{0,4},{4,0},{8,12},{12,8},{1,5},{5,1},{9,13},{13,9},{2,6},{6,2},{1... | collective-permute-start | bytes 393224 | tf_op jit(solution)/shard_map/ppermute | solution.py:57
  119.9 2.9 %collective-permute-done.22 = bf16[2,1,64,512]{3,2,1,0:T(8,128)(2,1)S(1)} collective-permute-done((bf16[2,1,64,512]{3,2,1,0:T(8,128)(2,1)S(1)}, bf16[2,1,64,512]{3,2,1,0:T(8,128)(2,1)S(1)}, u32[]{:S(2)}, u32[]{:S(2)}) %collective-permute-start.22) | collective-permute-done | bytes 131104 | tf_op jit(solution)/shard_map/ppermute | solution.py:57
  122.9 3.3 %collective-permute-done.27 = bf16[2,2,64,512]{3,2,1,0:T(8,128)(2,1)S(1)} collective-permute-done((bf16[2,2,64,512]{3,2,1,0:T(8,128)(2,1)S(1)}, bf16[2,2,64,512]{3,2,1,0:T(8,128)(2,1)S(1)}, u32[]{:S(2)}, u32[]{:S(2)}) %collective-permute-start.27) | collective-permute-done | bytes 262176 | tf_op jit(solution)/shard_map/ppermute | solution.py:63
  126.9 0.7 collective-permute-start.24
  127.6 2.4 %collective-permute-start.25 = (f32[32,1024]{1,0:T(8,128)S(1)}, f32[32,1024]{1,0:T(8,128)S(1)}, u32[]{:S(2)}, u32[]{:S(2)}) collective-permute-start(f32[32,1024]{1,0:T(8,128)S(1)} %add.94), channel_id=1, source_target_pairs={{0,8},{4,12},{8,0},{12,4},{1,9},{5,13},{9,1},{13,5},{2,10},{6,14},... | collective-permute-start | bytes 393224 | tf_op jit(solution)/shard_map/ppermute | solution.py:57
  130.4 6.4 %collective-permute-done.25 = f32[32,1024]{1,0:T(8,128)S(1)} collective-permute-done((f32[32,1024]{1,0:T(8,128)S(1)}, f32[32,1024]{1,0:T(8,128)S(1)}, u32[]{:S(2)}, u32[]{:S(2)}) %collective-permute-start.25) | collective-permute-done | bytes 131104 | tf_op jit(solution)/shard_map/ppermute | solution.py:57
  136.8 0.7 add.95.small_ref
  137.5 1.6 collective-permute-start.29
  139.1 1.1 copy-done.7
  140.2 5.7 %unpack_top.1 = (f32[1024,1024]{1,0:T(8,128)}, f32[1024,256]{1,0:T(8,128)}, f32[1,1024]{1,0:T(1,128)}, f32[31,1024]{1,0:T(8,128)}, f32[2,1,128]{2,1,0:T(1,128)}) custom-call(s32[3]{0:T(128)} %pad_add_fusion.own_ref, f32[32,1024]{1,0:T(8,128)} %add.95.small_ref, bf16[2,8,64,640]{3,2,1,0:T(8,128)(2,1)} %copy-done.3, bf16[2,8,64,640]{3,2,1,0:T(8,128)(2,1)} %copy-done.7, ...), custom_call_target="tpu_custom_call" | custom-call | flops 5750000128 | bytes 1048576 | tf_op jit(solution)/shard_map/unpack_top/pallas_call | solution.py:692
  146.9 0.8 slice_reduce_fusion
  147.6 1.1 collective-permute-done.32.refs_1_
  148.7 1.5 collective-permute-done.31.refs_3_
  150.2 1.0 copy-done.9
  151.2 7.8 %unpack_inner.1 = (f32[1024,2048]{1,0:T(8,128)}, f32[1,1024]{1,0:T(1,128)}) custom-call(s32[3]{0:T(128)} %pad_add_fusion.own_ref, f32[32,1024]{1,0:T(8,128)} %add.95.small_ref, bf16[1024,2048]{1,0:T(8,128)(2,1)} %weight_ref.1, f32[1,1024]{1,0:T(1,128)} %bitcast.13, bf16[2,8,64,512]{3,2,1,0:T(8,128)(2,1)} %copy-done.4, bf16[2,8,64,512]{3,2,1,0:T(8,128)(2,1)} %copy-done.8, ...), custom_call_target="tpu_custom_call" | custom-call | flops 9200000000 | bytes 1048576 | tf_op jit(solution)/shard_map/unpack_inner/pallas_call | solution.py:746
  (100 shorter events, 6.5 us)
Async XLA Ops:
  4.7 18.8 %collective-permute-start = (f32[2,256,256]{2,1,0:T(8,128)}, f32[2,256,256]{2,1,0:T(8,128)S(1)}, u32[]{:S(2)}, u32[]{:S(2)}) collective-permute-start(f32[2,256,256]{2,1,0:T(8,128)} %get-tuple-element.110), channel_id=1, source_target_pairs={{0,16},{16,0},{1,17},{17,1},{2,18},{18,2},{3,19},{19,3},{4,20},{20... | collective-permute-start | bytes 1572872 | tf_op jit(solution)/shard_map/ppermute | solution.py:57
  23.4 0.8 copy-start.10
  35.0 11.4 %collective-permute-start.2 = (bf16[2,8,64,640]{3,2,1,0:T(8,128)(2,1)}, bf16[2,8,64,640]{3,2,1,0:T(8,128)(2,1)S(1)}, u32[]{:S(2)}, u32[]{:S(2)}) collective-permute-start(bf16[2,8,64,640]{3,2,1,0:T(8,128)(2,1)} %get-tuple-element.124), channel_id=1, source_target_pairs={{0,1},{1,0},{2,3},{3,2},{4,5},{5,4},{6,7},{7,6},{8,9},{9,8},{10,11... | collective-permute-start | bytes 3932168 | tf_op jit(solution)/shard_map/ppermute | solution.py:57
  35.0 11.4 %copy-start = (bf16[2,8,64,640]{3,2,1,0:T(8,128)(2,1)S(1)}, bf16[2,8,64,640]{3,2,1,0:T(8,128)(2,1)}, u32[]{:S(2)}) copy-start(bf16[2,8,64,640]{3,2,1,0:T(8,128)(2,1)} %get-tuple-element.123) | copy-start | bytes 3932164
  45.9 14.2 %collective-permute-start.1 = (bf16[2,8,64,512]{3,2,1,0:T(8,128)(2,1)}, bf16[2,8,64,512]{3,2,1,0:T(8,128)(2,1)S(1)}, u32[]{:S(2)}, u32[]{:S(2)}) collective-permute-start(bf16[2,8,64,512]{3,2,1,0:T(8,128)(2,1)} %get-tuple-element.122), channel_id=1, source_target_pairs={{0,1},{1,0},{2,3},{3,2},{4,5},{5,4},{6,7},{7,6},{8,9},{9,8},{10,11... | collective-permute-start | bytes 3145736 | tf_op jit(solution)/shard_map/ppermute | solution.py:57
  46.8 12.1 %collective-permute-start.3 = (bf16[2,4,64,640]{3,2,1,0:T(8,128)(2,1)S(1)}, bf16[2,4,64,640]{3,2,1,0:T(8,128)(2,1)S(1)}, u32[]{:S(2)}, u32[]{:S(2)}) collective-permute-start(bf16[2,4,64,640]{3,2,1,0:T(8,128)(2,1)S(1)} %slice.58), channel_id=1, source_target_pairs={{0,16},{1,3},{2,18},{3,1},{4,20},{5,7},{6,22},{7,5},{8,24},{9,11},... | collective-permute-start | bytes 1966088 | tf_op jit(solution)/shard_map/ppermute | solution.py:63
  57.7 4.3 %collective-permute-start.6 = (bf16[2,8,64,512]{3,2,1,0:T(8,128)(2,1)}, bf16[2,8,64,512]{3,2,1,0:T(8,128)(2,1)S(1)}, u32[]{:S(2)}, u32[]{:S(2)}) collective-permute-start(bf16[2,8,64,512]{3,2,1,0:T(8,128)(2,1)} %get-tuple-element.136), channel_id=1, source_target_pairs={{0,1},{1,0},{2,3},{3,2},{4,5},{5,4},{6,7},{7,6},{8,9},{9,8},{10,11... | collective-permute-start | bytes 3145736 | tf_op jit(solution)/shard_map/ppermute | solution.py:57
  58.9 1.2 copy-start.1
  59.2 11.6 %collective-permute-start.5 = (bf16[2,2,64,640]{3,2,1,0:T(8,128)(2,1)S(1)}, bf16[2,2,64,640]{3,2,1,0:T(8,128)(2,1)S(1)}, u32[]{:S(2)}, u32[]{:S(2)}) collective-permute-start(bf16[2,2,64,640]{3,2,1,0:T(8,128)(2,1)S(1)} %slice.77), channel_id=1, source_target_pairs={{0,2},{1,17},{2,0},{3,19},{4,6},{5,21},{6,4},{7,23},{8,10},{9,25},... | collective-permute-start | bytes 983048 | tf_op jit(solution)/shard_map/ppermute | solution.py:63
  60.5 1.5 copy-start.2
  60.6 11.9 %collective-permute-start.4 = (bf16[2,4,64,512]{3,2,1,0:T(8,128)(2,1)S(1)}, bf16[2,4,64,512]{3,2,1,0:T(8,128)(2,1)S(1)}, u32[]{:S(2)}, u32[]{:S(2)}) collective-permute-start(bf16[2,4,64,512]{3,2,1,0:T(8,128)(2,1)S(1)} %slice.76), channel_id=1, source_target_pairs={{0,16},{1,3},{2,18},{3,1},{4,20},{5,7},{6,22},{7,5},{8,24},{9,11},... | collective-permute-start | bytes 1572872 | tf_op jit(solution)/shard_map/ppermute | solution.py:63
  62.4 15.1 %collective-permute-start.8 = (bf16[2,4,64,512]{3,2,1,0:T(8,128)(2,1)S(1)}, bf16[2,4,64,512]{3,2,1,0:T(8,128)(2,1)S(1)}, u32[]{:S(2)}, u32[]{:S(2)}) collective-permute-start(bf16[2,4,64,512]{3,2,1,0:T(8,128)(2,1)S(1)} %slice.79), channel_id=1, source_target_pairs={{0,16},{1,3},{2,18},{3,1},{4,20},{5,7},{6,22},{7,5},{8,24},{9,11},... | collective-permute-start | bytes 1572872 | tf_op jit(solution)/shard_map/ppermute | solution.py:63
  70.7 7.0 %collective-permute-start.10 = (f32[32,1024]{1,0:T(8,128)}, f32[32,1024]{1,0:T(8,128)S(1)}, u32[]{:S(2)}, u32[]{:S(2)}) collective-permute-start(f32[32,1024]{1,0:T(8,128)} %taps.1), channel_id=1, source_target_pairs={{0,1},{1,0},{2,3},{3,2},{4,5},{5,4},{6,7},{7,6},{8,9},{9,8},{10,11... | collective-permute-start | bytes 393224 | tf_op jit(solution)/shard_map/ppermute | solution.py:57
  70.8 10.8 %collective-permute-start.7 = (bf16[2,1,64,640]{3,2,1,0:T(8,128)(2,1)S(1)}, bf16[2,1,64,640]{3,2,1,0:T(8,128)(2,1)S(1)}, u32[]{:S(2)}, u32[]{:S(2)}) collective-permute-start(bf16[2,1,64,640]{3,2,1,0:T(8,128)(2,1)S(1)} %slice.78), channel_id=1, source_target_pairs={{0,4},{4,0},{8,12},{12,8},{1,5},{5,1},{9,13},{13,9},{2,6},{6,2},{1... | collective-permute-start | bytes 491528 | tf_op jit(solution)/shard_map/ppermute | solution.py:57
  72.6 5.1 %copy-start.6 = (f32[32,1024]{1,0:T(8,128)S(1)}, f32[32,1024]{1,0:T(8,128)}, u32[]{:S(2)}) copy-start(f32[32,1024]{1,0:T(8,128)} %taps.1) | copy-start | bytes 393220
  72.7 7.7 %collective-permute-start.9 = (bf16[2,2,64,512]{3,2,1,0:T(8,128)(2,1)S(1)}, bf16[2,2,64,512]{3,2,1,0:T(8,128)(2,1)S(1)}, u32[]{:S(2)}, u32[]{:S(2)}) collective-permute-start(bf16[2,2,64,512]{3,2,1,0:T(8,128)(2,1)S(1)} %slice.80), channel_id=1, source_target_pairs={{0,2},{1,17},{2,0},{3,19},{4,6},{5,21},{6,4},{7,23},{8,10},{9,25},... | collective-permute-start | bytes 786440 | tf_op jit(solution)/shard_map/ppermute | solution.py:63
  77.8 13.1 %collective-permute-start.12 = (f32[32,1024]{1,0:T(8,128)S(1)}, f32[32,1024]{1,0:T(8,128)S(1)}, u32[]{:S(2)}, u32[]{:S(2)}) collective-permute-start(f32[32,1024]{1,0:T(8,128)S(1)} %add.83), channel_id=1, source_target_pairs={{0,16},{1,3},{2,18},{3,1},{4,20},{5,7},{6,22},{7,5},{8,24},{9,11},... | collective-permute-start | bytes 393224 | tf_op jit(solution)/shard_map/ppermute | solution.py:63
  80.3 6.4 %collective-permute-start.14 = (bf16[2,2,64,512]{3,2,1,0:T(8,128)(2,1)S(1)}, bf16[2,2,64,512]{3,2,1,0:T(8,128)(2,1)S(1)}, u32[]{:S(2)}, u32[]{:S(2)}) collective-permute-start(bf16[2,2,64,512]{3,2,1,0:T(8,128)(2,1)S(1)} %slice.82), channel_id=1, source_target_pairs={{0,2},{1,17},{2,0},{3,19},{4,6},{5,21},{6,4},{7,23},{8,10},{9,25},... | collective-permute-start | bytes 786440 | tf_op jit(solution)/shard_map/ppermute | solution.py:63
  81.6 7.6 %collective-permute-start.13 = (bf16[2,1,64,512]{3,2,1,0:T(8,128)(2,1)S(1)}, bf16[2,1,64,512]{3,2,1,0:T(8,128)(2,1)S(1)}, u32[]{:S(2)}, u32[]{:S(2)}) collective-permute-start(bf16[2,1,64,512]{3,2,1,0:T(8,128)(2,1)S(1)} %slice.81), channel_id=1, source_target_pairs={{0,4},{4,0},{8,12},{12,8},{1,5},{5,1},{9,13},{13,9},{2,6},{6,2},{1... | collective-permute-start | bytes 393224 | tf_op jit(solution)/shard_map/ppermute | solution.py:57
  83.5 14.4 %collective-permute-start.11 = (bf16[2,1,64,640]{3,2,1,0:T(8,128)(2,1)S(1)}, bf16[2,1,64,640]{3,2,1,0:T(8,128)(2,1)S(1)}, u32[]{:S(2)}, u32[]{:S(2)}) collective-permute-start(bf16[2,1,64,640]{3,2,1,0:T(8,128)(2,1)S(1)} %add_convert_fusion.10), channel_id=1, source_target_pairs={{0,8},{4,12},{8,0},{12,4},{1,9},{5,13},{9,1},{13,5},{2,10},{6,14},... | collective-permute-start | bytes 491528 | tf_op jit(solution)/shard_map/ppermute | solution.py:57
  89.3 15.5 %collective-permute-start.16 = (bf16[2,1,64,512]{3,2,1,0:T(8,128)(2,1)S(1)}, bf16[2,1,64,512]{3,2,1,0:T(8,128)(2,1)S(1)}, u32[]{:S(2)}, u32[]{:S(2)}) collective-permute-start(bf16[2,1,64,512]{3,2,1,0:T(8,128)(2,1)S(1)} %add_convert_fusion.14), channel_id=1, source_target_pairs={{0,8},{4,12},{8,0},{12,4},{1,9},{5,13},{9,1},{13,5},{2,10},{6,14},... | collective-permute-start | bytes 393224 | tf_op jit(solution)/shard_map/ppermute | solution.py:57
  90.9 16.5 %collective-permute-start.15 = (f32[32,1024]{1,0:T(8,128)S(1)}, f32[32,1024]{1,0:T(8,128)S(1)}, u32[]{:S(2)}, u32[]{:S(2)}) collective-permute-start(f32[32,1024]{1,0:T(8,128)S(1)} %add.88), channel_id=1, source_target_pairs={{0,2},{1,17},{2,0},{3,19},{4,6},{5,21},{6,4},{7,23},{8,10},{9,25},... | collective-permute-start | bytes 393224 | tf_op jit(solution)/shard_map/ppermute | solution.py:63
  97.9 6.3 %collective-permute-start.17 = (bf16[2,1,64,512]{3,2,1,0:T(8,128)(2,1)S(1)}, bf16[2,1,64,512]{3,2,1,0:T(8,128)(2,1)S(1)}, u32[]{:S(2)}, u32[]{:S(2)}) collective-permute-start(bf16[2,1,64,512]{3,2,1,0:T(8,128)(2,1)S(1)} %slice.83), channel_id=1, source_target_pairs={{0,4},{4,0},{8,12},{12,8},{1,5},{5,1},{9,13},{13,9},{2,6},{6,2},{1... | collective-permute-start | bytes 393224 | tf_op jit(solution)/shard_map/ppermute | solution.py:57
  98.0 10.8 %collective-permute-start.21 = (bf16[2,1,64,640]{3,2,1,0:T(8,128)(2,1)S(1)}, bf16[2,1,64,640]{3,2,1,0:T(8,128)(2,1)S(1)}, u32[]{:S(2)}, u32[]{:S(2)}) collective-permute-start(bf16[2,1,64,640]{3,2,1,0:T(8,128)(2,1)S(1)} %add_convert_fusion.9), channel_id=1, source_target_pairs={{0,4},{4,0},{8,12},{12,8},{1,5},{5,1},{9,13},{13,9},{2,6},{6,2},{1... | collective-permute-start | bytes 491528 | tf_op jit(solution)/shard_map/ppermute | solution.py:57
  104.3 8.8 %collective-permute-start.19 = (bf16[2,1,64,512]{3,2,1,0:T(8,128)(2,1)S(1)}, bf16[2,1,64,512]{3,2,1,0:T(8,128)(2,1)S(1)}, u32[]{:S(2)}, u32[]{:S(2)}) collective-permute-start(bf16[2,1,64,512]{3,2,1,0:T(8,128)(2,1)S(1)} %add_convert_fusion.13), channel_id=1, source_target_pairs={{0,8},{4,12},{8,0},{12,4},{1,9},{5,13},{9,1},{13,5},{2,10},{6,14},... | collective-permute-start | bytes 393224 | tf_op jit(solution)/shard_map/ppermute | solution.py:57
  104.8 8.2 %collective-permute-start.20 = (bf16[2,1,64,512]{3,2,1,0:T(8,128)(2,1)S(1)}, bf16[2,1,64,512]{3,2,1,0:T(8,128)(2,1)S(1)}, u32[]{:S(2)}, u32[]{:S(2)}) collective-permute-start(bf16[2,1,64,512]{3,2,1,0:T(8,128)(2,1)S(1)} %add_convert_fusion.12), channel_id=1, source_target_pairs={{0,4},{4,0},{8,12},{12,8},{1,5},{5,1},{9,13},{13,9},{2,6},{6,2},{1... | collective-permute-start | bytes 393224 | tf_op jit(solution)/shard_map/ppermute | solution.py:57
  107.4 7.0 %collective-permute-start.18 = (f32[32,1024]{1,0:T(8,128)S(1)}, f32[32,1024]{1,0:T(8,128)S(1)}, u32[]{:S(2)}, u32[]{:S(2)}) collective-permute-start(f32[32,1024]{1,0:T(8,128)S(1)} %add.92), channel_id=1, source_target_pairs={{0,4},{4,0},{8,12},{12,8},{1,5},{5,1},{9,13},{13,9},{2,6},{6,2},{1... | collective-permute-start | bytes 393224 | tf_op jit(solution)/shard_map/ppermute | solution.py:57
  108.8 7.2 %collective-permute-start.23 = (bf16[2,2,64,640]{3,2,1,0:T(8,128)(2,1)S(1)}, bf16[2,2,64,640]{3,2,1,0:T(8,128)(2,1)S(1)}, u32[]{:S(2)}, u32[]{:S(2)}) collective-permute-start(bf16[2,2,64,640]{3,2,1,0:T(8,128)(2,1)S(1)} %constant_dynamic-update-slice_fusion), channel_id=1, source_target_pairs={{0,2},{1,17},{2,0},{3,19},{4,6},{5,21},{6,4},{7,23},{8,10},{9,25},... | collective-permute-start | bytes 983048 | tf_op jit(solution)/shard_map/ppermute | solution.py:63
  116.1 10.7 %collective-permute-start.26 = (bf16[2,4,64,640]{3,2,1,0:T(8,128)(2,1)S(1)}, bf16[2,4,64,640]{3,2,1,0:T(8,128)(2,1)S(1)}, u32[]{:S(2)}, u32[]{:S(2)}) collective-permute-start(bf16[2,4,64,640]{3,2,1,0:T(8,128)(2,1)S(1)} %constant_dynamic-update-slice_fusion.4), channel_id=1, source_target_pairs={{0,16},{1,3},{2,18},{3,1},{4,20},{5,7},{6,22},{7,5},{8,24},{9,11},... | collective-permute-start | bytes 1966088 | tf_op jit(solution)/shard_map/ppermute | solution.py:63
  116.2 6.7 %collective-permute-start.22 = (bf16[2,1,64,512]{3,2,1,0:T(8,128)(2,1)S(1)}, bf16[2,1,64,512]{3,2,1,0:T(8,128)(2,1)S(1)}, u32[]{:S(2)}, u32[]{:S(2)}) collective-permute-start(bf16[2,1,64,512]{3,2,1,0:T(8,128)(2,1)S(1)} %add_convert_fusion.11), channel_id=1, source_target_pairs={{0,4},{4,0},{8,12},{12,8},{1,5},{5,1},{9,13},{13,9},{2,6},{6,2},{1... | collective-permute-start | bytes 393224 | tf_op jit(solution)/shard_map/ppermute | solution.py:57
  119.9 6.4 %collective-permute-start.27 = (bf16[2,2,64,512]{3,2,1,0:T(8,128)(2,1)S(1)}, bf16[2,2,64,512]{3,2,1,0:T(8,128)(2,1)S(1)}, u32[]{:S(2)}, u32[]{:S(2)}) collective-permute-start(bf16[2,2,64,512]{3,2,1,0:T(8,128)(2,1)S(1)} %constant_dynamic-update-slice_fusion.2), channel_id=1, source_target_pairs={{0,2},{1,17},{2,0},{3,19},{4,6},{5,21},{6,4},{7,23},{8,10},{9,25},... | collective-permute-start | bytes 786440 | tf_op jit(solution)/shard_map/ppermute | solution.py:63
  126.8 12.3 %copy-start.3 = (bf16[2,8,64,640]{3,2,1,0:T(8,128)(2,1)}, bf16[2,8,64,640]{3,2,1,0:T(8,128)(2,1)S(1)}, u32[]{:S(2)}) copy-start(bf16[2,8,64,640]{3,2,1,0:T(8,128)(2,1)S(1)} %constant_dynamic-update-slice_fusion.10.mine_ref) | copy-start | bytes 3932164
  126.9 12.2 %collective-permute-start.28 = (bf16[2,8,64,640]{3,2,1,0:T(8,128)(2,1)S(1)}, bf16[2,8,64,640]{3,2,1,0:T(8,128)(2,1)S(1)}, u32[]{:S(2)}, u32[]{:S(2)}) collective-permute-start(bf16[2,8,64,640]{3,2,1,0:T(8,128)(2,1)S(1)} %constant_dynamic-update-slice_fusion.10.mine_ref), channel_id=1, source_target_pairs={{0,1},{1,0},{2,3},{3,2},{4,5},{5,4},{6,7},{7,6},{8,9},{9,8},{10,11... | collective-permute-start | bytes 3932168 | tf_op jit(solution)/shard_map/ppermute | solution.py:57
  126.9 10.5 %collective-permute-start.24 = (bf16[2,2,64,512]{3,2,1,0:T(8,128)(2,1)S(1)}, bf16[2,2,64,512]{3,2,1,0:T(8,128)(2,1)S(1)}, u32[]{:S(2)}, u32[]{:S(2)}) collective-permute-start(bf16[2,2,64,512]{3,2,1,0:T(8,128)(2,1)S(1)} %constant_dynamic-update-slice_fusion.6), channel_id=1, source_target_pairs={{0,2},{1,17},{2,0},{3,19},{4,6},{5,21},{6,4},{7,23},{8,10},{9,25},... | collective-permute-start | bytes 786440 | tf_op jit(solution)/shard_map/ppermute | solution.py:63
  127.6 9.2 %collective-permute-start.25 = (f32[32,1024]{1,0:T(8,128)S(1)}, f32[32,1024]{1,0:T(8,128)S(1)}, u32[]{:S(2)}, u32[]{:S(2)}) collective-permute-start(f32[32,1024]{1,0:T(8,128)S(1)} %add.94), channel_id=1, source_target_pairs={{0,8},{4,12},{8,0},{12,4},{1,9},{5,13},{9,1},{13,5},{2,10},{6,14},... | collective-permute-start | bytes 393224 | tf_op jit(solution)/shard_map/ppermute | solution.py:57
  130.0 15.9 %collective-permute-start.30 = (bf16[2,4,64,512]{3,2,1,0:T(8,128)(2,1)S(1)}, bf16[2,4,64,512]{3,2,1,0:T(8,128)(2,1)S(1)}, u32[]{:S(2)}, u32[]{:S(2)}) collective-permute-start(bf16[2,4,64,512]{3,2,1,0:T(8,128)(2,1)S(1)} %constant_dynamic-update-slice_fusion.8), channel_id=1, source_target_pairs={{0,16},{1,3},{2,18},{3,1},{4,20},{5,7},{6,22},{7,5},{8,24},{9,11},... | collective-permute-start | bytes 1572872 | tf_op jit(solution)/shard_map/ppermute | solution.py:63
  137.5 9.2 %collective-permute-start.29 = (bf16[2,4,64,512]{3,2,1,0:T(8,128)(2,1)S(1)}, bf16[2,4,64,512]{3,2,1,0:T(8,128)(2,1)S(1)}, u32[]{:S(2)}, u32[]{:S(2)}) collective-permute-start(bf16[2,4,64,512]{3,2,1,0:T(8,128)(2,1)S(1)} %constant_dynamic-update-slice_fusion.12), channel_id=1, source_target_pairs={{0,16},{1,3},{2,18},{3,1},{4,20},{5,7},{6,22},{7,5},{8,24},{9,11},... | collective-permute-start | bytes 1572872 | tf_op jit(solution)/shard_map/ppermute | solution.py:63
  139.1 1.1 copy-start.7
  145.9 4.2 %copy-start.4 = (bf16[2,8,64,512]{3,2,1,0:T(8,128)(2,1)}, bf16[2,8,64,512]{3,2,1,0:T(8,128)(2,1)S(1)}, u32[]{:S(2)}) copy-start(bf16[2,8,64,512]{3,2,1,0:T(8,128)(2,1)S(1)} %constant_dynamic-update-slice_fusion.14.refs_0_) | copy-start | bytes 3145732
  146.0 0.9 copy-start.11
  146.0 2.7 %collective-permute-start.32 = (bf16[2,8,64,512]{3,2,1,0:T(8,128)(2,1)S(1)}, bf16[2,8,64,512]{3,2,1,0:T(8,128)(2,1)S(1)}, u32[]{:S(2)}, u32[]{:S(2)}) collective-permute-start(bf16[2,8,64,512]{3,2,1,0:T(8,128)(2,1)S(1)} %constant_dynamic-update-slice_fusion.14.refs_0_), channel_id=1, source_target_pairs={{0,1},{1,0},{2,3},{3,2},{4,5},{5,4},{6,7},{7,6},{8,9},{9,8},{10,11... | collective-permute-start | bytes 3145736 | tf_op jit(solution)/shard_map/ppermute | solution.py:57
  146.8 3.4 %copy-start.5 = (bf16[2,8,64,512]{3,2,1,0:T(8,128)(2,1)}, bf16[2,8,64,512]{3,2,1,0:T(8,128)(2,1)S(1)}, u32[]{:S(2)}) copy-start(bf16[2,8,64,512]{3,2,1,0:T(8,128)(2,1)S(1)} %constant_dynamic-update-slice_fusion.16.refs_2_) | copy-start | bytes 3145732
  146.8 3.4 %collective-permute-start.31 = (bf16[2,8,64,512]{3,2,1,0:T(8,128)(2,1)S(1)}, bf16[2,8,64,512]{3,2,1,0:T(8,128)(2,1)S(1)}, u32[]{:S(2)}, u32[]{:S(2)}) collective-permute-start(bf16[2,8,64,512]{3,2,1,0:T(8,128)(2,1)S(1)} %constant_dynamic-update-slice_fusion.16.refs_2_), channel_id=1, source_target_pairs={{0,1},{1,0},{2,3},{3,2},{4,5},{5,4},{6,7},{7,6},{8,9},{9,8},{10,11... | collective-permute-start | bytes 3145736 | tf_op jit(solution)/shard_map/ppermute | solution.py:57
  148.7 1.5 copy-start.8
  150.2 1.0 copy-start.9

commit v9 on v8

--- a/solution.py
+++ b/solution.py
@@ -14,19 +14,18 @@
 TILE = 128
 MARGIN = 16
 CHUNKS = 2
-VMEM = 56 << 20
 ORDER = (
-    "top", "in0", "in1", "taps", "top", "in0", "in1", "small", "in0", "top", "in1", "in0",
-    "small", "top", "in1", "in0", "small", "top", "in0", "in1", "small", "top", "in1", "in0",
-    "top", "small", "in1", "top", "write_top", "in0", "in1", "in0", "in1", "write_in",
+    "top", "in0", "in1", "taps", "top", "small", "in0", "in1", "small", "top", "in0", "in1",
+    "small", "top", "in0", "in1", "small", "top", "in0", "in1", "small", "top", "in0", "in1",
+    "top", "in0", "in1", "top", "write_top", "in0", "in1", "in0", "in1", "write_in",
 )
 SMEM_SPEC = pl.BlockSpec(memory_space=pltpu.SMEM)
 F32 = jnp.float32
 BF16 = jnp.bfloat16
 
 
-def params():
-    return pltpu.CompilerParams(vmem_limit_bytes=VMEM)
+def params(mebibytes):
+    return pltpu.CompilerParams(vmem_limit_bytes=mebibytes << 20)
 
 
 def cost(microseconds):
@@ -47,20 +46,18 @@
 REST = "rest"
 CORE = "core"
 ALL = ("member", REST, FAR, "near", CORE)
-FIRST, SECOND = "first", "second"
-SMALL_STEPS = ((CORE, 1), (FIRST, 1), (SECOND, 1), (FAR, 1), (FAR, 2))
-
-
-def exchange(values, axis, bit=1):
-    if axis not in (FIRST, SECOND):
-        size = lax.axis_size(axis)
-        return lax.ppermute(values, axis, [(i, i ^ bit) for i in range(size)])
+STEPS = ("first", "second", "third", "fourth")
+
+
+def exchange(values, step):
+    if step in (CORE, "member"):
+        return lax.ppermute(values, step, [(0, 1), (1, 0)])
     count = 1
     for name in ALL:
         count *= lax.axis_size(name)
-    near, member = 2, count // 2
-    pairs = [(i, i ^ (member if (i % 2 == 0) == (axis == FIRST) else near)) for i in range(count)]
-    return lax.ppermute(values, ALL, pairs)
+    bits = (count // 2, 2, 4, 8)
+    place = STEPS.index(step)
+    return lax.ppermute(values, ALL, [(i, i ^ bits[place ^ (i % 2)]) for i in range(count)])
 
 
 def add(own, other):
@@ -69,8 +66,8 @@
 
 def own_places():
     core, member, near = lax.axis_index(CORE), lax.axis_index("member"), lax.axis_index("near")
-    low = lax.axis_index(FAR) & 1
-    places = (member * 4 + near * 2 + low, near * 4 + member * 2 + low)
+    far = lax.axis_index(FAR)
+    places = (member * 4 + near * 2 + (far & 1), near * 4 + member * 2 + (far >> 1))
     own = jnp.where(core == 0, places[0], places[1])
     other = jnp.where(core == 0, places[1], places[0])
     return jnp.stack([core, own, other]).astype(jnp.int32)
@@ -109,34 +106,29 @@
         self.pending[name] = exchange(send, CORE)
         self.steps[name] = [
             ("add", CORE),
-            ("halve", FIRST),
-            ("halve", SECOND),
-            ("halve", FAR),
-            ("double", FAR),
-            ("gather", FAR),
-            ("gather", SECOND),
-            ("gather", FIRST),
+            ("halve", "first"),
+            ("halve", "second"),
+            ("halve", "third"),
+            ("double", "fourth"),
+            ("gather", "third"),
+            ("gather", "second"),
+            ("gather", "first"),
             ("done", CORE),
         ]
 
     def begin_small(self, name, value):
         self.values[name] = value
-        self.steps[name] = [("sum", step) for step in SMALL_STEPS]
+        self.steps[name] = [("sum", step) for step in STEPS + (CORE,)]
         self.start(name)
 
     def start(self, name):
         if not self.steps[name]:
             return
-        kind, axis = self.steps[name][0]
+        kind, step = self.steps[name][0]
         values = self.values[name]
         if kind == "halve":
-            self.pending[name] = exchange(values[:, values.shape[1] // 2 :], axis)
-        elif kind == "double":
-            self.pending[name] = exchange(values, axis, 2)
-        elif kind == "sum":
-            self.pending[name] = exchange(values, *axis)
-        else:
-            self.pending[name] = exchange(values, axis)
+            values = values[:, values.shape[1] // 2 :]
+        self.pending[name] = exchange(values, step)
 
     def step(self, name, start=True):
         kind, _ = self.steps[name].pop(0)
@@ -214,7 +206,7 @@
                 ),
             ),
         ),
-        compiler_params=params(),
+        compiler_params=params(16),
         cost_estimate=cost(4),
         name="teachers",
     )(member, logits)
@@ -341,7 +333,7 @@
             pltpu.VMEM((rows, model), BF16),
             pltpu.VMEM((WIDE // LANES, utterances, frames + 2 * MARGIN, LANES), F32),
         ],
-        compiler_params=params(),
+        compiler_params=params(28),
         cost_estimate=cost(15),
         name="forward",
     )(lengths, features, gain, weight_in, weight_in, depth, weight_out)
@@ -407,7 +399,7 @@
             pl.BlockSpec((frames, symbols), lambda i: (i, 0)),
             per_row,
         ),
-        compiler_params=params(),
+        compiler_params=params(20),
         cost_estimate=cost(5),
         name="top",
     )(lengths, residual, gain, head, kept, got)
@@ -443,7 +435,7 @@
         ],
         out_specs=(out, out),
         scratch_shapes=[pltpu.VMEM((model, width), F32)],
-        compiler_params=params(),
+        compiler_params=params(20),
         cost_estimate=cost(5),
         name="outer",
     )(own, active, dresidual, final, dlogits)
@@ -537,7 +529,7 @@
             pltpu.VMEM((rows, WIDE), BF16),
             pltpu.VMEM((model, WIDE), F32),
         ],
-        compiler_params=params(),
+        compiler_params=params(24),
         cost_estimate=cost(11),
         name="inner",
     )(own, lengths, dresidual, weight_out, slope, gated, gate, turned, depth)
@@ -608,7 +600,7 @@
             pltpu.VMEM((WIDE // LANES, utterances, rows // utterances + 2 * MARGIN, LANES), F32),
             pltpu.VMEM((taps, 8, LANES), F32),
         ],
-        compiler_params=params(),
+        compiler_params=params(16),
         cost_estimate=cost(9),
         name="taps",
     )(lengths, gated, *dconvs)
@@ -629,12 +621,13 @@
     return (dot(ones, high, 1, 1) + dot(ones, low, 1, 1))[0:1, :]
 
 
-def write_rows(own_ref, piece_refs, group, scale, targets):
-    places, rows = piece_refs[0].shape[1:3]
+def write_rows(own_ref, piece_refs, places, group, scale, targets):
+    rows = piece_refs[0].shape[2]
     core = own_ref[0]
+    first_place = pl.program_id(0) * places
     for index in range(places):
         for whose, (side, source) in enumerate(zip((core, 1 - core), piece_refs)):
-            piece = index ^ (own_ref[1 + whose] & (places - 1))
+            piece = (first_place + index) ^ own_ref[1 + whose]
             here = pl.ds(pl.multiple_of(index * 2 * rows + side * rows, rows), rows)
             for target, there, first, width in targets:
                 target[here, there : there + width] = (
@@ -642,10 +635,7 @@
                 )
 
 
-def piece_spec(array, places, whose):
-    return pl.BlockSpec(
-        (2, places) + array.shape[2:], lambda i, own_ref: (0, i ^ (own_ref[1 + whose] // places), 0, 0)
-    )
+whole = pl.BlockSpec(memory_space=pltpu.VMEM)
 
 
 def unpack_top_kernel(
@@ -672,7 +662,7 @@
             (wout_ref, group * half_out, 0, half_out),
             (dhead_ref, group * half_head, half_out, half_head),
         )
-        write_rows(own_ref, (mine_ref, other_ref), group, scale, targets)
+        write_rows(own_ref, (mine_ref, other_ref), PLACES // 4, group, scale, targets)
     dgain_ref[...] = gain_row(gain_terms(head_ref[...], dhead_ref[...])) / gain_ref[...]
     depth_ref[...] = small_ref[:taps, :] * scale
     loss_ref[...] = losses_ref[...] * scale[None]
@@ -683,7 +673,6 @@
     model, symbols = head.shape
     rows = model // steps
     taps = small.shape[0] - 1
-    places = PLACES // steps
     row = pl.BlockSpec((1, rows), lambda i, own_ref: (0, i))
 
     def block(width):
@@ -703,8 +692,8 @@
             grid=(steps,),
             in_specs=[
                 fixed(*small.shape),
-                piece_spec(mine, places, 0),
-                piece_spec(other, places, 1),
+                whole,
+                whole,
                 block(symbols),
                 row,
                 fixed(*losses.shape),
@@ -717,7 +706,7 @@
                 fixed(*losses.shape),
             ),
         ),
-        compiler_params=params(),
+        compiler_params=params(20),
         cost_estimate=cost(5),
         name="unpack_top",
     )(own, small, mine, other, head, gain, losses)
@@ -732,7 +721,7 @@
         width = pair[0].shape[3]
         for group in range(2):
             targets = ((win_ref, group * half + chunk * width, 0, width),)
-            write_rows(own_ref, pair, group, scale, targets)
+            write_rows(own_ref, pair, PLACES // 4, group, scale, targets)
     dgain_ref[...] = gain_row(gain_terms(weight_ref[...], win_ref[...])) / gain_ref[...]
 
 
@@ -740,7 +729,6 @@
     steps = 4
     model, width = weight.shape
     rows = model // steps
-    places = PLACES // steps
     row = pl.BlockSpec((1, rows), lambda i, own_ref: (0, i))
     block = pl.BlockSpec((rows, width), lambda i, own_ref: (i, 0))
     return pl.pallas_call(
@@ -753,10 +741,10 @@
             num_scalar_prefetch=1,
             grid=(steps,),
             in_specs=[fixed(*small.shape), block, row]
-            + [piece_spec(array, places, index % 2) for index, array in enumerate(pieces)],
+            + [whole] * len(pieces),
             out_specs=(block, row),
         ),
-        compiler_params=params(),
+        compiler_params=params(24),
         cost_estimate=cost(8),
         name="unpack_inner",
     )(own, small, weight, gain, *pieces)

time: 159 us -> 155 us (0.975)
  Pallas kernels: 72.2 us -> 51.4 us
  local copies, waits for them, and re-layouts: 4.58 us -> 13.4 us
  starting transfers between devices: 35 us -> 39.7 us
  waiting for transfers between devices: 42.7 us -> 46.1 us
    unnamed x33 -> x57, local copies, waits for them, and re-layouts: 3.3 us -> 12.3 us
    pallas_call x2, Pallas kernels: 21.7 us -> 15.9 us  [inner(): pl.pallas_call(inner_kernel, grid=(steps,), out_shape=(shape, shape, jax....]
    ppermute x33, starting transfers between devices: 35 us -> 39.7 us  [the longest x25 34.6 us: exchange(): lax.ppermute(values, ALL, [(i, i ^ bits[place ^ i % 2]) for i in range(co...]
    pallas_call x1, Pallas kernels: 7.77 us -> 4.36 us  [unpack_inner(): pl.pallas_call(functools.partial(unpack_inner_kernel, utts), out_shape=(j...]
    ppermute x33, waiting for transfers between devices: 42.7 us -> 46.1 us  [the longest x25 44 us: exchange(): lax.ppermute(values, ALL, [(i, i ^ bits[place ^ i % 2]) for i in range(co...]
    pallas_call x1, Pallas kernels: 15.2 us -> 12.9 us  [forward(): pl.pallas_call(forward_kernel, grid=(steps,), out_shape=(jax.ShapeDtypeSt...]
    pallas_call x1, Pallas kernels: 5.69 us -> 3.46 us  [unpack_top(): pl.pallas_call(functools.partial(unpack_top_kernel, utts), out_shape=(jax...]
    pallas_call x1, Pallas kernels: 5.37 us -> 3.16 us  [outer(): pl.pallas_call(outer_kernel, grid=(2,), out_shape=(shape, shape), in_spec...]
  transfers between devices with their start and end apart: 33 -> 33, of which waited for: 17 -> 16; matrix products, arithmetic and copies ran while one was open for 3% -> 2% of each run, Pallas kernels for 31% -> 25%
where the time goes in v9:
time: 155 us; the launch traced here: 154 us
  Pallas kernels  51.4 us (33%)
  waiting for transfers between devices  46.1 us (30%)
  starting transfers between devices  39.7 us (26%)
  local copies, waits for them, and re-layouts  13.4 us (9%)
  other arithmetic  2.13 us (1%)
    ppermute x25, waiting for transfers between devices, exchange(): lax.ppermute(values, ALL, [(i, i ^ bits[place ^ i % 2]) for i in range(co...  44 us
    ppermute x25, starting transfers between devices, exchange(): lax.ppermute(values, ALL, [(i, i ^ bits[place ^ i % 2]) for i in range(co...  34.6 us
    pallas_call x2, Pallas kernels, inner(): pl.pallas_call(inner_kernel, grid=(steps,), out_shape=(shape, shape, jax....  15.9 us
    pallas_call x1, Pallas kernels, forward(): pl.pallas_call(forward_kernel, grid=(steps,), out_shape=(jax.ShapeDtypeSt...  12.9 us
    unnamed x57, local copies, waits for them, and re-layouts  12.3 us
    pallas_call x1, Pallas kernels, tap_sums(): pl.pallas_call(taps_kernel, grid=(steps,), out_shape=jax.ShapeDtypeStruct...  5.91 us
    ppermute x8, starting transfers between devices, exchange(): return lax.ppermute(values, step, [(0, 1), (1, 0)])  5.07 us
    pallas_call x1, Pallas kernels, unpack_inner(): pl.pallas_call(functools.partial(unpack_inner_kernel, utts), out_shape=(j...  4.36 us
  transfers between devices with their start and end apart: 33, of which 16 were waited for; matrix products, arithmetic and copies ran while one was open for 2% of the time, Pallas kernels for 25%

profile of v9, /device:TPU:0, one launch (start us, length us, event | category | flops | bytes accessed | tf_op | source)
XLA Modules:
  0.0 154.0 jit_solution(14063554817818890544)
XLA Ops:
  0.6 1.2 copy-done.3
  1.9 2.3 %teachers.1 = (f32[2,256,256]{2,1,0:T(8,128)}, f32[2,256,256]{2,1,0:T(8,128)S(1)}) custom-call(s32[1]{0:T(128)} %bitcast.6.member_ref, bf16[2,4,256,256]{3,2,1,0:T(8,128)(2,1)S(1)} %copy-done.3), custom_call_target="tpu_custom_call" | custom-call | flops 4600000000 | bytes 1048576 | tf_op jit(solution)/shard_map/teachers/pallas_call | solution.py:193
  5.0 2.9 %collective-permute-start = (f32[2,256,256]{2,1,0:T(8,128)}, f32[2,256,256]{2,1,0:T(8,128)S(1)}, u32[]{:S(2)}, u32[]{:S(2)}) collective-permute-start(f32[2,256,256]{2,1,0:T(8,128)} %get-tuple-element.110), channel_id=1, source_target_pairs={{0,16},{16,0},{1,17},{17,1},{2,18},{18,2},{3,19},{19,3},{4,20},{20... | collective-permute-start | bytes 1572872 | tf_op jit(solution)/shard_map/ppermute | solution.py:54
  8.0 12.9 %forward.1 = (bf16[1024,512]{1,0:T(8,128)(2,1)S(1)}, f32[512,1024]{1,0:T(8,128)S(1)}, f32[512,1024]{1,0:T(8,128)S(1)}, f32[512,1024]{1,0:T(8,128)S(1)}, bf16[512...) custom-call(s32[2]{0:T(128)S(1)} %copy-done.9, bf16[512,1024]{1,0:T(8,128)(2,1)S(1)} %bitcast.9, f32[1,1024]{1,0:T(1,128)S(1)} %bitcast.12, ...), custom_call_target="tpu_custom_call" | custom-call | flops 17250000896 | bytes 1048576 | tf_op jit(solution)/shard_map/forward/pallas_call | solution.py:318
  21.0 1.3 copy-done.10
  22.3 1.0 copy-done.12
  23.3 1.3 copy-done.16
  24.6 1.4 copy-done.18
  26.0 1.4 copy-done.20
  27.3 1.0 copy-done.22
  28.4 1.6 %copy-done.11 = f32[512,1024]{1,0:T(8,128)S(1)} copy-done((f32[512,1024]{1,0:T(8,128)S(1)}, f32[512,1024]{1,0:T(8,128)}, u32[]{:S(2)}) %copy-start.11) | copy-done | bytes 2097176
  30.0 1.0 copy-done.15
  31.0 3.4 %top.1 = (f32[2,1,128]{2,1,0:T(1,128)S(1)}, bf16[512,1024]{1,0:T(8,128)(2,1)S(1)}, bf16[512,256]{1,0:T(8,128)(2,1)S(1)}, bf16[512,1024]{1,0:T(8,128)(2,1)S(1)}) custom-call(s32[2]{0:T(128)S(1)} %copy-done.9, f32[512,1024]{1,0:T(8,128)S(1)} %copy-done.11, f32[1,1024]{1,0:T(1,128)S(1)} %bitcast.10, bf16[1024,256]{1,0:T(8,128)(2,1)S(1)} %copy-done.5, ...), custom_call_target="tpu_custom_call" | custom-call | flops 5750000128 | bytes 1048576 | tf_op jit(solution)/shard_map/top/pallas_call | solution.py:386
  34.5 3.2 %outer.1 = (bf16[2,8,64,640]{3,2,1,0:T(8,128)(2,1)S(1)}, bf16[2,8,64,640]{3,2,1,0:T(8,128)(2,1)S(1)}) custom-call(s32[3]{0:T(128)S(1)} %pad_add_fusion.own_ref, bf16[512,1024]{1,0:T(8,128)(2,1)S(1)} %copy-done.13, bf16[512,1024]{1,0:T(8,128)(2,1)S(1)} %get-tuple-element.125.dresidual_ref, bf16[512,1024]{1,0:T(8,128)(2,1)S(1)} %get-tuple-element.112.final_ref, ...), custom_call_target="tpu_custom_call" | custom-call | flops 5750000128 | bytes 1048576 | tf_op jit(solution)/shard_map/outer/pallas_call | solution.py:425
  37.8 7.9 %inner.2 = (bf16[2,8,64,512]{3,2,1,0:T(8,128)(2,1)S(1)}, bf16[2,8,64,512]{3,2,1,0:T(8,128)(2,1)S(1)}, f32[512,512]{1,0:T(8,128)S(1)}) custom-call(s32[3]{0:T(128)S(1)} %pad_add_fusion.own_ref, s32[2]{0:T(128)S(1)} %copy-done.9, bf16[512,1024]{1,0:T(8,128)(2,1)S(1)} %get-tuple-element.125.dresidual_ref, bf16[1024,1024]{1,0:T(8,128)(2,1)S(1)} %copy-done.2, ...), custom_call_target="tpu_custom_call" | custom-call | flops 12650000384 | bytes 1048576 | tf_op jit(solution)/shard_map/inner/pallas_call | solution.py:510
  46.9 7.9 %inner.3 = (bf16[2,8,64,512]{3,2,1,0:T(8,128)(2,1)S(1)}, bf16[2,8,64,512]{3,2,1,0:T(8,128)(2,1)S(1)}, f32[512,512]{1,0:T(8,128)S(1)}) custom-call(s32[3]{0:T(128)S(1)} %pad_add_fusion.own_ref, s32[2]{0:T(128)S(1)} %copy-done.9, bf16[512,1024]{1,0:T(8,128)(2,1)S(1)} %get-tuple-element.125.dresidual_ref, bf16[1024,1024]{1,0:T(8,128)(2,1)S(1)} %copy-done.2, ...), custom_call_target="tpu_custom_call" | custom-call | flops 12650000384 | bytes 1048576 | tf_op jit(solution)/shard_map/inner/pallas_call | solution.py:510
  54.8 1.2 collective-permute-start.2
  56.1 1.3 collective-permute-done.4
  57.6 1.6 %collective-permute-start.8 = (bf16[2,2,64,640]{3,2,1,0:T(8,128)(2,1)S(1)}, bf16[2,2,64,640]{3,2,1,0:T(8,128)(2,1)S(1)}, u32[]{:S(2)}, u32[]{:S(2)}) collective-permute-start(bf16[2,2,64,640]{3,2,1,0:T(8,128)(2,1)S(1)} %slice.78), channel_id=1, source_target_pairs={{0,2},{1,17},{2,0},{3,19},{4,6},{5,21},{6,4},{7,23},{8,10},{9,25},... | collective-permute-start | bytes 983048 | tf_op jit(solution)/shard_map/ppermute | solution.py:60
  60.5 1.6 %collective-permute-start.5 = (bf16[2,4,64,512]{3,2,1,0:T(8,128)(2,1)S(1)}, bf16[2,4,64,512]{3,2,1,0:T(8,128)(2,1)S(1)}, u32[]{:S(2)}, u32[]{:S(2)}) collective-permute-start(bf16[2,4,64,512]{3,2,1,0:T(8,128)(2,1)S(1)} %slice.76), channel_id=1, source_target_pairs={{0,16},{1,3},{2,18},{3,1},{4,20},{5,7},{6,22},{7,5},{8,24},{9,11},... | collective-permute-start | bytes 1572872 | tf_op jit(solution)/shard_map/ppermute | solution.py:60
  62.1 5.9 %taps.1 = f32[32,1024]{1,0:T(8,128)S(1)} custom-call(s32[2]{0:T(128)S(1)} %copy-done.9, f32[512,1024]{1,0:T(8,128)S(1)} %copy-done.17, f32[512,512]{1,0:T(8,128)S(1)} %get-tuple-element.138.refs_0_, f32[512,512]{1,0:T(8,128)S(1)} %get-tuple-element.139.refs_1_), custom_call_target="tpu_custom_call" | custom-call | flops 10350000128 | bytes 1048576 | tf_op jit(solution)/shard_map/taps/pallas_call | solution.py:592
  68.7 1.7 %collective-permute-start.10 = (bf16[2,1,64,640]{3,2,1,0:T(8,128)(2,1)S(1)}, bf16[2,1,64,640]{3,2,1,0:T(8,128)(2,1)S(1)}, u32[]{:S(2)}, u32[]{:S(2)}) collective-permute-start(bf16[2,1,64,640]{3,2,1,0:T(8,128)(2,1)S(1)} %slice.80), channel_id=1, source_target_pairs={{0,4},{1,9},{2,6},{3,11},{4,0},{5,13},{6,2},{7,15},{8,12},{9,1},{1... | collective-permute-start | bytes 491528 | tf_op jit(solution)/shard_map/ppermute | solution.py:60
  70.4 5.5 %collective-permute-done.7 = f32[32,1024]{1,0:T(8,128)S(1)} collective-permute-done((f32[32,1024]{1,0:T(8,128)S(1)}, f32[32,1024]{1,0:T(8,128)S(1)}, u32[]{:S(2)}, u32[]{:S(2)}) %collective-permute-start.7) | collective-permute-done | bytes 131104 | tf_op jit(solution)/shard_map/ppermute | solution.py:60
  75.9 1.3 collective-permute-start.11
  78.4 2.5 %collective-permute-done.11 = f32[32,1024]{1,0:T(8,128)S(1)} collective-permute-done((f32[32,1024]{1,0:T(8,128)S(1)}, f32[32,1024]{1,0:T(8,128)S(1)}, u32[]{:S(2)}, u32[]{:S(2)}) %collective-permute-start.11) | collective-permute-done | bytes 131104 | tf_op jit(solution)/shard_map/ppermute | solution.py:60
  80.9 1.6 %collective-permute-start.14 = (f32[32,1024]{1,0:T(8,128)S(1)}, f32[32,1024]{1,0:T(8,128)S(1)}, u32[]{:S(2)}, u32[]{:S(2)}) collective-permute-start(f32[32,1024]{1,0:T(8,128)S(1)} %add.84), channel_id=1, source_target_pairs={{0,4},{1,9},{2,6},{3,11},{4,0},{5,13},{6,2},{7,15},{8,12},{9,1},{1... | collective-permute-start | bytes 393224 | tf_op jit(solution)/shard_map/ppermute | solution.py:60
  82.6 1.3 collective-permute-start.15
  83.9 2.7 %collective-permute-start.13 = (bf16[2,1,64,640]{3,2,1,0:T(8,128)(2,1)S(1)}, bf16[2,1,64,640]{3,2,1,0:T(8,128)(2,1)S(1)}, u32[]{:S(2)}, u32[]{:S(2)}) collective-permute-start(bf16[2,1,64,640]{3,2,1,0:T(8,128)(2,1)S(1)} %add_convert_fusion.10), channel_id=1, source_target_pairs={{0,8},{1,5},{2,10},{3,7},{4,12},{5,1},{6,14},{7,3},{8,0},{9,13},{1... | collective-permute-start | bytes 491528 | tf_op jit(solution)/shard_map/ppermute | solution.py:60
  87.1 1.8 %collective-permute-done.15 = bf16[2,2,64,512]{3,2,1,0:T(8,128)(2,1)S(1)} collective-permute-done((bf16[2,2,64,512]{3,2,1,0:T(8,128)(2,1)S(1)}, bf16[2,2,64,512]{3,2,1,0:T(8,128)(2,1)S(1)}, u32[]{:S(2)}, u32[]{:S(2)}) %collective-permute-start.15) | collective-permute-done | bytes 262176 | tf_op jit(solution)/shard_map/ppermute | solution.py:60
  89.1 3.0 %collective-permute-start.17 = (f32[32,1024]{1,0:T(8,128)S(1)}, f32[32,1024]{1,0:T(8,128)S(1)}, u32[]{:S(2)}, u32[]{:S(2)}) collective-permute-start(f32[32,1024]{1,0:T(8,128)S(1)} %add.88), channel_id=1, source_target_pairs={{0,8},{1,5},{2,10},{3,7},{4,12},{5,1},{6,14},{7,3},{8,0},{9,13},{1... | collective-permute-start | bytes 393224 | tf_op jit(solution)/shard_map/ppermute | solution.py:60
  92.0 2.8 %collective-permute-done.13 = bf16[2,1,64,640]{3,2,1,0:T(8,128)(2,1)S(1)} collective-permute-done((bf16[2,1,64,640]{3,2,1,0:T(8,128)(2,1)S(1)}, bf16[2,1,64,640]{3,2,1,0:T(8,128)(2,1)S(1)}, u32[]{:S(2)}, u32[]{:S(2)}) %collective-permute-start.13) | collective-permute-done | bytes 163872 | tf_op jit(solution)/shard_map/ppermute | solution.py:60
  95.0 2.0 %collective-permute-start.18 = (bf16[2,1,64,512]{3,2,1,0:T(8,128)(2,1)S(1)}, bf16[2,1,64,512]{3,2,1,0:T(8,128)(2,1)S(1)}, u32[]{:S(2)}, u32[]{:S(2)}) collective-permute-start(bf16[2,1,64,512]{3,2,1,0:T(8,128)(2,1)S(1)} %slice.83), channel_id=1, source_target_pairs={{0,4},{1,9},{2,6},{3,11},{4,0},{5,13},{6,2},{7,15},{8,12},{9,1},{1... | collective-permute-start | bytes 393224 | tf_op jit(solution)/shard_map/ppermute | solution.py:60
  97.0 2.4 %collective-permute-start.22 = (bf16[2,1,64,512]{3,2,1,0:T(8,128)(2,1)S(1)}, bf16[2,1,64,512]{3,2,1,0:T(8,128)(2,1)S(1)}, u32[]{:S(2)}, u32[]{:S(2)}) collective-permute-start(bf16[2,1,64,512]{3,2,1,0:T(8,128)(2,1)S(1)} %add_convert_fusion.14), channel_id=1, source_target_pairs={{0,8},{1,5},{2,10},{3,7},{4,12},{5,1},{6,14},{7,3},{8,0},{9,13},{1... | collective-permute-start | bytes 393224 | tf_op jit(solution)/shard_map/ppermute | solution.py:60
  99.4 7.8 %collective-permute-done.18 = bf16[2,1,64,512]{3,2,1,0:T(8,128)(2,1)S(1)} collective-permute-done((bf16[2,1,64,512]{3,2,1,0:T(8,128)(2,1)S(1)}, bf16[2,1,64,512]{3,2,1,0:T(8,128)(2,1)S(1)}, u32[]{:S(2)}, u32[]{:S(2)}) %collective-permute-start.18) | collective-permute-done | bytes 131104 | tf_op jit(solution)/shard_map/ppermute | solution.py:60
  107.4 1.6 %collective-permute-start.19 = (bf16[2,2,64,640]{3,2,1,0:T(8,128)(2,1)S(1)}, bf16[2,2,64,640]{3,2,1,0:T(8,128)(2,1)S(1)}, u32[]{:S(2)}, u32[]{:S(2)}) collective-permute-start(bf16[2,2,64,640]{3,2,1,0:T(8,128)(2,1)S(1)} %constant_dynamic-update-slice_fusion), channel_id=1, source_target_pairs={{0,2},{1,17},{2,0},{3,19},{4,6},{5,21},{6,4},{7,23},{8,10},{9,25},... | collective-permute-start | bytes 983048 | tf_op jit(solution)/shard_map/ppermute | solution.py:60
  109.1 5.4 %collective-permute-done.21 = bf16[2,1,64,512]{3,2,1,0:T(8,128)(2,1)S(1)} collective-permute-done((bf16[2,1,64,512]{3,2,1,0:T(8,128)(2,1)S(1)}, bf16[2,1,64,512]{3,2,1,0:T(8,128)(2,1)S(1)}, u32[]{:S(2)}, u32[]{:S(2)}) %collective-permute-start.21) | collective-permute-done | bytes 131104 | tf_op jit(solution)/shard_map/ppermute | solution.py:60
  114.6 2.1 %collective-permute-start.24 = (bf16[2,4,64,640]{3,2,1,0:T(8,128)(2,1)S(1)}, bf16[2,4,64,640]{3,2,1,0:T(8,128)(2,1)S(1)}, u32[]{:S(2)}, u32[]{:S(2)}) collective-permute-start(bf16[2,4,64,640]{3,2,1,0:T(8,128)(2,1)S(1)} %constant_dynamic-update-slice_fusion.2), channel_id=1, source_target_pairs={{0,16},{1,3},{2,18},{3,1},{4,20},{5,7},{6,22},{7,5},{8,24},{9,11},... | collective-permute-start | bytes 1966088 | tf_op jit(solution)/shard_map/ppermute | solution.py:60
  116.8 2.4 %collective-permute-start.23 = (bf16[2,1,64,512]{3,2,1,0:T(8,128)(2,1)S(1)}, bf16[2,1,64,512]{3,2,1,0:T(8,128)(2,1)S(1)}, u32[]{:S(2)}, u32[]{:S(2)}) collective-permute-start(bf16[2,1,64,512]{3,2,1,0:T(8,128)(2,1)S(1)} %add_convert_fusion.12), channel_id=1, source_target_pairs={{0,4},{1,9},{2,6},{3,11},{4,0},{5,13},{6,2},{7,15},{8,12},{9,1},{1... | collective-permute-start | bytes 393224 | tf_op jit(solution)/shard_map/ppermute | solution.py:60
  119.3 4.3 %collective-permute-done.23 = bf16[2,1,64,512]{3,2,1,0:T(8,128)(2,1)S(1)} collective-permute-done((bf16[2,1,64,512]{3,2,1,0:T(8,128)(2,1)S(1)}, bf16[2,1,64,512]{3,2,1,0:T(8,128)(2,1)S(1)}, u32[]{:S(2)}, u32[]{:S(2)}) %collective-permute-start.23) | collective-permute-done | bytes 131104 | tf_op jit(solution)/shard_map/ppermute | solution.py:60
  123.6 1.4 collective-permute-done.25
  125.5 1.5 collective-permute-start.28
  127.6 4.3 %collective-permute-done.28 = bf16[2,2,64,512]{3,2,1,0:T(8,128)(2,1)S(1)} collective-permute-done((bf16[2,2,64,512]{3,2,1,0:T(8,128)(2,1)S(1)}, bf16[2,2,64,512]{3,2,1,0:T(8,128)(2,1)S(1)}, u32[]{:S(2)}, u32[]{:S(2)}) %collective-permute-start.28) | collective-permute-done | bytes 262176 | tf_op jit(solution)/shard_map/ppermute | solution.py:60
  132.0 2.1 %collective-permute-start.30 = (bf16[2,4,64,512]{3,2,1,0:T(8,128)(2,1)S(1)}, bf16[2,4,64,512]{3,2,1,0:T(8,128)(2,1)S(1)}, u32[]{:S(2)}, u32[]{:S(2)}) collective-permute-start(bf16[2,4,64,512]{3,2,1,0:T(8,128)(2,1)S(1)} %constant_dynamic-update-slice_fusion.10), channel_id=1, source_target_pairs={{0,16},{1,3},{2,18},{3,1},{4,20},{5,7},{6,22},{7,5},{8,24},{9,11},... | collective-permute-start | bytes 1572872 | tf_op jit(solution)/shard_map/ppermute | solution.py:60
  135.0 2.4 %collective-permute-start.29 = (bf16[2,4,64,512]{3,2,1,0:T(8,128)(2,1)S(1)}, bf16[2,4,64,512]{3,2,1,0:T(8,128)(2,1)S(1)}, u32[]{:S(2)}, u32[]{:S(2)}) collective-permute-start(bf16[2,4,64,512]{3,2,1,0:T(8,128)(2,1)S(1)} %constant_dynamic-update-slice_fusion.12), channel_id=1, source_target_pairs={{0,16},{1,3},{2,18},{3,1},{4,20},{5,7},{6,22},{7,5},{8,24},{9,11},... | collective-permute-start | bytes 1572872 | tf_op jit(solution)/shard_map/ppermute | solution.py:60
  137.4 3.5 %unpack_top.1 = (f32[1024,1024]{1,0:T(8,128)}, f32[1024,256]{1,0:T(8,128)}, f32[1,1024]{1,0:T(1,128)}, f32[31,1024]{1,0:T(8,128)}, f32[2,1,128]{2,1,0:T(1,128)S(1)}) custom-call(s32[3]{0:T(128)S(1)} %pad_add_fusion.own_ref, f32[32,1024]{1,0:T(8,128)S(1)} %add.95.small_ref, bf16[2,8,64,640]{3,2,1,0:T(8,128)(2,1)S(1)} %constant_dynamic-update-slice_fusion.8.mine_ref, ...), custom_call_target="tpu_custom_call" | custom-call | flops 5750000128 | bytes 1048576 | tf_op jit(solution)/shard_map/unpack_top/pallas_call | solution.py:681
  141.4 5.4 %collective-permute-done.29 = bf16[2,4,64,512]{3,2,1,0:T(8,128)(2,1)S(1)} collective-permute-done((bf16[2,4,64,512]{3,2,1,0:T(8,128)(2,1)S(1)}, bf16[2,4,64,512]{3,2,1,0:T(8,128)(2,1)S(1)}, u32[]{:S(2)}, u32[]{:S(2)}) %collective-permute-start.29) | collective-permute-done | bytes 524320 | tf_op jit(solution)/shard_map/ppermute | solution.py:60
  147.6 2.0 %collective-permute-done.31.refs_3_ = bf16[2,8,64,512]{3,2,1,0:T(8,128)(2,1)S(1)} collective-permute-done((bf16[2,8,64,512]{3,2,1,0:T(8,128)(2,1)S(1)}, bf16[2,8,64,512]{3,2,1,0:T(8,128)(2,1)S(1)}, u32[]{:S(2)}, u32[]{:S(2)}) %collective-permute-start.31) | collective-permute-done | bytes 1048608 | tf_op jit(solution)/shard_map/ppermute | solution.py:54
  149.6 4.4 %unpack_inner.1 = (f32[1024,2048]{1,0:T(8,128)}, f32[1,1024]{1,0:T(1,128)}) custom-call(s32[3]{0:T(128)S(1)} %pad_add_fusion.own_ref, f32[32,1024]{1,0:T(8,128)S(1)} %add.95.small_ref, bf16[1024,2048]{1,0:T(8,128)(2,1)S(1)} %copy-done.1, f32[1,1024]{1,0:T(1,128)S(1)} %bitcast.13, bf16[2,8,64,512]{3,2,1,0:T(8,128)(2,1)S(1)} %constant_dynamic-update-slice_fusion.14.refs_0_, ...), custom_call_target="tpu_custom_call" | custom-call | flops 9200000000 | bytes 1048576 | tf_op jit(solution)/shard_map/unpack_inner/pallas_call | solution.py:734
  (124 shorter events, 10.4 us)
Async XLA Ops:
  1.9 6.1 %copy-start = (bf16[1024,2048]{1,0:T(8,128)(2,1)S(1)}, bf16[1024,2048]{1,0:T(8,128)(2,1)}, u32[]{:S(2)}) copy-start(bf16[1024,2048]{1,0:T(8,128)(2,1)} %weight_ref.1) | copy-start | bytes 12582916
  1.9 6.1 %copy-start.2 = (bf16[1024,1024]{1,0:T(8,128)(2,1)S(1)}, bf16[1024,1024]{1,0:T(8,128)(2,1)}, u32[]{:S(2)}) copy-start(bf16[1024,1024]{1,0:T(8,128)(2,1)} %out_weight_ref.5) | copy-start | bytes 6291460
  1.9 6.1 %copy-start.4 = (bf16[2,256,1024]{2,1,0:T(8,128)(2,1)S(1)}, bf16[2,256,1024]{2,1,0:T(8,128)(2,1)}, u32[]{:S(2)}) copy-start(bf16[2,256,1024]{2,1,0:T(8,128)(2,1)} %param.9) | copy-start | bytes 3145732
  1.9 6.1 %copy-start.6 = (f32[31,1024]{1,0:T(8,128)S(1)}, f32[31,1024]{1,0:T(8,128)}, u32[]{:S(2)}) copy-start(f32[31,1024]{1,0:T(8,128)} %depth_ref.5) | copy-start | bytes 380932
  1.9 6.1 %copy-start.8 = (f32[1024]{0:T(1024)S(1)}, f32[1024]{0:T(1024)}, u32[]{:S(2)}) copy-start(f32[1024]{0:T(1024)} %param.12) | copy-start | bytes 12292
  1.9 6.1 %copy-start.9 = (s32[2]{0:T(128)S(1)}, s32[2]{0:T(128)}, u32[]{:S(2)}) copy-start(s32[2]{0:T(128)} %lengths_ref.9) | copy-start | bytes 28
  5.0 23.3 %collective-permute-start = (f32[2,256,256]{2,1,0:T(8,128)}, f32[2,256,256]{2,1,0:T(8,128)S(1)}, u32[]{:S(2)}, u32[]{:S(2)}) collective-permute-start(f32[2,256,256]{2,1,0:T(8,128)} %get-tuple-element.110), channel_id=1, source_target_pairs={{0,16},{16,0},{1,17},{17,1},{2,18},{18,2},{3,19},{19,3},{4,20},{20... | collective-permute-start | bytes 1572872 | tf_op jit(solution)/shard_map/ppermute | solution.py:54
  8.0 20.4 %copy-start.5 = (bf16[1024,256]{1,0:T(8,128)(2,1)S(1)}, bf16[1024,256]{1,0:T(8,128)(2,1)}, u32[]{:S(2)}) copy-start(bf16[1024,256]{1,0:T(8,128)(2,1)} %head_ref.3) | copy-start | bytes 1572868
  8.0 20.4 %copy-start.7 = (f32[1024]{0:T(1024)S(1)}, f32[1024]{0:T(1024)}, u32[]{:S(2)}) copy-start(f32[1024]{0:T(1024)} %param.16) | copy-start | bytes 12292
  28.4 1.6 %copy-start.11 = (f32[512,1024]{1,0:T(8,128)S(1)}, f32[512,1024]{1,0:T(8,128)}, u32[]{:S(2)}) copy-start(f32[512,1024]{1,0:T(8,128)} %copy-done.10) | copy-start | bytes 6291460
  31.0 3.4 %copy-start.13 = (bf16[512,1024]{1,0:T(8,128)(2,1)S(1)}, bf16[512,1024]{1,0:T(8,128)(2,1)}, u32[]{:S(2)}) copy-start(bf16[512,1024]{1,0:T(8,128)(2,1)} %copy-done.12) | copy-start | bytes 3145732
  34.4 3.3 %copy-start.17 = (f32[512,1024]{1,0:T(8,128)S(1)}, f32[512,1024]{1,0:T(8,128)}, u32[]{:S(2)}) copy-start(f32[512,1024]{1,0:T(8,128)} %copy-done.16) | copy-start | bytes 6291460
  34.4 3.3 %copy-start.19 = (f32[512,1024]{1,0:T(8,128)S(1)}, f32[512,1024]{1,0:T(8,128)}, u32[]{:S(2)}) copy-start(f32[512,1024]{1,0:T(8,128)} %copy-done.18) | copy-start | bytes 6291460
  34.5 3.3 %copy-start.21 = (f32[512,1024]{1,0:T(8,128)S(1)}, f32[512,1024]{1,0:T(8,128)}, u32[]{:S(2)}) copy-start(f32[512,1024]{1,0:T(8,128)} %copy-done.20) | copy-start | bytes 6291460
  34.5 3.3 %copy-start.23 = (bf16[1024,512]{1,0:T(8,128)(2,1)S(1)}, bf16[1024,512]{1,0:T(8,128)(2,1)}, u32[]{:S(2)}) copy-start(bf16[1024,512]{1,0:T(8,128)(2,1)} %copy-done.22) | copy-start | bytes 3145732
  37.6 8.6 %collective-permute-start.1 = (bf16[2,8,64,640]{3,2,1,0:T(8,128)(2,1)S(1)}, bf16[2,8,64,640]{3,2,1,0:T(8,128)(2,1)S(1)}, u32[]{:S(2)}, u32[]{:S(2)}) collective-permute-start(bf16[2,8,64,640]{3,2,1,0:T(8,128)(2,1)S(1)} %get-tuple-element.118), channel_id=1, source_target_pairs={{0,1},{1,0},{2,3},{3,2},{4,5},{5,4},{6,7},{7,6},{8,9},{9,8},{10,11... | collective-permute-start | bytes 3932168 | tf_op jit(solution)/shard_map/ppermute | solution.py:54
  45.7 13.5 %collective-permute-start.3 = (bf16[2,8,64,512]{3,2,1,0:T(8,128)(2,1)S(1)}, bf16[2,8,64,512]{3,2,1,0:T(8,128)(2,1)S(1)}, u32[]{:S(2)}, u32[]{:S(2)}) collective-permute-start(bf16[2,8,64,512]{3,2,1,0:T(8,128)(2,1)S(1)} %get-tuple-element.129), channel_id=1, source_target_pairs={{0,1},{1,0},{2,3},{3,2},{4,5},{5,4},{6,7},{7,6},{8,9},{9,8},{10,11... | collective-permute-start | bytes 3145736 | tf_op jit(solution)/shard_map/ppermute | solution.py:54
  46.7 10.7 %collective-permute-start.4 = (bf16[2,4,64,640]{3,2,1,0:T(8,128)(2,1)S(1)}, bf16[2,4,64,640]{3,2,1,0:T(8,128)(2,1)S(1)}, u32[]{:S(2)}, u32[]{:S(2)}) collective-permute-start(bf16[2,4,64,640]{3,2,1,0:T(8,128)(2,1)S(1)} %slice.58), channel_id=1, source_target_pairs={{0,16},{1,3},{2,18},{3,1},{4,20},{5,7},{6,22},{7,5},{8,24},{9,11},... | collective-permute-start | bytes 1966088 | tf_op jit(solution)/shard_map/ppermute | solution.py:60
  54.8 5.3 %collective-permute-start.2 = (bf16[2,8,64,512]{3,2,1,0:T(8,128)(2,1)S(1)}, bf16[2,8,64,512]{3,2,1,0:T(8,128)(2,1)S(1)}, u32[]{:S(2)}, u32[]{:S(2)}) collective-permute-start(bf16[2,8,64,512]{3,2,1,0:T(8,128)(2,1)S(1)} %get-tuple-element.127), channel_id=1, source_target_pairs={{0,1},{1,0},{2,3},{3,2},{4,5},{5,4},{6,7},{7,6},{8,9},{9,8},{10,11... | collective-permute-start | bytes 3145736 | tf_op jit(solution)/shard_map/ppermute | solution.py:54
  57.6 11.0 %collective-permute-start.8 = (bf16[2,2,64,640]{3,2,1,0:T(8,128)(2,1)S(1)}, bf16[2,2,64,640]{3,2,1,0:T(8,128)(2,1)S(1)}, u32[]{:S(2)}, u32[]{:S(2)}) collective-permute-start(bf16[2,2,64,640]{3,2,1,0:T(8,128)(2,1)S(1)} %slice.78), channel_id=1, source_target_pairs={{0,2},{1,17},{2,0},{3,19},{4,6},{5,21},{6,4},{7,23},{8,10},{9,25},... | collective-permute-start | bytes 983048 | tf_op jit(solution)/shard_map/ppermute | solution.py:60
  59.6 17.6 %collective-permute-start.6 = (bf16[2,4,64,512]{3,2,1,0:T(8,128)(2,1)S(1)}, bf16[2,4,64,512]{3,2,1,0:T(8,128)(2,1)S(1)}, u32[]{:S(2)}, u32[]{:S(2)}) collective-permute-start(bf16[2,4,64,512]{3,2,1,0:T(8,128)(2,1)S(1)} %slice.77), channel_id=1, source_target_pairs={{0,16},{1,3},{2,18},{3,1},{4,20},{5,7},{6,22},{7,5},{8,24},{9,11},... | collective-permute-start | bytes 1572872 | tf_op jit(solution)/shard_map/ppermute | solution.py:60
  60.5 17.7 %collective-permute-start.5 = (bf16[2,4,64,512]{3,2,1,0:T(8,128)(2,1)S(1)}, bf16[2,4,64,512]{3,2,1,0:T(8,128)(2,1)S(1)}, u32[]{:S(2)}, u32[]{:S(2)}) collective-permute-start(bf16[2,4,64,512]{3,2,1,0:T(8,128)(2,1)S(1)} %slice.76), channel_id=1, source_target_pairs={{0,16},{1,3},{2,18},{3,1},{4,20},{5,7},{6,22},{7,5},{8,24},{9,11},... | collective-permute-start | bytes 1572872 | tf_op jit(solution)/shard_map/ppermute | solution.py:60
  68.0 7.8 %collective-permute-start.7 = (f32[32,1024]{1,0:T(8,128)S(1)}, f32[32,1024]{1,0:T(8,128)S(1)}, u32[]{:S(2)}, u32[]{:S(2)}) collective-permute-start(f32[32,1024]{1,0:T(8,128)S(1)} %taps.1), channel_id=1, source_target_pairs={{0,16},{1,3},{2,18},{3,1},{4,20},{5,7},{6,22},{7,5},{8,24},{9,11},... | collective-permute-start | bytes 393224 | tf_op jit(solution)/shard_map/ppermute | solution.py:60
  68.7 13.8 %collective-permute-start.10 = (bf16[2,1,64,640]{3,2,1,0:T(8,128)(2,1)S(1)}, bf16[2,1,64,640]{3,2,1,0:T(8,128)(2,1)S(1)}, u32[]{:S(2)}, u32[]{:S(2)}) collective-permute-start(bf16[2,1,64,640]{3,2,1,0:T(8,128)(2,1)S(1)} %slice.80), channel_id=1, source_target_pairs={{0,4},{1,9},{2,6},{3,11},{4,0},{5,13},{6,2},{7,15},{8,12},{9,1},{1... | collective-permute-start | bytes 491528 | tf_op jit(solution)/shard_map/ppermute | solution.py:60
  75.9 5.0 %collective-permute-start.11 = (f32[32,1024]{1,0:T(8,128)S(1)}, f32[32,1024]{1,0:T(8,128)S(1)}, u32[]{:S(2)}, u32[]{:S(2)}) collective-permute-start(f32[32,1024]{1,0:T(8,128)S(1)} %add.81), channel_id=1, source_target_pairs={{0,2},{1,17},{2,0},{3,19},{4,6},{5,21},{6,4},{7,23},{8,10},{9,25},... | collective-permute-start | bytes 393224 | tf_op jit(solution)/shard_map/ppermute | solution.py:60
  77.4 9.2 %collective-permute-start.9 = (bf16[2,2,64,512]{3,2,1,0:T(8,128)(2,1)S(1)}, bf16[2,2,64,512]{3,2,1,0:T(8,128)(2,1)S(1)}, u32[]{:S(2)}, u32[]{:S(2)}) collective-permute-start(bf16[2,2,64,512]{3,2,1,0:T(8,128)(2,1)S(1)} %slice.79), channel_id=1, source_target_pairs={{0,2},{1,17},{2,0},{3,19},{4,6},{5,21},{6,4},{7,23},{8,10},{9,25},... | collective-permute-start | bytes 786440 | tf_op jit(solution)/shard_map/ppermute | solution.py:60
  80.9 8.1 %collective-permute-start.14 = (f32[32,1024]{1,0:T(8,128)S(1)}, f32[32,1024]{1,0:T(8,128)S(1)}, u32[]{:S(2)}, u32[]{:S(2)}) collective-permute-start(f32[32,1024]{1,0:T(8,128)S(1)} %add.84), channel_id=1, source_target_pairs={{0,4},{1,9},{2,6},{3,11},{4,0},{5,13},{6,2},{7,15},{8,12},{9,1},{1... | collective-permute-start | bytes 393224 | tf_op jit(solution)/shard_map/ppermute | solution.py:60
  82.6 6.4 %collective-permute-start.15 = (bf16[2,2,64,512]{3,2,1,0:T(8,128)(2,1)S(1)}, bf16[2,2,64,512]{3,2,1,0:T(8,128)(2,1)S(1)}, u32[]{:S(2)}, u32[]{:S(2)}) collective-permute-start(bf16[2,2,64,512]{3,2,1,0:T(8,128)(2,1)S(1)} %slice.82), channel_id=1, source_target_pairs={{0,2},{1,17},{2,0},{3,19},{4,6},{5,21},{6,4},{7,23},{8,10},{9,25},... | collective-permute-start | bytes 786440 | tf_op jit(solution)/shard_map/ppermute | solution.py:60
  83.9 11.0 %collective-permute-start.13 = (bf16[2,1,64,640]{3,2,1,0:T(8,128)(2,1)S(1)}, bf16[2,1,64,640]{3,2,1,0:T(8,128)(2,1)S(1)}, u32[]{:S(2)}, u32[]{:S(2)}) collective-permute-start(bf16[2,1,64,640]{3,2,1,0:T(8,128)(2,1)S(1)} %add_convert_fusion.10), channel_id=1, source_target_pairs={{0,8},{1,5},{2,10},{3,7},{4,12},{5,1},{6,14},{7,3},{8,0},{9,13},{1... | collective-permute-start | bytes 491528 | tf_op jit(solution)/shard_map/ppermute | solution.py:60
  86.6 8.3 %collective-permute-start.12 = (bf16[2,1,64,512]{3,2,1,0:T(8,128)(2,1)S(1)}, bf16[2,1,64,512]{3,2,1,0:T(8,128)(2,1)S(1)}, u32[]{:S(2)}, u32[]{:S(2)}) collective-permute-start(bf16[2,1,64,512]{3,2,1,0:T(8,128)(2,1)S(1)} %slice.81), channel_id=1, source_target_pairs={{0,4},{1,9},{2,6},{3,11},{4,0},{5,13},{6,2},{7,15},{8,12},{9,1},{1... | collective-permute-start | bytes 393224 | tf_op jit(solution)/shard_map/ppermute | solution.py:60
  89.1 18.2 %collective-permute-start.17 = (f32[32,1024]{1,0:T(8,128)S(1)}, f32[32,1024]{1,0:T(8,128)S(1)}, u32[]{:S(2)}, u32[]{:S(2)}) collective-permute-start(f32[32,1024]{1,0:T(8,128)S(1)} %add.88), channel_id=1, source_target_pairs={{0,8},{1,5},{2,10},{3,7},{4,12},{5,1},{6,14},{7,3},{8,0},{9,13},{1... | collective-permute-start | bytes 393224 | tf_op jit(solution)/shard_map/ppermute | solution.py:60
  94.9 12.5 %collective-permute-start.16 = (bf16[2,1,64,640]{3,2,1,0:T(8,128)(2,1)S(1)}, bf16[2,1,64,640]{3,2,1,0:T(8,128)(2,1)S(1)}, u32[]{:S(2)}, u32[]{:S(2)}) collective-permute-start(bf16[2,1,64,640]{3,2,1,0:T(8,128)(2,1)S(1)} %add_convert_fusion.9), channel_id=1, source_target_pairs={{0,4},{1,9},{2,6},{3,11},{4,0},{5,13},{6,2},{7,15},{8,12},{9,1},{1... | collective-permute-start | bytes 491528 | tf_op jit(solution)/shard_map/ppermute | solution.py:60
  95.0 12.2 %collective-permute-start.18 = (bf16[2,1,64,512]{3,2,1,0:T(8,128)(2,1)S(1)}, bf16[2,1,64,512]{3,2,1,0:T(8,128)(2,1)S(1)}, u32[]{:S(2)}, u32[]{:S(2)}) collective-permute-start(bf16[2,1,64,512]{3,2,1,0:T(8,128)(2,1)S(1)} %slice.83), channel_id=1, source_target_pairs={{0,4},{1,9},{2,6},{3,11},{4,0},{5,13},{6,2},{7,15},{8,12},{9,1},{1... | collective-permute-start | bytes 393224 | tf_op jit(solution)/shard_map/ppermute | solution.py:60
  97.0 12.0 %collective-permute-start.22 = (bf16[2,1,64,512]{3,2,1,0:T(8,128)(2,1)S(1)}, bf16[2,1,64,512]{3,2,1,0:T(8,128)(2,1)S(1)}, u32[]{:S(2)}, u32[]{:S(2)}) collective-permute-start(bf16[2,1,64,512]{3,2,1,0:T(8,128)(2,1)S(1)} %add_convert_fusion.14), channel_id=1, source_target_pairs={{0,8},{1,5},{2,10},{3,7},{4,12},{5,1},{6,14},{7,3},{8,0},{9,13},{1... | collective-permute-start | bytes 393224 | tf_op jit(solution)/shard_map/ppermute | solution.py:60
  107.2 7.3 %collective-permute-start.21 = (bf16[2,1,64,512]{3,2,1,0:T(8,128)(2,1)S(1)}, bf16[2,1,64,512]{3,2,1,0:T(8,128)(2,1)S(1)}, u32[]{:S(2)}, u32[]{:S(2)}) collective-permute-start(bf16[2,1,64,512]{3,2,1,0:T(8,128)(2,1)S(1)} %add_convert_fusion.13), channel_id=1, source_target_pairs={{0,8},{1,5},{2,10},{3,7},{4,12},{5,1},{6,14},{7,3},{8,0},{9,13},{1... | collective-permute-start | bytes 393224 | tf_op jit(solution)/shard_map/ppermute | solution.py:60
  107.3 7.2 %collective-permute-start.20 = (f32[32,1024]{1,0:T(8,128)S(1)}, f32[32,1024]{1,0:T(8,128)S(1)}, u32[]{:S(2)}, u32[]{:S(2)}) collective-permute-start(f32[32,1024]{1,0:T(8,128)S(1)} %add.92), channel_id=1, source_target_pairs={{0,1},{1,0},{2,3},{3,2},{4,5},{5,4},{6,7},{7,6},{8,9},{9,8},{10,11... | collective-permute-start | bytes 393224 | tf_op jit(solution)/shard_map/ppermute | solution.py:54
  107.4 7.1 %collective-permute-start.19 = (bf16[2,2,64,640]{3,2,1,0:T(8,128)(2,1)S(1)}, bf16[2,2,64,640]{3,2,1,0:T(8,128)(2,1)S(1)}, u32[]{:S(2)}, u32[]{:S(2)}) collective-permute-start(bf16[2,2,64,640]{3,2,1,0:T(8,128)(2,1)S(1)} %constant_dynamic-update-slice_fusion), channel_id=1, source_target_pairs={{0,2},{1,17},{2,0},{3,19},{4,6},{5,21},{6,4},{7,23},{8,10},{9,25},... | collective-permute-start | bytes 983048 | tf_op jit(solution)/shard_map/ppermute | solution.py:60
  114.6 10.7 %collective-permute-start.24 = (bf16[2,4,64,640]{3,2,1,0:T(8,128)(2,1)S(1)}, bf16[2,4,64,640]{3,2,1,0:T(8,128)(2,1)S(1)}, u32[]{:S(2)}, u32[]{:S(2)}) collective-permute-start(bf16[2,4,64,640]{3,2,1,0:T(8,128)(2,1)S(1)} %constant_dynamic-update-slice_fusion.2), channel_id=1, source_target_pairs={{0,16},{1,3},{2,18},{3,1},{4,20},{5,7},{6,22},{7,5},{8,24},{9,11},... | collective-permute-start | bytes 1966088 | tf_op jit(solution)/shard_map/ppermute | solution.py:60
  116.8 6.8 %collective-permute-start.23 = (bf16[2,1,64,512]{3,2,1,0:T(8,128)(2,1)S(1)}, bf16[2,1,64,512]{3,2,1,0:T(8,128)(2,1)S(1)}, u32[]{:S(2)}, u32[]{:S(2)}) collective-permute-start(bf16[2,1,64,512]{3,2,1,0:T(8,128)(2,1)S(1)} %add_convert_fusion.12), channel_id=1, source_target_pairs={{0,4},{1,9},{2,6},{3,11},{4,0},{5,13},{6,2},{7,15},{8,12},{9,1},{1... | collective-permute-start | bytes 393224 | tf_op jit(solution)/shard_map/ppermute | solution.py:60
  119.2 5.8 %collective-permute-start.25 = (bf16[2,1,64,512]{3,2,1,0:T(8,128)(2,1)S(1)}, bf16[2,1,64,512]{3,2,1,0:T(8,128)(2,1)S(1)}, u32[]{:S(2)}, u32[]{:S(2)}) collective-permute-start(bf16[2,1,64,512]{3,2,1,0:T(8,128)(2,1)S(1)} %add_convert_fusion.11), channel_id=1, source_target_pairs={{0,4},{1,9},{2,6},{3,11},{4,0},{5,13},{6,2},{7,15},{8,12},{9,1},{1... | collective-permute-start | bytes 393224 | tf_op jit(solution)/shard_map/ppermute | solution.py:60
  125.4 12.0 %collective-permute-start.26 = (bf16[2,8,64,640]{3,2,1,0:T(8,128)(2,1)S(1)}, bf16[2,8,64,640]{3,2,1,0:T(8,128)(2,1)S(1)}, u32[]{:S(2)}, u32[]{:S(2)}) collective-permute-start(bf16[2,8,64,640]{3,2,1,0:T(8,128)(2,1)S(1)} %constant_dynamic-update-slice_fusion.8.mine_ref), channel_id=1, source_target_pairs={{0,1},{1,0},{2,3},{3,2},{4,5},{5,4},{6,7},{7,6},{8,9},{9,8},{10,11... | collective-permute-start | bytes 3932168 | tf_op jit(solution)/shard_map/ppermute | solution.py:54
  125.5 6.4 %collective-permute-start.28 = (bf16[2,2,64,512]{3,2,1,0:T(8,128)(2,1)S(1)}, bf16[2,2,64,512]{3,2,1,0:T(8,128)(2,1)S(1)}, u32[]{:S(2)}, u32[]{:S(2)}) collective-permute-start(bf16[2,2,64,512]{3,2,1,0:T(8,128)(2,1)S(1)} %constant_dynamic-update-slice_fusion.4), channel_id=1, source_target_pairs={{0,2},{1,17},{2,0},{3,19},{4,6},{5,21},{6,4},{7,23},{8,10},{9,25},... | collective-permute-start | bytes 786440 | tf_op jit(solution)/shard_map/ppermute | solution.py:60
  127.0 8.0 %collective-permute-start.27 = (bf16[2,2,64,512]{3,2,1,0:T(8,128)(2,1)S(1)}, bf16[2,2,64,512]{3,2,1,0:T(8,128)(2,1)S(1)}, u32[]{:S(2)}, u32[]{:S(2)}) collective-permute-start(bf16[2,2,64,512]{3,2,1,0:T(8,128)(2,1)S(1)} %constant_dynamic-update-slice_fusion.6), channel_id=1, source_target_pairs={{0,2},{1,17},{2,0},{3,19},{4,6},{5,21},{6,4},{7,23},{8,10},{9,25},... | collective-permute-start | bytes 786440 | tf_op jit(solution)/shard_map/ppermute | solution.py:60
  132.0 9.2 %collective-permute-start.30 = (bf16[2,4,64,512]{3,2,1,0:T(8,128)(2,1)S(1)}, bf16[2,4,64,512]{3,2,1,0:T(8,128)(2,1)S(1)}, u32[]{:S(2)}, u32[]{:S(2)}) collective-permute-start(bf16[2,4,64,512]{3,2,1,0:T(8,128)(2,1)S(1)} %constant_dynamic-update-slice_fusion.10), channel_id=1, source_target_pairs={{0,16},{1,3},{2,18},{3,1},{4,20},{5,7},{6,22},{7,5},{8,24},{9,11},... | collective-permute-start | bytes 1572872 | tf_op jit(solution)/shard_map/ppermute | solution.py:60
  135.0 11.8 %collective-permute-start.29 = (bf16[2,4,64,512]{3,2,1,0:T(8,128)(2,1)S(1)}, bf16[2,4,64,512]{3,2,1,0:T(8,128)(2,1)S(1)}, u32[]{:S(2)}, u32[]{:S(2)}) collective-permute-start(bf16[2,4,64,512]{3,2,1,0:T(8,128)(2,1)S(1)} %constant_dynamic-update-slice_fusion.12), channel_id=1, source_target_pairs={{0,16},{1,3},{2,18},{3,1},{4,20},{5,7},{6,22},{7,5},{8,24},{9,11},... | collective-permute-start | bytes 1572872 | tf_op jit(solution)/shard_map/ppermute | solution.py:60
  137.4 12.2 %copy-start.1 = (bf16[1024,2048]{1,0:T(8,128)(2,1)S(1)}, bf16[1024,2048]{1,0:T(8,128)(2,1)}, u32[]{:S(2)}) copy-start(bf16[1024,2048]{1,0:T(8,128)(2,1)} %weight_ref.1) | copy-start | bytes 12582916
  141.3 6.3 %collective-permute-start.32 = (bf16[2,8,64,512]{3,2,1,0:T(8,128)(2,1)S(1)}, bf16[2,8,64,512]{3,2,1,0:T(8,128)(2,1)S(1)}, u32[]{:S(2)}, u32[]{:S(2)}) collective-permute-start(bf16[2,8,64,512]{3,2,1,0:T(8,128)(2,1)S(1)} %constant_dynamic-update-slice_fusion.14.refs_0_), channel_id=1, source_target_pairs={{0,1},{1,0},{2,3},{3,2},{4,5},{5,4},{6,7},{7,6},{8,9},{9,8},{10,11... | collective-permute-start | bytes 3145736 | tf_op jit(solution)/shard_map/ppermute | solution.py:54
  146.9 2.7 %collective-permute-start.31 = (bf16[2,8,64,512]{3,2,1,0:T(8,128)(2,1)S(1)}, bf16[2,8,64,512]{3,2,1,0:T(8,128)(2,1)S(1)}, u32[]{:S(2)}, u32[]{:S(2)}) collective-permute-start(bf16[2,8,64,512]{3,2,1,0:T(8,128)(2,1)S(1)} %constant_dynamic-update-slice_fusion.16.refs_2_), channel_id=1, source_target_pairs={{0,1},{1,0},{2,3},{3,2},{4,5},{5,4},{6,7},{7,6},{8,9},{9,8},{10,11... | collective-permute-start | bytes 3145736 | tf_op jit(solution)/shard_map/ppermute | solution.py:54
  (9 other events, 10.4 us)

commit v10 on v9

--- a/solution.py
+++ b/solution.py
@@ -15,8 +15,8 @@
 MARGIN = 16
 CHUNKS = 2
 ORDER = (
-    "top", "in0", "in1", "taps", "top", "small", "in0", "in1", "small", "top", "in0", "in1",
-    "small", "top", "in0", "in1", "small", "top", "in0", "in1", "small", "top", "in0", "in1",
+    "top", "in0", "in1", "taps", "top", "in0", "in1", "small", "top", "in0", "in1", "small",
+    "top", "in0", "in1", "small", "top", "in0", "in1", "small", "top", "in0", "in1", "small",
     "top", "in0", "in1", "top", "write_top", "in0", "in1", "in0", "in1", "write_in",
 )
 SMEM_SPEC = pl.BlockSpec(memory_space=pltpu.SMEM)
@@ -771,6 +771,7 @@
     utts = float(utterances * count)
     tie = lax.optimization_barrier
 
+    own, member, teacher_logits = tie((own, member, teacher_logits))
     give, kept = teacher_sums(member, teacher_logits, utterances)
     got = exchange(give, "member")
     flat = features.reshape(utterances * frames, model)

time: 155 us -> 148 us (0.955)
  local copies, waits for them, and re-layouts: 13.4 us -> 2.63 us
  starting transfers between devices: 39.7 us -> 49.6 us
  waiting for transfers between devices: 46.1 us -> 41.9 us
    ppermute x25, starting transfers between devices: 34.6 us -> 45.7 us  [exchange(): lax.ppermute(values, ALL, [(i, i ^ bits[place ^ i % 2]) for i in range(co...]
    unnamed x57 -> x27, local copies, waits for them, and re-layouts: 12.3 us -> 1.51 us
    ppermute x25, waiting for transfers between devices: 44 us -> 39.9 us  [exchange(): lax.ppermute(values, ALL, [(i, i ^ bits[place ^ i % 2]) for i in range(co...]
  transfers between devices with their start and end apart: 33 -> 33, of which waited for: 16 -> 17; matrix products, arithmetic and copies ran while one was open for 2% -> 2% of each run, Pallas kernels for 25% -> 26%
where the time goes in v10:
time: 148 us
  Pallas kernels  50.3 us (34%)
  starting transfers between devices  49.6 us (34%)
  waiting for transfers between devices  41.9 us (28%)
  local copies, waits for them, and re-layouts  2.63 us (2%)
  other arithmetic  2.12 us (1%)
    ppermute x25, starting transfers between devices, exchange(): lax.ppermute(values, ALL, [(i, i ^ bits[place ^ i % 2]) for i in range(co...  45.7 us
    ppermute x25, waiting for transfers between devices, exchange(): lax.ppermute(values, ALL, [(i, i ^ bits[place ^ i % 2]) for i in range(co...  39.9 us
    pallas_call x2, Pallas kernels, inner(): pl.pallas_call(inner_kernel, grid=(steps,), out_shape=(shape, shape, jax....  15.9 us
    pallas_call x1, Pallas kernels, forward(): pl.pallas_call(forward_kernel, grid=(steps,), out_shape=(jax.ShapeDtypeSt...  12.9 us
    pallas_call x1, Pallas kernels, tap_sums(): pl.pallas_call(taps_kernel, grid=(steps,), out_shape=jax.ShapeDtypeStruct...  5.91 us
    pallas_call x1, Pallas kernels, unpack_inner(): pl.pallas_call(functools.partial(unpack_inner_kernel, utts), out_shape=(j...  4.35 us
    ppermute x8, starting transfers between devices, exchange(): return lax.ppermute(values, step, [(0, 1), (1, 0)])  3.9 us
    pallas_call x1, Pallas kernels, unpack_top(): pl.pallas_call(functools.partial(unpack_top_kernel, utts), out_shape=(jax...  3.46 us
  transfers between devices with their start and end apart: 33, of which 17 were waited for; matrix products, arithmetic and copies ran while one was open for 2% of the time, Pallas kernels for 26%

profile of v10, /device:TPU:0, one launch (start us, length us, event | category | flops | bytes accessed | tf_op | source)
XLA Modules:
  0.0 147.7 jit_solution(13026315289609423704)
XLA Ops:
  0.7 1.2 copy-done.2
  2.0 1.2 teachers.1
  3.2 3.0 %collective-permute-start = (f32[2,256,256]{2,1,0:T(8,128)S(1)}, f32[2,256,256]{2,1,0:T(8,128)S(1)}, u32[]{:S(2)}, u32[]{:S(2)}) collective-permute-start(f32[2,256,256]{2,1,0:T(8,128)S(1)} %get-tuple-element.116), channel_id=1, source_target_pairs={{0,16},{16,0},{1,17},{17,1},{2,18},{18,2},{3,19},{19,3},{4,20},{20... | collective-permute-start | bytes 1572872 | tf_op jit(solution)/shard_map/ppermute | solution.py:54
  6.3 12.9 %forward.1 = (bf16[1024,512]{1,0:T(8,128)(2,1)S(1)}, f32[512,1024]{1,0:T(8,128)S(1)}, f32[512,1024]{1,0:T(8,128)S(1)}, f32[512,1024]{1,0:T(8,128)S(1)}, bf16[512...) custom-call(s32[2]{0:T(128)S(1)} %copy-done.8, bf16[512,1024]{1,0:T(8,128)(2,1)S(1)} %bitcast.9, f32[1,1024]{1,0:T(1,128)S(1)} %bitcast.12, ...), custom_call_target="tpu_custom_call" | custom-call | flops 17250000896 | bytes 1048576 | tf_op jit(solution)/shard_map/forward/pallas_call | solution.py:318
  19.2 3.4 %top.1 = (f32[2,1,128]{2,1,0:T(1,128)S(1)}, bf16[512,1024]{1,0:T(8,128)(2,1)S(1)}, bf16[512,256]{1,0:T(8,128)(2,1)S(1)}, bf16[512,1024]{1,0:T(8,128)(2,1)S(1)}) custom-call(s32[2]{0:T(128)S(1)} %copy-done.8, f32[512,1024]{1,0:T(8,128)S(1)} %get-tuple-element.112.residual_ref, f32[1,1024]{1,0:T(1,128)S(1)} %bitcast.10, bf16[1024,256]{1,0:T(8,128)(2,1)S(1)} %copy-done.4, ...), custom_call_target="tpu_custom_call" | custom-call | flops 5750000128 | bytes 1048576 | tf_op jit(solution)/shard_map/top/pallas_call | solution.py:386
  22.7 3.1 %outer.1 = (bf16[2,8,64,640]{3,2,1,0:T(8,128)(2,1)S(1)}, bf16[2,8,64,640]{3,2,1,0:T(8,128)(2,1)S(1)}) custom-call(s32[3]{0:T(128)S(1)} %pad_add_fusion.own_ref, bf16[512,1024]{1,0:T(8,128)(2,1)S(1)} %get-tuple-element.111.active_ref, bf16[512,1024]{1,0:T(8,128)(2,1)S(1)} %get-tuple-element.133.dresidual_ref, ...), custom_call_target="tpu_custom_call" | custom-call | flops 5750000128 | bytes 1048576 | tf_op jit(solution)/shard_map/outer/pallas_call | solution.py:425
  25.9 7.9 %inner.2 = (bf16[2,8,64,512]{3,2,1,0:T(8,128)(2,1)S(1)}, bf16[2,8,64,512]{3,2,1,0:T(8,128)(2,1)S(1)}, f32[512,512]{1,0:T(8,128)S(1)}) custom-call(s32[3]{0:T(128)S(1)} %pad_add_fusion.own_ref, s32[2]{0:T(128)S(1)} %copy-done.8, bf16[512,1024]{1,0:T(8,128)(2,1)S(1)} %get-tuple-element.133.dresidual_ref, bf16[1024,1024]{1,0:T(8,128)(2,1)S(1)} %copy-done.1, ...), custom_call_target="tpu_custom_call" | custom-call | flops 12650000384 | bytes 1048576 | tf_op jit(solution)/shard_map/inner/pallas_call | solution.py:510
  34.9 1.8 %collective-permute-start.2 = (bf16[2,4,64,640]{3,2,1,0:T(8,128)(2,1)S(1)}, bf16[2,4,64,640]{3,2,1,0:T(8,128)(2,1)S(1)}, u32[]{:S(2)}, u32[]{:S(2)}) collective-permute-start(bf16[2,4,64,640]{3,2,1,0:T(8,128)(2,1)S(1)} %slice.57), channel_id=1, source_target_pairs={{0,16},{1,3},{2,18},{3,1},{4,20},{5,7},{6,22},{7,5},{8,24},{9,11},... | collective-permute-start | bytes 1966088 | tf_op jit(solution)/shard_map/ppermute | solution.py:60
  36.7 7.9 %inner.3 = (bf16[2,8,64,512]{3,2,1,0:T(8,128)(2,1)S(1)}, bf16[2,8,64,512]{3,2,1,0:T(8,128)(2,1)S(1)}, f32[512,512]{1,0:T(8,128)S(1)}) custom-call(s32[3]{0:T(128)S(1)} %pad_add_fusion.own_ref, s32[2]{0:T(128)S(1)} %copy-done.8, bf16[512,1024]{1,0:T(8,128)(2,1)S(1)} %get-tuple-element.133.dresidual_ref, bf16[1024,1024]{1,0:T(8,128)(2,1)S(1)} %copy-done.1, ...), custom_call_target="tpu_custom_call" | custom-call | flops 12650000384 | bytes 1048576 | tf_op jit(solution)/shard_map/inner/pallas_call | solution.py:510
  44.7 0.8 collective-permute-done.2
  45.7 1.8 %collective-permute-start.7 = (bf16[2,2,64,640]{3,2,1,0:T(8,128)(2,1)S(1)}, bf16[2,2,64,640]{3,2,1,0:T(8,128)(2,1)S(1)}, u32[]{:S(2)}, u32[]{:S(2)}) collective-permute-start(bf16[2,2,64,640]{3,2,1,0:T(8,128)(2,1)S(1)} %slice.78), channel_id=1, source_target_pairs={{0,2},{1,17},{2,0},{3,19},{4,6},{5,21},{6,4},{7,23},{8,10},{9,25},... | collective-permute-start | bytes 983048 | tf_op jit(solution)/shard_map/ppermute | solution.py:60
  47.9 1.6 %collective-permute-start.6 = (bf16[2,4,64,512]{3,2,1,0:T(8,128)(2,1)S(1)}, bf16[2,4,64,512]{3,2,1,0:T(8,128)(2,1)S(1)}, u32[]{:S(2)}, u32[]{:S(2)}) collective-permute-start(bf16[2,4,64,512]{3,2,1,0:T(8,128)(2,1)S(1)} %slice.77), channel_id=1, source_target_pairs={{0,16},{1,3},{2,18},{3,1},{4,20},{5,7},{6,22},{7,5},{8,24},{9,11},... | collective-permute-start | bytes 1572872 | tf_op jit(solution)/shard_map/ppermute | solution.py:60
  50.5 5.9 %taps.1 = f32[32,1024]{1,0:T(8,128)S(1)} custom-call(s32[2]{0:T(128)S(1)} %copy-done.8, f32[512,1024]{1,0:T(8,128)S(1)} %get-tuple-element.125.gated_ref, f32[512,512]{1,0:T(8,128)S(1)} %get-tuple-element.146.refs_0_, f32[512,512]{1,0:T(8,128)S(1)} %get-tuple-element.147.refs_1_), custom_call_target="tpu_custom_call" | custom-call | flops 10350000128 | bytes 1048576 | tf_op jit(solution)/shard_map/taps/pallas_call | solution.py:592
  56.4 1.6 %collective-permute-start.11 = (f32[32,1024]{1,0:T(8,128)S(1)}, f32[32,1024]{1,0:T(8,128)S(1)}, u32[]{:S(2)}, u32[]{:S(2)}) collective-permute-start(f32[32,1024]{1,0:T(8,128)S(1)} %taps.1), channel_id=1, source_target_pairs={{0,16},{1,3},{2,18},{3,1},{4,20},{5,7},{6,22},{7,5},{8,24},{9,11},... | collective-permute-start | bytes 393224 | tf_op jit(solution)/shard_map/ppermute | solution.py:60
  58.1 1.6 %collective-permute-start.10 = (bf16[2,1,64,640]{3,2,1,0:T(8,128)(2,1)S(1)}, bf16[2,1,64,640]{3,2,1,0:T(8,128)(2,1)S(1)}, u32[]{:S(2)}, u32[]{:S(2)}) collective-permute-start(bf16[2,1,64,640]{3,2,1,0:T(8,128)(2,1)S(1)} %slice.81), channel_id=1, source_target_pairs={{0,4},{1,9},{2,6},{3,11},{4,0},{5,13},{6,2},{7,15},{8,12},{9,1},{1... | collective-permute-start | bytes 491528 | tf_op jit(solution)/shard_map/ppermute | solution.py:60
  60.5 3.6 %collective-permute-done.5 = bf16[2,4,64,512]{3,2,1,0:T(8,128)(2,1)S(1)} collective-permute-done((bf16[2,4,64,512]{3,2,1,0:T(8,128)(2,1)S(1)}, bf16[2,4,64,512]{3,2,1,0:T(8,128)(2,1)S(1)}, u32[]{:S(2)}, u32[]{:S(2)}) %collective-permute-start.5) | collective-permute-done | bytes 524320 | tf_op jit(solution)/shard_map/ppermute | solution.py:60
  64.3 2.6 %collective-permute-done.11 = f32[32,1024]{1,0:T(8,128)S(1)} collective-permute-done((f32[32,1024]{1,0:T(8,128)S(1)}, f32[32,1024]{1,0:T(8,128)S(1)}, u32[]{:S(2)}, u32[]{:S(2)}) %collective-permute-start.11) | collective-permute-done | bytes 131104 | tf_op jit(solution)/shard_map/ppermute | solution.py:60
  66.9 1.5 collective-permute-start.14
  68.4 0.6 collective-permute-start.8
  69.1 2.5 %collective-permute-start.13 = (bf16[2,1,64,640]{3,2,1,0:T(8,128)(2,1)S(1)}, bf16[2,1,64,640]{3,2,1,0:T(8,128)(2,1)S(1)}, u32[]{:S(2)}, u32[]{:S(2)}) collective-permute-start(bf16[2,1,64,640]{3,2,1,0:T(8,128)(2,1)S(1)} %add_convert_fusion.10), channel_id=1, source_target_pairs={{0,8},{1,5},{2,10},{3,7},{4,12},{5,1},{6,14},{7,3},{8,0},{9,13},{1... | collective-permute-start | bytes 491528 | tf_op jit(solution)/shard_map/ppermute | solution.py:60
  71.7 1.7 %collective-permute-start.12 = (bf16[2,1,64,512]{3,2,1,0:T(8,128)(2,1)S(1)}, bf16[2,1,64,512]{3,2,1,0:T(8,128)(2,1)S(1)}, u32[]{:S(2)}, u32[]{:S(2)}) collective-permute-start(bf16[2,1,64,512]{3,2,1,0:T(8,128)(2,1)S(1)} %slice.82), channel_id=1, source_target_pairs={{0,4},{1,9},{2,6},{3,11},{4,0},{5,13},{6,2},{7,15},{8,12},{9,1},{1... | collective-permute-start | bytes 393224 | tf_op jit(solution)/shard_map/ppermute | solution.py:60
  73.3 1.4 collective-permute-done.8
  74.9 1.6 %collective-permute-start.17 = (f32[32,1024]{1,0:T(8,128)S(1)}, f32[32,1024]{1,0:T(8,128)S(1)}, u32[]{:S(2)}, u32[]{:S(2)}) collective-permute-start(f32[32,1024]{1,0:T(8,128)S(1)} %add.87), channel_id=1, source_target_pairs={{0,4},{1,9},{2,6},{3,11},{4,0},{5,13},{6,2},{7,15},{8,12},{9,1},{1... | collective-permute-start | bytes 393224 | tf_op jit(solution)/shard_map/ppermute | solution.py:60
  76.5 0.9 collective-permute-done.13
  77.5 4.6 %collective-permute-start.16 = (bf16[2,1,64,640]{3,2,1,0:T(8,128)(2,1)S(1)}, bf16[2,1,64,640]{3,2,1,0:T(8,128)(2,1)S(1)}, u32[]{:S(2)}, u32[]{:S(2)}) collective-permute-start(bf16[2,1,64,640]{3,2,1,0:T(8,128)(2,1)S(1)} %add_convert_fusion.9), channel_id=1, source_target_pairs={{0,4},{1,9},{2,6},{3,11},{4,0},{5,13},{6,2},{7,15},{8,12},{9,1},{1... | collective-permute-start | bytes 491528 | tf_op jit(solution)/shard_map/ppermute | solution.py:60
  82.2 3.9 %collective-permute-start.15 = (bf16[2,1,64,512]{3,2,1,0:T(8,128)(2,1)S(1)}, bf16[2,1,64,512]{3,2,1,0:T(8,128)(2,1)S(1)}, u32[]{:S(2)}, u32[]{:S(2)}) collective-permute-start(bf16[2,1,64,512]{3,2,1,0:T(8,128)(2,1)S(1)} %add_convert_fusion.14), channel_id=1, source_target_pairs={{0,8},{1,5},{2,10},{3,7},{4,12},{5,1},{6,14},{7,3},{8,0},{9,13},{1... | collective-permute-start | bytes 393224 | tf_op jit(solution)/shard_map/ppermute | solution.py:60
  86.2 5.9 %collective-permute-done.18 = bf16[2,1,64,512]{3,2,1,0:T(8,128)(2,1)S(1)} collective-permute-done((bf16[2,1,64,512]{3,2,1,0:T(8,128)(2,1)S(1)}, bf16[2,1,64,512]{3,2,1,0:T(8,128)(2,1)S(1)}, u32[]{:S(2)}, u32[]{:S(2)}) %collective-permute-start.18) | collective-permute-done | bytes 131104 | tf_op jit(solution)/shard_map/ppermute | solution.py:60
  92.1 3.1 %collective-permute-start.21 = (bf16[2,1,64,512]{3,2,1,0:T(8,128)(2,1)S(1)}, bf16[2,1,64,512]{3,2,1,0:T(8,128)(2,1)S(1)}, u32[]{:S(2)}, u32[]{:S(2)}) collective-permute-start(bf16[2,1,64,512]{3,2,1,0:T(8,128)(2,1)S(1)} %add_convert_fusion.13), channel_id=1, source_target_pairs={{0,8},{1,5},{2,10},{3,7},{4,12},{5,1},{6,14},{7,3},{8,0},{9,13},{1... | collective-permute-start | bytes 393224 | tf_op jit(solution)/shard_map/ppermute | solution.py:60
  95.3 1.2 collective-permute-start.19
  96.7 1.5 %collective-permute-done.21 = bf16[2,1,64,512]{3,2,1,0:T(8,128)(2,1)S(1)} collective-permute-done((bf16[2,1,64,512]{3,2,1,0:T(8,128)(2,1)S(1)}, bf16[2,1,64,512]{3,2,1,0:T(8,128)(2,1)S(1)}, u32[]{:S(2)}, u32[]{:S(2)}) %collective-permute-start.21) | collective-permute-done | bytes 131104 | tf_op jit(solution)/shard_map/ppermute | solution.py:60
  98.2 3.3 %collective-permute-done.20 = f32[32,1024]{1,0:T(8,128)S(1)} collective-permute-done((f32[32,1024]{1,0:T(8,128)S(1)}, f32[32,1024]{1,0:T(8,128)S(1)}, u32[]{:S(2)}, u32[]{:S(2)}) %collective-permute-start.20) | collective-permute-done | bytes 131104 | tf_op jit(solution)/shard_map/ppermute | solution.py:60
  101.5 2.4 %collective-permute-done.19 = bf16[2,2,64,640]{3,2,1,0:T(8,128)(2,1)S(1)} collective-permute-done((bf16[2,2,64,640]{3,2,1,0:T(8,128)(2,1)S(1)}, bf16[2,2,64,640]{3,2,1,0:T(8,128)(2,1)S(1)}, u32[]{:S(2)}, u32[]{:S(2)}) %collective-permute-start.19) | collective-permute-done | bytes 327712 | tf_op jit(solution)/shard_map/ppermute | solution.py:60
  104.0 6.5 %collective-permute-start.22 = (bf16[2,4,64,640]{3,2,1,0:T(8,128)(2,1)S(1)}, bf16[2,4,64,640]{3,2,1,0:T(8,128)(2,1)S(1)}, u32[]{:S(2)}, u32[]{:S(2)}) collective-permute-start(bf16[2,4,64,640]{3,2,1,0:T(8,128)(2,1)S(1)} %constant_dynamic-update-slice_fusion.2), channel_id=1, source_target_pairs={{0,16},{1,3},{2,18},{3,1},{4,20},{5,7},{6,22},{7,5},{8,24},{9,11},... | collective-permute-start | bytes 1966088 | tf_op jit(solution)/shard_map/ppermute | solution.py:60
  110.5 2.0 %collective-permute-start.24 = (bf16[2,1,64,512]{3,2,1,0:T(8,128)(2,1)S(1)}, bf16[2,1,64,512]{3,2,1,0:T(8,128)(2,1)S(1)}, u32[]{:S(2)}, u32[]{:S(2)}) collective-permute-start(bf16[2,1,64,512]{3,2,1,0:T(8,128)(2,1)S(1)} %add_convert_fusion.11), channel_id=1, source_target_pairs={{0,4},{1,9},{2,6},{3,11},{4,0},{5,13},{6,2},{7,15},{8,12},{9,1},{1... | collective-permute-start | bytes 393224 | tf_op jit(solution)/shard_map/ppermute | solution.py:60
  112.6 4.3 %collective-permute-done.25 = bf16[2,1,64,512]{3,2,1,0:T(8,128)(2,1)S(1)} collective-permute-done((bf16[2,1,64,512]{3,2,1,0:T(8,128)(2,1)S(1)}, bf16[2,1,64,512]{3,2,1,0:T(8,128)(2,1)S(1)}, u32[]{:S(2)}, u32[]{:S(2)}) %collective-permute-start.25) | collective-permute-done | bytes 131104 | tf_op jit(solution)/shard_map/ppermute | solution.py:60
  116.9 1.4 collective-permute-done.24
  118.4 0.7 collective-permute-done.22
  119.3 1.3 collective-permute-start.28
  120.6 0.8 collective-permute-start.27
  121.4 4.3 %collective-permute-done.28 = bf16[2,2,64,512]{3,2,1,0:T(8,128)(2,1)S(1)} collective-permute-done((bf16[2,2,64,512]{3,2,1,0:T(8,128)(2,1)S(1)}, bf16[2,2,64,512]{3,2,1,0:T(8,128)(2,1)S(1)}, u32[]{:S(2)}, u32[]{:S(2)}) %collective-permute-start.28) | collective-permute-done | bytes 262176 | tf_op jit(solution)/shard_map/ppermute | solution.py:60
  125.7 2.1 %collective-permute-start.30 = (bf16[2,4,64,512]{3,2,1,0:T(8,128)(2,1)S(1)}, bf16[2,4,64,512]{3,2,1,0:T(8,128)(2,1)S(1)}, u32[]{:S(2)}, u32[]{:S(2)}) collective-permute-start(bf16[2,4,64,512]{3,2,1,0:T(8,128)(2,1)S(1)} %constant_dynamic-update-slice_fusion.10), channel_id=1, source_target_pairs={{0,16},{1,3},{2,18},{3,1},{4,20},{5,7},{6,22},{7,5},{8,24},{9,11},... | collective-permute-start | bytes 1572872 | tf_op jit(solution)/shard_map/ppermute | solution.py:60
  127.8 0.9 collective-permute-done.27
  128.7 2.4 %collective-permute-start.29 = (bf16[2,4,64,512]{3,2,1,0:T(8,128)(2,1)S(1)}, bf16[2,4,64,512]{3,2,1,0:T(8,128)(2,1)S(1)}, u32[]{:S(2)}, u32[]{:S(2)}) collective-permute-start(bf16[2,4,64,512]{3,2,1,0:T(8,128)(2,1)S(1)} %constant_dynamic-update-slice_fusion.12), channel_id=1, source_target_pairs={{0,16},{1,3},{2,18},{3,1},{4,20},{5,7},{6,22},{7,5},{8,24},{9,11},... | collective-permute-start | bytes 1572872 | tf_op jit(solution)/shard_map/ppermute | solution.py:60
  131.2 3.5 %unpack_top.1 = (f32[1024,1024]{1,0:T(8,128)}, f32[1024,256]{1,0:T(8,128)}, f32[1,1024]{1,0:T(1,128)}, f32[31,1024]{1,0:T(8,128)}, f32[2,1,128]{2,1,0:T(1,128)S(1)}) custom-call(s32[3]{0:T(128)S(1)} %pad_add_fusion.own_ref, f32[32,1024]{1,0:T(8,128)S(1)} %add.95.small_ref, bf16[2,8,64,640]{3,2,1,0:T(8,128)(2,1)S(1)} %constant_dynamic-update-slice_fusion.8.mine_ref, ...), custom_call_target="tpu_custom_call" | custom-call | flops 5750000128 | bytes 1048576 | tf_op jit(solution)/shard_map/unpack_top/pallas_call | solution.py:681
  135.1 5.5 %collective-permute-done.29 = bf16[2,4,64,512]{3,2,1,0:T(8,128)(2,1)S(1)} collective-permute-done((bf16[2,4,64,512]{3,2,1,0:T(8,128)(2,1)S(1)}, bf16[2,4,64,512]{3,2,1,0:T(8,128)(2,1)S(1)}, u32[]{:S(2)}, u32[]{:S(2)}) %collective-permute-start.29) | collective-permute-done | bytes 524320 | tf_op jit(solution)/shard_map/ppermute | solution.py:60
  140.7 0.6 slice_reduce_fusion
  141.3 2.0 %collective-permute-done.31.refs_3_ = bf16[2,8,64,512]{3,2,1,0:T(8,128)(2,1)S(1)} collective-permute-done((bf16[2,8,64,512]{3,2,1,0:T(8,128)(2,1)S(1)}, bf16[2,8,64,512]{3,2,1,0:T(8,128)(2,1)S(1)}, u32[]{:S(2)}, u32[]{:S(2)}) %collective-permute-start.31) | collective-permute-done | bytes 1048608 | tf_op jit(solution)/shard_map/ppermute | solution.py:54
  143.4 4.4 %unpack_inner.1 = (f32[1024,2048]{1,0:T(8,128)}, f32[1,1024]{1,0:T(1,128)}) custom-call(s32[3]{0:T(128)S(1)} %pad_add_fusion.own_ref, f32[32,1024]{1,0:T(8,128)S(1)} %add.95.small_ref, bf16[1024,2048]{1,0:T(8,128)(2,1)S(1)} %copy-done, f32[1,1024]{1,0:T(1,128)S(1)} %bitcast.13, bf16[2,8,64,512]{3,2,1,0:T(8,128)(2,1)S(1)} %constant_dynamic-update-slice_fusion.14.refs_0_, ...), custom_call_target="tpu_custom_call" | custom-call | flops 9200000000 | bytes 1048576 | tf_op jit(solution)/shard_map/unpack_inner/pallas_call | solution.py:734
  (94 shorter events, 5.6 us)
Async XLA Ops:
  0.7 1.2 copy-start.2
  2.0 4.3 %copy-start = (bf16[1024,2048]{1,0:T(8,128)(2,1)S(1)}, bf16[1024,2048]{1,0:T(8,128)(2,1)}, u32[]{:S(2)}) copy-start(bf16[1024,2048]{1,0:T(8,128)(2,1)} %weight_ref.1) | copy-start | bytes 12582916
  2.0 4.3 %copy-start.1 = (bf16[1024,1024]{1,0:T(8,128)(2,1)S(1)}, bf16[1024,1024]{1,0:T(8,128)(2,1)}, u32[]{:S(2)}) copy-start(bf16[1024,1024]{1,0:T(8,128)(2,1)} %out_weight_ref.5) | copy-start | bytes 6291460
  2.0 4.3 %copy-start.3 = (bf16[2,256,1024]{2,1,0:T(8,128)(2,1)S(1)}, bf16[2,256,1024]{2,1,0:T(8,128)(2,1)}, u32[]{:S(2)}) copy-start(bf16[2,256,1024]{2,1,0:T(8,128)(2,1)} %param.9) | copy-start | bytes 3145732
  2.0 4.3 %copy-start.5 = (f32[31,1024]{1,0:T(8,128)S(1)}, f32[31,1024]{1,0:T(8,128)}, u32[]{:S(2)}) copy-start(f32[31,1024]{1,0:T(8,128)} %depth_ref.5) | copy-start | bytes 380932
  2.0 4.3 %copy-start.7 = (f32[1024]{0:T(1024)S(1)}, f32[1024]{0:T(1024)}, u32[]{:S(2)}) copy-start(f32[1024]{0:T(1024)} %param.12) | copy-start | bytes 12292
  2.0 4.3 %copy-start.8 = (s32[2]{0:T(128)S(1)}, s32[2]{0:T(128)}, u32[]{:S(2)}) copy-start(s32[2]{0:T(128)} %lengths_ref.9) | copy-start | bytes 28
  3.2 16.0 %collective-permute-start = (f32[2,256,256]{2,1,0:T(8,128)S(1)}, f32[2,256,256]{2,1,0:T(8,128)S(1)}, u32[]{:S(2)}, u32[]{:S(2)}) collective-permute-start(f32[2,256,256]{2,1,0:T(8,128)S(1)} %get-tuple-element.116), channel_id=1, source_target_pairs={{0,16},{16,0},{1,17},{17,1},{2,18},{18,2},{3,19},{19,3},{4,20},{20... | collective-permute-start | bytes 1572872 | tf_op jit(solution)/shard_map/ppermute | solution.py:54
  6.3 13.0 %copy-start.4 = (bf16[1024,256]{1,0:T(8,128)(2,1)S(1)}, bf16[1024,256]{1,0:T(8,128)(2,1)}, u32[]{:S(2)}) copy-start(bf16[1024,256]{1,0:T(8,128)(2,1)} %head_ref.3) | copy-start | bytes 1572868
  6.3 13.0 %copy-start.6 = (f32[1024]{0:T(1024)S(1)}, f32[1024]{0:T(1024)}, u32[]{:S(2)}) copy-start(f32[1024]{0:T(1024)} %param.16) | copy-start | bytes 12292
  25.8 8.6 %collective-permute-start.1 = (bf16[2,8,64,640]{3,2,1,0:T(8,128)(2,1)S(1)}, bf16[2,8,64,640]{3,2,1,0:T(8,128)(2,1)S(1)}, u32[]{:S(2)}, u32[]{:S(2)}) collective-permute-start(bf16[2,8,64,640]{3,2,1,0:T(8,128)(2,1)S(1)} %get-tuple-element.122), channel_id=1, source_target_pairs={{0,1},{1,0},{2,3},{3,2},{4,5},{5,4},{6,7},{7,6},{8,9},{9,8},{10,11... | collective-permute-start | bytes 3932168 | tf_op jit(solution)/shard_map/ppermute | solution.py:54
  33.9 13.7 %collective-permute-start.4 = (bf16[2,8,64,512]{3,2,1,0:T(8,128)(2,1)S(1)}, bf16[2,8,64,512]{3,2,1,0:T(8,128)(2,1)S(1)}, u32[]{:S(2)}, u32[]{:S(2)}) collective-permute-start(bf16[2,8,64,512]{3,2,1,0:T(8,128)(2,1)S(1)} %get-tuple-element.139), channel_id=1, source_target_pairs={{0,1},{1,0},{2,3},{3,2},{4,5},{5,4},{6,7},{7,6},{8,9},{9,8},{10,11... | collective-permute-start | bytes 3145736 | tf_op jit(solution)/shard_map/ppermute | solution.py:54
  34.9 10.7 %collective-permute-start.2 = (bf16[2,4,64,640]{3,2,1,0:T(8,128)(2,1)S(1)}, bf16[2,4,64,640]{3,2,1,0:T(8,128)(2,1)S(1)}, u32[]{:S(2)}, u32[]{:S(2)}) collective-permute-start(bf16[2,4,64,640]{3,2,1,0:T(8,128)(2,1)S(1)} %slice.57), channel_id=1, source_target_pairs={{0,16},{1,3},{2,18},{3,1},{4,20},{5,7},{6,22},{7,5},{8,24},{9,11},... | collective-permute-start | bytes 1966088 | tf_op jit(solution)/shard_map/ppermute | solution.py:60
  44.6 4.9 %collective-permute-start.3 = (bf16[2,8,64,512]{3,2,1,0:T(8,128)(2,1)S(1)}, bf16[2,8,64,512]{3,2,1,0:T(8,128)(2,1)S(1)}, u32[]{:S(2)}, u32[]{:S(2)}) collective-permute-start(bf16[2,8,64,512]{3,2,1,0:T(8,128)(2,1)S(1)} %get-tuple-element.137), channel_id=1, source_target_pairs={{0,1},{1,0},{2,3},{3,2},{4,5},{5,4},{6,7},{7,6},{8,9},{9,8},{10,11... | collective-permute-start | bytes 3145736 | tf_op jit(solution)/shard_map/ppermute | solution.py:54
  45.7 12.2 %collective-permute-start.7 = (bf16[2,2,64,640]{3,2,1,0:T(8,128)(2,1)S(1)}, bf16[2,2,64,640]{3,2,1,0:T(8,128)(2,1)S(1)}, u32[]{:S(2)}, u32[]{:S(2)}) collective-permute-start(bf16[2,2,64,640]{3,2,1,0:T(8,128)(2,1)S(1)} %slice.78), channel_id=1, source_target_pairs={{0,2},{1,17},{2,0},{3,19},{4,6},{5,21},{6,4},{7,23},{8,10},{9,25},... | collective-permute-start | bytes 983048 | tf_op jit(solution)/shard_map/ppermute | solution.py:60
  47.9 11.8 %collective-permute-start.6 = (bf16[2,4,64,512]{3,2,1,0:T(8,128)(2,1)S(1)}, bf16[2,4,64,512]{3,2,1,0:T(8,128)(2,1)S(1)}, u32[]{:S(2)}, u32[]{:S(2)}) collective-permute-start(bf16[2,4,64,512]{3,2,1,0:T(8,128)(2,1)S(1)} %slice.77), channel_id=1, source_target_pairs={{0,16},{1,3},{2,18},{3,1},{4,20},{5,7},{6,22},{7,5},{8,24},{9,11},... | collective-permute-start | bytes 1572872 | tf_op jit(solution)/shard_map/ppermute | solution.py:60
  49.9 14.2 %collective-permute-start.5 = (bf16[2,4,64,512]{3,2,1,0:T(8,128)(2,1)S(1)}, bf16[2,4,64,512]{3,2,1,0:T(8,128)(2,1)S(1)}, u32[]{:S(2)}, u32[]{:S(2)}) collective-permute-start(bf16[2,4,64,512]{3,2,1,0:T(8,128)(2,1)S(1)} %slice.76), channel_id=1, source_target_pairs={{0,16},{1,3},{2,18},{3,1},{4,20},{5,7},{6,22},{7,5},{8,24},{9,11},... | collective-permute-start | bytes 1572872 | tf_op jit(solution)/shard_map/ppermute | solution.py:60
  56.4 10.5 %collective-permute-start.11 = (f32[32,1024]{1,0:T(8,128)S(1)}, f32[32,1024]{1,0:T(8,128)S(1)}, u32[]{:S(2)}, u32[]{:S(2)}) collective-permute-start(f32[32,1024]{1,0:T(8,128)S(1)} %taps.1), channel_id=1, source_target_pairs={{0,16},{1,3},{2,18},{3,1},{4,20},{5,7},{6,22},{7,5},{8,24},{9,11},... | collective-permute-start | bytes 393224 | tf_op jit(solution)/shard_map/ppermute | solution.py:60
  58.1 10.3 %collective-permute-start.10 = (bf16[2,1,64,640]{3,2,1,0:T(8,128)(2,1)S(1)}, bf16[2,1,64,640]{3,2,1,0:T(8,128)(2,1)S(1)}, u32[]{:S(2)}, u32[]{:S(2)}) collective-permute-start(bf16[2,1,64,640]{3,2,1,0:T(8,128)(2,1)S(1)} %slice.81), channel_id=1, source_target_pairs={{0,4},{1,9},{2,6},{3,11},{4,0},{5,13},{6,2},{7,15},{8,12},{9,1},{1... | collective-permute-start | bytes 491528 | tf_op jit(solution)/shard_map/ppermute | solution.py:60
  59.9 11.7 %collective-permute-start.9 = (bf16[2,2,64,512]{3,2,1,0:T(8,128)(2,1)S(1)}, bf16[2,2,64,512]{3,2,1,0:T(8,128)(2,1)S(1)}, u32[]{:S(2)}, u32[]{:S(2)}) collective-permute-start(bf16[2,2,64,512]{3,2,1,0:T(8,128)(2,1)S(1)} %slice.80), channel_id=1, source_target_pairs={{0,2},{1,17},{2,0},{3,19},{4,6},{5,21},{6,4},{7,23},{8,10},{9,25},... | collective-permute-start | bytes 786440 | tf_op jit(solution)/shard_map/ppermute | solution.py:60
  66.9 7.9 %collective-permute-start.14 = (f32[32,1024]{1,0:T(8,128)S(1)}, f32[32,1024]{1,0:T(8,128)S(1)}, u32[]{:S(2)}, u32[]{:S(2)}) collective-permute-start(f32[32,1024]{1,0:T(8,128)S(1)} %add.83), channel_id=1, source_target_pairs={{0,2},{1,17},{2,0},{3,19},{4,6},{5,21},{6,4},{7,23},{8,10},{9,25},... | collective-permute-start | bytes 393224 | tf_op jit(solution)/shard_map/ppermute | solution.py:60
  68.4 6.4 %collective-permute-start.8 = (bf16[2,2,64,512]{3,2,1,0:T(8,128)(2,1)S(1)}, bf16[2,2,64,512]{3,2,1,0:T(8,128)(2,1)S(1)}, u32[]{:S(2)}, u32[]{:S(2)}) collective-permute-start(bf16[2,2,64,512]{3,2,1,0:T(8,128)(2,1)S(1)} %slice.79), channel_id=1, source_target_pairs={{0,2},{1,17},{2,0},{3,19},{4,6},{5,21},{6,4},{7,23},{8,10},{9,25},... | collective-permute-start | bytes 786440 | tf_op jit(solution)/shard_map/ppermute | solution.py:60
  69.1 8.4 %collective-permute-start.13 = (bf16[2,1,64,640]{3,2,1,0:T(8,128)(2,1)S(1)}, bf16[2,1,64,640]{3,2,1,0:T(8,128)(2,1)S(1)}, u32[]{:S(2)}, u32[]{:S(2)}) collective-permute-start(bf16[2,1,64,640]{3,2,1,0:T(8,128)(2,1)S(1)} %add_convert_fusion.10), channel_id=1, source_target_pairs={{0,8},{1,5},{2,10},{3,7},{4,12},{5,1},{6,14},{7,3},{8,0},{9,13},{1... | collective-permute-start | bytes 491528 | tf_op jit(solution)/shard_map/ppermute | solution.py:60
  71.7 10.4 %collective-permute-start.12 = (bf16[2,1,64,512]{3,2,1,0:T(8,128)(2,1)S(1)}, bf16[2,1,64,512]{3,2,1,0:T(8,128)(2,1)S(1)}, u32[]{:S(2)}, u32[]{:S(2)}) collective-permute-start(bf16[2,1,64,512]{3,2,1,0:T(8,128)(2,1)S(1)} %slice.82), channel_id=1, source_target_pairs={{0,4},{1,9},{2,6},{3,11},{4,0},{5,13},{6,2},{7,15},{8,12},{9,1},{1... | collective-permute-start | bytes 393224 | tf_op jit(solution)/shard_map/ppermute | solution.py:60
  74.9 20.3 %collective-permute-start.17 = (f32[32,1024]{1,0:T(8,128)S(1)}, f32[32,1024]{1,0:T(8,128)S(1)}, u32[]{:S(2)}, u32[]{:S(2)}) collective-permute-start(f32[32,1024]{1,0:T(8,128)S(1)} %add.87), channel_id=1, source_target_pairs={{0,4},{1,9},{2,6},{3,11},{4,0},{5,13},{6,2},{7,15},{8,12},{9,1},{1... | collective-permute-start | bytes 393224 | tf_op jit(solution)/shard_map/ppermute | solution.py:60
  77.5 17.8 %collective-permute-start.16 = (bf16[2,1,64,640]{3,2,1,0:T(8,128)(2,1)S(1)}, bf16[2,1,64,640]{3,2,1,0:T(8,128)(2,1)S(1)}, u32[]{:S(2)}, u32[]{:S(2)}) collective-permute-start(bf16[2,1,64,640]{3,2,1,0:T(8,128)(2,1)S(1)} %add_convert_fusion.9), channel_id=1, source_target_pairs={{0,4},{1,9},{2,6},{3,11},{4,0},{5,13},{6,2},{7,15},{8,12},{9,1},{1... | collective-permute-start | bytes 491528 | tf_op jit(solution)/shard_map/ppermute | solution.py:60
  82.1 9.9 %collective-permute-start.18 = (bf16[2,1,64,512]{3,2,1,0:T(8,128)(2,1)S(1)}, bf16[2,1,64,512]{3,2,1,0:T(8,128)(2,1)S(1)}, u32[]{:S(2)}, u32[]{:S(2)}) collective-permute-start(bf16[2,1,64,512]{3,2,1,0:T(8,128)(2,1)S(1)} %slice.83), channel_id=1, source_target_pairs={{0,4},{1,9},{2,6},{3,11},{4,0},{5,13},{6,2},{7,15},{8,12},{9,1},{1... | collective-permute-start | bytes 393224 | tf_op jit(solution)/shard_map/ppermute | solution.py:60
  82.2 14.4 %collective-permute-start.15 = (bf16[2,1,64,512]{3,2,1,0:T(8,128)(2,1)S(1)}, bf16[2,1,64,512]{3,2,1,0:T(8,128)(2,1)S(1)}, u32[]{:S(2)}, u32[]{:S(2)}) collective-permute-start(bf16[2,1,64,512]{3,2,1,0:T(8,128)(2,1)S(1)} %add_convert_fusion.14), channel_id=1, source_target_pairs={{0,8},{1,5},{2,10},{3,7},{4,12},{5,1},{6,14},{7,3},{8,0},{9,13},{1... | collective-permute-start | bytes 393224 | tf_op jit(solution)/shard_map/ppermute | solution.py:60
  92.1 6.1 %collective-permute-start.21 = (bf16[2,1,64,512]{3,2,1,0:T(8,128)(2,1)S(1)}, bf16[2,1,64,512]{3,2,1,0:T(8,128)(2,1)S(1)}, u32[]{:S(2)}, u32[]{:S(2)}) collective-permute-start(bf16[2,1,64,512]{3,2,1,0:T(8,128)(2,1)S(1)} %add_convert_fusion.13), channel_id=1, source_target_pairs={{0,8},{1,5},{2,10},{3,7},{4,12},{5,1},{6,14},{7,3},{8,0},{9,13},{1... | collective-permute-start | bytes 393224 | tf_op jit(solution)/shard_map/ppermute | solution.py:60
  95.2 6.2 %collective-permute-start.20 = (f32[32,1024]{1,0:T(8,128)S(1)}, f32[32,1024]{1,0:T(8,128)S(1)}, u32[]{:S(2)}, u32[]{:S(2)}) collective-permute-start(f32[32,1024]{1,0:T(8,128)S(1)} %add.91), channel_id=1, source_target_pairs={{0,8},{1,5},{2,10},{3,7},{4,12},{5,1},{6,14},{7,3},{8,0},{9,13},{1... | collective-permute-start | bytes 393224 | tf_op jit(solution)/shard_map/ppermute | solution.py:60
  95.3 8.6 %collective-permute-start.19 = (bf16[2,2,64,640]{3,2,1,0:T(8,128)(2,1)S(1)}, bf16[2,2,64,640]{3,2,1,0:T(8,128)(2,1)S(1)}, u32[]{:S(2)}, u32[]{:S(2)}) collective-permute-start(bf16[2,2,64,640]{3,2,1,0:T(8,128)(2,1)S(1)} %constant_dynamic-update-slice_fusion), channel_id=1, source_target_pairs={{0,2},{1,17},{2,0},{3,19},{4,6},{5,21},{6,4},{7,23},{8,10},{9,25},... | collective-permute-start | bytes 983048 | tf_op jit(solution)/shard_map/ppermute | solution.py:60
  104.0 15.1 %collective-permute-start.22 = (bf16[2,4,64,640]{3,2,1,0:T(8,128)(2,1)S(1)}, bf16[2,4,64,640]{3,2,1,0:T(8,128)(2,1)S(1)}, u32[]{:S(2)}, u32[]{:S(2)}) collective-permute-start(bf16[2,4,64,640]{3,2,1,0:T(8,128)(2,1)S(1)} %constant_dynamic-update-slice_fusion.2), channel_id=1, source_target_pairs={{0,16},{1,3},{2,18},{3,1},{4,20},{5,7},{6,22},{7,5},{8,24},{9,11},... | collective-permute-start | bytes 1966088 | tf_op jit(solution)/shard_map/ppermute | solution.py:60
  110.5 6.4 %collective-permute-start.25 = (bf16[2,1,64,512]{3,2,1,0:T(8,128)(2,1)S(1)}, bf16[2,1,64,512]{3,2,1,0:T(8,128)(2,1)S(1)}, u32[]{:S(2)}, u32[]{:S(2)}) collective-permute-start(bf16[2,1,64,512]{3,2,1,0:T(8,128)(2,1)S(1)} %add_convert_fusion.12), channel_id=1, source_target_pairs={{0,4},{1,9},{2,6},{3,11},{4,0},{5,13},{6,2},{7,15},{8,12},{9,1},{1... | collective-permute-start | bytes 393224 | tf_op jit(solution)/shard_map/ppermute | solution.py:60
  110.5 7.8 %collective-permute-start.23 = (f32[32,1024]{1,0:T(8,128)S(1)}, f32[32,1024]{1,0:T(8,128)S(1)}, u32[]{:S(2)}, u32[]{:S(2)}) collective-permute-start(f32[32,1024]{1,0:T(8,128)S(1)} %add.94), channel_id=1, source_target_pairs={{0,1},{1,0},{2,3},{3,2},{4,5},{5,4},{6,7},{7,6},{8,9},{9,8},{10,11... | collective-permute-start | bytes 393224 | tf_op jit(solution)/shard_map/ppermute | solution.py:54
  110.5 7.8 %collective-permute-start.24 = (bf16[2,1,64,512]{3,2,1,0:T(8,128)(2,1)S(1)}, bf16[2,1,64,512]{3,2,1,0:T(8,128)(2,1)S(1)}, u32[]{:S(2)}, u32[]{:S(2)}) collective-permute-start(bf16[2,1,64,512]{3,2,1,0:T(8,128)(2,1)S(1)} %add_convert_fusion.11), channel_id=1, source_target_pairs={{0,4},{1,9},{2,6},{3,11},{4,0},{5,13},{6,2},{7,15},{8,12},{9,1},{1... | collective-permute-start | bytes 393224 | tf_op jit(solution)/shard_map/ppermute | solution.py:60
  119.2 12.0 %collective-permute-start.26 = (bf16[2,8,64,640]{3,2,1,0:T(8,128)(2,1)S(1)}, bf16[2,8,64,640]{3,2,1,0:T(8,128)(2,1)S(1)}, u32[]{:S(2)}, u32[]{:S(2)}) collective-permute-start(bf16[2,8,64,640]{3,2,1,0:T(8,128)(2,1)S(1)} %constant_dynamic-update-slice_fusion.8.mine_ref), channel_id=1, source_target_pairs={{0,1},{1,0},{2,3},{3,2},{4,5},{5,4},{6,7},{7,6},{8,9},{9,8},{10,11... | collective-permute-start | bytes 3932168 | tf_op jit(solution)/shard_map/ppermute | solution.py:54
  119.3 6.4 %collective-permute-start.28 = (bf16[2,2,64,512]{3,2,1,0:T(8,128)(2,1)S(1)}, bf16[2,2,64,512]{3,2,1,0:T(8,128)(2,1)S(1)}, u32[]{:S(2)}, u32[]{:S(2)}) collective-permute-start(bf16[2,2,64,512]{3,2,1,0:T(8,128)(2,1)S(1)} %constant_dynamic-update-slice_fusion.4), channel_id=1, source_target_pairs={{0,2},{1,17},{2,0},{3,19},{4,6},{5,21},{6,4},{7,23},{8,10},{9,25},... | collective-permute-start | bytes 786440 | tf_op jit(solution)/shard_map/ppermute | solution.py:60
  120.6 8.1 %collective-permute-start.27 = (bf16[2,2,64,512]{3,2,1,0:T(8,128)(2,1)S(1)}, bf16[2,2,64,512]{3,2,1,0:T(8,128)(2,1)S(1)}, u32[]{:S(2)}, u32[]{:S(2)}) collective-permute-start(bf16[2,2,64,512]{3,2,1,0:T(8,128)(2,1)S(1)} %constant_dynamic-update-slice_fusion.6), channel_id=1, source_target_pairs={{0,2},{1,17},{2,0},{3,19},{4,6},{5,21},{6,4},{7,23},{8,10},{9,25},... | collective-permute-start | bytes 786440 | tf_op jit(solution)/shard_map/ppermute | solution.py:60
  125.7 9.2 %collective-permute-start.30 = (bf16[2,4,64,512]{3,2,1,0:T(8,128)(2,1)S(1)}, bf16[2,4,64,512]{3,2,1,0:T(8,128)(2,1)S(1)}, u32[]{:S(2)}, u32[]{:S(2)}) collective-permute-start(bf16[2,4,64,512]{3,2,1,0:T(8,128)(2,1)S(1)} %constant_dynamic-update-slice_fusion.10), channel_id=1, source_target_pairs={{0,16},{1,3},{2,18},{3,1},{4,20},{5,7},{6,22},{7,5},{8,24},{9,11},... | collective-permute-start | bytes 1572872 | tf_op jit(solution)/shard_map/ppermute | solution.py:60
  128.7 11.8 %collective-permute-start.29 = (bf16[2,4,64,512]{3,2,1,0:T(8,128)(2,1)S(1)}, bf16[2,4,64,512]{3,2,1,0:T(8,128)(2,1)S(1)}, u32[]{:S(2)}, u32[]{:S(2)}) collective-permute-start(bf16[2,4,64,512]{3,2,1,0:T(8,128)(2,1)S(1)} %constant_dynamic-update-slice_fusion.12), channel_id=1, source_target_pairs={{0,16},{1,3},{2,18},{3,1},{4,20},{5,7},{6,22},{7,5},{8,24},{9,11},... | collective-permute-start | bytes 1572872 | tf_op jit(solution)/shard_map/ppermute | solution.py:60
  135.0 6.3 %collective-permute-start.32 = (bf16[2,8,64,512]{3,2,1,0:T(8,128)(2,1)S(1)}, bf16[2,8,64,512]{3,2,1,0:T(8,128)(2,1)S(1)}, u32[]{:S(2)}, u32[]{:S(2)}) collective-permute-start(bf16[2,8,64,512]{3,2,1,0:T(8,128)(2,1)S(1)} %constant_dynamic-update-slice_fusion.14.refs_0_), channel_id=1, source_target_pairs={{0,1},{1,0},{2,3},{3,2},{4,5},{5,4},{6,7},{7,6},{8,9},{9,8},{10,11... | collective-permute-start | bytes 3145736 | tf_op jit(solution)/shard_map/ppermute | solution.py:54
  140.6 2.7 %collective-permute-start.31 = (bf16[2,8,64,512]{3,2,1,0:T(8,128)(2,1)S(1)}, bf16[2,8,64,512]{3,2,1,0:T(8,128)(2,1)S(1)}, u32[]{:S(2)}, u32[]{:S(2)}) collective-permute-start(bf16[2,8,64,512]{3,2,1,0:T(8,128)(2,1)S(1)} %constant_dynamic-update-slice_fusion.16.refs_2_), channel_id=1, source_target_pairs={{0,1},{1,0},{2,3},{3,2},{4,5},{5,4},{6,7},{7,6},{8,9},{9,8},{10,11... | collective-permute-start | bytes 3145736 | tf_op jit(solution)/shard_map/ppermute | solution.py:54

commit v11 on v10

--- a/solution.py
+++ b/solution.py
@@ -15,9 +15,9 @@
 MARGIN = 16
 CHUNKS = 2
 ORDER = (
-    "top", "in0", "in1", "taps", "top", "in0", "in1", "small", "top", "in0", "in1", "small",
-    "top", "in0", "in1", "small", "top", "in0", "in1", "small", "top", "in0", "in1", "small",
-    "top", "in0", "in1", "top", "write_top", "in0", "in1", "in0", "in1", "write_in",
+    "taps", "in", "top", "small", "top", "small", "in", "top", "small", "top", "in", "top",
+    "small", "in", "top", "small", "in", "top", "in", "top", "write_top", "in", "in", "in",
+    "write_in",
 )
 SMEM_SPEC = pl.BlockSpec(memory_space=pltpu.SMEM)
 F32 = jnp.float32
@@ -451,14 +451,9 @@
     gate_ref,
     turned_ref,
     depth_ref,
-    send_ref,
-    keep_ref,
-    dconv_ref,
-    pad_ref,
-    dvalue_ref,
-    dgate_ref,
-    product_ref,
+    *refs,
 ):
+    send_ref, keep_ref, dconv_ref, pad_ref, dvalue_ref, dgate_ref, product_ref = refs[-7:]
     utterances = pad_ref.shape[1]
     frames = pad_ref.shape[2] - 2 * MARGIN
 
@@ -498,15 +493,15 @@
         write_pieces(own_ref, product_ref, send_ref, keep_ref, group)
 
 
-def inner(own, lengths, dresidual, weight_out, slope, gated, gate, turned, depth, chunk, utterances):
+def inner(own, lengths, dresidual, weight_out, slope, gated, gate, turned, depth, chunk, utterances, before):
     model, rows = turned.shape
     frames = rows // utterances
     steps = model // WIDE // CHUNKS
     first = chunk * steps
     column = pl.BlockSpec((rows, WIDE), lambda i: (0, first + i))
     piece = (2, PLACES, model // (2 * PLACES))
-    shape = jax.ShapeDtypeStruct(piece + (steps * WIDE,), BF16)
-    out = pl.BlockSpec(piece + (WIDE,), lambda i: (0, 0, 0, i))
+    shape = jax.ShapeDtypeStruct(piece + (model,), BF16)
+    out = pl.BlockSpec(piece + (WIDE,), lambda i: (0, 0, 0, first + i))
     return pl.pallas_call(
         inner_kernel,
         grid=(steps,),
@@ -521,7 +516,8 @@
             column,
             fixed(model, rows),
             pl.BlockSpec((depth.shape[0], WIDE), lambda i: (0, first + i)),
-        ],
+        ]
+        + [pl.BlockSpec(memory_space=pl.ANY)] * len(before),
         out_specs=(out, out, pl.BlockSpec((rows, WIDE), lambda i: (0, i))),
         scratch_shapes=[
             pltpu.VMEM((WIDE // LANES, utterances, frames + 2 * MARGIN, LANES), F32),
@@ -529,10 +525,11 @@
             pltpu.VMEM((rows, WIDE), BF16),
             pltpu.VMEM((model, WIDE), F32),
         ],
+        input_output_aliases={9: 0, 10: 1} if before else {},
         compiler_params=params(24),
         cost_estimate=cost(11),
         name="inner",
-    )(own, lengths, dresidual, weight_out, slope, gated, gate, turned, depth)
+    )(own, lengths, dresidual, weight_out, slope, gated, gate, turned, depth, *before)
 
 
 def taps_kernel(lengths_ref, gated_ref, *refs):
@@ -712,20 +709,18 @@
     )(own, small, mine, other, head, gain, losses)
 
 
-def unpack_inner_kernel(utts, own_ref, small_ref, weight_ref, gain_ref, *refs):
-    *piece_refs, win_ref, dgain_ref = refs
+def unpack_inner_kernel(
+    utts, own_ref, small_ref, weight_ref, gain_ref, mine_ref, other_ref, win_ref, dgain_ref
+):
     scale = utts / small_ref[small_ref.shape[0] - 1 :, 0:1]
     half = win_ref.shape[1] // 2
-    for chunk in range(CHUNKS):
-        pair = piece_refs[2 * chunk : 2 * chunk + 2]
-        width = pair[0].shape[3]
-        for group in range(2):
-            targets = ((win_ref, group * half + chunk * width, 0, width),)
-            write_rows(own_ref, pair, PLACES // 4, group, scale, targets)
+    for group in range(2):
+        targets = ((win_ref, group * half, 0, half),)
+        write_rows(own_ref, (mine_ref, other_ref), PLACES // 4, group, scale, targets)
     dgain_ref[...] = gain_row(gain_terms(weight_ref[...], win_ref[...])) / gain_ref[...]
 
 
-def unpack_inner(utts, own, small, pieces, weight, gain):
+def unpack_inner(utts, own, small, mine, other, weight, gain):
     steps = 4
     model, width = weight.shape
     rows = model // steps
@@ -740,14 +735,13 @@
         grid_spec=pltpu.PrefetchScalarGridSpec(
             num_scalar_prefetch=1,
             grid=(steps,),
-            in_specs=[fixed(*small.shape), block, row]
-            + [whole] * len(pieces),
+            in_specs=[fixed(*small.shape), block, row, whole, whole],
             out_specs=(block, row),
         ),
         compiler_params=params(24),
         cost_estimate=cost(8),
         name="unpack_inner",
-    )(own, small, weight, gain, *pieces)
+    )(own, small, weight, gain, mine, other)
 
 
 def on_device(
@@ -784,10 +778,10 @@
 
     line = Line()
 
-    def products(name, chunk):
+    def products(chunk, before):
         nonlocal dresidual
         dresidual = line.before_kernel(dresidual)
-        send, keep, dconv = inner(
+        send, keep, line.values["conv", chunk] = inner(
             own,
             lengths,
             dresidual,
@@ -799,16 +793,17 @@
             weight_depth,
             chunk,
             utterances,
+            before,
         )
-        line.begin(name, send, keep)
-        line.put(name + "_conv", dconv)
+        line.last = "conv", chunk
+        return send, keep
 
     send, keep = outer(own, active, dresidual, final, dlogits)
     send, keep, dresidual = tie((send, keep, dresidual))
     line.begin("top", send, keep)
-    products("in0", 0)
+    pieces = products(0, ())
     line.step("top", start=False)
-    products("in1", 1)
+    line.begin("in", *products(1, pieces))
     written = {}
 
     def write_top():
@@ -828,15 +823,14 @@
         line.put("by_head", by_head)
 
     def write_in():
-        pieces = [array for name in ("in0", "in1") for array in line.values[name]]
+        mine, other = line.values["in"]
         written["in"], by_in = unpack_inner(
-            utts, own, line.values["small"], pieces, weight_in, gain_conv[None]
+            utts, own, line.values["small"], mine, other, weight_in, gain_conv[None]
         )
         line.put("by_in", by_in)
 
     def sum_taps():
-        names = ("in0_conv", "in1_conv")
-        dconvs = line.after_last(tuple(line.values[name] for name in names))
+        dconvs = line.after_last(tuple(line.values["conv", chunk] for chunk in range(CHUNKS)))
         line.put("taps", tap_sums(lengths, gated, dconvs, taps, utterances))
         line.begin_small("small", line.values["taps"])
 

time: 148 us -> 163 us (1.10)
  waiting for transfers between devices: 41.9 us -> 74.7 us
  starting transfers between devices: 49.6 us -> 30.8 us
    ppermute x25 -> x18, waiting for transfers between devices: 39.9 us -> 69.8 us  [exchange(): lax.ppermute(values, ALL, [(i, i ^ bits[place ^ i % 2]) for i in range(co...]
    ppermute x25 -> x18, starting transfers between devices: 45.7 us -> 27.1 us  [exchange(): lax.ppermute(values, ALL, [(i, i ^ bits[place ^ i % 2]) for i in range(co...]
    ppermute x8 -> x6, waiting for transfers between devices: 2.05 us -> 4.89 us  [exchange(): return lax.ppermute(values, step, [(0, 1), (1, 0)])]
    ppermute x8 -> x6, starting transfers between devices: 3.9 us -> 3.76 us  [exchange(): return lax.ppermute(values, step, [(0, 1), (1, 0)])]
  transfers between devices with their start and end apart: 33 -> 24, of which waited for: 17 -> 14; matrix products, arithmetic and copies ran while one was open for 2% -> 2% of each run, Pallas kernels for 26% -> 19%
where the time goes in v11:
time: 163 us
  waiting for transfers between devices  74.7 us (46%)
  Pallas kernels  50.8 us (31%)
  starting transfers between devices  30.8 us (19%)
  other arithmetic  2.69 us (2%)
  local copies, waits for them, and re-layouts  2.63 us (2%)
    ppermute x18, waiting for transfers between devices, exchange(): lax.ppermute(values, ALL, [(i, i ^ bits[place ^ i % 2]) for i in range(co...  69.8 us
    ppermute x18, starting transfers between devices, exchange(): lax.ppermute(values, ALL, [(i, i ^ bits[place ^ i % 2]) for i in range(co...  27.1 us
    pallas_call x2, Pallas kernels, inner(): pl.pallas_call(inner_kernel, grid=(steps,), out_shape=(shape, shape, jax....  16.2 us
    pallas_call x1, Pallas kernels, forward(): pl.pallas_call(forward_kernel, grid=(steps,), out_shape=(jax.ShapeDtypeSt...  12.9 us
    pallas_call x1, Pallas kernels, tap_sums(): pl.pallas_call(taps_kernel, grid=(steps,), out_shape=jax.ShapeDtypeStruct...  6.09 us
    ppermute x6, waiting for transfers between devices, exchange(): return lax.ppermute(values, step, [(0, 1), (1, 0)])  4.89 us
    pallas_call x1, Pallas kernels, unpack_inner(): pl.pallas_call(functools.partial(unpack_inner_kernel, utts), out_shape=(j...  4.35 us
    ppermute x6, starting transfers between devices, exchange(): return lax.ppermute(values, step, [(0, 1), (1, 0)])  3.76 us
  transfers between devices with their start and end apart: 24, of which 14 were waited for; matrix products, arithmetic and copies ran while one was open for 2% of the time, Pallas kernels for 19%

profile of v11, /device:TPU:0, one launch (start us, length us, event | category | flops | bytes accessed | tf_op | source)
XLA Modules:
  0.0 162.7 jit_solution(18131159081307957450)
XLA Ops:
  0.7 1.2 copy-done.2
  2.0 1.2 teachers.1
  3.2 3.0 %collective-permute-start = (f32[2,256,256]{2,1,0:T(8,128)S(1)}, f32[2,256,256]{2,1,0:T(8,128)S(1)}, u32[]{:S(2)}, u32[]{:S(2)}) collective-permute-start(f32[2,256,256]{2,1,0:T(8,128)S(1)} %get-tuple-element.96), channel_id=1, source_target_pairs={{0,16},{16,0},{1,17},{17,1},{2,18},{18,2},{3,19},{19,3},{4,20},{20... | collective-permute-start | bytes 1572872 | tf_op jit(solution)/shard_map/ppermute | solution.py:54
  6.3 12.9 %forward.1 = (bf16[1024,512]{1,0:T(8,128)(2,1)S(1)}, f32[512,1024]{1,0:T(8,128)S(1)}, f32[512,1024]{1,0:T(8,128)S(1)}, f32[512,1024]{1,0:T(8,128)S(1)}, bf16[512...) custom-call(s32[2]{0:T(128)S(1)} %copy-done.8, bf16[512,1024]{1,0:T(8,128)(2,1)S(1)} %bitcast.9, f32[1,1024]{1,0:T(1,128)S(1)} %bitcast.12, ...), custom_call_target="tpu_custom_call" | custom-call | flops 17250000896 | bytes 1048576 | tf_op jit(solution)/shard_map/forward/pallas_call | solution.py:318
  19.2 3.4 %top.1 = (f32[2,1,128]{2,1,0:T(1,128)S(1)}, bf16[512,1024]{1,0:T(8,128)(2,1)S(1)}, bf16[512,256]{1,0:T(8,128)(2,1)S(1)}, bf16[512,1024]{1,0:T(8,128)(2,1)S(1)}) custom-call(s32[2]{0:T(128)S(1)} %copy-done.8, f32[512,1024]{1,0:T(8,128)S(1)} %get-tuple-element.92.residual_ref, f32[1,1024]{1,0:T(1,128)S(1)} %bitcast.10, bf16[1024,256]{1,0:T(8,128)(2,1)S(1)} %copy-done.4, ...), custom_call_target="tpu_custom_call" | custom-call | flops 5750000128 | bytes 1048576 | tf_op jit(solution)/shard_map/top/pallas_call | solution.py:386
  22.7 3.1 %outer.1 = (bf16[2,8,64,640]{3,2,1,0:T(8,128)(2,1)S(1)}, bf16[2,8,64,640]{3,2,1,0:T(8,128)(2,1)S(1)}) custom-call(s32[3]{0:T(128)S(1)} %pad_add_fusion.own_ref, bf16[512,1024]{1,0:T(8,128)(2,1)S(1)} %get-tuple-element.91.active_ref, bf16[512,1024]{1,0:T(8,128)(2,1)S(1)} %get-tuple-element.112.dresidual_ref, ...), custom_call_target="tpu_custom_call" | custom-call | flops 5750000128 | bytes 1048576 | tf_op jit(solution)/shard_map/outer/pallas_call | solution.py:425
  25.9 8.1 %inner.2 = (bf16[2,8,64,1024]{3,2,1,0:T(8,128)(2,1)S(1)}, bf16[2,8,64,1024]{3,2,1,0:T(8,128)(2,1)S(1)}, f32[512,512]{1,0:T(8,128)S(1)}) custom-call(s32[3]{0:T(128)S(1)} %pad_add_fusion.own_ref, s32[2]{0:T(128)S(1)} %copy-done.8, bf16[512,1024]{1,0:T(8,128)(2,1)S(1)} %get-tuple-element.112.dresidual_ref, bf16[1024,1024]{1,0:T(8,128)(2,1)S(1)} %copy-done.1, ...), custom_call_target="tpu_custom_call" | custom-call | flops 12650000384 | bytes 1048576 | tf_op jit(solution)/shard_map/inner/pallas_call | solution.py:505
  34.0 0.4 add_convert_fusion.1
  34.4 8.1 %inner.3 = (bf16[2,8,64,1024]{3,2,1,0:T(8,128)(2,1)S(1)}, bf16[2,8,64,1024]{3,2,1,0:T(8,128)(2,1)S(1)}, f32[512,512]{1,0:T(8,128)S(1)}) custom-call(s32[3]{0:T(128)S(1)} %pad_add_fusion.own_ref, s32[2]{0:T(128)S(1)} %copy-done.8, bf16[512,1024]{1,0:T(8,128)(2,1)S(1)} %get-tuple-element.112.dresidual_ref, ...), custom_call_target="tpu_custom_call", output_to_operand_aliasing={{0}: (9, {}), {1}: (10, {})} | custom-call | flops 12650000384 | bytes 1048576 | tf_op jit(solution)/shard_map/inner/pallas_call | solution.py:505
  42.5 0.5 collective-permute-start.3
  43.1 1.8 %collective-permute-start.2 = (bf16[2,4,64,640]{3,2,1,0:T(8,128)(2,1)S(1)}, bf16[2,4,64,640]{3,2,1,0:T(8,128)(2,1)S(1)}, u32[]{:S(2)}, u32[]{:S(2)}) collective-permute-start(bf16[2,4,64,640]{3,2,1,0:T(8,128)(2,1)S(1)} %slice.40), channel_id=1, source_target_pairs={{0,16},{1,3},{2,18},{3,1},{4,20},{5,7},{6,22},{7,5},{8,24},{9,11},... | collective-permute-start | bytes 1966088 | tf_op jit(solution)/shard_map/ppermute | solution.py:60
  44.9 6.1 %taps.1 = f32[32,1024]{1,0:T(8,128)S(1)} custom-call(s32[2]{0:T(128)S(1)} %copy-done.8, f32[512,1024]{1,0:T(8,128)S(1)} %get-tuple-element.106.gated_ref, f32[512,512]{1,0:T(8,128)S(1)} %get-tuple-element.119.refs_0_, f32[512,512]{1,0:T(8,128)S(1)} %get-tuple-element.120.refs_1_), custom_call_target="tpu_custom_call" | custom-call | flops 10350000128 | bytes 1048576 | tf_op jit(solution)/shard_map/taps/pallas_call | solution.py:589
  51.0 1.0 add_convert_fusion
  52.1 0.4 collective-permute-start.9
  52.5 1.3 collective-permute-done.2
  54.0 1.8 %collective-permute-start.4 = (bf16[2,2,64,640]{3,2,1,0:T(8,128)(2,1)S(1)}, bf16[2,2,64,640]{3,2,1,0:T(8,128)(2,1)S(1)}, u32[]{:S(2)}, u32[]{:S(2)}) collective-permute-start(bf16[2,2,64,640]{3,2,1,0:T(8,128)(2,1)S(1)} %slice.52), channel_id=1, source_target_pairs={{0,2},{1,17},{2,0},{3,19},{4,6},{5,21},{6,4},{7,23},{8,10},{9,25},... | collective-permute-start | bytes 983048 | tf_op jit(solution)/shard_map/ppermute | solution.py:60
  55.8 1.5 collective-permute-start.5
  57.3 14.6 %collective-permute-done.5 = f32[32,1024]{1,0:T(8,128)S(1)} collective-permute-done((f32[32,1024]{1,0:T(8,128)S(1)}, f32[32,1024]{1,0:T(8,128)S(1)}, u32[]{:S(2)}, u32[]{:S(2)}) %collective-permute-start.5) | collective-permute-done | bytes 131104 | tf_op jit(solution)/shard_map/ppermute | solution.py:60
  71.9 1.6 collective-permute-start.6
  73.6 3.3 %collective-permute-done.6 = f32[32,1024]{1,0:T(8,128)S(1)} collective-permute-done((f32[32,1024]{1,0:T(8,128)S(1)}, f32[32,1024]{1,0:T(8,128)S(1)}, u32[]{:S(2)}, u32[]{:S(2)}) %collective-permute-start.6) | collective-permute-done | bytes 131104 | tf_op jit(solution)/shard_map/ppermute | solution.py:60
  77.0 1.6 collective-permute-start.8
  78.6 0.4 add_convert_fusion.2
  79.0 3.9 %collective-permute-done.8 = bf16[2,1,64,640]{3,2,1,0:T(8,128)(2,1)S(1)} collective-permute-done((bf16[2,1,64,640]{3,2,1,0:T(8,128)(2,1)S(1)}, bf16[2,1,64,640]{3,2,1,0:T(8,128)(2,1)S(1)}, u32[]{:S(2)}, u32[]{:S(2)}) %collective-permute-start.8) | collective-permute-done | bytes 163872 | tf_op jit(solution)/shard_map/ppermute | solution.py:60
  82.9 1.1 collective-permute-start.12
  84.0 2.5 %collective-permute-start.10 = (bf16[2,1,64,640]{3,2,1,0:T(8,128)(2,1)S(1)}, bf16[2,1,64,640]{3,2,1,0:T(8,128)(2,1)S(1)}, u32[]{:S(2)}, u32[]{:S(2)}) collective-permute-start(bf16[2,1,64,640]{3,2,1,0:T(8,128)(2,1)S(1)} %add_convert_fusion.9), channel_id=1, source_target_pairs={{0,8},{1,5},{2,10},{3,7},{4,12},{5,1},{6,14},{7,3},{8,0},{9,13},{1... | collective-permute-start | bytes 491528 | tf_op jit(solution)/shard_map/ppermute | solution.py:60
  86.5 1.7 %collective-permute-start.7 = (f32[32,1024]{1,0:T(8,128)S(1)}, f32[32,1024]{1,0:T(8,128)S(1)}, u32[]{:S(2)}, u32[]{:S(2)}) collective-permute-start(f32[32,1024]{1,0:T(8,128)S(1)} %add.66), channel_id=1, source_target_pairs={{0,4},{1,9},{2,6},{3,11},{4,0},{5,13},{6,2},{7,15},{8,12},{9,1},{1... | collective-permute-start | bytes 393224 | tf_op jit(solution)/shard_map/ppermute | solution.py:60
  88.2 3.6 %collective-permute-done.7 = f32[32,1024]{1,0:T(8,128)S(1)} collective-permute-done((f32[32,1024]{1,0:T(8,128)S(1)}, f32[32,1024]{1,0:T(8,128)S(1)}, u32[]{:S(2)}, u32[]{:S(2)}) %collective-permute-start.7) | collective-permute-done | bytes 131104 | tf_op jit(solution)/shard_map/ppermute | solution.py:60
  91.8 2.8 %collective-permute-start.14 = (f32[32,1024]{1,0:T(8,128)S(1)}, f32[32,1024]{1,0:T(8,128)S(1)}, u32[]{:S(2)}, u32[]{:S(2)}) collective-permute-start(f32[32,1024]{1,0:T(8,128)S(1)} %add.69), channel_id=1, source_target_pairs={{0,8},{1,5},{2,10},{3,7},{4,12},{5,1},{6,14},{7,3},{8,0},{9,13},{1... | collective-permute-start | bytes 393224 | tf_op jit(solution)/shard_map/ppermute | solution.py:60
  94.8 0.2 add_convert_fusion.4
  95.0 2.1 %collective-permute-start.13 = (bf16[2,1,64,1024]{3,2,1,0:T(8,128)(2,1)S(1)}, bf16[2,1,64,1024]{3,2,1,0:T(8,128)(2,1)S(1)}, u32[]{:S(2)}, u32[]{:S(2)}) collective-permute-start(bf16[2,1,64,1024]{3,2,1,0:T(8,128)(2,1)S(1)} %slice.56), channel_id=1, source_target_pairs={{0,4},{1,9},{2,6},{3,11},{4,0},{5,13},{6,2},{7,15},{8,12},{9,1},{1... | collective-permute-start | bytes 786440 | tf_op jit(solution)/shard_map/ppermute | solution.py:60
  97.1 4.9 %collective-permute-done.11 = bf16[2,1,64,640]{3,2,1,0:T(8,128)(2,1)S(1)} collective-permute-done((bf16[2,1,64,640]{3,2,1,0:T(8,128)(2,1)S(1)}, bf16[2,1,64,640]{3,2,1,0:T(8,128)(2,1)S(1)}, u32[]{:S(2)}, u32[]{:S(2)}) %collective-permute-start.11) | collective-permute-done | bytes 163872 | tf_op jit(solution)/shard_map/ppermute | solution.py:60
  102.0 0.3 collective-permute-start.17
  102.3 4.6 %collective-permute-done.13 = bf16[2,1,64,1024]{3,2,1,0:T(8,128)(2,1)S(1)} collective-permute-done((bf16[2,1,64,1024]{3,2,1,0:T(8,128)(2,1)S(1)}, bf16[2,1,64,1024]{3,2,1,0:T(8,128)(2,1)S(1)}, u32[]{:S(2)}, u32[]{:S(2)}) %collective-permute-start.13) | collective-permute-done | bytes 262176 | tf_op jit(solution)/shard_map/ppermute | solution.py:60
  107.0 2.1 %collective-permute-done.17 = bf16[2,2,64,640]{3,2,1,0:T(8,128)(2,1)S(1)} collective-permute-done((bf16[2,2,64,640]{3,2,1,0:T(8,128)(2,1)S(1)}, bf16[2,2,64,640]{3,2,1,0:T(8,128)(2,1)S(1)}, u32[]{:S(2)}, u32[]{:S(2)}) %collective-permute-start.17) | collective-permute-done | bytes 327712 | tf_op jit(solution)/shard_map/ppermute | solution.py:60
  109.2 0.3 collective-permute-start.18
  109.5 3.4 %collective-permute-start.15 = (bf16[2,1,64,1024]{3,2,1,0:T(8,128)(2,1)S(1)}, bf16[2,1,64,1024]{3,2,1,0:T(8,128)(2,1)S(1)}, u32[]{:S(2)}, u32[]{:S(2)}) collective-permute-start(bf16[2,1,64,1024]{3,2,1,0:T(8,128)(2,1)S(1)} %add_convert_fusion.7), channel_id=1, source_target_pairs={{0,8},{1,5},{2,10},{3,7},{4,12},{5,1},{6,14},{7,3},{8,0},{9,13},{1... | collective-permute-start | bytes 786440 | tf_op jit(solution)/shard_map/ppermute | solution.py:60
  112.9 1.3 collective-permute-done.16
  114.3 5.8 %collective-permute-done.15 = bf16[2,1,64,1024]{3,2,1,0:T(8,128)(2,1)S(1)} collective-permute-done((bf16[2,1,64,1024]{3,2,1,0:T(8,128)(2,1)S(1)}, bf16[2,1,64,1024]{3,2,1,0:T(8,128)(2,1)S(1)}, u32[]{:S(2)}, u32[]{:S(2)}) %collective-permute-start.15) | collective-permute-done | bytes 262176 | tf_op jit(solution)/shard_map/ppermute | solution.py:60
  120.4 2.2 %collective-permute-start.20 = (bf16[2,1,64,1024]{3,2,1,0:T(8,128)(2,1)S(1)}, bf16[2,1,64,1024]{3,2,1,0:T(8,128)(2,1)S(1)}, u32[]{:S(2)}, u32[]{:S(2)}) collective-permute-start(bf16[2,1,64,1024]{3,2,1,0:T(8,128)(2,1)S(1)} %add_convert_fusion.6), channel_id=1, source_target_pairs={{0,4},{1,9},{2,6},{3,11},{4,0},{5,13},{6,2},{7,15},{8,12},{9,1},{1... | collective-permute-start | bytes 786440 | tf_op jit(solution)/shard_map/ppermute | solution.py:60
  122.5 7.2 %collective-permute-done.20 = bf16[2,1,64,1024]{3,2,1,0:T(8,128)(2,1)S(1)} collective-permute-done((bf16[2,1,64,1024]{3,2,1,0:T(8,128)(2,1)S(1)}, bf16[2,1,64,1024]{3,2,1,0:T(8,128)(2,1)S(1)}, u32[]{:S(2)}, u32[]{:S(2)}) %collective-permute-start.20) | collective-permute-done | bytes 262176 | tf_op jit(solution)/shard_map/ppermute | solution.py:60
  129.8 1.0 collective-permute-start.21
  130.8 3.5 %unpack_top.1 = (f32[1024,1024]{1,0:T(8,128)}, f32[1024,256]{1,0:T(8,128)}, f32[1,1024]{1,0:T(1,128)}, f32[31,1024]{1,0:T(8,128)}, f32[2,1,128]{2,1,0:T(1,128)S(1)}) custom-call(s32[3]{0:T(128)S(1)} %pad_add_fusion.own_ref, f32[32,1024]{1,0:T(8,128)S(1)} %add.74.small_ref, bf16[2,8,64,640]{3,2,1,0:T(8,128)(2,1)S(1)} %constant_dynamic-update-slice_fusion.4.mine_ref, ...), custom_call_target="tpu_custom_call" | custom-call | flops 5750000128 | bytes 1048576 | tf_op jit(solution)/shard_map/unpack_top/pallas_call | solution.py:678
  134.3 4.7 %collective-permute-done.21 = bf16[2,2,64,1024]{3,2,1,0:T(8,128)(2,1)S(1)} collective-permute-done((bf16[2,2,64,1024]{3,2,1,0:T(8,128)(2,1)S(1)}, bf16[2,2,64,1024]{3,2,1,0:T(8,128)(2,1)S(1)}, u32[]{:S(2)}, u32[]{:S(2)}) %collective-permute-start.21) | collective-permute-done | bytes 524320 | tf_op jit(solution)/shard_map/ppermute | solution.py:60
  139.0 1.0 collective-permute-start.22
  140.0 13.9 %collective-permute-done.22 = bf16[2,4,64,1024]{3,2,1,0:T(8,128)(2,1)S(1)} collective-permute-done((bf16[2,4,64,1024]{3,2,1,0:T(8,128)(2,1)S(1)}, bf16[2,4,64,1024]{3,2,1,0:T(8,128)(2,1)S(1)}, u32[]{:S(2)}, u32[]{:S(2)}) %collective-permute-start.22) | collective-permute-done | bytes 1048608 | tf_op jit(solution)/shard_map/ppermute | solution.py:60
  154.2 0.6 slice_reduce_fusion
  154.8 3.5 %collective-permute-done.23.other_ref = bf16[2,8,64,1024]{3,2,1,0:T(8,128)(2,1)S(1)} collective-permute-done((bf16[2,8,64,1024]{3,2,1,0:T(8,128)(2,1)S(1)}, bf16[2,8,64,1024]{3,2,1,0:T(8,128)(2,1)S(1)}, u32[]{:S(2)}, u32[]{:S(2)}) %collective-permute-start.23) | collective-permute-done | bytes 2097184 | tf_op jit(solution)/shard_map/ppermute | solution.py:54
  158.3 4.4 %unpack_inner.1 = (f32[1024,2048]{1,0:T(8,128)}, f32[1,1024]{1,0:T(1,128)}) custom-call(s32[3]{0:T(128)S(1)} %pad_add_fusion.own_ref, f32[32,1024]{1,0:T(8,128)S(1)} %add.74.small_ref, bf16[1024,2048]{1,0:T(8,128)(2,1)S(1)} %copy-done, f32[1,1024]{1,0:T(1,128)S(1)} %bitcast.13, bf16[2,8,64,1024]{3,2,1,0:T(8,128)(2,1)S(1)} %constant_dynamic-update-slice_fusion.10.mine_ref, ...), custom_call_target="tpu_custom_call" | custom-call | flops 9200000000 | bytes 1048576 | tf_op jit(solution)/shard_map/unpack_inner/pallas_call | solution.py:729
  (62 shorter events, 1.8 us)
Async XLA Ops:
  0.7 1.2 copy-start.2
  2.0 4.3 %copy-start = (bf16[1024,2048]{1,0:T(8,128)(2,1)S(1)}, bf16[1024,2048]{1,0:T(8,128)(2,1)}, u32[]{:S(2)}) copy-start(bf16[1024,2048]{1,0:T(8,128)(2,1)} %weight_ref.1) | copy-start | bytes 12582916
  2.0 4.3 %copy-start.1 = (bf16[1024,1024]{1,0:T(8,128)(2,1)S(1)}, bf16[1024,1024]{1,0:T(8,128)(2,1)}, u32[]{:S(2)}) copy-start(bf16[1024,1024]{1,0:T(8,128)(2,1)} %out_weight_ref.5) | copy-start | bytes 6291460
  2.0 4.3 %copy-start.3 = (bf16[2,256,1024]{2,1,0:T(8,128)(2,1)S(1)}, bf16[2,256,1024]{2,1,0:T(8,128)(2,1)}, u32[]{:S(2)}) copy-start(bf16[2,256,1024]{2,1,0:T(8,128)(2,1)} %param.9) | copy-start | bytes 3145732
  2.0 4.3 %copy-start.5 = (f32[31,1024]{1,0:T(8,128)S(1)}, f32[31,1024]{1,0:T(8,128)}, u32[]{:S(2)}) copy-start(f32[31,1024]{1,0:T(8,128)} %depth_ref.5) | copy-start | bytes 380932
  2.0 4.3 %copy-start.7 = (f32[1024]{0:T(1024)S(1)}, f32[1024]{0:T(1024)}, u32[]{:S(2)}) copy-start(f32[1024]{0:T(1024)} %param.12) | copy-start | bytes 12292
  2.0 4.3 %copy-start.8 = (s32[2]{0:T(128)S(1)}, s32[2]{0:T(128)}, u32[]{:S(2)}) copy-start(s32[2]{0:T(128)} %lengths_ref.9) | copy-start | bytes 28
  3.2 16.0 %collective-permute-start = (f32[2,256,256]{2,1,0:T(8,128)S(1)}, f32[2,256,256]{2,1,0:T(8,128)S(1)}, u32[]{:S(2)}, u32[]{:S(2)}) collective-permute-start(f32[2,256,256]{2,1,0:T(8,128)S(1)} %get-tuple-element.96), channel_id=1, source_target_pairs={{0,16},{16,0},{1,17},{17,1},{2,18},{18,2},{3,19},{19,3},{4,20},{20... | collective-permute-start | bytes 1572872 | tf_op jit(solution)/shard_map/ppermute | solution.py:54
  6.3 12.9 %copy-start.4 = (bf16[1024,256]{1,0:T(8,128)(2,1)S(1)}, bf16[1024,256]{1,0:T(8,128)(2,1)}, u32[]{:S(2)}) copy-start(bf16[1024,256]{1,0:T(8,128)(2,1)} %head_ref.3) | copy-start | bytes 1572868
  6.3 12.9 %copy-start.6 = (f32[1024]{0:T(1024)S(1)}, f32[1024]{0:T(1024)}, u32[]{:S(2)}) copy-start(f32[1024]{0:T(1024)} %param.16) | copy-start | bytes 12292
  25.8 8.2 %collective-permute-start.1 = (bf16[2,8,64,640]{3,2,1,0:T(8,128)(2,1)S(1)}, bf16[2,8,64,640]{3,2,1,0:T(8,128)(2,1)S(1)}, u32[]{:S(2)}, u32[]{:S(2)}) collective-permute-start(bf16[2,8,64,640]{3,2,1,0:T(8,128)(2,1)S(1)} %get-tuple-element.104), channel_id=1, source_target_pairs={{0,1},{1,0},{2,3},{3,2},{4,5},{5,4},{6,7},{7,6},{8,9},{9,8},{10,11... | collective-permute-start | bytes 3932168 | tf_op jit(solution)/shard_map/ppermute | solution.py:54
  42.5 8.5 %collective-permute-start.3 = (bf16[2,8,64,1024]{3,2,1,0:T(8,128)(2,1)S(1)}, bf16[2,8,64,1024]{3,2,1,0:T(8,128)(2,1)S(1)}, u32[]{:S(2)}, u32[]{:S(2)}) collective-permute-start(bf16[2,8,64,1024]{3,2,1,0:T(8,128)(2,1)S(1)} %get-tuple-element.116), channel_id=1, source_target_pairs={{0,1},{1,0},{2,3},{3,2},{4,5},{5,4},{6,7},{7,6},{8,9},{9,8},{10,11... | collective-permute-start | bytes 6291464 | tf_op jit(solution)/shard_map/ppermute | solution.py:54
  43.1 10.7 %collective-permute-start.2 = (bf16[2,4,64,640]{3,2,1,0:T(8,128)(2,1)S(1)}, bf16[2,4,64,640]{3,2,1,0:T(8,128)(2,1)S(1)}, u32[]{:S(2)}, u32[]{:S(2)}) collective-permute-start(bf16[2,4,64,640]{3,2,1,0:T(8,128)(2,1)S(1)} %slice.40), channel_id=1, source_target_pairs={{0,16},{1,3},{2,18},{3,1},{4,20},{5,7},{6,22},{7,5},{8,24},{9,11},... | collective-permute-start | bytes 1966088 | tf_op jit(solution)/shard_map/ppermute | solution.py:60
  52.1 26.4 %collective-permute-start.9 = (bf16[2,4,64,1024]{3,2,1,0:T(8,128)(2,1)S(1)}, bf16[2,4,64,1024]{3,2,1,0:T(8,128)(2,1)S(1)}, u32[]{:S(2)}, u32[]{:S(2)}) collective-permute-start(bf16[2,4,64,1024]{3,2,1,0:T(8,128)(2,1)S(1)} %slice.54), channel_id=1, source_target_pairs={{0,16},{1,3},{2,18},{3,1},{4,20},{5,7},{6,22},{7,5},{8,24},{9,11},... | collective-permute-start | bytes 3145736 | tf_op jit(solution)/shard_map/ppermute | solution.py:60
  54.0 19.5 %collective-permute-start.4 = (bf16[2,2,64,640]{3,2,1,0:T(8,128)(2,1)S(1)}, bf16[2,2,64,640]{3,2,1,0:T(8,128)(2,1)S(1)}, u32[]{:S(2)}, u32[]{:S(2)}) collective-permute-start(bf16[2,2,64,640]{3,2,1,0:T(8,128)(2,1)S(1)} %slice.52), channel_id=1, source_target_pairs={{0,2},{1,17},{2,0},{3,19},{4,6},{5,21},{6,4},{7,23},{8,10},{9,25},... | collective-permute-start | bytes 983048 | tf_op jit(solution)/shard_map/ppermute | solution.py:60
  55.8 16.1 %collective-permute-start.5 = (f32[32,1024]{1,0:T(8,128)S(1)}, f32[32,1024]{1,0:T(8,128)S(1)}, u32[]{:S(2)}, u32[]{:S(2)}) collective-permute-start(f32[32,1024]{1,0:T(8,128)S(1)} %taps.1), channel_id=1, source_target_pairs={{0,16},{1,3},{2,18},{3,1},{4,20},{5,7},{6,22},{7,5},{8,24},{9,11},... | collective-permute-start | bytes 393224 | tf_op jit(solution)/shard_map/ppermute | solution.py:60
  71.9 5.0 %collective-permute-start.6 = (f32[32,1024]{1,0:T(8,128)S(1)}, f32[32,1024]{1,0:T(8,128)S(1)}, u32[]{:S(2)}, u32[]{:S(2)}) collective-permute-start(f32[32,1024]{1,0:T(8,128)S(1)} %add.64), channel_id=1, source_target_pairs={{0,2},{1,17},{2,0},{3,19},{4,6},{5,21},{6,4},{7,23},{8,10},{9,25},... | collective-permute-start | bytes 393224 | tf_op jit(solution)/shard_map/ppermute | solution.py:60
  77.0 6.0 %collective-permute-start.8 = (bf16[2,1,64,640]{3,2,1,0:T(8,128)(2,1)S(1)}, bf16[2,1,64,640]{3,2,1,0:T(8,128)(2,1)S(1)}, u32[]{:S(2)}, u32[]{:S(2)}) collective-permute-start(bf16[2,1,64,640]{3,2,1,0:T(8,128)(2,1)S(1)} %slice.53), channel_id=1, source_target_pairs={{0,4},{1,9},{2,6},{3,11},{4,0},{5,13},{6,2},{7,15},{8,12},{9,1},{1... | collective-permute-start | bytes 491528 | tf_op jit(solution)/shard_map/ppermute | solution.py:60
  82.9 11.9 %collective-permute-start.12 = (bf16[2,2,64,1024]{3,2,1,0:T(8,128)(2,1)S(1)}, bf16[2,2,64,1024]{3,2,1,0:T(8,128)(2,1)S(1)}, u32[]{:S(2)}, u32[]{:S(2)}) collective-permute-start(bf16[2,2,64,1024]{3,2,1,0:T(8,128)(2,1)S(1)} %slice.55), channel_id=1, source_target_pairs={{0,2},{1,17},{2,0},{3,19},{4,6},{5,21},{6,4},{7,23},{8,10},{9,25},... | collective-permute-start | bytes 1572872 | tf_op jit(solution)/shard_map/ppermute | solution.py:60
  84.0 10.6 %collective-permute-start.10 = (bf16[2,1,64,640]{3,2,1,0:T(8,128)(2,1)S(1)}, bf16[2,1,64,640]{3,2,1,0:T(8,128)(2,1)S(1)}, u32[]{:S(2)}, u32[]{:S(2)}) collective-permute-start(bf16[2,1,64,640]{3,2,1,0:T(8,128)(2,1)S(1)} %add_convert_fusion.9), channel_id=1, source_target_pairs={{0,8},{1,5},{2,10},{3,7},{4,12},{5,1},{6,14},{7,3},{8,0},{9,13},{1... | collective-permute-start | bytes 491528 | tf_op jit(solution)/shard_map/ppermute | solution.py:60
  86.5 5.3 %collective-permute-start.7 = (f32[32,1024]{1,0:T(8,128)S(1)}, f32[32,1024]{1,0:T(8,128)S(1)}, u32[]{:S(2)}, u32[]{:S(2)}) collective-permute-start(f32[32,1024]{1,0:T(8,128)S(1)} %add.66), channel_id=1, source_target_pairs={{0,4},{1,9},{2,6},{3,11},{4,0},{5,13},{6,2},{7,15},{8,12},{9,1},{1... | collective-permute-start | bytes 393224 | tf_op jit(solution)/shard_map/ppermute | solution.py:60
  91.8 10.5 %collective-permute-start.14 = (f32[32,1024]{1,0:T(8,128)S(1)}, f32[32,1024]{1,0:T(8,128)S(1)}, u32[]{:S(2)}, u32[]{:S(2)}) collective-permute-start(f32[32,1024]{1,0:T(8,128)S(1)} %add.69), channel_id=1, source_target_pairs={{0,8},{1,5},{2,10},{3,7},{4,12},{5,1},{6,14},{7,3},{8,0},{9,13},{1... | collective-permute-start | bytes 393224 | tf_op jit(solution)/shard_map/ppermute | solution.py:60
  94.7 7.3 %collective-permute-start.11 = (bf16[2,1,64,640]{3,2,1,0:T(8,128)(2,1)S(1)}, bf16[2,1,64,640]{3,2,1,0:T(8,128)(2,1)S(1)}, u32[]{:S(2)}, u32[]{:S(2)}) collective-permute-start(bf16[2,1,64,640]{3,2,1,0:T(8,128)(2,1)S(1)} %add_convert_fusion.8), channel_id=1, source_target_pairs={{0,4},{1,9},{2,6},{3,11},{4,0},{5,13},{6,2},{7,15},{8,12},{9,1},{1... | collective-permute-start | bytes 491528 | tf_op jit(solution)/shard_map/ppermute | solution.py:60
  95.0 11.9 %collective-permute-start.13 = (bf16[2,1,64,1024]{3,2,1,0:T(8,128)(2,1)S(1)}, bf16[2,1,64,1024]{3,2,1,0:T(8,128)(2,1)S(1)}, u32[]{:S(2)}, u32[]{:S(2)}) collective-permute-start(bf16[2,1,64,1024]{3,2,1,0:T(8,128)(2,1)S(1)} %slice.56), channel_id=1, source_target_pairs={{0,4},{1,9},{2,6},{3,11},{4,0},{5,13},{6,2},{7,15},{8,12},{9,1},{1... | collective-permute-start | bytes 786440 | tf_op jit(solution)/shard_map/ppermute | solution.py:60
  102.0 7.1 %collective-permute-start.17 = (bf16[2,2,64,640]{3,2,1,0:T(8,128)(2,1)S(1)}, bf16[2,2,64,640]{3,2,1,0:T(8,128)(2,1)S(1)}, u32[]{:S(2)}, u32[]{:S(2)}) collective-permute-start(bf16[2,2,64,640]{3,2,1,0:T(8,128)(2,1)S(1)} %constant_dynamic-update-slice_fusion), channel_id=1, source_target_pairs={{0,2},{1,17},{2,0},{3,19},{4,6},{5,21},{6,4},{7,23},{8,10},{9,25},... | collective-permute-start | bytes 983048 | tf_op jit(solution)/shard_map/ppermute | solution.py:60
  109.2 11.0 %collective-permute-start.18 = (bf16[2,4,64,640]{3,2,1,0:T(8,128)(2,1)S(1)}, bf16[2,4,64,640]{3,2,1,0:T(8,128)(2,1)S(1)}, u32[]{:S(2)}, u32[]{:S(2)}) collective-permute-start(bf16[2,4,64,640]{3,2,1,0:T(8,128)(2,1)S(1)} %constant_dynamic-update-slice_fusion.2), channel_id=1, source_target_pairs={{0,16},{1,3},{2,18},{3,1},{4,20},{5,7},{6,22},{7,5},{8,24},{9,11},... | collective-permute-start | bytes 1966088 | tf_op jit(solution)/shard_map/ppermute | solution.py:60
  109.5 10.6 %collective-permute-start.15 = (bf16[2,1,64,1024]{3,2,1,0:T(8,128)(2,1)S(1)}, bf16[2,1,64,1024]{3,2,1,0:T(8,128)(2,1)S(1)}, u32[]{:S(2)}, u32[]{:S(2)}) collective-permute-start(bf16[2,1,64,1024]{3,2,1,0:T(8,128)(2,1)S(1)} %add_convert_fusion.7), channel_id=1, source_target_pairs={{0,8},{1,5},{2,10},{3,7},{4,12},{5,1},{6,14},{7,3},{8,0},{9,13},{1... | collective-permute-start | bytes 786440 | tf_op jit(solution)/shard_map/ppermute | solution.py:60
  112.9 1.3 collective-permute-start.16
  120.3 10.5 %collective-permute-start.19 = (bf16[2,8,64,640]{3,2,1,0:T(8,128)(2,1)S(1)}, bf16[2,8,64,640]{3,2,1,0:T(8,128)(2,1)S(1)}, u32[]{:S(2)}, u32[]{:S(2)}) collective-permute-start(bf16[2,8,64,640]{3,2,1,0:T(8,128)(2,1)S(1)} %constant_dynamic-update-slice_fusion.4.mine_ref), channel_id=1, source_target_pairs={{0,1},{1,0},{2,3},{3,2},{4,5},{5,4},{6,7},{7,6},{8,9},{9,8},{10,11... | collective-permute-start | bytes 3932168 | tf_op jit(solution)/shard_map/ppermute | solution.py:54
  120.4 9.4 %collective-permute-start.20 = (bf16[2,1,64,1024]{3,2,1,0:T(8,128)(2,1)S(1)}, bf16[2,1,64,1024]{3,2,1,0:T(8,128)(2,1)S(1)}, u32[]{:S(2)}, u32[]{:S(2)}) collective-permute-start(bf16[2,1,64,1024]{3,2,1,0:T(8,128)(2,1)S(1)} %add_convert_fusion.6), channel_id=1, source_target_pairs={{0,4},{1,9},{2,6},{3,11},{4,0},{5,13},{6,2},{7,15},{8,12},{9,1},{1... | collective-permute-start | bytes 786440 | tf_op jit(solution)/shard_map/ppermute | solution.py:60
  129.8 9.2 %collective-permute-start.21 = (bf16[2,2,64,1024]{3,2,1,0:T(8,128)(2,1)S(1)}, bf16[2,2,64,1024]{3,2,1,0:T(8,128)(2,1)S(1)}, u32[]{:S(2)}, u32[]{:S(2)}) collective-permute-start(bf16[2,2,64,1024]{3,2,1,0:T(8,128)(2,1)S(1)} %constant_dynamic-update-slice_fusion.6), channel_id=1, source_target_pairs={{0,2},{1,17},{2,0},{3,19},{4,6},{5,21},{6,4},{7,23},{8,10},{9,25},... | collective-permute-start | bytes 1572872 | tf_op jit(solution)/shard_map/ppermute | solution.py:60
  139.0 14.9 %collective-permute-start.22 = (bf16[2,4,64,1024]{3,2,1,0:T(8,128)(2,1)S(1)}, bf16[2,4,64,1024]{3,2,1,0:T(8,128)(2,1)S(1)}, u32[]{:S(2)}, u32[]{:S(2)}) collective-permute-start(bf16[2,4,64,1024]{3,2,1,0:T(8,128)(2,1)S(1)} %constant_dynamic-update-slice_fusion.8), channel_id=1, source_target_pairs={{0,16},{1,3},{2,18},{3,1},{4,20},{5,7},{6,22},{7,5},{8,24},{9,11},... | collective-permute-start | bytes 3145736 | tf_op jit(solution)/shard_map/ppermute | solution.py:60
  154.1 4.2 %collective-permute-start.23 = (bf16[2,8,64,1024]{3,2,1,0:T(8,128)(2,1)S(1)}, bf16[2,8,64,1024]{3,2,1,0:T(8,128)(2,1)S(1)}, u32[]{:S(2)}, u32[]{:S(2)}) collective-permute-start(bf16[2,8,64,1024]{3,2,1,0:T(8,128)(2,1)S(1)} %constant_dynamic-update-slice_fusion.10.mine_ref), channel_id=1, source_target_pairs={{0,1},{1,0},{2,3},{3,2},{4,5},{5,4},{6,7},{7,6},{8,9},{9,8},{10,11... | collective-permute-start | bytes 6291464 | tf_op jit(solution)/shard_map/ppermute | solution.py:54

commit v12 on v10

--- a/solution.py
+++ b/solution.py
@@ -14,10 +14,12 @@
 TILE = 128
 MARGIN = 16
 CHUNKS = 2
+FIRST_DIGIT = 32
+DIGITS = 12
 ORDER = (
-    "top", "in0", "in1", "taps", "top", "in0", "in1", "small", "top", "in0", "in1", "small",
-    "top", "in0", "in1", "small", "top", "in0", "in1", "small", "top", "in0", "in1", "small",
-    "top", "in0", "in1", "top", "write_top", "in0", "in1", "in0", "in1", "write_in",
+    "top", "in0", "in1", "top", "in0", "in1", "top", "in0", "in1", "top", "in0", "in1", "top",
+    "in0", "in1", "top", "in0", "in1", "top", "in0", "in1", "top", "write_top", "in0", "in1",
+    "in0", "in1", "write_in",
 )
 SMEM_SPEC = pl.BlockSpec(memory_space=pltpu.SMEM)
 F32 = jnp.float32
@@ -116,11 +118,6 @@
             ("done", CORE),
         ]
 
-    def begin_small(self, name, value):
-        self.values[name] = value
-        self.steps[name] = [("sum", step) for step in STEPS + (CORE,)]
-        self.start(name)
-
     def start(self, name):
         if not self.steps[name]:
             return
@@ -142,7 +139,7 @@
             result = (own, got)
         else:
             result = add(own, got)
-        if kind == "double" or (kind == "sum" and not self.steps[name]):
+        if kind == "double":
             result = over_rest(result)
         self.put(name, result)
         if start:
@@ -406,19 +403,21 @@
 
 
 def outer_kernel(
-    own_ref, active_ref, dresidual_ref, final_ref, dlogits_ref, send_ref, keep_ref, product_ref
+    own_ref, active_ref, dresidual_ref, final_ref, dlogits_ref, taps_ref, send_ref, keep_ref, product_ref
 ):
     width = dresidual_ref.shape[1]
     product_ref[:, :width] = dot(active_ref[...], dresidual_ref[...], 0, 0)
-    product_ref[:, width:] = dot(final_ref[...], dlogits_ref[...], 0, 0)
+    both = width + dlogits_ref.shape[1]
+    product_ref[:, width:both] = dot(final_ref[...], dlogits_ref[...], 0, 0)
+    product_ref[:, both:] = taps_ref[...]
     write_pieces(own_ref, product_ref, send_ref, keep_ref, 0)
 
 
-def outer(own, active, dresidual, final, dlogits):
+def outer(own, active, dresidual, final, dlogits, turned_taps):
     rows, model = active.shape
     half_out = dresidual.shape[1] // 2
     half_head = dlogits.shape[1] // 2
-    width = half_out + half_head
+    width = half_out + half_head + LANES
     piece = (PLACES, model // (2 * PLACES), width)
     shape = jax.ShapeDtypeStruct((2,) + piece, BF16)
     out = pl.BlockSpec((1,) + piece, lambda i: (i, 0, 0, 0))
@@ -432,28 +431,26 @@
             pl.BlockSpec((rows, half_out), lambda i: (0, i)),
             fixed(rows, model),
             pl.BlockSpec((rows, half_head), lambda i: (0, i)),
+            fixed(model, LANES),
         ],
         out_specs=(out, out),
         scratch_shapes=[pltpu.VMEM((model, width), F32)],
         compiler_params=params(20),
         cost_estimate=cost(5),
         name="outer",
-    )(own, active, dresidual, final, dlogits)
+    )(own, active, dresidual, final, dlogits, turned_taps)
 
 
 def inner_kernel(
     own_ref,
     lengths_ref,
-    dresidual_ref,
-    out_weight_ref,
-    slope_ref,
+    dconv_ref,
     gated_ref,
     gate_ref,
     turned_ref,
     depth_ref,
     send_ref,
     keep_ref,
-    dconv_ref,
     pad_ref,
     dvalue_ref,
     dgate_ref,
@@ -468,11 +465,9 @@
 
     for utterance in range(utterances):
         rows = slice(utterance * frames, (utterance + 1) * frames)
-        dconv = dot(dresidual_ref[rows, :], out_weight_ref[...], 1, 1) * slope_ref[rows, :]
-        dconv_ref[rows, :] = dconv
         for lane in range(WIDE // LANES):
-            pad_ref[lane, utterance, MARGIN : MARGIN + frames, :] = dconv[
-                :, lane * LANES : (lane + 1) * LANES
+            pad_ref[lane, utterance, MARGIN : MARGIN + frames, :] = dconv_ref[
+                rows, lane * LANES : (lane + 1) * LANES
             ]
 
     for lane in range(WIDE // LANES):
@@ -498,7 +493,7 @@
         write_pieces(own_ref, product_ref, send_ref, keep_ref, group)
 
 
-def inner(own, lengths, dresidual, weight_out, slope, gated, gate, turned, depth, chunk, utterances):
+def inner(own, lengths, dconv, gated, gate, turned, depth, chunk, utterances):
     model, rows = turned.shape
     frames = rows // utterances
     steps = model // WIDE // CHUNKS
@@ -510,19 +505,17 @@
     return pl.pallas_call(
         inner_kernel,
         grid=(steps,),
-        out_shape=(shape, shape, jax.ShapeDtypeStruct((rows, steps * WIDE), F32)),
+        out_shape=(shape, shape),
         in_specs=[
             SMEM_SPEC,
             SMEM_SPEC,
-            fixed(rows, model),
-            pl.BlockSpec((WIDE, model), lambda i: (first + i, 0)),
             column,
             column,
             column,
             fixed(model, rows),
             pl.BlockSpec((depth.shape[0], WIDE), lambda i: (0, first + i)),
         ],
-        out_specs=(out, out, pl.BlockSpec((rows, WIDE), lambda i: (0, i))),
+        out_specs=(out, out),
         scratch_shapes=[
             pltpu.VMEM((WIDE // LANES, utterances, frames + 2 * MARGIN, LANES), F32),
             pltpu.VMEM((rows, WIDE), BF16),
@@ -532,78 +525,88 @@
         compiler_params=params(24),
         cost_estimate=cost(11),
         name="inner",
-    )(own, lengths, dresidual, weight_out, slope, gated, gate, turned, depth)
-
-
-def taps_kernel(lengths_ref, gated_ref, *refs):
-    *dconv_refs, out_ref, pad_ref, sums_ref = refs
+    )(own, lengths, dconv, gated, gate, turned, depth)
+
+
+def taps_kernel(
+    lengths_ref,
+    dresidual_ref,
+    out_weight_ref,
+    slope_ref,
+    gated_ref,
+    dconv_ref,
+    turned_ref,
+    pad_ref,
+    sums_ref,
+    wide_ref,
+):
+    taps = sums_ref.shape[0]
     utterances = pad_ref.shape[1]
     frames = pad_ref.shape[2] - 2 * MARGIN
-    taps = out_ref.shape[0] - 1
-    step = pl.program_id(0)
-    per_chunk = pl.num_programs(0) // len(dconv_refs)
     valid = lengths_ref[0]
     for utterance in range(1, utterances):
         valid = valid + lengths_ref[utterance]
 
-    @pl.when(step == 0)
+    @pl.when(pl.program_id(0) == 0)
     def _():
         clear_margins(pad_ref)
+        wide_ref[...] = jnp.zeros_like(wide_ref)
+        for digit in range(DIGITS):
+            row = FIRST_DIGIT + digit
+            wide_ref[row : row + 1, :] = jnp.zeros((1, WIDE), F32) + ((valid >> digit) & 1).astype(F32)
+
+    for utterance in range(utterances):
+        rows = slice(utterance * frames, (utterance + 1) * frames)
+        dconv_ref[rows, :] = dot(dresidual_ref[rows, :], out_weight_ref[...], 1, 1) * slope_ref[rows, :]
+        for lane in range(WIDE // LANES):
+            pad_ref[lane, utterance, MARGIN : MARGIN + frames, :] = gated_ref[
+                rows, lane * LANES : (lane + 1) * LANES
+            ]
 
     for lane in range(WIDE // LANES):
         columns = slice(lane * LANES, (lane + 1) * LANES)
-        for utterance in range(utterances):
-            rows = slice(utterance * frames, (utterance + 1) * frames)
-            pad_ref[lane, utterance, MARGIN : MARGIN + frames, :] = gated_ref[rows, columns]
-
-    for chunk, dconv_ref in enumerate(dconv_refs):
-
-        @pl.when(step // per_chunk == chunk)
-        def _(dconv_ref=dconv_ref):
-            for lane in range(WIDE // LANES):
-                columns = slice(lane * LANES, (lane + 1) * LANES)
-                sums_ref[...] = jnp.zeros_like(sums_ref)
-
-                def one(utterance, carry, lane=lane, columns=columns):
-                    for start in range(0, frames, TILE):
-                        rows = pl.ds(pl.multiple_of(utterance * frames + start, TILE), TILE)
-                        dconv = dconv_ref[rows, columns]
-                        for tap, view in shifted_views(pad_ref, lane, utterance, start, taps):
-                            sums_ref[tap] += jnp.sum(
-                                (view * dconv).reshape(TILE // 8, 8, LANES), axis=0
-                            )
-                    return carry
-
-                lax.fori_loop(0, utterances, one, 0)
-                out_ref[:taps, columns] = jnp.sum(sums_ref[...], axis=1)
-
-    out_ref[taps:, :] = jnp.zeros((1, WIDE), F32) + valid.astype(F32)
-
-
-def tap_sums(lengths, gated, dconvs, taps, utterances):
+        sums_ref[...] = jnp.zeros_like(sums_ref)
+
+        def one(utterance, carry, lane=lane, columns=columns):
+            for start in range(0, frames, TILE):
+                rows = pl.ds(pl.multiple_of(utterance * frames + start, TILE), TILE)
+                dconv = dconv_ref[rows, columns]
+                for tap, view in shifted_views(pad_ref, lane, utterance, start, taps):
+                    sums_ref[tap] += jnp.sum((view * dconv).reshape(TILE // 8, 8, LANES), axis=0)
+            return carry
+
+        lax.fori_loop(0, utterances, one, 0)
+        wide_ref[:taps, columns] = jnp.sum(sums_ref[...], axis=1)
+    turned_ref[...] = wide_ref[...].T
+
+
+def tap_sums(lengths, dresidual, weight_out, slope, gated, taps, utterances):
     rows, model = gated.shape
-    steps = model // WIDE
-    per_chunk = steps // len(dconvs)
-
-    def part(chunk):
-        low = chunk * per_chunk
-        return pl.BlockSpec((rows, WIDE), lambda i: (0, jnp.clip(i - low, 0, per_chunk - 1)))
-
+    column = pl.BlockSpec((rows, WIDE), lambda i: (0, i))
     return pl.pallas_call(
         taps_kernel,
-        grid=(steps,),
-        out_shape=jax.ShapeDtypeStruct((taps + 1, model), F32),
-        in_specs=[SMEM_SPEC, pl.BlockSpec((rows, WIDE), lambda i: (0, i))]
-        + [part(chunk) for chunk in range(len(dconvs))],
-        out_specs=pl.BlockSpec((taps + 1, WIDE), lambda i: (0, i)),
+        grid=(model // WIDE,),
+        out_shape=(
+            jax.ShapeDtypeStruct((rows, model), F32),
+            jax.ShapeDtypeStruct((model, LANES), F32),
+        ),
+        in_specs=[
+            SMEM_SPEC,
+            fixed(rows, model),
+            pl.BlockSpec((WIDE, model), lambda i: (i, 0)),
+            column,
+            column,
+        ],
+        out_specs=(column, pl.BlockSpec((WIDE, LANES), lambda i: (i, 0))),
         scratch_shapes=[
             pltpu.VMEM((WIDE // LANES, utterances, rows // utterances + 2 * MARGIN, LANES), F32),
             pltpu.VMEM((taps, 8, LANES), F32),
+            pltpu.VMEM((LANES, WIDE), F32),
         ],
-        compiler_params=params(16),
-        cost_estimate=cost(9),
+        compiler_params=params(20),
+        cost_estimate=cost(8),
         name="taps",
-    )(lengths, gated, *dconvs)
+    )(lengths, dresidual, weight_out, slope, gated)
 
 
 def gain_terms(weight, grad):
@@ -641,7 +644,6 @@
 def unpack_top_kernel(
     utts,
     own_ref,
-    small_ref,
     mine_ref,
     other_ref,
     head_ref,
@@ -652,27 +654,36 @@
     dgain_ref,
     depth_ref,
     loss_ref,
+    scale_ref,
+    turned_ref,
 ):
-    taps = depth_ref.shape[0]
-    scale = utts / small_ref[taps:, 0:1]
     half_out = wout_ref.shape[1] // 2
     half_head = dhead_ref.shape[1] // 2
+    both = half_out + half_head
+    digits = mine_ref[0, 0, 0:16, both:].astype(F32)[0:1, :]
+    total = digits[:, FIRST_DIGIT : FIRST_DIGIT + 1]
+    for digit in range(1, DIGITS):
+        lane = FIRST_DIGIT + digit
+        total = total + digits[:, lane : lane + 1] * float(1 << digit)
+    scale = utts / total
     for group in range(2):
-        targets = (
+        targets = [
             (wout_ref, group * half_out, 0, half_out),
             (dhead_ref, group * half_head, half_out, half_head),
-        )
+        ]
+        if group == 0:
+            targets.append((turned_ref, 0, both, LANES))
         write_rows(own_ref, (mine_ref, other_ref), PLACES // 4, group, scale, targets)
     dgain_ref[...] = gain_row(gain_terms(head_ref[...], dhead_ref[...])) / gain_ref[...]
-    depth_ref[...] = small_ref[:taps, :] * scale
+    depth_ref[...] = turned_ref[...].T[: depth_ref.shape[0], :]
     loss_ref[...] = losses_ref[...] * scale[None]
-
-
-def unpack_top(utts, own, small, mine, other, head, gain, losses, width_out):
+    scale_ref[...] = jnp.broadcast_to(scale, scale_ref.shape)
+
+
+def unpack_top(utts, own, mine, other, head, gain, losses, width_out, taps):
     steps = 4
     model, symbols = head.shape
     rows = model // steps
-    taps = small.shape[0] - 1
     row = pl.BlockSpec((1, rows), lambda i, own_ref: (0, i))
 
     def block(width):
@@ -686,35 +697,31 @@
             jax.ShapeDtypeStruct((1, model), F32),
             jax.ShapeDtypeStruct((taps, model), F32),
             jax.ShapeDtypeStruct(losses.shape, F32),
+            jax.ShapeDtypeStruct((8, LANES), F32),
         ),
         grid_spec=pltpu.PrefetchScalarGridSpec(
             num_scalar_prefetch=1,
             grid=(steps,),
-            in_specs=[
-                fixed(*small.shape),
-                whole,
-                whole,
-                block(symbols),
-                row,
-                fixed(*losses.shape),
-            ],
+            in_specs=[whole, whole, block(symbols), row, fixed(*losses.shape)],
             out_specs=(
                 block(width_out),
                 block(symbols),
                 row,
-                fixed(taps, model),
+                pl.BlockSpec((taps, rows), lambda i, own_ref: (0, i)),
                 fixed(*losses.shape),
+                fixed(8, LANES),
             ),
+            scratch_shapes=[pltpu.VMEM((rows, LANES), F32)],
         ),
         compiler_params=params(20),
-        cost_estimate=cost(5),
+        cost_estimate=cost(4),
         name="unpack_top",
-    )(own, small, mine, other, head, gain, losses)
-
-
-def unpack_inner_kernel(utts, own_ref, small_ref, weight_ref, gain_ref, *refs):
+    )(own, mine, other, head, gain, losses)
+
+
+def unpack_inner_kernel(own_ref, scale_ref, weight_ref, gain_ref, *refs):
     *piece_refs, win_ref, dgain_ref = refs
-    scale = utts / small_ref[small_ref.shape[0] - 1 :, 0:1]
+    scale = scale_ref[0:1, 0:1]
     half = win_ref.shape[1] // 2
     for chunk in range(CHUNKS):
         pair = piece_refs[2 * chunk : 2 * chunk + 2]
@@ -725,14 +732,14 @@
     dgain_ref[...] = gain_row(gain_terms(weight_ref[...], win_ref[...])) / gain_ref[...]
 
 
-def unpack_inner(utts, own, small, pieces, weight, gain):
+def unpack_inner(own, scale, pieces, weight, gain):
     steps = 4
     model, width = weight.shape
     rows = model // steps
     row = pl.BlockSpec((1, rows), lambda i, own_ref: (0, i))
     block = pl.BlockSpec((rows, width), lambda i, own_ref: (i, 0))
     return pl.pallas_call(
-        functools.partial(unpack_inner_kernel, utts),
+        unpack_inner_kernel,
         out_shape=(
             jax.ShapeDtypeStruct((model, width), F32),
             jax.ShapeDtypeStruct((1, model), F32),
@@ -740,14 +747,13 @@
         grid_spec=pltpu.PrefetchScalarGridSpec(
             num_scalar_prefetch=1,
             grid=(steps,),
-            in_specs=[fixed(*small.shape), block, row]
-            + [whole] * len(pieces),
+            in_specs=[fixed(*scale.shape), block, row] + [whole] * len(pieces),
             out_specs=(block, row),
         ),
         compiler_params=params(24),
         cost_estimate=cost(8),
         name="unpack_inner",
-    )(own, small, weight, gain, *pieces)
+    )(own, scale, weight, gain, *pieces)
 
 
 def on_device(
@@ -785,26 +791,19 @@
     line = Line()
 
     def products(name, chunk):
-        nonlocal dresidual
-        dresidual = line.before_kernel(dresidual)
-        send, keep, dconv = inner(
-            own,
-            lengths,
-            dresidual,
-            weight_out,
-            slope,
-            gated,
-            gate,
-            turned,
-            weight_depth,
-            chunk,
-            utterances,
+        nonlocal dconv
+        dconv = line.before_kernel(dconv)
+        send, keep = inner(
+            own, lengths, dconv, gated, gate, turned, weight_depth, chunk, utterances
         )
         line.begin(name, send, keep)
-        line.put(name + "_conv", dconv)
-
-    send, keep = outer(own, active, dresidual, final, dlogits)
-    send, keep, dresidual = tie((send, keep, dresidual))
+        line.last = name
+
+    dconv, turned_taps = tap_sums(
+        lengths, dresidual, weight_out, slope, gated, taps, utterances
+    )
+    send, keep = outer(own, active, dresidual, final, dlogits, turned_taps)
+    send, keep, dconv = tie((send, keep, dconv))
     line.begin("top", send, keep)
     products("in0", 0)
     line.step("top", start=False)
@@ -813,38 +812,28 @@
 
     def write_top():
         mine, other = line.values["top"]
-        *rest, written["losses"] = unpack_top(
+        written["out"], written["head"], by_head, *rest = unpack_top(
             utts,
             own,
-            line.values["small"],
             line.after_last(mine),
             other,
             head_weight,
             gain_out[None],
             losses,
             weight_out.shape[1],
+            taps,
         )
-        written["out"], written["head"], by_head, written["depth"] = rest
+        written["depth"], written["losses"], written["scale"] = rest
         line.put("by_head", by_head)
 
     def write_in():
         pieces = [array for name in ("in0", "in1") for array in line.values[name]]
         written["in"], by_in = unpack_inner(
-            utts, own, line.values["small"], pieces, weight_in, gain_conv[None]
+            own, written["scale"], pieces, weight_in, gain_conv[None]
         )
         line.put("by_in", by_in)
 
-    def sum_taps():
-        names = ("in0_conv", "in1_conv")
-        dconvs = line.after_last(tuple(line.values[name] for name in names))
-        line.put("taps", tap_sums(lengths, gated, dconvs, taps, utterances))
-        line.begin_small("small", line.values["taps"])
-
-    kernels = {
-        "taps": sum_taps,
-        "write_top": write_top,
-        "write_in": write_in,
-    }
+    kernels = {"write_top": write_top, "write_in": write_in}
     for name in ORDER:
         if name in kernels:
             kernels[name]()

time: 148 us -> 155 us (1.047); the launches traced: 148 us -> 152 us
  waiting for transfers between devices: 41.9 us -> 51.5 us
  starting transfers between devices: 49.6 us -> 43.2 us
    ppermute x25 -> x21, waiting for transfers between devices: 39.9 us -> 49.4 us  [exchange(): lax.ppermute(values, ALL, [(i, i ^ bits[place ^ i % 2]) for i in range(co...]
    ppermute x25 -> x21, starting transfers between devices: 45.7 us -> 39.3 us  [exchange(): lax.ppermute(values, ALL, [(i, i ^ bits[place ^ i % 2]) for i in range(co...]
    ppermute x8 -> x7, starting transfers between devices: 3.9 us -> 3.9 us  [exchange(): return lax.ppermute(values, step, [(0, 1), (1, 0)])]
  transfers between devices with their start and end apart: 33 -> 28, of which waited for: 17 -> 14; matrix products, arithmetic and copies ran while one was open for 2% -> 2% of each run, Pallas kernels for 26% -> 20%
where the time goes in v12:
time: 155 us; the launch traced here: 152 us
  waiting for transfers between devices  51.5 us (33%)
  Pallas kernels  51.3 us (33%)
  starting transfers between devices  43.2 us (28%)
  local copies, waits for them, and re-layouts  2.54 us (2%)
  other arithmetic  2.16 us (1%)
    ppermute x21, waiting for transfers between devices, exchange(): lax.ppermute(values, ALL, [(i, i ^ bits[place ^ i % 2]) for i in range(co...  49.4 us
    ppermute x21, starting transfers between devices, exchange(): lax.ppermute(values, ALL, [(i, i ^ bits[place ^ i % 2]) for i in range(co...  39.3 us
    pallas_call x2, Pallas kernels, inner(): pl.pallas_call(inner_kernel, grid=(steps,), out_shape=(shape, shape), in_...  14.1 us
    pallas_call x1, Pallas kernels, forward(): pl.pallas_call(forward_kernel, grid=(steps,), out_shape=(jax.ShapeDtypeSt...  12.9 us
    pallas_call x1, Pallas kernels, tap_sums(): pl.pallas_call(taps_kernel, grid=(model // WIDE,), out_shape=(jax.ShapeDt...  8.19 us
    pallas_call x1, Pallas kernels, unpack_inner(): pl.pallas_call(unpack_inner_kernel, out_shape=(jax.ShapeDtypeStruct((mode...  4.25 us
    pallas_call x1, Pallas kernels, unpack_top(): pl.pallas_call(functools.partial(unpack_top_kernel, utts), out_shape=(jax...  4.02 us
    ppermute x7, starting transfers between devices, exchange(): return lax.ppermute(values, step, [(0, 1), (1, 0)])  3.9 us
  transfers between devices with their start and end apart: 28, of which 14 were waited for; matrix products, arithmetic and copies ran while one was open for 2% of the time, Pallas kernels for 20%

profile of v12, /device:TPU:0, one launch (start us, length us, event | category | flops | bytes accessed | tf_op | source)
XLA Modules:
  0.0 151.8 jit_solution(10000176788743717571)
XLA Ops:
  0.7 1.2 copy-done.2
  2.0 1.2 teachers.1
  3.2 3.0 %collective-permute-start = (f32[2,256,256]{2,1,0:T(8,128)S(1)}, f32[2,256,256]{2,1,0:T(8,128)S(1)}, u32[]{:S(2)}, u32[]{:S(2)}) collective-permute-start(f32[2,256,256]{2,1,0:T(8,128)S(1)} %get-tuple-element.105), channel_id=1, source_target_pairs={{0,16},{16,0},{1,17},{17,1},{2,18},{18,2},{3,19},{19,3},{4,20},{20... | collective-permute-start | bytes 1572872 | tf_op jit(solution)/shard_map/ppermute | solution.py:56
  6.3 12.9 %forward.1 = (bf16[1024,512]{1,0:T(8,128)(2,1)S(1)}, f32[512,1024]{1,0:T(8,128)S(1)}, f32[512,1024]{1,0:T(8,128)S(1)}, f32[512,1024]{1,0:T(8,128)S(1)}, bf16[512...) custom-call(s32[2]{0:T(128)S(1)} %copy-done.8, bf16[512,1024]{1,0:T(8,128)(2,1)S(1)} %bitcast.9, f32[1,1024]{1,0:T(1,128)S(1)} %bitcast.12, ...), custom_call_target="tpu_custom_call" | custom-call | flops 17250000896 | bytes 1048576 | tf_op jit(solution)/shard_map/forward/pallas_call | solution.py:315
  19.2 3.4 %top.1 = (f32[2,1,128]{2,1,0:T(1,128)S(1)}, bf16[512,1024]{1,0:T(8,128)(2,1)S(1)}, bf16[512,256]{1,0:T(8,128)(2,1)S(1)}, bf16[512,1024]{1,0:T(8,128)(2,1)S(1)}) custom-call(s32[2]{0:T(128)S(1)} %copy-done.8, f32[512,1024]{1,0:T(8,128)S(1)} %get-tuple-element.101.residual_ref, f32[1,1024]{1,0:T(1,128)S(1)} %bitcast.10, bf16[1024,256]{1,0:T(8,128)(2,1)S(1)} %copy-done.4, ...), custom_call_target="tpu_custom_call" | custom-call | flops 5750000128 | bytes 1048576 | tf_op jit(solution)/shard_map/top/pallas_call | solution.py:383
  22.7 8.2 %taps.1 = (f32[512,1024]{1,0:T(8,128)S(1)}, f32[1024,128]{1,0:T(8,128)S(1)}) custom-call(s32[2]{0:T(128)S(1)} %copy-done.8, bf16[512,1024]{1,0:T(8,128)(2,1)S(1)} %get-tuple-element.106.dresidual_ref, bf16[1024,1024]{1,0:T(8,128)(2,1)S(1)} %copy-done.1, f32[512,1024]{1,0:T(8,128)S(1)} %get-tuple-element.109.slope_ref, ...), custom_call_target="tpu_custom_call" | custom-call | flops 9200000000 | bytes 1048576 | tf_op jit(solution)/shard_map/taps/pallas_call | solution.py:586
  30.9 3.2 %outer.1 = (bf16[2,8,64,768]{3,2,1,0:T(8,128)(2,1)S(1)}, bf16[2,8,64,768]{3,2,1,0:T(8,128)(2,1)S(1)}) custom-call(s32[3]{0:T(128)S(1)} %pad_add_fusion.own_ref, bf16[512,1024]{1,0:T(8,128)(2,1)S(1)} %get-tuple-element.100.active_ref, bf16[512,1024]{1,0:T(8,128)(2,1)S(1)} %get-tuple-element.106.dresidual_ref, ...), custom_call_target="tpu_custom_call" | custom-call | flops 5750000128 | bytes 1048576 | tf_op jit(solution)/shard_map/outer/pallas_call | solution.py:424
  34.1 7.0 %inner.2 = (bf16[2,8,64,512]{3,2,1,0:T(8,128)(2,1)S(1)}, bf16[2,8,64,512]{3,2,1,0:T(8,128)(2,1)S(1)}) custom-call(s32[3]{0:T(128)S(1)} %pad_add_fusion.own_ref, s32[2]{0:T(128)S(1)} %copy-done.8, f32[512,1024]{1,0:T(8,128)S(1)} %get-tuple-element.125.dconv_ref, f32[512,1024]{1,0:T(8,128)S(1)} %get-tuple-element.110.gated_ref, ...), custom_call_target="tpu_custom_call" | custom-call | flops 12650000384 | bytes 1048576 | tf_op jit(solution)/shard_map/inner/pallas_call | solution.py:505
  41.1 0.5 collective-permute-start.2
  41.7 0.5 add_convert_fusion
  42.2 1.8 %collective-permute-start.3 = (bf16[2,4,64,768]{3,2,1,0:T(8,128)(2,1)S(1)}, bf16[2,4,64,768]{3,2,1,0:T(8,128)(2,1)S(1)}, u32[]{:S(2)}, u32[]{:S(2)}) collective-permute-start(bf16[2,4,64,768]{3,2,1,0:T(8,128)(2,1)S(1)} %slice.58), channel_id=1, source_target_pairs={{0,16},{1,3},{2,18},{3,1},{4,20},{5,7},{6,22},{7,5},{8,24},{9,11},... | collective-permute-start | bytes 2359304 | tf_op jit(solution)/shard_map/ppermute | solution.py:62
  44.0 7.1 %inner.3 = (bf16[2,8,64,512]{3,2,1,0:T(8,128)(2,1)S(1)}, bf16[2,8,64,512]{3,2,1,0:T(8,128)(2,1)S(1)}) custom-call(s32[3]{0:T(128)S(1)} %pad_add_fusion.own_ref, s32[2]{0:T(128)S(1)} %copy-done.8, f32[512,1024]{1,0:T(8,128)S(1)} %get-tuple-element.125.dconv_ref, f32[512,1024]{1,0:T(8,128)S(1)} %get-tuple-element.110.gated_ref, ...), custom_call_target="tpu_custom_call" | custom-call | flops 12650000384 | bytes 1048576 | tf_op jit(solution)/shard_map/inner/pallas_call | solution.py:505
  51.2 3.0 %collective-permute-done.3 = bf16[2,4,64,768]{3,2,1,0:T(8,128)(2,1)S(1)} collective-permute-done((bf16[2,4,64,768]{3,2,1,0:T(8,128)(2,1)S(1)}, bf16[2,4,64,768]{3,2,1,0:T(8,128)(2,1)S(1)}, u32[]{:S(2)}, u32[]{:S(2)}) %collective-permute-start.3) | collective-permute-done | bytes 786464 | tf_op jit(solution)/shard_map/ppermute | solution.py:62
  54.5 1.8 %collective-permute-start.5 = (bf16[2,2,64,768]{3,2,1,0:T(8,128)(2,1)S(1)}, bf16[2,2,64,768]{3,2,1,0:T(8,128)(2,1)S(1)}, u32[]{:S(2)}, u32[]{:S(2)}) collective-permute-start(bf16[2,2,64,768]{3,2,1,0:T(8,128)(2,1)S(1)} %slice.77), channel_id=1, source_target_pairs={{0,2},{1,17},{2,0},{3,19},{4,6},{5,21},{6,4},{7,23},{8,10},{9,25},... | collective-permute-start | bytes 1179656 | tf_op jit(solution)/shard_map/ppermute | solution.py:62
  56.3 0.3 add_convert_fusion.2
  56.7 1.6 %collective-permute-start.4 = (bf16[2,4,64,512]{3,2,1,0:T(8,128)(2,1)S(1)}, bf16[2,4,64,512]{3,2,1,0:T(8,128)(2,1)S(1)}, u32[]{:S(2)}, u32[]{:S(2)}) collective-permute-start(bf16[2,4,64,512]{3,2,1,0:T(8,128)(2,1)S(1)} %slice.76), channel_id=1, source_target_pairs={{0,16},{1,3},{2,18},{3,1},{4,20},{5,7},{6,22},{7,5},{8,24},{9,11},... | collective-permute-start | bytes 1572872 | tf_op jit(solution)/shard_map/ppermute | solution.py:62
  58.3 0.3 add_convert_fusion.1
  58.6 0.6 collective-permute-start.8
  59.2 7.2 %collective-permute-done.5 = bf16[2,2,64,768]{3,2,1,0:T(8,128)(2,1)S(1)} collective-permute-done((bf16[2,2,64,768]{3,2,1,0:T(8,128)(2,1)S(1)}, bf16[2,2,64,768]{3,2,1,0:T(8,128)(2,1)S(1)}, u32[]{:S(2)}, u32[]{:S(2)}) %collective-permute-start.5) | collective-permute-done | bytes 393248 | tf_op jit(solution)/shard_map/ppermute | solution.py:62
  66.6 2.0 %collective-permute-start.7 = (bf16[2,1,64,768]{3,2,1,0:T(8,128)(2,1)S(1)}, bf16[2,1,64,768]{3,2,1,0:T(8,128)(2,1)S(1)}, u32[]{:S(2)}, u32[]{:S(2)}) collective-permute-start(bf16[2,1,64,768]{3,2,1,0:T(8,128)(2,1)S(1)} %slice.78), channel_id=1, source_target_pairs={{0,4},{1,9},{2,6},{3,11},{4,0},{5,13},{6,2},{7,15},{8,12},{9,1},{1... | collective-permute-start | bytes 589832 | tf_op jit(solution)/shard_map/ppermute | solution.py:62
  68.8 1.6 %collective-permute-start.11 = (bf16[2,2,64,512]{3,2,1,0:T(8,128)(2,1)S(1)}, bf16[2,2,64,512]{3,2,1,0:T(8,128)(2,1)S(1)}, u32[]{:S(2)}, u32[]{:S(2)}) collective-permute-start(bf16[2,2,64,512]{3,2,1,0:T(8,128)(2,1)S(1)} %slice.81), channel_id=1, source_target_pairs={{0,2},{1,17},{2,0},{3,19},{4,6},{5,21},{6,4},{7,23},{8,10},{9,25},... | collective-permute-start | bytes 786440 | tf_op jit(solution)/shard_map/ppermute | solution.py:62
  70.3 2.9 %collective-permute-done.8 = bf16[2,4,64,512]{3,2,1,0:T(8,128)(2,1)S(1)} collective-permute-done((bf16[2,4,64,512]{3,2,1,0:T(8,128)(2,1)S(1)}, bf16[2,4,64,512]{3,2,1,0:T(8,128)(2,1)S(1)}, u32[]{:S(2)}, u32[]{:S(2)}) %collective-permute-start.8) | collective-permute-done | bytes 524320 | tf_op jit(solution)/shard_map/ppermute | solution.py:62
  73.4 1.4 collective-permute-start.10
  74.8 2.7 %collective-permute-start.9 = (bf16[2,1,64,768]{3,2,1,0:T(8,128)(2,1)S(1)}, bf16[2,1,64,768]{3,2,1,0:T(8,128)(2,1)S(1)}, u32[]{:S(2)}, u32[]{:S(2)}) collective-permute-start(bf16[2,1,64,768]{3,2,1,0:T(8,128)(2,1)S(1)} %add_convert_fusion.10), channel_id=1, source_target_pairs={{0,8},{1,5},{2,10},{3,7},{4,12},{5,1},{6,14},{7,3},{8,0},{9,13},{1... | collective-permute-start | bytes 589832 | tf_op jit(solution)/shard_map/ppermute | solution.py:62
  77.6 1.6 %collective-permute-start.13 = (bf16[2,1,64,512]{3,2,1,0:T(8,128)(2,1)S(1)}, bf16[2,1,64,512]{3,2,1,0:T(8,128)(2,1)S(1)}, u32[]{:S(2)}, u32[]{:S(2)}) collective-permute-start(bf16[2,1,64,512]{3,2,1,0:T(8,128)(2,1)S(1)} %slice.83), channel_id=1, source_target_pairs={{0,4},{1,9},{2,6},{3,11},{4,0},{5,13},{6,2},{7,15},{8,12},{9,1},{1... | collective-permute-start | bytes 393224 | tf_op jit(solution)/shard_map/ppermute | solution.py:62
  79.2 0.6 collective-permute-done.10
  79.9 4.4 %collective-permute-done.9 = bf16[2,1,64,768]{3,2,1,0:T(8,128)(2,1)S(1)} collective-permute-done((bf16[2,1,64,768]{3,2,1,0:T(8,128)(2,1)S(1)}, bf16[2,1,64,768]{3,2,1,0:T(8,128)(2,1)S(1)}, u32[]{:S(2)}, u32[]{:S(2)}) %collective-permute-start.9) | collective-permute-done | bytes 196640 | tf_op jit(solution)/shard_map/ppermute | solution.py:62
  84.4 2.7 %collective-permute-start.16 = (bf16[2,1,64,768]{3,2,1,0:T(8,128)(2,1)S(1)}, bf16[2,1,64,768]{3,2,1,0:T(8,128)(2,1)S(1)}, u32[]{:S(2)}, u32[]{:S(2)}) collective-permute-start(bf16[2,1,64,768]{3,2,1,0:T(8,128)(2,1)S(1)} %add_convert_fusion.9), channel_id=1, source_target_pairs={{0,4},{1,9},{2,6},{3,11},{4,0},{5,13},{6,2},{7,15},{8,12},{9,1},{1... | collective-permute-start | bytes 589832 | tf_op jit(solution)/shard_map/ppermute | solution.py:62
  87.1 1.0 collective-permute-start.12
  88.1 2.7 %collective-permute-start.15 = (bf16[2,1,64,512]{3,2,1,0:T(8,128)(2,1)S(1)}, bf16[2,1,64,512]{3,2,1,0:T(8,128)(2,1)S(1)}, u32[]{:S(2)}, u32[]{:S(2)}) collective-permute-start(bf16[2,1,64,512]{3,2,1,0:T(8,128)(2,1)S(1)} %add_convert_fusion.14), channel_id=1, source_target_pairs={{0,8},{1,5},{2,10},{3,7},{4,12},{5,1},{6,14},{7,3},{8,0},{9,13},{1... | collective-permute-start | bytes 393224 | tf_op jit(solution)/shard_map/ppermute | solution.py:62
  90.8 7.7 %collective-permute-done.12 = bf16[2,1,64,512]{3,2,1,0:T(8,128)(2,1)S(1)} collective-permute-done((bf16[2,1,64,512]{3,2,1,0:T(8,128)(2,1)S(1)}, bf16[2,1,64,512]{3,2,1,0:T(8,128)(2,1)S(1)}, u32[]{:S(2)}, u32[]{:S(2)}) %collective-permute-start.12) | collective-permute-done | bytes 131104 | tf_op jit(solution)/shard_map/ppermute | solution.py:62
  98.5 3.0 %collective-permute-start.14 = (bf16[2,1,64,512]{3,2,1,0:T(8,128)(2,1)S(1)}, bf16[2,1,64,512]{3,2,1,0:T(8,128)(2,1)S(1)}, u32[]{:S(2)}, u32[]{:S(2)}) collective-permute-start(bf16[2,1,64,512]{3,2,1,0:T(8,128)(2,1)S(1)} %add_convert_fusion.13), channel_id=1, source_target_pairs={{0,8},{1,5},{2,10},{3,7},{4,12},{5,1},{6,14},{7,3},{8,0},{9,13},{1... | collective-permute-start | bytes 393224 | tf_op jit(solution)/shard_map/ppermute | solution.py:62
  101.7 2.8 %collective-permute-done.14 = bf16[2,1,64,512]{3,2,1,0:T(8,128)(2,1)S(1)} collective-permute-done((bf16[2,1,64,512]{3,2,1,0:T(8,128)(2,1)S(1)}, bf16[2,1,64,512]{3,2,1,0:T(8,128)(2,1)S(1)}, u32[]{:S(2)}, u32[]{:S(2)}) %collective-permute-start.14) | collective-permute-done | bytes 131104 | tf_op jit(solution)/shard_map/ppermute | solution.py:62
  104.5 4.9 %collective-permute-done.18 = bf16[2,2,64,768]{3,2,1,0:T(8,128)(2,1)S(1)} collective-permute-done((bf16[2,2,64,768]{3,2,1,0:T(8,128)(2,1)S(1)}, bf16[2,2,64,768]{3,2,1,0:T(8,128)(2,1)S(1)}, u32[]{:S(2)}, u32[]{:S(2)}) %collective-permute-start.18) | collective-permute-done | bytes 393248 | tf_op jit(solution)/shard_map/ppermute | solution.py:62
  109.4 3.8 %collective-permute-start.20 = (bf16[2,4,64,768]{3,2,1,0:T(8,128)(2,1)S(1)}, bf16[2,4,64,768]{3,2,1,0:T(8,128)(2,1)S(1)}, u32[]{:S(2)}, u32[]{:S(2)}) collective-permute-start(bf16[2,4,64,768]{3,2,1,0:T(8,128)(2,1)S(1)} %constant_dynamic-update-slice_fusion.2), channel_id=1, source_target_pairs={{0,16},{1,3},{2,18},{3,1},{4,20},{5,7},{6,22},{7,5},{8,24},{9,11},... | collective-permute-start | bytes 2359304 | tf_op jit(solution)/shard_map/ppermute | solution.py:62
  113.2 5.1 %collective-permute-start.17 = (bf16[2,1,64,512]{3,2,1,0:T(8,128)(2,1)S(1)}, bf16[2,1,64,512]{3,2,1,0:T(8,128)(2,1)S(1)}, u32[]{:S(2)}, u32[]{:S(2)}) collective-permute-start(bf16[2,1,64,512]{3,2,1,0:T(8,128)(2,1)S(1)} %add_convert_fusion.12), channel_id=1, source_target_pairs={{0,4},{1,9},{2,6},{3,11},{4,0},{5,13},{6,2},{7,15},{8,12},{9,1},{1... | collective-permute-start | bytes 393224 | tf_op jit(solution)/shard_map/ppermute | solution.py:62
  118.3 2.9 %collective-permute-done.17 = bf16[2,1,64,512]{3,2,1,0:T(8,128)(2,1)S(1)} collective-permute-done((bf16[2,1,64,512]{3,2,1,0:T(8,128)(2,1)S(1)}, bf16[2,1,64,512]{3,2,1,0:T(8,128)(2,1)S(1)}, u32[]{:S(2)}, u32[]{:S(2)}) %collective-permute-start.17) | collective-permute-done | bytes 131104 | tf_op jit(solution)/shard_map/ppermute | solution.py:62
  121.2 2.0 %collective-permute-done.21 = bf16[2,1,64,512]{3,2,1,0:T(8,128)(2,1)S(1)} collective-permute-done((bf16[2,1,64,512]{3,2,1,0:T(8,128)(2,1)S(1)}, bf16[2,1,64,512]{3,2,1,0:T(8,128)(2,1)S(1)}, u32[]{:S(2)}, u32[]{:S(2)}) %collective-permute-start.21) | collective-permute-done | bytes 131104 | tf_op jit(solution)/shard_map/ppermute | solution.py:62
  123.6 2.0 %collective-permute-start.23 = (bf16[2,2,64,512]{3,2,1,0:T(8,128)(2,1)S(1)}, bf16[2,2,64,512]{3,2,1,0:T(8,128)(2,1)S(1)}, u32[]{:S(2)}, u32[]{:S(2)}) collective-permute-start(bf16[2,2,64,512]{3,2,1,0:T(8,128)(2,1)S(1)} %constant_dynamic-update-slice_fusion.6), channel_id=1, source_target_pairs={{0,2},{1,17},{2,0},{3,19},{4,6},{5,21},{6,4},{7,23},{8,10},{9,25},... | collective-permute-start | bytes 786440 | tf_op jit(solution)/shard_map/ppermute | solution.py:62
  125.6 4.3 %collective-permute-done.19 = bf16[2,2,64,512]{3,2,1,0:T(8,128)(2,1)S(1)} collective-permute-done((bf16[2,2,64,512]{3,2,1,0:T(8,128)(2,1)S(1)}, bf16[2,2,64,512]{3,2,1,0:T(8,128)(2,1)S(1)}, u32[]{:S(2)}, u32[]{:S(2)}) %collective-permute-start.19) | collective-permute-done | bytes 262176 | tf_op jit(solution)/shard_map/ppermute | solution.py:62
  130.0 1.9 %collective-permute-start.25 = (bf16[2,4,64,512]{3,2,1,0:T(8,128)(2,1)S(1)}, bf16[2,4,64,512]{3,2,1,0:T(8,128)(2,1)S(1)}, u32[]{:S(2)}, u32[]{:S(2)}) collective-permute-start(bf16[2,4,64,512]{3,2,1,0:T(8,128)(2,1)S(1)} %constant_dynamic-update-slice_fusion.10), channel_id=1, source_target_pairs={{0,16},{1,3},{2,18},{3,1},{4,20},{5,7},{6,22},{7,5},{8,24},{9,11},... | collective-permute-start | bytes 1572872 | tf_op jit(solution)/shard_map/ppermute | solution.py:62
  131.9 1.2 collective-permute-done.23
  133.2 2.0 %collective-permute-start.24 = (bf16[2,4,64,512]{3,2,1,0:T(8,128)(2,1)S(1)}, bf16[2,4,64,512]{3,2,1,0:T(8,128)(2,1)S(1)}, u32[]{:S(2)}, u32[]{:S(2)}) collective-permute-start(bf16[2,4,64,512]{3,2,1,0:T(8,128)(2,1)S(1)} %constant_dynamic-update-slice_fusion.12), channel_id=1, source_target_pairs={{0,16},{1,3},{2,18},{3,1},{4,20},{5,7},{6,22},{7,5},{8,24},{9,11},... | collective-permute-start | bytes 1572872 | tf_op jit(solution)/shard_map/ppermute | solution.py:62
  135.2 4.0 %unpack_top.1 = (f32[1024,1024]{1,0:T(8,128)}, f32[1024,256]{1,0:T(8,128)}, f32[1,1024]{1,0:T(1,128)}, f32[31,1024]{1,0:T(8,128)}, f32[2,1,128]{2,1,0:T(1,128)S(1)}, /*index=5*/f32[8,128]{1,0:T(8,128)S(1)}) custom-call(s32[3]{0:T(128)S(1)} %pad_add_fusion.own_ref, bf16[2,8,64,768]{3,2,1,0:T(8,128)(2,1)S(1)} %constant_dynamic-update-slice_fusion.8.mine_ref, ...), custom_call_target="tpu_custom_call" | custom-call | flops 4600000000 | bytes 1048576 | tf_op jit(solution)/shard_map/unpack_top/pallas_call | solution.py:692
  139.4 5.4 %collective-permute-done.24 = bf16[2,4,64,512]{3,2,1,0:T(8,128)(2,1)S(1)} collective-permute-done((bf16[2,4,64,512]{3,2,1,0:T(8,128)(2,1)S(1)}, bf16[2,4,64,512]{3,2,1,0:T(8,128)(2,1)S(1)}, u32[]{:S(2)}, u32[]{:S(2)}) %collective-permute-start.24) | collective-permute-done | bytes 524320 | tf_op jit(solution)/shard_map/ppermute | solution.py:62
  144.9 0.6 slice_reduce_fusion
  145.6 2.0 %collective-permute-done.26.refs_3_ = bf16[2,8,64,512]{3,2,1,0:T(8,128)(2,1)S(1)} collective-permute-done((bf16[2,8,64,512]{3,2,1,0:T(8,128)(2,1)S(1)}, bf16[2,8,64,512]{3,2,1,0:T(8,128)(2,1)S(1)}, u32[]{:S(2)}, u32[]{:S(2)}) %collective-permute-start.26) | collective-permute-done | bytes 1048608 | tf_op jit(solution)/shard_map/ppermute | solution.py:56
  147.6 4.3 %unpack_inner.1 = (f32[1024,2048]{1,0:T(8,128)}, f32[1,1024]{1,0:T(1,128)}) custom-call(s32[3]{0:T(128)S(1)} %pad_add_fusion.own_ref, f32[8,128]{1,0:T(8,128)S(1)} %get-tuple-element.172.scale_ref, bf16[1024,2048]{1,0:T(8,128)(2,1)S(1)} %copy-done, f32[1,1024]{1,0:T(1,128)S(1)} %bitcast.13, ...), custom_call_target="tpu_custom_call" | custom-call | flops 9200000000 | bytes 1048576 | tf_op jit(solution)/shard_map/unpack_inner/pallas_call | solution.py:741
  (79 shorter events, 2.3 us)
Async XLA Ops:
  0.7 1.2 copy-start.2
  2.0 4.3 %copy-start = (bf16[1024,2048]{1,0:T(8,128)(2,1)S(1)}, bf16[1024,2048]{1,0:T(8,128)(2,1)}, u32[]{:S(2)}) copy-start(bf16[1024,2048]{1,0:T(8,128)(2,1)} %weight_ref.1) | copy-start | bytes 12582916
  2.0 4.3 %copy-start.1 = (bf16[1024,1024]{1,0:T(8,128)(2,1)S(1)}, bf16[1024,1024]{1,0:T(8,128)(2,1)}, u32[]{:S(2)}) copy-start(bf16[1024,1024]{1,0:T(8,128)(2,1)} %out_weight_ref.3) | copy-start | bytes 6291460
  2.0 4.3 %copy-start.3 = (bf16[2,256,1024]{2,1,0:T(8,128)(2,1)S(1)}, bf16[2,256,1024]{2,1,0:T(8,128)(2,1)}, u32[]{:S(2)}) copy-start(bf16[2,256,1024]{2,1,0:T(8,128)(2,1)} %param.9) | copy-start | bytes 3145732
  2.0 4.3 %copy-start.5 = (f32[31,1024]{1,0:T(8,128)S(1)}, f32[31,1024]{1,0:T(8,128)}, u32[]{:S(2)}) copy-start(f32[31,1024]{1,0:T(8,128)} %depth_ref.5) | copy-start | bytes 380932
  2.0 4.3 %copy-start.7 = (f32[1024]{0:T(1024)S(1)}, f32[1024]{0:T(1024)}, u32[]{:S(2)}) copy-start(f32[1024]{0:T(1024)} %param.12) | copy-start | bytes 12292
  2.0 4.3 %copy-start.8 = (s32[2]{0:T(128)S(1)}, s32[2]{0:T(128)}, u32[]{:S(2)}) copy-start(s32[2]{0:T(128)} %lengths_ref.9) | copy-start | bytes 28
  3.2 16.0 %collective-permute-start = (f32[2,256,256]{2,1,0:T(8,128)S(1)}, f32[2,256,256]{2,1,0:T(8,128)S(1)}, u32[]{:S(2)}, u32[]{:S(2)}) collective-permute-start(f32[2,256,256]{2,1,0:T(8,128)S(1)} %get-tuple-element.105), channel_id=1, source_target_pairs={{0,16},{16,0},{1,17},{17,1},{2,18},{18,2},{3,19},{19,3},{4,20},{20... | collective-permute-start | bytes 1572872 | tf_op jit(solution)/shard_map/ppermute | solution.py:56
  6.3 13.0 %copy-start.4 = (bf16[1024,256]{1,0:T(8,128)(2,1)S(1)}, bf16[1024,256]{1,0:T(8,128)(2,1)}, u32[]{:S(2)}) copy-start(bf16[1024,256]{1,0:T(8,128)(2,1)} %head_ref.3) | copy-start | bytes 1572868
  6.3 13.0 %copy-start.6 = (f32[1024]{0:T(1024)S(1)}, f32[1024]{0:T(1024)}, u32[]{:S(2)}) copy-start(f32[1024]{0:T(1024)} %param.16) | copy-start | bytes 12292
  34.1 7.6 %collective-permute-start.1 = (bf16[2,8,64,768]{3,2,1,0:T(8,128)(2,1)S(1)}, bf16[2,8,64,768]{3,2,1,0:T(8,128)(2,1)S(1)}, u32[]{:S(2)}, u32[]{:S(2)}) collective-permute-start(bf16[2,8,64,768]{3,2,1,0:T(8,128)(2,1)S(1)} %get-tuple-element.115), channel_id=1, source_target_pairs={{0,1},{1,0},{2,3},{3,2},{4,5},{5,4},{6,7},{7,6},{8,9},{9,8},{10,11... | collective-permute-start | bytes 4718600 | tf_op jit(solution)/shard_map/ppermute | solution.py:56
  41.1 15.2 %collective-permute-start.2 = (bf16[2,8,64,512]{3,2,1,0:T(8,128)(2,1)S(1)}, bf16[2,8,64,512]{3,2,1,0:T(8,128)(2,1)S(1)}, u32[]{:S(2)}, u32[]{:S(2)}) collective-permute-start(bf16[2,8,64,512]{3,2,1,0:T(8,128)(2,1)S(1)} %get-tuple-element.121), channel_id=1, source_target_pairs={{0,1},{1,0},{2,3},{3,2},{4,5},{5,4},{6,7},{7,6},{8,9},{9,8},{10,11... | collective-permute-start | bytes 3145736 | tf_op jit(solution)/shard_map/ppermute | solution.py:56
  42.2 12.1 %collective-permute-start.3 = (bf16[2,4,64,768]{3,2,1,0:T(8,128)(2,1)S(1)}, bf16[2,4,64,768]{3,2,1,0:T(8,128)(2,1)S(1)}, u32[]{:S(2)}, u32[]{:S(2)}) collective-permute-start(bf16[2,4,64,768]{3,2,1,0:T(8,128)(2,1)S(1)} %slice.58), channel_id=1, source_target_pairs={{0,16},{1,3},{2,18},{3,1},{4,20},{5,7},{6,22},{7,5},{8,24},{9,11},... | collective-permute-start | bytes 2359304 | tf_op jit(solution)/shard_map/ppermute | solution.py:62
  51.2 7.1 %collective-permute-start.6 = (bf16[2,8,64,512]{3,2,1,0:T(8,128)(2,1)S(1)}, bf16[2,8,64,512]{3,2,1,0:T(8,128)(2,1)S(1)}, u32[]{:S(2)}, u32[]{:S(2)}) collective-permute-start(bf16[2,8,64,512]{3,2,1,0:T(8,128)(2,1)S(1)} %get-tuple-element.131), channel_id=1, source_target_pairs={{0,1},{1,0},{2,3},{3,2},{4,5},{5,4},{6,7},{7,6},{8,9},{9,8},{10,11... | collective-permute-start | bytes 3145736 | tf_op jit(solution)/shard_map/ppermute | solution.py:56
  54.5 12.0 %collective-permute-start.5 = (bf16[2,2,64,768]{3,2,1,0:T(8,128)(2,1)S(1)}, bf16[2,2,64,768]{3,2,1,0:T(8,128)(2,1)S(1)}, u32[]{:S(2)}, u32[]{:S(2)}) collective-permute-start(bf16[2,2,64,768]{3,2,1,0:T(8,128)(2,1)S(1)} %slice.77), channel_id=1, source_target_pairs={{0,2},{1,17},{2,0},{3,19},{4,6},{5,21},{6,4},{7,23},{8,10},{9,25},... | collective-permute-start | bytes 1179656 | tf_op jit(solution)/shard_map/ppermute | solution.py:62
  56.7 11.9 %collective-permute-start.4 = (bf16[2,4,64,512]{3,2,1,0:T(8,128)(2,1)S(1)}, bf16[2,4,64,512]{3,2,1,0:T(8,128)(2,1)S(1)}, u32[]{:S(2)}, u32[]{:S(2)}) collective-permute-start(bf16[2,4,64,512]{3,2,1,0:T(8,128)(2,1)S(1)} %slice.76), channel_id=1, source_target_pairs={{0,16},{1,3},{2,18},{3,1},{4,20},{5,7},{6,22},{7,5},{8,24},{9,11},... | collective-permute-start | bytes 1572872 | tf_op jit(solution)/shard_map/ppermute | solution.py:62
  58.6 14.6 %collective-permute-start.8 = (bf16[2,4,64,512]{3,2,1,0:T(8,128)(2,1)S(1)}, bf16[2,4,64,512]{3,2,1,0:T(8,128)(2,1)S(1)}, u32[]{:S(2)}, u32[]{:S(2)}) collective-permute-start(bf16[2,4,64,512]{3,2,1,0:T(8,128)(2,1)S(1)} %slice.79), channel_id=1, source_target_pairs={{0,16},{1,3},{2,18},{3,1},{4,20},{5,7},{6,22},{7,5},{8,24},{9,11},... | collective-permute-start | bytes 1572872 | tf_op jit(solution)/shard_map/ppermute | solution.py:62
  66.6 6.8 %collective-permute-start.7 = (bf16[2,1,64,768]{3,2,1,0:T(8,128)(2,1)S(1)}, bf16[2,1,64,768]{3,2,1,0:T(8,128)(2,1)S(1)}, u32[]{:S(2)}, u32[]{:S(2)}) collective-permute-start(bf16[2,1,64,768]{3,2,1,0:T(8,128)(2,1)S(1)} %slice.78), channel_id=1, source_target_pairs={{0,4},{1,9},{2,6},{3,11},{4,0},{5,13},{6,2},{7,15},{8,12},{9,1},{1... | collective-permute-start | bytes 589832 | tf_op jit(solution)/shard_map/ppermute | solution.py:62
  68.8 8.7 %collective-permute-start.11 = (bf16[2,2,64,512]{3,2,1,0:T(8,128)(2,1)S(1)}, bf16[2,2,64,512]{3,2,1,0:T(8,128)(2,1)S(1)}, u32[]{:S(2)}, u32[]{:S(2)}) collective-permute-start(bf16[2,2,64,512]{3,2,1,0:T(8,128)(2,1)S(1)} %slice.81), channel_id=1, source_target_pairs={{0,2},{1,17},{2,0},{3,19},{4,6},{5,21},{6,4},{7,23},{8,10},{9,25},... | collective-permute-start | bytes 786440 | tf_op jit(solution)/shard_map/ppermute | solution.py:62
  73.4 6.4 %collective-permute-start.10 = (bf16[2,2,64,512]{3,2,1,0:T(8,128)(2,1)S(1)}, bf16[2,2,64,512]{3,2,1,0:T(8,128)(2,1)S(1)}, u32[]{:S(2)}, u32[]{:S(2)}) collective-permute-start(bf16[2,2,64,512]{3,2,1,0:T(8,128)(2,1)S(1)} %slice.80), channel_id=1, source_target_pairs={{0,2},{1,17},{2,0},{3,19},{4,6},{5,21},{6,4},{7,23},{8,10},{9,25},... | collective-permute-start | bytes 786440 | tf_op jit(solution)/shard_map/ppermute | solution.py:62
  74.8 9.5 %collective-permute-start.9 = (bf16[2,1,64,768]{3,2,1,0:T(8,128)(2,1)S(1)}, bf16[2,1,64,768]{3,2,1,0:T(8,128)(2,1)S(1)}, u32[]{:S(2)}, u32[]{:S(2)}) collective-permute-start(bf16[2,1,64,768]{3,2,1,0:T(8,128)(2,1)S(1)} %add_convert_fusion.10), channel_id=1, source_target_pairs={{0,8},{1,5},{2,10},{3,7},{4,12},{5,1},{6,14},{7,3},{8,0},{9,13},{1... | collective-permute-start | bytes 589832 | tf_op jit(solution)/shard_map/ppermute | solution.py:62
  77.6 9.5 %collective-permute-start.13 = (bf16[2,1,64,512]{3,2,1,0:T(8,128)(2,1)S(1)}, bf16[2,1,64,512]{3,2,1,0:T(8,128)(2,1)S(1)}, u32[]{:S(2)}, u32[]{:S(2)}) collective-permute-start(bf16[2,1,64,512]{3,2,1,0:T(8,128)(2,1)S(1)} %slice.83), channel_id=1, source_target_pairs={{0,4},{1,9},{2,6},{3,11},{4,0},{5,13},{6,2},{7,15},{8,12},{9,1},{1... | collective-permute-start | bytes 393224 | tf_op jit(solution)/shard_map/ppermute | solution.py:62
  84.4 17.1 %collective-permute-start.16 = (bf16[2,1,64,768]{3,2,1,0:T(8,128)(2,1)S(1)}, bf16[2,1,64,768]{3,2,1,0:T(8,128)(2,1)S(1)}, u32[]{:S(2)}, u32[]{:S(2)}) collective-permute-start(bf16[2,1,64,768]{3,2,1,0:T(8,128)(2,1)S(1)} %add_convert_fusion.9), channel_id=1, source_target_pairs={{0,4},{1,9},{2,6},{3,11},{4,0},{5,13},{6,2},{7,15},{8,12},{9,1},{1... | collective-permute-start | bytes 589832 | tf_op jit(solution)/shard_map/ppermute | solution.py:62
  87.1 11.4 %collective-permute-start.12 = (bf16[2,1,64,512]{3,2,1,0:T(8,128)(2,1)S(1)}, bf16[2,1,64,512]{3,2,1,0:T(8,128)(2,1)S(1)}, u32[]{:S(2)}, u32[]{:S(2)}) collective-permute-start(bf16[2,1,64,512]{3,2,1,0:T(8,128)(2,1)S(1)} %slice.82), channel_id=1, source_target_pairs={{0,4},{1,9},{2,6},{3,11},{4,0},{5,13},{6,2},{7,15},{8,12},{9,1},{1... | collective-permute-start | bytes 393224 | tf_op jit(solution)/shard_map/ppermute | solution.py:62
  88.1 13.5 %collective-permute-start.15 = (bf16[2,1,64,512]{3,2,1,0:T(8,128)(2,1)S(1)}, bf16[2,1,64,512]{3,2,1,0:T(8,128)(2,1)S(1)}, u32[]{:S(2)}, u32[]{:S(2)}) collective-permute-start(bf16[2,1,64,512]{3,2,1,0:T(8,128)(2,1)S(1)} %add_convert_fusion.14), channel_id=1, source_target_pairs={{0,8},{1,5},{2,10},{3,7},{4,12},{5,1},{6,14},{7,3},{8,0},{9,13},{1... | collective-permute-start | bytes 393224 | tf_op jit(solution)/shard_map/ppermute | solution.py:62
  98.5 5.9 %collective-permute-start.14 = (bf16[2,1,64,512]{3,2,1,0:T(8,128)(2,1)S(1)}, bf16[2,1,64,512]{3,2,1,0:T(8,128)(2,1)S(1)}, u32[]{:S(2)}, u32[]{:S(2)}) collective-permute-start(bf16[2,1,64,512]{3,2,1,0:T(8,128)(2,1)S(1)} %add_convert_fusion.13), channel_id=1, source_target_pairs={{0,8},{1,5},{2,10},{3,7},{4,12},{5,1},{6,14},{7,3},{8,0},{9,13},{1... | collective-permute-start | bytes 393224 | tf_op jit(solution)/shard_map/ppermute | solution.py:62
  101.5 7.8 %collective-permute-start.18 = (bf16[2,2,64,768]{3,2,1,0:T(8,128)(2,1)S(1)}, bf16[2,2,64,768]{3,2,1,0:T(8,128)(2,1)S(1)}, u32[]{:S(2)}, u32[]{:S(2)}) collective-permute-start(bf16[2,2,64,768]{3,2,1,0:T(8,128)(2,1)S(1)} %constant_dynamic-update-slice_fusion), channel_id=1, source_target_pairs={{0,2},{1,17},{2,0},{3,19},{4,6},{5,21},{6,4},{7,23},{8,10},{9,25},... | collective-permute-start | bytes 1179656 | tf_op jit(solution)/shard_map/ppermute | solution.py:62
  109.4 14.0 %collective-permute-start.20 = (bf16[2,4,64,768]{3,2,1,0:T(8,128)(2,1)S(1)}, bf16[2,4,64,768]{3,2,1,0:T(8,128)(2,1)S(1)}, u32[]{:S(2)}, u32[]{:S(2)}) collective-permute-start(bf16[2,4,64,768]{3,2,1,0:T(8,128)(2,1)S(1)} %constant_dynamic-update-slice_fusion.2), channel_id=1, source_target_pairs={{0,16},{1,3},{2,18},{3,1},{4,20},{5,7},{6,22},{7,5},{8,24},{9,11},... | collective-permute-start | bytes 2359304 | tf_op jit(solution)/shard_map/ppermute | solution.py:62
  113.2 8.0 %collective-permute-start.17 = (bf16[2,1,64,512]{3,2,1,0:T(8,128)(2,1)S(1)}, bf16[2,1,64,512]{3,2,1,0:T(8,128)(2,1)S(1)}, u32[]{:S(2)}, u32[]{:S(2)}) collective-permute-start(bf16[2,1,64,512]{3,2,1,0:T(8,128)(2,1)S(1)} %add_convert_fusion.12), channel_id=1, source_target_pairs={{0,4},{1,9},{2,6},{3,11},{4,0},{5,13},{6,2},{7,15},{8,12},{9,1},{1... | collective-permute-start | bytes 393224 | tf_op jit(solution)/shard_map/ppermute | solution.py:62
  118.3 5.0 %collective-permute-start.21 = (bf16[2,1,64,512]{3,2,1,0:T(8,128)(2,1)S(1)}, bf16[2,1,64,512]{3,2,1,0:T(8,128)(2,1)S(1)}, u32[]{:S(2)}, u32[]{:S(2)}) collective-permute-start(bf16[2,1,64,512]{3,2,1,0:T(8,128)(2,1)S(1)} %add_convert_fusion.11), channel_id=1, source_target_pairs={{0,4},{1,9},{2,6},{3,11},{4,0},{5,13},{6,2},{7,15},{8,12},{9,1},{1... | collective-permute-start | bytes 393224 | tf_op jit(solution)/shard_map/ppermute | solution.py:62
  123.4 11.8 %collective-permute-start.22 = (bf16[2,8,64,768]{3,2,1,0:T(8,128)(2,1)S(1)}, bf16[2,8,64,768]{3,2,1,0:T(8,128)(2,1)S(1)}, u32[]{:S(2)}, u32[]{:S(2)}) collective-permute-start(bf16[2,8,64,768]{3,2,1,0:T(8,128)(2,1)S(1)} %constant_dynamic-update-slice_fusion.8.mine_ref), channel_id=1, source_target_pairs={{0,1},{1,0},{2,3},{3,2},{4,5},{5,4},{6,7},{7,6},{8,9},{9,8},{10,11... | collective-permute-start | bytes 4718600 | tf_op jit(solution)/shard_map/ppermute | solution.py:56
  123.5 6.4 %collective-permute-start.19 = (bf16[2,2,64,512]{3,2,1,0:T(8,128)(2,1)S(1)}, bf16[2,2,64,512]{3,2,1,0:T(8,128)(2,1)S(1)}, u32[]{:S(2)}, u32[]{:S(2)}) collective-permute-start(bf16[2,2,64,512]{3,2,1,0:T(8,128)(2,1)S(1)} %constant_dynamic-update-slice_fusion.4), channel_id=1, source_target_pairs={{0,2},{1,17},{2,0},{3,19},{4,6},{5,21},{6,4},{7,23},{8,10},{9,25},... | collective-permute-start | bytes 786440 | tf_op jit(solution)/shard_map/ppermute | solution.py:62
  123.6 9.5 %collective-permute-start.23 = (bf16[2,2,64,512]{3,2,1,0:T(8,128)(2,1)S(1)}, bf16[2,2,64,512]{3,2,1,0:T(8,128)(2,1)S(1)}, u32[]{:S(2)}, u32[]{:S(2)}) collective-permute-start(bf16[2,2,64,512]{3,2,1,0:T(8,128)(2,1)S(1)} %constant_dynamic-update-slice_fusion.6), channel_id=1, source_target_pairs={{0,2},{1,17},{2,0},{3,19},{4,6},{5,21},{6,4},{7,23},{8,10},{9,25},... | collective-permute-start | bytes 786440 | tf_op jit(solution)/shard_map/ppermute | solution.py:62
  130.0 9.3 %collective-permute-start.25 = (bf16[2,4,64,512]{3,2,1,0:T(8,128)(2,1)S(1)}, bf16[2,4,64,512]{3,2,1,0:T(8,128)(2,1)S(1)}, u32[]{:S(2)}, u32[]{:S(2)}) collective-permute-start(bf16[2,4,64,512]{3,2,1,0:T(8,128)(2,1)S(1)} %constant_dynamic-update-slice_fusion.10), channel_id=1, source_target_pairs={{0,16},{1,3},{2,18},{3,1},{4,20},{5,7},{6,22},{7,5},{8,24},{9,11},... | collective-permute-start | bytes 1572872 | tf_op jit(solution)/shard_map/ppermute | solution.py:62
  133.2 11.7 %collective-permute-start.24 = (bf16[2,4,64,512]{3,2,1,0:T(8,128)(2,1)S(1)}, bf16[2,4,64,512]{3,2,1,0:T(8,128)(2,1)S(1)}, u32[]{:S(2)}, u32[]{:S(2)}) collective-permute-start(bf16[2,4,64,512]{3,2,1,0:T(8,128)(2,1)S(1)} %constant_dynamic-update-slice_fusion.12), channel_id=1, source_target_pairs={{0,16},{1,3},{2,18},{3,1},{4,20},{5,7},{6,22},{7,5},{8,24},{9,11},... | collective-permute-start | bytes 1572872 | tf_op jit(solution)/shard_map/ppermute | solution.py:62
  139.3 6.2 %collective-permute-start.27 = (bf16[2,8,64,512]{3,2,1,0:T(8,128)(2,1)S(1)}, bf16[2,8,64,512]{3,2,1,0:T(8,128)(2,1)S(1)}, u32[]{:S(2)}, u32[]{:S(2)}) collective-permute-start(bf16[2,8,64,512]{3,2,1,0:T(8,128)(2,1)S(1)} %constant_dynamic-update-slice_fusion.14.refs_0_), channel_id=1, source_target_pairs={{0,1},{1,0},{2,3},{3,2},{4,5},{5,4},{6,7},{7,6},{8,9},{9,8},{10,11... | collective-permute-start | bytes 3145736 | tf_op jit(solution)/shard_map/ppermute | solution.py:56
  144.9 2.7 %collective-permute-start.26 = (bf16[2,8,64,512]{3,2,1,0:T(8,128)(2,1)S(1)}, bf16[2,8,64,512]{3,2,1,0:T(8,128)(2,1)S(1)}, u32[]{:S(2)}, u32[]{:S(2)}) collective-permute-start(bf16[2,8,64,512]{3,2,1,0:T(8,128)(2,1)S(1)} %constant_dynamic-update-slice_fusion.16.refs_2_), channel_id=1, source_target_pairs={{0,1},{1,0},{2,3},{3,2},{4,5},{5,4},{6,7},{7,6},{8,9},{9,8},{10,11... | collective-permute-start | bytes 3145736 | tf_op jit(solution)/shard_map/ppermute | solution.py:56

commit v13 on v10

--- a/solution.py
+++ b/solution.py
@@ -15,9 +15,9 @@
 MARGIN = 16
 CHUNKS = 2
 ORDER = (
-    "top", "in0", "in1", "taps", "top", "in0", "in1", "small", "top", "in0", "in1", "small",
-    "top", "in0", "in1", "small", "top", "in0", "in1", "small", "top", "in0", "in1", "small",
-    "top", "in0", "in1", "top", "write_top", "in0", "in1", "in0", "in1", "write_in",
+    "top", "in0", "in1", "taps", "in0", "top", "in1", "small", "in0", "top", "in1", "in0",
+    "top", "in1", "in0", "top", "in1", "in0", "top", "in1", "small", "in0", "top", "small",
+    "in1", "in0", "top", "small", "in0", "in1", "small", "write_top", "in1", "write_in",
 )
 SMEM_SPEC = pl.BlockSpec(memory_space=pltpu.SMEM)
 F32 = jnp.float32
@@ -263,11 +263,13 @@
     residual_ref,
     normed_ref,
     pad_ref,
+    kept_ref,
 ):
     utterances = pad_ref.shape[1]
     frames = pad_ref.shape[2] - 2 * MARGIN
-
-    @pl.when(pl.program_id(0) == 0)
+    step = pl.program_id(0)
+
+    @pl.when(step == 0)
     def _():
         values = features_ref[...].astype(F32)
         centred = values - jnp.mean(values, axis=-1, keepdims=True)
@@ -275,16 +277,14 @@
         normed = centred * lax.rsqrt(spread + 1e-05) * gain_ref[...]
         normed_ref[...] = normed.astype(BF16)
         turned_ref[...] = normed.T.astype(BF16)
-        residual_ref[...] = values
         clear_margins(pad_ref)
 
+    gate = jax.nn.sigmoid(dot(normed_ref[...], gate_weight_ref[...]))
+    gate_ref[...] = gate
+    values = dot(normed_ref[...], value_weight_ref[...]) * gate
     for utterance in range(utterances):
         rows = slice(utterance * frames, (utterance + 1) * frames)
-        normed = normed_ref[rows, :]
-        gate = jax.nn.sigmoid(dot(normed, gate_weight_ref[...]))
-        gated = dot(normed, value_weight_ref[...]) * gate
-        gated = gated * live_column(lengths_ref, utterance, frames)
-        gate_ref[rows, :] = gate
+        gated = values[rows, :] * live_column(lengths_ref, utterance, frames)
         gated_ref[rows, :] = gated
         for lane in range(WIDE // LANES):
             pad_ref[lane, utterance, MARGIN : MARGIN + frames, :] = gated[
@@ -299,13 +299,18 @@
                 rows = pl.ds(pl.multiple_of(utterance * frames + start, TILE), TILE)
                 convolved = convolve(pad_ref, lane, utterance, start, depth_ref, False)
                 squash = jax.nn.sigmoid(convolved)
-                active_ref[rows, columns] = (convolved * squash).astype(BF16)
+                active = (convolved * squash).astype(BF16)
+                active_ref[rows, columns] = active
+                kept_ref[step, rows, columns] = active
                 slope_ref[rows, columns] = squash * (1.0 + convolved * (1.0 - squash))
             return carry
 
         lax.fori_loop(0, utterances, one, 0)
 
-    residual_ref[...] += dot(active_ref[...], out_weight_ref[...])
+    @pl.when(step == kept_ref.shape[0] - 1)
+    def _():
+        active = jnp.concatenate([kept_ref[part] for part in range(kept_ref.shape[0])], axis=1)
+        residual_ref[...] = features_ref[...].astype(F32) + dot(active, out_weight_ref[...])
 
 
 def forward(lengths, features, gain, weight_in, depth, weight_out, utterances):
@@ -326,14 +331,15 @@
             pl.BlockSpec((model, WIDE), lambda i: (0, i)),
             pl.BlockSpec((model, WIDE), lambda i: (0, steps + i)),
             pl.BlockSpec((depth.shape[0], WIDE), lambda i: (0, i)),
-            pl.BlockSpec((WIDE, model), lambda i: (i, 0)),
+            fixed(model, model),
         ],
         out_specs=(fixed(model, rows), column, column, column, column, fixed(rows, model)),
         scratch_shapes=[
             pltpu.VMEM((rows, model), BF16),
             pltpu.VMEM((WIDE // LANES, utterances, frames + 2 * MARGIN, LANES), F32),
+            pltpu.VMEM((steps, rows, WIDE), BF16),
         ],
-        compiler_params=params(28),
+        compiler_params=params(32),
         cost_estimate=cost(15),
         name="forward",
     )(lengths, features, gain, weight_in, weight_in, depth, weight_out)
@@ -466,13 +472,13 @@
     def _():
         clear_margins(pad_ref)
 
+    dconv = dot(dresidual_ref[...], out_weight_ref[...], 1, 1) * slope_ref[...]
+    dconv_ref[...] = dconv
     for utterance in range(utterances):
         rows = slice(utterance * frames, (utterance + 1) * frames)
-        dconv = dot(dresidual_ref[rows, :], out_weight_ref[...], 1, 1) * slope_ref[rows, :]
-        dconv_ref[rows, :] = dconv
         for lane in range(WIDE // LANES):
             pad_ref[lane, utterance, MARGIN : MARGIN + frames, :] = dconv[
-                :, lane * LANES : (lane + 1) * LANES
+                rows, lane * LANES : (lane + 1) * LANES
             ]
 
     for lane in range(WIDE // LANES):

time: 148 us -> 141 us (0.953)
  waiting for transfers between devices: 41.9 us -> 37.5 us
  starting transfers between devices: 49.6 us -> 47.6 us
    ppermute x25, waiting for transfers between devices: 39.9 us -> 35.1 us  [exchange(): lax.ppermute(values, ALL, [(i, i ^ bits[place ^ i % 2]) for i in range(co...]
    ppermute x25, starting transfers between devices: 45.7 us -> 42.7 us  [exchange(): lax.ppermute(values, ALL, [(i, i ^ bits[place ^ i % 2]) for i in range(co...]
  transfers between devices with their start and end apart: 33 -> 33, of which waited for: 17 -> 17; matrix products, arithmetic and copies ran while one was open for 2% -> 2% of each run, Pallas kernels for 26% -> 27%
where the time goes in v13:
time: 141 us
  Pallas kernels  50.2 us (36%)
  starting transfers between devices  47.6 us (34%)
  waiting for transfers between devices  37.5 us (27%)
  local copies, waits for them, and re-layouts  2.64 us (2%)
  other arithmetic  2.12 us (2%)
    ppermute x25, starting transfers between devices, exchange(): lax.ppermute(values, ALL, [(i, i ^ bits[place ^ i % 2]) for i in range(co...  42.7 us
    ppermute x25, waiting for transfers between devices, exchange(): lax.ppermute(values, ALL, [(i, i ^ bits[place ^ i % 2]) for i in range(co...  35.1 us
    pallas_call x2, Pallas kernels, inner(): pl.pallas_call(inner_kernel, grid=(steps,), out_shape=(shape, shape, jax....  16.1 us
    pallas_call x1, Pallas kernels, forward(): pl.pallas_call(forward_kernel, grid=(steps,), out_shape=(jax.ShapeDtypeSt...  12.6 us
    pallas_call x1, Pallas kernels, tap_sums(): pl.pallas_call(taps_kernel, grid=(steps,), out_shape=jax.ShapeDtypeStruct...  5.91 us
    ppermute x8, starting transfers between devices, exchange(): return lax.ppermute(values, step, [(0, 1), (1, 0)])  4.84 us
    pallas_call x1, Pallas kernels, unpack_inner(): pl.pallas_call(functools.partial(unpack_inner_kernel, utts), out_shape=(j...  4.36 us
    pallas_call x1, Pallas kernels, unpack_top(): pl.pallas_call(functools.partial(unpack_top_kernel, utts), out_shape=(jax...  3.46 us
  transfers between devices with their start and end apart: 33, of which 17 were waited for; matrix products, arithmetic and copies ran while one was open for 2% of the time, Pallas kernels for 27%

profile of v13, /device:TPU:0, one launch (start us, length us, event | category | flops | bytes accessed | tf_op | source)
XLA Modules:
  0.0 141.2 jit_solution(14760056029768866673)
XLA Ops:
  0.7 1.2 copy-done.2
  2.0 1.2 teachers.1
  3.2 3.0 %collective-permute-start = (f32[2,256,256]{2,1,0:T(8,128)S(1)}, f32[2,256,256]{2,1,0:T(8,128)S(1)}, u32[]{:S(2)}, u32[]{:S(2)}) collective-permute-start(f32[2,256,256]{2,1,0:T(8,128)S(1)} %get-tuple-element.118), channel_id=1, source_target_pairs={{0,16},{16,0},{1,17},{17,1},{2,18},{18,2},{3,19},{19,3},{4,20},{20... | collective-permute-start | bytes 1572872 | tf_op jit(solution)/shard_map/ppermute | solution.py:54
  6.3 12.6 %forward.1 = (bf16[1024,512]{1,0:T(8,128)(2,1)S(1)}, f32[512,1024]{1,0:T(8,128)S(1)}, f32[512,1024]{1,0:T(8,128)S(1)}, f32[512,1024]{1,0:T(8,128)S(1)}, bf16[512...) custom-call(s32[2]{0:T(128)S(1)} %copy-done.8, bf16[512,1024]{1,0:T(8,128)(2,1)S(1)} %bitcast.9, f32[1,1024]{1,0:T(1,128)S(1)} %bitcast.12, ...), custom_call_target="tpu_custom_call" | custom-call | flops 17250000896 | bytes 1048576 | tf_op jit(solution)/shard_map/forward/pallas_call | solution.py:323
  18.9 3.4 %top.1 = (f32[2,1,128]{2,1,0:T(1,128)S(1)}, bf16[512,1024]{1,0:T(8,128)(2,1)S(1)}, bf16[512,256]{1,0:T(8,128)(2,1)S(1)}, bf16[512,1024]{1,0:T(8,128)(2,1)S(1)}) custom-call(s32[2]{0:T(128)S(1)} %copy-done.8, f32[512,1024]{1,0:T(8,128)S(1)} %get-tuple-element.114.residual_ref, f32[1,1024]{1,0:T(1,128)S(1)} %bitcast.10, bf16[1024,256]{1,0:T(8,128)(2,1)S(1)} %copy-done.4, ...), custom_call_target="tpu_custom_call" | custom-call | flops 5750000128 | bytes 1048576 | tf_op jit(solution)/shard_map/top/pallas_call | solution.py:392
  22.4 3.2 %outer.1 = (bf16[2,8,64,640]{3,2,1,0:T(8,128)(2,1)S(1)}, bf16[2,8,64,640]{3,2,1,0:T(8,128)(2,1)S(1)}) custom-call(s32[3]{0:T(128)S(1)} %pad_add_fusion.own_ref, bf16[512,1024]{1,0:T(8,128)(2,1)S(1)} %get-tuple-element.113.active_ref, bf16[512,1024]{1,0:T(8,128)(2,1)S(1)} %get-tuple-element.135.dresidual_ref, ...), custom_call_target="tpu_custom_call" | custom-call | flops 5750000128 | bytes 1048576 | tf_op jit(solution)/shard_map/outer/pallas_call | solution.py:431
  25.6 8.0 %inner.2 = (bf16[2,8,64,512]{3,2,1,0:T(8,128)(2,1)S(1)}, bf16[2,8,64,512]{3,2,1,0:T(8,128)(2,1)S(1)}, f32[512,512]{1,0:T(8,128)S(1)}) custom-call(s32[3]{0:T(128)S(1)} %pad_add_fusion.own_ref, s32[2]{0:T(128)S(1)} %copy-done.8, bf16[512,1024]{1,0:T(8,128)(2,1)S(1)} %get-tuple-element.135.dresidual_ref, bf16[1024,1024]{1,0:T(8,128)(2,1)S(1)} %copy-done.1, ...), custom_call_target="tpu_custom_call" | custom-call | flops 12650000384 | bytes 1048576 | tf_op jit(solution)/shard_map/inner/pallas_call | solution.py:516
  34.6 1.8 %collective-permute-start.2 = (bf16[2,4,64,640]{3,2,1,0:T(8,128)(2,1)S(1)}, bf16[2,4,64,640]{3,2,1,0:T(8,128)(2,1)S(1)}, u32[]{:S(2)}, u32[]{:S(2)}) collective-permute-start(bf16[2,4,64,640]{3,2,1,0:T(8,128)(2,1)S(1)} %slice.57), channel_id=1, source_target_pairs={{0,16},{1,3},{2,18},{3,1},{4,20},{5,7},{6,22},{7,5},{8,24},{9,11},... | collective-permute-start | bytes 1966088 | tf_op jit(solution)/shard_map/ppermute | solution.py:60
  36.4 8.1 %inner.3 = (bf16[2,8,64,512]{3,2,1,0:T(8,128)(2,1)S(1)}, bf16[2,8,64,512]{3,2,1,0:T(8,128)(2,1)S(1)}, f32[512,512]{1,0:T(8,128)S(1)}) custom-call(s32[3]{0:T(128)S(1)} %pad_add_fusion.own_ref, s32[2]{0:T(128)S(1)} %copy-done.8, bf16[512,1024]{1,0:T(8,128)(2,1)S(1)} %get-tuple-element.135.dresidual_ref, bf16[1024,1024]{1,0:T(8,128)(2,1)S(1)} %copy-done.1, ...), custom_call_target="tpu_custom_call" | custom-call | flops 12650000384 | bytes 1048576 | tf_op jit(solution)/shard_map/inner/pallas_call | solution.py:516
  44.6 0.7 collective-permute-done.2
  45.4 1.8 %collective-permute-start.6 = (bf16[2,2,64,640]{3,2,1,0:T(8,128)(2,1)S(1)}, bf16[2,2,64,640]{3,2,1,0:T(8,128)(2,1)S(1)}, u32[]{:S(2)}, u32[]{:S(2)}) collective-permute-start(bf16[2,2,64,640]{3,2,1,0:T(8,128)(2,1)S(1)} %slice.77), channel_id=1, source_target_pairs={{0,2},{1,17},{2,0},{3,19},{4,6},{5,21},{6,4},{7,23},{8,10},{9,25},... | collective-permute-start | bytes 983048 | tf_op jit(solution)/shard_map/ppermute | solution.py:60
  47.6 1.6 %collective-permute-start.7 = (bf16[2,4,64,512]{3,2,1,0:T(8,128)(2,1)S(1)}, bf16[2,4,64,512]{3,2,1,0:T(8,128)(2,1)S(1)}, u32[]{:S(2)}, u32[]{:S(2)}) collective-permute-start(bf16[2,4,64,512]{3,2,1,0:T(8,128)(2,1)S(1)} %slice.78), channel_id=1, source_target_pairs={{0,16},{1,3},{2,18},{3,1},{4,20},{5,7},{6,22},{7,5},{8,24},{9,11},... | collective-permute-start | bytes 1572872 | tf_op jit(solution)/shard_map/ppermute | solution.py:60
  49.6 0.6 collective-permute-start.5
  50.2 5.9 %taps.1 = f32[32,1024]{1,0:T(8,128)S(1)} custom-call(s32[2]{0:T(128)S(1)} %copy-done.8, f32[512,1024]{1,0:T(8,128)S(1)} %get-tuple-element.127.gated_ref, f32[512,512]{1,0:T(8,128)S(1)} %get-tuple-element.148.refs_0_, f32[512,512]{1,0:T(8,128)S(1)} %get-tuple-element.149.refs_1_), custom_call_target="tpu_custom_call" | custom-call | flops 10350000128 | bytes 1048576 | tf_op jit(solution)/shard_map/taps/pallas_call | solution.py:598
  56.1 1.6 %collective-permute-start.11 = (f32[32,1024]{1,0:T(8,128)S(1)}, f32[32,1024]{1,0:T(8,128)S(1)}, u32[]{:S(2)}, u32[]{:S(2)}) collective-permute-start(f32[32,1024]{1,0:T(8,128)S(1)} %taps.1), channel_id=1, source_target_pairs={{0,16},{1,3},{2,18},{3,1},{4,20},{5,7},{6,22},{7,5},{8,24},{9,11},... | collective-permute-start | bytes 393224 | tf_op jit(solution)/shard_map/ppermute | solution.py:60
  58.0 1.6 %collective-permute-start.9 = (bf16[2,1,64,640]{3,2,1,0:T(8,128)(2,1)S(1)}, bf16[2,1,64,640]{3,2,1,0:T(8,128)(2,1)S(1)}, u32[]{:S(2)}, u32[]{:S(2)}) collective-permute-start(bf16[2,1,64,640]{3,2,1,0:T(8,128)(2,1)S(1)} %slice.80), channel_id=1, source_target_pairs={{0,4},{1,9},{2,6},{3,11},{4,0},{5,13},{6,2},{7,15},{8,12},{9,1},{1... | collective-permute-start | bytes 491528 | tf_op jit(solution)/shard_map/ppermute | solution.py:60
  59.6 0.9 collective-permute-start.10
  60.5 2.1 %collective-permute-done.5 = bf16[2,4,64,512]{3,2,1,0:T(8,128)(2,1)S(1)} collective-permute-done((bf16[2,4,64,512]{3,2,1,0:T(8,128)(2,1)S(1)}, bf16[2,4,64,512]{3,2,1,0:T(8,128)(2,1)S(1)}, u32[]{:S(2)}, u32[]{:S(2)}) %collective-permute-start.5) | collective-permute-done | bytes 524320 | tf_op jit(solution)/shard_map/ppermute | solution.py:60
  62.9 1.6 %collective-permute-done.11 = f32[32,1024]{1,0:T(8,128)S(1)} collective-permute-done((f32[32,1024]{1,0:T(8,128)S(1)}, f32[32,1024]{1,0:T(8,128)S(1)}, u32[]{:S(2)}, u32[]{:S(2)}) %collective-permute-start.11) | collective-permute-done | bytes 131104 | tf_op jit(solution)/shard_map/ppermute | solution.py:60
  64.5 1.6 %collective-permute-start.20 = (f32[32,1024]{1,0:T(8,128)S(1)}, f32[32,1024]{1,0:T(8,128)S(1)}, u32[]{:S(2)}, u32[]{:S(2)}) collective-permute-start(f32[32,1024]{1,0:T(8,128)S(1)} %add.83), channel_id=1, source_target_pairs={{0,2},{1,17},{2,0},{3,19},{4,6},{5,21},{6,4},{7,23},{8,10},{9,25},... | collective-permute-start | bytes 393224 | tf_op jit(solution)/shard_map/ppermute | solution.py:60
  66.0 2.0 %collective-permute-done.10 = bf16[2,2,64,512]{3,2,1,0:T(8,128)(2,1)S(1)} collective-permute-done((bf16[2,2,64,512]{3,2,1,0:T(8,128)(2,1)S(1)}, bf16[2,2,64,512]{3,2,1,0:T(8,128)(2,1)S(1)}, u32[]{:S(2)}, u32[]{:S(2)}) %collective-permute-start.10) | collective-permute-done | bytes 262176 | tf_op jit(solution)/shard_map/ppermute | solution.py:60
  68.0 1.6 %collective-permute-start.8 = (bf16[2,2,64,512]{3,2,1,0:T(8,128)(2,1)S(1)}, bf16[2,2,64,512]{3,2,1,0:T(8,128)(2,1)S(1)}, u32[]{:S(2)}, u32[]{:S(2)}) collective-permute-start(bf16[2,2,64,512]{3,2,1,0:T(8,128)(2,1)S(1)} %slice.79), channel_id=1, source_target_pairs={{0,2},{1,17},{2,0},{3,19},{4,6},{5,21},{6,4},{7,23},{8,10},{9,25},... | collective-permute-start | bytes 786440 | tf_op jit(solution)/shard_map/ppermute | solution.py:60
  69.8 0.6 collective-permute-start.13
  70.5 2.8 %collective-permute-start.12 = (bf16[2,1,64,640]{3,2,1,0:T(8,128)(2,1)S(1)}, bf16[2,1,64,640]{3,2,1,0:T(8,128)(2,1)S(1)}, u32[]{:S(2)}, u32[]{:S(2)}) collective-permute-start(bf16[2,1,64,640]{3,2,1,0:T(8,128)(2,1)S(1)} %add_convert_fusion.10), channel_id=1, source_target_pairs={{0,8},{1,5},{2,10},{3,7},{4,12},{5,1},{6,14},{7,3},{8,0},{9,13},{1... | collective-permute-start | bytes 491528 | tf_op jit(solution)/shard_map/ppermute | solution.py:60
  73.2 1.2 collective-permute-done.8
  74.5 3.7 %collective-permute-done.13 = bf16[2,1,64,512]{3,2,1,0:T(8,128)(2,1)S(1)} collective-permute-done((bf16[2,1,64,512]{3,2,1,0:T(8,128)(2,1)S(1)}, bf16[2,1,64,512]{3,2,1,0:T(8,128)(2,1)S(1)}, u32[]{:S(2)}, u32[]{:S(2)}) %collective-permute-start.13) | collective-permute-done | bytes 131104 | tf_op jit(solution)/shard_map/ppermute | solution.py:60
  78.2 0.7 collective-permute-start.15
  78.9 2.5 %collective-permute-start.16 = (bf16[2,1,64,512]{3,2,1,0:T(8,128)(2,1)S(1)}, bf16[2,1,64,512]{3,2,1,0:T(8,128)(2,1)S(1)}, u32[]{:S(2)}, u32[]{:S(2)}) collective-permute-start(bf16[2,1,64,512]{3,2,1,0:T(8,128)(2,1)S(1)} %slice.83), channel_id=1, source_target_pairs={{0,4},{1,9},{2,6},{3,11},{4,0},{5,13},{6,2},{7,15},{8,12},{9,1},{1... | collective-permute-start | bytes 393224 | tf_op jit(solution)/shard_map/ppermute | solution.py:60
  81.5 3.8 %collective-permute-done.16 = bf16[2,1,64,512]{3,2,1,0:T(8,128)(2,1)S(1)} collective-permute-done((bf16[2,1,64,512]{3,2,1,0:T(8,128)(2,1)S(1)}, bf16[2,1,64,512]{3,2,1,0:T(8,128)(2,1)S(1)}, u32[]{:S(2)}, u32[]{:S(2)}) %collective-permute-start.16) | collective-permute-done | bytes 131104 | tf_op jit(solution)/shard_map/ppermute | solution.py:60
  85.3 3.3 %collective-permute-start.18 = (bf16[2,1,64,512]{3,2,1,0:T(8,128)(2,1)S(1)}, bf16[2,1,64,512]{3,2,1,0:T(8,128)(2,1)S(1)}, u32[]{:S(2)}, u32[]{:S(2)}) collective-permute-start(bf16[2,1,64,512]{3,2,1,0:T(8,128)(2,1)S(1)} %add_convert_fusion.13), channel_id=1, source_target_pairs={{0,8},{1,5},{2,10},{3,7},{4,12},{5,1},{6,14},{7,3},{8,0},{9,13},{1... | collective-permute-start | bytes 393224 | tf_op jit(solution)/shard_map/ppermute | solution.py:60
  89.5 5.3 %collective-permute-start.22 = (bf16[2,2,64,640]{3,2,1,0:T(8,128)(2,1)S(1)}, bf16[2,2,64,640]{3,2,1,0:T(8,128)(2,1)S(1)}, u32[]{:S(2)}, u32[]{:S(2)}) collective-permute-start(bf16[2,2,64,640]{3,2,1,0:T(8,128)(2,1)S(1)} %constant_dynamic-update-slice_fusion), channel_id=1, source_target_pairs={{0,2},{1,17},{2,0},{3,19},{4,6},{5,21},{6,4},{7,23},{8,10},{9,25},... | collective-permute-start | bytes 983048 | tf_op jit(solution)/shard_map/ppermute | solution.py:60
  95.0 2.1 %collective-permute-done.17 = bf16[2,1,64,512]{3,2,1,0:T(8,128)(2,1)S(1)} collective-permute-done((bf16[2,1,64,512]{3,2,1,0:T(8,128)(2,1)S(1)}, bf16[2,1,64,512]{3,2,1,0:T(8,128)(2,1)S(1)}, u32[]{:S(2)}, u32[]{:S(2)}) %collective-permute-start.17) | collective-permute-done | bytes 131104 | tf_op jit(solution)/shard_map/ppermute | solution.py:60
  97.1 3.8 %collective-permute-start.19 = (bf16[2,2,64,512]{3,2,1,0:T(8,128)(2,1)S(1)}, bf16[2,2,64,512]{3,2,1,0:T(8,128)(2,1)S(1)}, u32[]{:S(2)}, u32[]{:S(2)}) collective-permute-start(bf16[2,2,64,512]{3,2,1,0:T(8,128)(2,1)S(1)} %constant_dynamic-update-slice_fusion.2), channel_id=1, source_target_pairs={{0,2},{1,17},{2,0},{3,19},{4,6},{5,21},{6,4},{7,23},{8,10},{9,25},... | collective-permute-start | bytes 786440 | tf_op jit(solution)/shard_map/ppermute | solution.py:60
  101.0 1.3 collective-permute-start.24
  102.4 5.3 %collective-permute-done.19 = bf16[2,2,64,512]{3,2,1,0:T(8,128)(2,1)S(1)} collective-permute-done((bf16[2,2,64,512]{3,2,1,0:T(8,128)(2,1)S(1)}, bf16[2,2,64,512]{3,2,1,0:T(8,128)(2,1)S(1)}, u32[]{:S(2)}, u32[]{:S(2)}) %collective-permute-start.19) | collective-permute-done | bytes 262176 | tf_op jit(solution)/shard_map/ppermute | solution.py:60
  107.7 1.6 %collective-permute-start.27 = (bf16[2,4,64,512]{3,2,1,0:T(8,128)(2,1)S(1)}, bf16[2,4,64,512]{3,2,1,0:T(8,128)(2,1)S(1)}, u32[]{:S(2)}, u32[]{:S(2)}) collective-permute-start(bf16[2,4,64,512]{3,2,1,0:T(8,128)(2,1)S(1)} %constant_dynamic-update-slice_fusion.8), channel_id=1, source_target_pairs={{0,16},{1,3},{2,18},{3,1},{4,20},{5,7},{6,22},{7,5},{8,24},{9,11},... | collective-permute-start | bytes 1572872 | tf_op jit(solution)/shard_map/ppermute | solution.py:60
  109.3 0.9 collective-permute-start.23
  110.3 2.0 %collective-permute-start.28 = (bf16[2,2,64,512]{3,2,1,0:T(8,128)(2,1)S(1)}, bf16[2,2,64,512]{3,2,1,0:T(8,128)(2,1)S(1)}, u32[]{:S(2)}, u32[]{:S(2)}) collective-permute-start(bf16[2,2,64,512]{3,2,1,0:T(8,128)(2,1)S(1)} %constant_dynamic-update-slice_fusion.6), channel_id=1, source_target_pairs={{0,2},{1,17},{2,0},{3,19},{4,6},{5,21},{6,4},{7,23},{8,10},{9,25},... | collective-permute-start | bytes 786440 | tf_op jit(solution)/shard_map/ppermute | solution.py:60
  112.4 1.4 collective-permute-done.24
  114.5 5.0 %collective-permute-done.28 = bf16[2,2,64,512]{3,2,1,0:T(8,128)(2,1)S(1)} collective-permute-done((bf16[2,2,64,512]{3,2,1,0:T(8,128)(2,1)S(1)}, bf16[2,2,64,512]{3,2,1,0:T(8,128)(2,1)S(1)}, u32[]{:S(2)}, u32[]{:S(2)}) %collective-permute-start.28) | collective-permute-done | bytes 262176 | tf_op jit(solution)/shard_map/ppermute | solution.py:60
  120.6 1.2 collective-permute-start.31
  121.8 3.0 %collective-permute-start.25 = (f32[32,1024]{1,0:T(8,128)S(1)}, f32[32,1024]{1,0:T(8,128)S(1)}, u32[]{:S(2)}, u32[]{:S(2)}) collective-permute-start(f32[32,1024]{1,0:T(8,128)S(1)} %add.93), channel_id=1, source_target_pairs={{0,8},{1,5},{2,10},{3,7},{4,12},{5,1},{6,14},{7,3},{8,0},{9,13},{1... | collective-permute-start | bytes 393224 | tf_op jit(solution)/shard_map/ppermute | solution.py:60
  124.9 4.2 %collective-permute-done.25 = f32[32,1024]{1,0:T(8,128)S(1)} collective-permute-done((f32[32,1024]{1,0:T(8,128)S(1)}, f32[32,1024]{1,0:T(8,128)S(1)}, u32[]{:S(2)}, u32[]{:S(2)}) %collective-permute-start.25) | collective-permute-done | bytes 131104 | tf_op jit(solution)/shard_map/ppermute | solution.py:60
  129.2 0.7 collective-permute-done.31
  130.4 2.3 %collective-permute-done.30 = f32[32,1024]{1,0:T(8,128)S(1)} collective-permute-done((f32[32,1024]{1,0:T(8,128)S(1)}, f32[32,1024]{1,0:T(8,128)S(1)}, u32[]{:S(2)}, u32[]{:S(2)}) %collective-permute-start.30) | collective-permute-done | bytes 131104 | tf_op jit(solution)/shard_map/ppermute | solution.py:54
  132.8 3.5 %unpack_top.1 = (f32[1024,1024]{1,0:T(8,128)}, f32[1024,256]{1,0:T(8,128)}, f32[1,1024]{1,0:T(1,128)}, f32[31,1024]{1,0:T(8,128)}, f32[2,1,128]{2,1,0:T(1,128)S(1)}) custom-call(s32[3]{0:T(128)S(1)} %pad_add_fusion.own_ref, f32[32,1024]{1,0:T(8,128)S(1)} %add.95.small_ref, bf16[2,8,64,640]{3,2,1,0:T(8,128)(2,1)S(1)} %constant_dynamic-update-slice_fusion.10.mine_ref, ...), custom_call_target="tpu_custom_call" | custom-call | flops 5750000128 | bytes 1048576 | tf_op jit(solution)/shard_map/unpack_top/pallas_call | solution.py:687
  136.3 0.6 slice_reduce_fusion
  136.9 4.4 %unpack_inner.1 = (f32[1024,2048]{1,0:T(8,128)}, f32[1,1024]{1,0:T(1,128)}) custom-call(s32[3]{0:T(128)S(1)} %pad_add_fusion.own_ref, f32[32,1024]{1,0:T(8,128)S(1)} %add.95.small_ref, bf16[1024,2048]{1,0:T(8,128)(2,1)S(1)} %copy-done, f32[1,1024]{1,0:T(1,128)S(1)} %bitcast.13, bf16[2,8,64,512]{3,2,1,0:T(8,128)(2,1)S(1)} %constant_dynamic-update-slice_fusion.14.refs_0_, ...), custom_call_target="tpu_custom_call" | custom-call | flops 9200000000 | bytes 1048576 | tf_op jit(solution)/shard_map/unpack_inner/pallas_call | solution.py:740
  (94 shorter events, 6.9 us)
Async XLA Ops:
  0.7 1.2 copy-start.2
  2.0 4.3 %copy-start = (bf16[1024,2048]{1,0:T(8,128)(2,1)S(1)}, bf16[1024,2048]{1,0:T(8,128)(2,1)}, u32[]{:S(2)}) copy-start(bf16[1024,2048]{1,0:T(8,128)(2,1)} %weight_ref.1) | copy-start | bytes 12582916
  2.0 4.3 %copy-start.1 = (bf16[1024,1024]{1,0:T(8,128)(2,1)S(1)}, bf16[1024,1024]{1,0:T(8,128)(2,1)}, u32[]{:S(2)}) copy-start(bf16[1024,1024]{1,0:T(8,128)(2,1)} %out_weight_ref.5) | copy-start | bytes 6291460
  2.0 4.3 %copy-start.3 = (bf16[2,256,1024]{2,1,0:T(8,128)(2,1)S(1)}, bf16[2,256,1024]{2,1,0:T(8,128)(2,1)}, u32[]{:S(2)}) copy-start(bf16[2,256,1024]{2,1,0:T(8,128)(2,1)} %param.9) | copy-start | bytes 3145732
  2.0 4.3 %copy-start.5 = (f32[31,1024]{1,0:T(8,128)S(1)}, f32[31,1024]{1,0:T(8,128)}, u32[]{:S(2)}) copy-start(f32[31,1024]{1,0:T(8,128)} %depth_ref.5) | copy-start | bytes 380932
  2.0 4.3 %copy-start.7 = (f32[1024]{0:T(1024)S(1)}, f32[1024]{0:T(1024)}, u32[]{:S(2)}) copy-start(f32[1024]{0:T(1024)} %param.12) | copy-start | bytes 12292
  2.0 4.3 %copy-start.8 = (s32[2]{0:T(128)S(1)}, s32[2]{0:T(128)}, u32[]{:S(2)}) copy-start(s32[2]{0:T(128)} %lengths_ref.9) | copy-start | bytes 28
  3.2 15.6 %collective-permute-start = (f32[2,256,256]{2,1,0:T(8,128)S(1)}, f32[2,256,256]{2,1,0:T(8,128)S(1)}, u32[]{:S(2)}, u32[]{:S(2)}) collective-permute-start(f32[2,256,256]{2,1,0:T(8,128)S(1)} %get-tuple-element.118), channel_id=1, source_target_pairs={{0,16},{16,0},{1,17},{17,1},{2,18},{18,2},{3,19},{19,3},{4,20},{20... | collective-permute-start | bytes 1572872 | tf_op jit(solution)/shard_map/ppermute | solution.py:54
  6.3 12.6 %copy-start.4 = (bf16[1024,256]{1,0:T(8,128)(2,1)S(1)}, bf16[1024,256]{1,0:T(8,128)(2,1)}, u32[]{:S(2)}) copy-start(bf16[1024,256]{1,0:T(8,128)(2,1)} %head_ref.3) | copy-start | bytes 1572868
  6.3 12.6 %copy-start.6 = (f32[1024]{0:T(1024)S(1)}, f32[1024]{0:T(1024)}, u32[]{:S(2)}) copy-start(f32[1024]{0:T(1024)} %param.16) | copy-start | bytes 12292
  25.5 8.6 %collective-permute-start.1 = (bf16[2,8,64,640]{3,2,1,0:T(8,128)(2,1)S(1)}, bf16[2,8,64,640]{3,2,1,0:T(8,128)(2,1)S(1)}, u32[]{:S(2)}, u32[]{:S(2)}) collective-permute-start(bf16[2,8,64,640]{3,2,1,0:T(8,128)(2,1)S(1)} %get-tuple-element.124), channel_id=1, source_target_pairs={{0,1},{1,0},{2,3},{3,2},{4,5},{5,4},{6,7},{7,6},{8,9},{9,8},{10,11... | collective-permute-start | bytes 3932168 | tf_op jit(solution)/shard_map/ppermute | solution.py:54
  33.6 13.7 %collective-permute-start.4 = (bf16[2,8,64,512]{3,2,1,0:T(8,128)(2,1)S(1)}, bf16[2,8,64,512]{3,2,1,0:T(8,128)(2,1)S(1)}, u32[]{:S(2)}, u32[]{:S(2)}) collective-permute-start(bf16[2,8,64,512]{3,2,1,0:T(8,128)(2,1)S(1)} %get-tuple-element.141), channel_id=1, source_target_pairs={{0,1},{1,0},{2,3},{3,2},{4,5},{5,4},{6,7},{7,6},{8,9},{9,8},{10,11... | collective-permute-start | bytes 3145736 | tf_op jit(solution)/shard_map/ppermute | solution.py:54
  34.6 10.7 %collective-permute-start.2 = (bf16[2,4,64,640]{3,2,1,0:T(8,128)(2,1)S(1)}, bf16[2,4,64,640]{3,2,1,0:T(8,128)(2,1)S(1)}, u32[]{:S(2)}, u32[]{:S(2)}) collective-permute-start(bf16[2,4,64,640]{3,2,1,0:T(8,128)(2,1)S(1)} %slice.57), channel_id=1, source_target_pairs={{0,16},{1,3},{2,18},{3,1},{4,20},{5,7},{6,22},{7,5},{8,24},{9,11},... | collective-permute-start | bytes 1966088 | tf_op jit(solution)/shard_map/ppermute | solution.py:60
  44.5 4.7 %collective-permute-start.3 = (bf16[2,8,64,512]{3,2,1,0:T(8,128)(2,1)S(1)}, bf16[2,8,64,512]{3,2,1,0:T(8,128)(2,1)S(1)}, u32[]{:S(2)}, u32[]{:S(2)}) collective-permute-start(bf16[2,8,64,512]{3,2,1,0:T(8,128)(2,1)S(1)} %get-tuple-element.139), channel_id=1, source_target_pairs={{0,1},{1,0},{2,3},{3,2},{4,5},{5,4},{6,7},{7,6},{8,9},{9,8},{10,11... | collective-permute-start | bytes 3145736 | tf_op jit(solution)/shard_map/ppermute | solution.py:54
  45.4 12.4 %collective-permute-start.6 = (bf16[2,2,64,640]{3,2,1,0:T(8,128)(2,1)S(1)}, bf16[2,2,64,640]{3,2,1,0:T(8,128)(2,1)S(1)}, u32[]{:S(2)}, u32[]{:S(2)}) collective-permute-start(bf16[2,2,64,640]{3,2,1,0:T(8,128)(2,1)S(1)} %slice.77), channel_id=1, source_target_pairs={{0,2},{1,17},{2,0},{3,19},{4,6},{5,21},{6,4},{7,23},{8,10},{9,25},... | collective-permute-start | bytes 983048 | tf_op jit(solution)/shard_map/ppermute | solution.py:60
  47.6 10.0 %collective-permute-start.7 = (bf16[2,4,64,512]{3,2,1,0:T(8,128)(2,1)S(1)}, bf16[2,4,64,512]{3,2,1,0:T(8,128)(2,1)S(1)}, u32[]{:S(2)}, u32[]{:S(2)}) collective-permute-start(bf16[2,4,64,512]{3,2,1,0:T(8,128)(2,1)S(1)} %slice.78), channel_id=1, source_target_pairs={{0,16},{1,3},{2,18},{3,1},{4,20},{5,7},{6,22},{7,5},{8,24},{9,11},... | collective-permute-start | bytes 1572872 | tf_op jit(solution)/shard_map/ppermute | solution.py:60
  49.6 13.1 %collective-permute-start.5 = (bf16[2,4,64,512]{3,2,1,0:T(8,128)(2,1)S(1)}, bf16[2,4,64,512]{3,2,1,0:T(8,128)(2,1)S(1)}, u32[]{:S(2)}, u32[]{:S(2)}) collective-permute-start(bf16[2,4,64,512]{3,2,1,0:T(8,128)(2,1)S(1)} %slice.76), channel_id=1, source_target_pairs={{0,16},{1,3},{2,18},{3,1},{4,20},{5,7},{6,22},{7,5},{8,24},{9,11},... | collective-permute-start | bytes 1572872 | tf_op jit(solution)/shard_map/ppermute | solution.py:60
  56.1 8.3 %collective-permute-start.11 = (f32[32,1024]{1,0:T(8,128)S(1)}, f32[32,1024]{1,0:T(8,128)S(1)}, u32[]{:S(2)}, u32[]{:S(2)}) collective-permute-start(f32[32,1024]{1,0:T(8,128)S(1)} %taps.1), channel_id=1, source_target_pairs={{0,16},{1,3},{2,18},{3,1},{4,20},{5,7},{6,22},{7,5},{8,24},{9,11},... | collective-permute-start | bytes 393224 | tf_op jit(solution)/shard_map/ppermute | solution.py:60
  58.0 11.8 %collective-permute-start.9 = (bf16[2,1,64,640]{3,2,1,0:T(8,128)(2,1)S(1)}, bf16[2,1,64,640]{3,2,1,0:T(8,128)(2,1)S(1)}, u32[]{:S(2)}, u32[]{:S(2)}) collective-permute-start(bf16[2,1,64,640]{3,2,1,0:T(8,128)(2,1)S(1)} %slice.80), channel_id=1, source_target_pairs={{0,4},{1,9},{2,6},{3,11},{4,0},{5,13},{6,2},{7,15},{8,12},{9,1},{1... | collective-permute-start | bytes 491528 | tf_op jit(solution)/shard_map/ppermute | solution.py:60
  59.6 8.4 %collective-permute-start.10 = (bf16[2,2,64,512]{3,2,1,0:T(8,128)(2,1)S(1)}, bf16[2,2,64,512]{3,2,1,0:T(8,128)(2,1)S(1)}, u32[]{:S(2)}, u32[]{:S(2)}) collective-permute-start(bf16[2,2,64,512]{3,2,1,0:T(8,128)(2,1)S(1)} %slice.81), channel_id=1, source_target_pairs={{0,2},{1,17},{2,0},{3,19},{4,6},{5,21},{6,4},{7,23},{8,10},{9,25},... | collective-permute-start | bytes 786440 | tf_op jit(solution)/shard_map/ppermute | solution.py:60
  64.5 37.8 %collective-permute-start.20 = (f32[32,1024]{1,0:T(8,128)S(1)}, f32[32,1024]{1,0:T(8,128)S(1)}, u32[]{:S(2)}, u32[]{:S(2)}) collective-permute-start(f32[32,1024]{1,0:T(8,128)S(1)} %add.83), channel_id=1, source_target_pairs={{0,2},{1,17},{2,0},{3,19},{4,6},{5,21},{6,4},{7,23},{8,10},{9,25},... | collective-permute-start | bytes 393224 | tf_op jit(solution)/shard_map/ppermute | solution.py:60
  68.0 6.4 %collective-permute-start.8 = (bf16[2,2,64,512]{3,2,1,0:T(8,128)(2,1)S(1)}, bf16[2,2,64,512]{3,2,1,0:T(8,128)(2,1)S(1)}, u32[]{:S(2)}, u32[]{:S(2)}) collective-permute-start(bf16[2,2,64,512]{3,2,1,0:T(8,128)(2,1)S(1)} %slice.79), channel_id=1, source_target_pairs={{0,2},{1,17},{2,0},{3,19},{4,6},{5,21},{6,4},{7,23},{8,10},{9,25},... | collective-permute-start | bytes 786440 | tf_op jit(solution)/shard_map/ppermute | solution.py:60
  69.8 8.4 %collective-permute-start.13 = (bf16[2,1,64,512]{3,2,1,0:T(8,128)(2,1)S(1)}, bf16[2,1,64,512]{3,2,1,0:T(8,128)(2,1)S(1)}, u32[]{:S(2)}, u32[]{:S(2)}) collective-permute-start(bf16[2,1,64,512]{3,2,1,0:T(8,128)(2,1)S(1)} %slice.82), channel_id=1, source_target_pairs={{0,4},{1,9},{2,6},{3,11},{4,0},{5,13},{6,2},{7,15},{8,12},{9,1},{1... | collective-permute-start | bytes 393224 | tf_op jit(solution)/shard_map/ppermute | solution.py:60
  70.5 8.5 %collective-permute-start.12 = (bf16[2,1,64,640]{3,2,1,0:T(8,128)(2,1)S(1)}, bf16[2,1,64,640]{3,2,1,0:T(8,128)(2,1)S(1)}, u32[]{:S(2)}, u32[]{:S(2)}) collective-permute-start(bf16[2,1,64,640]{3,2,1,0:T(8,128)(2,1)S(1)} %add_convert_fusion.10), channel_id=1, source_target_pairs={{0,8},{1,5},{2,10},{3,7},{4,12},{5,1},{6,14},{7,3},{8,0},{9,13},{1... | collective-permute-start | bytes 491528 | tf_op jit(solution)/shard_map/ppermute | solution.py:60
  78.2 10.7 %collective-permute-start.15 = (bf16[2,1,64,512]{3,2,1,0:T(8,128)(2,1)S(1)}, bf16[2,1,64,512]{3,2,1,0:T(8,128)(2,1)S(1)}, u32[]{:S(2)}, u32[]{:S(2)}) collective-permute-start(bf16[2,1,64,512]{3,2,1,0:T(8,128)(2,1)S(1)} %add_convert_fusion.14), channel_id=1, source_target_pairs={{0,8},{1,5},{2,10},{3,7},{4,12},{5,1},{6,14},{7,3},{8,0},{9,13},{1... | collective-permute-start | bytes 393224 | tf_op jit(solution)/shard_map/ppermute | solution.py:60
  78.9 6.4 %collective-permute-start.16 = (bf16[2,1,64,512]{3,2,1,0:T(8,128)(2,1)S(1)}, bf16[2,1,64,512]{3,2,1,0:T(8,128)(2,1)S(1)}, u32[]{:S(2)}, u32[]{:S(2)}) collective-permute-start(bf16[2,1,64,512]{3,2,1,0:T(8,128)(2,1)S(1)} %slice.83), channel_id=1, source_target_pairs={{0,4},{1,9},{2,6},{3,11},{4,0},{5,13},{6,2},{7,15},{8,12},{9,1},{1... | collective-permute-start | bytes 393224 | tf_op jit(solution)/shard_map/ppermute | solution.py:60
  81.5 8.1 %collective-permute-start.14 = (bf16[2,1,64,640]{3,2,1,0:T(8,128)(2,1)S(1)}, bf16[2,1,64,640]{3,2,1,0:T(8,128)(2,1)S(1)}, u32[]{:S(2)}, u32[]{:S(2)}) collective-permute-start(bf16[2,1,64,640]{3,2,1,0:T(8,128)(2,1)S(1)} %add_convert_fusion.9), channel_id=1, source_target_pairs={{0,4},{1,9},{2,6},{3,11},{4,0},{5,13},{6,2},{7,15},{8,12},{9,1},{1... | collective-permute-start | bytes 491528 | tf_op jit(solution)/shard_map/ppermute | solution.py:60
  85.3 9.5 %collective-permute-start.18 = (bf16[2,1,64,512]{3,2,1,0:T(8,128)(2,1)S(1)}, bf16[2,1,64,512]{3,2,1,0:T(8,128)(2,1)S(1)}, u32[]{:S(2)}, u32[]{:S(2)}) collective-permute-start(bf16[2,1,64,512]{3,2,1,0:T(8,128)(2,1)S(1)} %add_convert_fusion.13), channel_id=1, source_target_pairs={{0,8},{1,5},{2,10},{3,7},{4,12},{5,1},{6,14},{7,3},{8,0},{9,13},{1... | collective-permute-start | bytes 393224 | tf_op jit(solution)/shard_map/ppermute | solution.py:60
  89.0 8.1 %collective-permute-start.17 = (bf16[2,1,64,512]{3,2,1,0:T(8,128)(2,1)S(1)}, bf16[2,1,64,512]{3,2,1,0:T(8,128)(2,1)S(1)}, u32[]{:S(2)}, u32[]{:S(2)}) collective-permute-start(bf16[2,1,64,512]{3,2,1,0:T(8,128)(2,1)S(1)} %add_convert_fusion.12), channel_id=1, source_target_pairs={{0,4},{1,9},{2,6},{3,11},{4,0},{5,13},{6,2},{7,15},{8,12},{9,1},{1... | collective-permute-start | bytes 393224 | tf_op jit(solution)/shard_map/ppermute | solution.py:60
  89.5 11.3 %collective-permute-start.22 = (bf16[2,2,64,640]{3,2,1,0:T(8,128)(2,1)S(1)}, bf16[2,2,64,640]{3,2,1,0:T(8,128)(2,1)S(1)}, u32[]{:S(2)}, u32[]{:S(2)}) collective-permute-start(bf16[2,2,64,640]{3,2,1,0:T(8,128)(2,1)S(1)} %constant_dynamic-update-slice_fusion), channel_id=1, source_target_pairs={{0,2},{1,17},{2,0},{3,19},{4,6},{5,21},{6,4},{7,23},{8,10},{9,25},... | collective-permute-start | bytes 983048 | tf_op jit(solution)/shard_map/ppermute | solution.py:60
  94.9 7.4 %collective-permute-start.21 = (bf16[2,1,64,512]{3,2,1,0:T(8,128)(2,1)S(1)}, bf16[2,1,64,512]{3,2,1,0:T(8,128)(2,1)S(1)}, u32[]{:S(2)}, u32[]{:S(2)}) collective-permute-start(bf16[2,1,64,512]{3,2,1,0:T(8,128)(2,1)S(1)} %add_convert_fusion.11), channel_id=1, source_target_pairs={{0,4},{1,9},{2,6},{3,11},{4,0},{5,13},{6,2},{7,15},{8,12},{9,1},{1... | collective-permute-start | bytes 393224 | tf_op jit(solution)/shard_map/ppermute | solution.py:60
  97.1 10.6 %collective-permute-start.19 = (bf16[2,2,64,512]{3,2,1,0:T(8,128)(2,1)S(1)}, bf16[2,2,64,512]{3,2,1,0:T(8,128)(2,1)S(1)}, u32[]{:S(2)}, u32[]{:S(2)}) collective-permute-start(bf16[2,2,64,512]{3,2,1,0:T(8,128)(2,1)S(1)} %constant_dynamic-update-slice_fusion.2), channel_id=1, source_target_pairs={{0,2},{1,17},{2,0},{3,19},{4,6},{5,21},{6,4},{7,23},{8,10},{9,25},... | collective-permute-start | bytes 786440 | tf_op jit(solution)/shard_map/ppermute | solution.py:60
  101.0 12.8 %collective-permute-start.24 = (bf16[2,4,64,640]{3,2,1,0:T(8,128)(2,1)S(1)}, bf16[2,4,64,640]{3,2,1,0:T(8,128)(2,1)S(1)}, u32[]{:S(2)}, u32[]{:S(2)}) collective-permute-start(bf16[2,4,64,640]{3,2,1,0:T(8,128)(2,1)S(1)} %constant_dynamic-update-slice_fusion.4), channel_id=1, source_target_pairs={{0,16},{1,3},{2,18},{3,1},{4,20},{5,7},{6,22},{7,5},{8,24},{9,11},... | collective-permute-start | bytes 1966088 | tf_op jit(solution)/shard_map/ppermute | solution.py:60
  107.7 12.3 %collective-permute-start.27 = (bf16[2,4,64,512]{3,2,1,0:T(8,128)(2,1)S(1)}, bf16[2,4,64,512]{3,2,1,0:T(8,128)(2,1)S(1)}, u32[]{:S(2)}, u32[]{:S(2)}) collective-permute-start(bf16[2,4,64,512]{3,2,1,0:T(8,128)(2,1)S(1)} %constant_dynamic-update-slice_fusion.8), channel_id=1, source_target_pairs={{0,16},{1,3},{2,18},{3,1},{4,20},{5,7},{6,22},{7,5},{8,24},{9,11},... | collective-permute-start | bytes 1572872 | tf_op jit(solution)/shard_map/ppermute | solution.py:60
  109.3 5.1 %collective-permute-start.23 = (f32[32,1024]{1,0:T(8,128)S(1)}, f32[32,1024]{1,0:T(8,128)S(1)}, u32[]{:S(2)}, u32[]{:S(2)}) collective-permute-start(f32[32,1024]{1,0:T(8,128)S(1)} %add.92), channel_id=1, source_target_pairs={{0,4},{1,9},{2,6},{3,11},{4,0},{5,13},{6,2},{7,15},{8,12},{9,1},{1... | collective-permute-start | bytes 393224 | tf_op jit(solution)/shard_map/ppermute | solution.py:60
  110.3 9.2 %collective-permute-start.28 = (bf16[2,2,64,512]{3,2,1,0:T(8,128)(2,1)S(1)}, bf16[2,2,64,512]{3,2,1,0:T(8,128)(2,1)S(1)}, u32[]{:S(2)}, u32[]{:S(2)}) collective-permute-start(bf16[2,2,64,512]{3,2,1,0:T(8,128)(2,1)S(1)} %constant_dynamic-update-slice_fusion.6), channel_id=1, source_target_pairs={{0,2},{1,17},{2,0},{3,19},{4,6},{5,21},{6,4},{7,23},{8,10},{9,25},... | collective-permute-start | bytes 786440 | tf_op jit(solution)/shard_map/ppermute | solution.py:60
  113.9 11.0 %collective-permute-start.26 = (bf16[2,8,64,640]{3,2,1,0:T(8,128)(2,1)S(1)}, bf16[2,8,64,640]{3,2,1,0:T(8,128)(2,1)S(1)}, u32[]{:S(2)}, u32[]{:S(2)}) collective-permute-start(bf16[2,8,64,640]{3,2,1,0:T(8,128)(2,1)S(1)} %constant_dynamic-update-slice_fusion.10.mine_ref), channel_id=1, source_target_pairs={{0,1},{1,0},{2,3},{3,2},{4,5},{5,4},{6,7},{7,6},{8,9},{9,8},{10,11... | collective-permute-start | bytes 3932168 | tf_op jit(solution)/shard_map/ppermute | solution.py:54
  120.1 9.0 %collective-permute-start.29 = (bf16[2,8,64,512]{3,2,1,0:T(8,128)(2,1)S(1)}, bf16[2,8,64,512]{3,2,1,0:T(8,128)(2,1)S(1)}, u32[]{:S(2)}, u32[]{:S(2)}) collective-permute-start(bf16[2,8,64,512]{3,2,1,0:T(8,128)(2,1)S(1)} %constant_dynamic-update-slice_fusion.14.refs_0_), channel_id=1, source_target_pairs={{0,1},{1,0},{2,3},{3,2},{4,5},{5,4},{6,7},{7,6},{8,9},{9,8},{10,11... | collective-permute-start | bytes 3145736 | tf_op jit(solution)/shard_map/ppermute | solution.py:54
  120.6 9.2 %collective-permute-start.31 = (bf16[2,4,64,512]{3,2,1,0:T(8,128)(2,1)S(1)}, bf16[2,4,64,512]{3,2,1,0:T(8,128)(2,1)S(1)}, u32[]{:S(2)}, u32[]{:S(2)}) collective-permute-start(bf16[2,4,64,512]{3,2,1,0:T(8,128)(2,1)S(1)} %constant_dynamic-update-slice_fusion.12), channel_id=1, source_target_pairs={{0,16},{1,3},{2,18},{3,1},{4,20},{5,7},{6,22},{7,5},{8,24},{9,11},... | collective-permute-start | bytes 1572872 | tf_op jit(solution)/shard_map/ppermute | solution.py:60
  121.8 7.3 %collective-permute-start.25 = (f32[32,1024]{1,0:T(8,128)S(1)}, f32[32,1024]{1,0:T(8,128)S(1)}, u32[]{:S(2)}, u32[]{:S(2)}) collective-permute-start(f32[32,1024]{1,0:T(8,128)S(1)} %add.93), channel_id=1, source_target_pairs={{0,8},{1,5},{2,10},{3,7},{4,12},{5,1},{6,14},{7,3},{8,0},{9,13},{1... | collective-permute-start | bytes 393224 | tf_op jit(solution)/shard_map/ppermute | solution.py:60
  129.9 7.0 %collective-permute-start.32 = (bf16[2,8,64,512]{3,2,1,0:T(8,128)(2,1)S(1)}, bf16[2,8,64,512]{3,2,1,0:T(8,128)(2,1)S(1)}, u32[]{:S(2)}, u32[]{:S(2)}) collective-permute-start(bf16[2,8,64,512]{3,2,1,0:T(8,128)(2,1)S(1)} %constant_dynamic-update-slice_fusion.16.refs_2_), channel_id=1, source_target_pairs={{0,1},{1,0},{2,3},{3,2},{4,5},{5,4},{6,7},{7,6},{8,9},{9,8},{10,11... | collective-permute-start | bytes 3145736 | tf_op jit(solution)/shard_map/ppermute | solution.py:54
  129.9 2.8 %collective-permute-start.30 = (f32[32,1024]{1,0:T(8,128)S(1)}, f32[32,1024]{1,0:T(8,128)S(1)}, u32[]{:S(2)}, u32[]{:S(2)}) collective-permute-start(f32[32,1024]{1,0:T(8,128)S(1)} %add.94), channel_id=1, source_target_pairs={{0,1},{1,0},{2,3},{3,2},{4,5},{5,4},{6,7},{7,6},{8,9},{9,8},{10,11... | collective-permute-start | bytes 393224 | tf_op jit(solution)/shard_map/ppermute | solution.py:54

commit v14 on v13

--- a/solution.py
+++ b/solution.py
@@ -16,8 +16,8 @@
 CHUNKS = 2
 ORDER = (
     "top", "in0", "in1", "taps", "in0", "top", "in1", "small", "in0", "top", "in1", "in0",
-    "top", "in1", "in0", "top", "in1", "in0", "top", "in1", "small", "in0", "top", "small",
-    "in1", "in0", "top", "small", "in0", "in1", "small", "write_top", "in1", "write_in",
+    "top", "in1", "in0", "top", "in1", "small", "in0", "top", "in1", "small", "in0", "top",
+    "in1", "small", "in0", "top", "small", "in0", "in1", "write_top", "in1", "write_in",
 )
 SMEM_SPEC = pl.BlockSpec(memory_space=pltpu.SMEM)
 F32 = jnp.float32

time: 141 us -> 142 us (level)
  transfers between devices with their start and end apart: 33 -> 33, of which waited for: 17 -> 14; matrix products, arithmetic and copies ran while one was open for 2% -> 2% of each run, Pallas kernels for 27% -> 27%
where the time goes in v14:
time: 142 us; the launch traced here: 141 us
  Pallas kernels  50.2 us (35%)
  starting transfers between devices  47.4 us (33%)
  waiting for transfers between devices  37.9 us (27%)
  local copies, waits for them, and re-layouts  2.64 us (2%)
  other arithmetic  2.13 us (2%)
    ppermute x25, starting transfers between devices, exchange(): lax.ppermute(values, ALL, [(i, i ^ bits[place ^ i % 2]) for i in range(co...  43 us
    ppermute x25, waiting for transfers between devices, exchange(): lax.ppermute(values, ALL, [(i, i ^ bits[place ^ i % 2]) for i in range(co...  35.6 us
    pallas_call x2, Pallas kernels, inner(): pl.pallas_call(inner_kernel, grid=(steps,), out_shape=(shape, shape, jax....  16.1 us
    pallas_call x1, Pallas kernels, forward(): pl.pallas_call(forward_kernel, grid=(steps,), out_shape=(jax.ShapeDtypeSt...  12.6 us
    pallas_call x1, Pallas kernels, tap_sums(): pl.pallas_call(taps_kernel, grid=(steps,), out_shape=jax.ShapeDtypeStruct...  5.91 us
    pallas_call x1, Pallas kernels, unpack_inner(): pl.pallas_call(functools.partial(unpack_inner_kernel, utts), out_shape=(j...  4.36 us
    ppermute x8, starting transfers between devices, exchange(): return lax.ppermute(values, step, [(0, 1), (1, 0)])  4.32 us
    pallas_call x1, Pallas kernels, unpack_top(): pl.pallas_call(functools.partial(unpack_top_kernel, utts), out_shape=(jax...  3.46 us
  transfers between devices with their start and end apart: 33, of which 14 were waited for; matrix products, arithmetic and copies ran while one was open for 2% of the time, Pallas kernels for 27%

profile of v14, /device:TPU:0, one launch (start us, length us, event | category | flops | bytes accessed | tf_op | source)
XLA Modules:
  0.0 141.5 jit_solution(8857566146614465910)
XLA Ops:
  0.7 1.2 copy-done.2
  2.0 1.2 teachers.1
  3.2 3.0 %collective-permute-start = (f32[2,256,256]{2,1,0:T(8,128)S(1)}, f32[2,256,256]{2,1,0:T(8,128)S(1)}, u32[]{:S(2)}, u32[]{:S(2)}) collective-permute-start(f32[2,256,256]{2,1,0:T(8,128)S(1)} %get-tuple-element.118), channel_id=1, source_target_pairs={{0,16},{16,0},{1,17},{17,1},{2,18},{18,2},{3,19},{19,3},{4,20},{20... | collective-permute-start | bytes 1572872 | tf_op jit(solution)/shard_map/ppermute | solution.py:54
  6.3 12.6 %forward.1 = (bf16[1024,512]{1,0:T(8,128)(2,1)S(1)}, f32[512,1024]{1,0:T(8,128)S(1)}, f32[512,1024]{1,0:T(8,128)S(1)}, f32[512,1024]{1,0:T(8,128)S(1)}, bf16[512...) custom-call(s32[2]{0:T(128)S(1)} %copy-done.8, bf16[512,1024]{1,0:T(8,128)(2,1)S(1)} %bitcast.9, f32[1,1024]{1,0:T(1,128)S(1)} %bitcast.12, ...), custom_call_target="tpu_custom_call" | custom-call | flops 17250000896 | bytes 1048576 | tf_op jit(solution)/shard_map/forward/pallas_call | solution.py:323
  18.9 3.4 %top.1 = (f32[2,1,128]{2,1,0:T(1,128)S(1)}, bf16[512,1024]{1,0:T(8,128)(2,1)S(1)}, bf16[512,256]{1,0:T(8,128)(2,1)S(1)}, bf16[512,1024]{1,0:T(8,128)(2,1)S(1)}) custom-call(s32[2]{0:T(128)S(1)} %copy-done.8, f32[512,1024]{1,0:T(8,128)S(1)} %get-tuple-element.114.residual_ref, f32[1,1024]{1,0:T(1,128)S(1)} %bitcast.10, bf16[1024,256]{1,0:T(8,128)(2,1)S(1)} %copy-done.4, ...), custom_call_target="tpu_custom_call" | custom-call | flops 5750000128 | bytes 1048576 | tf_op jit(solution)/shard_map/top/pallas_call | solution.py:392
  22.4 3.2 %outer.1 = (bf16[2,8,64,640]{3,2,1,0:T(8,128)(2,1)S(1)}, bf16[2,8,64,640]{3,2,1,0:T(8,128)(2,1)S(1)}) custom-call(s32[3]{0:T(128)S(1)} %pad_add_fusion.own_ref, bf16[512,1024]{1,0:T(8,128)(2,1)S(1)} %get-tuple-element.113.active_ref, bf16[512,1024]{1,0:T(8,128)(2,1)S(1)} %get-tuple-element.134.dresidual_ref, ...), custom_call_target="tpu_custom_call" | custom-call | flops 5750000128 | bytes 1048576 | tf_op jit(solution)/shard_map/outer/pallas_call | solution.py:431
  25.6 8.0 %inner.2 = (bf16[2,8,64,512]{3,2,1,0:T(8,128)(2,1)S(1)}, bf16[2,8,64,512]{3,2,1,0:T(8,128)(2,1)S(1)}, f32[512,512]{1,0:T(8,128)S(1)}) custom-call(s32[3]{0:T(128)S(1)} %pad_add_fusion.own_ref, s32[2]{0:T(128)S(1)} %copy-done.8, bf16[512,1024]{1,0:T(8,128)(2,1)S(1)} %get-tuple-element.134.dresidual_ref, bf16[1024,1024]{1,0:T(8,128)(2,1)S(1)} %copy-done.1, ...), custom_call_target="tpu_custom_call" | custom-call | flops 12650000384 | bytes 1048576 | tf_op jit(solution)/shard_map/inner/pallas_call | solution.py:516
  33.6 0.5 collective-permute-start.5
  34.1 0.4 add_convert_fusion
  34.6 1.8 %collective-permute-start.2 = (bf16[2,4,64,640]{3,2,1,0:T(8,128)(2,1)S(1)}, bf16[2,4,64,640]{3,2,1,0:T(8,128)(2,1)S(1)}, u32[]{:S(2)}, u32[]{:S(2)}) collective-permute-start(bf16[2,4,64,640]{3,2,1,0:T(8,128)(2,1)S(1)} %slice.58), channel_id=1, source_target_pairs={{0,16},{1,3},{2,18},{3,1},{4,20},{5,7},{6,22},{7,5},{8,24},{9,11},... | collective-permute-start | bytes 1966088 | tf_op jit(solution)/shard_map/ppermute | solution.py:60
  36.4 8.1 %inner.3 = (bf16[2,8,64,512]{3,2,1,0:T(8,128)(2,1)S(1)}, bf16[2,8,64,512]{3,2,1,0:T(8,128)(2,1)S(1)}, f32[512,512]{1,0:T(8,128)S(1)}) custom-call(s32[3]{0:T(128)S(1)} %pad_add_fusion.own_ref, s32[2]{0:T(128)S(1)} %copy-done.8, bf16[512,1024]{1,0:T(8,128)(2,1)S(1)} %get-tuple-element.134.dresidual_ref, bf16[1024,1024]{1,0:T(8,128)(2,1)S(1)} %copy-done.1, ...), custom_call_target="tpu_custom_call" | custom-call | flops 12650000384 | bytes 1048576 | tf_op jit(solution)/shard_map/inner/pallas_call | solution.py:516
  44.6 0.7 collective-permute-done.2
  45.4 1.8 %collective-permute-start.3 = (bf16[2,2,64,640]{3,2,1,0:T(8,128)(2,1)S(1)}, bf16[2,2,64,640]{3,2,1,0:T(8,128)(2,1)S(1)}, u32[]{:S(2)}, u32[]{:S(2)}) collective-permute-start(bf16[2,2,64,640]{3,2,1,0:T(8,128)(2,1)S(1)} %slice.76), channel_id=1, source_target_pairs={{0,2},{1,17},{2,0},{3,19},{4,6},{5,21},{6,4},{7,23},{8,10},{9,25},... | collective-permute-start | bytes 983048 | tf_op jit(solution)/shard_map/ppermute | solution.py:60
  47.6 1.6 %collective-permute-start.6 = (bf16[2,4,64,512]{3,2,1,0:T(8,128)(2,1)S(1)}, bf16[2,4,64,512]{3,2,1,0:T(8,128)(2,1)S(1)}, u32[]{:S(2)}, u32[]{:S(2)}) collective-permute-start(bf16[2,4,64,512]{3,2,1,0:T(8,128)(2,1)S(1)} %slice.77), channel_id=1, source_target_pairs={{0,16},{1,3},{2,18},{3,1},{4,20},{5,7},{6,22},{7,5},{8,24},{9,11},... | collective-permute-start | bytes 1572872 | tf_op jit(solution)/shard_map/ppermute | solution.py:60
  49.6 0.6 collective-permute-start.9
  50.2 5.9 %taps.1 = f32[32,1024]{1,0:T(8,128)S(1)} custom-call(s32[2]{0:T(128)S(1)} %copy-done.8, f32[512,1024]{1,0:T(8,128)S(1)} %get-tuple-element.128.gated_ref, f32[512,512]{1,0:T(8,128)S(1)} %get-tuple-element.146.refs_0_, f32[512,512]{1,0:T(8,128)S(1)} %get-tuple-element.147.refs_1_), custom_call_target="tpu_custom_call" | custom-call | flops 10350000128 | bytes 1048576 | tf_op jit(solution)/shard_map/taps/pallas_call | solution.py:598
  56.1 1.6 %collective-permute-start.8 = (f32[32,1024]{1,0:T(8,128)S(1)}, f32[32,1024]{1,0:T(8,128)S(1)}, u32[]{:S(2)}, u32[]{:S(2)}) collective-permute-start(f32[32,1024]{1,0:T(8,128)S(1)} %taps.1), channel_id=1, source_target_pairs={{0,16},{1,3},{2,18},{3,1},{4,20},{5,7},{6,22},{7,5},{8,24},{9,11},... | collective-permute-start | bytes 393224 | tf_op jit(solution)/shard_map/ppermute | solution.py:60
  58.0 1.6 %collective-permute-start.12 = (bf16[2,1,64,640]{3,2,1,0:T(8,128)(2,1)S(1)}, bf16[2,1,64,640]{3,2,1,0:T(8,128)(2,1)S(1)}, u32[]{:S(2)}, u32[]{:S(2)}) collective-permute-start(bf16[2,1,64,640]{3,2,1,0:T(8,128)(2,1)S(1)} %slice.82), channel_id=1, source_target_pairs={{0,4},{1,9},{2,6},{3,11},{4,0},{5,13},{6,2},{7,15},{8,12},{9,1},{1... | collective-permute-start | bytes 491528 | tf_op jit(solution)/shard_map/ppermute | solution.py:60
  59.6 0.9 collective-permute-start.7
  60.5 2.1 %collective-permute-done.9 = bf16[2,4,64,512]{3,2,1,0:T(8,128)(2,1)S(1)} collective-permute-done((bf16[2,4,64,512]{3,2,1,0:T(8,128)(2,1)S(1)}, bf16[2,4,64,512]{3,2,1,0:T(8,128)(2,1)S(1)}, u32[]{:S(2)}, u32[]{:S(2)}) %collective-permute-start.9) | collective-permute-done | bytes 524320 | tf_op jit(solution)/shard_map/ppermute | solution.py:60
  62.9 1.6 %collective-permute-done.8 = f32[32,1024]{1,0:T(8,128)S(1)} collective-permute-done((f32[32,1024]{1,0:T(8,128)S(1)}, f32[32,1024]{1,0:T(8,128)S(1)}, u32[]{:S(2)}, u32[]{:S(2)}) %collective-permute-start.8) | collective-permute-done | bytes 131104 | tf_op jit(solution)/shard_map/ppermute | solution.py:60
  64.5 1.6 %collective-permute-start.20 = (f32[32,1024]{1,0:T(8,128)S(1)}, f32[32,1024]{1,0:T(8,128)S(1)}, u32[]{:S(2)}, u32[]{:S(2)}) collective-permute-start(f32[32,1024]{1,0:T(8,128)S(1)} %add.83), channel_id=1, source_target_pairs={{0,2},{1,17},{2,0},{3,19},{4,6},{5,21},{6,4},{7,23},{8,10},{9,25},... | collective-permute-start | bytes 393224 | tf_op jit(solution)/shard_map/ppermute | solution.py:60
  66.0 2.0 %collective-permute-done.7 = bf16[2,2,64,512]{3,2,1,0:T(8,128)(2,1)S(1)} collective-permute-done((bf16[2,2,64,512]{3,2,1,0:T(8,128)(2,1)S(1)}, bf16[2,2,64,512]{3,2,1,0:T(8,128)(2,1)S(1)}, u32[]{:S(2)}, u32[]{:S(2)}) %collective-permute-start.7) | collective-permute-done | bytes 262176 | tf_op jit(solution)/shard_map/ppermute | solution.py:60
  68.0 1.6 %collective-permute-start.11 = (bf16[2,2,64,512]{3,2,1,0:T(8,128)(2,1)S(1)}, bf16[2,2,64,512]{3,2,1,0:T(8,128)(2,1)S(1)}, u32[]{:S(2)}, u32[]{:S(2)}) collective-permute-start(bf16[2,2,64,512]{3,2,1,0:T(8,128)(2,1)S(1)} %slice.81), channel_id=1, source_target_pairs={{0,2},{1,17},{2,0},{3,19},{4,6},{5,21},{6,4},{7,23},{8,10},{9,25},... | collective-permute-start | bytes 786440 | tf_op jit(solution)/shard_map/ppermute | solution.py:60
  69.8 0.6 collective-permute-start.10
  70.5 2.8 %collective-permute-start.14 = (bf16[2,1,64,640]{3,2,1,0:T(8,128)(2,1)S(1)}, bf16[2,1,64,640]{3,2,1,0:T(8,128)(2,1)S(1)}, u32[]{:S(2)}, u32[]{:S(2)}) collective-permute-start(bf16[2,1,64,640]{3,2,1,0:T(8,128)(2,1)S(1)} %add_convert_fusion.10), channel_id=1, source_target_pairs={{0,8},{1,5},{2,10},{3,7},{4,12},{5,1},{6,14},{7,3},{8,0},{9,13},{1... | collective-permute-start | bytes 491528 | tf_op jit(solution)/shard_map/ppermute | solution.py:60
  73.2 1.2 collective-permute-done.11
  74.5 3.7 %collective-permute-done.10 = bf16[2,1,64,512]{3,2,1,0:T(8,128)(2,1)S(1)} collective-permute-done((bf16[2,1,64,512]{3,2,1,0:T(8,128)(2,1)S(1)}, bf16[2,1,64,512]{3,2,1,0:T(8,128)(2,1)S(1)}, u32[]{:S(2)}, u32[]{:S(2)}) %collective-permute-start.10) | collective-permute-done | bytes 131104 | tf_op jit(solution)/shard_map/ppermute | solution.py:60
  78.2 0.7 collective-permute-start.17
  78.9 2.5 %collective-permute-start.13 = (bf16[2,1,64,512]{3,2,1,0:T(8,128)(2,1)S(1)}, bf16[2,1,64,512]{3,2,1,0:T(8,128)(2,1)S(1)}, u32[]{:S(2)}, u32[]{:S(2)}) collective-permute-start(bf16[2,1,64,512]{3,2,1,0:T(8,128)(2,1)S(1)} %slice.83), channel_id=1, source_target_pairs={{0,4},{1,9},{2,6},{3,11},{4,0},{5,13},{6,2},{7,15},{8,12},{9,1},{1... | collective-permute-start | bytes 393224 | tf_op jit(solution)/shard_map/ppermute | solution.py:60
  81.5 3.8 %collective-permute-done.13 = bf16[2,1,64,512]{3,2,1,0:T(8,128)(2,1)S(1)} collective-permute-done((bf16[2,1,64,512]{3,2,1,0:T(8,128)(2,1)S(1)}, bf16[2,1,64,512]{3,2,1,0:T(8,128)(2,1)S(1)}, u32[]{:S(2)}, u32[]{:S(2)}) %collective-permute-start.13) | collective-permute-done | bytes 131104 | tf_op jit(solution)/shard_map/ppermute | solution.py:60
  85.3 3.3 %collective-permute-start.15 = (bf16[2,1,64,512]{3,2,1,0:T(8,128)(2,1)S(1)}, bf16[2,1,64,512]{3,2,1,0:T(8,128)(2,1)S(1)}, u32[]{:S(2)}, u32[]{:S(2)}) collective-permute-start(bf16[2,1,64,512]{3,2,1,0:T(8,128)(2,1)S(1)} %add_convert_fusion.13), channel_id=1, source_target_pairs={{0,8},{1,5},{2,10},{3,7},{4,12},{5,1},{6,14},{7,3},{8,0},{9,13},{1... | collective-permute-start | bytes 393224 | tf_op jit(solution)/shard_map/ppermute | solution.py:60
  89.0 0.5 collective-permute-start.19
  89.5 5.3 %collective-permute-start.18 = (bf16[2,2,64,640]{3,2,1,0:T(8,128)(2,1)S(1)}, bf16[2,2,64,640]{3,2,1,0:T(8,128)(2,1)S(1)}, u32[]{:S(2)}, u32[]{:S(2)}) collective-permute-start(bf16[2,2,64,640]{3,2,1,0:T(8,128)(2,1)S(1)} %constant_dynamic-update-slice_fusion), channel_id=1, source_target_pairs={{0,2},{1,17},{2,0},{3,19},{4,6},{5,21},{6,4},{7,23},{8,10},{9,25},... | collective-permute-start | bytes 983048 | tf_op jit(solution)/shard_map/ppermute | solution.py:60
  95.0 2.1 %collective-permute-start.23 = (f32[32,1024]{1,0:T(8,128)S(1)}, f32[32,1024]{1,0:T(8,128)S(1)}, u32[]{:S(2)}, u32[]{:S(2)}) collective-permute-start(f32[32,1024]{1,0:T(8,128)S(1)} %add.92), channel_id=1, source_target_pairs={{0,4},{1,9},{2,6},{3,11},{4,0},{5,13},{6,2},{7,15},{8,12},{9,1},{1... | collective-permute-start | bytes 393224 | tf_op jit(solution)/shard_map/ppermute | solution.py:60
  97.1 7.3 %collective-permute-start.22 = (bf16[2,2,64,512]{3,2,1,0:T(8,128)(2,1)S(1)}, bf16[2,2,64,512]{3,2,1,0:T(8,128)(2,1)S(1)}, u32[]{:S(2)}, u32[]{:S(2)}) collective-permute-start(bf16[2,2,64,512]{3,2,1,0:T(8,128)(2,1)S(1)} %constant_dynamic-update-slice_fusion.2), channel_id=1, source_target_pairs={{0,2},{1,17},{2,0},{3,19},{4,6},{5,21},{6,4},{7,23},{8,10},{9,25},... | collective-permute-start | bytes 786440 | tf_op jit(solution)/shard_map/ppermute | solution.py:60
  104.6 6.9 %collective-permute-done.22 = bf16[2,2,64,512]{3,2,1,0:T(8,128)(2,1)S(1)} collective-permute-done((bf16[2,2,64,512]{3,2,1,0:T(8,128)(2,1)S(1)}, bf16[2,2,64,512]{3,2,1,0:T(8,128)(2,1)S(1)}, u32[]{:S(2)}, u32[]{:S(2)}) %collective-permute-start.22) | collective-permute-done | bytes 262176 | tf_op jit(solution)/shard_map/ppermute | solution.py:60
  111.7 2.6 %collective-permute-start.26 = (f32[32,1024]{1,0:T(8,128)S(1)}, f32[32,1024]{1,0:T(8,128)S(1)}, u32[]{:S(2)}, u32[]{:S(2)}) collective-permute-start(f32[32,1024]{1,0:T(8,128)S(1)} %add.93), channel_id=1, source_target_pairs={{0,8},{1,5},{2,10},{3,7},{4,12},{5,1},{6,14},{7,3},{8,0},{9,13},{1... | collective-permute-start | bytes 393224 | tf_op jit(solution)/shard_map/ppermute | solution.py:60
  114.3 2.0 %collective-permute-start.27 = (bf16[2,2,64,512]{3,2,1,0:T(8,128)(2,1)S(1)}, bf16[2,2,64,512]{3,2,1,0:T(8,128)(2,1)S(1)}, u32[]{:S(2)}, u32[]{:S(2)}) collective-permute-start(bf16[2,2,64,512]{3,2,1,0:T(8,128)(2,1)S(1)} %constant_dynamic-update-slice_fusion.6), channel_id=1, source_target_pairs={{0,2},{1,17},{2,0},{3,19},{4,6},{5,21},{6,4},{7,23},{8,10},{9,25},... | collective-permute-start | bytes 786440 | tf_op jit(solution)/shard_map/ppermute | solution.py:60
  116.4 1.5 %collective-permute-done.21 = bf16[2,4,64,640]{3,2,1,0:T(8,128)(2,1)S(1)} collective-permute-done((bf16[2,4,64,640]{3,2,1,0:T(8,128)(2,1)S(1)}, bf16[2,4,64,640]{3,2,1,0:T(8,128)(2,1)S(1)}, u32[]{:S(2)}, u32[]{:S(2)}) %collective-permute-start.21) | collective-permute-done | bytes 655392 | tf_op jit(solution)/shard_map/ppermute | solution.py:60
  118.1 3.4 %collective-permute-done.27 = bf16[2,2,64,512]{3,2,1,0:T(8,128)(2,1)S(1)} collective-permute-done((bf16[2,2,64,512]{3,2,1,0:T(8,128)(2,1)S(1)}, bf16[2,2,64,512]{3,2,1,0:T(8,128)(2,1)S(1)}, u32[]{:S(2)}, u32[]{:S(2)}) %collective-permute-start.27) | collective-permute-done | bytes 262176 | tf_op jit(solution)/shard_map/ppermute | solution.py:60
  121.6 1.9 %collective-permute-done.25 = bf16[2,4,64,512]{3,2,1,0:T(8,128)(2,1)S(1)} collective-permute-done((bf16[2,4,64,512]{3,2,1,0:T(8,128)(2,1)S(1)}, bf16[2,4,64,512]{3,2,1,0:T(8,128)(2,1)S(1)}, u32[]{:S(2)}, u32[]{:S(2)}) %collective-permute-start.25) | collective-permute-done | bytes 524320 | tf_op jit(solution)/shard_map/ppermute | solution.py:60
  123.8 0.4 collective-permute-start.29
  124.2 2.3 %collective-permute-done.29 = f32[32,1024]{1,0:T(8,128)S(1)} collective-permute-done((f32[32,1024]{1,0:T(8,128)S(1)}, f32[32,1024]{1,0:T(8,128)S(1)}, u32[]{:S(2)}, u32[]{:S(2)}) %collective-permute-start.29) | collective-permute-done | bytes 131104 | tf_op jit(solution)/shard_map/ppermute | solution.py:54
  126.6 6.4 %collective-permute-done.31 = bf16[2,4,64,512]{3,2,1,0:T(8,128)(2,1)S(1)} collective-permute-done((bf16[2,4,64,512]{3,2,1,0:T(8,128)(2,1)S(1)}, bf16[2,4,64,512]{3,2,1,0:T(8,128)(2,1)S(1)}, u32[]{:S(2)}, u32[]{:S(2)}) %collective-permute-start.31) | collective-permute-done | bytes 524320 | tf_op jit(solution)/shard_map/ppermute | solution.py:60
  133.1 3.5 %unpack_top.1 = (f32[1024,1024]{1,0:T(8,128)}, f32[1024,256]{1,0:T(8,128)}, f32[1,1024]{1,0:T(1,128)}, f32[31,1024]{1,0:T(8,128)}, f32[2,1,128]{2,1,0:T(1,128)S(1)}) custom-call(s32[3]{0:T(128)S(1)} %pad_add_fusion.own_ref, f32[32,1024]{1,0:T(8,128)S(1)} %add.95.small_ref, bf16[2,8,64,640]{3,2,1,0:T(8,128)(2,1)S(1)} %constant_dynamic-update-slice_fusion.10.mine_ref, ...), custom_call_target="tpu_custom_call" | custom-call | flops 5750000128 | bytes 1048576 | tf_op jit(solution)/shard_map/unpack_top/pallas_call | solution.py:687
  136.5 0.6 slice_reduce_fusion
  137.1 4.4 %unpack_inner.1 = (f32[1024,2048]{1,0:T(8,128)}, f32[1,1024]{1,0:T(1,128)}) custom-call(s32[3]{0:T(128)S(1)} %pad_add_fusion.own_ref, f32[32,1024]{1,0:T(8,128)S(1)} %add.95.small_ref, bf16[1024,2048]{1,0:T(8,128)(2,1)S(1)} %copy-done, f32[1,1024]{1,0:T(1,128)S(1)} %bitcast.13, bf16[2,8,64,512]{3,2,1,0:T(8,128)(2,1)S(1)} %constant_dynamic-update-slice_fusion.14.refs_0_, ...), custom_call_target="tpu_custom_call" | custom-call | flops 9200000000 | bytes 1048576 | tf_op jit(solution)/shard_map/unpack_inner/pallas_call | solution.py:740
  (94 shorter events, 3.7 us)
Async XLA Ops:
  0.7 1.2 copy-start.2
  2.0 4.3 %copy-start = (bf16[1024,2048]{1,0:T(8,128)(2,1)S(1)}, bf16[1024,2048]{1,0:T(8,128)(2,1)}, u32[]{:S(2)}) copy-start(bf16[1024,2048]{1,0:T(8,128)(2,1)} %weight_ref.1) | copy-start | bytes 12582916
  2.0 4.3 %copy-start.1 = (bf16[1024,1024]{1,0:T(8,128)(2,1)S(1)}, bf16[1024,1024]{1,0:T(8,128)(2,1)}, u32[]{:S(2)}) copy-start(bf16[1024,1024]{1,0:T(8,128)(2,1)} %out_weight_ref.5) | copy-start | bytes 6291460
  2.0 4.3 %copy-start.3 = (bf16[2,256,1024]{2,1,0:T(8,128)(2,1)S(1)}, bf16[2,256,1024]{2,1,0:T(8,128)(2,1)}, u32[]{:S(2)}) copy-start(bf16[2,256,1024]{2,1,0:T(8,128)(2,1)} %param.9) | copy-start | bytes 3145732
  2.0 4.3 %copy-start.5 = (f32[31,1024]{1,0:T(8,128)S(1)}, f32[31,1024]{1,0:T(8,128)}, u32[]{:S(2)}) copy-start(f32[31,1024]{1,0:T(8,128)} %depth_ref.5) | copy-start | bytes 380932
  2.0 4.3 %copy-start.7 = (f32[1024]{0:T(1024)S(1)}, f32[1024]{0:T(1024)}, u32[]{:S(2)}) copy-start(f32[1024]{0:T(1024)} %param.12) | copy-start | bytes 12292
  2.0 4.3 %copy-start.8 = (s32[2]{0:T(128)S(1)}, s32[2]{0:T(128)}, u32[]{:S(2)}) copy-start(s32[2]{0:T(128)} %lengths_ref.9) | copy-start | bytes 28
  3.2 15.6 %collective-permute-start = (f32[2,256,256]{2,1,0:T(8,128)S(1)}, f32[2,256,256]{2,1,0:T(8,128)S(1)}, u32[]{:S(2)}, u32[]{:S(2)}) collective-permute-start(f32[2,256,256]{2,1,0:T(8,128)S(1)} %get-tuple-element.118), channel_id=1, source_target_pairs={{0,16},{16,0},{1,17},{17,1},{2,18},{18,2},{3,19},{19,3},{4,20},{20... | collective-permute-start | bytes 1572872 | tf_op jit(solution)/shard_map/ppermute | solution.py:54
  6.3 12.6 %copy-start.4 = (bf16[1024,256]{1,0:T(8,128)(2,1)S(1)}, bf16[1024,256]{1,0:T(8,128)(2,1)}, u32[]{:S(2)}) copy-start(bf16[1024,256]{1,0:T(8,128)(2,1)} %head_ref.3) | copy-start | bytes 1572868
  6.3 12.6 %copy-start.6 = (f32[1024]{0:T(1024)S(1)}, f32[1024]{0:T(1024)}, u32[]{:S(2)}) copy-start(f32[1024]{0:T(1024)} %param.16) | copy-start | bytes 12292
  25.5 8.6 %collective-permute-start.1 = (bf16[2,8,64,640]{3,2,1,0:T(8,128)(2,1)S(1)}, bf16[2,8,64,640]{3,2,1,0:T(8,128)(2,1)S(1)}, u32[]{:S(2)}, u32[]{:S(2)}) collective-permute-start(bf16[2,8,64,640]{3,2,1,0:T(8,128)(2,1)S(1)} %get-tuple-element.126), channel_id=1, source_target_pairs={{0,1},{1,0},{2,3},{3,2},{4,5},{5,4},{6,7},{7,6},{8,9},{9,8},{10,11... | collective-permute-start | bytes 3932168 | tf_op jit(solution)/shard_map/ppermute | solution.py:54
  33.6 13.7 %collective-permute-start.5 = (bf16[2,8,64,512]{3,2,1,0:T(8,128)(2,1)S(1)}, bf16[2,8,64,512]{3,2,1,0:T(8,128)(2,1)S(1)}, u32[]{:S(2)}, u32[]{:S(2)}) collective-permute-start(bf16[2,8,64,512]{3,2,1,0:T(8,128)(2,1)S(1)} %get-tuple-element.139), channel_id=1, source_target_pairs={{0,1},{1,0},{2,3},{3,2},{4,5},{5,4},{6,7},{7,6},{8,9},{9,8},{10,11... | collective-permute-start | bytes 3145736 | tf_op jit(solution)/shard_map/ppermute | solution.py:54
  34.6 10.7 %collective-permute-start.2 = (bf16[2,4,64,640]{3,2,1,0:T(8,128)(2,1)S(1)}, bf16[2,4,64,640]{3,2,1,0:T(8,128)(2,1)S(1)}, u32[]{:S(2)}, u32[]{:S(2)}) collective-permute-start(bf16[2,4,64,640]{3,2,1,0:T(8,128)(2,1)S(1)} %slice.58), channel_id=1, source_target_pairs={{0,16},{1,3},{2,18},{3,1},{4,20},{5,7},{6,22},{7,5},{8,24},{9,11},... | collective-permute-start | bytes 1966088 | tf_op jit(solution)/shard_map/ppermute | solution.py:60
  44.5 4.7 %collective-permute-start.4 = (bf16[2,8,64,512]{3,2,1,0:T(8,128)(2,1)S(1)}, bf16[2,8,64,512]{3,2,1,0:T(8,128)(2,1)S(1)}, u32[]{:S(2)}, u32[]{:S(2)}) collective-permute-start(bf16[2,8,64,512]{3,2,1,0:T(8,128)(2,1)S(1)} %get-tuple-element.137), channel_id=1, source_target_pairs={{0,1},{1,0},{2,3},{3,2},{4,5},{5,4},{6,7},{7,6},{8,9},{9,8},{10,11... | collective-permute-start | bytes 3145736 | tf_op jit(solution)/shard_map/ppermute | solution.py:54
  45.4 12.4 %collective-permute-start.3 = (bf16[2,2,64,640]{3,2,1,0:T(8,128)(2,1)S(1)}, bf16[2,2,64,640]{3,2,1,0:T(8,128)(2,1)S(1)}, u32[]{:S(2)}, u32[]{:S(2)}) collective-permute-start(bf16[2,2,64,640]{3,2,1,0:T(8,128)(2,1)S(1)} %slice.76), channel_id=1, source_target_pairs={{0,2},{1,17},{2,0},{3,19},{4,6},{5,21},{6,4},{7,23},{8,10},{9,25},... | collective-permute-start | bytes 983048 | tf_op jit(solution)/shard_map/ppermute | solution.py:60
  47.6 10.0 %collective-permute-start.6 = (bf16[2,4,64,512]{3,2,1,0:T(8,128)(2,1)S(1)}, bf16[2,4,64,512]{3,2,1,0:T(8,128)(2,1)S(1)}, u32[]{:S(2)}, u32[]{:S(2)}) collective-permute-start(bf16[2,4,64,512]{3,2,1,0:T(8,128)(2,1)S(1)} %slice.77), channel_id=1, source_target_pairs={{0,16},{1,3},{2,18},{3,1},{4,20},{5,7},{6,22},{7,5},{8,24},{9,11},... | collective-permute-start | bytes 1572872 | tf_op jit(solution)/shard_map/ppermute | solution.py:60
  49.6 13.1 %collective-permute-start.9 = (bf16[2,4,64,512]{3,2,1,0:T(8,128)(2,1)S(1)}, bf16[2,4,64,512]{3,2,1,0:T(8,128)(2,1)S(1)}, u32[]{:S(2)}, u32[]{:S(2)}) collective-permute-start(bf16[2,4,64,512]{3,2,1,0:T(8,128)(2,1)S(1)} %slice.79), channel_id=1, source_target_pairs={{0,16},{1,3},{2,18},{3,1},{4,20},{5,7},{6,22},{7,5},{8,24},{9,11},... | collective-permute-start | bytes 1572872 | tf_op jit(solution)/shard_map/ppermute | solution.py:60
  56.1 8.3 %collective-permute-start.8 = (f32[32,1024]{1,0:T(8,128)S(1)}, f32[32,1024]{1,0:T(8,128)S(1)}, u32[]{:S(2)}, u32[]{:S(2)}) collective-permute-start(f32[32,1024]{1,0:T(8,128)S(1)} %taps.1), channel_id=1, source_target_pairs={{0,16},{1,3},{2,18},{3,1},{4,20},{5,7},{6,22},{7,5},{8,24},{9,11},... | collective-permute-start | bytes 393224 | tf_op jit(solution)/shard_map/ppermute | solution.py:60
  58.0 11.8 %collective-permute-start.12 = (bf16[2,1,64,640]{3,2,1,0:T(8,128)(2,1)S(1)}, bf16[2,1,64,640]{3,2,1,0:T(8,128)(2,1)S(1)}, u32[]{:S(2)}, u32[]{:S(2)}) collective-permute-start(bf16[2,1,64,640]{3,2,1,0:T(8,128)(2,1)S(1)} %slice.82), channel_id=1, source_target_pairs={{0,4},{1,9},{2,6},{3,11},{4,0},{5,13},{6,2},{7,15},{8,12},{9,1},{1... | collective-permute-start | bytes 491528 | tf_op jit(solution)/shard_map/ppermute | solution.py:60
  59.6 8.4 %collective-permute-start.7 = (bf16[2,2,64,512]{3,2,1,0:T(8,128)(2,1)S(1)}, bf16[2,2,64,512]{3,2,1,0:T(8,128)(2,1)S(1)}, u32[]{:S(2)}, u32[]{:S(2)}) collective-permute-start(bf16[2,2,64,512]{3,2,1,0:T(8,128)(2,1)S(1)} %slice.78), channel_id=1, source_target_pairs={{0,2},{1,17},{2,0},{3,19},{4,6},{5,21},{6,4},{7,23},{8,10},{9,25},... | collective-permute-start | bytes 786440 | tf_op jit(solution)/shard_map/ppermute | solution.py:60
  64.5 30.5 %collective-permute-start.20 = (f32[32,1024]{1,0:T(8,128)S(1)}, f32[32,1024]{1,0:T(8,128)S(1)}, u32[]{:S(2)}, u32[]{:S(2)}) collective-permute-start(f32[32,1024]{1,0:T(8,128)S(1)} %add.83), channel_id=1, source_target_pairs={{0,2},{1,17},{2,0},{3,19},{4,6},{5,21},{6,4},{7,23},{8,10},{9,25},... | collective-permute-start | bytes 393224 | tf_op jit(solution)/shard_map/ppermute | solution.py:60
  68.0 6.4 %collective-permute-start.11 = (bf16[2,2,64,512]{3,2,1,0:T(8,128)(2,1)S(1)}, bf16[2,2,64,512]{3,2,1,0:T(8,128)(2,1)S(1)}, u32[]{:S(2)}, u32[]{:S(2)}) collective-permute-start(bf16[2,2,64,512]{3,2,1,0:T(8,128)(2,1)S(1)} %slice.81), channel_id=1, source_target_pairs={{0,2},{1,17},{2,0},{3,19},{4,6},{5,21},{6,4},{7,23},{8,10},{9,25},... | collective-permute-start | bytes 786440 | tf_op jit(solution)/shard_map/ppermute | solution.py:60
  69.8 8.4 %collective-permute-start.10 = (bf16[2,1,64,512]{3,2,1,0:T(8,128)(2,1)S(1)}, bf16[2,1,64,512]{3,2,1,0:T(8,128)(2,1)S(1)}, u32[]{:S(2)}, u32[]{:S(2)}) collective-permute-start(bf16[2,1,64,512]{3,2,1,0:T(8,128)(2,1)S(1)} %slice.80), channel_id=1, source_target_pairs={{0,4},{1,9},{2,6},{3,11},{4,0},{5,13},{6,2},{7,15},{8,12},{9,1},{1... | collective-permute-start | bytes 393224 | tf_op jit(solution)/shard_map/ppermute | solution.py:60
  70.5 8.5 %collective-permute-start.14 = (bf16[2,1,64,640]{3,2,1,0:T(8,128)(2,1)S(1)}, bf16[2,1,64,640]{3,2,1,0:T(8,128)(2,1)S(1)}, u32[]{:S(2)}, u32[]{:S(2)}) collective-permute-start(bf16[2,1,64,640]{3,2,1,0:T(8,128)(2,1)S(1)} %add_convert_fusion.10), channel_id=1, source_target_pairs={{0,8},{1,5},{2,10},{3,7},{4,12},{5,1},{6,14},{7,3},{8,0},{9,13},{1... | collective-permute-start | bytes 491528 | tf_op jit(solution)/shard_map/ppermute | solution.py:60
  78.2 10.7 %collective-permute-start.17 = (bf16[2,1,64,512]{3,2,1,0:T(8,128)(2,1)S(1)}, bf16[2,1,64,512]{3,2,1,0:T(8,128)(2,1)S(1)}, u32[]{:S(2)}, u32[]{:S(2)}) collective-permute-start(bf16[2,1,64,512]{3,2,1,0:T(8,128)(2,1)S(1)} %add_convert_fusion.14), channel_id=1, source_target_pairs={{0,8},{1,5},{2,10},{3,7},{4,12},{5,1},{6,14},{7,3},{8,0},{9,13},{1... | collective-permute-start | bytes 393224 | tf_op jit(solution)/shard_map/ppermute | solution.py:60
  78.9 6.4 %collective-permute-start.13 = (bf16[2,1,64,512]{3,2,1,0:T(8,128)(2,1)S(1)}, bf16[2,1,64,512]{3,2,1,0:T(8,128)(2,1)S(1)}, u32[]{:S(2)}, u32[]{:S(2)}) collective-permute-start(bf16[2,1,64,512]{3,2,1,0:T(8,128)(2,1)S(1)} %slice.83), channel_id=1, source_target_pairs={{0,4},{1,9},{2,6},{3,11},{4,0},{5,13},{6,2},{7,15},{8,12},{9,1},{1... | collective-permute-start | bytes 393224 | tf_op jit(solution)/shard_map/ppermute | solution.py:60
  81.5 8.1 %collective-permute-start.16 = (bf16[2,1,64,640]{3,2,1,0:T(8,128)(2,1)S(1)}, bf16[2,1,64,640]{3,2,1,0:T(8,128)(2,1)S(1)}, u32[]{:S(2)}, u32[]{:S(2)}) collective-permute-start(bf16[2,1,64,640]{3,2,1,0:T(8,128)(2,1)S(1)} %add_convert_fusion.9), channel_id=1, source_target_pairs={{0,4},{1,9},{2,6},{3,11},{4,0},{5,13},{6,2},{7,15},{8,12},{9,1},{1... | collective-permute-start | bytes 491528 | tf_op jit(solution)/shard_map/ppermute | solution.py:60
  85.3 9.5 %collective-permute-start.15 = (bf16[2,1,64,512]{3,2,1,0:T(8,128)(2,1)S(1)}, bf16[2,1,64,512]{3,2,1,0:T(8,128)(2,1)S(1)}, u32[]{:S(2)}, u32[]{:S(2)}) collective-permute-start(bf16[2,1,64,512]{3,2,1,0:T(8,128)(2,1)S(1)} %add_convert_fusion.13), channel_id=1, source_target_pairs={{0,8},{1,5},{2,10},{3,7},{4,12},{5,1},{6,14},{7,3},{8,0},{9,13},{1... | collective-permute-start | bytes 393224 | tf_op jit(solution)/shard_map/ppermute | solution.py:60
  89.0 8.1 %collective-permute-start.19 = (bf16[2,1,64,512]{3,2,1,0:T(8,128)(2,1)S(1)}, bf16[2,1,64,512]{3,2,1,0:T(8,128)(2,1)S(1)}, u32[]{:S(2)}, u32[]{:S(2)}) collective-permute-start(bf16[2,1,64,512]{3,2,1,0:T(8,128)(2,1)S(1)} %add_convert_fusion.12), channel_id=1, source_target_pairs={{0,4},{1,9},{2,6},{3,11},{4,0},{5,13},{6,2},{7,15},{8,12},{9,1},{1... | collective-permute-start | bytes 393224 | tf_op jit(solution)/shard_map/ppermute | solution.py:60
  89.5 14.8 %collective-permute-start.18 = (bf16[2,2,64,640]{3,2,1,0:T(8,128)(2,1)S(1)}, bf16[2,2,64,640]{3,2,1,0:T(8,128)(2,1)S(1)}, u32[]{:S(2)}, u32[]{:S(2)}) collective-permute-start(bf16[2,2,64,640]{3,2,1,0:T(8,128)(2,1)S(1)} %constant_dynamic-update-slice_fusion), channel_id=1, source_target_pairs={{0,2},{1,17},{2,0},{3,19},{4,6},{5,21},{6,4},{7,23},{8,10},{9,25},... | collective-permute-start | bytes 983048 | tf_op jit(solution)/shard_map/ppermute | solution.py:60
  94.9 9.7 %collective-permute-start.24 = (bf16[2,1,64,512]{3,2,1,0:T(8,128)(2,1)S(1)}, bf16[2,1,64,512]{3,2,1,0:T(8,128)(2,1)S(1)}, u32[]{:S(2)}, u32[]{:S(2)}) collective-permute-start(bf16[2,1,64,512]{3,2,1,0:T(8,128)(2,1)S(1)} %add_convert_fusion.11), channel_id=1, source_target_pairs={{0,4},{1,9},{2,6},{3,11},{4,0},{5,13},{6,2},{7,15},{8,12},{9,1},{1... | collective-permute-start | bytes 393224 | tf_op jit(solution)/shard_map/ppermute | solution.py:60
  95.0 9.6 %collective-permute-start.23 = (f32[32,1024]{1,0:T(8,128)S(1)}, f32[32,1024]{1,0:T(8,128)S(1)}, u32[]{:S(2)}, u32[]{:S(2)}) collective-permute-start(f32[32,1024]{1,0:T(8,128)S(1)} %add.92), channel_id=1, source_target_pairs={{0,4},{1,9},{2,6},{3,11},{4,0},{5,13},{6,2},{7,15},{8,12},{9,1},{1... | collective-permute-start | bytes 393224 | tf_op jit(solution)/shard_map/ppermute | solution.py:60
  97.1 14.5 %collective-permute-start.22 = (bf16[2,2,64,512]{3,2,1,0:T(8,128)(2,1)S(1)}, bf16[2,2,64,512]{3,2,1,0:T(8,128)(2,1)S(1)}, u32[]{:S(2)}, u32[]{:S(2)}) collective-permute-start(bf16[2,2,64,512]{3,2,1,0:T(8,128)(2,1)S(1)} %constant_dynamic-update-slice_fusion.2), channel_id=1, source_target_pairs={{0,2},{1,17},{2,0},{3,19},{4,6},{5,21},{6,4},{7,23},{8,10},{9,25},... | collective-permute-start | bytes 786440 | tf_op jit(solution)/shard_map/ppermute | solution.py:60
  104.4 13.5 %collective-permute-start.21 = (bf16[2,4,64,640]{3,2,1,0:T(8,128)(2,1)S(1)}, bf16[2,4,64,640]{3,2,1,0:T(8,128)(2,1)S(1)}, u32[]{:S(2)}, u32[]{:S(2)}) collective-permute-start(bf16[2,4,64,640]{3,2,1,0:T(8,128)(2,1)S(1)} %constant_dynamic-update-slice_fusion.4), channel_id=1, source_target_pairs={{0,16},{1,3},{2,18},{3,1},{4,20},{5,7},{6,22},{7,5},{8,24},{9,11},... | collective-permute-start | bytes 1966088 | tf_op jit(solution)/shard_map/ppermute | solution.py:60
  111.6 11.9 %collective-permute-start.25 = (bf16[2,4,64,512]{3,2,1,0:T(8,128)(2,1)S(1)}, bf16[2,4,64,512]{3,2,1,0:T(8,128)(2,1)S(1)}, u32[]{:S(2)}, u32[]{:S(2)}) collective-permute-start(bf16[2,4,64,512]{3,2,1,0:T(8,128)(2,1)S(1)} %constant_dynamic-update-slice_fusion.8), channel_id=1, source_target_pairs={{0,16},{1,3},{2,18},{3,1},{4,20},{5,7},{6,22},{7,5},{8,24},{9,11},... | collective-permute-start | bytes 1572872 | tf_op jit(solution)/shard_map/ppermute | solution.py:60
  111.7 9.9 %collective-permute-start.26 = (f32[32,1024]{1,0:T(8,128)S(1)}, f32[32,1024]{1,0:T(8,128)S(1)}, u32[]{:S(2)}, u32[]{:S(2)}) collective-permute-start(f32[32,1024]{1,0:T(8,128)S(1)} %add.93), channel_id=1, source_target_pairs={{0,8},{1,5},{2,10},{3,7},{4,12},{5,1},{6,14},{7,3},{8,0},{9,13},{1... | collective-permute-start | bytes 393224 | tf_op jit(solution)/shard_map/ppermute | solution.py:60
  114.3 7.2 %collective-permute-start.27 = (bf16[2,2,64,512]{3,2,1,0:T(8,128)(2,1)S(1)}, bf16[2,2,64,512]{3,2,1,0:T(8,128)(2,1)S(1)}, u32[]{:S(2)}, u32[]{:S(2)}) collective-permute-start(bf16[2,2,64,512]{3,2,1,0:T(8,128)(2,1)S(1)} %constant_dynamic-update-slice_fusion.6), channel_id=1, source_target_pairs={{0,2},{1,17},{2,0},{3,19},{4,6},{5,21},{6,4},{7,23},{8,10},{9,25},... | collective-permute-start | bytes 786440 | tf_op jit(solution)/shard_map/ppermute | solution.py:60
  118.0 6.2 %collective-permute-start.30 = (bf16[2,8,64,640]{3,2,1,0:T(8,128)(2,1)S(1)}, bf16[2,8,64,640]{3,2,1,0:T(8,128)(2,1)S(1)}, u32[]{:S(2)}, u32[]{:S(2)}) collective-permute-start(bf16[2,8,64,640]{3,2,1,0:T(8,128)(2,1)S(1)} %constant_dynamic-update-slice_fusion.10.mine_ref), channel_id=1, source_target_pairs={{0,1},{1,0},{2,3},{3,2},{4,5},{5,4},{6,7},{7,6},{8,9},{9,8},{10,11... | collective-permute-start | bytes 3932168 | tf_op jit(solution)/shard_map/ppermute | solution.py:54
  123.6 2.9 %collective-permute-start.28 = (bf16[2,8,64,512]{3,2,1,0:T(8,128)(2,1)S(1)}, bf16[2,8,64,512]{3,2,1,0:T(8,128)(2,1)S(1)}, u32[]{:S(2)}, u32[]{:S(2)}) collective-permute-start(bf16[2,8,64,512]{3,2,1,0:T(8,128)(2,1)S(1)} %constant_dynamic-update-slice_fusion.14.refs_0_), channel_id=1, source_target_pairs={{0,1},{1,0},{2,3},{3,2},{4,5},{5,4},{6,7},{7,6},{8,9},{9,8},{10,11... | collective-permute-start | bytes 3145736 | tf_op jit(solution)/shard_map/ppermute | solution.py:54
  123.7 9.2 %collective-permute-start.31 = (bf16[2,4,64,512]{3,2,1,0:T(8,128)(2,1)S(1)}, bf16[2,4,64,512]{3,2,1,0:T(8,128)(2,1)S(1)}, u32[]{:S(2)}, u32[]{:S(2)}) collective-permute-start(bf16[2,4,64,512]{3,2,1,0:T(8,128)(2,1)S(1)} %constant_dynamic-update-slice_fusion.12), channel_id=1, source_target_pairs={{0,16},{1,3},{2,18},{3,1},{4,20},{5,7},{6,22},{7,5},{8,24},{9,11},... | collective-permute-start | bytes 1572872 | tf_op jit(solution)/shard_map/ppermute | solution.py:60
  123.8 2.8 %collective-permute-start.29 = (f32[32,1024]{1,0:T(8,128)S(1)}, f32[32,1024]{1,0:T(8,128)S(1)}, u32[]{:S(2)}, u32[]{:S(2)}) collective-permute-start(f32[32,1024]{1,0:T(8,128)S(1)} %add.94), channel_id=1, source_target_pairs={{0,1},{1,0},{2,3},{3,2},{4,5},{5,4},{6,7},{7,6},{8,9},{9,8},{10,11... | collective-permute-start | bytes 393224 | tf_op jit(solution)/shard_map/ppermute | solution.py:54
  133.0 4.2 %collective-permute-start.32 = (bf16[2,8,64,512]{3,2,1,0:T(8,128)(2,1)S(1)}, bf16[2,8,64,512]{3,2,1,0:T(8,128)(2,1)S(1)}, u32[]{:S(2)}, u32[]{:S(2)}) collective-permute-start(bf16[2,8,64,512]{3,2,1,0:T(8,128)(2,1)S(1)} %constant_dynamic-update-slice_fusion.16.refs_2_), channel_id=1, source_target_pairs={{0,1},{1,0},{2,3},{3,2},{4,5},{5,4},{6,7},{7,6},{8,9},{9,8},{10,11... | collective-permute-start | bytes 3145736 | tf_op jit(solution)/shard_map/ppermute | solution.py:54

commit v15 on v14

--- a/solution.py
+++ b/solution.py
@@ -17,7 +17,7 @@
 ORDER = (
     "top", "in0", "in1", "taps", "in0", "top", "in1", "small", "in0", "top", "in1", "in0",
     "top", "in1", "in0", "top", "in1", "small", "in0", "top", "in1", "small", "in0", "top",
-    "in1", "small", "in0", "top", "small", "in0", "in1", "write_top", "in1", "write_in",
+    "in1", "small", "in0", "top", "small", "in0", "write_top", "in1", "in1", "write_in",
 )
 SMEM_SPEC = pl.BlockSpec(memory_space=pltpu.SMEM)
 F32 = jnp.float32

time: 142 us -> 141 us (level)
    ppermute x25, waiting for transfers between devices: 35.6 us -> 32.6 us  [exchange(): lax.ppermute(values, ALL, [(i, i ^ bits[place ^ i % 2]) for i in range(co...]
    ppermute x8, waiting for transfers between devices: 2.3 us -> 4.32 us  [exchange(): return lax.ppermute(values, step, [(0, 1), (1, 0)])]
  transfers between devices with their start and end apart: 33 -> 33, of which waited for: 14 -> 15; matrix products, arithmetic and copies ran while one was open for 2% -> 2% of each run, Pallas kernels for 27% -> 27%
where the time goes in v15:
time: 141 us; the launch traced here: 140 us
  Pallas kernels  50.2 us (36%)
  starting transfers between devices  47.4 us (34%)
  waiting for transfers between devices  36.9 us (26%)
  local copies, waits for them, and re-layouts  2.65 us (2%)
  other arithmetic  2.13 us (2%)
    ppermute x25, starting transfers between devices, exchange(): lax.ppermute(values, ALL, [(i, i ^ bits[place ^ i % 2]) for i in range(co...  43 us
    ppermute x25, waiting for transfers between devices, exchange(): lax.ppermute(values, ALL, [(i, i ^ bits[place ^ i % 2]) for i in range(co...  32.6 us
    pallas_call x2, Pallas kernels, inner(): pl.pallas_call(inner_kernel, grid=(steps,), out_shape=(shape, shape, jax....  16.1 us
    pallas_call x1, Pallas kernels, forward(): pl.pallas_call(forward_kernel, grid=(steps,), out_shape=(jax.ShapeDtypeSt...  12.6 us
    pallas_call x1, Pallas kernels, tap_sums(): pl.pallas_call(taps_kernel, grid=(steps,), out_shape=jax.ShapeDtypeStruct...  5.91 us
    ppermute x8, starting transfers between devices, exchange(): return lax.ppermute(values, step, [(0, 1), (1, 0)])  4.4 us
    pallas_call x1, Pallas kernels, unpack_inner(): pl.pallas_call(functools.partial(unpack_inner_kernel, utts), out_shape=(j...  4.35 us
    ppermute x8, waiting for transfers between devices, exchange(): return lax.ppermute(values, step, [(0, 1), (1, 0)])  4.32 us
  transfers between devices with their start and end apart: 33, of which 15 were waited for; matrix products, arithmetic and copies ran while one was open for 2% of the time, Pallas kernels for 27%

profile of v15, /device:TPU:0, one launch (start us, length us, event | category | flops | bytes accessed | tf_op | source)
XLA Modules:
  0.0 140.5 jit_solution(11319349992112353347)
XLA Ops:
  0.7 1.2 copy-done.2
  2.0 1.2 teachers.1
  3.2 3.0 %collective-permute-start = (f32[2,256,256]{2,1,0:T(8,128)S(1)}, f32[2,256,256]{2,1,0:T(8,128)S(1)}, u32[]{:S(2)}, u32[]{:S(2)}) collective-permute-start(f32[2,256,256]{2,1,0:T(8,128)S(1)} %get-tuple-element.118), channel_id=1, source_target_pairs={{0,16},{16,0},{1,17},{17,1},{2,18},{18,2},{3,19},{19,3},{4,20},{20... | collective-permute-start | bytes 1572872 | tf_op jit(solution)/shard_map/ppermute | solution.py:54
  6.3 12.6 %forward.1 = (bf16[1024,512]{1,0:T(8,128)(2,1)S(1)}, f32[512,1024]{1,0:T(8,128)S(1)}, f32[512,1024]{1,0:T(8,128)S(1)}, f32[512,1024]{1,0:T(8,128)S(1)}, bf16[512...) custom-call(s32[2]{0:T(128)S(1)} %copy-done.8, bf16[512,1024]{1,0:T(8,128)(2,1)S(1)} %bitcast.9, f32[1,1024]{1,0:T(1,128)S(1)} %bitcast.12, ...), custom_call_target="tpu_custom_call" | custom-call | flops 17250000896 | bytes 1048576 | tf_op jit(solution)/shard_map/forward/pallas_call | solution.py:323
  18.9 3.4 %top.1 = (f32[2,1,128]{2,1,0:T(1,128)S(1)}, bf16[512,1024]{1,0:T(8,128)(2,1)S(1)}, bf16[512,256]{1,0:T(8,128)(2,1)S(1)}, bf16[512,1024]{1,0:T(8,128)(2,1)S(1)}) custom-call(s32[2]{0:T(128)S(1)} %copy-done.8, f32[512,1024]{1,0:T(8,128)S(1)} %get-tuple-element.114.residual_ref, f32[1,1024]{1,0:T(1,128)S(1)} %bitcast.10, bf16[1024,256]{1,0:T(8,128)(2,1)S(1)} %copy-done.4, ...), custom_call_target="tpu_custom_call" | custom-call | flops 5750000128 | bytes 1048576 | tf_op jit(solution)/shard_map/top/pallas_call | solution.py:392
  22.4 3.2 %outer.1 = (bf16[2,8,64,640]{3,2,1,0:T(8,128)(2,1)S(1)}, bf16[2,8,64,640]{3,2,1,0:T(8,128)(2,1)S(1)}) custom-call(s32[3]{0:T(128)S(1)} %pad_add_fusion.own_ref, bf16[512,1024]{1,0:T(8,128)(2,1)S(1)} %get-tuple-element.113.active_ref, bf16[512,1024]{1,0:T(8,128)(2,1)S(1)} %get-tuple-element.134.dresidual_ref, ...), custom_call_target="tpu_custom_call" | custom-call | flops 5750000128 | bytes 1048576 | tf_op jit(solution)/shard_map/outer/pallas_call | solution.py:431
  25.6 8.0 %inner.2 = (bf16[2,8,64,512]{3,2,1,0:T(8,128)(2,1)S(1)}, bf16[2,8,64,512]{3,2,1,0:T(8,128)(2,1)S(1)}, f32[512,512]{1,0:T(8,128)S(1)}) custom-call(s32[3]{0:T(128)S(1)} %pad_add_fusion.own_ref, s32[2]{0:T(128)S(1)} %copy-done.8, bf16[512,1024]{1,0:T(8,128)(2,1)S(1)} %get-tuple-element.134.dresidual_ref, bf16[1024,1024]{1,0:T(8,128)(2,1)S(1)} %copy-done.1, ...), custom_call_target="tpu_custom_call" | custom-call | flops 12650000384 | bytes 1048576 | tf_op jit(solution)/shard_map/inner/pallas_call | solution.py:516
  33.6 0.5 collective-permute-start.5
  34.6 1.8 %collective-permute-start.2 = (bf16[2,4,64,640]{3,2,1,0:T(8,128)(2,1)S(1)}, bf16[2,4,64,640]{3,2,1,0:T(8,128)(2,1)S(1)}, u32[]{:S(2)}, u32[]{:S(2)}) collective-permute-start(bf16[2,4,64,640]{3,2,1,0:T(8,128)(2,1)S(1)} %slice.58), channel_id=1, source_target_pairs={{0,16},{1,3},{2,18},{3,1},{4,20},{5,7},{6,22},{7,5},{8,24},{9,11},... | collective-permute-start | bytes 1966088 | tf_op jit(solution)/shard_map/ppermute | solution.py:60
  36.4 8.1 %inner.3 = (bf16[2,8,64,512]{3,2,1,0:T(8,128)(2,1)S(1)}, bf16[2,8,64,512]{3,2,1,0:T(8,128)(2,1)S(1)}, f32[512,512]{1,0:T(8,128)S(1)}) custom-call(s32[3]{0:T(128)S(1)} %pad_add_fusion.own_ref, s32[2]{0:T(128)S(1)} %copy-done.8, bf16[512,1024]{1,0:T(8,128)(2,1)S(1)} %get-tuple-element.134.dresidual_ref, bf16[1024,1024]{1,0:T(8,128)(2,1)S(1)} %copy-done.1, ...), custom_call_target="tpu_custom_call" | custom-call | flops 12650000384 | bytes 1048576 | tf_op jit(solution)/shard_map/inner/pallas_call | solution.py:516
  44.6 0.7 collective-permute-done.2
  45.4 1.8 %collective-permute-start.3 = (bf16[2,2,64,640]{3,2,1,0:T(8,128)(2,1)S(1)}, bf16[2,2,64,640]{3,2,1,0:T(8,128)(2,1)S(1)}, u32[]{:S(2)}, u32[]{:S(2)}) collective-permute-start(bf16[2,2,64,640]{3,2,1,0:T(8,128)(2,1)S(1)} %slice.76), channel_id=1, source_target_pairs={{0,2},{1,17},{2,0},{3,19},{4,6},{5,21},{6,4},{7,23},{8,10},{9,25},... | collective-permute-start | bytes 983048 | tf_op jit(solution)/shard_map/ppermute | solution.py:60
  47.6 1.6 %collective-permute-start.6 = (bf16[2,4,64,512]{3,2,1,0:T(8,128)(2,1)S(1)}, bf16[2,4,64,512]{3,2,1,0:T(8,128)(2,1)S(1)}, u32[]{:S(2)}, u32[]{:S(2)}) collective-permute-start(bf16[2,4,64,512]{3,2,1,0:T(8,128)(2,1)S(1)} %slice.77), channel_id=1, source_target_pairs={{0,16},{1,3},{2,18},{3,1},{4,20},{5,7},{6,22},{7,5},{8,24},{9,11},... | collective-permute-start | bytes 1572872 | tf_op jit(solution)/shard_map/ppermute | solution.py:60
  49.6 0.6 collective-permute-start.9
  50.2 5.9 %taps.1 = f32[32,1024]{1,0:T(8,128)S(1)} custom-call(s32[2]{0:T(128)S(1)} %copy-done.8, f32[512,1024]{1,0:T(8,128)S(1)} %get-tuple-element.128.gated_ref, f32[512,512]{1,0:T(8,128)S(1)} %get-tuple-element.146.refs_0_, f32[512,512]{1,0:T(8,128)S(1)} %get-tuple-element.147.refs_1_), custom_call_target="tpu_custom_call" | custom-call | flops 10350000128 | bytes 1048576 | tf_op jit(solution)/shard_map/taps/pallas_call | solution.py:598
  56.1 1.6 %collective-permute-start.8 = (f32[32,1024]{1,0:T(8,128)S(1)}, f32[32,1024]{1,0:T(8,128)S(1)}, u32[]{:S(2)}, u32[]{:S(2)}) collective-permute-start(f32[32,1024]{1,0:T(8,128)S(1)} %taps.1), channel_id=1, source_target_pairs={{0,16},{1,3},{2,18},{3,1},{4,20},{5,7},{6,22},{7,5},{8,24},{9,11},... | collective-permute-start | bytes 393224 | tf_op jit(solution)/shard_map/ppermute | solution.py:60
  58.0 1.6 %collective-permute-start.12 = (bf16[2,1,64,640]{3,2,1,0:T(8,128)(2,1)S(1)}, bf16[2,1,64,640]{3,2,1,0:T(8,128)(2,1)S(1)}, u32[]{:S(2)}, u32[]{:S(2)}) collective-permute-start(bf16[2,1,64,640]{3,2,1,0:T(8,128)(2,1)S(1)} %slice.82), channel_id=1, source_target_pairs={{0,4},{1,9},{2,6},{3,11},{4,0},{5,13},{6,2},{7,15},{8,12},{9,1},{1... | collective-permute-start | bytes 491528 | tf_op jit(solution)/shard_map/ppermute | solution.py:60
  59.6 0.9 collective-permute-start.7
  60.5 2.1 %collective-permute-done.9 = bf16[2,4,64,512]{3,2,1,0:T(8,128)(2,1)S(1)} collective-permute-done((bf16[2,4,64,512]{3,2,1,0:T(8,128)(2,1)S(1)}, bf16[2,4,64,512]{3,2,1,0:T(8,128)(2,1)S(1)}, u32[]{:S(2)}, u32[]{:S(2)}) %collective-permute-start.9) | collective-permute-done | bytes 524320 | tf_op jit(solution)/shard_map/ppermute | solution.py:60
  62.9 1.6 %collective-permute-done.8 = f32[32,1024]{1,0:T(8,128)S(1)} collective-permute-done((f32[32,1024]{1,0:T(8,128)S(1)}, f32[32,1024]{1,0:T(8,128)S(1)}, u32[]{:S(2)}, u32[]{:S(2)}) %collective-permute-start.8) | collective-permute-done | bytes 131104 | tf_op jit(solution)/shard_map/ppermute | solution.py:60
  64.5 1.6 %collective-permute-start.20 = (f32[32,1024]{1,0:T(8,128)S(1)}, f32[32,1024]{1,0:T(8,128)S(1)}, u32[]{:S(2)}, u32[]{:S(2)}) collective-permute-start(f32[32,1024]{1,0:T(8,128)S(1)} %add.83), channel_id=1, source_target_pairs={{0,2},{1,17},{2,0},{3,19},{4,6},{5,21},{6,4},{7,23},{8,10},{9,25},... | collective-permute-start | bytes 393224 | tf_op jit(solution)/shard_map/ppermute | solution.py:60
  66.0 2.0 %collective-permute-done.7 = bf16[2,2,64,512]{3,2,1,0:T(8,128)(2,1)S(1)} collective-permute-done((bf16[2,2,64,512]{3,2,1,0:T(8,128)(2,1)S(1)}, bf16[2,2,64,512]{3,2,1,0:T(8,128)(2,1)S(1)}, u32[]{:S(2)}, u32[]{:S(2)}) %collective-permute-start.7) | collective-permute-done | bytes 262176 | tf_op jit(solution)/shard_map/ppermute | solution.py:60
  68.0 1.6 %collective-permute-start.11 = (bf16[2,2,64,512]{3,2,1,0:T(8,128)(2,1)S(1)}, bf16[2,2,64,512]{3,2,1,0:T(8,128)(2,1)S(1)}, u32[]{:S(2)}, u32[]{:S(2)}) collective-permute-start(bf16[2,2,64,512]{3,2,1,0:T(8,128)(2,1)S(1)} %slice.81), channel_id=1, source_target_pairs={{0,2},{1,17},{2,0},{3,19},{4,6},{5,21},{6,4},{7,23},{8,10},{9,25},... | collective-permute-start | bytes 786440 | tf_op jit(solution)/shard_map/ppermute | solution.py:60
  69.8 0.6 collective-permute-start.10
  70.5 2.8 %collective-permute-start.14 = (bf16[2,1,64,640]{3,2,1,0:T(8,128)(2,1)S(1)}, bf16[2,1,64,640]{3,2,1,0:T(8,128)(2,1)S(1)}, u32[]{:S(2)}, u32[]{:S(2)}) collective-permute-start(bf16[2,1,64,640]{3,2,1,0:T(8,128)(2,1)S(1)} %add_convert_fusion.10), channel_id=1, source_target_pairs={{0,8},{1,5},{2,10},{3,7},{4,12},{5,1},{6,14},{7,3},{8,0},{9,13},{1... | collective-permute-start | bytes 491528 | tf_op jit(solution)/shard_map/ppermute | solution.py:60
  73.2 1.2 collective-permute-done.11
  74.5 3.7 %collective-permute-done.10 = bf16[2,1,64,512]{3,2,1,0:T(8,128)(2,1)S(1)} collective-permute-done((bf16[2,1,64,512]{3,2,1,0:T(8,128)(2,1)S(1)}, bf16[2,1,64,512]{3,2,1,0:T(8,128)(2,1)S(1)}, u32[]{:S(2)}, u32[]{:S(2)}) %collective-permute-start.10) | collective-permute-done | bytes 131104 | tf_op jit(solution)/shard_map/ppermute | solution.py:60
  78.2 0.7 collective-permute-start.17
  78.9 2.5 %collective-permute-start.13 = (bf16[2,1,64,512]{3,2,1,0:T(8,128)(2,1)S(1)}, bf16[2,1,64,512]{3,2,1,0:T(8,128)(2,1)S(1)}, u32[]{:S(2)}, u32[]{:S(2)}) collective-permute-start(bf16[2,1,64,512]{3,2,1,0:T(8,128)(2,1)S(1)} %slice.83), channel_id=1, source_target_pairs={{0,4},{1,9},{2,6},{3,11},{4,0},{5,13},{6,2},{7,15},{8,12},{9,1},{1... | collective-permute-start | bytes 393224 | tf_op jit(solution)/shard_map/ppermute | solution.py:60
  81.5 3.8 %collective-permute-done.13 = bf16[2,1,64,512]{3,2,1,0:T(8,128)(2,1)S(1)} collective-permute-done((bf16[2,1,64,512]{3,2,1,0:T(8,128)(2,1)S(1)}, bf16[2,1,64,512]{3,2,1,0:T(8,128)(2,1)S(1)}, u32[]{:S(2)}, u32[]{:S(2)}) %collective-permute-start.13) | collective-permute-done | bytes 131104 | tf_op jit(solution)/shard_map/ppermute | solution.py:60
  85.3 3.3 %collective-permute-start.15 = (bf16[2,1,64,512]{3,2,1,0:T(8,128)(2,1)S(1)}, bf16[2,1,64,512]{3,2,1,0:T(8,128)(2,1)S(1)}, u32[]{:S(2)}, u32[]{:S(2)}) collective-permute-start(bf16[2,1,64,512]{3,2,1,0:T(8,128)(2,1)S(1)} %add_convert_fusion.13), channel_id=1, source_target_pairs={{0,8},{1,5},{2,10},{3,7},{4,12},{5,1},{6,14},{7,3},{8,0},{9,13},{1... | collective-permute-start | bytes 393224 | tf_op jit(solution)/shard_map/ppermute | solution.py:60
  89.0 0.5 collective-permute-start.19
  89.5 5.3 %collective-permute-start.18 = (bf16[2,2,64,640]{3,2,1,0:T(8,128)(2,1)S(1)}, bf16[2,2,64,640]{3,2,1,0:T(8,128)(2,1)S(1)}, u32[]{:S(2)}, u32[]{:S(2)}) collective-permute-start(bf16[2,2,64,640]{3,2,1,0:T(8,128)(2,1)S(1)} %constant_dynamic-update-slice_fusion), channel_id=1, source_target_pairs={{0,2},{1,17},{2,0},{3,19},{4,6},{5,21},{6,4},{7,23},{8,10},{9,25},... | collective-permute-start | bytes 983048 | tf_op jit(solution)/shard_map/ppermute | solution.py:60
  95.0 2.1 %collective-permute-start.23 = (f32[32,1024]{1,0:T(8,128)S(1)}, f32[32,1024]{1,0:T(8,128)S(1)}, u32[]{:S(2)}, u32[]{:S(2)}) collective-permute-start(f32[32,1024]{1,0:T(8,128)S(1)} %add.92), channel_id=1, source_target_pairs={{0,4},{1,9},{2,6},{3,11},{4,0},{5,13},{6,2},{7,15},{8,12},{9,1},{1... | collective-permute-start | bytes 393224 | tf_op jit(solution)/shard_map/ppermute | solution.py:60
  97.1 7.3 %collective-permute-start.22 = (bf16[2,2,64,512]{3,2,1,0:T(8,128)(2,1)S(1)}, bf16[2,2,64,512]{3,2,1,0:T(8,128)(2,1)S(1)}, u32[]{:S(2)}, u32[]{:S(2)}) collective-permute-start(bf16[2,2,64,512]{3,2,1,0:T(8,128)(2,1)S(1)} %constant_dynamic-update-slice_fusion.2), channel_id=1, source_target_pairs={{0,2},{1,17},{2,0},{3,19},{4,6},{5,21},{6,4},{7,23},{8,10},{9,25},... | collective-permute-start | bytes 786440 | tf_op jit(solution)/shard_map/ppermute | solution.py:60
  104.6 6.9 %collective-permute-done.22 = bf16[2,2,64,512]{3,2,1,0:T(8,128)(2,1)S(1)} collective-permute-done((bf16[2,2,64,512]{3,2,1,0:T(8,128)(2,1)S(1)}, bf16[2,2,64,512]{3,2,1,0:T(8,128)(2,1)S(1)}, u32[]{:S(2)}, u32[]{:S(2)}) %collective-permute-start.22) | collective-permute-done | bytes 262176 | tf_op jit(solution)/shard_map/ppermute | solution.py:60
  111.7 2.6 %collective-permute-start.26 = (f32[32,1024]{1,0:T(8,128)S(1)}, f32[32,1024]{1,0:T(8,128)S(1)}, u32[]{:S(2)}, u32[]{:S(2)}) collective-permute-start(f32[32,1024]{1,0:T(8,128)S(1)} %add.93), channel_id=1, source_target_pairs={{0,8},{1,5},{2,10},{3,7},{4,12},{5,1},{6,14},{7,3},{8,0},{9,13},{1... | collective-permute-start | bytes 393224 | tf_op jit(solution)/shard_map/ppermute | solution.py:60
  114.3 2.0 %collective-permute-start.27 = (bf16[2,2,64,512]{3,2,1,0:T(8,128)(2,1)S(1)}, bf16[2,2,64,512]{3,2,1,0:T(8,128)(2,1)S(1)}, u32[]{:S(2)}, u32[]{:S(2)}) collective-permute-start(bf16[2,2,64,512]{3,2,1,0:T(8,128)(2,1)S(1)} %constant_dynamic-update-slice_fusion.6), channel_id=1, source_target_pairs={{0,2},{1,17},{2,0},{3,19},{4,6},{5,21},{6,4},{7,23},{8,10},{9,25},... | collective-permute-start | bytes 786440 | tf_op jit(solution)/shard_map/ppermute | solution.py:60
  116.4 1.5 %collective-permute-done.21 = bf16[2,4,64,640]{3,2,1,0:T(8,128)(2,1)S(1)} collective-permute-done((bf16[2,4,64,640]{3,2,1,0:T(8,128)(2,1)S(1)}, bf16[2,4,64,640]{3,2,1,0:T(8,128)(2,1)S(1)}, u32[]{:S(2)}, u32[]{:S(2)}) %collective-permute-start.21) | collective-permute-done | bytes 655392 | tf_op jit(solution)/shard_map/ppermute | solution.py:60
  118.1 3.4 %collective-permute-done.27 = bf16[2,2,64,512]{3,2,1,0:T(8,128)(2,1)S(1)} collective-permute-done((bf16[2,2,64,512]{3,2,1,0:T(8,128)(2,1)S(1)}, bf16[2,2,64,512]{3,2,1,0:T(8,128)(2,1)S(1)}, u32[]{:S(2)}, u32[]{:S(2)}) %collective-permute-start.27) | collective-permute-done | bytes 262176 | tf_op jit(solution)/shard_map/ppermute | solution.py:60
  121.6 1.9 %collective-permute-done.25 = bf16[2,4,64,512]{3,2,1,0:T(8,128)(2,1)S(1)} collective-permute-done((bf16[2,4,64,512]{3,2,1,0:T(8,128)(2,1)S(1)}, bf16[2,4,64,512]{3,2,1,0:T(8,128)(2,1)S(1)}, u32[]{:S(2)}, u32[]{:S(2)}) %collective-permute-start.25) | collective-permute-done | bytes 524320 | tf_op jit(solution)/shard_map/ppermute | solution.py:60
  123.7 0.5 collective-permute-start.29
  124.3 2.3 %collective-permute-done.29 = f32[32,1024]{1,0:T(8,128)S(1)} collective-permute-done((f32[32,1024]{1,0:T(8,128)S(1)}, f32[32,1024]{1,0:T(8,128)S(1)}, u32[]{:S(2)}, u32[]{:S(2)}) %collective-permute-start.29) | collective-permute-done | bytes 131104 | tf_op jit(solution)/shard_map/ppermute | solution.py:54
  126.6 3.5 %unpack_top.1 = (f32[1024,1024]{1,0:T(8,128)}, f32[1024,256]{1,0:T(8,128)}, f32[1,1024]{1,0:T(1,128)}, f32[31,1024]{1,0:T(8,128)}, f32[2,1,128]{2,1,0:T(1,128)S(1)}) custom-call(s32[3]{0:T(128)S(1)} %pad_add_fusion.own_ref, f32[32,1024]{1,0:T(8,128)S(1)} %add.95.small_ref, bf16[2,8,64,640]{3,2,1,0:T(8,128)(2,1)S(1)} %constant_dynamic-update-slice_fusion.10.mine_ref, ...), custom_call_target="tpu_custom_call" | custom-call | flops 5750000128 | bytes 1048576 | tf_op jit(solution)/shard_map/unpack_top/pallas_call | solution.py:687
  130.0 3.3 %collective-permute-done.31 = bf16[2,4,64,512]{3,2,1,0:T(8,128)(2,1)S(1)} collective-permute-done((bf16[2,4,64,512]{3,2,1,0:T(8,128)(2,1)S(1)}, bf16[2,4,64,512]{3,2,1,0:T(8,128)(2,1)S(1)}, u32[]{:S(2)}, u32[]{:S(2)}) %collective-permute-start.31) | collective-permute-done | bytes 524320 | tf_op jit(solution)/shard_map/ppermute | solution.py:60
  133.5 0.6 slice_reduce_fusion
  134.1 2.0 %collective-permute-done.32.refs_3_ = bf16[2,8,64,512]{3,2,1,0:T(8,128)(2,1)S(1)} collective-permute-done((bf16[2,8,64,512]{3,2,1,0:T(8,128)(2,1)S(1)}, bf16[2,8,64,512]{3,2,1,0:T(8,128)(2,1)S(1)}, u32[]{:S(2)}, u32[]{:S(2)}) %collective-permute-start.32) | collective-permute-done | bytes 1048608 | tf_op jit(solution)/shard_map/ppermute | solution.py:54
  136.1 4.4 %unpack_inner.1 = (f32[1024,2048]{1,0:T(8,128)}, f32[1,1024]{1,0:T(1,128)}) custom-call(s32[3]{0:T(128)S(1)} %pad_add_fusion.own_ref, f32[32,1024]{1,0:T(8,128)S(1)} %add.95.small_ref, bf16[1024,2048]{1,0:T(8,128)(2,1)S(1)} %copy-done, f32[1,1024]{1,0:T(1,128)S(1)} %bitcast.13, bf16[2,8,64,512]{3,2,1,0:T(8,128)(2,1)S(1)} %constant_dynamic-update-slice_fusion.14.refs_0_, ...), custom_call_target="tpu_custom_call" | custom-call | flops 9200000000 | bytes 1048576 | tf_op jit(solution)/shard_map/unpack_inner/pallas_call | solution.py:740
  (94 shorter events, 4.0 us)
Async XLA Ops:
  0.7 1.2 copy-start.2
  2.0 4.3 %copy-start = (bf16[1024,2048]{1,0:T(8,128)(2,1)S(1)}, bf16[1024,2048]{1,0:T(8,128)(2,1)}, u32[]{:S(2)}) copy-start(bf16[1024,2048]{1,0:T(8,128)(2,1)} %weight_ref.1) | copy-start | bytes 12582916
  2.0 4.3 %copy-start.1 = (bf16[1024,1024]{1,0:T(8,128)(2,1)S(1)}, bf16[1024,1024]{1,0:T(8,128)(2,1)}, u32[]{:S(2)}) copy-start(bf16[1024,1024]{1,0:T(8,128)(2,1)} %out_weight_ref.5) | copy-start | bytes 6291460
  2.0 4.3 %copy-start.3 = (bf16[2,256,1024]{2,1,0:T(8,128)(2,1)S(1)}, bf16[2,256,1024]{2,1,0:T(8,128)(2,1)}, u32[]{:S(2)}) copy-start(bf16[2,256,1024]{2,1,0:T(8,128)(2,1)} %param.9) | copy-start | bytes 3145732
  2.0 4.3 %copy-start.5 = (f32[31,1024]{1,0:T(8,128)S(1)}, f32[31,1024]{1,0:T(8,128)}, u32[]{:S(2)}) copy-start(f32[31,1024]{1,0:T(8,128)} %depth_ref.5) | copy-start | bytes 380932
  2.0 4.3 %copy-start.7 = (f32[1024]{0:T(1024)S(1)}, f32[1024]{0:T(1024)}, u32[]{:S(2)}) copy-start(f32[1024]{0:T(1024)} %param.12) | copy-start | bytes 12292
  2.0 4.3 %copy-start.8 = (s32[2]{0:T(128)S(1)}, s32[2]{0:T(128)}, u32[]{:S(2)}) copy-start(s32[2]{0:T(128)} %lengths_ref.9) | copy-start | bytes 28
  3.2 15.6 %collective-permute-start = (f32[2,256,256]{2,1,0:T(8,128)S(1)}, f32[2,256,256]{2,1,0:T(8,128)S(1)}, u32[]{:S(2)}, u32[]{:S(2)}) collective-permute-start(f32[2,256,256]{2,1,0:T(8,128)S(1)} %get-tuple-element.118), channel_id=1, source_target_pairs={{0,16},{16,0},{1,17},{17,1},{2,18},{18,2},{3,19},{19,3},{4,20},{20... | collective-permute-start | bytes 1572872 | tf_op jit(solution)/shard_map/ppermute | solution.py:54
  6.3 12.6 %copy-start.4 = (bf16[1024,256]{1,0:T(8,128)(2,1)S(1)}, bf16[1024,256]{1,0:T(8,128)(2,1)}, u32[]{:S(2)}) copy-start(bf16[1024,256]{1,0:T(8,128)(2,1)} %head_ref.3) | copy-start | bytes 1572868
  6.3 12.6 %copy-start.6 = (f32[1024]{0:T(1024)S(1)}, f32[1024]{0:T(1024)}, u32[]{:S(2)}) copy-start(f32[1024]{0:T(1024)} %param.16) | copy-start | bytes 12292
  25.5 8.6 %collective-permute-start.1 = (bf16[2,8,64,640]{3,2,1,0:T(8,128)(2,1)S(1)}, bf16[2,8,64,640]{3,2,1,0:T(8,128)(2,1)S(1)}, u32[]{:S(2)}, u32[]{:S(2)}) collective-permute-start(bf16[2,8,64,640]{3,2,1,0:T(8,128)(2,1)S(1)} %get-tuple-element.126), channel_id=1, source_target_pairs={{0,1},{1,0},{2,3},{3,2},{4,5},{5,4},{6,7},{7,6},{8,9},{9,8},{10,11... | collective-permute-start | bytes 3932168 | tf_op jit(solution)/shard_map/ppermute | solution.py:54
  33.6 13.7 %collective-permute-start.5 = (bf16[2,8,64,512]{3,2,1,0:T(8,128)(2,1)S(1)}, bf16[2,8,64,512]{3,2,1,0:T(8,128)(2,1)S(1)}, u32[]{:S(2)}, u32[]{:S(2)}) collective-permute-start(bf16[2,8,64,512]{3,2,1,0:T(8,128)(2,1)S(1)} %get-tuple-element.139), channel_id=1, source_target_pairs={{0,1},{1,0},{2,3},{3,2},{4,5},{5,4},{6,7},{7,6},{8,9},{9,8},{10,11... | collective-permute-start | bytes 3145736 | tf_op jit(solution)/shard_map/ppermute | solution.py:54
  34.6 10.7 %collective-permute-start.2 = (bf16[2,4,64,640]{3,2,1,0:T(8,128)(2,1)S(1)}, bf16[2,4,64,640]{3,2,1,0:T(8,128)(2,1)S(1)}, u32[]{:S(2)}, u32[]{:S(2)}) collective-permute-start(bf16[2,4,64,640]{3,2,1,0:T(8,128)(2,1)S(1)} %slice.58), channel_id=1, source_target_pairs={{0,16},{1,3},{2,18},{3,1},{4,20},{5,7},{6,22},{7,5},{8,24},{9,11},... | collective-permute-start | bytes 1966088 | tf_op jit(solution)/shard_map/ppermute | solution.py:60
  44.5 4.7 %collective-permute-start.4 = (bf16[2,8,64,512]{3,2,1,0:T(8,128)(2,1)S(1)}, bf16[2,8,64,512]{3,2,1,0:T(8,128)(2,1)S(1)}, u32[]{:S(2)}, u32[]{:S(2)}) collective-permute-start(bf16[2,8,64,512]{3,2,1,0:T(8,128)(2,1)S(1)} %get-tuple-element.137), channel_id=1, source_target_pairs={{0,1},{1,0},{2,3},{3,2},{4,5},{5,4},{6,7},{7,6},{8,9},{9,8},{10,11... | collective-permute-start | bytes 3145736 | tf_op jit(solution)/shard_map/ppermute | solution.py:54
  45.4 12.4 %collective-permute-start.3 = (bf16[2,2,64,640]{3,2,1,0:T(8,128)(2,1)S(1)}, bf16[2,2,64,640]{3,2,1,0:T(8,128)(2,1)S(1)}, u32[]{:S(2)}, u32[]{:S(2)}) collective-permute-start(bf16[2,2,64,640]{3,2,1,0:T(8,128)(2,1)S(1)} %slice.76), channel_id=1, source_target_pairs={{0,2},{1,17},{2,0},{3,19},{4,6},{5,21},{6,4},{7,23},{8,10},{9,25},... | collective-permute-start | bytes 983048 | tf_op jit(solution)/shard_map/ppermute | solution.py:60
  47.6 10.0 %collective-permute-start.6 = (bf16[2,4,64,512]{3,2,1,0:T(8,128)(2,1)S(1)}, bf16[2,4,64,512]{3,2,1,0:T(8,128)(2,1)S(1)}, u32[]{:S(2)}, u32[]{:S(2)}) collective-permute-start(bf16[2,4,64,512]{3,2,1,0:T(8,128)(2,1)S(1)} %slice.77), channel_id=1, source_target_pairs={{0,16},{1,3},{2,18},{3,1},{4,20},{5,7},{6,22},{7,5},{8,24},{9,11},... | collective-permute-start | bytes 1572872 | tf_op jit(solution)/shard_map/ppermute | solution.py:60
  49.6 13.1 %collective-permute-start.9 = (bf16[2,4,64,512]{3,2,1,0:T(8,128)(2,1)S(1)}, bf16[2,4,64,512]{3,2,1,0:T(8,128)(2,1)S(1)}, u32[]{:S(2)}, u32[]{:S(2)}) collective-permute-start(bf16[2,4,64,512]{3,2,1,0:T(8,128)(2,1)S(1)} %slice.79), channel_id=1, source_target_pairs={{0,16},{1,3},{2,18},{3,1},{4,20},{5,7},{6,22},{7,5},{8,24},{9,11},... | collective-permute-start | bytes 1572872 | tf_op jit(solution)/shard_map/ppermute | solution.py:60
  56.1 8.3 %collective-permute-start.8 = (f32[32,1024]{1,0:T(8,128)S(1)}, f32[32,1024]{1,0:T(8,128)S(1)}, u32[]{:S(2)}, u32[]{:S(2)}) collective-permute-start(f32[32,1024]{1,0:T(8,128)S(1)} %taps.1), channel_id=1, source_target_pairs={{0,16},{1,3},{2,18},{3,1},{4,20},{5,7},{6,22},{7,5},{8,24},{9,11},... | collective-permute-start | bytes 393224 | tf_op jit(solution)/shard_map/ppermute | solution.py:60
  58.0 11.8 %collective-permute-start.12 = (bf16[2,1,64,640]{3,2,1,0:T(8,128)(2,1)S(1)}, bf16[2,1,64,640]{3,2,1,0:T(8,128)(2,1)S(1)}, u32[]{:S(2)}, u32[]{:S(2)}) collective-permute-start(bf16[2,1,64,640]{3,2,1,0:T(8,128)(2,1)S(1)} %slice.82), channel_id=1, source_target_pairs={{0,4},{1,9},{2,6},{3,11},{4,0},{5,13},{6,2},{7,15},{8,12},{9,1},{1... | collective-permute-start | bytes 491528 | tf_op jit(solution)/shard_map/ppermute | solution.py:60
  59.6 8.4 %collective-permute-start.7 = (bf16[2,2,64,512]{3,2,1,0:T(8,128)(2,1)S(1)}, bf16[2,2,64,512]{3,2,1,0:T(8,128)(2,1)S(1)}, u32[]{:S(2)}, u32[]{:S(2)}) collective-permute-start(bf16[2,2,64,512]{3,2,1,0:T(8,128)(2,1)S(1)} %slice.78), channel_id=1, source_target_pairs={{0,2},{1,17},{2,0},{3,19},{4,6},{5,21},{6,4},{7,23},{8,10},{9,25},... | collective-permute-start | bytes 786440 | tf_op jit(solution)/shard_map/ppermute | solution.py:60
  64.5 30.5 %collective-permute-start.20 = (f32[32,1024]{1,0:T(8,128)S(1)}, f32[32,1024]{1,0:T(8,128)S(1)}, u32[]{:S(2)}, u32[]{:S(2)}) collective-permute-start(f32[32,1024]{1,0:T(8,128)S(1)} %add.83), channel_id=1, source_target_pairs={{0,2},{1,17},{2,0},{3,19},{4,6},{5,21},{6,4},{7,23},{8,10},{9,25},... | collective-permute-start | bytes 393224 | tf_op jit(solution)/shard_map/ppermute | solution.py:60
  68.0 6.4 %collective-permute-start.11 = (bf16[2,2,64,512]{3,2,1,0:T(8,128)(2,1)S(1)}, bf16[2,2,64,512]{3,2,1,0:T(8,128)(2,1)S(1)}, u32[]{:S(2)}, u32[]{:S(2)}) collective-permute-start(bf16[2,2,64,512]{3,2,1,0:T(8,128)(2,1)S(1)} %slice.81), channel_id=1, source_target_pairs={{0,2},{1,17},{2,0},{3,19},{4,6},{5,21},{6,4},{7,23},{8,10},{9,25},... | collective-permute-start | bytes 786440 | tf_op jit(solution)/shard_map/ppermute | solution.py:60
  69.8 8.4 %collective-permute-start.10 = (bf16[2,1,64,512]{3,2,1,0:T(8,128)(2,1)S(1)}, bf16[2,1,64,512]{3,2,1,0:T(8,128)(2,1)S(1)}, u32[]{:S(2)}, u32[]{:S(2)}) collective-permute-start(bf16[2,1,64,512]{3,2,1,0:T(8,128)(2,1)S(1)} %slice.80), channel_id=1, source_target_pairs={{0,4},{1,9},{2,6},{3,11},{4,0},{5,13},{6,2},{7,15},{8,12},{9,1},{1... | collective-permute-start | bytes 393224 | tf_op jit(solution)/shard_map/ppermute | solution.py:60
  70.5 8.5 %collective-permute-start.14 = (bf16[2,1,64,640]{3,2,1,0:T(8,128)(2,1)S(1)}, bf16[2,1,64,640]{3,2,1,0:T(8,128)(2,1)S(1)}, u32[]{:S(2)}, u32[]{:S(2)}) collective-permute-start(bf16[2,1,64,640]{3,2,1,0:T(8,128)(2,1)S(1)} %add_convert_fusion.10), channel_id=1, source_target_pairs={{0,8},{1,5},{2,10},{3,7},{4,12},{5,1},{6,14},{7,3},{8,0},{9,13},{1... | collective-permute-start | bytes 491528 | tf_op jit(solution)/shard_map/ppermute | solution.py:60
  78.2 10.7 %collective-permute-start.17 = (bf16[2,1,64,512]{3,2,1,0:T(8,128)(2,1)S(1)}, bf16[2,1,64,512]{3,2,1,0:T(8,128)(2,1)S(1)}, u32[]{:S(2)}, u32[]{:S(2)}) collective-permute-start(bf16[2,1,64,512]{3,2,1,0:T(8,128)(2,1)S(1)} %add_convert_fusion.14), channel_id=1, source_target_pairs={{0,8},{1,5},{2,10},{3,7},{4,12},{5,1},{6,14},{7,3},{8,0},{9,13},{1... | collective-permute-start | bytes 393224 | tf_op jit(solution)/shard_map/ppermute | solution.py:60
  78.9 6.4 %collective-permute-start.13 = (bf16[2,1,64,512]{3,2,1,0:T(8,128)(2,1)S(1)}, bf16[2,1,64,512]{3,2,1,0:T(8,128)(2,1)S(1)}, u32[]{:S(2)}, u32[]{:S(2)}) collective-permute-start(bf16[2,1,64,512]{3,2,1,0:T(8,128)(2,1)S(1)} %slice.83), channel_id=1, source_target_pairs={{0,4},{1,9},{2,6},{3,11},{4,0},{5,13},{6,2},{7,15},{8,12},{9,1},{1... | collective-permute-start | bytes 393224 | tf_op jit(solution)/shard_map/ppermute | solution.py:60
  81.5 8.1 %collective-permute-start.16 = (bf16[2,1,64,640]{3,2,1,0:T(8,128)(2,1)S(1)}, bf16[2,1,64,640]{3,2,1,0:T(8,128)(2,1)S(1)}, u32[]{:S(2)}, u32[]{:S(2)}) collective-permute-start(bf16[2,1,64,640]{3,2,1,0:T(8,128)(2,1)S(1)} %add_convert_fusion.9), channel_id=1, source_target_pairs={{0,4},{1,9},{2,6},{3,11},{4,0},{5,13},{6,2},{7,15},{8,12},{9,1},{1... | collective-permute-start | bytes 491528 | tf_op jit(solution)/shard_map/ppermute | solution.py:60
  85.3 9.5 %collective-permute-start.15 = (bf16[2,1,64,512]{3,2,1,0:T(8,128)(2,1)S(1)}, bf16[2,1,64,512]{3,2,1,0:T(8,128)(2,1)S(1)}, u32[]{:S(2)}, u32[]{:S(2)}) collective-permute-start(bf16[2,1,64,512]{3,2,1,0:T(8,128)(2,1)S(1)} %add_convert_fusion.13), channel_id=1, source_target_pairs={{0,8},{1,5},{2,10},{3,7},{4,12},{5,1},{6,14},{7,3},{8,0},{9,13},{1... | collective-permute-start | bytes 393224 | tf_op jit(solution)/shard_map/ppermute | solution.py:60
  89.0 8.1 %collective-permute-start.19 = (bf16[2,1,64,512]{3,2,1,0:T(8,128)(2,1)S(1)}, bf16[2,1,64,512]{3,2,1,0:T(8,128)(2,1)S(1)}, u32[]{:S(2)}, u32[]{:S(2)}) collective-permute-start(bf16[2,1,64,512]{3,2,1,0:T(8,128)(2,1)S(1)} %add_convert_fusion.12), channel_id=1, source_target_pairs={{0,4},{1,9},{2,6},{3,11},{4,0},{5,13},{6,2},{7,15},{8,12},{9,1},{1... | collective-permute-start | bytes 393224 | tf_op jit(solution)/shard_map/ppermute | solution.py:60
  89.5 14.8 %collective-permute-start.18 = (bf16[2,2,64,640]{3,2,1,0:T(8,128)(2,1)S(1)}, bf16[2,2,64,640]{3,2,1,0:T(8,128)(2,1)S(1)}, u32[]{:S(2)}, u32[]{:S(2)}) collective-permute-start(bf16[2,2,64,640]{3,2,1,0:T(8,128)(2,1)S(1)} %constant_dynamic-update-slice_fusion), channel_id=1, source_target_pairs={{0,2},{1,17},{2,0},{3,19},{4,6},{5,21},{6,4},{7,23},{8,10},{9,25},... | collective-permute-start | bytes 983048 | tf_op jit(solution)/shard_map/ppermute | solution.py:60
  94.9 9.7 %collective-permute-start.24 = (bf16[2,1,64,512]{3,2,1,0:T(8,128)(2,1)S(1)}, bf16[2,1,64,512]{3,2,1,0:T(8,128)(2,1)S(1)}, u32[]{:S(2)}, u32[]{:S(2)}) collective-permute-start(bf16[2,1,64,512]{3,2,1,0:T(8,128)(2,1)S(1)} %add_convert_fusion.11), channel_id=1, source_target_pairs={{0,4},{1,9},{2,6},{3,11},{4,0},{5,13},{6,2},{7,15},{8,12},{9,1},{1... | collective-permute-start | bytes 393224 | tf_op jit(solution)/shard_map/ppermute | solution.py:60
  95.0 9.6 %collective-permute-start.23 = (f32[32,1024]{1,0:T(8,128)S(1)}, f32[32,1024]{1,0:T(8,128)S(1)}, u32[]{:S(2)}, u32[]{:S(2)}) collective-permute-start(f32[32,1024]{1,0:T(8,128)S(1)} %add.92), channel_id=1, source_target_pairs={{0,4},{1,9},{2,6},{3,11},{4,0},{5,13},{6,2},{7,15},{8,12},{9,1},{1... | collective-permute-start | bytes 393224 | tf_op jit(solution)/shard_map/ppermute | solution.py:60
  97.1 14.5 %collective-permute-start.22 = (bf16[2,2,64,512]{3,2,1,0:T(8,128)(2,1)S(1)}, bf16[2,2,64,512]{3,2,1,0:T(8,128)(2,1)S(1)}, u32[]{:S(2)}, u32[]{:S(2)}) collective-permute-start(bf16[2,2,64,512]{3,2,1,0:T(8,128)(2,1)S(1)} %constant_dynamic-update-slice_fusion.2), channel_id=1, source_target_pairs={{0,2},{1,17},{2,0},{3,19},{4,6},{5,21},{6,4},{7,23},{8,10},{9,25},... | collective-permute-start | bytes 786440 | tf_op jit(solution)/shard_map/ppermute | solution.py:60
  104.4 13.5 %collective-permute-start.21 = (bf16[2,4,64,640]{3,2,1,0:T(8,128)(2,1)S(1)}, bf16[2,4,64,640]{3,2,1,0:T(8,128)(2,1)S(1)}, u32[]{:S(2)}, u32[]{:S(2)}) collective-permute-start(bf16[2,4,64,640]{3,2,1,0:T(8,128)(2,1)S(1)} %constant_dynamic-update-slice_fusion.4), channel_id=1, source_target_pairs={{0,16},{1,3},{2,18},{3,1},{4,20},{5,7},{6,22},{7,5},{8,24},{9,11},... | collective-permute-start | bytes 1966088 | tf_op jit(solution)/shard_map/ppermute | solution.py:60
  111.6 11.9 %collective-permute-start.25 = (bf16[2,4,64,512]{3,2,1,0:T(8,128)(2,1)S(1)}, bf16[2,4,64,512]{3,2,1,0:T(8,128)(2,1)S(1)}, u32[]{:S(2)}, u32[]{:S(2)}) collective-permute-start(bf16[2,4,64,512]{3,2,1,0:T(8,128)(2,1)S(1)} %constant_dynamic-update-slice_fusion.8), channel_id=1, source_target_pairs={{0,16},{1,3},{2,18},{3,1},{4,20},{5,7},{6,22},{7,5},{8,24},{9,11},... | collective-permute-start | bytes 1572872 | tf_op jit(solution)/shard_map/ppermute | solution.py:60
  111.7 9.9 %collective-permute-start.26 = (f32[32,1024]{1,0:T(8,128)S(1)}, f32[32,1024]{1,0:T(8,128)S(1)}, u32[]{:S(2)}, u32[]{:S(2)}) collective-permute-start(f32[32,1024]{1,0:T(8,128)S(1)} %add.93), channel_id=1, source_target_pairs={{0,8},{1,5},{2,10},{3,7},{4,12},{5,1},{6,14},{7,3},{8,0},{9,13},{1... | collective-permute-start | bytes 393224 | tf_op jit(solution)/shard_map/ppermute | solution.py:60
  114.3 7.2 %collective-permute-start.27 = (bf16[2,2,64,512]{3,2,1,0:T(8,128)(2,1)S(1)}, bf16[2,2,64,512]{3,2,1,0:T(8,128)(2,1)S(1)}, u32[]{:S(2)}, u32[]{:S(2)}) collective-permute-start(bf16[2,2,64,512]{3,2,1,0:T(8,128)(2,1)S(1)} %constant_dynamic-update-slice_fusion.6), channel_id=1, source_target_pairs={{0,2},{1,17},{2,0},{3,19},{4,6},{5,21},{6,4},{7,23},{8,10},{9,25},... | collective-permute-start | bytes 786440 | tf_op jit(solution)/shard_map/ppermute | solution.py:60
  118.0 6.2 %collective-permute-start.30 = (bf16[2,8,64,640]{3,2,1,0:T(8,128)(2,1)S(1)}, bf16[2,8,64,640]{3,2,1,0:T(8,128)(2,1)S(1)}, u32[]{:S(2)}, u32[]{:S(2)}) collective-permute-start(bf16[2,8,64,640]{3,2,1,0:T(8,128)(2,1)S(1)} %constant_dynamic-update-slice_fusion.10.mine_ref), channel_id=1, source_target_pairs={{0,1},{1,0},{2,3},{3,2},{4,5},{5,4},{6,7},{7,6},{8,9},{9,8},{10,11... | collective-permute-start | bytes 3932168 | tf_op jit(solution)/shard_map/ppermute | solution.py:54
  123.6 2.9 %collective-permute-start.28 = (bf16[2,8,64,512]{3,2,1,0:T(8,128)(2,1)S(1)}, bf16[2,8,64,512]{3,2,1,0:T(8,128)(2,1)S(1)}, u32[]{:S(2)}, u32[]{:S(2)}) collective-permute-start(bf16[2,8,64,512]{3,2,1,0:T(8,128)(2,1)S(1)} %constant_dynamic-update-slice_fusion.14.refs_0_), channel_id=1, source_target_pairs={{0,1},{1,0},{2,3},{3,2},{4,5},{5,4},{6,7},{7,6},{8,9},{9,8},{10,11... | collective-permute-start | bytes 3145736 | tf_op jit(solution)/shard_map/ppermute | solution.py:54
  123.7 2.8 %collective-permute-start.29 = (f32[32,1024]{1,0:T(8,128)S(1)}, f32[32,1024]{1,0:T(8,128)S(1)}, u32[]{:S(2)}, u32[]{:S(2)}) collective-permute-start(f32[32,1024]{1,0:T(8,128)S(1)} %add.94), channel_id=1, source_target_pairs={{0,1},{1,0},{2,3},{3,2},{4,5},{5,4},{6,7},{7,6},{8,9},{9,8},{10,11... | collective-permute-start | bytes 393224 | tf_op jit(solution)/shard_map/ppermute | solution.py:54
  124.2 9.2 %collective-permute-start.31 = (bf16[2,4,64,512]{3,2,1,0:T(8,128)(2,1)S(1)}, bf16[2,4,64,512]{3,2,1,0:T(8,128)(2,1)S(1)}, u32[]{:S(2)}, u32[]{:S(2)}) collective-permute-start(bf16[2,4,64,512]{3,2,1,0:T(8,128)(2,1)S(1)} %constant_dynamic-update-slice_fusion.12), channel_id=1, source_target_pairs={{0,16},{1,3},{2,18},{3,1},{4,20},{5,7},{6,22},{7,5},{8,24},{9,11},... | collective-permute-start | bytes 1572872 | tf_op jit(solution)/shard_map/ppermute | solution.py:60
  133.4 2.7 %collective-permute-start.32 = (bf16[2,8,64,512]{3,2,1,0:T(8,128)(2,1)S(1)}, bf16[2,8,64,512]{3,2,1,0:T(8,128)(2,1)S(1)}, u32[]{:S(2)}, u32[]{:S(2)}) collective-permute-start(bf16[2,8,64,512]{3,2,1,0:T(8,128)(2,1)S(1)} %constant_dynamic-update-slice_fusion.16.refs_2_), channel_id=1, source_target_pairs={{0,1},{1,0},{2,3},{3,2},{4,5},{5,4},{6,7},{7,6},{8,9},{9,8},{10,11... | collective-permute-start | bytes 3145736 | tf_op jit(solution)/shard_map/ppermute | solution.py:54
